TPU v7x, 32 devices: a whole 2x2x4 slice. The times are simulated.
32 devices in a mesh: groups: 2 (over y), owner: 4 (over z), helper: 2 (over x), sub: 2 (over core).
Axes of the slice: x: 2, y: 2, z: 4, core: 2. Of those that a mesh axis runs over, the one named last changes fastest.
Arguments:
- embeddings: bfloat16 [8192, 1024], P(('groups', 'owner', 'helper', 'sub')), parts along dimension 0, may hold values from -128 to 128
- cluster_id: int32 [8192], P(('groups', 'owner', 'helper', 'sub')), parts along dimension 0, may hold values from 0 to 7, as said below
Outputs:
- dup_count: float32 [8192], P(('groups', 'owner', 'helper', 'sub')), parts along dimension 0
There are 2 independent parts, one for each index of `groups`. A program takes and returns all parts, laid end to end along the dimension named above; each array names one. Nothing has to cross between parts.
Inputs may be any that keep to these rules, and one draw needn't show every extreme that they name: `cluster_id`: among the documents of one device no cluster is named more than 64 times, and on every device one cluster is named exactly 64 times. Among the documents of the 4 devices that share a helper and a sub index no cluster is named more than 256 times, and one cluster is named exactly 256 times.
All inputs are finite; a program needn't handle non-finite values.
Results may differ from a plain program's by a relative error of at most 0.0024.
Values may be sent and summed in bfloat16 or wider, within the bound.
No kernel may reach another device: no remote copies, remote signals or barrier semaphores. Data moves between devices by JAX's collectives and lax.ppermute only.
A program may use at most 64 MiB of HBM per device.

v0:
```python
import jax
import jax.numpy as jnp
from jax import lax
from jax.sharding import PartitionSpec as P

CL_OWN = 2


epsilon = 1e-06
threshold = 0.8
sharpness = 0.05


def cluster_weights(own_rows, other_rows, own_first):
    scores = jnp.einsum("md,nd->mn", own_rows, other_rows, preferred_element_type=jnp.float32)
    own_pos = own_first + jnp.arange(own_rows.shape[0], dtype=jnp.int32)
    other_pos = jnp.arange(other_rows.shape[0], dtype=jnp.int32)
    live_cols = jnp.any(other_rows != 0, axis=-1)
    live_rows = jnp.any(own_rows != 0, axis=-1)
    keep_mask = live_rows[:, None] & live_cols[None, :] & (own_pos[:, None] != other_pos[None, :])
    weights = jax.nn.sigmoid((scores - threshold) / sharpness)
    return jnp.where(keep_mask, weights, jnp.zeros_like(weights))


def body(embeddings, cluster_id):
    doc_count, feature_count = embeddings.shape
    owners = lax.axis_size("owner")
    clusters = CL_OWN * owners
    capacity = 2 * doc_count // clusters
    widened = embeddings.astype(jnp.float32)
    factor = lax.rsqrt(
        jnp.mean(widened * widened, axis=-1, keepdims=True) + epsilon
    ) * feature_count ** (-0.5)
    unit_rows = (widened * factor).astype(jnp.bfloat16)
    doc_order = jnp.arange(doc_count, dtype=jnp.int32)
    same_cluster = (cluster_id[:, None] == cluster_id[None, :]) & (
        doc_order[:, None] > doc_order[None, :]
    )
    doc_rank = jnp.sum(same_cluster.astype(jnp.int32), axis=1)
    slot_index = cluster_id * capacity + doc_rank
    slot_range = jnp.arange(clusters * capacity, dtype=jnp.int32)
    dispatch = (slot_index[None, :] == slot_range[:, None]).astype(jnp.bfloat16)
    outgoing = jnp.dot(dispatch, unit_rows, preferred_element_type=jnp.float32).astype(jnp.bfloat16)
    outgoing = outgoing.reshape(owners, CL_OWN, capacity, feature_count)
    arrived = lax.all_to_all(outgoing, "owner", split_axis=0, concat_axis=2, tiled=True)
    members = arrived[0]
    member_count = members.shape[1]
    position = lax.axis_index("helper") * lax.axis_size("sub") + lax.axis_index("sub")
    own_first = position * member_count
    block_rows = lax.all_gather(members, ("helper", "sub"), axis=1, tiled=True)
    counts = jnp.stack(
        [
            jnp.sum(cluster_weights(members[cluster], block_rows[cluster], own_first), axis=1)
            for cluster in range(CL_OWN)
        ]
    )
    per_slot = lax.all_to_all(
        counts.reshape(CL_OWN, owners, capacity), "owner", split_axis=1, concat_axis=0, tiled=True
    )
    return jnp.take(per_slot.reshape(-1), slot_index)


def solution(mesh):
    in_specs = (
        P(("groups", "owner", "helper", "sub"), None),
        P(("groups", "owner", "helper", "sub")),
    )
    out_specs = P(("groups", "owner", "helper", "sub"))
    return jax.shard_map(body, mesh=mesh, in_specs=in_specs, out_specs=out_specs, check_vma=False)
```

profile of v0, /device:TPU:0, one launch (start us, length us, event | category | flops | bytes accessed | tf_op | source)
XLA Modules:
  0.0 106.6 jit_solution(14814060323125217103)
XLA Ops:
  6.5 0.0 all-gather.2.cloned.1.call-start
  6.5 0.9 convert_reduce_fusion
  7.5 0.7 compare_select_fusion
  8.2 1.2 %fusion.18 = f32[256]{0:T(256)S(1)} fusion(bf16[256,1024]{1,0:T(8,128)(2,1)} %param.2), kind=kLoop, calls=%fused_computation.26 | loop fusion | flops 786176 | bytes 525312 | tf_op jit(solution)/shard_map/reduce_sum | solution.py:32
  9.4 1.6 %convolution_convert_fusion = bf16[512,1024]{1,0:T(8,128)(2,1)S(1)} fusion(bf16[256,1024]{1,0:T(8,128)(2,1)} %param.2, f32[256]{0:T(256)S(1)} %rsqrt_multiply_fusion, s32[256]{0:T(256)S(1)} %get-tuple-element.10), kind=kOutput, calls=%fused_computation.7 | convolution fusion | flops 269877248 | bytes 1574912 | tf_op jit(solution)/shard_map/dot_general | solution.py:43
  11.0 31.8 %all_to_all.30 = bf16[4,2,64,1024]{3,2,1,0:T(8,128)(2,1)S(1)} all-to-all(bf16[4,2,64,1024]{3,2,1,0:T(8,128)(2,1)S(1)} %bitcast.66), channel_id=1, replica_groups=mesh['groups'=2,'owner'=4,'helper'=2,'sub'=2] {'owner'}, dimensions={0} | all-to-all | bytes 2097152 | tf_op jit(solution)/shard_map/all_to_all | solution.py:45
  42.8 1.1 %copy.8 = bf16[4,2,64,1024]{3,2,0,1:T(8,128)(2,1)} copy(bf16[4,2,64,1024]{3,2,1,0:T(8,128)(2,1)S(1)} %all_to_all.30) | data formatting | bytes 2097152 | tf_op jit(solution)/shard_map/all_to_all | solution.py:45
  43.9 0.0 copy-start
  43.9 0.0 all-gather.2.cloned.1.call-update
  43.9 1.6 %compare_reduce_fusion.3 = (pred[4,64]{1,0:T(4,128)(4,1)S(1)}, pred[4,64]{1,0:T(4,128)(4,1)S(1)}) fusion(bf16[1,2,4,64,1024]{4,3,2,1,0:T(8,128)(2,1)} %bitcast.64), kind=kLoop, calls=%fused_computation.32 | loop fusion | flops 1048064 | bytes 1049088 | tf_op jit(solution)/shard_map/reduce_or | solution.py:19
  45.6 0.1 and.48
  45.7 0.1 and.53
  45.7 0.0 copy-done
  45.7 0.1 fusion.26
  45.8 31.9 %all-gather.2.cloned.1.call-done = bf16[2,1024,1024]{2,1,0:T(8,128)(2,1)} async-done(((bf16[2,256,1024]{2,1,0:T(8,128)(2,1)}), bf16[2,1024,1024]{2,1,0:T(8,128)(2,1)}) %all-gather.2.cloned.1.call-update) | async-done | bytes 4194320 | tf_op jit(solution)/shard_map/all_gather | solution.py:50
  77.7 0.0 copy-start.1
  77.7 3.4 %compare_reduce_fusion.1 = (pred[1024]{0:T(1024)(128)(4,1)S(1)}, pred[1024]{0:T(1024)(128)(4,1)S(1)}) fusion(bf16[2,1024,1024]{2,1,0:T(8,128)(2,1)} %all-gather.2.cloned.1.call-done), kind=kLoop, calls=%fused_computation.2 | loop fusion | flops 4192256 | bytes 4196352 | tf_op jit(solution)/shard_map/reduce_or | solution.py:18
  81.1 0.0 copy-done.1
  81.1 1.1 %fusion.14 = f32[256]{0:T(256)S(1)} fusion(bf16[256,1024]{1,0:T(8,128)(2,1)S(1)} %bitcast.68, bf16[2,1024,1024]{2,1,0:T(8,128)(2,1)S(1)} %copy-done.1, s32[256]{0:T(256)S(1)} %iota_add_fusion, pred[1024]{0:T(1024)(128)(4,1)S(1)} %get-tuple-element.5, pred[256]{0:T(512)(128)(4,1)S(1)} %and.48), kind=kOutput, calls=%fused_computation.22 | convolution fusion | flops 539492096 | bytes 2625024 | tf_op jit(solution)/shard_map/md,nd->mn/dot_general | solution.py:15
  82.3 0.1 stack.9
  82.3 2.7 %fusion.17 = f32[256]{0:T(256)S(1)} fusion(bf16[256,1024]{1,0:T(8,128)(2,1)S(1)} %bitcast.67, bf16[2,1024,1024]{2,1,0:T(8,128)(2,1)} %all-gather.2.cloned.1.call-done, s32[256]{0:T(256)S(1)} %iota_add_fusion, pred[1024]{0:T(1024)(128)(4,1)S(1)} %get-tuple-element.6, pred[256]{0:T(512)(128)(4,1)S(1)} %and.53), kind=kOutput, calls=%fused_computation.25 | convolution fusion | flops 539492096 | bytes 2624768 | tf_op jit(solution)/shard_map/md,nd->mn/dot_general | solution.py:15
  85.1 0.1 stack.10
  85.2 0.7 reshape.58
  85.9 4.6 %all-to-all-start.1 = ((f32[4,1,128]{2,1,0:T(1,128)}), f32[4,1,128]{2,1,0:T(1,128)S(1)}, u32[]{:S(2)}, u32[]{:S(2)}) async-start(f32[4,1,128]{2,1,0:T(1,128)} %reshape.58), calls=%async_computation.1 | async-start | bytes 4096 | tf_op jit(solution)/shard_map/all_to_all | solution.py:57
  90.5 5.4 %all-to-all-done.1 = f32[4,1,128]{2,1,0:T(1,128)S(1)} async-done(((f32[4,1,128]{2,1,0:T(1,128)}), f32[4,1,128]{2,1,0:T(1,128)S(1)}, u32[]{:S(2)}, u32[]{:S(2)}) %all-to-all-start.1) | async-done | bytes 2080 | tf_op jit(solution)/shard_map/all_to_all | solution.py:57
  95.9 0.5 broadcast.73
  96.4 0.7 reduce.2
  97.0 0.1 reshape.59
  97.1 0.1 reshape.48
  97.2 1.9 %gather_fusion = f32[256]{0:T(256)S(1)} fusion(f32[512]{0:T(512)S(1)} %reshape.48, s32[1024]{0:T(1024)S(1)} %pad_clamp_fusion), kind=kCustom, calls=%fused_computation | custom fusion | bytes 3072 | tf_op jit(solution)/shard_map/jit(_take)/gather | solution.py:60
  99.2 0.6 and_select_fusion
  (5 shorter events, 0.0 us)
Async XLA Ops:
  6.5 71.1 %all-gather.2.cloned.1.call-start = ((), (), s32[]{:S(2)}) async-start(), calls=%async_computation.2 | async-start | bytes 5242880 | tf_op jit(solution)/shard_map/all_gather | solution.py:50
  43.9 1.8 %copy-start = (bf16[4,2,64,1024]{3,2,0,1:T(8,128)(2,1)S(1)}, bf16[4,2,64,1024]{3,2,0,1:T(8,128)(2,1)}, u32[]{:S(2)}) copy-start(bf16[4,2,64,1024]{3,2,0,1:T(8,128)(2,1)} %copy.8) | copy-start | bytes 3145732
  77.7 3.4 %copy-start.1 = (bf16[2,1024,1024]{2,1,0:T(8,128)(2,1)S(1)}, bf16[2,1024,1024]{2,1,0:T(8,128)(2,1)}, u32[]{:S(2)}) copy-start(bf16[2,1024,1024]{2,1,0:T(8,128)(2,1)} %all-gather.2.cloned.1.call-done) | copy-start | bytes 12582916
  85.9 10.0 %all-to-all-start.1 = ((f32[4,1,128]{2,1,0:T(1,128)}), f32[4,1,128]{2,1,0:T(1,128)S(1)}, u32[]{:S(2)}, u32[]{:S(2)}) async-start(f32[4,1,128]{2,1,0:T(1,128)} %reshape.58), calls=%async_computation.1 | async-start | bytes 4096 | tf_op jit(solution)/shard_map/all_to_all | solution.py:57
Sparse Core Ops, SparseCore 0:
  44.0 33.5 all-gather.1
where the time goes:
time: 107 us
  waiting for transfers between devices  37.3 us (35%)
  blocking collectives  31.8 us (30%)
  between operations  13.5 us (13%)
  other arithmetic  9.12 us (9%)
  matrix products  5.45 us (5%)
  local copies, waits for them, and re-layouts  4.86 us (5%)
  starting transfers between devices  4.6 us (4%)
    all_gather x1, waiting for transfers between devices, body(): block_rows = lax.all_gather(members, ('helper', 'sub'), axis=1, tiled=True)  31.9 us
    all_to_all x1, blocking collectives, body(): lax.all_to_all(outgoing, 'owner', split_axis=0, concat_axis=2, tiled=True)  31.8 us
    all_to_all x1, waiting for transfers between devices, body(): lax.all_to_all(counts.reshape(CL_OWN, owners, capacity), 'owner', split_a...  5.38 us
    all_to_all x1, starting transfers between devices, body(): lax.all_to_all(counts.reshape(CL_OWN, owners, capacity), 'owner', split_a...  4.6 us
    dot_general x2, matrix products, cluster_weights(): jnp.einsum('md,nd->mn', own_rows, other_rows, preferred_element_type=jnp....  3.88 us
    reduce_or x1, other arithmetic, cluster_weights(): live_cols = jnp.any(other_rows != 0, axis=-1)  3.4 us
  transfers between devices with their start and end apart: 2, of which 2 were waited for; matrix products, arithmetic and copies ran while one was open for 2% of the time, Pallas kernels for 0%

commit v1 on v0

v1 whole, which is shorter than its diff:
```python
import functools
import math

import jax
import jax.numpy as jnp
from jax import lax
from jax.experimental import pallas as pl
from jax.experimental.pallas import tpu as pltpu
from jax.sharding import PartitionSpec as P

CL_OWN = 2

epsilon = 1e-06
threshold = 0.8
sharpness = 0.05

EMPTY = 4.0
TILE = 256
VMEM = pl.BlockSpec(memory_space=pltpu.VMEM)
ANY = pl.BlockSpec(memory_space=pl.ANY)


def route_kernel(clusters, capacity, by_chip, rows_ref, ids_ref, *out_refs):
    piece_refs, slot_ref = out_refs[:-1], out_refs[-1]
    doc_count, feature_count = rows_ref.shape
    widened = rows_ref[...].astype(jnp.float32)
    factor = lax.rsqrt(
        jnp.mean(widened * widened, axis=-1, keepdims=True) + epsilon
    ) * feature_count ** (-0.5)
    unit_rows = (widened * factor).astype(jnp.bfloat16)

    ids = ids_ref[...]
    member = lax.broadcasted_iota(jnp.int32, (clusters, doc_count), 0) == ids
    earlier = lax.broadcasted_iota(jnp.int32, (doc_count, doc_count), 0) < (
        lax.broadcasted_iota(jnp.int32, (doc_count, doc_count), 1)
    )
    ahead = jnp.dot(
        member.astype(jnp.bfloat16), earlier.astype(jnp.bfloat16), preferred_element_type=jnp.float32
    )
    rank = jnp.sum(jnp.where(member, ahead, 0.0), axis=0, keepdims=True).astype(jnp.int32)
    if by_chip:
        ids = ids ^ (lax.axis_index("owner") * CL_OWN + lax.axis_index("helper"))
    slot = ids * capacity + rank
    slot_ref[...] = slot

    slots = clusters * capacity
    dispatch = lax.broadcasted_iota(jnp.int32, (slots, doc_count), 0) == slot
    filled = jnp.sum(dispatch.astype(jnp.float32), axis=1, keepdims=True) > 0
    dispatch = dispatch.astype(jnp.bfloat16)
    piece_rows = slots // len(piece_refs)
    for first in range(0, feature_count, TILE):
        columns = slice(first, first + TILE)
        laid = jnp.dot(dispatch, unit_rows[:, columns], preferred_element_type=jnp.float32)
        if first == 0:
            lane = lax.broadcasted_iota(jnp.int32, (slots, TILE), 1)
            laid = jnp.where(filled | (lane > 0), laid, EMPTY)
        laid = laid.astype(jnp.bfloat16)
        for k, piece in enumerate(piece_refs):
            piece[:, columns] = laid[k * piece_rows : (k + 1) * piece_rows]


def route(embeddings, cluster_id, clusters, capacity, pieces, by_chip):
    doc_count, feature_count = embeddings.shape
    piece = jax.ShapeDtypeStruct((clusters * capacity // pieces, feature_count), jnp.bfloat16)
    *laid, slot = pl.pallas_call(
        functools.partial(route_kernel, clusters, capacity, by_chip),
        out_shape=[piece] * pieces + [jax.ShapeDtypeStruct((1, doc_count), jnp.int32)],
        in_specs=[VMEM, VMEM],
        out_specs=[VMEM] * (pieces + 1),
        compiler_params=pltpu.CompilerParams(vmem_limit_bytes=32 * 2**20),
        name="route",
    )(embeddings, cluster_id.reshape(1, doc_count))
    return laid, slot


def count_kernel(own_pieces, *refs):
    rows, sem = refs[-2:]
    count_refs = refs[-2 - own_pieces : -2]
    piece_refs = refs[: -2 - own_pieces]
    copies, first = [], 0
    for k, piece in enumerate(piece_refs):
        copies.append(
            pltpu.make_async_copy(piece, rows.at[pl.ds(first, piece.shape[0])], sem.at[k])
        )
        first += piece.shape[0]
    for copy in copies:
        copy.start()
    for copy in copies:
        copy.wait()
    own_count = sum(piece.shape[0] for piece in piece_refs[:own_pieces])
    own = rows[:own_count]
    slope = -math.log2(math.e) / sharpness
    total = jnp.zeros((1, own_count), jnp.float32)
    for first in range(0, first, TILE):
        other = rows[first : first + TILE]
        scores = lax.dot_general(
            other, own, (((1,), (1,)), ((), ())), preferred_element_type=jnp.float32
        )
        weights = 1.0 / (1.0 + jnp.exp2(scores * slope - threshold * slope))
        keep = other[:, :1].astype(jnp.float32) < 0.5 * EMPTY
        if first < own_count:
            keep = keep & (
                lax.broadcasted_iota(jnp.int32, scores.shape, 0) + first
                != lax.broadcasted_iota(jnp.int32, scores.shape, 1)
            )
        total = total + jnp.sum(jnp.where(keep, weights, 0.0), axis=0, keepdims=True)
    first = 0
    for count in count_refs:
        count[...] = total[:, first : first + count.shape[1]]
        first += count.shape[1]


def soft_counts(own, others):
    pieces = own + others
    total = sum(piece.shape[0] for piece in pieces)
    return pl.pallas_call(
        functools.partial(count_kernel, len(own)),
        out_shape=[jax.ShapeDtypeStruct((1, piece.shape[0]), jnp.float32) for piece in own],
        in_specs=[ANY] * len(pieces),
        out_specs=[VMEM] * len(own),
        scratch_shapes=[
            pltpu.VMEM((total, own[0].shape[1]), jnp.bfloat16),
            pltpu.SemaphoreType.DMA((len(pieces),)),
        ],
        compiler_params=pltpu.CompilerParams(vmem_limit_bytes=32 * 2**20),
        name="count",
    )(*pieces)


def select_kernel(capacity, *refs):
    *count_refs, slot_ref, out_ref = refs
    counts = jnp.concatenate([count[...] for count in count_refs], axis=0)
    slot = slot_ref[...]
    doc_count = slot.shape[1]
    block = slot // capacity
    rank = slot - block * capacity
    hot = (lax.broadcasted_iota(jnp.int32, (capacity, doc_count), 0) == rank).astype(jnp.float32)
    by_block = jnp.dot(
        counts, hot, precision=lax.Precision.HIGHEST, preferred_element_type=jnp.float32
    )
    chosen = lax.broadcasted_iota(jnp.int32, by_block.shape, 0) == block
    out_ref[...] = jnp.sum(jnp.where(chosen, by_block, 0.0), axis=0, keepdims=True)


def select(counts, slot, capacity):
    return pl.pallas_call(
        functools.partial(select_kernel, capacity),
        out_shape=jax.ShapeDtypeStruct(slot.shape, jnp.float32),
        in_specs=[VMEM] * (len(counts) + 1),
        out_specs=VMEM,
        name="select",
    )(*counts, slot)[0]


def swap_cores(x):
    cores = lax.axis_size("sub")
    return lax.ppermute(x, "sub", [(i, i ^ 1) for i in range(cores)])


def body_by_chip(embeddings, cluster_id):
    doc_count = embeddings.shape[0]
    clusters = CL_OWN * lax.axis_size("owner")
    capacity = 2 * doc_count // clusters

    def across(x, k):
        if k == 0:
            return x
        return lax.ppermute(x, ("owner", "helper"), [(i, i ^ k) for i in range(clusters)])

    pieces, slot = route(embeddings, cluster_id, clusters, capacity, clusters, True)
    order = list(range(clusters - 1, -1, -1))
    own = {k: across(pieces[k], k) for k in order}
    others = {k: swap_cores(own[k]) for k in own}
    counts = soft_counts([own[k] for k in range(clusters)], [others[k] for k in range(clusters)])
    back = [across(counts[k], k) for k in range(clusters)]
    return select(back, slot, capacity)


def body_by_owner(embeddings, cluster_id):
    doc_count, feature_count = embeddings.shape
    owners, helpers = lax.axis_size("owner"), lax.axis_size("helper")
    clusters = CL_OWN * owners
    capacity = 2 * doc_count // clusters
    mine = lax.axis_index("helper") % CL_OWN

    def partner(x):
        return lax.ppermute(x, "helper", [(i, i ^ 1) for i in range(helpers)])

    (outgoing,), slot = route(embeddings, cluster_id, clusters, capacity, 1, False)
    outgoing = outgoing.reshape(owners, CL_OWN, capacity, feature_count)
    arrived = lax.all_to_all(outgoing, "owner", split_axis=0, concat_axis=0, tiled=True)
    kept = lax.dynamic_index_in_dim(arrived, mine, 1, keepdims=False)
    given = partner(lax.dynamic_index_in_dim(arrived, 1 - mine, 1, keepdims=False))
    own = jnp.stack([kept, given]).reshape(CL_OWN * owners * capacity, feature_count)
    others = [swap_cores(own)]
    for step in range(CL_OWN, helpers, CL_OWN):
        turn = [(i, (i + step) % helpers) for i in range(helpers)]
        others += [lax.ppermute(x, "helper", turn) for x in (own, others[0])]
    (counts,) = soft_counts([own], others)
    counts = counts.reshape(CL_OWN, owners, capacity)
    kept, given = counts[0], partner(counts[1])
    counts = jnp.where(mine == 0, jnp.stack([kept, given], 1), jnp.stack([given, kept], 1))
    back = lax.all_to_all(counts, "owner", split_axis=0, concat_axis=0, tiled=True)
    return select([back.reshape(clusters, capacity)], slot, capacity)


def solution(mesh):
    in_specs = (
        P(("groups", "owner", "helper", "sub"), None),
        P(("groups", "owner", "helper", "sub")),
    )
    out_specs = P(("groups", "owner", "helper", "sub"))
    body = body_by_chip if mesh.shape["helper"] == CL_OWN else body_by_owner
    return jax.shard_map(body, mesh=mesh, in_specs=in_specs, out_specs=out_specs, check_vma=False)
```

time: 107 us -> 58.9 us (0.55)
  blocking collectives: 31.8 us -> 0 us
  starting transfers between devices: 4.6 us -> 29.9 us
  waiting for transfers between devices: 37.3 us -> 18.1 us
  between operations: 13.5 us -> 0.1 us
  other arithmetic: 9.12 us -> 0 us
  Pallas kernels: 0 us -> 6.78 us
  matrix products: 5.45 us -> 0 us
    all_gather x1 -> x0, waiting for transfers between devices: 31.9 us -> none  [body(): block_rows = lax.all_gather(members, ('helper', 'sub'), axis=1, tiled=True)]
    all_to_all x1 -> x0, blocking collectives: 31.8 us -> none  [body(): lax.all_to_all(outgoing, 'owner', split_axis=0, concat_axis=2, tiled=True)]
    ppermute x0 -> x22, starting transfers between devices: none -> 29.9 us  [the longest x14 28.1 us: across(): lax.ppermute(x, ('owner', 'helper'), [(i, i ^ k) for i in range(clusters)])]
    ppermute x0 -> x22, waiting for transfers between devices: none -> 18.1 us  [the longest x14 16.7 us: across(): lax.ppermute(x, ('owner', 'helper'), [(i, i ^ k) for i in range(clusters)])]
    pallas_call x0 -> x3, Pallas kernels: none -> 6.78 us  [the longest x1 4.69 us: soft_counts(): pl.pallas_call(functools.partial(count_kernel, len(own)), out_shape=[jax....]
    dot_general x3 -> x0, matrix products: 5.45 us -> none  [the longest x2 3.88 us: cluster_weights(): jnp.einsum('md,nd->mn', own_rows, other_rows, preferred_element_type=jnp....]
    all_to_all x1 -> x0, waiting for transfers between devices: 5.38 us -> none  [body(): lax.all_to_all(counts.reshape(CL_OWN, owners, capacity), 'owner', split_a...]
    reduce_or x2 -> x0, other arithmetic: 5.02 us -> none  [the longest x1 3.4 us: cluster_weights(): live_cols = jnp.any(other_rows != 0, axis=-1)]
  transfers between devices with their start and end apart: 2 -> 22, of which waited for: 2 -> 10; matrix products, arithmetic and copies ran while one was open for 2% -> 0% of each run, Pallas kernels for 0% -> 0%
where the time goes in v1:
time: 58.9 us; the launch traced here: 58.7 us
  starting transfers between devices  29.9 us (51%)
  waiting for transfers between devices  18.1 us (31%)
  Pallas kernels  6.78 us (12%)
  local copies, waits for them, and re-layouts  3.88 us (7%)
    ppermute x14, starting transfers between devices, across(): lax.ppermute(x, ('owner', 'helper'), [(i, i ^ k) for i in range(clusters)])  28.1 us
    ppermute x14, waiting for transfers between devices, across(): lax.ppermute(x, ('owner', 'helper'), [(i, i ^ k) for i in range(clusters)])  16.7 us
    pallas_call x1, Pallas kernels, soft_counts(): pl.pallas_call(functools.partial(count_kernel, len(own)), out_shape=[jax....  4.69 us
    unnamed x22, local copies, waits for them, and re-layouts  3.88 us
    ppermute x8, starting transfers between devices, swap_cores(): return lax.ppermute(x, 'sub', [(i, i ^ 1) for i in range(cores)])  1.8 us
    pallas_call x1, Pallas kernels, select(): pl.pallas_call(functools.partial(select_kernel, capacity), out_shape=jax....  1.42 us
    ppermute x8, waiting for transfers between devices, swap_cores(): return lax.ppermute(x, 'sub', [(i, i ^ 1) for i in range(cores)])  1.39 us
  transfers between devices with their start and end apart: 22, of which 10 were waited for; matrix products, arithmetic and copies ran while one was open for 0% of the time, Pallas kernels for 0%

profile of v1, /device:TPU:0, one launch (start us, length us, event | category | flops | bytes accessed | tf_op | source)
XLA Modules:
  0.0 58.7 jit_solution(11263683123150941511)
XLA Ops:
  0.0 0.7 %copy-done.1 = s32[256]{0:T(256)S(1)} copy-done((s32[256]{0:T(256)S(1)}, s32[256]{0:T(256)}, u32[]{:S(2)}) %copy-start.1) | copy-done | bytes 1048
  0.7 1.0 %copy-done = bf16[256,1024]{1,0:T(8,128)(2,1)S(1)} copy-done((bf16[256,1024]{1,0:T(8,128)(2,1)S(1)}, bf16[256,1024]{1,0:T(8,128)(2,1)}, u32[]{:S(2)}) %copy-start) | copy-done | bytes 524312
  1.7 0.7 %route.1 = (bf16[64,1024]{1,0:T(8,128)(2,1)S(1)}, bf16[64,1024]{1,0:T(8,128)(2,1)S(1)}, bf16[64,1024]{1,0:T(8,128)(2,1)S(1)}, bf16[64,1024]{1,0:T(8,128)(2,1)S(1...) custom-call(bf16[256,1024]{1,0:T(8,128)(2,1)S(1)} %copy-done, ...), custom_call_target="tpu_custom_call" | custom-call | tf_op jit(solution)/shard_map/route/pallas_call | solution.py:65
  2.4 3.0 %collective-permute-start = (bf16[64,1024]{1,0:T(8,128)(2,1)S(1)}, bf16[64,1024]{1,0:T(8,128)(2,1)S(1)}, u32[]{:S(2)}, u32[]{:S(2)}) collective-permute-start(bf16[64,1024]{1,0:T(8,128)(2,1)S(1)} %get-tuple-element.23), channel_id=1, source_target_pairs={{0,2},{2,0},{4,6},{6,4},{8,10},{10,8},{12,14},{14,12},{1,3},{3,1},... | collective-permute-start | bytes 393224 | tf_op jit(solution)/shard_map/ppermute | solution.py:168
  5.4 1.6 %collective-permute-start.1 = (bf16[64,1024]{1,0:T(8,128)(2,1)S(1)}, bf16[64,1024]{1,0:T(8,128)(2,1)S(1)}, u32[]{:S(2)}, u32[]{:S(2)}) collective-permute-start(bf16[64,1024]{1,0:T(8,128)(2,1)S(1)} %get-tuple-element.24), channel_id=1, source_target_pairs={{0,4},{2,6},{4,0},{6,2},{8,12},{10,14},{12,8},{14,10},{1,5},{3,7},... | collective-permute-start | bytes 393224 | tf_op jit(solution)/shard_map/ppermute | solution.py:168
  7.0 0.3 collective-permute-start.2
  7.4 2.7 %collective-permute-start.3 = (bf16[64,1024]{1,0:T(8,128)(2,1)S(1)}, bf16[64,1024]{1,0:T(8,128)(2,1)S(1)}, u32[]{:S(2)}, u32[]{:S(2)}) collective-permute-start(bf16[64,1024]{1,0:T(8,128)(2,1)S(1)} %get-tuple-element.26), channel_id=1, source_target_pairs={{0,8},{2,10},{4,12},{6,14},{8,0},{10,2},{12,4},{14,6},{1,9},{3,11}... | collective-permute-start | bytes 393224 | tf_op jit(solution)/shard_map/ppermute | solution.py:168
  10.0 1.3 %collective-permute-start.4 = (bf16[64,1024]{1,0:T(8,128)(2,1)S(1)}, bf16[64,1024]{1,0:T(8,128)(2,1)S(1)}, u32[]{:S(2)}, u32[]{:S(2)}) collective-permute-start(bf16[64,1024]{1,0:T(8,128)(2,1)S(1)} %get-tuple-element.27), channel_id=1, source_target_pairs={{0,10},{2,8},{4,14},{6,12},{8,2},{10,0},{12,6},{14,4},{1,11},{3,9}... | collective-permute-start | bytes 393224 | tf_op jit(solution)/shard_map/ppermute | solution.py:168
  11.3 3.6 %collective-permute-start.5 = (bf16[64,1024]{1,0:T(8,128)(2,1)S(1)}, bf16[64,1024]{1,0:T(8,128)(2,1)S(1)}, u32[]{:S(2)}, u32[]{:S(2)}) collective-permute-start(bf16[64,1024]{1,0:T(8,128)(2,1)S(1)} %get-tuple-element.28), channel_id=1, source_target_pairs={{0,12},{2,14},{4,8},{6,10},{8,4},{10,6},{12,0},{14,2},{1,13},{3,15... | collective-permute-start | bytes 393224 | tf_op jit(solution)/shard_map/ppermute | solution.py:168
  14.9 1.2 %collective-permute-done.1.refs_2_ = bf16[64,1024]{1,0:T(8,128)(2,1)S(1)} collective-permute-done((bf16[64,1024]{1,0:T(8,128)(2,1)S(1)}, bf16[64,1024]{1,0:T(8,128)(2,1)S(1)}, u32[]{:S(2)}, u32[]{:S(2)}) %collective-permute-start.1) | collective-permute-done | bytes 131104 | tf_op jit(solution)/shard_map/ppermute | solution.py:168
  16.1 1.2 %collective-permute-start.6 = (bf16[64,1024]{1,0:T(8,128)(2,1)S(1)}, bf16[64,1024]{1,0:T(8,128)(2,1)S(1)}, u32[]{:S(2)}, u32[]{:S(2)}) collective-permute-start(bf16[64,1024]{1,0:T(8,128)(2,1)S(1)} %get-tuple-element.29), channel_id=1, source_target_pairs={{0,14},{2,12},{4,10},{6,8},{8,6},{10,4},{12,2},{14,0},{1,15},{3,13... | collective-permute-start | bytes 393224 | tf_op jit(solution)/shard_map/ppermute | solution.py:168
  17.4 0.5 collective-permute-start.8
  17.9 11.3 %collective-permute-done.4.refs_5_ = bf16[64,1024]{1,0:T(8,128)(2,1)S(1)} collective-permute-done((bf16[64,1024]{1,0:T(8,128)(2,1)S(1)}, bf16[64,1024]{1,0:T(8,128)(2,1)S(1)}, u32[]{:S(2)}, u32[]{:S(2)}) %collective-permute-start.4) | collective-permute-done | bytes 131104 | tf_op jit(solution)/shard_map/ppermute | solution.py:168
  29.3 0.5 collective-permute-start.10
  29.9 0.4 collective-permute-start.12
  30.4 0.2 collective-permute-done.9.refs_10_
  30.8 0.3 collective-permute-done.11.refs_12_
  31.3 0.3 collective-permute-done.13.refs_14_
  31.7 0.3 collective-permute-done.14.refs_15_
  32.0 4.7 %count.1 = (f32[1,64]{1,0:T(1,128)S(1)}, f32[1,64]{1,0:T(1,128)S(1)}, f32[1,64]{1,0:T(1,128)S(1)}, f32[1,64]{1,0:T(1,128)S(1)}, f32[1,64]{1,0:T(1,128)S(1)}, /*i...) custom-call(bf16[64,1024]{1,0:T(8,128)(2,1)S(1)} %get-tuple-element.22.refs_0_, ...), custom_call_target="tpu_custom_call" | custom-call | tf_op jit(solution)/shard_map/count/pallas_call | solution.py:116
  36.7 0.5 copy-done.3
  37.2 0.9 %collective-permute-start.15 = (f32[1,64]{1,0:T(1,128)S(1)}, f32[1,64]{1,0:T(1,128)S(1)}, u32[]{:S(2)}, u32[]{:S(2)}) collective-permute-start(f32[1,64]{1,0:T(1,128)S(1)} %get-tuple-element.31), channel_id=1, source_target_pairs={{0,2},{2,0},{4,6},{6,4},{8,10},{10,8},{12,14},{14,12},{1,3},{3,1},... | collective-permute-start | bytes 776 | tf_op jit(solution)/shard_map/ppermute | solution.py:168
  38.1 4.1 %collective-permute-start.16 = (f32[1,64]{1,0:T(1,128)S(1)}, f32[1,64]{1,0:T(1,128)S(1)}, u32[]{:S(2)}, u32[]{:S(2)}) collective-permute-start(f32[1,64]{1,0:T(1,128)S(1)} %get-tuple-element.32), channel_id=1, source_target_pairs={{0,4},{2,6},{4,0},{6,2},{8,12},{10,14},{12,8},{14,10},{1,5},{3,7},... | collective-permute-start | bytes 776 | tf_op jit(solution)/shard_map/ppermute | solution.py:168
  42.2 1.0 %collective-permute-start.17 = (f32[1,64]{1,0:T(1,128)S(1)}, f32[1,64]{1,0:T(1,128)S(1)}, u32[]{:S(2)}, u32[]{:S(2)}) collective-permute-start(f32[1,64]{1,0:T(1,128)S(1)} %get-tuple-element.33), channel_id=1, source_target_pairs={{0,6},{2,4},{4,2},{6,0},{8,14},{10,12},{12,10},{14,8},{1,7},{3,5},... | collective-permute-start | bytes 776 | tf_op jit(solution)/shard_map/ppermute | solution.py:168
  43.2 3.6 %collective-permute-start.18 = (f32[1,64]{1,0:T(1,128)S(1)}, f32[1,64]{1,0:T(1,128)S(1)}, u32[]{:S(2)}, u32[]{:S(2)}) collective-permute-start(f32[1,64]{1,0:T(1,128)S(1)} %get-tuple-element.34), channel_id=1, source_target_pairs={{0,8},{2,10},{4,12},{6,14},{8,0},{10,2},{12,4},{14,6},{1,9},{3,11}... | collective-permute-start | bytes 776 | tf_op jit(solution)/shard_map/ppermute | solution.py:168
  47.0 0.6 copy-done.4
  47.6 2.4 %collective-permute-start.20 = (f32[1,64]{1,0:T(1,128)S(1)}, f32[1,64]{1,0:T(1,128)S(1)}, u32[]{:S(2)}, u32[]{:S(2)}) collective-permute-start(f32[1,64]{1,0:T(1,128)S(1)} %get-tuple-element.36), channel_id=1, source_target_pairs={{0,12},{2,14},{4,8},{6,10},{8,4},{10,6},{12,0},{14,2},{1,13},{3,15... | collective-permute-start | bytes 776 | tf_op jit(solution)/shard_map/ppermute | solution.py:168
  49.9 0.6 copy-done.5
  50.5 2.2 %collective-permute-start.21 = (f32[1,64]{1,0:T(1,128)S(1)}, f32[1,64]{1,0:T(1,128)S(1)}, u32[]{:S(2)}, u32[]{:S(2)}) collective-permute-start(f32[1,64]{1,0:T(1,128)S(1)} %get-tuple-element.37), channel_id=1, source_target_pairs={{0,14},{2,12},{4,10},{6,8},{8,6},{10,4},{12,2},{14,0},{1,15},{3,13... | collective-permute-start | bytes 776 | tf_op jit(solution)/shard_map/ppermute | solution.py:168
  52.9 3.8 %collective-permute-done.21.refs_7_ = f32[1,64]{1,0:T(1,128)S(1)} collective-permute-done((f32[1,64]{1,0:T(1,128)S(1)}, f32[1,64]{1,0:T(1,128)S(1)}, u32[]{:S(2)}, u32[]{:S(2)}) %collective-permute-start.21) | collective-permute-done | bytes 288 | tf_op jit(solution)/shard_map/ppermute | solution.py:168
  56.8 0.5 copy-done.10
  57.3 1.4 %select.1 = f32[1,256]{1,0:T(1,128)} custom-call(f32[1,64]{1,0:T(1,128)} %copy-done.3, f32[1,64]{1,0:T(1,128)} %copy-done.4, f32[1,64]{1,0:T(1,128)} %copy-done.5, f32[1,64]{1,0:T(1,128)} %copy-done.6, f32[1,64]{1,0:T(1,128)} %copy-done.7, f32[1,64]{1,0:T(1,128)} %copy-done.8, f32[1,64]{1,0:T(1,128)} %copy-done.9, f32[1,64]{1,0:T(1,128)} %copy-done.10, ...), custom_call_target="tpu_custom_call" | custom-call | tf_op jit(solution)/shard_map/select/pallas_call | solution.py:146
  (37 shorter events, 1.0 us)
Async XLA Ops:
  0.0 0.7 %copy-start.1 = (s32[256]{0:T(256)S(1)}, s32[256]{0:T(256)}, u32[]{:S(2)}) copy-start(s32[256]{0:T(256)} %param.3) | copy-start | bytes 3076
  0.7 1.0 %copy-start = (bf16[256,1024]{1,0:T(8,128)(2,1)S(1)}, bf16[256,1024]{1,0:T(8,128)(2,1)}, u32[]{:S(2)}) copy-start(bf16[256,1024]{1,0:T(8,128)(2,1)} %rows_ref.1) | copy-start | bytes 1572868
  2.4 3.0 %copy-start.2 = (s32[1,256]{1,0:T(1,128)}, s32[1,256]{1,0:T(1,128)S(1)}, u32[]{:S(2)}) copy-start(s32[1,256]{1,0:T(1,128)S(1)} %get-tuple-element.38.refs_8_) | copy-start | bytes 3076
  2.4 8.9 %collective-permute-start = (bf16[64,1024]{1,0:T(8,128)(2,1)S(1)}, bf16[64,1024]{1,0:T(8,128)(2,1)S(1)}, u32[]{:S(2)}, u32[]{:S(2)}) collective-permute-start(bf16[64,1024]{1,0:T(8,128)(2,1)S(1)} %get-tuple-element.23), channel_id=1, source_target_pairs={{0,2},{2,0},{4,6},{6,4},{8,10},{10,8},{12,14},{14,12},{1,3},{3,1},... | collective-permute-start | bytes 393224 | tf_op jit(solution)/shard_map/ppermute | solution.py:168
  5.4 10.7 %collective-permute-start.1 = (bf16[64,1024]{1,0:T(8,128)(2,1)S(1)}, bf16[64,1024]{1,0:T(8,128)(2,1)S(1)}, u32[]{:S(2)}, u32[]{:S(2)}) collective-permute-start(bf16[64,1024]{1,0:T(8,128)(2,1)S(1)} %get-tuple-element.24), channel_id=1, source_target_pairs={{0,4},{2,6},{4,0},{6,2},{8,12},{10,14},{12,8},{14,10},{1,5},{3,7},... | collective-permute-start | bytes 393224 | tf_op jit(solution)/shard_map/ppermute | solution.py:168
  7.0 10.4 %collective-permute-start.2 = (bf16[64,1024]{1,0:T(8,128)(2,1)S(1)}, bf16[64,1024]{1,0:T(8,128)(2,1)S(1)}, u32[]{:S(2)}, u32[]{:S(2)}) collective-permute-start(bf16[64,1024]{1,0:T(8,128)(2,1)S(1)} %get-tuple-element.25), channel_id=1, source_target_pairs={{0,6},{2,4},{4,2},{6,0},{8,14},{10,12},{12,10},{14,8},{1,7},{3,5},... | collective-permute-start | bytes 393224 | tf_op jit(solution)/shard_map/ppermute | solution.py:168
  7.4 10.1 %collective-permute-start.3 = (bf16[64,1024]{1,0:T(8,128)(2,1)S(1)}, bf16[64,1024]{1,0:T(8,128)(2,1)S(1)}, u32[]{:S(2)}, u32[]{:S(2)}) collective-permute-start(bf16[64,1024]{1,0:T(8,128)(2,1)S(1)} %get-tuple-element.26), channel_id=1, source_target_pairs={{0,8},{2,10},{4,12},{6,14},{8,0},{10,2},{12,4},{14,6},{1,9},{3,11}... | collective-permute-start | bytes 393224 | tf_op jit(solution)/shard_map/ppermute | solution.py:168
  10.0 19.3 %collective-permute-start.4 = (bf16[64,1024]{1,0:T(8,128)(2,1)S(1)}, bf16[64,1024]{1,0:T(8,128)(2,1)S(1)}, u32[]{:S(2)}, u32[]{:S(2)}) collective-permute-start(bf16[64,1024]{1,0:T(8,128)(2,1)S(1)} %get-tuple-element.27), channel_id=1, source_target_pairs={{0,10},{2,8},{4,14},{6,12},{8,2},{10,0},{12,6},{14,4},{1,11},{3,9}... | collective-permute-start | bytes 393224 | tf_op jit(solution)/shard_map/ppermute | solution.py:168
  11.3 18.0 %collective-permute-start.5 = (bf16[64,1024]{1,0:T(8,128)(2,1)S(1)}, bf16[64,1024]{1,0:T(8,128)(2,1)S(1)}, u32[]{:S(2)}, u32[]{:S(2)}) collective-permute-start(bf16[64,1024]{1,0:T(8,128)(2,1)S(1)} %get-tuple-element.28), channel_id=1, source_target_pairs={{0,12},{2,14},{4,8},{6,10},{8,4},{10,6},{12,0},{14,2},{1,13},{3,15... | collective-permute-start | bytes 393224 | tf_op jit(solution)/shard_map/ppermute | solution.py:168
  16.1 13.7 %collective-permute-start.6 = (bf16[64,1024]{1,0:T(8,128)(2,1)S(1)}, bf16[64,1024]{1,0:T(8,128)(2,1)S(1)}, u32[]{:S(2)}, u32[]{:S(2)}) collective-permute-start(bf16[64,1024]{1,0:T(8,128)(2,1)S(1)} %get-tuple-element.29), channel_id=1, source_target_pairs={{0,14},{2,12},{4,10},{6,8},{8,6},{10,4},{12,2},{14,0},{1,15},{3,13... | collective-permute-start | bytes 393224 | tf_op jit(solution)/shard_map/ppermute | solution.py:168
  17.4 12.4 %collective-permute-start.7 = (bf16[64,1024]{1,0:T(8,128)(2,1)S(1)}, bf16[64,1024]{1,0:T(8,128)(2,1)S(1)}, u32[]{:S(2)}, u32[]{:S(2)}) collective-permute-start(bf16[64,1024]{1,0:T(8,128)(2,1)S(1)} %get-tuple-element.22.refs_0_), channel_id=1, source_target_pairs={{0,1},{1,0},{2,3},{3,2},{4,5},{5,4},{6,7},{7,6},{8,9},{9,8},{10,11... | collective-permute-start | bytes 393224 | tf_op jit(solution)/shard_map/ppermute | solution.py:157
  17.4 12.9 %collective-permute-start.8 = (bf16[64,1024]{1,0:T(8,128)(2,1)S(1)}, bf16[64,1024]{1,0:T(8,128)(2,1)S(1)}, u32[]{:S(2)}, u32[]{:S(2)}) collective-permute-start(bf16[64,1024]{1,0:T(8,128)(2,1)S(1)} %collective-permute-done.refs_1_), channel_id=1, source_target_pairs={{0,1},{1,0},{2,3},{3,2},{4,5},{5,4},{6,7},{7,6},{8,9},{9,8},{10,11... | collective-permute-start | bytes 393224 | tf_op jit(solution)/shard_map/ppermute | solution.py:157
  29.3 1.3 %collective-permute-start.9 = (bf16[64,1024]{1,0:T(8,128)(2,1)S(1)}, bf16[64,1024]{1,0:T(8,128)(2,1)S(1)}, u32[]{:S(2)}, u32[]{:S(2)}) collective-permute-start(bf16[64,1024]{1,0:T(8,128)(2,1)S(1)} %collective-permute-done.1.refs_2_), channel_id=1, source_target_pairs={{0,1},{1,0},{2,3},{3,2},{4,5},{5,4},{6,7},{7,6},{8,9},{9,8},{10,11... | collective-permute-start | bytes 393224 | tf_op jit(solution)/shard_map/ppermute | solution.py:157
  29.3 1.5 %collective-permute-start.10 = (bf16[64,1024]{1,0:T(8,128)(2,1)S(1)}, bf16[64,1024]{1,0:T(8,128)(2,1)S(1)}, u32[]{:S(2)}, u32[]{:S(2)}) collective-permute-start(bf16[64,1024]{1,0:T(8,128)(2,1)S(1)} %collective-permute-done.2.refs_3_), channel_id=1, source_target_pairs={{0,1},{1,0},{2,3},{3,2},{4,5},{5,4},{6,7},{7,6},{8,9},{9,8},{10,11... | collective-permute-start | bytes 393224 | tf_op jit(solution)/shard_map/ppermute | solution.py:157
  29.8 1.3 %collective-permute-start.11 = (bf16[64,1024]{1,0:T(8,128)(2,1)S(1)}, bf16[64,1024]{1,0:T(8,128)(2,1)S(1)}, u32[]{:S(2)}, u32[]{:S(2)}) collective-permute-start(bf16[64,1024]{1,0:T(8,128)(2,1)S(1)} %collective-permute-done.3.refs_4_), channel_id=1, source_target_pairs={{0,1},{1,0},{2,3},{3,2},{4,5},{5,4},{6,7},{7,6},{8,9},{9,8},{10,11... | collective-permute-start | bytes 393224 | tf_op jit(solution)/shard_map/ppermute | solution.py:157
  29.9 1.5 %collective-permute-start.12 = (bf16[64,1024]{1,0:T(8,128)(2,1)S(1)}, bf16[64,1024]{1,0:T(8,128)(2,1)S(1)}, u32[]{:S(2)}, u32[]{:S(2)}) collective-permute-start(bf16[64,1024]{1,0:T(8,128)(2,1)S(1)} %collective-permute-done.4.refs_5_), channel_id=1, source_target_pairs={{0,1},{1,0},{2,3},{3,2},{4,5},{5,4},{6,7},{7,6},{8,9},{9,8},{10,11... | collective-permute-start | bytes 393224 | tf_op jit(solution)/shard_map/ppermute | solution.py:157
  30.3 1.3 %collective-permute-start.13 = (bf16[64,1024]{1,0:T(8,128)(2,1)S(1)}, bf16[64,1024]{1,0:T(8,128)(2,1)S(1)}, u32[]{:S(2)}, u32[]{:S(2)}) collective-permute-start(bf16[64,1024]{1,0:T(8,128)(2,1)S(1)} %collective-permute-done.5.refs_6_), channel_id=1, source_target_pairs={{0,1},{1,0},{2,3},{3,2},{4,5},{5,4},{6,7},{7,6},{8,9},{9,8},{10,11... | collective-permute-start | bytes 393224 | tf_op jit(solution)/shard_map/ppermute | solution.py:157
  30.6 1.3 %collective-permute-start.14 = (bf16[64,1024]{1,0:T(8,128)(2,1)S(1)}, bf16[64,1024]{1,0:T(8,128)(2,1)S(1)}, u32[]{:S(2)}, u32[]{:S(2)}) collective-permute-start(bf16[64,1024]{1,0:T(8,128)(2,1)S(1)} %collective-permute-done.6.refs_7_), channel_id=1, source_target_pairs={{0,1},{1,0},{2,3},{3,2},{4,5},{5,4},{6,7},{7,6},{8,9},{9,8},{10,11... | collective-permute-start | bytes 393224 | tf_op jit(solution)/shard_map/ppermute | solution.py:157
  37.2 9.8 %collective-permute-start.15 = (f32[1,64]{1,0:T(1,128)S(1)}, f32[1,64]{1,0:T(1,128)S(1)}, u32[]{:S(2)}, u32[]{:S(2)}) collective-permute-start(f32[1,64]{1,0:T(1,128)S(1)} %get-tuple-element.31), channel_id=1, source_target_pairs={{0,2},{2,0},{4,6},{6,4},{8,10},{10,8},{12,14},{14,12},{1,3},{3,1},... | collective-permute-start | bytes 776 | tf_op jit(solution)/shard_map/ppermute | solution.py:168
  38.1 11.8 %collective-permute-start.16 = (f32[1,64]{1,0:T(1,128)S(1)}, f32[1,64]{1,0:T(1,128)S(1)}, u32[]{:S(2)}, u32[]{:S(2)}) collective-permute-start(f32[1,64]{1,0:T(1,128)S(1)} %get-tuple-element.32), channel_id=1, source_target_pairs={{0,4},{2,6},{4,0},{6,2},{8,12},{10,14},{12,8},{14,10},{1,5},{3,7},... | collective-permute-start | bytes 776 | tf_op jit(solution)/shard_map/ppermute | solution.py:168
  42.2 10.5 %collective-permute-start.17 = (f32[1,64]{1,0:T(1,128)S(1)}, f32[1,64]{1,0:T(1,128)S(1)}, u32[]{:S(2)}, u32[]{:S(2)}) collective-permute-start(f32[1,64]{1,0:T(1,128)S(1)} %get-tuple-element.33), channel_id=1, source_target_pairs={{0,6},{2,4},{4,2},{6,0},{8,14},{10,12},{12,10},{14,8},{1,7},{3,5},... | collective-permute-start | bytes 776 | tf_op jit(solution)/shard_map/ppermute | solution.py:168
  43.2 9.5 %collective-permute-start.18 = (f32[1,64]{1,0:T(1,128)S(1)}, f32[1,64]{1,0:T(1,128)S(1)}, u32[]{:S(2)}, u32[]{:S(2)}) collective-permute-start(f32[1,64]{1,0:T(1,128)S(1)} %get-tuple-element.34), channel_id=1, source_target_pairs={{0,8},{2,10},{4,12},{6,14},{8,0},{10,2},{12,4},{14,6},{1,9},{3,11}... | collective-permute-start | bytes 776 | tf_op jit(solution)/shard_map/ppermute | solution.py:168
  46.8 5.9 %collective-permute-start.19 = (f32[1,64]{1,0:T(1,128)S(1)}, f32[1,64]{1,0:T(1,128)S(1)}, u32[]{:S(2)}, u32[]{:S(2)}) collective-permute-start(f32[1,64]{1,0:T(1,128)S(1)} %get-tuple-element.35), channel_id=1, source_target_pairs={{0,10},{2,8},{4,14},{6,12},{8,2},{10,0},{12,6},{14,4},{1,11},{3,9}... | collective-permute-start | bytes 776 | tf_op jit(solution)/shard_map/ppermute | solution.py:168
  47.0 0.6 copy-start.4
  47.6 5.3 %collective-permute-start.20 = (f32[1,64]{1,0:T(1,128)S(1)}, f32[1,64]{1,0:T(1,128)S(1)}, u32[]{:S(2)}, u32[]{:S(2)}) collective-permute-start(f32[1,64]{1,0:T(1,128)S(1)} %get-tuple-element.36), channel_id=1, source_target_pairs={{0,12},{2,14},{4,8},{6,10},{8,4},{10,6},{12,0},{14,2},{1,13},{3,15... | collective-permute-start | bytes 776 | tf_op jit(solution)/shard_map/ppermute | solution.py:168
  49.9 0.6 copy-start.5
  50.5 6.2 %collective-permute-start.21 = (f32[1,64]{1,0:T(1,128)S(1)}, f32[1,64]{1,0:T(1,128)S(1)}, u32[]{:S(2)}, u32[]{:S(2)}) collective-permute-start(f32[1,64]{1,0:T(1,128)S(1)} %get-tuple-element.37), channel_id=1, source_target_pairs={{0,14},{2,12},{4,10},{6,8},{8,6},{10,4},{12,2},{14,0},{1,15},{3,13... | collective-permute-start | bytes 776 | tf_op jit(solution)/shard_map/ppermute | solution.py:168
  52.7 4.1 %copy-start.6 = (f32[1,64]{1,0:T(1,128)}, f32[1,64]{1,0:T(1,128)S(1)}, u32[]{:S(2)}) copy-start(f32[1,64]{1,0:T(1,128)S(1)} %collective-permute-done.17.refs_3_) | copy-start | bytes 772
  52.7 4.0 %copy-start.7 = (f32[1,64]{1,0:T(1,128)}, f32[1,64]{1,0:T(1,128)S(1)}, u32[]{:S(2)}) copy-start(f32[1,64]{1,0:T(1,128)S(1)} %collective-permute-done.18.refs_4_) | copy-start | bytes 772
  52.7 4.0 %copy-start.8 = (f32[1,64]{1,0:T(1,128)}, f32[1,64]{1,0:T(1,128)S(1)}, u32[]{:S(2)}) copy-start(f32[1,64]{1,0:T(1,128)S(1)} %collective-permute-done.19.refs_5_) | copy-start | bytes 772
  52.9 3.9 %copy-start.9 = (f32[1,64]{1,0:T(1,128)}, f32[1,64]{1,0:T(1,128)S(1)}, u32[]{:S(2)}) copy-start(f32[1,64]{1,0:T(1,128)S(1)} %collective-permute-done.20.refs_6_) | copy-start | bytes 772
  56.8 0.5 copy-start.10
  (1 other events, 0.5 us)

commit v2 on v1

--- a/solution.py
+++ b/solution.py
@@ -17,7 +17,10 @@
 EMPTY = 4.0
 TILE = 256
 VMEM = pl.BlockSpec(memory_space=pltpu.VMEM)
-ANY = pl.BlockSpec(memory_space=pl.ANY)
+
+
+def chip_index():
+    return lax.axis_index("owner") * CL_OWN + lax.axis_index("helper")
 
 
 def route_kernel(clusters, capacity, by_chip, rows_ref, ids_ref, *out_refs):
@@ -38,10 +41,10 @@
         member.astype(jnp.bfloat16), earlier.astype(jnp.bfloat16), preferred_element_type=jnp.float32
     )
     rank = jnp.sum(jnp.where(member, ahead, 0.0), axis=0, keepdims=True).astype(jnp.int32)
+    slot_ref[...] = ids * capacity + rank
     if by_chip:
-        ids = ids ^ (lax.axis_index("owner") * CL_OWN + lax.axis_index("helper"))
+        ids = ids ^ chip_index()
     slot = ids * capacity + rank
-    slot_ref[...] = slot
 
     slots = clusters * capacity
     dispatch = lax.broadcasted_iota(jnp.int32, (slots, doc_count), 0) == slot
@@ -73,63 +76,47 @@
     return laid, slot
 
 
-def count_kernel(own_pieces, *refs):
-    rows, sem = refs[-2:]
-    count_refs = refs[-2 - own_pieces : -2]
-    piece_refs = refs[: -2 - own_pieces]
-    copies, first = [], 0
-    for k, piece in enumerate(piece_refs):
-        copies.append(
-            pltpu.make_async_copy(piece, rows.at[pl.ds(first, piece.shape[0])], sem.at[k])
-        )
-        first += piece.shape[0]
-    for copy in copies:
-        copy.start()
-    for copy in copies:
-        copy.wait()
-    own_count = sum(piece.shape[0] for piece in piece_refs[:own_pieces])
-    own = rows[:own_count]
+def count_kernel(distances, *refs):
+    *piece_refs, count_ref = refs
+    pieces = [piece[...] for piece in piece_refs]
+    piece_rows = pieces[0].shape[0]
+    own = jnp.concatenate(pieces[: len(distances)], axis=0)
+    own_count = own.shape[0]
     slope = -math.log2(math.e) / sharpness
     total = jnp.zeros((1, own_count), jnp.float32)
-    for first in range(0, first, TILE):
-        other = rows[first : first + TILE]
+    per_tile = max(1, TILE // piece_rows)
+    for k in range(0, len(pieces), per_tile):
+        other = jnp.concatenate(pieces[k : k + per_tile], axis=0)
         scores = lax.dot_general(
             other, own, (((1,), (1,)), ((), ())), preferred_element_type=jnp.float32
         )
         weights = 1.0 / (1.0 + jnp.exp2(scores * slope - threshold * slope))
         keep = other[:, :1].astype(jnp.float32) < 0.5 * EMPTY
-        if first < own_count:
+        if k < len(distances):
             keep = keep & (
-                lax.broadcasted_iota(jnp.int32, scores.shape, 0) + first
+                lax.broadcasted_iota(jnp.int32, scores.shape, 0) + k * piece_rows
                 != lax.broadcasted_iota(jnp.int32, scores.shape, 1)
             )
         total = total + jnp.sum(jnp.where(keep, weights, 0.0), axis=0, keepdims=True)
-    first = 0
-    for count in count_refs:
-        count[...] = total[:, first : first + count.shape[1]]
-        first += count.shape[1]
-
-
-def soft_counts(own, others):
+    for k, distance in enumerate(distances):
+        place = chip_index() ^ distance if len(distances) > 1 else 0
+        count_ref[pl.ds(place, 1), 0, :] = total[:, k * piece_rows : (k + 1) * piece_rows]
+
+
+def soft_counts(own, others, distances):
     pieces = own + others
-    total = sum(piece.shape[0] for piece in pieces)
     return pl.pallas_call(
-        functools.partial(count_kernel, len(own)),
-        out_shape=[jax.ShapeDtypeStruct((1, piece.shape[0]), jnp.float32) for piece in own],
-        in_specs=[ANY] * len(pieces),
-        out_specs=[VMEM] * len(own),
-        scratch_shapes=[
-            pltpu.VMEM((total, own[0].shape[1]), jnp.bfloat16),
-            pltpu.SemaphoreType.DMA((len(pieces),)),
-        ],
+        functools.partial(count_kernel, distances),
+        out_shape=jax.ShapeDtypeStruct((len(own), 1, own[0].shape[0]), jnp.float32),
+        in_specs=[VMEM] * len(pieces),
+        out_specs=VMEM,
         compiler_params=pltpu.CompilerParams(vmem_limit_bytes=32 * 2**20),
         name="count",
     )(*pieces)
 
 
-def select_kernel(capacity, *refs):
-    *count_refs, slot_ref, out_ref = refs
-    counts = jnp.concatenate([count[...] for count in count_refs], axis=0)
+def select_kernel(capacity, counts_ref, slot_ref, out_ref):
+    counts = counts_ref[:, 0, :]
     slot = slot_ref[...]
     doc_count = slot.shape[1]
     block = slot // capacity
@@ -146,10 +133,11 @@
     return pl.pallas_call(
         functools.partial(select_kernel, capacity),
         out_shape=jax.ShapeDtypeStruct(slot.shape, jnp.float32),
-        in_specs=[VMEM] * (len(counts) + 1),
+        in_specs=[VMEM, VMEM],
         out_specs=VMEM,
+        compiler_params=pltpu.CompilerParams(vmem_limit_bytes=8 * 2**20),
         name="select",
-    )(*counts, slot)[0]
+    )(counts, slot)[0]
 
 
 def swap_cores(x):
@@ -168,11 +156,11 @@
         return lax.ppermute(x, ("owner", "helper"), [(i, i ^ k) for i in range(clusters)])
 
     pieces, slot = route(embeddings, cluster_id, clusters, capacity, clusters, True)
-    order = list(range(clusters - 1, -1, -1))
-    own = {k: across(pieces[k], k) for k in order}
-    others = {k: swap_cores(own[k]) for k in own}
-    counts = soft_counts([own[k] for k in range(clusters)], [others[k] for k in range(clusters)])
-    back = [across(counts[k], k) for k in range(clusters)]
+    distances = sorted(range(clusters), key=lambda k: (-(k // CL_OWN).bit_length(), k))
+    own = [across(pieces[k], k) for k in distances]
+    others = [swap_cores(piece) for piece in own]
+    counts = soft_counts(own, others, distances)
+    back = lax.all_to_all(counts, ("owner", "helper"), split_axis=0, concat_axis=0, tiled=True)
     return select(back, slot, capacity)
 
 
@@ -196,12 +184,12 @@
     for step in range(CL_OWN, helpers, CL_OWN):
         turn = [(i, (i + step) % helpers) for i in range(helpers)]
         others += [lax.ppermute(x, "helper", turn) for x in (own, others[0])]
-    (counts,) = soft_counts([own], others)
+    counts = soft_counts([own], others, [0])
     counts = counts.reshape(CL_OWN, owners, capacity)
     kept, given = counts[0], partner(counts[1])
     counts = jnp.where(mine == 0, jnp.stack([kept, given], 1), jnp.stack([given, kept], 1))
     back = lax.all_to_all(counts, "owner", split_axis=0, concat_axis=0, tiled=True)
-    return select([back.reshape(clusters, capacity)], slot, capacity)
+    return select(back.reshape(clusters, 1, capacity), slot, capacity)
 
 
 def solution(mesh):

time: 58.9 us -> 48.3 us (0.82)
  starting transfers between devices: 29.9 us -> 11.6 us
  blocking collectives: 0 us -> 12 us
  Pallas kernels: 6.78 us -> 2.99 us
  local copies, waits for them, and re-layouts: 3.88 us -> 1.72 us
  waiting for transfers between devices: 18.1 us -> 19.7 us
    ppermute x14 -> x7, starting transfers between devices: 28.1 us -> 10 us  [across(): lax.ppermute(x, ('owner', 'helper'), [(i, i ^ k) for i in range(clusters)])]
    all_to_all x0 -> x1, blocking collectives: none -> 12 us  [body_by_chip(): lax.all_to_all(counts, ('owner', 'helper'), split_axis=0, concat_axis=0,...]
    pallas_call x1, Pallas kernels: 4.69 us -> 1.59 us  [soft_counts(): pl.pallas_call(functools.partial(count_kernel, distances), out_shape=jax....]
    unnamed x22 -> x4, local copies, waits for them, and re-layouts: 3.88 us -> 1.72 us
    ppermute x14 -> x7, waiting for transfers between devices: 16.7 us -> 18.7 us  [across(): lax.ppermute(x, ('owner', 'helper'), [(i, i ^ k) for i in range(clusters)])]
    pallas_call x1, Pallas kernels: 1.42 us -> 0.73 us  [select(): pl.pallas_call(functools.partial(select_kernel, capacity), out_shape=jax....]
  transfers between devices with their start and end apart: 22 -> 15, of which waited for: 10 -> 8; matrix products, arithmetic and copies ran while one was open for 0% -> 0% of each run, Pallas kernels for 0% -> 0%
where the time goes in v2:
time: 48.3 us; the launch traced here: 48.1 us
  waiting for transfers between devices  19.7 us (41%)
  blocking collectives  12 us (25%)
  starting transfers between devices  11.6 us (24%)
  Pallas kernels  2.99 us (6%)
  local copies, waits for them, and re-layouts  1.72 us (4%)
    ppermute x7, waiting for transfers between devices, across(): lax.ppermute(x, ('owner', 'helper'), [(i, i ^ k) for i in range(clusters)])  18.7 us
    all_to_all x1, blocking collectives, body_by_chip(): lax.all_to_all(counts, ('owner', 'helper'), split_axis=0, concat_axis=0,...  12 us
    ppermute x7, starting transfers between devices, across(): lax.ppermute(x, ('owner', 'helper'), [(i, i ^ k) for i in range(clusters)])  10 us
    unnamed x4, local copies, waits for them, and re-layouts  1.72 us
    ppermute x8, starting transfers between devices, swap_cores(): return lax.ppermute(x, 'sub', [(i, i ^ 1) for i in range(cores)])  1.6 us
    pallas_call x1, Pallas kernels, soft_counts(): pl.pallas_call(functools.partial(count_kernel, distances), out_shape=jax....  1.59 us
    ppermute x8, waiting for transfers between devices, swap_cores(): return lax.ppermute(x, 'sub', [(i, i ^ 1) for i in range(cores)])  1.03 us
  transfers between devices with their start and end apart: 15, of which 8 were waited for; matrix products, arithmetic and copies ran while one was open for 0% of the time, Pallas kernels for 0%

profile of v2, /device:TPU:0, one launch (start us, length us, event | category | flops | bytes accessed | tf_op | source)
XLA Modules:
  0.0 48.1 jit_solution(202790034495886956)
XLA Ops:
  0.0 0.7 %copy-done.1 = s32[256]{0:T(256)S(1)} copy-done((s32[256]{0:T(256)S(1)}, s32[256]{0:T(256)}, u32[]{:S(2)}) %copy-start.1) | copy-done | bytes 1048
  0.7 1.0 %copy-done = bf16[256,1024]{1,0:T(8,128)(2,1)S(1)} copy-done((bf16[256,1024]{1,0:T(8,128)(2,1)S(1)}, bf16[256,1024]{1,0:T(8,128)(2,1)}, u32[]{:S(2)}) %copy-start) | copy-done | bytes 524312
  1.7 0.7 %route.1 = (bf16[64,1024]{1,0:T(8,128)(2,1)S(1)}, bf16[64,1024]{1,0:T(8,128)(2,1)S(1)}, bf16[64,1024]{1,0:T(8,128)(2,1)S(1)}, bf16[64,1024]{1,0:T(8,128)(2,1)S(1...) custom-call(bf16[256,1024]{1,0:T(8,128)(2,1)S(1)} %copy-done, ...), custom_call_target="tpu_custom_call" | custom-call | tf_op jit(solution)/shard_map/route/pallas_call | solution.py:68
  2.4 4.1 %collective-permute-start = (bf16[64,1024]{1,0:T(8,128)(2,1)S(1)}, bf16[64,1024]{1,0:T(8,128)(2,1)S(1)}, u32[]{:S(2)}, u32[]{:S(2)}) collective-permute-start(bf16[64,1024]{1,0:T(8,128)(2,1)S(1)} %get-tuple-element.14), channel_id=1, source_target_pairs={{0,8},{2,10},{4,12},{6,14},{8,0},{10,2},{12,4},{14,6},{1,9},{3,11}... | collective-permute-start | bytes 393224 | tf_op jit(solution)/shard_map/ppermute | solution.py:156
  6.5 1.3 %collective-permute-start.1 = (bf16[64,1024]{1,0:T(8,128)(2,1)S(1)}, bf16[64,1024]{1,0:T(8,128)(2,1)S(1)}, u32[]{:S(2)}, u32[]{:S(2)}) collective-permute-start(bf16[64,1024]{1,0:T(8,128)(2,1)S(1)} %get-tuple-element.15), channel_id=1, source_target_pairs={{0,10},{2,8},{4,14},{6,12},{8,2},{10,0},{12,6},{14,4},{1,11},{3,9}... | collective-permute-start | bytes 393224 | tf_op jit(solution)/shard_map/ppermute | solution.py:156
  7.8 3.6 %collective-permute-start.2 = (bf16[64,1024]{1,0:T(8,128)(2,1)S(1)}, bf16[64,1024]{1,0:T(8,128)(2,1)S(1)}, u32[]{:S(2)}, u32[]{:S(2)}) collective-permute-start(bf16[64,1024]{1,0:T(8,128)(2,1)S(1)} %get-tuple-element.16), channel_id=1, source_target_pairs={{0,12},{2,14},{4,8},{6,10},{8,4},{10,6},{12,0},{14,2},{1,13},{3,15... | collective-permute-start | bytes 393224 | tf_op jit(solution)/shard_map/ppermute | solution.py:156
  11.4 10.8 %collective-permute-done.refs_0_ = bf16[64,1024]{1,0:T(8,128)(2,1)S(1)} collective-permute-done((bf16[64,1024]{1,0:T(8,128)(2,1)S(1)}, bf16[64,1024]{1,0:T(8,128)(2,1)S(1)}, u32[]{:S(2)}, u32[]{:S(2)}) %collective-permute-start) | collective-permute-done | bytes 131104 | tf_op jit(solution)/shard_map/ppermute | solution.py:156
  22.2 0.9 %collective-permute-start.5 = (bf16[64,1024]{1,0:T(8,128)(2,1)S(1)}, bf16[64,1024]{1,0:T(8,128)(2,1)S(1)}, u32[]{:S(2)}, u32[]{:S(2)}) collective-permute-start(bf16[64,1024]{1,0:T(8,128)(2,1)S(1)} %get-tuple-element.19), channel_id=1, source_target_pairs={{0,6},{2,4},{4,2},{6,0},{8,14},{10,12},{12,10},{14,8},{1,7},{3,5},... | collective-permute-start | bytes 393224 | tf_op jit(solution)/shard_map/ppermute | solution.py:156
  23.0 3.2 %collective-permute-done.1.refs_1_ = bf16[64,1024]{1,0:T(8,128)(2,1)S(1)} collective-permute-done((bf16[64,1024]{1,0:T(8,128)(2,1)S(1)}, bf16[64,1024]{1,0:T(8,128)(2,1)S(1)}, u32[]{:S(2)}, u32[]{:S(2)}) %collective-permute-start.1) | collective-permute-done | bytes 131104 | tf_op jit(solution)/shard_map/ppermute | solution.py:156
  26.2 0.2 collective-permute-start.6
  26.4 0.0 collective-permute-done.2.refs_2_
  26.4 0.0 collective-permute-start.13
  26.4 0.0 collective-permute-done.3.refs_3_
  26.4 0.5 %collective-permute-start.7 = (bf16[64,1024]{1,0:T(8,128)(2,1)S(1)}, bf16[64,1024]{1,0:T(8,128)(2,1)S(1)}, u32[]{:S(2)}, u32[]{:S(2)}) collective-permute-start(bf16[64,1024]{1,0:T(8,128)(2,1)S(1)} %collective-permute-done.refs_0_), channel_id=1, source_target_pairs={{0,1},{1,0},{2,3},{3,2},{4,5},{5,4},{6,7},{7,6},{8,9},{9,8},{10,11... | collective-permute-start | bytes 393224 | tf_op jit(solution)/shard_map/ppermute | solution.py:145
  26.9 0.1 collective-permute-start.8
  27.0 2.7 %collective-permute-done.5.refs_5_ = bf16[64,1024]{1,0:T(8,128)(2,1)S(1)} collective-permute-done((bf16[64,1024]{1,0:T(8,128)(2,1)S(1)}, bf16[64,1024]{1,0:T(8,128)(2,1)S(1)}, u32[]{:S(2)}, u32[]{:S(2)}) %collective-permute-start.5) | collective-permute-done | bytes 131104 | tf_op jit(solution)/shard_map/ppermute | solution.py:156
  29.7 0.0 collective-permute-start.9
  29.7 2.0 %collective-permute-done.6.refs_7_ = bf16[64,1024]{1,0:T(8,128)(2,1)S(1)} collective-permute-done((bf16[64,1024]{1,0:T(8,128)(2,1)S(1)}, bf16[64,1024]{1,0:T(8,128)(2,1)S(1)}, u32[]{:S(2)}, u32[]{:S(2)}) %collective-permute-start.6) | collective-permute-done | bytes 131104 | tf_op jit(solution)/shard_map/ppermute | solution.py:156
  31.7 0.0 collective-permute-start.10
  31.7 0.0 collective-permute-done.13.refs_14_
  31.7 0.5 %collective-permute-start.11 = (bf16[64,1024]{1,0:T(8,128)(2,1)S(1)}, bf16[64,1024]{1,0:T(8,128)(2,1)S(1)}, u32[]{:S(2)}, u32[]{:S(2)}) collective-permute-start(bf16[64,1024]{1,0:T(8,128)(2,1)S(1)} %collective-permute-done.4.refs_4_), channel_id=1, source_target_pairs={{0,1},{1,0},{2,3},{3,2},{4,5},{5,4},{6,7},{7,6},{8,9},{9,8},{10,11... | collective-permute-start | bytes 393224 | tf_op jit(solution)/shard_map/ppermute | solution.py:145
  32.3 0.0 collective-permute-done.7.refs_8_
  32.3 0.1 collective-permute-start.12
  32.3 0.0 collective-permute-done.8.refs_9_
  32.3 0.4 collective-permute-start.14
  32.8 0.3 collective-permute-done.10.refs_11_
  33.1 0.2 collective-permute-done.11.refs_12_
  33.3 0.3 collective-permute-done.12.refs_13_
  33.6 0.2 collective-permute-done.14.refs_15_
  33.8 1.6 %count.1 = f32[8,1,64]{2,1,0:T(1,128)S(1)} custom-call(bf16[64,1024]{1,0:T(8,128)(2,1)S(1)} %collective-permute-done.refs_0_, bf16[64,1024]{1,0:T(8,128)(2,1)S(1)} %collective-permute-done.1.refs_1_, bf16[64,1024]{1,0:T(8,128)(2,1)S(1)} %collective-permute-done.2.refs_2_, bf16[64,1024]{1,0:T(8,128)(2,1)S(1)} %collective-permute-done.3.refs_3_, ...), custom_call_target="tpu_custom_call" | custom-call | tf_op jit(solution)/shard_map/count/pallas_call | solution.py:108
  35.4 12.0 %all_to_all.5.counts_ref = f32[8,1,64]{2,1,0:T(1,128)S(1)} all-to-all(f32[8,1,64]{2,1,0:T(1,128)S(1)} %count.1), channel_id=1, replica_groups=mesh['groups'=2,'owner'=4,'helper'=2,'sub'=2] {'owner','helper'}, dimensions={0} | all-to-all | bytes 4096 | tf_op jit(solution)/shard_map/all_to_all | solution.py:163
  47.4 0.7 %select.1 = f32[1,256]{1,0:T(1,128)} custom-call(f32[8,1,64]{2,1,0:T(1,128)S(1)} %all_to_all.5.counts_ref, s32[1,256]{1,0:T(1,128)S(1)} %get-tuple-element.22.slot_ref), custom_call_target="tpu_custom_call" | custom-call | tf_op jit(solution)/shard_map/select/pallas_call | solution.py:133
  (6 shorter events, 0.0 us)
Async XLA Ops:
  0.0 0.7 %copy-start.1 = (s32[256]{0:T(256)S(1)}, s32[256]{0:T(256)}, u32[]{:S(2)}) copy-start(s32[256]{0:T(256)} %param.3) | copy-start | bytes 3076
  0.7 1.0 %copy-start = (bf16[256,1024]{1,0:T(8,128)(2,1)S(1)}, bf16[256,1024]{1,0:T(8,128)(2,1)}, u32[]{:S(2)}) copy-start(bf16[256,1024]{1,0:T(8,128)(2,1)} %rows_ref.1) | copy-start | bytes 1572868
  2.4 19.8 %collective-permute-start = (bf16[64,1024]{1,0:T(8,128)(2,1)S(1)}, bf16[64,1024]{1,0:T(8,128)(2,1)S(1)}, u32[]{:S(2)}, u32[]{:S(2)}) collective-permute-start(bf16[64,1024]{1,0:T(8,128)(2,1)S(1)} %get-tuple-element.14), channel_id=1, source_target_pairs={{0,8},{2,10},{4,12},{6,14},{8,0},{10,2},{12,4},{14,6},{1,9},{3,11}... | collective-permute-start | bytes 393224 | tf_op jit(solution)/shard_map/ppermute | solution.py:156
  6.5 19.7 %collective-permute-start.1 = (bf16[64,1024]{1,0:T(8,128)(2,1)S(1)}, bf16[64,1024]{1,0:T(8,128)(2,1)S(1)}, u32[]{:S(2)}, u32[]{:S(2)}) collective-permute-start(bf16[64,1024]{1,0:T(8,128)(2,1)S(1)} %get-tuple-element.15), channel_id=1, source_target_pairs={{0,10},{2,8},{4,14},{6,12},{8,2},{10,0},{12,6},{14,4},{1,11},{3,9}... | collective-permute-start | bytes 393224 | tf_op jit(solution)/shard_map/ppermute | solution.py:156
  7.8 18.6 %collective-permute-start.2 = (bf16[64,1024]{1,0:T(8,128)(2,1)S(1)}, bf16[64,1024]{1,0:T(8,128)(2,1)S(1)}, u32[]{:S(2)}, u32[]{:S(2)}) collective-permute-start(bf16[64,1024]{1,0:T(8,128)(2,1)S(1)} %get-tuple-element.16), channel_id=1, source_target_pairs={{0,12},{2,14},{4,8},{6,10},{8,4},{10,6},{12,0},{14,2},{1,13},{3,15... | collective-permute-start | bytes 393224 | tf_op jit(solution)/shard_map/ppermute | solution.py:156
  11.4 15.0 %collective-permute-start.3 = (bf16[64,1024]{1,0:T(8,128)(2,1)S(1)}, bf16[64,1024]{1,0:T(8,128)(2,1)S(1)}, u32[]{:S(2)}, u32[]{:S(2)}) collective-permute-start(bf16[64,1024]{1,0:T(8,128)(2,1)S(1)} %get-tuple-element.17), channel_id=1, source_target_pairs={{0,14},{2,12},{4,10},{6,8},{8,6},{10,4},{12,2},{14,0},{1,15},{3,13... | collective-permute-start | bytes 393224 | tf_op jit(solution)/shard_map/ppermute | solution.py:156
  11.4 15.5 %collective-permute-start.4 = (bf16[64,1024]{1,0:T(8,128)(2,1)S(1)}, bf16[64,1024]{1,0:T(8,128)(2,1)S(1)}, u32[]{:S(2)}, u32[]{:S(2)}) collective-permute-start(bf16[64,1024]{1,0:T(8,128)(2,1)S(1)} %get-tuple-element.18), channel_id=1, source_target_pairs={{0,4},{2,6},{4,0},{6,2},{8,12},{10,14},{12,8},{14,10},{1,5},{3,7},... | collective-permute-start | bytes 393224 | tf_op jit(solution)/shard_map/ppermute | solution.py:156
  22.2 7.5 %collective-permute-start.5 = (bf16[64,1024]{1,0:T(8,128)(2,1)S(1)}, bf16[64,1024]{1,0:T(8,128)(2,1)S(1)}, u32[]{:S(2)}, u32[]{:S(2)}) collective-permute-start(bf16[64,1024]{1,0:T(8,128)(2,1)S(1)} %get-tuple-element.19), channel_id=1, source_target_pairs={{0,6},{2,4},{4,2},{6,0},{8,14},{10,12},{12,10},{14,8},{1,7},{3,5},... | collective-permute-start | bytes 393224 | tf_op jit(solution)/shard_map/ppermute | solution.py:156
  26.2 5.5 %collective-permute-start.6 = (bf16[64,1024]{1,0:T(8,128)(2,1)S(1)}, bf16[64,1024]{1,0:T(8,128)(2,1)S(1)}, u32[]{:S(2)}, u32[]{:S(2)}) collective-permute-start(bf16[64,1024]{1,0:T(8,128)(2,1)S(1)} %get-tuple-element.21), channel_id=1, source_target_pairs={{0,2},{2,0},{4,6},{6,4},{8,10},{10,8},{12,14},{14,12},{1,3},{3,1},... | collective-permute-start | bytes 393224 | tf_op jit(solution)/shard_map/ppermute | solution.py:156
  26.4 5.4 %collective-permute-start.13 = (bf16[64,1024]{1,0:T(8,128)(2,1)S(1)}, bf16[64,1024]{1,0:T(8,128)(2,1)S(1)}, u32[]{:S(2)}, u32[]{:S(2)}) collective-permute-start(bf16[64,1024]{1,0:T(8,128)(2,1)S(1)} %get-tuple-element.20.refs_6_), channel_id=1, source_target_pairs={{0,1},{1,0},{2,3},{3,2},{4,5},{5,4},{6,7},{7,6},{8,9},{9,8},{10,11... | collective-permute-start | bytes 393224 | tf_op jit(solution)/shard_map/ppermute | solution.py:145
  26.4 5.9 %collective-permute-start.7 = (bf16[64,1024]{1,0:T(8,128)(2,1)S(1)}, bf16[64,1024]{1,0:T(8,128)(2,1)S(1)}, u32[]{:S(2)}, u32[]{:S(2)}) collective-permute-start(bf16[64,1024]{1,0:T(8,128)(2,1)S(1)} %collective-permute-done.refs_0_), channel_id=1, source_target_pairs={{0,1},{1,0},{2,3},{3,2},{4,5},{5,4},{6,7},{7,6},{8,9},{9,8},{10,11... | collective-permute-start | bytes 393224 | tf_op jit(solution)/shard_map/ppermute | solution.py:145
  26.9 5.4 %collective-permute-start.8 = (bf16[64,1024]{1,0:T(8,128)(2,1)S(1)}, bf16[64,1024]{1,0:T(8,128)(2,1)S(1)}, u32[]{:S(2)}, u32[]{:S(2)}) collective-permute-start(bf16[64,1024]{1,0:T(8,128)(2,1)S(1)} %collective-permute-done.1.refs_1_), channel_id=1, source_target_pairs={{0,1},{1,0},{2,3},{3,2},{4,5},{5,4},{6,7},{7,6},{8,9},{9,8},{10,11... | collective-permute-start | bytes 393224 | tf_op jit(solution)/shard_map/ppermute | solution.py:145
  29.7 3.1 %collective-permute-start.9 = (bf16[64,1024]{1,0:T(8,128)(2,1)S(1)}, bf16[64,1024]{1,0:T(8,128)(2,1)S(1)}, u32[]{:S(2)}, u32[]{:S(2)}) collective-permute-start(bf16[64,1024]{1,0:T(8,128)(2,1)S(1)} %collective-permute-done.2.refs_2_), channel_id=1, source_target_pairs={{0,1},{1,0},{2,3},{3,2},{4,5},{5,4},{6,7},{7,6},{8,9},{9,8},{10,11... | collective-permute-start | bytes 393224 | tf_op jit(solution)/shard_map/ppermute | solution.py:145
  31.7 1.3 %collective-permute-start.10 = (bf16[64,1024]{1,0:T(8,128)(2,1)S(1)}, bf16[64,1024]{1,0:T(8,128)(2,1)S(1)}, u32[]{:S(2)}, u32[]{:S(2)}) collective-permute-start(bf16[64,1024]{1,0:T(8,128)(2,1)S(1)} %collective-permute-done.3.refs_3_), channel_id=1, source_target_pairs={{0,1},{1,0},{2,3},{3,2},{4,5},{5,4},{6,7},{7,6},{8,9},{9,8},{10,11... | collective-permute-start | bytes 393224 | tf_op jit(solution)/shard_map/ppermute | solution.py:145
  31.7 1.5 %collective-permute-start.11 = (bf16[64,1024]{1,0:T(8,128)(2,1)S(1)}, bf16[64,1024]{1,0:T(8,128)(2,1)S(1)}, u32[]{:S(2)}, u32[]{:S(2)}) collective-permute-start(bf16[64,1024]{1,0:T(8,128)(2,1)S(1)} %collective-permute-done.4.refs_4_), channel_id=1, source_target_pairs={{0,1},{1,0},{2,3},{3,2},{4,5},{5,4},{6,7},{7,6},{8,9},{9,8},{10,11... | collective-permute-start | bytes 393224 | tf_op jit(solution)/shard_map/ppermute | solution.py:145
  32.3 1.3 %collective-permute-start.12 = (bf16[64,1024]{1,0:T(8,128)(2,1)S(1)}, bf16[64,1024]{1,0:T(8,128)(2,1)S(1)}, u32[]{:S(2)}, u32[]{:S(2)}) collective-permute-start(bf16[64,1024]{1,0:T(8,128)(2,1)S(1)} %collective-permute-done.5.refs_5_), channel_id=1, source_target_pairs={{0,1},{1,0},{2,3},{3,2},{4,5},{5,4},{6,7},{7,6},{8,9},{9,8},{10,11... | collective-permute-start | bytes 393224 | tf_op jit(solution)/shard_map/ppermute | solution.py:145
  32.3 1.5 %collective-permute-start.14 = (bf16[64,1024]{1,0:T(8,128)(2,1)S(1)}, bf16[64,1024]{1,0:T(8,128)(2,1)S(1)}, u32[]{:S(2)}, u32[]{:S(2)}) collective-permute-start(bf16[64,1024]{1,0:T(8,128)(2,1)S(1)} %collective-permute-done.6.refs_7_), channel_id=1, source_target_pairs={{0,1},{1,0},{2,3},{3,2},{4,5},{5,4},{6,7},{7,6},{8,9},{9,8},{10,11... | collective-permute-start | bytes 393224 | tf_op jit(solution)/shard_map/ppermute | solution.py:145

commit v3 on v2

v3 whole, which is shorter than its diff:
```python
import functools
import math

import jax
import jax.numpy as jnp
from jax import lax
from jax.experimental import pallas as pl
from jax.experimental.pallas import tpu as pltpu
from jax.sharding import PartitionSpec as P

CL_OWN = 2

epsilon = 1e-06
threshold = 0.8
sharpness = 0.05

EMPTY = 4.0
TILE = 256
VMEM = pl.BlockSpec(memory_space=pltpu.VMEM)


def chip_index():
    return lax.axis_index("owner") * CL_OWN + lax.axis_index("helper")


def unit_rows_of(rows_ref):
    widened = rows_ref[...].astype(jnp.float32)
    factor = lax.rsqrt(
        jnp.mean(widened * widened, axis=-1, keepdims=True) + epsilon
    ) * rows_ref.shape[1] ** (-0.5)
    return (widened * factor).astype(jnp.bfloat16)


def slots_of(ids, clusters, capacity):
    doc_count = ids.shape[1]
    member = lax.broadcasted_iota(jnp.int32, (clusters, doc_count), 0) == ids
    earlier = lax.broadcasted_iota(jnp.int32, (doc_count, doc_count), 0) < (
        lax.broadcasted_iota(jnp.int32, (doc_count, doc_count), 1)
    )
    ahead = jnp.dot(
        member.astype(jnp.bfloat16), earlier.astype(jnp.bfloat16), preferred_element_type=jnp.float32
    )
    rank = jnp.sum(jnp.where(member, ahead, 0.0), axis=0, keepdims=True).astype(jnp.int32)
    return ids * capacity + rank


def lay(unit_rows, slot, slots):
    doc_count, feature_count = unit_rows.shape
    dispatch = lax.broadcasted_iota(jnp.int32, (slots, doc_count), 0) == slot
    filled = jnp.sum(dispatch.astype(jnp.float32), axis=1, keepdims=True) > 0
    dispatch = dispatch.astype(jnp.bfloat16)
    for column in range(0, feature_count, TILE):
        columns = slice(column, column + TILE)
        laid = jnp.dot(dispatch, unit_rows[:, columns], preferred_element_type=jnp.float32)
        if column == 0:
            lane = lax.broadcasted_iota(jnp.int32, (slots, TILE), 1)
            laid = jnp.where(filled | (lane > 0), laid, EMPTY)
        yield columns, laid.astype(jnp.bfloat16)


def route_chip_kernel(clusters, capacity, *refs):
    own_rows, other_rows, own_ids, other_ids, *piece_refs, slot_ref = refs
    core = lax.axis_index("sub")
    for part, (rows_ref, ids_ref) in enumerate(((own_rows, own_ids), (other_rows, other_ids))):
        slot = slots_of(ids_ref[...], clusters, capacity)
        if part == 0:
            slot_ref[...] = slot
        ids = ids_ref[...]
        rank = slot - ids * capacity
        distance = ids ^ chip_index()
        here = jnp.where((distance & 1) == core, (distance >> 1) * capacity + rank, -1)
        rows = slice(part * capacity, (part + 1) * capacity)
        for columns, laid in lay(unit_rows_of(rows_ref), here, len(piece_refs) * capacity):
            for p, piece in enumerate(piece_refs):
                piece[rows, columns] = laid[p * capacity : (p + 1) * capacity]


def route_kernel(clusters, capacity, rows_ref, ids_ref, piece_ref, slot_ref):
    slot = slots_of(ids_ref[...], clusters, capacity)
    slot_ref[...] = slot
    for columns, laid in lay(unit_rows_of(rows_ref), slot, piece_ref.shape[0]):
        piece_ref[:, columns] = laid


def call_kernel(name, kernel, out_shape, *args, limit=32):
    return pl.pallas_call(
        kernel,
        out_shape=out_shape,
        in_specs=[VMEM] * len(args),
        out_specs=jax.tree.map(lambda _: VMEM, out_shape),
        compiler_params=pltpu.CompilerParams(vmem_limit_bytes=limit * 2**20),
        name=name,
    )(*args)


def count_kernel(starts, places, *refs):
    *piece_refs, count_ref = refs
    rows = jnp.concatenate([piece[...] for piece in piece_refs], axis=0)
    size = count_ref.shape[2]
    own = jnp.concatenate([rows[start : start + size] for start in starts], axis=0)
    column = lax.broadcasted_iota(jnp.int32, (1, own.shape[0]), 1)
    itself = column
    for k, start in enumerate(starts):
        itself = jnp.where(column // size == k, column + (start - k * size), itself)
    slope = -math.log2(math.e) / sharpness
    total = jnp.zeros((1, own.shape[0]), jnp.float32)
    for first in range(0, rows.shape[0], TILE):
        other = rows[first : first + TILE]
        scores = lax.dot_general(
            other, own, (((1,), (1,)), ((), ())), preferred_element_type=jnp.float32
        )
        weights = 1.0 / (1.0 + jnp.exp2(scores * slope - threshold * slope))
        live = other[:, :1].astype(jnp.float32) < 0.5 * EMPTY
        keep = live & (lax.broadcasted_iota(jnp.int32, scores.shape, 0) + first != itself)
        total = total + jnp.sum(jnp.where(keep, weights, 0.0), axis=0, keepdims=True)
    for k, place in enumerate(places()):
        count_ref[pl.ds(place, 1), 0, :] = total[:, k * size : (k + 1) * size]


def soft_counts(pieces, size, starts, places):
    out_shape = jax.ShapeDtypeStruct((len(starts), 1, size), jnp.float32)
    return call_kernel("count", functools.partial(count_kernel, starts, places), out_shape, *pieces)


def select_kernel(capacity, counts_ref, slot_ref, out_ref):
    counts = counts_ref[:, 0, :]
    slot = slot_ref[...]
    doc_count = slot.shape[1]
    block = slot // capacity
    rank = slot - block * capacity
    hot = (lax.broadcasted_iota(jnp.int32, (capacity, doc_count), 0) == rank).astype(jnp.float32)
    by_block = jnp.dot(
        counts, hot, precision=lax.Precision.HIGHEST, preferred_element_type=jnp.float32
    )
    chosen = lax.broadcasted_iota(jnp.int32, by_block.shape, 0) == block
    out_ref[...] = jnp.sum(jnp.where(chosen, by_block, 0.0), axis=0, keepdims=True)


def select(counts, slot, capacity):
    out_shape = jax.ShapeDtypeStruct(slot.shape, jnp.float32)
    kernel = functools.partial(select_kernel, capacity)
    return call_kernel("select", kernel, out_shape, counts, slot, limit=8)[0]


def swap_cores(x):
    cores = lax.axis_size("sub")
    return lax.ppermute(x, "sub", [(i, i ^ 1) for i in range(cores)])


def body_by_chip(embeddings, cluster_id):
    doc_count, feature_count = embeddings.shape
    clusters = CL_OWN * lax.axis_size("owner")
    capacity = 2 * doc_count // clusters
    cores = lax.axis_size("sub")
    steps = clusters // cores

    def across(x, p):
        pairs = [
            (chip * cores + core, (chip ^ (p * cores + core)) * cores + core)
            for chip in range(clusters)
            for core in range(cores)
        ]
        return lax.ppermute(x, ("owner", "helper", "sub"), pairs)

    ids = cluster_id.reshape(1, doc_count)
    piece = jax.ShapeDtypeStruct((cores * capacity, feature_count), jnp.bfloat16)
    *pieces, slot = call_kernel(
        "route",
        functools.partial(route_chip_kernel, clusters, capacity),
        [piece] * steps + [jax.ShapeDtypeStruct((1, doc_count), jnp.int32)],
        embeddings,
        swap_cores(embeddings),
        ids,
        swap_cores(ids),
    )
    order = [steps // 2, *range(steps // 2), *range(steps // 2 + 1, steps)]
    arrived = [across(pieces[p], p) for p in order]
    swapped = [swap_cores(x) for x in arrived]

    def places():
        chip, core = chip_index(), lax.axis_index("sub")
        return [chip ^ (p * cores + core) for p in order] + [
            chip ^ (p * cores + 1 - core) for p in order
        ]

    span = cores * capacity
    starts = [k * span for k in range(steps)] + [k * span + capacity for k in range(steps, 2 * steps)]
    counts = soft_counts(arrived + swapped, capacity, starts, places)
    back = lax.all_to_all(counts, ("owner", "helper"), split_axis=0, concat_axis=0, tiled=True)
    return select(back, slot, capacity)


def body_by_owner(embeddings, cluster_id):
    doc_count, feature_count = embeddings.shape
    owners, helpers = lax.axis_size("owner"), lax.axis_size("helper")
    clusters = CL_OWN * owners
    capacity = 2 * doc_count // clusters
    mine = lax.axis_index("helper") % CL_OWN

    def partner(x):
        return lax.ppermute(x, "helper", [(i, i ^ 1) for i in range(helpers)])

    outgoing, slot = call_kernel(
        "route",
        functools.partial(route_kernel, clusters, capacity),
        [
            jax.ShapeDtypeStruct((clusters * capacity, feature_count), jnp.bfloat16),
            jax.ShapeDtypeStruct((1, doc_count), jnp.int32),
        ],
        embeddings,
        cluster_id.reshape(1, doc_count),
    )
    outgoing = outgoing.reshape(owners, CL_OWN, capacity, feature_count)
    arrived = lax.all_to_all(outgoing, "owner", split_axis=0, concat_axis=0, tiled=True)
    kept = lax.dynamic_index_in_dim(arrived, mine, 1, keepdims=False)
    given = partner(lax.dynamic_index_in_dim(arrived, 1 - mine, 1, keepdims=False))
    own = jnp.stack([kept, given]).reshape(CL_OWN * owners * capacity, feature_count)
    others = [swap_cores(own)]
    for step in range(CL_OWN, helpers, CL_OWN):
        turn = [(i, (i + step) % helpers) for i in range(helpers)]
        others += [lax.ppermute(x, "helper", turn) for x in (own, others[0])]
    counts = soft_counts([own, *others], own.shape[0], [0], lambda: [0])
    counts = counts.reshape(CL_OWN, owners, capacity)
    kept, given = counts[0], partner(counts[1])
    counts = jnp.where(mine == 0, jnp.stack([kept, given], 1), jnp.stack([given, kept], 1))
    back = lax.all_to_all(counts, "owner", split_axis=0, concat_axis=0, tiled=True)
    return select(back.reshape(clusters, 1, capacity), slot, capacity)


def solution(mesh):
    in_specs = (
        P(("groups", "owner", "helper", "sub"), None),
        P(("groups", "owner", "helper", "sub")),
    )
    out_specs = P(("groups", "owner", "helper", "sub"))
    body = body_by_chip if mesh.shape["helper"] == CL_OWN else body_by_owner
    return jax.shard_map(body, mesh=mesh, in_specs=in_specs, out_specs=out_specs, check_vma=False)
```

time: 48.3 us -> 47.3 us (0.979)
  waiting for transfers between devices: 19.7 us -> 12.8 us
  starting transfers between devices: 11.6 us -> 15.5 us
  blocking collectives: 12 us -> 14.1 us
    ppermute x7 -> x4, waiting for transfers between devices: 18.7 us -> 10.2 us  [across(): return lax.ppermute(x, ('owner', 'helper', 'sub'), pairs)]
    ppermute x8 -> x6, starting transfers between devices: 1.6 us -> 9.13 us  [swap_cores(): return lax.ppermute(x, 'sub', [(i, i ^ 1) for i in range(cores)])]
    ppermute x7 -> x4, starting transfers between devices: 10 us -> 6.33 us  [across(): return lax.ppermute(x, ('owner', 'helper', 'sub'), pairs)]
    all_to_all x1, blocking collectives: 12 us -> 14.1 us  [body_by_chip(): lax.all_to_all(counts, ('owner', 'helper'), split_axis=0, concat_axis=0,...]
    ppermute x8 -> x6, waiting for transfers between devices: 1.03 us -> 2.59 us  [swap_cores(): return lax.ppermute(x, 'sub', [(i, i ^ 1) for i in range(cores)])]
  transfers between devices with their start and end apart: 15 -> 10, of which waited for: 8 -> 5; matrix products, arithmetic and copies ran while one was open for 0% -> 0% of each run, Pallas kernels for 0% -> 0%
where the time goes in v3:
time: 47.3 us; the launch traced here: 47.1 us
  starting transfers between devices  15.5 us (33%)
  blocking collectives  14.1 us (30%)
  waiting for transfers between devices  12.8 us (27%)
  Pallas kernels  3.45 us (7%)
  local copies, waits for them, and re-layouts  1.27 us (3%)
    all_to_all x1, blocking collectives, body_by_chip(): lax.all_to_all(counts, ('owner', 'helper'), split_axis=0, concat_axis=0,...  14.1 us
    ppermute x4, waiting for transfers between devices, across(): return lax.ppermute(x, ('owner', 'helper', 'sub'), pairs)  10.2 us
    ppermute x6, starting transfers between devices, swap_cores(): return lax.ppermute(x, 'sub', [(i, i ^ 1) for i in range(cores)])  9.13 us
    ppermute x4, starting transfers between devices, across(): return lax.ppermute(x, ('owner', 'helper', 'sub'), pairs)  6.33 us
    pallas_call x3, Pallas kernels, call_kernel(): pl.pallas_call(kernel, out_shape=out_shape, in_specs=[VMEM] * len(args),...  3.45 us
    ppermute x6, waiting for transfers between devices, swap_cores(): return lax.ppermute(x, 'sub', [(i, i ^ 1) for i in range(cores)])  2.59 us
    unnamed x4, local copies, waits for them, and re-layouts  1.27 us
  transfers between devices with their start and end apart: 10, of which 5 were waited for; matrix products, arithmetic and copies ran while one was open for 0% of the time, Pallas kernels for 0%

profile of v3, /device:TPU:0, one launch (start us, length us, event | category | flops | bytes accessed | tf_op | source)
XLA Modules:
  0.0 47.1 jit_solution(5837066572016113840)
XLA Ops:
  0.0 0.0 copy-start.1
  0.0 0.5 collective-permute-start
  0.5 0.2 copy-done.1
  0.7 0.5 collective-permute-start.1
  1.1 0.9 %collective-permute-done.1.refs_3_ = s32[1,256]{1,0:T(1,128)S(1)} collective-permute-done((s32[1,256]{1,0:T(1,128)S(1)}, s32[1,256]{1,0:T(1,128)S(1)}, u32[]{:S(2)}, u32[]{:S(2)}) %collective-permute-start.1) | collective-permute-done | bytes 1056 | tf_op jit(solution)/shard_map/ppermute | solution.py:147
  2.0 0.2 collective-permute-done.refs_1_
  2.2 0.0 copy-start
  2.2 1.0 %copy-done = bf16[256,1024]{1,0:T(8,128)(2,1)S(1)} copy-done((bf16[256,1024]{1,0:T(8,128)(2,1)S(1)}, bf16[256,1024]{1,0:T(8,128)(2,1)}, u32[]{:S(2)}) %copy-start) | copy-done | bytes 524312
  3.2 0.9 %route.1 = (bf16[128,1024]{1,0:T(8,128)(2,1)S(1)}, bf16[128,1024]{1,0:T(8,128)(2,1)S(1)}, bf16[128,1024]{1,0:T(8,128)(2,1)S(1)}, bf16[128,1024]{1,0:T(8,128)(2,1)S(1)}, s32[1,256]{1,0:T(1,128)S(1)}) custom-call(bf16[256,1024]{1,0:T(8,128)(2,1)S(1)} %copy-done, bf16[256,1024]{1,0:T(8,128)(2,1)S(1)} %collective-permute-done.refs_1_, s32[1,256]{1,0:T(1,128)S(1)} %bitcast.3, ...), custom_call_target="tpu_custom_call" | custom-call | tf_op jit(solution)/shard_map/route/pallas_call | solution.py:86
  4.2 4.0 %collective-permute-start.2 = (bf16[128,1024]{1,0:T(8,128)(2,1)S(1)}, bf16[128,1024]{1,0:T(8,128)(2,1)S(1)}, u32[]{:S(2)}, u32[]{:S(2)}) collective-permute-start(bf16[128,1024]{1,0:T(8,128)(2,1)S(1)} %get-tuple-element.10), channel_id=1, source_target_pairs={{0,8},{1,11},{2,10},{3,9},{4,12},{5,15},{6,14},{7,13},{8,0},{9,3},... | collective-permute-start | bytes 786440 | tf_op jit(solution)/shard_map/ppermute | solution.py:163
  8.2 0.7 %collective-permute-start.3 = (bf16[128,1024]{1,0:T(8,128)(2,1)S(1)}, bf16[128,1024]{1,0:T(8,128)(2,1)S(1)}, u32[]{:S(2)}, u32[]{:S(2)}) collective-permute-start(bf16[128,1024]{1,0:T(8,128)(2,1)S(1)} %get-tuple-element.11), channel_id=1, source_target_pairs={{0,0},{1,3},{2,2},{3,1},{4,4},{5,7},{6,6},{7,5},{8,8},{9,11},{10,1... | collective-permute-start | bytes 786440 | tf_op jit(solution)/shard_map/ppermute | solution.py:163
  8.8 1.6 %collective-permute-start.4 = (bf16[128,1024]{1,0:T(8,128)(2,1)S(1)}, bf16[128,1024]{1,0:T(8,128)(2,1)S(1)}, u32[]{:S(2)}, u32[]{:S(2)}) collective-permute-start(bf16[128,1024]{1,0:T(8,128)(2,1)S(1)} %get-tuple-element.12), channel_id=1, source_target_pairs={{0,4},{1,7},{2,6},{3,5},{4,0},{5,3},{6,2},{7,1},{8,12},{9,15},{10,... | collective-permute-start | bytes 786440 | tf_op jit(solution)/shard_map/ppermute | solution.py:163
  10.5 0.0 collective-permute-start.5
  10.5 10.2 %collective-permute-done.2.refs_0_ = bf16[128,1024]{1,0:T(8,128)(2,1)S(1)} collective-permute-done((bf16[128,1024]{1,0:T(8,128)(2,1)S(1)}, bf16[128,1024]{1,0:T(8,128)(2,1)S(1)}, u32[]{:S(2)}, u32[]{:S(2)}) %collective-permute-start.2) | collective-permute-done | bytes 262176 | tf_op jit(solution)/shard_map/ppermute | solution.py:163
  20.7 0.0 collective-permute-start.6
  20.7 0.0 collective-permute-done.3.refs_1_
  20.7 0.5 %collective-permute-start.7 = (bf16[128,1024]{1,0:T(8,128)(2,1)S(1)}, bf16[128,1024]{1,0:T(8,128)(2,1)S(1)}, u32[]{:S(2)}, u32[]{:S(2)}) collective-permute-start(bf16[128,1024]{1,0:T(8,128)(2,1)S(1)} %collective-permute-done.3.refs_1_), channel_id=1, source_target_pairs={{0,1},{1,0},{2,3},{3,2},{4,5},{5,4},{6,7},{7,6},{8,9},{9,8},{10,11... | collective-permute-start | bytes 786440 | tf_op jit(solution)/shard_map/ppermute | solution.py:147
  21.2 0.0 collective-permute-done.4.refs_2_
  21.2 7.7 %collective-permute-start.8 = (bf16[128,1024]{1,0:T(8,128)(2,1)S(1)}, bf16[128,1024]{1,0:T(8,128)(2,1)S(1)}, u32[]{:S(2)}, u32[]{:S(2)}) collective-permute-start(bf16[128,1024]{1,0:T(8,128)(2,1)S(1)} %collective-permute-done.4.refs_2_), channel_id=1, source_target_pairs={{0,1},{1,0},{2,3},{3,2},{4,5},{5,4},{6,7},{7,6},{8,9},{9,8},{10,11... | collective-permute-start | bytes 786440 | tf_op jit(solution)/shard_map/ppermute | solution.py:147
  28.9 0.0 collective-permute-done.5.refs_3_
  28.9 0.0 collective-permute-start.9
  28.9 0.0 collective-permute-done.6.refs_4_
  29.0 0.0 collective-permute-done.7.refs_5_
  29.0 1.1 %collective-permute-done.8.refs_6_ = bf16[128,1024]{1,0:T(8,128)(2,1)S(1)} collective-permute-done((bf16[128,1024]{1,0:T(8,128)(2,1)S(1)}, bf16[128,1024]{1,0:T(8,128)(2,1)S(1)}, u32[]{:S(2)}, u32[]{:S(2)}) %collective-permute-start.8) | collective-permute-done | bytes 262176 | tf_op jit(solution)/shard_map/ppermute | solution.py:147
  30.1 0.4 collective-permute-done.9.refs_7_
  30.5 1.8 %count.1 = f32[8,1,64]{2,1,0:T(1,128)S(1)} custom-call(bf16[128,1024]{1,0:T(8,128)(2,1)S(1)} %collective-permute-done.2.refs_0_, bf16[128,1024]{1,0:T(8,128)(2,1)S(1)} %collective-permute-done.3.refs_1_, bf16[128,1024]{1,0:T(8,128)(2,1)S(1)} %collective-permute-done.4.refs_2_, bf16[128,1024]{1,0:T(8,128)(2,1)S(1)} %collective-permute-done.5.refs_3_, ...), custom_call_target="tpu_custom_call" | custom-call | tf_op jit(solution)/shard_map/count/pallas_call | solution.py:86
  32.3 14.1 %all_to_all.5.counts_ref = f32[8,1,64]{2,1,0:T(1,128)S(1)} all-to-all(f32[8,1,64]{2,1,0:T(1,128)S(1)} %count.1), channel_id=1, replica_groups=mesh['groups'=2,'owner'=4,'helper'=2,'sub'=2] {'owner','helper'}, dimensions={0} | all-to-all | bytes 4096 | tf_op jit(solution)/shard_map/all_to_all | solution.py:189
  46.4 0.7 %select.1 = f32[1,256]{1,0:T(1,128)} custom-call(f32[8,1,64]{2,1,0:T(1,128)S(1)} %all_to_all.5.counts_ref, s32[1,256]{1,0:T(1,128)S(1)} %get-tuple-element.14.slot_ref), custom_call_target="tpu_custom_call" | custom-call | tf_op jit(solution)/shard_map/select/pallas_call | solution.py:86
Async XLA Ops:
  0.0 0.7 %copy-start.1 = (s32[256]{0:T(256)S(1)}, s32[256]{0:T(256)}, u32[]{:S(2)}) copy-start(s32[256]{0:T(256)} %param.3) | copy-start | bytes 3076
  0.0 2.2 %collective-permute-start = (bf16[256,1024]{1,0:T(8,128)(2,1)}, bf16[256,1024]{1,0:T(8,128)(2,1)S(1)}, u32[]{:S(2)}, u32[]{:S(2)}) collective-permute-start(bf16[256,1024]{1,0:T(8,128)(2,1)} %refs_0_.1), channel_id=1, source_target_pairs={{0,1},{1,0},{2,3},{3,2},{4,5},{5,4},{6,7},{7,6},{8,9},{9,8},{10,11... | collective-permute-start | bytes 1572872 | tf_op jit(solution)/shard_map/ppermute | solution.py:147
  0.7 1.3 %collective-permute-start.1 = (s32[1,256]{1,0:T(1,128)S(1)}, s32[1,256]{1,0:T(1,128)S(1)}, u32[]{:S(2)}, u32[]{:S(2)}) collective-permute-start(s32[1,256]{1,0:T(1,128)S(1)} %bitcast.2), channel_id=1, source_target_pairs={{0,1},{1,0},{2,3},{3,2},{4,5},{5,4},{6,7},{7,6},{8,9},{9,8},{10,11... | collective-permute-start | bytes 3080 | tf_op jit(solution)/shard_map/ppermute | solution.py:147
  2.2 1.0 %copy-start = (bf16[256,1024]{1,0:T(8,128)(2,1)S(1)}, bf16[256,1024]{1,0:T(8,128)(2,1)}, u32[]{:S(2)}) copy-start(bf16[256,1024]{1,0:T(8,128)(2,1)} %refs_0_.1) | copy-start | bytes 1572868
  4.2 16.6 %collective-permute-start.2 = (bf16[128,1024]{1,0:T(8,128)(2,1)S(1)}, bf16[128,1024]{1,0:T(8,128)(2,1)S(1)}, u32[]{:S(2)}, u32[]{:S(2)}) collective-permute-start(bf16[128,1024]{1,0:T(8,128)(2,1)S(1)} %get-tuple-element.10), channel_id=1, source_target_pairs={{0,8},{1,11},{2,10},{3,9},{4,12},{5,15},{6,14},{7,13},{8,0},{9,3},... | collective-permute-start | bytes 786440 | tf_op jit(solution)/shard_map/ppermute | solution.py:163
  8.2 12.5 %collective-permute-start.3 = (bf16[128,1024]{1,0:T(8,128)(2,1)S(1)}, bf16[128,1024]{1,0:T(8,128)(2,1)S(1)}, u32[]{:S(2)}, u32[]{:S(2)}) collective-permute-start(bf16[128,1024]{1,0:T(8,128)(2,1)S(1)} %get-tuple-element.11), channel_id=1, source_target_pairs={{0,0},{1,3},{2,2},{3,1},{4,4},{5,7},{6,6},{7,5},{8,8},{9,11},{10,1... | collective-permute-start | bytes 786440 | tf_op jit(solution)/shard_map/ppermute | solution.py:163
  8.8 12.4 %collective-permute-start.4 = (bf16[128,1024]{1,0:T(8,128)(2,1)S(1)}, bf16[128,1024]{1,0:T(8,128)(2,1)S(1)}, u32[]{:S(2)}, u32[]{:S(2)}) collective-permute-start(bf16[128,1024]{1,0:T(8,128)(2,1)S(1)} %get-tuple-element.12), channel_id=1, source_target_pairs={{0,4},{1,7},{2,6},{3,5},{4,0},{5,3},{6,2},{7,1},{8,12},{9,15},{10,... | collective-permute-start | bytes 786440 | tf_op jit(solution)/shard_map/ppermute | solution.py:163
  10.5 18.5 %collective-permute-start.5 = (bf16[128,1024]{1,0:T(8,128)(2,1)S(1)}, bf16[128,1024]{1,0:T(8,128)(2,1)S(1)}, u32[]{:S(2)}, u32[]{:S(2)}) collective-permute-start(bf16[128,1024]{1,0:T(8,128)(2,1)S(1)} %get-tuple-element.13), channel_id=1, source_target_pairs={{0,12},{1,15},{2,14},{3,13},{4,8},{5,11},{6,10},{7,9},{8,4},{9,7},... | collective-permute-start | bytes 786440 | tf_op jit(solution)/shard_map/ppermute | solution.py:163
  20.7 8.2 %collective-permute-start.6 = (bf16[128,1024]{1,0:T(8,128)(2,1)S(1)}, bf16[128,1024]{1,0:T(8,128)(2,1)S(1)}, u32[]{:S(2)}, u32[]{:S(2)}) collective-permute-start(bf16[128,1024]{1,0:T(8,128)(2,1)S(1)} %collective-permute-done.2.refs_0_), channel_id=1, source_target_pairs={{0,1},{1,0},{2,3},{3,2},{4,5},{5,4},{6,7},{7,6},{8,9},{9,8},{10,11... | collective-permute-start | bytes 786440 | tf_op jit(solution)/shard_map/ppermute | solution.py:147
  20.7 8.2 %collective-permute-start.7 = (bf16[128,1024]{1,0:T(8,128)(2,1)S(1)}, bf16[128,1024]{1,0:T(8,128)(2,1)S(1)}, u32[]{:S(2)}, u32[]{:S(2)}) collective-permute-start(bf16[128,1024]{1,0:T(8,128)(2,1)S(1)} %collective-permute-done.3.refs_1_), channel_id=1, source_target_pairs={{0,1},{1,0},{2,3},{3,2},{4,5},{5,4},{6,7},{7,6},{8,9},{9,8},{10,11... | collective-permute-start | bytes 786440 | tf_op jit(solution)/shard_map/ppermute | solution.py:147
  21.2 8.9 %collective-permute-start.8 = (bf16[128,1024]{1,0:T(8,128)(2,1)S(1)}, bf16[128,1024]{1,0:T(8,128)(2,1)S(1)}, u32[]{:S(2)}, u32[]{:S(2)}) collective-permute-start(bf16[128,1024]{1,0:T(8,128)(2,1)S(1)} %collective-permute-done.4.refs_2_), channel_id=1, source_target_pairs={{0,1},{1,0},{2,3},{3,2},{4,5},{5,4},{6,7},{7,6},{8,9},{9,8},{10,11... | collective-permute-start | bytes 786440 | tf_op jit(solution)/shard_map/ppermute | solution.py:147
  28.9 1.5 %collective-permute-start.9 = (bf16[128,1024]{1,0:T(8,128)(2,1)S(1)}, bf16[128,1024]{1,0:T(8,128)(2,1)S(1)}, u32[]{:S(2)}, u32[]{:S(2)}) collective-permute-start(bf16[128,1024]{1,0:T(8,128)(2,1)S(1)} %collective-permute-done.5.refs_3_), channel_id=1, source_target_pairs={{0,1},{1,0},{2,3},{3,2},{4,5},{5,4},{6,7},{7,6},{8,9},{9,8},{10,11... | collective-permute-start | bytes 786440 | tf_op jit(solution)/shard_map/ppermute | solution.py:147

commit v4 on v3

v4 whole, which is shorter than its diff:
```python
import functools
import math

import jax
import jax.numpy as jnp
from jax import lax
from jax.experimental import pallas as pl
from jax.experimental.pallas import tpu as pltpu
from jax.sharding import PartitionSpec as P

CL_OWN = 2

epsilon = 1e-06
threshold = 0.8
sharpness = 0.05

EMPTY = 4.0
TILE = 256
VMEM = pl.BlockSpec(memory_space=pltpu.VMEM)


def chip_index():
    return lax.axis_index("owner") * CL_OWN + lax.axis_index("helper")


def slots_of(ids, clusters, capacity):
    doc_count = ids.shape[1]
    member = lax.broadcasted_iota(jnp.int32, (clusters, doc_count), 0) == ids
    earlier = lax.broadcasted_iota(jnp.int32, (doc_count, doc_count), 0) < (
        lax.broadcasted_iota(jnp.int32, (doc_count, doc_count), 1)
    )
    ahead = jnp.dot(
        member.astype(jnp.bfloat16), earlier.astype(jnp.bfloat16), preferred_element_type=jnp.float32
    )
    rank = jnp.sum(jnp.where(member, ahead, 0.0), axis=0, keepdims=True).astype(jnp.int32)
    return ids * capacity + rank


def lay(rows_ref, slot, slots):
    doc_count, feature_count = rows_ref.shape
    dispatch = lax.broadcasted_iota(jnp.int32, (slots, doc_count), 0) == slot
    filled = jnp.sum(dispatch.astype(jnp.float32), axis=1, keepdims=True) > 0
    laid = jnp.dot(
        dispatch.astype(jnp.bfloat16), rows_ref[...], preferred_element_type=jnp.float32
    )
    factor = lax.rsqrt(
        jnp.mean(laid * laid, axis=-1, keepdims=True) + epsilon
    ) * feature_count ** (-0.5)
    lane = lax.broadcasted_iota(jnp.int32, laid.shape, 1)
    return jnp.where(filled | (lane > 0), laid * factor, EMPTY).astype(jnp.bfloat16)


def slots_of_steps(slot, capacity, steps):
    cores = lax.axis_size("sub")
    by_distance = slot ^ (chip_index() * capacity)
    distance = by_distance // capacity
    rank = by_distance - distance * capacity
    step = jnp.full_like(slot, -1)
    for place, p in enumerate(steps):
        step = jnp.where(distance == p * cores + lax.axis_index("sub"), place, step)
    return jnp.where(step < 0, -1, step * capacity + rank)


def route_own_kernel(clusters, capacity, rows_ref, ids_ref, laid_ref, slot_ref):
    steps = range(laid_ref.shape[0] // capacity)
    slot = slots_of(ids_ref[...], clusters, capacity)
    slot_ref[...] = slot
    laid_ref[...] = lay(rows_ref, slots_of_steps(slot, capacity, steps), laid_ref.shape[0])


def route_other_kernel(clusters, capacity, rows_ref, ids_ref, laid_ref, *piece_refs):
    slot = slots_of(ids_ref[...], clusters, capacity)
    slot = slots_of_steps(slot, capacity, range(len(piece_refs)))
    laid = lay(rows_ref, slot, laid_ref.shape[0])
    for p, piece in enumerate(piece_refs):
        rows = slice(p * capacity, (p + 1) * capacity)
        piece[:capacity] = laid_ref[rows]
        piece[capacity:] = laid[rows]


def route_kernel(clusters, capacity, rows_ref, ids_ref, piece_ref, slot_ref):
    slot = slots_of(ids_ref[...], clusters, capacity)
    slot_ref[...] = slot
    piece_ref[...] = lay(rows_ref, slot, piece_ref.shape[0])


def call_kernel(name, kernel, out_shape, *args, limit=32 * 2**20):
    return pl.pallas_call(
        kernel,
        out_shape=out_shape,
        in_specs=[VMEM] * len(args),
        out_specs=jax.tree.map(lambda _: VMEM, out_shape),
        compiler_params=pltpu.CompilerParams(vmem_limit_bytes=limit),
        name=name,
    )(*args)


def blocks(rows, starts, size):
    return jnp.concatenate([rows[start : start + size] for start in starts], axis=0)


def count_against(rows, own, starts, size):
    column = lax.broadcasted_iota(jnp.int32, (1, own.shape[0]), 1)
    itself = jnp.full_like(column, -1)
    for k, start in enumerate(starts):
        itself = jnp.where(column // size == k, column + (start - k * size), itself)
    slope = -math.log2(math.e) / sharpness
    total = jnp.zeros((1, own.shape[0]), jnp.float32)
    for first in range(0, rows.shape[0], TILE):
        other = rows[first : first + TILE]
        scores = lax.dot_general(
            other, own, (((1,), (1,)), ((), ())), preferred_element_type=jnp.float32
        )
        weights = 1.0 / (1.0 + jnp.exp2(scores * slope - threshold * slope))
        keep = other[:, :1].astype(jnp.float32) < 0.5 * EMPTY
        if starts:
            keep = keep & (lax.broadcasted_iota(jnp.int32, scores.shape, 0) + first != itself)
        total = total + jnp.sum(jnp.where(keep, weights, 0.0), axis=0, keepdims=True)
    return total


def count_kernel(starts, size, *refs):
    *piece_refs, count_ref = refs
    rows = jnp.concatenate([piece[...] for piece in piece_refs], axis=0)
    count_ref[...] = count_against(rows, blocks(rows, starts, size), starts, size)


def soft_counts(pieces, starts, size):
    out_shape = jax.ShapeDtypeStruct((1, len(starts) * size), jnp.float32)
    return call_kernel("count", functools.partial(count_kernel, starts, size), out_shape, *pieces)


def finish_kernel(starts, late_pieces, late_starts, places, *refs):
    *piece_refs, early_ref, count_ref = refs
    size = count_ref.shape[2]
    early = jnp.concatenate([piece[...] for piece in piece_refs[:-late_pieces]], axis=0)
    late = jnp.concatenate([piece[...] for piece in piece_refs[-late_pieces:]], axis=0)
    own = blocks(early, starts, size)
    late_own = blocks(late, late_starts, size)
    total = early_ref[...] + count_against(late, own, [], size)
    late_total = count_against(early, late_own, [], size) + count_against(
        late, late_own, late_starts, size
    )
    for k, place in enumerate(places()):
        source, j = (total, k) if k < len(starts) else (late_total, k - len(starts))
        count_ref[pl.ds(place, 1), 0, :] = source[:, j * size : (j + 1) * size]


def select_kernel(capacity, counts_ref, slot_ref, out_ref):
    counts = counts_ref[:, 0, :]
    slot = slot_ref[...]
    doc_count = slot.shape[1]
    block = slot // capacity
    rank = slot - block * capacity
    hot = (lax.broadcasted_iota(jnp.int32, (capacity, doc_count), 0) == rank).astype(jnp.float32)
    by_block = jnp.dot(
        counts, hot, precision=lax.Precision.HIGHEST, preferred_element_type=jnp.float32
    )
    chosen = lax.broadcasted_iota(jnp.int32, by_block.shape, 0) == block
    out_ref[...] = jnp.sum(jnp.where(chosen, by_block, 0.0), axis=0, keepdims=True)


def select(counts, slot, capacity):
    out_shape = jax.ShapeDtypeStruct(slot.shape, jnp.float32)
    kernel = functools.partial(select_kernel, capacity)
    return call_kernel("select", kernel, out_shape, counts, slot, limit=8 * 2**20)[0]


def swap_cores(x):
    cores = lax.axis_size("sub")
    return lax.ppermute(x, "sub", [(i, i ^ 1) for i in range(cores)])


def body_by_chip(embeddings, cluster_id):
    doc_count, feature_count = embeddings.shape
    clusters = CL_OWN * lax.axis_size("owner")
    capacity = 2 * doc_count // clusters
    cores = lax.axis_size("sub")
    steps = clusters // cores

    def across(x, p):
        pairs = [
            (chip * cores + core, (chip ^ (p * cores + core)) * cores + core)
            for chip in range(clusters)
            for core in range(cores)
        ]
        return lax.ppermute(x, ("owner", "helper", "sub"), pairs)

    ids = cluster_id.reshape(1, doc_count)
    other_rows, other_ids = swap_cores(embeddings), swap_cores(ids)
    first, last = steps // 2, steps - 1
    middle = [p for p in range(steps) if p not in (first, last)]
    own_laid, slot = call_kernel(
        "route_own",
        functools.partial(route_own_kernel, clusters, capacity),
        [
            jax.ShapeDtypeStruct((steps * capacity, feature_count), jnp.bfloat16),
            jax.ShapeDtypeStruct((1, doc_count), jnp.int32),
        ],
        embeddings,
        ids,
    )
    pieces = call_kernel(
        "route_other",
        functools.partial(route_other_kernel, clusters, capacity),
        [jax.ShapeDtypeStruct((cores * capacity, feature_count), jnp.bfloat16)] * steps,
        other_rows,
        other_ids,
        own_laid,
    )
    arrived = [across(pieces[p], p) for p in (first, *middle, last)]
    swapped = [swap_cores(x) for x in arrived]

    early = arrived[:-1] + swapped[:-1]
    late = [arrived[-1], swapped[-1]]
    span = cores * capacity
    starts = [k * span for k in range(steps - 1)]
    starts += [k * span + capacity for k in range(steps - 1, 2 * (steps - 1))]
    late_starts = [0, span + capacity]

    def places():
        chip, core = chip_index(), lax.axis_index("sub")
        return (
            [chip ^ (p * cores + core) for p in (first, *middle)]
            + [chip ^ (p * cores + 1 - core) for p in (first, *middle)]
            + [chip ^ (last * cores + core), chip ^ (last * cores + 1 - core)]
        )

    counts = call_kernel(
        "finish",
        functools.partial(finish_kernel, starts, len(late), late_starts, places),
        jax.ShapeDtypeStruct((clusters, 1, capacity), jnp.float32),
        *early,
        *late,
        soft_counts(early, starts, capacity),
    )
    back = lax.all_to_all(counts, ("owner", "helper"), split_axis=0, concat_axis=0, tiled=True)
    return select(back, slot, capacity)


def body_by_owner(embeddings, cluster_id):
    doc_count, feature_count = embeddings.shape
    owners, helpers = lax.axis_size("owner"), lax.axis_size("helper")
    clusters = CL_OWN * owners
    capacity = 2 * doc_count // clusters
    mine = lax.axis_index("helper") % CL_OWN

    def partner(x):
        return lax.ppermute(x, "helper", [(i, i ^ 1) for i in range(helpers)])

    outgoing, slot = call_kernel(
        "route",
        functools.partial(route_kernel, clusters, capacity),
        [
            jax.ShapeDtypeStruct((clusters * capacity, feature_count), jnp.bfloat16),
            jax.ShapeDtypeStruct((1, doc_count), jnp.int32),
        ],
        embeddings,
        cluster_id.reshape(1, doc_count),
    )
    outgoing = outgoing.reshape(owners, CL_OWN, capacity, feature_count)
    arrived = lax.all_to_all(outgoing, "owner", split_axis=0, concat_axis=0, tiled=True)
    kept = lax.dynamic_index_in_dim(arrived, mine, 1, keepdims=False)
    given = partner(lax.dynamic_index_in_dim(arrived, 1 - mine, 1, keepdims=False))
    own = jnp.stack([kept, given]).reshape(CL_OWN * owners * capacity, feature_count)
    others = [swap_cores(own)]
    for step in range(CL_OWN, helpers, CL_OWN):
        turn = [(i, (i + step) % helpers) for i in range(helpers)]
        others += [lax.ppermute(x, "helper", turn) for x in (own, others[0])]
    counts = soft_counts([own, *others], [0], own.shape[0])
    counts = counts.reshape(CL_OWN, owners, capacity)
    kept, given = counts[0], partner(counts[1])
    counts = jnp.where(mine == 0, jnp.stack([kept, given], 1), jnp.stack([given, kept], 1))
    back = lax.all_to_all(counts, "owner", split_axis=0, concat_axis=0, tiled=True)
    return select(back.reshape(clusters, 1, capacity), slot, capacity)


def solution(mesh):
    in_specs = (
        P(("groups", "owner", "helper", "sub"), None),
        P(("groups", "owner", "helper", "sub")),
    )
    out_specs = P(("groups", "owner", "helper", "sub"))
    body = body_by_chip if mesh.shape["helper"] == CL_OWN else body_by_owner
    return jax.shard_map(body, mesh=mesh, in_specs=in_specs, out_specs=out_specs, check_vma=False)
```

time: 47.3 us -> 45.6 us (0.964)
  waiting for transfers between devices: 12.8 us -> 10.9 us
  Pallas kernels: 3.45 us -> 4.19 us
  blocking collectives: 14.1 us -> 13.4 us
    ppermute x6, waiting for transfers between devices: 2.59 us -> 1.15 us  [swap_cores(): return lax.ppermute(x, 'sub', [(i, i ^ 1) for i in range(cores)])]
    pallas_call x3 -> x5, Pallas kernels: 3.45 us -> 4.19 us  [call_kernel(): pl.pallas_call(kernel, out_shape=out_shape, in_specs=[VMEM] * len(args),...]
    all_to_all x1, blocking collectives: 14.1 us -> 13.4 us  [body_by_chip(): lax.all_to_all(counts, ('owner', 'helper'), split_axis=0, concat_axis=0,...]
    ppermute x6, starting transfers between devices: 9.13 us -> 9.65 us  [swap_cores(): return lax.ppermute(x, 'sub', [(i, i ^ 1) for i in range(cores)])]
    ppermute x4, waiting for transfers between devices: 10.2 us -> 9.72 us  [across(): return lax.ppermute(x, ('owner', 'helper', 'sub'), pairs)]
  transfers between devices with their start and end apart: 10 -> 10, of which waited for: 5 -> 2; matrix products, arithmetic and copies ran while one was open for 0% -> 0% of each run, Pallas kernels for 0% -> 4%
where the time goes in v4:
time: 45.6 us; the launch traced here: 45.4 us
  starting transfers between devices  15.6 us (34%)
  blocking collectives  13.4 us (29%)
  waiting for transfers between devices  10.9 us (24%)
  Pallas kernels  4.19 us (9%)
  local copies, waits for them, and re-layouts  1.27 us (3%)
    all_to_all x1, blocking collectives, body_by_chip(): lax.all_to_all(counts, ('owner', 'helper'), split_axis=0, concat_axis=0,...  13.4 us
    ppermute x4, waiting for transfers between devices, across(): return lax.ppermute(x, ('owner', 'helper', 'sub'), pairs)  9.72 us
    ppermute x6, starting transfers between devices, swap_cores(): return lax.ppermute(x, 'sub', [(i, i ^ 1) for i in range(cores)])  9.65 us
    ppermute x4, starting transfers between devices, across(): return lax.ppermute(x, ('owner', 'helper', 'sub'), pairs)  5.97 us
    pallas_call x5, Pallas kernels, call_kernel(): pl.pallas_call(kernel, out_shape=out_shape, in_specs=[VMEM] * len(args),...  4.19 us
    unnamed x4, local copies, waits for them, and re-layouts  1.27 us
    ppermute x6, waiting for transfers between devices, swap_cores(): return lax.ppermute(x, 'sub', [(i, i ^ 1) for i in range(cores)])  1.15 us
  transfers between devices with their start and end apart: 10, of which 2 were waited for; matrix products, arithmetic and copies ran while one was open for 0% of the time, Pallas kernels for 4%

profile of v4, /device:TPU:0, one launch (start us, length us, event | category | flops | bytes accessed | tf_op | source)
XLA Modules:
  0.0 45.4 jit_solution(8757499990973026200)
XLA Ops:
  0.0 0.0 copy-start.1
  0.0 0.5 collective-permute-start
  0.5 0.2 copy-done.1
  0.7 0.5 collective-permute-start.1
  1.1 0.0 copy-start
  1.1 1.0 %copy-done = bf16[256,1024]{1,0:T(8,128)(2,1)S(1)} copy-done((bf16[256,1024]{1,0:T(8,128)(2,1)S(1)}, bf16[256,1024]{1,0:T(8,128)(2,1)}, u32[]{:S(2)}) %copy-start) | copy-done | bytes 524312
  2.2 0.6 %route_own.1 = (bf16[256,1024]{1,0:T(8,128)(2,1)S(1)}, s32[1,256]{1,0:T(1,128)S(1)}) custom-call(bf16[256,1024]{1,0:T(8,128)(2,1)S(1)} %copy-done, s32[1,256]{1,0:T(1,128)S(1)} %bitcast.3), custom_call_target="tpu_custom_call" | custom-call | tf_op jit(solution)/shard_map/route_own/pallas_call | solution.py:88
  2.8 0.0 collective-permute-done.1.ids_ref
  2.8 0.0 collective-permute-done.rows_ref
  2.8 0.6 %route_other.1 = (bf16[128,1024]{1,0:T(8,128)(2,1)S(1)}, bf16[128,1024]{1,0:T(8,128)(2,1)S(1)}, bf16[128,1024]{1,0:T(8,128)(2,1)S(1)}, bf16[128,1024]{1,0:T(8,128)(2,1)S(1)}) custom-call(bf16[256,1024]{1,0:T(8,128)(2,1)S(1)} %collective-permute-done.rows_ref, s32[1,256]{1,0:T(1,128)S(1)} %collective-permute-done.1.ids_ref, ...), custom_call_target="tpu_custom_call" | custom-call | tf_op jit(solution)/shard_map/route_other/pallas_call | solution.py:88
  3.4 3.7 %collective-permute-start.2 = (bf16[128,1024]{1,0:T(8,128)(2,1)S(1)}, bf16[128,1024]{1,0:T(8,128)(2,1)S(1)}, u32[]{:S(2)}, u32[]{:S(2)}) collective-permute-start(bf16[128,1024]{1,0:T(8,128)(2,1)S(1)} %get-tuple-element.12), channel_id=1, source_target_pairs={{0,8},{1,11},{2,10},{3,9},{4,12},{5,15},{6,14},{7,13},{8,0},{9,3},... | collective-permute-start | bytes 786440 | tf_op jit(solution)/shard_map/ppermute | solution.py:187
  7.1 0.7 %collective-permute-start.3 = (bf16[128,1024]{1,0:T(8,128)(2,1)S(1)}, bf16[128,1024]{1,0:T(8,128)(2,1)S(1)}, u32[]{:S(2)}, u32[]{:S(2)}) collective-permute-start(bf16[128,1024]{1,0:T(8,128)(2,1)S(1)} %get-tuple-element.13), channel_id=1, source_target_pairs={{0,0},{1,3},{2,2},{3,1},{4,4},{5,7},{6,6},{7,5},{8,8},{9,11},{10,1... | collective-permute-start | bytes 786440 | tf_op jit(solution)/shard_map/ppermute | solution.py:187
  7.7 1.6 %collective-permute-start.4 = (bf16[128,1024]{1,0:T(8,128)(2,1)S(1)}, bf16[128,1024]{1,0:T(8,128)(2,1)S(1)}, u32[]{:S(2)}, u32[]{:S(2)}) collective-permute-start(bf16[128,1024]{1,0:T(8,128)(2,1)S(1)} %get-tuple-element.14), channel_id=1, source_target_pairs={{0,4},{1,7},{2,6},{3,5},{4,0},{5,3},{6,2},{7,1},{8,12},{9,15},{10,... | collective-permute-start | bytes 786440 | tf_op jit(solution)/shard_map/ppermute | solution.py:187
  9.4 0.0 collective-permute-start.8
  9.4 9.7 %collective-permute-done.2.refs_0_ = bf16[128,1024]{1,0:T(8,128)(2,1)S(1)} collective-permute-done((bf16[128,1024]{1,0:T(8,128)(2,1)S(1)}, bf16[128,1024]{1,0:T(8,128)(2,1)S(1)}, u32[]{:S(2)}, u32[]{:S(2)}) %collective-permute-start.2) | collective-permute-done | bytes 262176 | tf_op jit(solution)/shard_map/ppermute | solution.py:187
  19.1 1.0 %collective-permute-start.5 = (bf16[128,1024]{1,0:T(8,128)(2,1)S(1)}, bf16[128,1024]{1,0:T(8,128)(2,1)S(1)}, u32[]{:S(2)}, u32[]{:S(2)}) collective-permute-start(bf16[128,1024]{1,0:T(8,128)(2,1)S(1)} %collective-permute-done.2.refs_0_), channel_id=1, source_target_pairs={{0,1},{1,0},{2,3},{3,2},{4,5},{5,4},{6,7},{7,6},{8,9},{9,8},{10,11... | collective-permute-start | bytes 786440 | tf_op jit(solution)/shard_map/ppermute | solution.py:171
  20.1 0.0 collective-permute-done.3.refs_1_
  20.1 0.0 collective-permute-start.6
  20.1 0.0 collective-permute-done.4.refs_2_
  20.1 7.7 %collective-permute-start.7 = (bf16[128,1024]{1,0:T(8,128)(2,1)S(1)}, bf16[128,1024]{1,0:T(8,128)(2,1)S(1)}, u32[]{:S(2)}, u32[]{:S(2)}) collective-permute-start(bf16[128,1024]{1,0:T(8,128)(2,1)S(1)} %collective-permute-done.4.refs_2_), channel_id=1, source_target_pairs={{0,1},{1,0},{2,3},{3,2},{4,5},{5,4},{6,7},{7,6},{8,9},{9,8},{10,11... | collective-permute-start | bytes 786440 | tf_op jit(solution)/shard_map/ppermute | solution.py:171
  27.8 0.0 collective-permute-done.8.refs_6_
  27.8 0.0 collective-permute-start.9
  27.8 0.0 collective-permute-done.5.refs_3_
  27.8 0.0 collective-permute-done.6.refs_4_
  27.9 1.1 %collective-permute-done.7.refs_5_ = bf16[128,1024]{1,0:T(8,128)(2,1)S(1)} collective-permute-done((bf16[128,1024]{1,0:T(8,128)(2,1)S(1)}, bf16[128,1024]{1,0:T(8,128)(2,1)S(1)}, u32[]{:S(2)}, u32[]{:S(2)}) %collective-permute-start.7) | collective-permute-done | bytes 262176 | tf_op jit(solution)/shard_map/ppermute | solution.py:171
  29.0 1.1 %count.1.refs_8_ = f32[1,384]{1,0:T(1,128)S(1)} custom-call(bf16[128,1024]{1,0:T(8,128)(2,1)S(1)} %collective-permute-done.2.refs_0_, bf16[128,1024]{1,0:T(8,128)(2,1)S(1)} %collective-permute-done.3.refs_1_, bf16[128,1024]{1,0:T(8,128)(2,1)S(1)} %collective-permute-done.4.refs_2_, bf16[128,1024]{1,0:T(8,128)(2,1)S(1)} %collective-permute-done.5.refs_3_, ...), custom_call_target="tpu_custom_call" | custom-call | tf_op jit(solution)/shard_map/count/pallas_call | solution.py:88
  30.2 0.0 collective-permute-done.9.refs_7_
  30.2 1.1 %finish.1 = f32[8,1,64]{2,1,0:T(1,128)S(1)} custom-call(bf16[128,1024]{1,0:T(8,128)(2,1)S(1)} %collective-permute-done.2.refs_0_, bf16[128,1024]{1,0:T(8,128)(2,1)S(1)} %collective-permute-done.3.refs_1_, bf16[128,1024]{1,0:T(8,128)(2,1)S(1)} %collective-permute-done.4.refs_2_, bf16[128,1024]{1,0:T(8,128)(2,1)S(1)} %collective-permute-done.5.refs_3_, ...), custom_call_target="tpu_custom_call" | custom-call | tf_op jit(solution)/shard_map/finish/pallas_call | solution.py:88
  31.3 13.4 %all_to_all.5.counts_ref = f32[8,1,64]{2,1,0:T(1,128)S(1)} all-to-all(f32[8,1,64]{2,1,0:T(1,128)S(1)} %finish.1), channel_id=1, replica_groups=mesh['groups'=2,'owner'=4,'helper'=2,'sub'=2] {'owner','helper'}, dimensions={0} | all-to-all | bytes 4096 | tf_op jit(solution)/shard_map/all_to_all | solution.py:237
  44.7 0.7 %select.1 = f32[1,256]{1,0:T(1,128)} custom-call(f32[8,1,64]{2,1,0:T(1,128)S(1)} %all_to_all.5.counts_ref, s32[1,256]{1,0:T(1,128)S(1)} %get-tuple-element.16.slot_ref), custom_call_target="tpu_custom_call" | custom-call | tf_op jit(solution)/shard_map/select/pallas_call | solution.py:88
Async XLA Ops:
  0.0 0.7 %copy-start.1 = (s32[256]{0:T(256)S(1)}, s32[256]{0:T(256)}, u32[]{:S(2)}) copy-start(s32[256]{0:T(256)} %param.3) | copy-start | bytes 3076
  0.0 2.8 %collective-permute-start = (bf16[256,1024]{1,0:T(8,128)(2,1)}, bf16[256,1024]{1,0:T(8,128)(2,1)S(1)}, u32[]{:S(2)}, u32[]{:S(2)}) collective-permute-start(bf16[256,1024]{1,0:T(8,128)(2,1)} %rows_ref.1), channel_id=1, source_target_pairs={{0,1},{1,0},{2,3},{3,2},{4,5},{5,4},{6,7},{7,6},{8,9},{9,8},{10,11... | collective-permute-start | bytes 1572872 | tf_op jit(solution)/shard_map/ppermute | solution.py:171
  0.7 2.1 %collective-permute-start.1 = (s32[1,256]{1,0:T(1,128)S(1)}, s32[1,256]{1,0:T(1,128)S(1)}, u32[]{:S(2)}, u32[]{:S(2)}) collective-permute-start(s32[1,256]{1,0:T(1,128)S(1)} %bitcast.2), channel_id=1, source_target_pairs={{0,1},{1,0},{2,3},{3,2},{4,5},{5,4},{6,7},{7,6},{8,9},{9,8},{10,11... | collective-permute-start | bytes 3080 | tf_op jit(solution)/shard_map/ppermute | solution.py:171
  1.1 1.0 %copy-start = (bf16[256,1024]{1,0:T(8,128)(2,1)S(1)}, bf16[256,1024]{1,0:T(8,128)(2,1)}, u32[]{:S(2)}) copy-start(bf16[256,1024]{1,0:T(8,128)(2,1)} %rows_ref.1) | copy-start | bytes 1572868
  3.4 15.7 %collective-permute-start.2 = (bf16[128,1024]{1,0:T(8,128)(2,1)S(1)}, bf16[128,1024]{1,0:T(8,128)(2,1)S(1)}, u32[]{:S(2)}, u32[]{:S(2)}) collective-permute-start(bf16[128,1024]{1,0:T(8,128)(2,1)S(1)} %get-tuple-element.12), channel_id=1, source_target_pairs={{0,8},{1,11},{2,10},{3,9},{4,12},{5,15},{6,14},{7,13},{8,0},{9,3},... | collective-permute-start | bytes 786440 | tf_op jit(solution)/shard_map/ppermute | solution.py:187
  7.1 13.0 %collective-permute-start.3 = (bf16[128,1024]{1,0:T(8,128)(2,1)S(1)}, bf16[128,1024]{1,0:T(8,128)(2,1)S(1)}, u32[]{:S(2)}, u32[]{:S(2)}) collective-permute-start(bf16[128,1024]{1,0:T(8,128)(2,1)S(1)} %get-tuple-element.13), channel_id=1, source_target_pairs={{0,0},{1,3},{2,2},{3,1},{4,4},{5,7},{6,6},{7,5},{8,8},{9,11},{10,1... | collective-permute-start | bytes 786440 | tf_op jit(solution)/shard_map/ppermute | solution.py:187
  7.7 12.3 %collective-permute-start.4 = (bf16[128,1024]{1,0:T(8,128)(2,1)S(1)}, bf16[128,1024]{1,0:T(8,128)(2,1)S(1)}, u32[]{:S(2)}, u32[]{:S(2)}) collective-permute-start(bf16[128,1024]{1,0:T(8,128)(2,1)S(1)} %get-tuple-element.14), channel_id=1, source_target_pairs={{0,4},{1,7},{2,6},{3,5},{4,0},{5,3},{6,2},{7,1},{8,12},{9,15},{10,... | collective-permute-start | bytes 786440 | tf_op jit(solution)/shard_map/ppermute | solution.py:187
  9.4 18.5 %collective-permute-start.8 = (bf16[128,1024]{1,0:T(8,128)(2,1)S(1)}, bf16[128,1024]{1,0:T(8,128)(2,1)S(1)}, u32[]{:S(2)}, u32[]{:S(2)}) collective-permute-start(bf16[128,1024]{1,0:T(8,128)(2,1)S(1)} %get-tuple-element.15), channel_id=1, source_target_pairs={{0,12},{1,15},{2,14},{3,13},{4,8},{5,11},{6,10},{7,9},{8,4},{9,7},... | collective-permute-start | bytes 786440 | tf_op jit(solution)/shard_map/ppermute | solution.py:187
  19.1 8.8 %collective-permute-start.5 = (bf16[128,1024]{1,0:T(8,128)(2,1)S(1)}, bf16[128,1024]{1,0:T(8,128)(2,1)S(1)}, u32[]{:S(2)}, u32[]{:S(2)}) collective-permute-start(bf16[128,1024]{1,0:T(8,128)(2,1)S(1)} %collective-permute-done.2.refs_0_), channel_id=1, source_target_pairs={{0,1},{1,0},{2,3},{3,2},{4,5},{5,4},{6,7},{7,6},{8,9},{9,8},{10,11... | collective-permute-start | bytes 786440 | tf_op jit(solution)/shard_map/ppermute | solution.py:171
  20.1 7.8 %collective-permute-start.6 = (bf16[128,1024]{1,0:T(8,128)(2,1)S(1)}, bf16[128,1024]{1,0:T(8,128)(2,1)S(1)}, u32[]{:S(2)}, u32[]{:S(2)}) collective-permute-start(bf16[128,1024]{1,0:T(8,128)(2,1)S(1)} %collective-permute-done.3.refs_1_), channel_id=1, source_target_pairs={{0,1},{1,0},{2,3},{3,2},{4,5},{5,4},{6,7},{7,6},{8,9},{9,8},{10,11... | collective-permute-start | bytes 786440 | tf_op jit(solution)/shard_map/ppermute | solution.py:171
  20.1 8.9 %collective-permute-start.7 = (bf16[128,1024]{1,0:T(8,128)(2,1)S(1)}, bf16[128,1024]{1,0:T(8,128)(2,1)S(1)}, u32[]{:S(2)}, u32[]{:S(2)}) collective-permute-start(bf16[128,1024]{1,0:T(8,128)(2,1)S(1)} %collective-permute-done.4.refs_2_), channel_id=1, source_target_pairs={{0,1},{1,0},{2,3},{3,2},{4,5},{5,4},{6,7},{7,6},{8,9},{9,8},{10,11... | collective-permute-start | bytes 786440 | tf_op jit(solution)/shard_map/ppermute | solution.py:171
  27.8 2.3 %collective-permute-start.9 = (bf16[128,1024]{1,0:T(8,128)(2,1)S(1)}, bf16[128,1024]{1,0:T(8,128)(2,1)S(1)}, u32[]{:S(2)}, u32[]{:S(2)}) collective-permute-start(bf16[128,1024]{1,0:T(8,128)(2,1)S(1)} %collective-permute-done.8.refs_6_), channel_id=1, source_target_pairs={{0,1},{1,0},{2,3},{3,2},{4,5},{5,4},{6,7},{7,6},{8,9},{9,8},{10,11... | collective-permute-start | bytes 786440 | tf_op jit(solution)/shard_map/ppermute | solution.py:171

commit v5 on v4

--- a/solution.py
+++ b/solution.py
@@ -188,7 +188,7 @@
 
     ids = cluster_id.reshape(1, doc_count)
     other_rows, other_ids = swap_cores(embeddings), swap_cores(ids)
-    first, last = steps // 2, steps - 1
+    first, last = steps - 1, steps // 2
     middle = [p for p in range(steps) if p not in (first, last)]
     own_laid, slot = call_kernel(
         "route_own",

time: 45.6 us -> 45.6 us (level)
  waiting for transfers between devices: 10.9 us -> 16.2 us
  starting transfers between devices: 15.6 us -> 12.8 us
  blocking collectives: 13.4 us -> 10.9 us
    ppermute x4, waiting for transfers between devices: 9.72 us -> 16.1 us  [across(): return lax.ppermute(x, ('owner', 'helper', 'sub'), pairs)]
    ppermute x6, starting transfers between devices: 9.65 us -> 6.79 us  [swap_cores(): return lax.ppermute(x, 'sub', [(i, i ^ 1) for i in range(cores)])]
    all_to_all x1, blocking collectives: 13.4 us -> 10.9 us  [body_by_chip(): lax.all_to_all(counts, ('owner', 'helper'), split_axis=0, concat_axis=0,...]
    ppermute x6, waiting for transfers between devices: 1.15 us -> 0.15 us  [swap_cores(): return lax.ppermute(x, 'sub', [(i, i ^ 1) for i in range(cores)])]
  transfers between devices with their start and end apart: 10 -> 10, of which waited for: 2 -> 4; matrix products, arithmetic and copies ran while one was open for 0% -> 0% of each run, Pallas kernels for 4% -> 4%
where the time goes in v5:
time: 45.6 us; the launch traced here: 45.4 us
  waiting for transfers between devices  16.2 us (36%)
  starting transfers between devices  12.8 us (28%)
  blocking collectives  10.9 us (24%)
  Pallas kernels  4.19 us (9%)
  local copies, waits for them, and re-layouts  1.27 us (3%)
    ppermute x4, waiting for transfers between devices, across(): return lax.ppermute(x, ('owner', 'helper', 'sub'), pairs)  16.1 us
    all_to_all x1, blocking collectives, body_by_chip(): lax.all_to_all(counts, ('owner', 'helper'), split_axis=0, concat_axis=0,...  10.9 us
    ppermute x6, starting transfers between devices, swap_cores(): return lax.ppermute(x, 'sub', [(i, i ^ 1) for i in range(cores)])  6.79 us
    ppermute x4, starting transfers between devices, across(): return lax.ppermute(x, ('owner', 'helper', 'sub'), pairs)  5.98 us
    pallas_call x5, Pallas kernels, call_kernel(): pl.pallas_call(kernel, out_shape=out_shape, in_specs=[VMEM] * len(args),...  4.19 us
    unnamed x4, local copies, waits for them, and re-layouts  1.27 us
  transfers between devices with their start and end apart: 10, of which 4 were waited for; matrix products, arithmetic and copies ran while one was open for 0% of the time, Pallas kernels for 4%

profile of v5, /device:TPU:0, one launch (start us, length us, event | category | flops | bytes accessed | tf_op | source)
XLA Modules:
  0.0 45.4 jit_solution(7082060642131971128)
XLA Ops:
  0.0 0.0 copy-start.1
  0.0 0.5 collective-permute-start
  0.5 0.2 copy-done.1
  0.7 0.5 collective-permute-start.1
  1.1 0.0 copy-start
  1.1 1.0 %copy-done = bf16[256,1024]{1,0:T(8,128)(2,1)S(1)} copy-done((bf16[256,1024]{1,0:T(8,128)(2,1)S(1)}, bf16[256,1024]{1,0:T(8,128)(2,1)}, u32[]{:S(2)}) %copy-start) | copy-done | bytes 524312
  2.2 0.6 %route_own.1 = (bf16[256,1024]{1,0:T(8,128)(2,1)S(1)}, s32[1,256]{1,0:T(1,128)S(1)}) custom-call(bf16[256,1024]{1,0:T(8,128)(2,1)S(1)} %copy-done, s32[1,256]{1,0:T(1,128)S(1)} %bitcast.3), custom_call_target="tpu_custom_call" | custom-call | tf_op jit(solution)/shard_map/route_own/pallas_call | solution.py:88
  2.8 0.0 collective-permute-done.1.ids_ref
  2.8 0.0 collective-permute-done.rows_ref
  2.8 0.6 %route_other.1 = (bf16[128,1024]{1,0:T(8,128)(2,1)S(1)}, bf16[128,1024]{1,0:T(8,128)(2,1)S(1)}, bf16[128,1024]{1,0:T(8,128)(2,1)S(1)}, bf16[128,1024]{1,0:T(8,128)(2,1)S(1)}) custom-call(bf16[256,1024]{1,0:T(8,128)(2,1)S(1)} %collective-permute-done.rows_ref, s32[1,256]{1,0:T(1,128)S(1)} %collective-permute-done.1.ids_ref, ...), custom_call_target="tpu_custom_call" | custom-call | tf_op jit(solution)/shard_map/route_other/pallas_call | solution.py:88
  3.4 4.7 %collective-permute-start.2 = (bf16[128,1024]{1,0:T(8,128)(2,1)S(1)}, bf16[128,1024]{1,0:T(8,128)(2,1)S(1)}, u32[]{:S(2)}, u32[]{:S(2)}) collective-permute-start(bf16[128,1024]{1,0:T(8,128)(2,1)S(1)} %get-tuple-element.12), channel_id=1, source_target_pairs={{0,12},{1,15},{2,14},{3,13},{4,8},{5,11},{6,10},{7,9},{8,4},{9,7},... | collective-permute-start | bytes 786440 | tf_op jit(solution)/shard_map/ppermute | solution.py:187
  8.1 0.7 %collective-permute-start.3 = (bf16[128,1024]{1,0:T(8,128)(2,1)S(1)}, bf16[128,1024]{1,0:T(8,128)(2,1)S(1)}, u32[]{:S(2)}, u32[]{:S(2)}) collective-permute-start(bf16[128,1024]{1,0:T(8,128)(2,1)S(1)} %get-tuple-element.13), channel_id=1, source_target_pairs={{0,0},{1,3},{2,2},{3,1},{4,4},{5,7},{6,6},{7,5},{8,8},{9,11},{10,1... | collective-permute-start | bytes 786440 | tf_op jit(solution)/shard_map/ppermute | solution.py:187
  8.8 0.1 collective-permute-start.4
  8.8 0.6 %collective-permute-start.8 = (bf16[128,1024]{1,0:T(8,128)(2,1)S(1)}, bf16[128,1024]{1,0:T(8,128)(2,1)S(1)}, u32[]{:S(2)}, u32[]{:S(2)}) collective-permute-start(bf16[128,1024]{1,0:T(8,128)(2,1)S(1)} %get-tuple-element.15), channel_id=1, source_target_pairs={{0,8},{1,11},{2,10},{3,9},{4,12},{5,15},{6,14},{7,13},{8,0},{9,3},... | collective-permute-start | bytes 786440 | tf_op jit(solution)/shard_map/ppermute | solution.py:187
  9.4 5.4 %collective-permute-done.2.refs_0_ = bf16[128,1024]{1,0:T(8,128)(2,1)S(1)} collective-permute-done((bf16[128,1024]{1,0:T(8,128)(2,1)S(1)}, bf16[128,1024]{1,0:T(8,128)(2,1)S(1)}, u32[]{:S(2)}, u32[]{:S(2)}) %collective-permute-start.2) | collective-permute-done | bytes 262176 | tf_op jit(solution)/shard_map/ppermute | solution.py:187
  14.8 0.9 %collective-permute-start.5 = (bf16[128,1024]{1,0:T(8,128)(2,1)S(1)}, bf16[128,1024]{1,0:T(8,128)(2,1)S(1)}, u32[]{:S(2)}, u32[]{:S(2)}) collective-permute-start(bf16[128,1024]{1,0:T(8,128)(2,1)S(1)} %collective-permute-done.2.refs_0_), channel_id=1, source_target_pairs={{0,1},{1,0},{2,3},{3,2},{4,5},{5,4},{6,7},{7,6},{8,9},{9,8},{10,11... | collective-permute-start | bytes 786440 | tf_op jit(solution)/shard_map/ppermute | solution.py:171
  15.7 0.0 collective-permute-done.3.refs_1_
  15.7 3.4 %collective-permute-start.6 = (bf16[128,1024]{1,0:T(8,128)(2,1)S(1)}, bf16[128,1024]{1,0:T(8,128)(2,1)S(1)}, u32[]{:S(2)}, u32[]{:S(2)}) collective-permute-start(bf16[128,1024]{1,0:T(8,128)(2,1)S(1)} %collective-permute-done.3.refs_1_), channel_id=1, source_target_pairs={{0,1},{1,0},{2,3},{3,2},{4,5},{5,4},{6,7},{7,6},{8,9},{9,8},{10,11... | collective-permute-start | bytes 786440 | tf_op jit(solution)/shard_map/ppermute | solution.py:171
  19.1 2.4 %collective-permute-done.4.refs_2_ = bf16[128,1024]{1,0:T(8,128)(2,1)S(1)} collective-permute-done((bf16[128,1024]{1,0:T(8,128)(2,1)S(1)}, bf16[128,1024]{1,0:T(8,128)(2,1)S(1)}, u32[]{:S(2)}, u32[]{:S(2)}) %collective-permute-start.4) | collective-permute-done | bytes 262176 | tf_op jit(solution)/shard_map/ppermute | solution.py:187
  21.4 1.4 %collective-permute-start.7 = (bf16[128,1024]{1,0:T(8,128)(2,1)S(1)}, bf16[128,1024]{1,0:T(8,128)(2,1)S(1)}, u32[]{:S(2)}, u32[]{:S(2)}) collective-permute-start(bf16[128,1024]{1,0:T(8,128)(2,1)S(1)} %collective-permute-done.4.refs_2_), channel_id=1, source_target_pairs={{0,1},{1,0},{2,3},{3,2},{4,5},{5,4},{6,7},{7,6},{8,9},{9,8},{10,11... | collective-permute-start | bytes 786440 | tf_op jit(solution)/shard_map/ppermute | solution.py:171
  22.8 8.3 %collective-permute-done.8.refs_6_ = bf16[128,1024]{1,0:T(8,128)(2,1)S(1)} collective-permute-done((bf16[128,1024]{1,0:T(8,128)(2,1)S(1)}, bf16[128,1024]{1,0:T(8,128)(2,1)S(1)}, u32[]{:S(2)}, u32[]{:S(2)}) %collective-permute-start.8) | collective-permute-done | bytes 262176 | tf_op jit(solution)/shard_map/ppermute | solution.py:187
  31.1 0.2 collective-permute-start.9
  31.3 0.0 collective-permute-done.5.refs_3_
  31.4 0.0 collective-permute-done.6.refs_4_
  31.4 0.0 collective-permute-done.7.refs_5_
  31.4 1.2 %count.1.refs_8_ = f32[1,384]{1,0:T(1,128)S(1)} custom-call(bf16[128,1024]{1,0:T(8,128)(2,1)S(1)} %collective-permute-done.2.refs_0_, bf16[128,1024]{1,0:T(8,128)(2,1)S(1)} %collective-permute-done.3.refs_1_, bf16[128,1024]{1,0:T(8,128)(2,1)S(1)} %collective-permute-done.4.refs_2_, bf16[128,1024]{1,0:T(8,128)(2,1)S(1)} %collective-permute-done.5.refs_3_, ...), custom_call_target="tpu_custom_call" | custom-call | tf_op jit(solution)/shard_map/count/pallas_call | solution.py:88
  32.5 0.1 collective-permute-done.9.refs_7_
  32.7 1.1 %finish.1 = f32[8,1,64]{2,1,0:T(1,128)S(1)} custom-call(bf16[128,1024]{1,0:T(8,128)(2,1)S(1)} %collective-permute-done.2.refs_0_, bf16[128,1024]{1,0:T(8,128)(2,1)S(1)} %collective-permute-done.3.refs_1_, bf16[128,1024]{1,0:T(8,128)(2,1)S(1)} %collective-permute-done.4.refs_2_, bf16[128,1024]{1,0:T(8,128)(2,1)S(1)} %collective-permute-done.5.refs_3_, ...), custom_call_target="tpu_custom_call" | custom-call | tf_op jit(solution)/shard_map/finish/pallas_call | solution.py:88
  33.8 10.9 %all_to_all.5.counts_ref = f32[8,1,64]{2,1,0:T(1,128)S(1)} all-to-all(f32[8,1,64]{2,1,0:T(1,128)S(1)} %finish.1), channel_id=1, replica_groups=mesh['groups'=2,'owner'=4,'helper'=2,'sub'=2] {'owner','helper'}, dimensions={0} | all-to-all | bytes 4096 | tf_op jit(solution)/shard_map/all_to_all | solution.py:237
  44.7 0.7 %select.1 = f32[1,256]{1,0:T(1,128)} custom-call(f32[8,1,64]{2,1,0:T(1,128)S(1)} %all_to_all.5.counts_ref, s32[1,256]{1,0:T(1,128)S(1)} %get-tuple-element.16.slot_ref), custom_call_target="tpu_custom_call" | custom-call | tf_op jit(solution)/shard_map/select/pallas_call | solution.py:88
Async XLA Ops:
  0.0 0.7 %copy-start.1 = (s32[256]{0:T(256)S(1)}, s32[256]{0:T(256)}, u32[]{:S(2)}) copy-start(s32[256]{0:T(256)} %param.3) | copy-start | bytes 3076
  0.0 2.8 %collective-permute-start = (bf16[256,1024]{1,0:T(8,128)(2,1)}, bf16[256,1024]{1,0:T(8,128)(2,1)S(1)}, u32[]{:S(2)}, u32[]{:S(2)}) collective-permute-start(bf16[256,1024]{1,0:T(8,128)(2,1)} %rows_ref.1), channel_id=1, source_target_pairs={{0,1},{1,0},{2,3},{3,2},{4,5},{5,4},{6,7},{7,6},{8,9},{9,8},{10,11... | collective-permute-start | bytes 1572872 | tf_op jit(solution)/shard_map/ppermute | solution.py:171
  0.7 2.1 %collective-permute-start.1 = (s32[1,256]{1,0:T(1,128)S(1)}, s32[1,256]{1,0:T(1,128)S(1)}, u32[]{:S(2)}, u32[]{:S(2)}) collective-permute-start(s32[1,256]{1,0:T(1,128)S(1)} %bitcast.2), channel_id=1, source_target_pairs={{0,1},{1,0},{2,3},{3,2},{4,5},{5,4},{6,7},{7,6},{8,9},{9,8},{10,11... | collective-permute-start | bytes 3080 | tf_op jit(solution)/shard_map/ppermute | solution.py:171
  1.1 1.0 %copy-start = (bf16[256,1024]{1,0:T(8,128)(2,1)S(1)}, bf16[256,1024]{1,0:T(8,128)(2,1)}, u32[]{:S(2)}) copy-start(bf16[256,1024]{1,0:T(8,128)(2,1)} %rows_ref.1) | copy-start | bytes 1572868
  3.4 11.4 %collective-permute-start.2 = (bf16[128,1024]{1,0:T(8,128)(2,1)S(1)}, bf16[128,1024]{1,0:T(8,128)(2,1)S(1)}, u32[]{:S(2)}, u32[]{:S(2)}) collective-permute-start(bf16[128,1024]{1,0:T(8,128)(2,1)S(1)} %get-tuple-element.12), channel_id=1, source_target_pairs={{0,12},{1,15},{2,14},{3,13},{4,8},{5,11},{6,10},{7,9},{8,4},{9,7},... | collective-permute-start | bytes 786440 | tf_op jit(solution)/shard_map/ppermute | solution.py:187
  8.1 7.6 %collective-permute-start.3 = (bf16[128,1024]{1,0:T(8,128)(2,1)S(1)}, bf16[128,1024]{1,0:T(8,128)(2,1)S(1)}, u32[]{:S(2)}, u32[]{:S(2)}) collective-permute-start(bf16[128,1024]{1,0:T(8,128)(2,1)S(1)} %get-tuple-element.13), channel_id=1, source_target_pairs={{0,0},{1,3},{2,2},{3,1},{4,4},{5,7},{6,6},{7,5},{8,8},{9,11},{10,1... | collective-permute-start | bytes 786440 | tf_op jit(solution)/shard_map/ppermute | solution.py:187
  8.8 12.7 %collective-permute-start.4 = (bf16[128,1024]{1,0:T(8,128)(2,1)S(1)}, bf16[128,1024]{1,0:T(8,128)(2,1)S(1)}, u32[]{:S(2)}, u32[]{:S(2)}) collective-permute-start(bf16[128,1024]{1,0:T(8,128)(2,1)S(1)} %get-tuple-element.14), channel_id=1, source_target_pairs={{0,4},{1,7},{2,6},{3,5},{4,0},{5,3},{6,2},{7,1},{8,12},{9,15},{10,... | collective-permute-start | bytes 786440 | tf_op jit(solution)/shard_map/ppermute | solution.py:187
  8.8 22.3 %collective-permute-start.8 = (bf16[128,1024]{1,0:T(8,128)(2,1)S(1)}, bf16[128,1024]{1,0:T(8,128)(2,1)S(1)}, u32[]{:S(2)}, u32[]{:S(2)}) collective-permute-start(bf16[128,1024]{1,0:T(8,128)(2,1)S(1)} %get-tuple-element.15), channel_id=1, source_target_pairs={{0,8},{1,11},{2,10},{3,9},{4,12},{5,15},{6,14},{7,13},{8,0},{9,3},... | collective-permute-start | bytes 786440 | tf_op jit(solution)/shard_map/ppermute | solution.py:187
  14.8 16.5 %collective-permute-start.5 = (bf16[128,1024]{1,0:T(8,128)(2,1)S(1)}, bf16[128,1024]{1,0:T(8,128)(2,1)S(1)}, u32[]{:S(2)}, u32[]{:S(2)}) collective-permute-start(bf16[128,1024]{1,0:T(8,128)(2,1)S(1)} %collective-permute-done.2.refs_0_), channel_id=1, source_target_pairs={{0,1},{1,0},{2,3},{3,2},{4,5},{5,4},{6,7},{7,6},{8,9},{9,8},{10,11... | collective-permute-start | bytes 786440 | tf_op jit(solution)/shard_map/ppermute | solution.py:171
  15.7 15.7 %collective-permute-start.6 = (bf16[128,1024]{1,0:T(8,128)(2,1)S(1)}, bf16[128,1024]{1,0:T(8,128)(2,1)S(1)}, u32[]{:S(2)}, u32[]{:S(2)}) collective-permute-start(bf16[128,1024]{1,0:T(8,128)(2,1)S(1)} %collective-permute-done.3.refs_1_), channel_id=1, source_target_pairs={{0,1},{1,0},{2,3},{3,2},{4,5},{5,4},{6,7},{7,6},{8,9},{9,8},{10,11... | collective-permute-start | bytes 786440 | tf_op jit(solution)/shard_map/ppermute | solution.py:171
  21.4 9.9 %collective-permute-start.7 = (bf16[128,1024]{1,0:T(8,128)(2,1)S(1)}, bf16[128,1024]{1,0:T(8,128)(2,1)S(1)}, u32[]{:S(2)}, u32[]{:S(2)}) collective-permute-start(bf16[128,1024]{1,0:T(8,128)(2,1)S(1)} %collective-permute-done.4.refs_2_), channel_id=1, source_target_pairs={{0,1},{1,0},{2,3},{3,2},{4,5},{5,4},{6,7},{7,6},{8,9},{9,8},{10,11... | collective-permute-start | bytes 786440 | tf_op jit(solution)/shard_map/ppermute | solution.py:171
  31.1 1.5 %collective-permute-start.9 = (bf16[128,1024]{1,0:T(8,128)(2,1)S(1)}, bf16[128,1024]{1,0:T(8,128)(2,1)S(1)}, u32[]{:S(2)}, u32[]{:S(2)}) collective-permute-start(bf16[128,1024]{1,0:T(8,128)(2,1)S(1)} %collective-permute-done.8.refs_6_), channel_id=1, source_target_pairs={{0,1},{1,0},{2,3},{3,2},{4,5},{5,4},{6,7},{7,6},{8,9},{9,8},{10,11... | collective-permute-start | bytes 786440 | tf_op jit(solution)/shard_map/ppermute | solution.py:171

commit v6 on v5

--- a/solution.py
+++ b/solution.py
@@ -50,27 +50,33 @@
     return jnp.where(filled | (lane > 0), laid * factor, EMPTY).astype(jnp.bfloat16)
 
 
-def slots_of_steps(slot, capacity, steps):
-    cores = lax.axis_size("sub")
+def steps_of(owner, sends):
+    middle = (owner == 1) | (owner == 2)
+    if isinstance(owner, int):
+        near, far = (2, 1) if middle else (1, 2)
+    else:
+        near, far = jnp.where(middle, 2, 1), jnp.where(middle, 1, 2)
+    return [3, 0, near, far] if sends else [3, 0, far, near]
+
+
+def slots_of_steps(slot, capacity):
     by_distance = slot ^ (chip_index() * capacity)
     distance = by_distance // capacity
     rank = by_distance - distance * capacity
     step = jnp.full_like(slot, -1)
-    for place, p in enumerate(steps):
-        step = jnp.where(distance == p * cores + lax.axis_index("sub"), place, step)
+    for k, far in enumerate(steps_of(lax.axis_index("owner"), True)):
+        step = jnp.where(distance == far * CL_OWN + lax.axis_index("sub"), k, step)
     return jnp.where(step < 0, -1, step * capacity + rank)
 
 
 def route_own_kernel(clusters, capacity, rows_ref, ids_ref, laid_ref, slot_ref):
-    steps = range(laid_ref.shape[0] // capacity)
     slot = slots_of(ids_ref[...], clusters, capacity)
     slot_ref[...] = slot
-    laid_ref[...] = lay(rows_ref, slots_of_steps(slot, capacity, steps), laid_ref.shape[0])
+    laid_ref[...] = lay(rows_ref, slots_of_steps(slot, capacity), laid_ref.shape[0])
 
 
 def route_other_kernel(clusters, capacity, rows_ref, ids_ref, laid_ref, *piece_refs):
-    slot = slots_of(ids_ref[...], clusters, capacity)
-    slot = slots_of_steps(slot, capacity, range(len(piece_refs)))
+    slot = slots_of_steps(slots_of(ids_ref[...], clusters, capacity), capacity)
     laid = lay(rows_ref, slot, laid_ref.shape[0])
     for p, piece in enumerate(piece_refs):
         rows = slice(p * capacity, (p + 1) * capacity)
@@ -178,18 +184,16 @@
     cores = lax.axis_size("sub")
     steps = clusters // cores
 
-    def across(x, p):
-        pairs = [
-            (chip * cores + core, (chip ^ (p * cores + core)) * cores + core)
-            for chip in range(clusters)
-            for core in range(cores)
-        ]
+    def across(x, step):
+        pairs = []
+        for chip in range(clusters):
+            distance = steps_of(chip // CL_OWN, True)[step] * CL_OWN
+            for core in range(cores):
+                pairs.append((chip * cores + core, (chip ^ (distance + core)) * cores + core))
         return lax.ppermute(x, ("owner", "helper", "sub"), pairs)
 
     ids = cluster_id.reshape(1, doc_count)
     other_rows, other_ids = swap_cores(embeddings), swap_cores(ids)
-    first, last = steps - 1, steps // 2
-    middle = [p for p in range(steps) if p not in (first, last)]
     own_laid, slot = call_kernel(
         "route_own",
         functools.partial(route_own_kernel, clusters, capacity),
@@ -208,7 +212,7 @@
         other_ids,
         own_laid,
     )
-    arrived = [across(pieces[p], p) for p in (first, *middle, last)]
+    arrived = [across(piece, step) for step, piece in enumerate(pieces)]
     swapped = [swap_cores(x) for x in arrived]
 
     early = arrived[:-1] + swapped[:-1]
@@ -220,11 +224,9 @@
 
     def places():
         chip, core = chip_index(), lax.axis_index("sub")
-        return (
-            [chip ^ (p * cores + core) for p in (first, *middle)]
-            + [chip ^ (p * cores + 1 - core) for p in (first, *middle)]
-            + [chip ^ (last * cores + core), chip ^ (last * cores + 1 - core)]
-        )
+        far = [chip ^ (d * CL_OWN) for d in steps_of(lax.axis_index("owner"), False)]
+        own, other = [x ^ core for x in far], [x ^ (1 - core) for x in far]
+        return own[:-1] + other[:-1] + [own[-1], other[-1]]
 
     counts = call_kernel(
         "finish",
@@ -281,5 +283,6 @@
         P(("groups", "owner", "helper", "sub")),
     )
     out_specs = P(("groups", "owner", "helper", "sub"))
-    body = body_by_chip if mesh.shape["helper"] == CL_OWN else body_by_owner
+    line_of_chips = mesh.shape["owner"] == 4 and mesh.shape["helper"] == CL_OWN
+    body = body_by_chip if line_of_chips and mesh.shape["sub"] == 2 else body_by_owner
     return jax.shard_map(body, mesh=mesh, in_specs=in_specs, out_specs=out_specs, check_vma=False)

time: 45.6 us -> 46.8 us (1.026)
  starting transfers between devices: 12.8 us -> 14 us
    ppermute x4, starting transfers between devices: 5.98 us -> 8.31 us  [across(): return lax.ppermute(x, ('owner', 'helper', 'sub'), pairs)]
    ppermute x6, starting transfers between devices: 6.79 us -> 5.65 us  [swap_cores(): return lax.ppermute(x, 'sub', [(i, i ^ 1) for i in range(cores)])]
    ppermute x4, waiting for transfers between devices: 16.1 us -> 15.2 us  [across(): return lax.ppermute(x, ('owner', 'helper', 'sub'), pairs)]
    ppermute x6, waiting for transfers between devices: 0.15 us -> 1.03 us  [swap_cores(): return lax.ppermute(x, 'sub', [(i, i ^ 1) for i in range(cores)])]
  transfers between devices with their start and end apart: 10 -> 10, of which waited for: 4 -> 3; matrix products, arithmetic and copies ran while one was open for 0% -> 0% of each run, Pallas kernels for 4% -> 4%
where the time goes in v6:
time: 46.8 us; the launch traced here: 46.5 us
  waiting for transfers between devices  16.2 us (35%)
  starting transfers between devices  14 us (30%)
  blocking collectives  10.9 us (23%)
  Pallas kernels  4.18 us (9%)
  local copies, waits for them, and re-layouts  1.27 us (3%)
    ppermute x4, waiting for transfers between devices, across(): return lax.ppermute(x, ('owner', 'helper', 'sub'), pairs)  15.2 us
    all_to_all x1, blocking collectives, body_by_chip(): lax.all_to_all(counts, ('owner', 'helper'), split_axis=0, concat_axis=0,...  10.9 us
    ppermute x4, starting transfers between devices, across(): return lax.ppermute(x, ('owner', 'helper', 'sub'), pairs)  8.31 us
    ppermute x6, starting transfers between devices, swap_cores(): return lax.ppermute(x, 'sub', [(i, i ^ 1) for i in range(cores)])  5.65 us
    pallas_call x5, Pallas kernels, call_kernel(): pl.pallas_call(kernel, out_shape=out_shape, in_specs=[VMEM] * len(args),...  4.18 us
    unnamed x4, local copies, waits for them, and re-layouts  1.27 us
    ppermute x6, waiting for transfers between devices, swap_cores(): return lax.ppermute(x, 'sub', [(i, i ^ 1) for i in range(cores)])  1.03 us
  transfers between devices with their start and end apart: 10, of which 3 were waited for; matrix products, arithmetic and copies ran while one was open for 0% of the time, Pallas kernels for 4%

profile of v6, /device:TPU:0, one launch (start us, length us, event | category | flops | bytes accessed | tf_op | source)
XLA Modules:
  0.0 46.5 jit_solution(17074828031952453881)
XLA Ops:
  0.0 0.0 copy-start.1
  0.0 0.5 collective-permute-start
  0.5 0.2 copy-done.1
  0.7 0.5 collective-permute-start.1
  1.1 0.0 copy-start
  1.1 1.0 %copy-done = bf16[256,1024]{1,0:T(8,128)(2,1)S(1)} copy-done((bf16[256,1024]{1,0:T(8,128)(2,1)S(1)}, bf16[256,1024]{1,0:T(8,128)(2,1)}, u32[]{:S(2)}) %copy-start) | copy-done | bytes 524312
  2.2 0.6 %route_own.1 = (bf16[256,1024]{1,0:T(8,128)(2,1)S(1)}, s32[1,256]{1,0:T(1,128)S(1)}) custom-call(bf16[256,1024]{1,0:T(8,128)(2,1)S(1)} %copy-done, s32[1,256]{1,0:T(1,128)S(1)} %bitcast.3), custom_call_target="tpu_custom_call" | custom-call | tf_op jit(solution)/shard_map/route_own/pallas_call | solution.py:94
  2.8 0.0 collective-permute-done.1.ids_ref
  2.8 0.0 collective-permute-done.rows_ref
  2.8 0.6 %route_other.1 = (bf16[128,1024]{1,0:T(8,128)(2,1)S(1)}, bf16[128,1024]{1,0:T(8,128)(2,1)S(1)}, bf16[128,1024]{1,0:T(8,128)(2,1)S(1)}, bf16[128,1024]{1,0:T(8,128)(2,1)S(1)}) custom-call(bf16[256,1024]{1,0:T(8,128)(2,1)S(1)} %collective-permute-done.rows_ref, s32[1,256]{1,0:T(1,128)S(1)} %collective-permute-done.1.ids_ref, ...), custom_call_target="tpu_custom_call" | custom-call | tf_op jit(solution)/shard_map/route_other/pallas_call | solution.py:94
  3.4 4.7 %collective-permute-start.2 = (bf16[128,1024]{1,0:T(8,128)(2,1)S(1)}, bf16[128,1024]{1,0:T(8,128)(2,1)S(1)}, u32[]{:S(2)}, u32[]{:S(2)}) collective-permute-start(bf16[128,1024]{1,0:T(8,128)(2,1)S(1)} %get-tuple-element.12), channel_id=1, source_target_pairs={{0,12},{1,15},{2,14},{3,13},{4,8},{5,11},{6,10},{7,9},{8,4},{9,7},... | collective-permute-start | bytes 786440 | tf_op jit(solution)/shard_map/ppermute | solution.py:193
  8.1 0.7 %collective-permute-start.3 = (bf16[128,1024]{1,0:T(8,128)(2,1)S(1)}, bf16[128,1024]{1,0:T(8,128)(2,1)S(1)}, u32[]{:S(2)}, u32[]{:S(2)}) collective-permute-start(bf16[128,1024]{1,0:T(8,128)(2,1)S(1)} %get-tuple-element.13), channel_id=1, source_target_pairs={{0,0},{1,3},{2,2},{3,1},{4,4},{5,7},{6,6},{7,5},{8,8},{9,11},{10,1... | collective-permute-start | bytes 786440 | tf_op jit(solution)/shard_map/ppermute | solution.py:193
  8.8 0.1 collective-permute-start.4
  8.8 2.9 %collective-permute-start.8 = (bf16[128,1024]{1,0:T(8,128)(2,1)S(1)}, bf16[128,1024]{1,0:T(8,128)(2,1)S(1)}, u32[]{:S(2)}, u32[]{:S(2)}) collective-permute-start(bf16[128,1024]{1,0:T(8,128)(2,1)S(1)} %get-tuple-element.15), channel_id=1, source_target_pairs={{0,8},{1,11},{2,10},{3,9},{4,0},{5,3},{6,2},{7,1},{8,12},{9,15},{1... | collective-permute-start | bytes 786440 | tf_op jit(solution)/shard_map/ppermute | solution.py:193
  11.7 3.1 %collective-permute-done.2.refs_0_ = bf16[128,1024]{1,0:T(8,128)(2,1)S(1)} collective-permute-done((bf16[128,1024]{1,0:T(8,128)(2,1)S(1)}, bf16[128,1024]{1,0:T(8,128)(2,1)S(1)}, u32[]{:S(2)}, u32[]{:S(2)}) %collective-permute-start.2) | collective-permute-done | bytes 262176 | tf_op jit(solution)/shard_map/ppermute | solution.py:193
  14.8 0.9 %collective-permute-start.5 = (bf16[128,1024]{1,0:T(8,128)(2,1)S(1)}, bf16[128,1024]{1,0:T(8,128)(2,1)S(1)}, u32[]{:S(2)}, u32[]{:S(2)}) collective-permute-start(bf16[128,1024]{1,0:T(8,128)(2,1)S(1)} %collective-permute-done.2.refs_0_), channel_id=1, source_target_pairs={{0,1},{1,0},{2,3},{3,2},{4,5},{5,4},{6,7},{7,6},{8,9},{9,8},{10,11... | collective-permute-start | bytes 786440 | tf_op jit(solution)/shard_map/ppermute | solution.py:177
  15.7 0.0 collective-permute-done.3.refs_1_
  15.7 3.4 %collective-permute-start.6 = (bf16[128,1024]{1,0:T(8,128)(2,1)S(1)}, bf16[128,1024]{1,0:T(8,128)(2,1)S(1)}, u32[]{:S(2)}, u32[]{:S(2)}) collective-permute-start(bf16[128,1024]{1,0:T(8,128)(2,1)S(1)} %collective-permute-done.3.refs_1_), channel_id=1, source_target_pairs={{0,1},{1,0},{2,3},{3,2},{4,5},{5,4},{6,7},{7,6},{8,9},{9,8},{10,11... | collective-permute-start | bytes 786440 | tf_op jit(solution)/shard_map/ppermute | solution.py:177
  19.1 12.1 %collective-permute-done.4.refs_2_ = bf16[128,1024]{1,0:T(8,128)(2,1)S(1)} collective-permute-done((bf16[128,1024]{1,0:T(8,128)(2,1)S(1)}, bf16[128,1024]{1,0:T(8,128)(2,1)S(1)}, u32[]{:S(2)}, u32[]{:S(2)}) %collective-permute-start.4) | collective-permute-done | bytes 262176 | tf_op jit(solution)/shard_map/ppermute | solution.py:193
  31.1 0.2 collective-permute-start.7
  31.3 0.0 collective-permute-done.8.refs_6_
  31.4 0.3 collective-permute-start.9
  31.6 0.0 collective-permute-done.5.refs_3_
  31.6 0.0 collective-permute-done.6.refs_4_
  31.6 1.0 %collective-permute-done.7.refs_5_ = bf16[128,1024]{1,0:T(8,128)(2,1)S(1)} collective-permute-done((bf16[128,1024]{1,0:T(8,128)(2,1)S(1)}, bf16[128,1024]{1,0:T(8,128)(2,1)S(1)}, u32[]{:S(2)}, u32[]{:S(2)}) %collective-permute-start.7) | collective-permute-done | bytes 262176 | tf_op jit(solution)/shard_map/ppermute | solution.py:177
  32.7 1.1 %count.1.refs_8_ = f32[1,384]{1,0:T(1,128)S(1)} custom-call(bf16[128,1024]{1,0:T(8,128)(2,1)S(1)} %collective-permute-done.2.refs_0_, bf16[128,1024]{1,0:T(8,128)(2,1)S(1)} %collective-permute-done.3.refs_1_, bf16[128,1024]{1,0:T(8,128)(2,1)S(1)} %collective-permute-done.4.refs_2_, bf16[128,1024]{1,0:T(8,128)(2,1)S(1)} %collective-permute-done.5.refs_3_, ...), custom_call_target="tpu_custom_call" | custom-call | tf_op jit(solution)/shard_map/count/pallas_call | solution.py:94
  33.8 0.0 collective-permute-done.9.refs_7_
  33.8 1.1 %finish.1 = f32[8,1,64]{2,1,0:T(1,128)S(1)} custom-call(bf16[128,1024]{1,0:T(8,128)(2,1)S(1)} %collective-permute-done.2.refs_0_, bf16[128,1024]{1,0:T(8,128)(2,1)S(1)} %collective-permute-done.3.refs_1_, bf16[128,1024]{1,0:T(8,128)(2,1)S(1)} %collective-permute-done.4.refs_2_, bf16[128,1024]{1,0:T(8,128)(2,1)S(1)} %collective-permute-done.5.refs_3_, ...), custom_call_target="tpu_custom_call" | custom-call | tf_op jit(solution)/shard_map/finish/pallas_call | solution.py:94
  34.9 10.9 %all_to_all.5.counts_ref = f32[8,1,64]{2,1,0:T(1,128)S(1)} all-to-all(f32[8,1,64]{2,1,0:T(1,128)S(1)} %finish.1), channel_id=1, replica_groups=mesh['groups'=2,'owner'=4,'helper'=2,'sub'=2] {'owner','helper'}, dimensions={0} | all-to-all | bytes 4096 | tf_op jit(solution)/shard_map/all_to_all | solution.py:239
  45.8 0.7 %select.1 = f32[1,256]{1,0:T(1,128)} custom-call(f32[8,1,64]{2,1,0:T(1,128)S(1)} %all_to_all.5.counts_ref, s32[1,256]{1,0:T(1,128)S(1)} %get-tuple-element.16.slot_ref), custom_call_target="tpu_custom_call" | custom-call | tf_op jit(solution)/shard_map/select/pallas_call | solution.py:94
Async XLA Ops:
  0.0 0.7 %copy-start.1 = (s32[256]{0:T(256)S(1)}, s32[256]{0:T(256)}, u32[]{:S(2)}) copy-start(s32[256]{0:T(256)} %param.3) | copy-start | bytes 3076
  0.0 2.8 %collective-permute-start = (bf16[256,1024]{1,0:T(8,128)(2,1)}, bf16[256,1024]{1,0:T(8,128)(2,1)S(1)}, u32[]{:S(2)}, u32[]{:S(2)}) collective-permute-start(bf16[256,1024]{1,0:T(8,128)(2,1)} %rows_ref.1), channel_id=1, source_target_pairs={{0,1},{1,0},{2,3},{3,2},{4,5},{5,4},{6,7},{7,6},{8,9},{9,8},{10,11... | collective-permute-start | bytes 1572872 | tf_op jit(solution)/shard_map/ppermute | solution.py:177
  0.7 2.1 %collective-permute-start.1 = (s32[1,256]{1,0:T(1,128)S(1)}, s32[1,256]{1,0:T(1,128)S(1)}, u32[]{:S(2)}, u32[]{:S(2)}) collective-permute-start(s32[1,256]{1,0:T(1,128)S(1)} %bitcast.2), channel_id=1, source_target_pairs={{0,1},{1,0},{2,3},{3,2},{4,5},{5,4},{6,7},{7,6},{8,9},{9,8},{10,11... | collective-permute-start | bytes 3080 | tf_op jit(solution)/shard_map/ppermute | solution.py:177
  1.1 1.0 %copy-start = (bf16[256,1024]{1,0:T(8,128)(2,1)S(1)}, bf16[256,1024]{1,0:T(8,128)(2,1)}, u32[]{:S(2)}) copy-start(bf16[256,1024]{1,0:T(8,128)(2,1)} %rows_ref.1) | copy-start | bytes 1572868
  3.4 11.4 %collective-permute-start.2 = (bf16[128,1024]{1,0:T(8,128)(2,1)S(1)}, bf16[128,1024]{1,0:T(8,128)(2,1)S(1)}, u32[]{:S(2)}, u32[]{:S(2)}) collective-permute-start(bf16[128,1024]{1,0:T(8,128)(2,1)S(1)} %get-tuple-element.12), channel_id=1, source_target_pairs={{0,12},{1,15},{2,14},{3,13},{4,8},{5,11},{6,10},{7,9},{8,4},{9,7},... | collective-permute-start | bytes 786440 | tf_op jit(solution)/shard_map/ppermute | solution.py:193
  8.1 7.6 %collective-permute-start.3 = (bf16[128,1024]{1,0:T(8,128)(2,1)S(1)}, bf16[128,1024]{1,0:T(8,128)(2,1)S(1)}, u32[]{:S(2)}, u32[]{:S(2)}) collective-permute-start(bf16[128,1024]{1,0:T(8,128)(2,1)S(1)} %get-tuple-element.13), channel_id=1, source_target_pairs={{0,0},{1,3},{2,2},{3,1},{4,4},{5,7},{6,6},{7,5},{8,8},{9,11},{10,1... | collective-permute-start | bytes 786440 | tf_op jit(solution)/shard_map/ppermute | solution.py:193
  8.8 22.4 %collective-permute-start.4 = (bf16[128,1024]{1,0:T(8,128)(2,1)S(1)}, bf16[128,1024]{1,0:T(8,128)(2,1)S(1)}, u32[]{:S(2)}, u32[]{:S(2)}) collective-permute-start(bf16[128,1024]{1,0:T(8,128)(2,1)S(1)} %get-tuple-element.14), channel_id=1, source_target_pairs={{0,4},{1,7},{2,6},{3,5},{4,12},{5,15},{6,14},{7,13},{8,0},{9,3},{1... | collective-permute-start | bytes 786440 | tf_op jit(solution)/shard_map/ppermute | solution.py:193
  8.8 22.5 %collective-permute-start.8 = (bf16[128,1024]{1,0:T(8,128)(2,1)S(1)}, bf16[128,1024]{1,0:T(8,128)(2,1)S(1)}, u32[]{:S(2)}, u32[]{:S(2)}) collective-permute-start(bf16[128,1024]{1,0:T(8,128)(2,1)S(1)} %get-tuple-element.15), channel_id=1, source_target_pairs={{0,8},{1,11},{2,10},{3,9},{4,0},{5,3},{6,2},{7,1},{8,12},{9,15},{1... | collective-permute-start | bytes 786440 | tf_op jit(solution)/shard_map/ppermute | solution.py:193
  14.8 16.8 %collective-permute-start.5 = (bf16[128,1024]{1,0:T(8,128)(2,1)S(1)}, bf16[128,1024]{1,0:T(8,128)(2,1)S(1)}, u32[]{:S(2)}, u32[]{:S(2)}) collective-permute-start(bf16[128,1024]{1,0:T(8,128)(2,1)S(1)} %collective-permute-done.2.refs_0_), channel_id=1, source_target_pairs={{0,1},{1,0},{2,3},{3,2},{4,5},{5,4},{6,7},{7,6},{8,9},{9,8},{10,11... | collective-permute-start | bytes 786440 | tf_op jit(solution)/shard_map/ppermute | solution.py:177
  15.7 16.0 %collective-permute-start.6 = (bf16[128,1024]{1,0:T(8,128)(2,1)S(1)}, bf16[128,1024]{1,0:T(8,128)(2,1)S(1)}, u32[]{:S(2)}, u32[]{:S(2)}) collective-permute-start(bf16[128,1024]{1,0:T(8,128)(2,1)S(1)} %collective-permute-done.3.refs_1_), channel_id=1, source_target_pairs={{0,1},{1,0},{2,3},{3,2},{4,5},{5,4},{6,7},{7,6},{8,9},{9,8},{10,11... | collective-permute-start | bytes 786440 | tf_op jit(solution)/shard_map/ppermute | solution.py:177
  31.1 1.5 %collective-permute-start.7 = (bf16[128,1024]{1,0:T(8,128)(2,1)S(1)}, bf16[128,1024]{1,0:T(8,128)(2,1)S(1)}, u32[]{:S(2)}, u32[]{:S(2)}) collective-permute-start(bf16[128,1024]{1,0:T(8,128)(2,1)S(1)} %collective-permute-done.4.refs_2_), channel_id=1, source_target_pairs={{0,1},{1,0},{2,3},{3,2},{4,5},{5,4},{6,7},{7,6},{8,9},{9,8},{10,11... | collective-permute-start | bytes 786440 | tf_op jit(solution)/shard_map/ppermute | solution.py:177
  31.4 2.5 %collective-permute-start.9 = (bf16[128,1024]{1,0:T(8,128)(2,1)S(1)}, bf16[128,1024]{1,0:T(8,128)(2,1)S(1)}, u32[]{:S(2)}, u32[]{:S(2)}) collective-permute-start(bf16[128,1024]{1,0:T(8,128)(2,1)S(1)} %collective-permute-done.8.refs_6_), channel_id=1, source_target_pairs={{0,1},{1,0},{2,3},{3,2},{4,5},{5,4},{6,7},{7,6},{8,9},{9,8},{10,11... | collective-permute-start | bytes 786440 | tf_op jit(solution)/shard_map/ppermute | solution.py:177

commit v7 on v4

--- a/solution.py
+++ b/solution.py
@@ -61,21 +61,24 @@
     return jnp.where(step < 0, -1, step * capacity + rank)
 
 
-def route_own_kernel(clusters, capacity, rows_ref, ids_ref, laid_ref, slot_ref):
-    steps = range(laid_ref.shape[0] // capacity)
+def route_first_kernel(clusters, capacity, step, rows_ref, ids_ref, piece_ref, slot_ref):
     slot = slots_of(ids_ref[...], clusters, capacity)
     slot_ref[...] = slot
-    laid_ref[...] = lay(rows_ref, slots_of_steps(slot, capacity, steps), laid_ref.shape[0])
-
-
-def route_other_kernel(clusters, capacity, rows_ref, ids_ref, laid_ref, *piece_refs):
-    slot = slots_of(ids_ref[...], clusters, capacity)
-    slot = slots_of_steps(slot, capacity, range(len(piece_refs)))
-    laid = lay(rows_ref, slot, laid_ref.shape[0])
-    for p, piece in enumerate(piece_refs):
-        rows = slice(p * capacity, (p + 1) * capacity)
-        piece[:capacity] = laid_ref[rows]
-        piece[capacity:] = laid[rows]
+    piece_ref[...] = lay(rows_ref, slots_of_steps(slot, capacity, [step]), capacity)
+
+
+def route_rest_kernel(clusters, capacity, first, steps, *refs):
+    own_rows, other_rows, own_slot, other_ids, first_ref, *piece_refs = refs
+    slot = slots_of_steps(own_slot[...], capacity, steps)
+    laid = lay(own_rows, slot, len(steps) * capacity)
+    for k, piece in enumerate(piece_refs):
+        piece[:capacity] = laid[k * capacity : (k + 1) * capacity]
+    slot = slots_of(other_ids[...], clusters, capacity)
+    slot = slots_of_steps(slot, capacity, [first, *steps])
+    laid = lay(other_rows, slot, (1 + len(steps)) * capacity)
+    first_ref[...] = laid[:capacity]
+    for k, piece in enumerate(piece_refs):
+        piece[capacity:] = laid[(k + 1) * capacity : (k + 2) * capacity]
 
 
 def route_kernel(clusters, capacity, rows_ref, ids_ref, piece_ref, slot_ref):
@@ -84,15 +87,23 @@
     piece_ref[...] = lay(rows_ref, slot, piece_ref.shape[0])
 
 
-def call_kernel(name, kernel, out_shape, *args, limit=32 * 2**20):
+def call_kernel(name, kernel, out_shape, *args, limit=32 * 2**20, flops=0):
+    cost = pl.CostEstimate(flops=flops, bytes_accessed=0, transcendentals=0) if flops else None
     return pl.pallas_call(
         kernel,
         out_shape=out_shape,
         in_specs=[VMEM] * len(args),
         out_specs=jax.tree.map(lambda _: VMEM, out_shape),
         compiler_params=pltpu.CompilerParams(vmem_limit_bytes=limit),
+        cost_estimate=cost,
         name=name,
     )(*args)
+
+
+def join_kernel(first_ref, second_ref, out_ref):
+    rows = first_ref.shape[0]
+    out_ref[:rows] = first_ref[...]
+    out_ref[rows:] = second_ref[...]
 
 
 def blocks(rows, starts, size):
@@ -190,32 +201,37 @@
     other_rows, other_ids = swap_cores(embeddings), swap_cores(ids)
     first, last = steps // 2, steps - 1
     middle = [p for p in range(steps) if p not in (first, last)]
-    own_laid, slot = call_kernel(
-        "route_own",
-        functools.partial(route_own_kernel, clusters, capacity),
-        [
-            jax.ShapeDtypeStruct((steps * capacity, feature_count), jnp.bfloat16),
-            jax.ShapeDtypeStruct((1, doc_count), jnp.int32),
-        ],
+    half = jax.ShapeDtypeStruct((capacity, feature_count), jnp.bfloat16)
+    whole = jax.ShapeDtypeStruct((cores * capacity, feature_count), jnp.bfloat16)
+
+    first_own, slot = call_kernel(
+        "route_first",
+        functools.partial(route_first_kernel, clusters, capacity, first),
+        [half, jax.ShapeDtypeStruct((1, doc_count), jnp.int32)],
         embeddings,
         ids,
     )
-    pieces = call_kernel(
-        "route_other",
-        functools.partial(route_other_kernel, clusters, capacity),
-        [jax.ShapeDtypeStruct((cores * capacity, feature_count), jnp.bfloat16)] * steps,
+    first_own = across(first_own, first)
+    first_other, *rest = call_kernel(
+        "route_rest",
+        functools.partial(route_rest_kernel, clusters, capacity, first, [*middle, last]),
+        [half] + [whole] * (steps - 1),
+        embeddings,
         other_rows,
+        slot,
         other_ids,
-        own_laid,
-    )
-    arrived = [across(pieces[p], p) for p in (first, *middle, last)]
-    swapped = [swap_cores(x) for x in arrived]
-
-    early = arrived[:-1] + swapped[:-1]
-    late = [arrived[-1], swapped[-1]]
+    )
+    first_other = across(first_other, first)
+    rest = [across(piece, p) for piece, p in zip(rest, [*middle, last])]
+
+    first_both = call_kernel("join", join_kernel, whole, first_own, first_other, flops=10**10)
+    early = [first_both, *rest[:-1]]
+    early += [swap_cores(x) for x in early]
+    late = [rest[-1], swap_cores(rest[-1])]
     span = cores * capacity
+    half_way = span * (steps - 1)
     starts = [k * span for k in range(steps - 1)]
-    starts += [k * span + capacity for k in range(steps - 1, 2 * (steps - 1))]
+    starts += [half_way + start + capacity for start in starts]
     late_starts = [0, span + capacity]
 
     def places():

time: 45.6 us -> 44.8 us (0.982)
  starting transfers between devices: 15.6 us -> 19.4 us
  waiting for transfers between devices: 10.9 us -> 7.34 us
  blocking collectives: 13.4 us -> 12.4 us
    ppermute x4 -> x5, waiting for transfers between devices: 9.72 us -> 6.19 us  [across(): return lax.ppermute(x, ('owner', 'helper', 'sub'), pairs)]
    ppermute x4 -> x5, starting transfers between devices: 5.97 us -> 8.83 us  [across(): return lax.ppermute(x, ('owner', 'helper', 'sub'), pairs)]
    all_to_all x1, blocking collectives: 13.4 us -> 12.4 us  [body_by_chip(): lax.all_to_all(counts, ('owner', 'helper'), split_axis=0, concat_axis=0,...]
    ppermute x6, starting transfers between devices: 9.65 us -> 10.5 us  [swap_cores(): return lax.ppermute(x, 'sub', [(i, i ^ 1) for i in range(cores)])]
    pallas_call x5 -> x6, Pallas kernels: 4.19 us -> 4.21 us  [call_kernel(): pl.pallas_call(kernel, out_shape=out_shape, in_specs=[VMEM] * len(args),...]
  transfers between devices with their start and end apart: 10 -> 11, of which waited for: 2 -> 3; matrix products, arithmetic and copies ran while one was open for 0% -> 0% of each run, Pallas kernels for 4% -> 5%
where the time goes in v7:
time: 44.8 us; the launch traced here: 44.6 us
  starting transfers between devices  19.4 us (43%)
  blocking collectives  12.4 us (28%)
  waiting for transfers between devices  7.34 us (16%)
  Pallas kernels  4.21 us (9%)
  local copies, waits for them, and re-layouts  1.27 us (3%)
    all_to_all x1, blocking collectives, body_by_chip(): lax.all_to_all(counts, ('owner', 'helper'), split_axis=0, concat_axis=0,...  12.4 us
    ppermute x6, starting transfers between devices, swap_cores(): return lax.ppermute(x, 'sub', [(i, i ^ 1) for i in range(cores)])  10.5 us
    ppermute x5, starting transfers between devices, across(): return lax.ppermute(x, ('owner', 'helper', 'sub'), pairs)  8.83 us
    ppermute x5, waiting for transfers between devices, across(): return lax.ppermute(x, ('owner', 'helper', 'sub'), pairs)  6.19 us
    pallas_call x6, Pallas kernels, call_kernel(): pl.pallas_call(kernel, out_shape=out_shape, in_specs=[VMEM] * len(args),...  4.21 us
    unnamed x4, local copies, waits for them, and re-layouts  1.27 us
    ppermute x6, waiting for transfers between devices, swap_cores(): return lax.ppermute(x, 'sub', [(i, i ^ 1) for i in range(cores)])  1.15 us
  transfers between devices with their start and end apart: 11, of which 3 were waited for; matrix products, arithmetic and copies ran while one was open for 0% of the time, Pallas kernels for 5%

profile of v7, /device:TPU:0, one launch (start us, length us, event | category | flops | bytes accessed | tf_op | source)
XLA Modules:
  0.0 44.6 jit_solution(6415291714352814765)
XLA Ops:
  0.0 0.0 copy-start.1
  0.0 0.5 %collective-permute-start.1 = (bf16[256,1024]{1,0:T(8,128)(2,1)}, bf16[256,1024]{1,0:T(8,128)(2,1)S(1)}, u32[]{:S(2)}, u32[]{:S(2)}) collective-permute-start(bf16[256,1024]{1,0:T(8,128)(2,1)} %refs_0_.1), channel_id=1, source_target_pairs={{0,1},{1,0},{2,3},{3,2},{4,5},{5,4},{6,7},{7,6},{8,9},{9,8},{10,11... | collective-permute-start | bytes 1572872 | tf_op jit(solution)/shard_map/ppermute | solution.py:182
  0.5 0.2 copy-done.1
  0.7 0.5 %collective-permute-start.2 = (s32[1,256]{1,0:T(1,128)S(1)}, s32[1,256]{1,0:T(1,128)S(1)}, u32[]{:S(2)}, u32[]{:S(2)}) collective-permute-start(s32[1,256]{1,0:T(1,128)S(1)} %bitcast.2), channel_id=1, source_target_pairs={{0,1},{1,0},{2,3},{3,2},{4,5},{5,4},{6,7},{7,6},{8,9},{9,8},{10,11... | collective-permute-start | bytes 3080 | tf_op jit(solution)/shard_map/ppermute | solution.py:182
  1.1 0.0 copy-start
  1.1 1.0 %copy-done = bf16[256,1024]{1,0:T(8,128)(2,1)S(1)} copy-done((bf16[256,1024]{1,0:T(8,128)(2,1)S(1)}, bf16[256,1024]{1,0:T(8,128)(2,1)}, u32[]{:S(2)}) %copy-start) | copy-done | bytes 524312
  2.2 0.5 %route_first.1 = (bf16[64,1024]{1,0:T(8,128)(2,1)S(1)}, s32[1,256]{1,0:T(1,128)S(1)}) custom-call(bf16[256,1024]{1,0:T(8,128)(2,1)S(1)} %copy-done, s32[1,256]{1,0:T(1,128)S(1)} %bitcast.3), custom_call_target="tpu_custom_call" | custom-call | tf_op jit(solution)/shard_map/route_first/pallas_call | solution.py:92
  2.6 3.7 %collective-permute-start = (bf16[64,1024]{1,0:T(8,128)(2,1)S(1)}, bf16[64,1024]{1,0:T(8,128)(2,1)S(1)}, u32[]{:S(2)}, u32[]{:S(2)}) collective-permute-start(bf16[64,1024]{1,0:T(8,128)(2,1)S(1)} %get-tuple-element.11), channel_id=1, source_target_pairs={{0,8},{1,11},{2,10},{3,9},{4,12},{5,15},{6,14},{7,13},{8,0},{9,3},... | collective-permute-start | bytes 393224 | tf_op jit(solution)/shard_map/ppermute | solution.py:198
  6.3 0.0 collective-permute-done.2.refs_3_
  6.3 0.0 collective-permute-done.1.refs_1_
  6.3 0.7 %route_rest.1 = (bf16[64,1024]{1,0:T(8,128)(2,1)S(1)}, bf16[128,1024]{1,0:T(8,128)(2,1)S(1)}, bf16[128,1024]{1,0:T(8,128)(2,1)S(1)}, bf16[128,1024]{1,0:T(8,128)(2,1)S(1)}) custom-call(bf16[256,1024]{1,0:T(8,128)(2,1)S(1)} %copy-done, bf16[256,1024]{1,0:T(8,128)(2,1)S(1)} %collective-permute-done.1.refs_1_, s32[1,256]{1,0:T(1,128)S(1)} %get-tuple-element.12.refs_2_.slot_ref, ...), custom_call_target="tpu_custom_call" | custom-call | tf_op jit(solution)/shard_map/route_rest/pallas_call | solution.py:92
  7.0 0.1 collective-permute-start.3
  7.1 0.7 %collective-permute-start.4 = (bf16[128,1024]{1,0:T(8,128)(2,1)S(1)}, bf16[128,1024]{1,0:T(8,128)(2,1)S(1)}, u32[]{:S(2)}, u32[]{:S(2)}) collective-permute-start(bf16[128,1024]{1,0:T(8,128)(2,1)S(1)} %get-tuple-element.14), channel_id=1, source_target_pairs={{0,0},{1,3},{2,2},{3,1},{4,4},{5,7},{6,6},{7,5},{8,8},{9,11},{10,1... | collective-permute-start | bytes 786440 | tf_op jit(solution)/shard_map/ppermute | solution.py:198
  7.8 1.9 %collective-permute-start.5 = (bf16[128,1024]{1,0:T(8,128)(2,1)S(1)}, bf16[128,1024]{1,0:T(8,128)(2,1)S(1)}, u32[]{:S(2)}, u32[]{:S(2)}) collective-permute-start(bf16[128,1024]{1,0:T(8,128)(2,1)S(1)} %get-tuple-element.15), channel_id=1, source_target_pairs={{0,4},{1,7},{2,6},{3,5},{4,0},{5,3},{6,2},{7,1},{8,12},{9,15},{10,... | collective-permute-start | bytes 786440 | tf_op jit(solution)/shard_map/ppermute | solution.py:198
  9.8 2.5 %collective-permute-start.9 = (bf16[128,1024]{1,0:T(8,128)(2,1)S(1)}, bf16[128,1024]{1,0:T(8,128)(2,1)S(1)}, u32[]{:S(2)}, u32[]{:S(2)}) collective-permute-start(bf16[128,1024]{1,0:T(8,128)(2,1)S(1)} %get-tuple-element.16), channel_id=1, source_target_pairs={{0,12},{1,15},{2,14},{3,13},{4,8},{5,11},{6,10},{7,9},{8,4},{9,7},... | collective-permute-start | bytes 786440 | tf_op jit(solution)/shard_map/ppermute | solution.py:198
  12.2 3.2 %collective-permute-done.first_ref = bf16[64,1024]{1,0:T(8,128)(2,1)S(1)} collective-permute-done((bf16[64,1024]{1,0:T(8,128)(2,1)S(1)}, bf16[64,1024]{1,0:T(8,128)(2,1)S(1)}, u32[]{:S(2)}, u32[]{:S(2)}) %collective-permute-start) | collective-permute-done | bytes 131104 | tf_op jit(solution)/shard_map/ppermute | solution.py:198
  15.4 3.0 %collective-permute-done.3.second_ref = bf16[64,1024]{1,0:T(8,128)(2,1)S(1)} collective-permute-done((bf16[64,1024]{1,0:T(8,128)(2,1)S(1)}, bf16[64,1024]{1,0:T(8,128)(2,1)S(1)}, u32[]{:S(2)}, u32[]{:S(2)}) %collective-permute-start.3) | collective-permute-done | bytes 131104 | tf_op jit(solution)/shard_map/ppermute | solution.py:198
  18.4 0.9 %collective-permute-start.6 = (bf16[128,1024]{1,0:T(8,128)(2,1)S(1)}, bf16[128,1024]{1,0:T(8,128)(2,1)S(1)}, u32[]{:S(2)}, u32[]{:S(2)}) collective-permute-start(bf16[128,1024]{1,0:T(8,128)(2,1)S(1)} %join.1.refs_0_), channel_id=1, source_target_pairs={{0,1},{1,0},{2,3},{3,2},{4,5},{5,4},{6,7},{7,6},{8,9},{9,8},{10,11... | collective-permute-start | bytes 786440 | tf_op jit(solution)/shard_map/ppermute | solution.py:182
  19.4 0.0 collective-permute-done.4.refs_1_
  19.4 0.1 collective-permute-start.7
  19.5 0.0 collective-permute-done.5.refs_2_
  19.5 8.6 %collective-permute-start.8 = (bf16[128,1024]{1,0:T(8,128)(2,1)S(1)}, bf16[128,1024]{1,0:T(8,128)(2,1)S(1)}, u32[]{:S(2)}, u32[]{:S(2)}) collective-permute-start(bf16[128,1024]{1,0:T(8,128)(2,1)S(1)} %collective-permute-done.5.refs_2_), channel_id=1, source_target_pairs={{0,1},{1,0},{2,3},{3,2},{4,5},{5,4},{6,7},{7,6},{8,9},{9,8},{10,11... | collective-permute-start | bytes 786440 | tf_op jit(solution)/shard_map/ppermute | solution.py:182
  28.1 0.0 collective-permute-done.9.refs_6_
  28.1 0.0 collective-permute-start.10
  28.1 0.0 collective-permute-done.6.refs_3_
  28.1 0.0 collective-permute-done.7.refs_4_
  28.1 1.1 %collective-permute-done.8.refs_5_ = bf16[128,1024]{1,0:T(8,128)(2,1)S(1)} collective-permute-done((bf16[128,1024]{1,0:T(8,128)(2,1)S(1)}, bf16[128,1024]{1,0:T(8,128)(2,1)S(1)}, u32[]{:S(2)}, u32[]{:S(2)}) %collective-permute-start.8) | collective-permute-done | bytes 262176 | tf_op jit(solution)/shard_map/ppermute | solution.py:182
  29.2 1.2 %count.1.refs_8_ = f32[1,384]{1,0:T(1,128)S(1)} custom-call(bf16[128,1024]{1,0:T(8,128)(2,1)S(1)} %join.1.refs_0_, bf16[128,1024]{1,0:T(8,128)(2,1)S(1)} %collective-permute-done.4.refs_1_, bf16[128,1024]{1,0:T(8,128)(2,1)S(1)} %collective-permute-done.5.refs_2_, bf16[128,1024]{1,0:T(8,128)(2,1)S(1)} %collective-permute-done.6.refs_3_, ...), custom_call_target="tpu_custom_call" | custom-call | tf_op jit(solution)/shard_map/count/pallas_call | solution.py:92
  30.4 0.0 collective-permute-done.10.refs_7_
  30.4 1.1 %finish.1 = f32[8,1,64]{2,1,0:T(1,128)S(1)} custom-call(bf16[128,1024]{1,0:T(8,128)(2,1)S(1)} %join.1.refs_0_, bf16[128,1024]{1,0:T(8,128)(2,1)S(1)} %collective-permute-done.4.refs_1_, bf16[128,1024]{1,0:T(8,128)(2,1)S(1)} %collective-permute-done.5.refs_2_, bf16[128,1024]{1,0:T(8,128)(2,1)S(1)} %collective-permute-done.6.refs_3_, ...), custom_call_target="tpu_custom_call" | custom-call | tf_op jit(solution)/shard_map/finish/pallas_call | solution.py:92
  31.5 12.4 %all_to_all.5.counts_ref = f32[8,1,64]{2,1,0:T(1,128)S(1)} all-to-all(f32[8,1,64]{2,1,0:T(1,128)S(1)} %finish.1), channel_id=1, replica_groups=mesh['groups'=2,'owner'=4,'helper'=2,'sub'=2] {'owner','helper'}, dimensions={0} | all-to-all | bytes 4096 | tf_op jit(solution)/shard_map/all_to_all | solution.py:253
  43.9 0.7 %select.1 = f32[1,256]{1,0:T(1,128)} custom-call(f32[8,1,64]{2,1,0:T(1,128)S(1)} %all_to_all.5.counts_ref, s32[1,256]{1,0:T(1,128)S(1)} %get-tuple-element.12.refs_2_.slot_ref), custom_call_target="tpu_custom_call" | custom-call | tf_op jit(solution)/shard_map/select/pallas_call | solution.py:92
  (1 shorter events, 0.0 us)
Async XLA Ops:
  0.0 0.7 %copy-start.1 = (s32[256]{0:T(256)S(1)}, s32[256]{0:T(256)}, u32[]{:S(2)}) copy-start(s32[256]{0:T(256)} %param.3) | copy-start | bytes 3076
  0.0 6.3 %collective-permute-start.1 = (bf16[256,1024]{1,0:T(8,128)(2,1)}, bf16[256,1024]{1,0:T(8,128)(2,1)S(1)}, u32[]{:S(2)}, u32[]{:S(2)}) collective-permute-start(bf16[256,1024]{1,0:T(8,128)(2,1)} %refs_0_.1), channel_id=1, source_target_pairs={{0,1},{1,0},{2,3},{3,2},{4,5},{5,4},{6,7},{7,6},{8,9},{9,8},{10,11... | collective-permute-start | bytes 1572872 | tf_op jit(solution)/shard_map/ppermute | solution.py:182
  0.7 5.6 %collective-permute-start.2 = (s32[1,256]{1,0:T(1,128)S(1)}, s32[1,256]{1,0:T(1,128)S(1)}, u32[]{:S(2)}, u32[]{:S(2)}) collective-permute-start(s32[1,256]{1,0:T(1,128)S(1)} %bitcast.2), channel_id=1, source_target_pairs={{0,1},{1,0},{2,3},{3,2},{4,5},{5,4},{6,7},{7,6},{8,9},{9,8},{10,11... | collective-permute-start | bytes 3080 | tf_op jit(solution)/shard_map/ppermute | solution.py:182
  1.1 1.0 %copy-start = (bf16[256,1024]{1,0:T(8,128)(2,1)S(1)}, bf16[256,1024]{1,0:T(8,128)(2,1)}, u32[]{:S(2)}) copy-start(bf16[256,1024]{1,0:T(8,128)(2,1)} %refs_0_.1) | copy-start | bytes 1572868
  2.6 12.8 %collective-permute-start = (bf16[64,1024]{1,0:T(8,128)(2,1)S(1)}, bf16[64,1024]{1,0:T(8,128)(2,1)S(1)}, u32[]{:S(2)}, u32[]{:S(2)}) collective-permute-start(bf16[64,1024]{1,0:T(8,128)(2,1)S(1)} %get-tuple-element.11), channel_id=1, source_target_pairs={{0,8},{1,11},{2,10},{3,9},{4,12},{5,15},{6,14},{7,13},{8,0},{9,3},... | collective-permute-start | bytes 393224 | tf_op jit(solution)/shard_map/ppermute | solution.py:198
  7.0 11.4 %collective-permute-start.3 = (bf16[64,1024]{1,0:T(8,128)(2,1)S(1)}, bf16[64,1024]{1,0:T(8,128)(2,1)S(1)}, u32[]{:S(2)}, u32[]{:S(2)}) collective-permute-start(bf16[64,1024]{1,0:T(8,128)(2,1)S(1)} %get-tuple-element.13), channel_id=1, source_target_pairs={{0,8},{1,11},{2,10},{3,9},{4,12},{5,15},{6,14},{7,13},{8,0},{9,3},... | collective-permute-start | bytes 393224 | tf_op jit(solution)/shard_map/ppermute | solution.py:198
  7.1 12.3 %collective-permute-start.4 = (bf16[128,1024]{1,0:T(8,128)(2,1)S(1)}, bf16[128,1024]{1,0:T(8,128)(2,1)S(1)}, u32[]{:S(2)}, u32[]{:S(2)}) collective-permute-start(bf16[128,1024]{1,0:T(8,128)(2,1)S(1)} %get-tuple-element.14), channel_id=1, source_target_pairs={{0,0},{1,3},{2,2},{3,1},{4,4},{5,7},{6,6},{7,5},{8,8},{9,11},{10,1... | collective-permute-start | bytes 786440 | tf_op jit(solution)/shard_map/ppermute | solution.py:198
  7.8 11.7 %collective-permute-start.5 = (bf16[128,1024]{1,0:T(8,128)(2,1)S(1)}, bf16[128,1024]{1,0:T(8,128)(2,1)S(1)}, u32[]{:S(2)}, u32[]{:S(2)}) collective-permute-start(bf16[128,1024]{1,0:T(8,128)(2,1)S(1)} %get-tuple-element.15), channel_id=1, source_target_pairs={{0,4},{1,7},{2,6},{3,5},{4,0},{5,3},{6,2},{7,1},{8,12},{9,15},{10,... | collective-permute-start | bytes 786440 | tf_op jit(solution)/shard_map/ppermute | solution.py:198
  9.8 18.3 %collective-permute-start.9 = (bf16[128,1024]{1,0:T(8,128)(2,1)S(1)}, bf16[128,1024]{1,0:T(8,128)(2,1)S(1)}, u32[]{:S(2)}, u32[]{:S(2)}) collective-permute-start(bf16[128,1024]{1,0:T(8,128)(2,1)S(1)} %get-tuple-element.16), channel_id=1, source_target_pairs={{0,12},{1,15},{2,14},{3,13},{4,8},{5,11},{6,10},{7,9},{8,4},{9,7},... | collective-permute-start | bytes 786440 | tf_op jit(solution)/shard_map/ppermute | solution.py:198
  18.4 9.6 %collective-permute-start.6 = (bf16[128,1024]{1,0:T(8,128)(2,1)S(1)}, bf16[128,1024]{1,0:T(8,128)(2,1)S(1)}, u32[]{:S(2)}, u32[]{:S(2)}) collective-permute-start(bf16[128,1024]{1,0:T(8,128)(2,1)S(1)} %join.1.refs_0_), channel_id=1, source_target_pairs={{0,1},{1,0},{2,3},{3,2},{4,5},{5,4},{6,7},{7,6},{8,9},{9,8},{10,11... | collective-permute-start | bytes 786440 | tf_op jit(solution)/shard_map/ppermute | solution.py:182
  19.4 8.7 %collective-permute-start.7 = (bf16[128,1024]{1,0:T(8,128)(2,1)S(1)}, bf16[128,1024]{1,0:T(8,128)(2,1)S(1)}, u32[]{:S(2)}, u32[]{:S(2)}) collective-permute-start(bf16[128,1024]{1,0:T(8,128)(2,1)S(1)} %collective-permute-done.4.refs_1_), channel_id=1, source_target_pairs={{0,1},{1,0},{2,3},{3,2},{4,5},{5,4},{6,7},{7,6},{8,9},{9,8},{10,11... | collective-permute-start | bytes 786440 | tf_op jit(solution)/shard_map/ppermute | solution.py:182
  19.5 9.8 %collective-permute-start.8 = (bf16[128,1024]{1,0:T(8,128)(2,1)S(1)}, bf16[128,1024]{1,0:T(8,128)(2,1)S(1)}, u32[]{:S(2)}, u32[]{:S(2)}) collective-permute-start(bf16[128,1024]{1,0:T(8,128)(2,1)S(1)} %collective-permute-done.5.refs_2_), channel_id=1, source_target_pairs={{0,1},{1,0},{2,3},{3,2},{4,5},{5,4},{6,7},{7,6},{8,9},{9,8},{10,11... | collective-permute-start | bytes 786440 | tf_op jit(solution)/shard_map/ppermute | solution.py:182
  28.1 2.3 %collective-permute-start.10 = (bf16[128,1024]{1,0:T(8,128)(2,1)S(1)}, bf16[128,1024]{1,0:T(8,128)(2,1)S(1)}, u32[]{:S(2)}, u32[]{:S(2)}) collective-permute-start(bf16[128,1024]{1,0:T(8,128)(2,1)S(1)} %collective-permute-done.9.refs_6_), channel_id=1, source_target_pairs={{0,1},{1,0},{2,3},{3,2},{4,5},{5,4},{6,7},{7,6},{8,9},{9,8},{10,11... | collective-permute-start | bytes 786440 | tf_op jit(solution)/shard_map/ppermute | solution.py:182

commit v8 on v7

--- a/solution.py
+++ b/solution.py
@@ -67,18 +67,20 @@
     piece_ref[...] = lay(rows_ref, slots_of_steps(slot, capacity, [step]), capacity)
 
 
-def route_rest_kernel(clusters, capacity, first, steps, *refs):
-    own_rows, other_rows, own_slot, other_ids, first_ref, *piece_refs = refs
+def route_rest_kernel(clusters, capacity, halves, steps, *refs):
+    own_rows, other_rows, own_slot, other_ids, *piece_refs = refs
+    half_refs, whole_refs = piece_refs[: len(halves)], piece_refs[len(halves) :]
     slot = slots_of_steps(own_slot[...], capacity, steps)
     laid = lay(own_rows, slot, len(steps) * capacity)
-    for k, piece in enumerate(piece_refs):
+    for k, piece in enumerate(whole_refs):
         piece[:capacity] = laid[k * capacity : (k + 1) * capacity]
     slot = slots_of(other_ids[...], clusters, capacity)
-    slot = slots_of_steps(slot, capacity, [first, *steps])
-    laid = lay(other_rows, slot, (1 + len(steps)) * capacity)
-    first_ref[...] = laid[:capacity]
-    for k, piece in enumerate(piece_refs):
-        piece[capacity:] = laid[(k + 1) * capacity : (k + 2) * capacity]
+    slot = slots_of_steps(slot, capacity, [*halves, *steps])
+    laid = lay(other_rows, slot, (len(halves) + len(steps)) * capacity)
+    for k, piece in enumerate(half_refs):
+        piece[...] = laid[k * capacity : (k + 1) * capacity]
+    for k, piece in enumerate(whole_refs, len(halves)):
+        piece[capacity:] = laid[k * capacity : (k + 1) * capacity]
 
 
 def route_kernel(clusters, capacity, rows_ref, ids_ref, piece_ref, slot_ref):
@@ -212,22 +214,27 @@
         ids,
     )
     first_own = across(first_own, first)
-    first_other, *rest = call_kernel(
-        "route_rest",
-        functools.partial(route_rest_kernel, clusters, capacity, first, [*middle, last]),
-        [half] + [whole] * (steps - 1),
-        embeddings,
-        other_rows,
-        slot,
-        other_ids,
-    )
-    first_other = across(first_other, first)
-    rest = [across(piece, p) for piece, p in zip(rest, [*middle, last])]
+
+    def route_rest(name, halves, steps):
+        return call_kernel(
+            name,
+            functools.partial(route_rest_kernel, clusters, capacity, halves, steps),
+            [half] * len(halves) + [whole] * len(steps),
+            embeddings,
+            other_rows,
+            slot,
+            other_ids,
+        )
+
+    first_other, last_piece = route_rest("route_far", [first], [last])
+    first_other, last_piece = across(first_other, first), across(last_piece, last)
+    near = route_rest("route_near", [], middle)
+    near = [across(piece, p) for piece, p in zip(near, middle)]
 
     first_both = call_kernel("join", join_kernel, whole, first_own, first_other, flops=10**10)
-    early = [first_both, *rest[:-1]]
+    early = [first_both, *near]
     early += [swap_cores(x) for x in early]
-    late = [rest[-1], swap_cores(rest[-1])]
+    late = [last_piece, swap_cores(last_piece)]
     span = cores * capacity
     half_way = span * (steps - 1)
     starts = [k * span for k in range(steps - 1)]

time: 44.8 us -> 45.5 us (1.016)
  waiting for transfers between devices: 7.34 us -> 18 us
  starting transfers between devices: 19.4 us -> 11 us
  blocking collectives: 12.4 us -> 10.2 us
  Pallas kernels: 4.21 us -> 4.67 us
    ppermute x5, waiting for transfers between devices: 6.19 us -> 16.9 us  [across(): return lax.ppermute(x, ('owner', 'helper', 'sub'), pairs)]
    ppermute x6, starting transfers between devices: 10.5 us -> 2.6 us  [swap_cores(): return lax.ppermute(x, 'sub', [(i, i ^ 1) for i in range(cores)])]
    all_to_all x1, blocking collectives: 12.4 us -> 10.2 us  [body_by_chip(): lax.all_to_all(counts, ('owner', 'helper'), split_axis=0, concat_axis=0,...]
    pallas_call x6 -> x7, Pallas kernels: 4.21 us -> 4.67 us  [call_kernel(): pl.pallas_call(kernel, out_shape=out_shape, in_specs=[VMEM] * len(args),...]
  transfers between devices with their start and end apart: 11 -> 11, of which waited for: 3 -> 4; matrix products, arithmetic and copies ran while one was open for 0% -> 0% of each run, Pallas kernels for 5% -> 6%
where the time goes in v8:
time: 45.5 us; the launch traced here: 45.3 us
  waiting for transfers between devices  18 us (40%)
  starting transfers between devices  11 us (24%)
  blocking collectives  10.2 us (22%)
  Pallas kernels  4.67 us (10%)
  local copies, waits for them, and re-layouts  1.27 us (3%)
    ppermute x5, waiting for transfers between devices, across(): return lax.ppermute(x, ('owner', 'helper', 'sub'), pairs)  16.9 us
    all_to_all x1, blocking collectives, body_by_chip(): lax.all_to_all(counts, ('owner', 'helper'), split_axis=0, concat_axis=0,...  10.2 us
    ppermute x5, starting transfers between devices, across(): return lax.ppermute(x, ('owner', 'helper', 'sub'), pairs)  8.4 us
    pallas_call x7, Pallas kernels, call_kernel(): pl.pallas_call(kernel, out_shape=out_shape, in_specs=[VMEM] * len(args),...  4.67 us
    ppermute x6, starting transfers between devices, swap_cores(): return lax.ppermute(x, 'sub', [(i, i ^ 1) for i in range(cores)])  2.6 us
    unnamed x4, local copies, waits for them, and re-layouts  1.27 us
    ppermute x6, waiting for transfers between devices, swap_cores(): return lax.ppermute(x, 'sub', [(i, i ^ 1) for i in range(cores)])  1.15 us
  transfers between devices with their start and end apart: 11, of which 4 were waited for; matrix products, arithmetic and copies ran while one was open for 0% of the time, Pallas kernels for 6%

profile of v8, /device:TPU:0, one launch (start us, length us, event | category | flops | bytes accessed | tf_op | source)
XLA Modules:
  0.0 45.3 jit_solution(17159565829174053005)
XLA Ops:
  0.0 0.0 copy-start.1
  0.0 0.5 collective-permute-start.1
  0.5 0.2 copy-done.1
  0.7 0.5 collective-permute-start.2
  1.1 1.0 %copy-done = bf16[256,1024]{1,0:T(8,128)(2,1)S(1)} copy-done((bf16[256,1024]{1,0:T(8,128)(2,1)S(1)}, bf16[256,1024]{1,0:T(8,128)(2,1)}, u32[]{:S(2)}) %copy-start) | copy-done | bytes 524312
  2.2 0.5 %route_first.1 = (bf16[64,1024]{1,0:T(8,128)(2,1)S(1)}, s32[1,256]{1,0:T(1,128)S(1)}) custom-call(bf16[256,1024]{1,0:T(8,128)(2,1)S(1)} %copy-done, s32[1,256]{1,0:T(1,128)S(1)} %bitcast.3), custom_call_target="tpu_custom_call" | custom-call | tf_op jit(solution)/shard_map/route_first/pallas_call | solution.py:94
  2.6 3.7 %collective-permute-start = (bf16[64,1024]{1,0:T(8,128)(2,1)S(1)}, bf16[64,1024]{1,0:T(8,128)(2,1)S(1)}, u32[]{:S(2)}, u32[]{:S(2)}) collective-permute-start(bf16[64,1024]{1,0:T(8,128)(2,1)S(1)} %get-tuple-element.11), channel_id=1, source_target_pairs={{0,8},{1,11},{2,10},{3,9},{4,12},{5,15},{6,14},{7,13},{8,0},{9,3},... | collective-permute-start | bytes 393224 | tf_op jit(solution)/shard_map/ppermute | solution.py:200
  6.3 0.0 collective-permute-done.2.refs_3_
  6.3 0.0 collective-permute-done.1.refs_1_
  6.3 0.6 %route_far.1 = (bf16[64,1024]{1,0:T(8,128)(2,1)S(1)}, bf16[128,1024]{1,0:T(8,128)(2,1)S(1)}) custom-call(bf16[256,1024]{1,0:T(8,128)(2,1)S(1)} %copy-done, bf16[256,1024]{1,0:T(8,128)(2,1)S(1)} %collective-permute-done.1.refs_1_, s32[1,256]{1,0:T(1,128)S(1)} %get-tuple-element.12.refs_2_.slot_ref, s32[1,256]{1,0:T(1,128)S(1)} %collective-permute-done.2.refs_3_), custom_call_target="tpu_custom_call" | custom-call | tf_op jit(solution)/shard_map/route_far/pallas_call | solution.py:94
  6.9 0.1 collective-permute-start.3
  7.0 3.9 %collective-permute-start.9 = (bf16[128,1024]{1,0:T(8,128)(2,1)S(1)}, bf16[128,1024]{1,0:T(8,128)(2,1)S(1)}, u32[]{:S(2)}, u32[]{:S(2)}) collective-permute-start(bf16[128,1024]{1,0:T(8,128)(2,1)S(1)} %get-tuple-element.16), channel_id=1, source_target_pairs={{0,12},{1,15},{2,14},{3,13},{4,8},{5,11},{6,10},{7,9},{8,4},{9,7},... | collective-permute-start | bytes 786440 | tf_op jit(solution)/shard_map/ppermute | solution.py:200
  10.9 0.6 %route_near.1 = (bf16[128,1024]{1,0:T(8,128)(2,1)S(1)}, bf16[128,1024]{1,0:T(8,128)(2,1)S(1)}) custom-call(bf16[256,1024]{1,0:T(8,128)(2,1)S(1)} %copy-done, bf16[256,1024]{1,0:T(8,128)(2,1)S(1)} %collective-permute-done.1.refs_1_, s32[1,256]{1,0:T(1,128)S(1)} %get-tuple-element.12.refs_2_.slot_ref, s32[1,256]{1,0:T(1,128)S(1)} %collective-permute-done.2.refs_3_), custom_call_target="tpu_custom_call" | custom-call | tf_op jit(solution)/shard_map/route_near/pallas_call | solution.py:94
  11.5 0.7 %collective-permute-start.4 = (bf16[128,1024]{1,0:T(8,128)(2,1)S(1)}, bf16[128,1024]{1,0:T(8,128)(2,1)S(1)}, u32[]{:S(2)}, u32[]{:S(2)}) collective-permute-start(bf16[128,1024]{1,0:T(8,128)(2,1)S(1)} %get-tuple-element.14), channel_id=1, source_target_pairs={{0,0},{1,3},{2,2},{3,1},{4,4},{5,7},{6,6},{7,5},{8,8},{9,11},{10,1... | collective-permute-start | bytes 786440 | tf_op jit(solution)/shard_map/ppermute | solution.py:200
  12.2 0.1 collective-permute-start.5
  12.3 8.9 %collective-permute-done.first_ref = bf16[64,1024]{1,0:T(8,128)(2,1)S(1)} collective-permute-done((bf16[64,1024]{1,0:T(8,128)(2,1)S(1)}, bf16[64,1024]{1,0:T(8,128)(2,1)S(1)}, u32[]{:S(2)}, u32[]{:S(2)}) %collective-permute-start) | collective-permute-done | bytes 131104 | tf_op jit(solution)/shard_map/ppermute | solution.py:200
  21.2 2.8 %collective-permute-done.3.second_ref = bf16[64,1024]{1,0:T(8,128)(2,1)S(1)} collective-permute-done((bf16[64,1024]{1,0:T(8,128)(2,1)S(1)}, bf16[64,1024]{1,0:T(8,128)(2,1)S(1)}, u32[]{:S(2)}, u32[]{:S(2)}) %collective-permute-start.3) | collective-permute-done | bytes 131104 | tf_op jit(solution)/shard_map/ppermute | solution.py:200
  24.1 0.9 %collective-permute-start.6 = (bf16[128,1024]{1,0:T(8,128)(2,1)S(1)}, bf16[128,1024]{1,0:T(8,128)(2,1)S(1)}, u32[]{:S(2)}, u32[]{:S(2)}) collective-permute-start(bf16[128,1024]{1,0:T(8,128)(2,1)S(1)} %join.1.refs_0_), channel_id=1, source_target_pairs={{0,1},{1,0},{2,3},{3,2},{4,5},{5,4},{6,7},{7,6},{8,9},{9,8},{10,11... | collective-permute-start | bytes 786440 | tf_op jit(solution)/shard_map/ppermute | solution.py:184
  25.0 0.0 collective-permute-done.4.refs_1_
  25.0 0.1 collective-permute-start.7
  25.1 5.1 %collective-permute-done.5.refs_2_ = bf16[128,1024]{1,0:T(8,128)(2,1)S(1)} collective-permute-done((bf16[128,1024]{1,0:T(8,128)(2,1)S(1)}, bf16[128,1024]{1,0:T(8,128)(2,1)S(1)}, u32[]{:S(2)}, u32[]{:S(2)}) %collective-permute-start.5) | collective-permute-done | bytes 262176 | tf_op jit(solution)/shard_map/ppermute | solution.py:200
  30.2 0.7 %collective-permute-start.8 = (bf16[128,1024]{1,0:T(8,128)(2,1)S(1)}, bf16[128,1024]{1,0:T(8,128)(2,1)S(1)}, u32[]{:S(2)}, u32[]{:S(2)}) collective-permute-start(bf16[128,1024]{1,0:T(8,128)(2,1)S(1)} %collective-permute-done.5.refs_2_), channel_id=1, source_target_pairs={{0,1},{1,0},{2,3},{3,2},{4,5},{5,4},{6,7},{7,6},{8,9},{9,8},{10,11... | collective-permute-start | bytes 786440 | tf_op jit(solution)/shard_map/ppermute | solution.py:184
  30.9 0.0 collective-permute-done.9.refs_6_
  30.9 0.0 collective-permute-start.10
  30.9 0.0 collective-permute-done.6.refs_3_
  30.9 0.0 collective-permute-done.7.refs_4_
  30.9 1.1 %collective-permute-done.8.refs_5_ = bf16[128,1024]{1,0:T(8,128)(2,1)S(1)} collective-permute-done((bf16[128,1024]{1,0:T(8,128)(2,1)S(1)}, bf16[128,1024]{1,0:T(8,128)(2,1)S(1)}, u32[]{:S(2)}, u32[]{:S(2)}) %collective-permute-start.8) | collective-permute-done | bytes 262176 | tf_op jit(solution)/shard_map/ppermute | solution.py:184
  32.0 1.1 %count.1.refs_8_ = f32[1,384]{1,0:T(1,128)S(1)} custom-call(bf16[128,1024]{1,0:T(8,128)(2,1)S(1)} %join.1.refs_0_, bf16[128,1024]{1,0:T(8,128)(2,1)S(1)} %collective-permute-done.4.refs_1_, bf16[128,1024]{1,0:T(8,128)(2,1)S(1)} %collective-permute-done.5.refs_2_, bf16[128,1024]{1,0:T(8,128)(2,1)S(1)} %collective-permute-done.6.refs_3_, ...), custom_call_target="tpu_custom_call" | custom-call | tf_op jit(solution)/shard_map/count/pallas_call | solution.py:94
  33.2 0.0 collective-permute-done.10.refs_7_
  33.2 1.1 %finish.1 = f32[8,1,64]{2,1,0:T(1,128)S(1)} custom-call(bf16[128,1024]{1,0:T(8,128)(2,1)S(1)} %join.1.refs_0_, bf16[128,1024]{1,0:T(8,128)(2,1)S(1)} %collective-permute-done.4.refs_1_, bf16[128,1024]{1,0:T(8,128)(2,1)S(1)} %collective-permute-done.5.refs_2_, bf16[128,1024]{1,0:T(8,128)(2,1)S(1)} %collective-permute-done.6.refs_3_, ...), custom_call_target="tpu_custom_call" | custom-call | tf_op jit(solution)/shard_map/finish/pallas_call | solution.py:94
  34.3 10.2 %all_to_all.5.counts_ref = f32[8,1,64]{2,1,0:T(1,128)S(1)} all-to-all(f32[8,1,64]{2,1,0:T(1,128)S(1)} %finish.1), channel_id=1, replica_groups=mesh['groups'=2,'owner'=4,'helper'=2,'sub'=2] {'owner','helper'}, dimensions={0} | all-to-all | bytes 4096 | tf_op jit(solution)/shard_map/all_to_all | solution.py:260
  44.5 0.7 %select.1 = f32[1,256]{1,0:T(1,128)} custom-call(f32[8,1,64]{2,1,0:T(1,128)S(1)} %all_to_all.5.counts_ref, s32[1,256]{1,0:T(1,128)S(1)} %get-tuple-element.12.refs_2_.slot_ref), custom_call_target="tpu_custom_call" | custom-call | tf_op jit(solution)/shard_map/select/pallas_call | solution.py:94
  (2 shorter events, 0.0 us)
Async XLA Ops:
  0.0 0.7 %copy-start.1 = (s32[256]{0:T(256)S(1)}, s32[256]{0:T(256)}, u32[]{:S(2)}) copy-start(s32[256]{0:T(256)} %param.3) | copy-start | bytes 3076
  0.0 6.3 %collective-permute-start.1 = (bf16[256,1024]{1,0:T(8,128)(2,1)}, bf16[256,1024]{1,0:T(8,128)(2,1)S(1)}, u32[]{:S(2)}, u32[]{:S(2)}) collective-permute-start(bf16[256,1024]{1,0:T(8,128)(2,1)} %refs_0_.3), channel_id=1, source_target_pairs={{0,1},{1,0},{2,3},{3,2},{4,5},{5,4},{6,7},{7,6},{8,9},{9,8},{10,11... | collective-permute-start | bytes 1572872 | tf_op jit(solution)/shard_map/ppermute | solution.py:184
  0.7 5.6 %collective-permute-start.2 = (s32[1,256]{1,0:T(1,128)S(1)}, s32[1,256]{1,0:T(1,128)S(1)}, u32[]{:S(2)}, u32[]{:S(2)}) collective-permute-start(s32[1,256]{1,0:T(1,128)S(1)} %bitcast.2), channel_id=1, source_target_pairs={{0,1},{1,0},{2,3},{3,2},{4,5},{5,4},{6,7},{7,6},{8,9},{9,8},{10,11... | collective-permute-start | bytes 3080 | tf_op jit(solution)/shard_map/ppermute | solution.py:184
  1.1 1.0 %copy-start = (bf16[256,1024]{1,0:T(8,128)(2,1)S(1)}, bf16[256,1024]{1,0:T(8,128)(2,1)}, u32[]{:S(2)}) copy-start(bf16[256,1024]{1,0:T(8,128)(2,1)} %refs_0_.3) | copy-start | bytes 1572868
  2.6 18.6 %collective-permute-start = (bf16[64,1024]{1,0:T(8,128)(2,1)S(1)}, bf16[64,1024]{1,0:T(8,128)(2,1)S(1)}, u32[]{:S(2)}, u32[]{:S(2)}) collective-permute-start(bf16[64,1024]{1,0:T(8,128)(2,1)S(1)} %get-tuple-element.11), channel_id=1, source_target_pairs={{0,8},{1,11},{2,10},{3,9},{4,12},{5,15},{6,14},{7,13},{8,0},{9,3},... | collective-permute-start | bytes 393224 | tf_op jit(solution)/shard_map/ppermute | solution.py:200
  6.9 17.1 %collective-permute-start.3 = (bf16[64,1024]{1,0:T(8,128)(2,1)S(1)}, bf16[64,1024]{1,0:T(8,128)(2,1)S(1)}, u32[]{:S(2)}, u32[]{:S(2)}) collective-permute-start(bf16[64,1024]{1,0:T(8,128)(2,1)S(1)} %get-tuple-element.13), channel_id=1, source_target_pairs={{0,8},{1,11},{2,10},{3,9},{4,12},{5,15},{6,14},{7,13},{8,0},{9,3},... | collective-permute-start | bytes 393224 | tf_op jit(solution)/shard_map/ppermute | solution.py:200
  7.0 23.9 %collective-permute-start.9 = (bf16[128,1024]{1,0:T(8,128)(2,1)S(1)}, bf16[128,1024]{1,0:T(8,128)(2,1)S(1)}, u32[]{:S(2)}, u32[]{:S(2)}) collective-permute-start(bf16[128,1024]{1,0:T(8,128)(2,1)S(1)} %get-tuple-element.16), channel_id=1, source_target_pairs={{0,12},{1,15},{2,14},{3,13},{4,8},{5,11},{6,10},{7,9},{8,4},{9,7},... | collective-permute-start | bytes 786440 | tf_op jit(solution)/shard_map/ppermute | solution.py:200
  11.5 13.5 %collective-permute-start.4 = (bf16[128,1024]{1,0:T(8,128)(2,1)S(1)}, bf16[128,1024]{1,0:T(8,128)(2,1)S(1)}, u32[]{:S(2)}, u32[]{:S(2)}) collective-permute-start(bf16[128,1024]{1,0:T(8,128)(2,1)S(1)} %get-tuple-element.14), channel_id=1, source_target_pairs={{0,0},{1,3},{2,2},{3,1},{4,4},{5,7},{6,6},{7,5},{8,8},{9,11},{10,1... | collective-permute-start | bytes 786440 | tf_op jit(solution)/shard_map/ppermute | solution.py:200
  12.2 18.0 %collective-permute-start.5 = (bf16[128,1024]{1,0:T(8,128)(2,1)S(1)}, bf16[128,1024]{1,0:T(8,128)(2,1)S(1)}, u32[]{:S(2)}, u32[]{:S(2)}) collective-permute-start(bf16[128,1024]{1,0:T(8,128)(2,1)S(1)} %get-tuple-element.15), channel_id=1, source_target_pairs={{0,4},{1,7},{2,6},{3,5},{4,0},{5,3},{6,2},{7,1},{8,12},{9,15},{10,... | collective-permute-start | bytes 786440 | tf_op jit(solution)/shard_map/ppermute | solution.py:200
  24.1 6.8 %collective-permute-start.6 = (bf16[128,1024]{1,0:T(8,128)(2,1)S(1)}, bf16[128,1024]{1,0:T(8,128)(2,1)S(1)}, u32[]{:S(2)}, u32[]{:S(2)}) collective-permute-start(bf16[128,1024]{1,0:T(8,128)(2,1)S(1)} %join.1.refs_0_), channel_id=1, source_target_pairs={{0,1},{1,0},{2,3},{3,2},{4,5},{5,4},{6,7},{7,6},{8,9},{9,8},{10,11... | collective-permute-start | bytes 786440 | tf_op jit(solution)/shard_map/ppermute | solution.py:184
  25.0 5.9 %collective-permute-start.7 = (bf16[128,1024]{1,0:T(8,128)(2,1)S(1)}, bf16[128,1024]{1,0:T(8,128)(2,1)S(1)}, u32[]{:S(2)}, u32[]{:S(2)}) collective-permute-start(bf16[128,1024]{1,0:T(8,128)(2,1)S(1)} %collective-permute-done.4.refs_1_), channel_id=1, source_target_pairs={{0,1},{1,0},{2,3},{3,2},{4,5},{5,4},{6,7},{7,6},{8,9},{9,8},{10,11... | collective-permute-start | bytes 786440 | tf_op jit(solution)/shard_map/ppermute | solution.py:184
  30.2 1.8 %collective-permute-start.8 = (bf16[128,1024]{1,0:T(8,128)(2,1)S(1)}, bf16[128,1024]{1,0:T(8,128)(2,1)S(1)}, u32[]{:S(2)}, u32[]{:S(2)}) collective-permute-start(bf16[128,1024]{1,0:T(8,128)(2,1)S(1)} %collective-permute-done.5.refs_2_), channel_id=1, source_target_pairs={{0,1},{1,0},{2,3},{3,2},{4,5},{5,4},{6,7},{7,6},{8,9},{9,8},{10,11... | collective-permute-start | bytes 786440 | tf_op jit(solution)/shard_map/ppermute | solution.py:184
  30.9 2.3 %collective-permute-start.10 = (bf16[128,1024]{1,0:T(8,128)(2,1)S(1)}, bf16[128,1024]{1,0:T(8,128)(2,1)S(1)}, u32[]{:S(2)}, u32[]{:S(2)}) collective-permute-start(bf16[128,1024]{1,0:T(8,128)(2,1)S(1)} %collective-permute-done.9.refs_6_), channel_id=1, source_target_pairs={{0,1},{1,0},{2,3},{3,2},{4,5},{5,4},{6,7},{7,6},{8,9},{9,8},{10,11... | collective-permute-start | bytes 786440 | tf_op jit(solution)/shard_map/ppermute | solution.py:184

commit v9 on v7

--- a/solution.py
+++ b/solution.py
@@ -16,7 +16,9 @@
 
 EMPTY = 4.0
 TILE = 256
+CHUNKS = 4
 VMEM = pl.BlockSpec(memory_space=pltpu.VMEM)
+ANY = pl.BlockSpec(memory_space=pl.ANY)
 
 
 def chip_index():
@@ -36,18 +38,24 @@
     return ids * capacity + rank
 
 
-def lay(rows_ref, slot, slots):
-    doc_count, feature_count = rows_ref.shape
-    dispatch = lax.broadcasted_iota(jnp.int32, (slots, doc_count), 0) == slot
-    filled = jnp.sum(dispatch.astype(jnp.float32), axis=1, keepdims=True) > 0
-    laid = jnp.dot(
-        dispatch.astype(jnp.bfloat16), rows_ref[...], preferred_element_type=jnp.float32
-    )
+def mark_and_scale(laid, filled):
     factor = lax.rsqrt(
         jnp.mean(laid * laid, axis=-1, keepdims=True) + epsilon
-    ) * feature_count ** (-0.5)
+    ) * laid.shape[1] ** (-0.5)
     lane = lax.broadcasted_iota(jnp.int32, laid.shape, 1)
     return jnp.where(filled | (lane > 0), laid * factor, EMPTY).astype(jnp.bfloat16)
+
+
+def dispatch_of(slot, slots):
+    dispatch = lax.broadcasted_iota(jnp.int32, (slots, slot.shape[1]), 0) == slot
+    filled = jnp.sum(dispatch.astype(jnp.float32), axis=1, keepdims=True) > 0
+    return dispatch.astype(jnp.bfloat16), filled
+
+
+def lay(rows_ref, slot, slots):
+    dispatch, filled = dispatch_of(slot, slots)
+    laid = jnp.dot(dispatch, rows_ref[...], preferred_element_type=jnp.float32)
+    return mark_and_scale(laid, filled)
 
 
 def slots_of_steps(slot, capacity, steps):
@@ -61,10 +69,30 @@
     return jnp.where(step < 0, -1, step * capacity + rank)
 
 
-def route_first_kernel(clusters, capacity, step, rows_ref, ids_ref, piece_ref, slot_ref):
-    slot = slots_of(ids_ref[...], clusters, capacity)
+def route_first_kernel(clusters, capacity, step, *refs):
+    rows_ref, ids_ref, piece_ref, slot_ref, rows, ids, row_sems, ids_sem = refs
+    ids_copy = pltpu.make_async_copy(ids_ref, ids, ids_sem)
+    ids_copy.start()
+    chunk = rows.shape[0] // CHUNKS
+    parts = [pl.ds(k * chunk, chunk) for k in range(CHUNKS)]
+    copies = [
+        pltpu.make_async_copy(rows_ref.at[part], rows.at[part], row_sems.at[k])
+        for k, part in enumerate(parts)
+    ]
+    for copy in copies:
+        copy.start()
+    ids_copy.wait()
+    slot = slots_of(ids[...], clusters, capacity)
     slot_ref[...] = slot
-    piece_ref[...] = lay(rows_ref, slots_of_steps(slot, capacity, [step]), capacity)
+    dispatch, filled = dispatch_of(slots_of_steps(slot, capacity, [step]), capacity)
+    laid = jnp.zeros(piece_ref.shape, jnp.float32)
+    for k, copy in enumerate(copies):
+        copy.wait()
+        columns = slice(k * chunk, (k + 1) * chunk)
+        laid = laid + jnp.dot(
+            dispatch[:, columns], rows[columns], preferred_element_type=jnp.float32
+        )
+    piece_ref[...] = mark_and_scale(laid, filled)
 
 
 def route_rest_kernel(clusters, capacity, first, steps, *refs):
@@ -87,13 +115,14 @@
     piece_ref[...] = lay(rows_ref, slot, piece_ref.shape[0])
 
 
-def call_kernel(name, kernel, out_shape, *args, limit=32 * 2**20, flops=0):
+def call_kernel(name, kernel, out_shape, *args, limit=32 * 2**20, flops=0, scratch=()):
     cost = pl.CostEstimate(flops=flops, bytes_accessed=0, transcendentals=0) if flops else None
     return pl.pallas_call(
         kernel,
         out_shape=out_shape,
-        in_specs=[VMEM] * len(args),
+        in_specs=[ANY if scratch else VMEM] * len(args),
         out_specs=jax.tree.map(lambda _: VMEM, out_shape),
+        scratch_shapes=scratch,
         compiler_params=pltpu.CompilerParams(vmem_limit_bytes=limit),
         cost_estimate=cost,
         name=name,
@@ -210,6 +239,13 @@
         [half, jax.ShapeDtypeStruct((1, doc_count), jnp.int32)],
         embeddings,
         ids,
+        limit=60 * 2**20,
+        scratch=[
+            pltpu.VMEM((doc_count, feature_count), jnp.bfloat16),
+            pltpu.VMEM((1, doc_count), jnp.int32),
+            pltpu.SemaphoreType.DMA((CHUNKS,)),
+            pltpu.SemaphoreType.DMA,
+        ],
     )
     first_own = across(first_own, first)
     first_other, *rest = call_kernel(

time: 44.8 us -> 45.8 us (1.022)
  Pallas kernels: 4.21 us -> 6.22 us
  local copies, waits for them, and re-layouts: 1.27 us -> 0.01 us
  starting transfers between devices: 19.4 us -> 18.5 us
  waiting for transfers between devices: 7.34 us -> 8.05 us
    pallas_call x6, Pallas kernels: 4.21 us -> 6.22 us  [call_kernel(): pl.pallas_call(kernel, out_shape=out_shape, in_specs=[ANY if scratch else...]
    ppermute x6, starting transfers between devices: 10.5 us -> 9.18 us  [swap_cores(): return lax.ppermute(x, 'sub', [(i, i ^ 1) for i in range(cores)])]
    unnamed x4, local copies, waits for them, and re-layouts: 1.27 us -> 0.01 us
    ppermute x5, waiting for transfers between devices: 6.19 us -> 6.9 us  [across(): return lax.ppermute(x, ('owner', 'helper', 'sub'), pairs)]
  transfers between devices with their start and end apart: 11 -> 11, of which waited for: 3 -> 3; matrix products, arithmetic and copies ran while one was open for 0% -> 0% of each run, Pallas kernels for 5% -> 10%
where the time goes in v9:
time: 45.8 us; the launch traced here: 45.6 us
  starting transfers between devices  18.5 us (40%)
  blocking collectives  12.8 us (28%)
  waiting for transfers between devices  8.05 us (18%)
  Pallas kernels  6.22 us (14%)
    all_to_all x1, blocking collectives, body_by_chip(): lax.all_to_all(counts, ('owner', 'helper'), split_axis=0, concat_axis=0,...  12.8 us
    ppermute x5, starting transfers between devices, across(): return lax.ppermute(x, ('owner', 'helper', 'sub'), pairs)  9.28 us
    ppermute x6, starting transfers between devices, swap_cores(): return lax.ppermute(x, 'sub', [(i, i ^ 1) for i in range(cores)])  9.18 us
    ppermute x5, waiting for transfers between devices, across(): return lax.ppermute(x, ('owner', 'helper', 'sub'), pairs)  6.9 us
    pallas_call x6, Pallas kernels, call_kernel(): pl.pallas_call(kernel, out_shape=out_shape, in_specs=[ANY if scratch else...  6.22 us
    ppermute x6, waiting for transfers between devices, swap_cores(): return lax.ppermute(x, 'sub', [(i, i ^ 1) for i in range(cores)])  1.15 us
  transfers between devices with their start and end apart: 11, of which 3 were waited for; matrix products, arithmetic and copies ran while one was open for 0% of the time, Pallas kernels for 10%

profile of v9, /device:TPU:0, one launch (start us, length us, event | category | flops | bytes accessed | tf_op | source)
XLA Modules:
  0.0 45.6 jit_solution(16272903229703326993)
XLA Ops:
  0.0 0.0 copy-start
  0.0 0.5 collective-permute-start.1
  0.5 0.1 collective-permute-start.2
  0.5 2.5 %route_first.1 = (bf16[64,1024]{1,0:T(8,128)(2,1)}, s32[1,256]{1,0:T(1,128)}) custom-call(bf16[256,1024]{1,0:T(8,128)(2,1)} %refs_0_.3, s32[1,256]{1,0:T(1,128)} %bitcast.3), custom_call_target="tpu_custom_call" | custom-call | tf_op jit(solution)/shard_map/route_first/pallas_call | solution.py:120
  3.0 0.0 copy-start.1
  3.0 4.1 %collective-permute-start = (bf16[64,1024]{1,0:T(8,128)(2,1)}, bf16[64,1024]{1,0:T(8,128)(2,1)S(1)}, u32[]{:S(2)}, u32[]{:S(2)}) collective-permute-start(bf16[64,1024]{1,0:T(8,128)(2,1)} %get-tuple-element.11), channel_id=1, source_target_pairs={{0,8},{1,11},{2,10},{3,9},{4,12},{5,15},{6,14},{7,13},{8,0},{9,3},... | collective-permute-start | bytes 393224 | tf_op jit(solution)/shard_map/ppermute | solution.py:227
  7.1 0.0 collective-permute-done.2.refs_3_
  7.1 0.0 collective-permute-done.1.refs_1_
  7.1 0.0 copy-done
  7.1 0.0 copy-done.1
  7.1 0.7 %route_rest.1 = (bf16[64,1024]{1,0:T(8,128)(2,1)S(1)}, bf16[128,1024]{1,0:T(8,128)(2,1)S(1)}, bf16[128,1024]{1,0:T(8,128)(2,1)S(1)}, bf16[128,1024]{1,0:T(8,128)(2,1)S(1)}) custom-call(bf16[256,1024]{1,0:T(8,128)(2,1)S(1)} %copy-done, bf16[256,1024]{1,0:T(8,128)(2,1)S(1)} %collective-permute-done.1.refs_1_, s32[1,256]{1,0:T(1,128)S(1)} %copy-done.1, ...), custom_call_target="tpu_custom_call" | custom-call | tf_op jit(solution)/shard_map/route_rest/pallas_call | solution.py:120
  7.9 0.6 %collective-permute-start.3 = (bf16[64,1024]{1,0:T(8,128)(2,1)S(1)}, bf16[64,1024]{1,0:T(8,128)(2,1)S(1)}, u32[]{:S(2)}, u32[]{:S(2)}) collective-permute-start(bf16[64,1024]{1,0:T(8,128)(2,1)S(1)} %get-tuple-element.13), channel_id=1, source_target_pairs={{0,8},{1,11},{2,10},{3,9},{4,12},{5,15},{6,14},{7,13},{8,0},{9,3},... | collective-permute-start | bytes 393224 | tf_op jit(solution)/shard_map/ppermute | solution.py:227
  8.5 0.7 %collective-permute-start.4 = (bf16[128,1024]{1,0:T(8,128)(2,1)S(1)}, bf16[128,1024]{1,0:T(8,128)(2,1)S(1)}, u32[]{:S(2)}, u32[]{:S(2)}) collective-permute-start(bf16[128,1024]{1,0:T(8,128)(2,1)S(1)} %get-tuple-element.14), channel_id=1, source_target_pairs={{0,0},{1,3},{2,2},{3,1},{4,4},{5,7},{6,6},{7,5},{8,8},{9,11},{10,1... | collective-permute-start | bytes 786440 | tf_op jit(solution)/shard_map/ppermute | solution.py:227
  9.2 1.6 %collective-permute-start.5 = (bf16[128,1024]{1,0:T(8,128)(2,1)S(1)}, bf16[128,1024]{1,0:T(8,128)(2,1)S(1)}, u32[]{:S(2)}, u32[]{:S(2)}) collective-permute-start(bf16[128,1024]{1,0:T(8,128)(2,1)S(1)} %get-tuple-element.15), channel_id=1, source_target_pairs={{0,4},{1,7},{2,6},{3,5},{4,0},{5,3},{6,2},{7,1},{8,12},{9,15},{10,... | collective-permute-start | bytes 786440 | tf_op jit(solution)/shard_map/ppermute | solution.py:227
  10.8 2.2 %collective-permute-start.9 = (bf16[128,1024]{1,0:T(8,128)(2,1)S(1)}, bf16[128,1024]{1,0:T(8,128)(2,1)S(1)}, u32[]{:S(2)}, u32[]{:S(2)}) collective-permute-start(bf16[128,1024]{1,0:T(8,128)(2,1)S(1)} %get-tuple-element.16), channel_id=1, source_target_pairs={{0,12},{1,15},{2,14},{3,13},{4,8},{5,11},{6,10},{7,9},{8,4},{9,7},... | collective-permute-start | bytes 786440 | tf_op jit(solution)/shard_map/ppermute | solution.py:227
  13.1 4.1 %collective-permute-done.first_ref = bf16[64,1024]{1,0:T(8,128)(2,1)S(1)} collective-permute-done((bf16[64,1024]{1,0:T(8,128)(2,1)}, bf16[64,1024]{1,0:T(8,128)(2,1)S(1)}, u32[]{:S(2)}, u32[]{:S(2)}) %collective-permute-start) | collective-permute-done | bytes 131104 | tf_op jit(solution)/shard_map/ppermute | solution.py:227
  17.1 2.8 %collective-permute-done.3.second_ref = bf16[64,1024]{1,0:T(8,128)(2,1)S(1)} collective-permute-done((bf16[64,1024]{1,0:T(8,128)(2,1)S(1)}, bf16[64,1024]{1,0:T(8,128)(2,1)S(1)}, u32[]{:S(2)}, u32[]{:S(2)}) %collective-permute-start.3) | collective-permute-done | bytes 131104 | tf_op jit(solution)/shard_map/ppermute | solution.py:227
  20.0 0.1 collective-permute-start.6
  20.0 0.0 collective-permute-done.4.refs_1_
  20.1 0.5 %collective-permute-start.7 = (bf16[128,1024]{1,0:T(8,128)(2,1)S(1)}, bf16[128,1024]{1,0:T(8,128)(2,1)S(1)}, u32[]{:S(2)}, u32[]{:S(2)}) collective-permute-start(bf16[128,1024]{1,0:T(8,128)(2,1)S(1)} %collective-permute-done.4.refs_1_), channel_id=1, source_target_pairs={{0,1},{1,0},{2,3},{3,2},{4,5},{5,4},{6,7},{7,6},{8,9},{9,8},{10,11... | collective-permute-start | bytes 786440 | tf_op jit(solution)/shard_map/ppermute | solution.py:211
  20.5 0.0 collective-permute-done.5.refs_2_
  20.6 8.1 %collective-permute-start.8 = (bf16[128,1024]{1,0:T(8,128)(2,1)S(1)}, bf16[128,1024]{1,0:T(8,128)(2,1)S(1)}, u32[]{:S(2)}, u32[]{:S(2)}) collective-permute-start(bf16[128,1024]{1,0:T(8,128)(2,1)S(1)} %collective-permute-done.5.refs_2_), channel_id=1, source_target_pairs={{0,1},{1,0},{2,3},{3,2},{4,5},{5,4},{6,7},{7,6},{8,9},{9,8},{10,11... | collective-permute-start | bytes 786440 | tf_op jit(solution)/shard_map/ppermute | solution.py:211
  28.6 0.0 collective-permute-done.9.refs_6_
  28.7 0.0 collective-permute-start.10
  28.7 0.0 collective-permute-done.6.refs_3_
  28.7 0.0 collective-permute-done.7.refs_4_
  28.7 1.1 %collective-permute-done.8.refs_5_ = bf16[128,1024]{1,0:T(8,128)(2,1)S(1)} collective-permute-done((bf16[128,1024]{1,0:T(8,128)(2,1)S(1)}, bf16[128,1024]{1,0:T(8,128)(2,1)S(1)}, u32[]{:S(2)}, u32[]{:S(2)}) %collective-permute-start.8) | collective-permute-done | bytes 262176 | tf_op jit(solution)/shard_map/ppermute | solution.py:211
  29.8 1.1 %count.1.refs_8_ = f32[1,384]{1,0:T(1,128)S(1)} custom-call(bf16[128,1024]{1,0:T(8,128)(2,1)S(1)} %join.1.refs_0_, bf16[128,1024]{1,0:T(8,128)(2,1)S(1)} %collective-permute-done.4.refs_1_, bf16[128,1024]{1,0:T(8,128)(2,1)S(1)} %collective-permute-done.5.refs_2_, bf16[128,1024]{1,0:T(8,128)(2,1)S(1)} %collective-permute-done.6.refs_3_, ...), custom_call_target="tpu_custom_call" | custom-call | tf_op jit(solution)/shard_map/count/pallas_call | solution.py:120
  31.0 0.0 collective-permute-done.10.refs_7_
  31.0 1.1 %finish.1 = f32[8,1,64]{2,1,0:T(1,128)S(1)} custom-call(bf16[128,1024]{1,0:T(8,128)(2,1)S(1)} %join.1.refs_0_, bf16[128,1024]{1,0:T(8,128)(2,1)S(1)} %collective-permute-done.4.refs_1_, bf16[128,1024]{1,0:T(8,128)(2,1)S(1)} %collective-permute-done.5.refs_2_, bf16[128,1024]{1,0:T(8,128)(2,1)S(1)} %collective-permute-done.6.refs_3_, ...), custom_call_target="tpu_custom_call" | custom-call | tf_op jit(solution)/shard_map/finish/pallas_call | solution.py:120
  32.1 12.8 %all_to_all.5.counts_ref = f32[8,1,64]{2,1,0:T(1,128)S(1)} all-to-all(f32[8,1,64]{2,1,0:T(1,128)S(1)} %finish.1), channel_id=1, replica_groups=mesh['groups'=2,'owner'=4,'helper'=2,'sub'=2] {'owner','helper'}, dimensions={0} | all-to-all | bytes 4096 | tf_op jit(solution)/shard_map/all_to_all | solution.py:289
  44.9 0.7 %select.1 = f32[1,256]{1,0:T(1,128)} custom-call(f32[8,1,64]{2,1,0:T(1,128)S(1)} %all_to_all.5.counts_ref, s32[1,256]{1,0:T(1,128)S(1)} %copy-done.1), custom_call_target="tpu_custom_call" | custom-call | tf_op jit(solution)/shard_map/select/pallas_call | solution.py:120
  (1 shorter events, 0.0 us)
Async XLA Ops:
  0.0 7.1 %copy-start = (bf16[256,1024]{1,0:T(8,128)(2,1)S(1)}, bf16[256,1024]{1,0:T(8,128)(2,1)}, u32[]{:S(2)}) copy-start(bf16[256,1024]{1,0:T(8,128)(2,1)} %refs_0_.3) | copy-start | bytes 1572868
  0.0 7.1 %collective-permute-start.1 = (bf16[256,1024]{1,0:T(8,128)(2,1)}, bf16[256,1024]{1,0:T(8,128)(2,1)S(1)}, u32[]{:S(2)}, u32[]{:S(2)}) collective-permute-start(bf16[256,1024]{1,0:T(8,128)(2,1)} %refs_0_.3), channel_id=1, source_target_pairs={{0,1},{1,0},{2,3},{3,2},{4,5},{5,4},{6,7},{7,6},{8,9},{9,8},{10,11... | collective-permute-start | bytes 1572872 | tf_op jit(solution)/shard_map/ppermute | solution.py:211
  0.5 6.7 %collective-permute-start.2 = (s32[1,256]{1,0:T(1,128)}, s32[1,256]{1,0:T(1,128)S(1)}, u32[]{:S(2)}, u32[]{:S(2)}) collective-permute-start(s32[1,256]{1,0:T(1,128)} %bitcast.2), channel_id=1, source_target_pairs={{0,1},{1,0},{2,3},{3,2},{4,5},{5,4},{6,7},{7,6},{8,9},{9,8},{10,11... | collective-permute-start | bytes 3080 | tf_op jit(solution)/shard_map/ppermute | solution.py:211
  3.0 4.1 %copy-start.1 = (s32[1,256]{1,0:T(1,128)S(1)}, s32[1,256]{1,0:T(1,128)}, u32[]{:S(2)}) copy-start(s32[1,256]{1,0:T(1,128)} %get-tuple-element.12.refs_2_.slot_ref) | copy-start | bytes 3076
  3.0 14.1 %collective-permute-start = (bf16[64,1024]{1,0:T(8,128)(2,1)}, bf16[64,1024]{1,0:T(8,128)(2,1)S(1)}, u32[]{:S(2)}, u32[]{:S(2)}) collective-permute-start(bf16[64,1024]{1,0:T(8,128)(2,1)} %get-tuple-element.11), channel_id=1, source_target_pairs={{0,8},{1,11},{2,10},{3,9},{4,12},{5,15},{6,14},{7,13},{8,0},{9,3},... | collective-permute-start | bytes 393224 | tf_op jit(solution)/shard_map/ppermute | solution.py:227
  7.9 12.1 %collective-permute-start.3 = (bf16[64,1024]{1,0:T(8,128)(2,1)S(1)}, bf16[64,1024]{1,0:T(8,128)(2,1)S(1)}, u32[]{:S(2)}, u32[]{:S(2)}) collective-permute-start(bf16[64,1024]{1,0:T(8,128)(2,1)S(1)} %get-tuple-element.13), channel_id=1, source_target_pairs={{0,8},{1,11},{2,10},{3,9},{4,12},{5,15},{6,14},{7,13},{8,0},{9,3},... | collective-permute-start | bytes 393224 | tf_op jit(solution)/shard_map/ppermute | solution.py:227
  8.5 11.5 %collective-permute-start.4 = (bf16[128,1024]{1,0:T(8,128)(2,1)S(1)}, bf16[128,1024]{1,0:T(8,128)(2,1)S(1)}, u32[]{:S(2)}, u32[]{:S(2)}) collective-permute-start(bf16[128,1024]{1,0:T(8,128)(2,1)S(1)} %get-tuple-element.14), channel_id=1, source_target_pairs={{0,0},{1,3},{2,2},{3,1},{4,4},{5,7},{6,6},{7,5},{8,8},{9,11},{10,1... | collective-permute-start | bytes 786440 | tf_op jit(solution)/shard_map/ppermute | solution.py:227
  9.2 11.4 %collective-permute-start.5 = (bf16[128,1024]{1,0:T(8,128)(2,1)S(1)}, bf16[128,1024]{1,0:T(8,128)(2,1)S(1)}, u32[]{:S(2)}, u32[]{:S(2)}) collective-permute-start(bf16[128,1024]{1,0:T(8,128)(2,1)S(1)} %get-tuple-element.15), channel_id=1, source_target_pairs={{0,4},{1,7},{2,6},{3,5},{4,0},{5,3},{6,2},{7,1},{8,12},{9,15},{10,... | collective-permute-start | bytes 786440 | tf_op jit(solution)/shard_map/ppermute | solution.py:227
  10.8 17.8 %collective-permute-start.9 = (bf16[128,1024]{1,0:T(8,128)(2,1)S(1)}, bf16[128,1024]{1,0:T(8,128)(2,1)S(1)}, u32[]{:S(2)}, u32[]{:S(2)}) collective-permute-start(bf16[128,1024]{1,0:T(8,128)(2,1)S(1)} %get-tuple-element.16), channel_id=1, source_target_pairs={{0,12},{1,15},{2,14},{3,13},{4,8},{5,11},{6,10},{7,9},{8,4},{9,7},... | collective-permute-start | bytes 786440 | tf_op jit(solution)/shard_map/ppermute | solution.py:227
  20.0 8.7 %collective-permute-start.6 = (bf16[128,1024]{1,0:T(8,128)(2,1)S(1)}, bf16[128,1024]{1,0:T(8,128)(2,1)S(1)}, u32[]{:S(2)}, u32[]{:S(2)}) collective-permute-start(bf16[128,1024]{1,0:T(8,128)(2,1)S(1)} %join.1.refs_0_), channel_id=1, source_target_pairs={{0,1},{1,0},{2,3},{3,2},{4,5},{5,4},{6,7},{7,6},{8,9},{9,8},{10,11... | collective-permute-start | bytes 786440 | tf_op jit(solution)/shard_map/ppermute | solution.py:211
  20.1 8.6 %collective-permute-start.7 = (bf16[128,1024]{1,0:T(8,128)(2,1)S(1)}, bf16[128,1024]{1,0:T(8,128)(2,1)S(1)}, u32[]{:S(2)}, u32[]{:S(2)}) collective-permute-start(bf16[128,1024]{1,0:T(8,128)(2,1)S(1)} %collective-permute-done.4.refs_1_), channel_id=1, source_target_pairs={{0,1},{1,0},{2,3},{3,2},{4,5},{5,4},{6,7},{7,6},{8,9},{9,8},{10,11... | collective-permute-start | bytes 786440 | tf_op jit(solution)/shard_map/ppermute | solution.py:211
  20.6 9.3 %collective-permute-start.8 = (bf16[128,1024]{1,0:T(8,128)(2,1)S(1)}, bf16[128,1024]{1,0:T(8,128)(2,1)S(1)}, u32[]{:S(2)}, u32[]{:S(2)}) collective-permute-start(bf16[128,1024]{1,0:T(8,128)(2,1)S(1)} %collective-permute-done.5.refs_2_), channel_id=1, source_target_pairs={{0,1},{1,0},{2,3},{3,2},{4,5},{5,4},{6,7},{7,6},{8,9},{9,8},{10,11... | collective-permute-start | bytes 786440 | tf_op jit(solution)/shard_map/ppermute | solution.py:211
  28.7 2.3 %collective-permute-start.10 = (bf16[128,1024]{1,0:T(8,128)(2,1)S(1)}, bf16[128,1024]{1,0:T(8,128)(2,1)S(1)}, u32[]{:S(2)}, u32[]{:S(2)}) collective-permute-start(bf16[128,1024]{1,0:T(8,128)(2,1)S(1)} %collective-permute-done.9.refs_6_), channel_id=1, source_target_pairs={{0,1},{1,0},{2,3},{3,2},{4,5},{5,4},{6,7},{7,6},{8,9},{9,8},{10,11... | collective-permute-start | bytes 786440 | tf_op jit(solution)/shard_map/ppermute | solution.py:211

commit v10 on v3

v10 whole, which is shorter than its diff:
```python
import functools
import math

import jax
import jax.numpy as jnp
from jax import lax
from jax.experimental import pallas as pl
from jax.experimental.pallas import tpu as pltpu
from jax.sharding import PartitionSpec as P

CL_OWN = 2

epsilon = 1e-06
threshold = 0.8
sharpness = 0.05

EMPTY = 4.0
TILE = 256
VMEM = pl.BlockSpec(memory_space=pltpu.VMEM)


def slots_of(ids, clusters, capacity):
    doc_count = ids.shape[1]
    member = lax.broadcasted_iota(jnp.int32, (clusters, doc_count), 0) == ids
    earlier = lax.broadcasted_iota(jnp.int32, (doc_count, doc_count), 0) < (
        lax.broadcasted_iota(jnp.int32, (doc_count, doc_count), 1)
    )
    ahead = jnp.dot(
        member.astype(jnp.bfloat16), earlier.astype(jnp.bfloat16), preferred_element_type=jnp.float32
    )
    rank = jnp.sum(jnp.where(member, ahead, 0.0), axis=0, keepdims=True).astype(jnp.int32)
    return ids * capacity + rank


def lay(rows_ref, slot, slots):
    doc_count, feature_count = rows_ref.shape
    dispatch = lax.broadcasted_iota(jnp.int32, (slots, doc_count), 0) == slot
    filled = jnp.sum(dispatch.astype(jnp.float32), axis=1, keepdims=True) > 0
    laid = jnp.dot(
        dispatch.astype(jnp.bfloat16), rows_ref[...], preferred_element_type=jnp.float32
    )
    factor = lax.rsqrt(
        jnp.mean(laid * laid, axis=-1, keepdims=True) + epsilon
    ) * feature_count ** (-0.5)
    lane = lax.broadcasted_iota(jnp.int32, laid.shape, 1)
    return jnp.where(filled | (lane > 0), laid * factor, EMPTY).astype(jnp.bfloat16)


def route_kernel(clusters, capacity, rows_ref, ids_ref, piece_ref, slot_ref):
    slot = slots_of(ids_ref[...], clusters, capacity)
    slot_ref[...] = slot
    piece_ref[...] = lay(rows_ref, slot, piece_ref.shape[0])


def call_kernel(name, kernel, out_shape, *args, limit=32 * 2**20, flops=0):
    cost = pl.CostEstimate(flops=flops, bytes_accessed=0, transcendentals=0) if flops else None
    return pl.pallas_call(
        kernel,
        out_shape=out_shape,
        in_specs=[VMEM] * len(args),
        out_specs=jax.tree.map(lambda _: VMEM, out_shape),
        compiler_params=pltpu.CompilerParams(vmem_limit_bytes=limit),
        cost_estimate=cost,
        name=name,
    )(*args)


def unit_rows_of(rows):
    widened = rows.astype(jnp.float32)
    factor = lax.rsqrt(
        jnp.mean(widened * widened, axis=-1, keepdims=True) + epsilon
    ) * rows.shape[1] ** (-0.5)
    return (widened * factor).astype(jnp.bfloat16)


def weights_of(others, own):
    scores = lax.dot_general(
        others, own, (((1,), (1,)), ((), ())), preferred_element_type=jnp.float32
    )
    slope = -math.log2(math.e) / sharpness
    return 1.0 / (1.0 + jnp.exp2(scores * slope - threshold * slope))


def count_kernel(*refs):
    *piece_refs, count_ref = refs
    own = piece_refs[0][...]
    total = jnp.zeros((1, own.shape[0]), jnp.float32)
    for k, piece in enumerate(piece_refs):
        for first in range(0, piece.shape[0], TILE):
            other = piece[first : first + TILE]
            weights = weights_of(other, own)
            keep = other[:, :1].astype(jnp.float32) < 0.5 * EMPTY
            if k == 0:
                keep = keep & (
                    lax.broadcasted_iota(jnp.int32, weights.shape, 0) + first
                    != lax.broadcasted_iota(jnp.int32, weights.shape, 1)
                )
            total = total + jnp.sum(jnp.where(keep, weights, 0.0), axis=0, keepdims=True)
    count_ref[...] = total


def soft_counts(pieces):
    out_shape = jax.ShapeDtypeStruct((1, pieces[0].shape[0]), jnp.float32)
    return call_kernel("count", count_kernel, out_shape, *pieces)


def column_of(row):
    size = row.shape[1]
    diagonal = lax.broadcasted_iota(jnp.int32, (size, size), 0) == (
        lax.broadcasted_iota(jnp.int32, (size, size), 1)
    )
    return jnp.sum(jnp.where(diagonal, row, 0), axis=1, keepdims=True)


def pair_counts(others, other_ids, own, own_ids, itself=None):
    weights = weights_of(others, own)
    keep = column_of(other_ids) == own_ids
    if itself is not None:
        keep = keep & (
            lax.broadcasted_iota(jnp.int32, weights.shape, 0)
            != lax.broadcasted_iota(jnp.int32, weights.shape, 1) + itself
        )
    return jnp.sum(jnp.where(keep, weights, 0.0), axis=0, keepdims=True)


def pair_up_kernel(first_ref, second_ref, out_ref):
    rows = first_ref.shape[0]
    out_ref[:rows] = first_ref[...]
    out_ref[rows:] = second_ref[...]


def pair_up(first, second):
    out_shape = jax.ShapeDtypeStruct((2 * first.shape[0], first.shape[1]), first.dtype)
    return call_kernel("pair_up", pair_up_kernel, out_shape, first, second)


OWN, OTHER, END, END_OTHER = range(4)


def first_kernel(ids_ref, next_ids_ref, across_ids_ref, *refs):
    *piece_refs, across_ref, unit_ref, across_unit_ref = refs[:-3]
    count_refs = refs[-3:]
    own, own_other, next_own, next_other, end_a, end_b, end_other_a, end_other_b = piece_refs
    blocks = [
        ([own], ids_ref, OWN),
        ([end_a, end_b], ids_ref, END),
        ([own_other], ids_ref, OTHER),
        ([end_other_a, end_other_b], ids_ref, END_OTHER),
        ([next_own], next_ids_ref, OWN),
        ([next_other], next_ids_ref, OTHER),
    ]
    size = own.shape[0]
    for k, (pieces, _, _) in enumerate(blocks):
        first = k * size
        for piece in pieces:
            unit_ref[first : first + piece.shape[0]] = unit_rows_of(piece[...])
            first += piece.shape[0]
    across_unit_ref[...] = unit_rows_of(across_ref[...])
    wanted = [
        (unit_ref[:size], ids_ref[OWN : OWN + 1], 0),
        (unit_ref[size : 2 * size], ids_ref[END : END + 1], 1),
        (across_unit_ref[...], across_ids_ref[OWN : OWN + 1], -1),
    ]
    for j, (rows, row_ids, place) in enumerate(wanted):
        total = jnp.zeros((1, size), jnp.float32)
        for k, (_, block_ids, which) in enumerate(blocks):
            total = total + pair_counts(
                unit_ref[k * size : (k + 1) * size],
                block_ids[which : which + 1],
                rows,
                row_ids,
                0 if k == place else None,
            )
        count_refs[j][...] = total


def more_kernel(half, ids_ref, next_ids_ref, across_ids_ref, unit_ref, across_unit_ref, *refs):
    far, far_other, across_end, *refs = refs
    if half == 0:
        *refs, far_unit_ref, end_unit_ref = refs
    else:
        before_ref, before_end_ref, end_count_ref, *refs = refs
    *refs, end_out_ref = refs
    count_refs, out_refs = refs[:3], refs[3:]
    size = ids_ref.shape[1]
    part = far.shape[0]
    lanes = slice(half * part, (half + 1) * part)
    fresh = jnp.concatenate([unit_rows_of(far[...]), unit_rows_of(far_other[...])], axis=0)
    fresh_ids = jnp.concatenate(
        [next_ids_ref[END : END + 1, lanes], next_ids_ref[END_OTHER : END_OTHER + 1, lanes]], axis=1
    )
    end = unit_rows_of(across_end[...])
    end_ids = across_ids_ref[END : END + 1, lanes]
    wanted = [
        (unit_ref[:size], ids_ref[OWN : OWN + 1]),
        (unit_ref[size : 2 * size], ids_ref[END : END + 1]),
        (across_unit_ref[...], across_ids_ref[OWN : OWN + 1]),
    ]
    for j, (rows, row_ids) in enumerate(wanted):
        out_refs[j][...] = count_refs[j][...] + pair_counts(fresh, fresh_ids, rows, row_ids)

    def against_column(rows, row_ids):
        total = pair_counts(fresh, fresh_ids, rows, row_ids)
        blocks = [(ids_ref, OWN), (ids_ref, END), (ids_ref, OTHER), (ids_ref, END_OTHER)]
        blocks += [(next_ids_ref, OWN), (next_ids_ref, OTHER)]
        for k, (block_ids, which) in enumerate(blocks):
            total = total + pair_counts(
                unit_ref[k * size : (k + 1) * size], block_ids[which : which + 1], rows, row_ids
            )
        return total

    if half == 0:
        far_unit_ref[...] = fresh
        end_unit_ref[...] = end
        end_out_ref[...] = against_column(end, end_ids)
    else:
        before_ids = jnp.concatenate(
            [next_ids_ref[END : END + 1, :part], next_ids_ref[END_OTHER : END_OTHER + 1, :part]],
            axis=1,
        )
        end_out_ref[:, :part] = end_count_ref[...] + pair_counts(
            fresh, fresh_ids, before_end_ref[...], across_ids_ref[END : END + 1, :part]
        )
        end_out_ref[:, part:] = against_column(end, end_ids) + pair_counts(
            before_ref[...], before_ids, end, end_ids
        )


def add_kernel(counts_ref, x_ref, z_ref, xz_ref, out_ref):
    owner = lax.axis_index("owner")
    own = jnp.where((owner == 1) | (owner == 2), counts_ref[...], 0.0)
    out_ref[...] = own + x_ref[...] + z_ref[...] + xz_ref[...]


def select_kernel(capacity, counts_ref, slot_ref, out_ref):
    counts = counts_ref[:, 0, :]
    slot = slot_ref[...]
    doc_count = slot.shape[1]
    block = slot // capacity
    rank = slot - block * capacity
    hot = (lax.broadcasted_iota(jnp.int32, (capacity, doc_count), 0) == rank).astype(jnp.float32)
    by_block = jnp.dot(
        counts, hot, precision=lax.Precision.HIGHEST, preferred_element_type=jnp.float32
    )
    chosen = lax.broadcasted_iota(jnp.int32, by_block.shape, 0) == block
    out_ref[...] = jnp.sum(jnp.where(chosen, by_block, 0.0), axis=0, keepdims=True)


def select(counts, slot, capacity):
    out_shape = jax.ShapeDtypeStruct(slot.shape, jnp.float32)
    kernel = functools.partial(select_kernel, capacity)
    return call_kernel("select", kernel, out_shape, counts, slot, limit=8 * 2**20)[0]


def swap_cores(x):
    cores = lax.axis_size("sub")
    return lax.ppermute(x, "sub", [(i, i ^ 1) for i in range(cores)])


def body_by_column(embeddings, cluster_id):
    doc_count, feature_count = embeddings.shape
    helpers, cores = lax.axis_size("helper"), lax.axis_size("sub")
    part = doc_count // 2

    def send(x, hops, turn=0, swap=0):
        pairs = [
            (
                (here * helpers + h) * cores + c,
                (there * helpers + (h ^ turn)) * cores + (c ^ swap),
            )
            for here, there in hops
            for h in range(helpers)
            for c in range(cores)
        ]
        return lax.ppermute(x, ("owner", "helper", "sub"), pairs)

    inwards, outwards = [(0, 1), (3, 2)], [(1, 0), (2, 3)]
    middle, still = [(1, 2), (2, 1)], [(1, 1), (2, 2)]

    ids = cluster_id.reshape(1, doc_count)
    next_own = send(embeddings, middle)
    across = send(embeddings, still, turn=1)
    own_other = send(embeddings, still, swap=1)
    end = [send(embeddings[first : first + part], inwards) for first in (0, part)]
    here_ids = pair_up(ids, swap_cores(ids))
    here_ids = pair_up(here_ids, send(here_ids, inwards))
    next_ids = send(here_ids, middle)
    across_ids = send(here_ids, still, turn=1)
    end_other = [send(x, still, swap=1) for x in end]
    far = [send(x, middle) for x in end]
    across_end = [send(x, still, turn=1) for x in end]
    next_other = send(next_own, still, swap=1)
    far_other = [send(x, still, swap=1) for x in far]

    rows = functools.partial(jax.ShapeDtypeStruct, dtype=jnp.bfloat16)
    sums = functools.partial(jax.ShapeDtypeStruct, dtype=jnp.float32)
    all_ids = (here_ids, next_ids, across_ids)
    units, across_units, *counts = call_kernel(
        "first",
        first_kernel,
        [
            rows((6 * doc_count, feature_count)),
            rows((doc_count, feature_count)),
        ]
        + [sums((1, doc_count))] * 3,
        *all_ids,
        embeddings,
        own_other,
        next_own,
        next_other,
        *end,
        *end_other,
        across,
    )
    *counts, end_counts, far_units, end_units = call_kernel(
        "more",
        functools.partial(more_kernel, 0),
        [sums((1, doc_count))] * 3
        + [
            sums((1, part)),
            rows((2 * part, feature_count)),
            rows((part, feature_count)),
        ],
        *all_ids,
        units,
        across_units,
        far[0],
        far_other[0],
        across_end[0],
        *counts,
    )
    *counts, end_counts = call_kernel(
        "last",
        functools.partial(more_kernel, 1),
        [sums((1, doc_count))] * 4,
        *all_ids,
        units,
        across_units,
        far[1],
        far_other[1],
        across_end[1],
        far_units,
        end_units,
        end_counts,
        *counts,
    )
    own_counts, inner_counts, across_counts = counts
    return call_kernel(
        "add",
        add_kernel,
        sums((1, doc_count)),
        own_counts,
        send(across_counts, still, turn=1),
        send(inner_counts, outwards),
        send(end_counts, outwards, turn=1),
        limit=8 * 2**20,
    )[0]


def body_by_owner(embeddings, cluster_id):
    doc_count, feature_count = embeddings.shape
    owners, helpers = lax.axis_size("owner"), lax.axis_size("helper")
    clusters = CL_OWN * owners
    capacity = 2 * doc_count // clusters
    mine = lax.axis_index("helper") % CL_OWN

    def partner(x):
        return lax.ppermute(x, "helper", [(i, i ^ 1) for i in range(helpers)])

    outgoing, slot = call_kernel(
        "route",
        functools.partial(route_kernel, clusters, capacity),
        [
            jax.ShapeDtypeStruct((clusters * capacity, feature_count), jnp.bfloat16),
            jax.ShapeDtypeStruct((1, doc_count), jnp.int32),
        ],
        embeddings,
        cluster_id.reshape(1, doc_count),
    )
    outgoing = outgoing.reshape(owners, CL_OWN, capacity, feature_count)
    arrived = lax.all_to_all(outgoing, "owner", split_axis=0, concat_axis=0, tiled=True)
    kept = lax.dynamic_index_in_dim(arrived, mine, 1, keepdims=False)
    given = partner(lax.dynamic_index_in_dim(arrived, 1 - mine, 1, keepdims=False))
    own = jnp.stack([kept, given]).reshape(CL_OWN * owners * capacity, feature_count)
    others = [swap_cores(own)]
    for step in range(CL_OWN, helpers, CL_OWN):
        turn = [(i, (i + step) % helpers) for i in range(helpers)]
        others += [lax.ppermute(x, "helper", turn) for x in (own, others[0])]
    counts = soft_counts([own, *others])
    counts = counts.reshape(CL_OWN, owners, capacity)
    kept, given = counts[0], partner(counts[1])
    counts = jnp.where(mine == 0, jnp.stack([kept, given], 1), jnp.stack([given, kept], 1))
    back = lax.all_to_all(counts, "owner", split_axis=0, concat_axis=0, tiled=True)
    return select(back.reshape(clusters, 1, capacity), slot, capacity)


def solution(mesh):
    in_specs = (
        P(("groups", "owner", "helper", "sub"), None),
        P(("groups", "owner", "helper", "sub")),
    )
    out_specs = P(("groups", "owner", "helper", "sub"))
    columns = tuple(mesh.shape[axis] for axis in ("owner", "helper", "sub")) == (4, 2, 2)
    body = body_by_column if columns else body_by_owner
    return jax.shard_map(body, mesh=mesh, in_specs=in_specs, out_specs=out_specs, check_vma=False)
```

time: 47.3 us -> 76.6 us (1.62)
  waiting for transfers between devices: 12.8 us -> 40.8 us
  blocking collectives: 14.1 us -> 0 us
  starting transfers between devices: 15.5 us -> 23.1 us
  Pallas kernels: 3.45 us -> 8.91 us
  local copies, waits for them, and re-layouts: 1.27 us -> 2.78 us
    ppermute x4 -> x20, waiting for transfers between devices: 10.2 us -> 39.4 us  [send(): return lax.ppermute(x, ('owner', 'helper', 'sub'), pairs)]
    ppermute x4 -> x20, starting transfers between devices: 6.33 us -> 23.1 us  [send(): return lax.ppermute(x, ('owner', 'helper', 'sub'), pairs)]
    all_to_all x1 -> x0, blocking collectives: 14.1 us -> none  [body_by_chip(): lax.all_to_all(counts, ('owner', 'helper'), split_axis=0, concat_axis=0,...]
    ppermute x6 -> x1, starting transfers between devices: 9.13 us -> 0.07 us  [swap_cores(): return lax.ppermute(x, 'sub', [(i, i ^ 1) for i in range(cores)])]
    pallas_call x3 -> x6, Pallas kernels: 3.45 us -> 8.91 us  [call_kernel(): pl.pallas_call(kernel, out_shape=out_shape, in_specs=[VMEM] * len(args),...]
    ppermute x6 -> x1, waiting for transfers between devices: 2.59 us -> 1.33 us  [swap_cores(): return lax.ppermute(x, 'sub', [(i, i ^ 1) for i in range(cores)])]
    slice x0 -> x1, local copies, waits for them, and re-layouts: none -> 1.07 us  [body_by_column(): end = [send(embeddings[first:first + part], inwards) for first in (0, part)]]
  transfers between devices with their start and end apart: 10 -> 21, of which waited for: 5 -> 4; matrix products, arithmetic and copies ran while one was open for 0% -> 1% of each run, Pallas kernels for 0% -> 8%
where the time goes in v10:
time: 76.6 us; the launch traced here: 75.9 us
  waiting for transfers between devices  40.8 us (53%)
  starting transfers between devices  23.1 us (30%)
  Pallas kernels  8.91 us (12%)
  local copies, waits for them, and re-layouts  2.78 us (4%)
    ppermute x20, waiting for transfers between devices, send(): return lax.ppermute(x, ('owner', 'helper', 'sub'), pairs)  39.4 us
    ppermute x20, starting transfers between devices, send(): return lax.ppermute(x, ('owner', 'helper', 'sub'), pairs)  23.1 us
    pallas_call x6, Pallas kernels, call_kernel(): pl.pallas_call(kernel, out_shape=out_shape, in_specs=[VMEM] * len(args),...  8.91 us
    unnamed x4, local copies, waits for them, and re-layouts  1.72 us
  transfers between devices with their start and end apart: 21, of which 4 were waited for; matrix products, arithmetic and copies ran while one was open for 1% of the time, Pallas kernels for 8%

profile of v10, /device:TPU:0, one launch (start us, length us, event | category | flops | bytes accessed | tf_op | source)
XLA Modules:
  0.0 75.9 jit_solution(15854424205740966089)
XLA Ops:
  0.0 0.7 collective-permute-start.5
  0.7 1.1 %fusion = (bf16[128,1024]{1,0:T(8,128)(2,1)S(1)}, bf16[128,1024]{1,0:T(8,128)(2,1)S(1)}) fusion(bf16[256,1024]{1,0:T(8,128)(2,1)} %refs_0_.1), kind=kLoop, calls=%fused_computation | loop fusion | bytes 1048576 | tf_op jit(solution)/shard_map/slice | solution.py:284
  1.8 7.7 %collective-permute-start.8 = (bf16[128,1024]{1,0:T(8,128)(2,1)S(1)}, bf16[128,1024]{1,0:T(8,128)(2,1)S(1)}, u32[]{:S(2)}, u32[]{:S(2)}) collective-permute-start(bf16[128,1024]{1,0:T(8,128)(2,1)S(1)} %get-tuple-element.35), channel_id=1, source_target_pairs={{0,4},{1,5},{2,6},{3,7},{12,8},{13,9},{14,10},{15,11},{16,20},{17,... | collective-permute-start | bytes 786440 | tf_op jit(solution)/shard_map/ppermute | solution.py:275
  9.5 1.3 %collective-permute-start.7 = (bf16[128,1024]{1,0:T(8,128)(2,1)S(1)}, bf16[128,1024]{1,0:T(8,128)(2,1)S(1)}, u32[]{:S(2)}, u32[]{:S(2)}) collective-permute-start(bf16[128,1024]{1,0:T(8,128)(2,1)S(1)} %get-tuple-element.36), channel_id=1, source_target_pairs={{0,4},{1,5},{2,6},{3,7},{12,8},{13,9},{14,10},{15,11},{16,20},{17,... | collective-permute-start | bytes 786440 | tf_op jit(solution)/shard_map/ppermute | solution.py:275
  10.8 0.1 collective-permute-start
  10.9 1.3 %collective-permute-done.second_ref = s32[1,256]{1,0:T(1,128)S(1)} collective-permute-done((s32[1,256]{1,0:T(1,128)}, s32[1,256]{1,0:T(1,128)S(1)}, u32[]{:S(2)}, u32[]{:S(2)}) %collective-permute-start) | collective-permute-done | bytes 1056 | tf_op jit(solution)/shard_map/ppermute | solution.py:257
  12.2 0.7 copy-done.1
  12.9 1.3 %collective-permute-start.1 = (s32[2,256]{1,0:T(2,128)S(1)}, s32[2,256]{1,0:T(2,128)S(1)}, u32[]{:S(2)}, u32[]{:S(2)}) collective-permute-start(s32[2,256]{1,0:T(2,128)S(1)} %pair_up.2.first_ref), channel_id=1, source_target_pairs={{0,4},{1,5},{2,6},{3,7},{12,8},{13,9},{14,10},{15,11},{16,20},{17,... | collective-permute-start | bytes 6152 | tf_op jit(solution)/shard_map/ppermute | solution.py:275
  14.2 6.2 %collective-permute-done.1.second_ref = s32[2,256]{1,0:T(2,128)S(1)} collective-permute-done((s32[2,256]{1,0:T(2,128)S(1)}, s32[2,256]{1,0:T(2,128)S(1)}, u32[]{:S(2)}, u32[]{:S(2)}) %collective-permute-start.1) | collective-permute-done | bytes 2080 | tf_op jit(solution)/shard_map/ppermute | solution.py:275
  20.4 0.6 collective-permute-start.2
  21.1 0.7 collective-permute-start.3
  21.8 0.7 collective-permute-start.11
  22.5 0.7 collective-permute-start.10
  23.2 0.7 collective-permute-start.4
  23.9 0.7 collective-permute-start.9
  24.6 0.7 collective-permute-start.6
  25.3 0.7 collective-permute-start.15
  26.0 0.7 collective-permute-start.12
  26.7 0.7 collective-permute-start.17
  27.4 0.7 collective-permute-start.16
  28.1 0.7 collective-permute-start.14
  28.8 0.7 collective-permute-start.13
  29.5 1.0 %copy-done = bf16[256,1024]{1,0:T(8,128)(2,1)S(1)} copy-done((bf16[256,1024]{1,0:T(8,128)(2,1)S(1)}, bf16[256,1024]{1,0:T(8,128)(2,1)}, u32[]{:S(2)}) %copy-start) | copy-done | bytes 524312
  30.5 4.3 %first.1 = (bf16[1536,1024]{1,0:T(8,128)(2,1)S(1)}, bf16[256,1024]{1,0:T(8,128)(2,1)S(1)}, f32[1,256]{1,0:T(1,128)S(1)}, f32[1,256]{1,0:T(1,128)S(1)}, f32[1,256]{1,0:T(1,128)S(1)}) custom-call(s32[4,256]{1,0:T(4,128)S(1)} %pair_up.3.ids_ref, s32[4,256]{1,0:T(4,128)S(1)} %collective-permute-done.2.next_ids_ref, ...), custom_call_target="tpu_custom_call" | custom-call | tf_op jit(solution)/shard_map/first/pallas_call | solution.py:57
  34.9 1.8 %more.1 = (f32[1,256]{1,0:T(1,128)S(1)}, f32[1,256]{1,0:T(1,128)S(1)}, f32[1,256]{1,0:T(1,128)S(1)}, f32[1,128]{1,0:T(1,128)S(1)}, bf16[256,1024]{1,0:T(8,128)(2,1)S(1)}, /*index=5*/bf16[128,1024]{1,0:T(8,128)(2,1)S(1)}) custom-call(s32[4,256]{1,0:T(4,128)S(1)} %pair_up.3.ids_ref, s32[4,256]{1,0:T(4,128)S(1)} %collective-permute-done.2.next_ids_ref, ...), custom_call_target="tpu_custom_call" | custom-call | tf_op jit(solution)/shard_map/more/pallas_call | solution.py:57
  36.7 2.1 %last.1 = (f32[1,256]{1,0:T(1,128)S(1)}, f32[1,256]{1,0:T(1,128)S(1)}, f32[1,256]{1,0:T(1,128)S(1)}, f32[1,256]{1,0:T(1,128)S(1)}) custom-call(s32[4,256]{1,0:T(4,128)S(1)} %pair_up.3.ids_ref, s32[4,256]{1,0:T(4,128)S(1)} %collective-permute-done.2.next_ids_ref, s32[4,256]{1,0:T(4,128)S(1)} %collective-permute-done.3.across_ids_ref, ...), custom_call_target="tpu_custom_call" | custom-call | tf_op jit(solution)/shard_map/last/pallas_call | solution.py:57
  38.9 0.7 collective-permute-start.18
  39.6 1.3 %collective-permute-start.19 = (f32[1,256]{1,0:T(1,128)S(1)}, f32[1,256]{1,0:T(1,128)S(1)}, u32[]{:S(2)}, u32[]{:S(2)}) collective-permute-start(f32[1,256]{1,0:T(1,128)S(1)} %get-tuple-element.33), channel_id=1, source_target_pairs={{4,0},{5,1},{6,2},{7,3},{8,12},{9,13},{10,14},{11,15},{20,16},{21,... | collective-permute-start | bytes 3080 | tf_op jit(solution)/shard_map/ppermute | solution.py:275
  40.9 1.3 %collective-permute-start.20 = (f32[1,256]{1,0:T(1,128)S(1)}, f32[1,256]{1,0:T(1,128)S(1)}, u32[]{:S(2)}, u32[]{:S(2)}) collective-permute-start(f32[1,256]{1,0:T(1,128)S(1)} %get-tuple-element.34), channel_id=1, source_target_pairs={{4,2},{5,3},{6,0},{7,1},{8,14},{9,15},{10,12},{11,13},{20,18},{21,... | collective-permute-start | bytes 3080 | tf_op jit(solution)/shard_map/ppermute | solution.py:275
  42.2 31.6 %collective-permute-done.19.z_ref = f32[1,256]{1,0:T(1,128)S(1)} collective-permute-done((f32[1,256]{1,0:T(1,128)S(1)}, f32[1,256]{1,0:T(1,128)S(1)}, u32[]{:S(2)}, u32[]{:S(2)}) %collective-permute-start.19) | collective-permute-done | bytes 1056 | tf_op jit(solution)/shard_map/ppermute | solution.py:275
  73.8 1.6 %collective-permute-done.20.xz_ref = f32[1,256]{1,0:T(1,128)S(1)} collective-permute-done((f32[1,256]{1,0:T(1,128)S(1)}, f32[1,256]{1,0:T(1,128)S(1)}, u32[]{:S(2)}, u32[]{:S(2)}) %collective-permute-start.20) | collective-permute-done | bytes 1056 | tf_op jit(solution)/shard_map/ppermute | solution.py:275
  75.4 0.6 add.1
  (21 shorter events, 0.1 us)
Async XLA Ops:
  0.0 24.6 %collective-permute-start.5 = (bf16[256,1024]{1,0:T(8,128)(2,1)}, bf16[256,1024]{1,0:T(8,128)(2,1)S(1)}, u32[]{:S(2)}, u32[]{:S(2)}) collective-permute-start(bf16[256,1024]{1,0:T(8,128)(2,1)} %refs_0_.1), channel_id=1, source_target_pairs={{4,8},{5,9},{6,10},{7,11},{8,4},{9,5},{10,6},{11,7},{20,24},{21,25... | collective-permute-start | bytes 1572872 | tf_op jit(solution)/shard_map/ppermute | solution.py:275
  1.8 20.7 %collective-permute-start.8 = (bf16[128,1024]{1,0:T(8,128)(2,1)S(1)}, bf16[128,1024]{1,0:T(8,128)(2,1)S(1)}, u32[]{:S(2)}, u32[]{:S(2)}) collective-permute-start(bf16[128,1024]{1,0:T(8,128)(2,1)S(1)} %get-tuple-element.35), channel_id=1, source_target_pairs={{0,4},{1,5},{2,6},{3,7},{12,8},{13,9},{14,10},{15,11},{16,20},{17,... | collective-permute-start | bytes 786440 | tf_op jit(solution)/shard_map/ppermute | solution.py:275
  9.5 14.4 %collective-permute-start.7 = (bf16[128,1024]{1,0:T(8,128)(2,1)S(1)}, bf16[128,1024]{1,0:T(8,128)(2,1)S(1)}, u32[]{:S(2)}, u32[]{:S(2)}) collective-permute-start(bf16[128,1024]{1,0:T(8,128)(2,1)S(1)} %get-tuple-element.36), channel_id=1, source_target_pairs={{0,4},{1,5},{2,6},{3,7},{12,8},{13,9},{14,10},{15,11},{16,20},{17,... | collective-permute-start | bytes 786440 | tf_op jit(solution)/shard_map/ppermute | solution.py:275
  10.8 1.4 %collective-permute-start = (s32[1,256]{1,0:T(1,128)}, s32[1,256]{1,0:T(1,128)S(1)}, u32[]{:S(2)}, u32[]{:S(2)}) collective-permute-start(s32[1,256]{1,0:T(1,128)} %bitcast.2), channel_id=1, source_target_pairs={{0,1},{1,0},{2,3},{3,2},{4,5},{5,4},{6,7},{7,6},{8,9},{9,8},{10,11... | collective-permute-start | bytes 3080 | tf_op jit(solution)/shard_map/ppermute | solution.py:257
  12.2 0.7 copy-start.1
  12.9 7.5 %collective-permute-start.1 = (s32[2,256]{1,0:T(2,128)S(1)}, s32[2,256]{1,0:T(2,128)S(1)}, u32[]{:S(2)}, u32[]{:S(2)}) collective-permute-start(s32[2,256]{1,0:T(2,128)S(1)} %pair_up.2.first_ref), channel_id=1, source_target_pairs={{0,4},{1,5},{2,6},{3,7},{12,8},{13,9},{14,10},{15,11},{16,20},{17,... | collective-permute-start | bytes 6152 | tf_op jit(solution)/shard_map/ppermute | solution.py:275
  20.4 1.3 %collective-permute-start.2 = (s32[4,256]{1,0:T(4,128)S(1)}, s32[4,256]{1,0:T(4,128)S(1)}, u32[]{:S(2)}, u32[]{:S(2)}) collective-permute-start(s32[4,256]{1,0:T(4,128)S(1)} %pair_up.3.ids_ref), channel_id=1, source_target_pairs={{4,8},{5,9},{6,10},{7,11},{8,4},{9,5},{10,6},{11,7},{20,24},{21,25... | collective-permute-start | bytes 12296 | tf_op jit(solution)/shard_map/ppermute | solution.py:275
  21.1 2.1 %collective-permute-start.3 = (s32[4,256]{1,0:T(4,128)S(1)}, s32[4,256]{1,0:T(4,128)S(1)}, u32[]{:S(2)}, u32[]{:S(2)}) collective-permute-start(s32[4,256]{1,0:T(4,128)S(1)} %pair_up.3.ids_ref), channel_id=1, source_target_pairs={{4,6},{5,7},{6,4},{7,5},{8,10},{9,11},{10,8},{11,9},{20,22},{21,23... | collective-permute-start | bytes 12296 | tf_op jit(solution)/shard_map/ppermute | solution.py:275
  21.8 4.9 %collective-permute-start.11 = (bf16[256,1024]{1,0:T(8,128)(2,1)}, bf16[256,1024]{1,0:T(8,128)(2,1)S(1)}, u32[]{:S(2)}, u32[]{:S(2)}) collective-permute-start(bf16[256,1024]{1,0:T(8,128)(2,1)} %refs_0_.1), channel_id=1, source_target_pairs={{4,6},{5,7},{6,4},{7,5},{8,10},{9,11},{10,8},{11,9},{20,22},{21,23... | collective-permute-start | bytes 1572872 | tf_op jit(solution)/shard_map/ppermute | solution.py:275
  22.5 2.8 %collective-permute-start.10 = (bf16[128,1024]{1,0:T(8,128)(2,1)S(1)}, bf16[128,1024]{1,0:T(8,128)(2,1)S(1)}, u32[]{:S(2)}, u32[]{:S(2)}) collective-permute-start(bf16[128,1024]{1,0:T(8,128)(2,1)S(1)} %collective-permute-done.8.refs_5_), channel_id=1, source_target_pairs={{4,5},{5,4},{6,7},{7,6},{8,9},{9,8},{10,11},{11,10},{20,21},{21,20... | collective-permute-start | bytes 786440 | tf_op jit(solution)/shard_map/ppermute | solution.py:275
  23.2 4.9 %collective-permute-start.4 = (bf16[256,1024]{1,0:T(8,128)(2,1)}, bf16[256,1024]{1,0:T(8,128)(2,1)S(1)}, u32[]{:S(2)}, u32[]{:S(2)}) collective-permute-start(bf16[256,1024]{1,0:T(8,128)(2,1)} %refs_0_.1), channel_id=1, source_target_pairs={{4,5},{5,4},{6,7},{7,6},{8,9},{9,8},{10,11},{11,10},{20,21},{21,20... | collective-permute-start | bytes 1572872 | tf_op jit(solution)/shard_map/ppermute | solution.py:275
  23.9 2.1 %collective-permute-start.9 = (bf16[128,1024]{1,0:T(8,128)(2,1)S(1)}, bf16[128,1024]{1,0:T(8,128)(2,1)S(1)}, u32[]{:S(2)}, u32[]{:S(2)}) collective-permute-start(bf16[128,1024]{1,0:T(8,128)(2,1)S(1)} %collective-permute-done.7.refs_4_), channel_id=1, source_target_pairs={{4,5},{5,4},{6,7},{7,6},{8,9},{9,8},{10,11},{11,10},{20,21},{21,20... | collective-permute-start | bytes 786440 | tf_op jit(solution)/shard_map/ppermute | solution.py:275
  24.6 4.9 %collective-permute-start.6 = (bf16[256,1024]{1,0:T(8,128)(2,1)S(1)}, bf16[256,1024]{1,0:T(8,128)(2,1)S(1)}, u32[]{:S(2)}, u32[]{:S(2)}) collective-permute-start(bf16[256,1024]{1,0:T(8,128)(2,1)S(1)} %collective-permute-done.5.refs_2_), channel_id=1, source_target_pairs={{4,5},{5,4},{6,7},{7,6},{8,9},{9,8},{10,11},{11,10},{20,21},{21,20... | collective-permute-start | bytes 1572872 | tf_op jit(solution)/shard_map/ppermute | solution.py:275
  25.3 2.1 %collective-permute-start.15 = (bf16[128,1024]{1,0:T(8,128)(2,1)S(1)}, bf16[128,1024]{1,0:T(8,128)(2,1)S(1)}, u32[]{:S(2)}, u32[]{:S(2)}) collective-permute-start(bf16[128,1024]{1,0:T(8,128)(2,1)S(1)} %collective-permute-done.7.refs_4_), channel_id=1, source_target_pairs={{4,8},{5,9},{6,10},{7,11},{8,4},{9,5},{10,6},{11,7},{20,24},{21,25... | collective-permute-start | bytes 786440 | tf_op jit(solution)/shard_map/ppermute | solution.py:275
  26.0 2.8 %collective-permute-start.12 = (bf16[128,1024]{1,0:T(8,128)(2,1)S(1)}, bf16[128,1024]{1,0:T(8,128)(2,1)S(1)}, u32[]{:S(2)}, u32[]{:S(2)}) collective-permute-start(bf16[128,1024]{1,0:T(8,128)(2,1)S(1)} %collective-permute-done.8.refs_5_), channel_id=1, source_target_pairs={{4,8},{5,9},{6,10},{7,11},{8,4},{9,5},{10,6},{11,7},{20,24},{21,25... | collective-permute-start | bytes 786440 | tf_op jit(solution)/shard_map/ppermute | solution.py:275
  26.7 8.2 %collective-permute-start.17 = (bf16[128,1024]{1,0:T(8,128)(2,1)S(1)}, bf16[128,1024]{1,0:T(8,128)(2,1)S(1)}, u32[]{:S(2)}, u32[]{:S(2)}) collective-permute-start(bf16[128,1024]{1,0:T(8,128)(2,1)S(1)} %collective-permute-done.7.refs_4_), channel_id=1, source_target_pairs={{4,6},{5,7},{6,4},{7,5},{8,10},{9,11},{10,8},{11,9},{20,22},{21,23... | collective-permute-start | bytes 786440 | tf_op jit(solution)/shard_map/ppermute | solution.py:275
  27.4 7.5 %collective-permute-start.16 = (bf16[128,1024]{1,0:T(8,128)(2,1)S(1)}, bf16[128,1024]{1,0:T(8,128)(2,1)S(1)}, u32[]{:S(2)}, u32[]{:S(2)}) collective-permute-start(bf16[128,1024]{1,0:T(8,128)(2,1)S(1)} %collective-permute-done.15.refs_0_), channel_id=1, source_target_pairs={{4,5},{5,4},{6,7},{7,6},{8,9},{9,8},{10,11},{11,10},{20,21},{21,20... | collective-permute-start | bytes 786440 | tf_op jit(solution)/shard_map/ppermute | solution.py:275
  28.1 8.7 %collective-permute-start.14 = (bf16[128,1024]{1,0:T(8,128)(2,1)S(1)}, bf16[128,1024]{1,0:T(8,128)(2,1)S(1)}, u32[]{:S(2)}, u32[]{:S(2)}) collective-permute-start(bf16[128,1024]{1,0:T(8,128)(2,1)S(1)} %collective-permute-done.8.refs_5_), channel_id=1, source_target_pairs={{4,6},{5,7},{6,4},{7,5},{8,10},{9,11},{10,8},{11,9},{20,22},{21,23... | collective-permute-start | bytes 786440 | tf_op jit(solution)/shard_map/ppermute | solution.py:275
  28.8 8.0 %collective-permute-start.13 = (bf16[128,1024]{1,0:T(8,128)(2,1)S(1)}, bf16[128,1024]{1,0:T(8,128)(2,1)S(1)}, u32[]{:S(2)}, u32[]{:S(2)}) collective-permute-start(bf16[128,1024]{1,0:T(8,128)(2,1)S(1)} %collective-permute-done.12.refs_0_), channel_id=1, source_target_pairs={{4,5},{5,4},{6,7},{7,6},{8,9},{9,8},{10,11},{11,10},{20,21},{21,20... | collective-permute-start | bytes 786440 | tf_op jit(solution)/shard_map/ppermute | solution.py:275
  29.5 1.0 %copy-start = (bf16[256,1024]{1,0:T(8,128)(2,1)S(1)}, bf16[256,1024]{1,0:T(8,128)(2,1)}, u32[]{:S(2)}) copy-start(bf16[256,1024]{1,0:T(8,128)(2,1)} %refs_0_.1) | copy-start | bytes 1572868
  38.9 3.3 %collective-permute-start.18 = (f32[1,256]{1,0:T(1,128)S(1)}, f32[1,256]{1,0:T(1,128)S(1)}, u32[]{:S(2)}, u32[]{:S(2)}) collective-permute-start(f32[1,256]{1,0:T(1,128)S(1)} %get-tuple-element.32), channel_id=1, source_target_pairs={{4,6},{5,7},{6,4},{7,5},{8,10},{9,11},{10,8},{11,9},{20,22},{21,23... | collective-permute-start | bytes 3080 | tf_op jit(solution)/shard_map/ppermute | solution.py:275
  39.6 34.2 %collective-permute-start.19 = (f32[1,256]{1,0:T(1,128)S(1)}, f32[1,256]{1,0:T(1,128)S(1)}, u32[]{:S(2)}, u32[]{:S(2)}) collective-permute-start(f32[1,256]{1,0:T(1,128)S(1)} %get-tuple-element.33), channel_id=1, source_target_pairs={{4,0},{5,1},{6,2},{7,3},{8,12},{9,13},{10,14},{11,15},{20,16},{21,... | collective-permute-start | bytes 3080 | tf_op jit(solution)/shard_map/ppermute | solution.py:275
  40.9 34.5 %collective-permute-start.20 = (f32[1,256]{1,0:T(1,128)S(1)}, f32[1,256]{1,0:T(1,128)S(1)}, u32[]{:S(2)}, u32[]{:S(2)}) collective-permute-start(f32[1,256]{1,0:T(1,128)S(1)} %get-tuple-element.34), channel_id=1, source_target_pairs={{4,2},{5,3},{6,0},{7,1},{8,14},{9,15},{10,12},{11,13},{20,18},{21,... | collective-permute-start | bytes 3080 | tf_op jit(solution)/shard_map/ppermute | solution.py:275

commit v11 on v10

--- a/solution.py
+++ b/solution.py
@@ -16,6 +16,7 @@
 
 EMPTY = 4.0
 TILE = 256
+ID_ROWS = 16
 VMEM = pl.BlockSpec(memory_space=pltpu.VMEM)
 
 
@@ -109,7 +110,7 @@
     diagonal = lax.broadcasted_iota(jnp.int32, (size, size), 0) == (
         lax.broadcasted_iota(jnp.int32, (size, size), 1)
     )
-    return jnp.sum(jnp.where(diagonal, row, 0), axis=1, keepdims=True)
+    return jnp.sum(jnp.where(diagonal, row, 0.0), axis=1, keepdims=True)
 
 
 def pair_counts(others, other_ids, own, own_ids, itself=None):
@@ -123,113 +124,66 @@
     return jnp.sum(jnp.where(keep, weights, 0.0), axis=0, keepdims=True)
 
 
-def pair_up_kernel(first_ref, second_ref, out_ref):
-    rows = first_ref.shape[0]
-    out_ref[:rows] = first_ref[...]
-    out_ref[rows:] = second_ref[...]
-
-
-def pair_up(first, second):
-    out_shape = jax.ShapeDtypeStruct((2 * first.shape[0], first.shape[1]), first.dtype)
-    return call_kernel("pair_up", pair_up_kernel, out_shape, first, second)
-
-
-OWN, OTHER, END, END_OTHER = range(4)
-
-
-def first_kernel(ids_ref, next_ids_ref, across_ids_ref, *refs):
-    *piece_refs, across_ref, unit_ref, across_unit_ref = refs[:-3]
-    count_refs = refs[-3:]
-    own, own_other, next_own, next_other, end_a, end_b, end_other_a, end_other_b = piece_refs
-    blocks = [
-        ([own], ids_ref, OWN),
-        ([end_a, end_b], ids_ref, END),
-        ([own_other], ids_ref, OTHER),
-        ([end_other_a, end_other_b], ids_ref, END_OTHER),
-        ([next_own], next_ids_ref, OWN),
-        ([next_other], next_ids_ref, OTHER),
-    ]
-    size = own.shape[0]
-    for k, (pieces, _, _) in enumerate(blocks):
-        first = k * size
-        for piece in pieces:
-            unit_ref[first : first + piece.shape[0]] = unit_rows_of(piece[...])
-            first += piece.shape[0]
-    across_unit_ref[...] = unit_rows_of(across_ref[...])
-    wanted = [
-        (unit_ref[:size], ids_ref[OWN : OWN + 1], 0),
-        (unit_ref[size : 2 * size], ids_ref[END : END + 1], 1),
-        (across_unit_ref[...], across_ids_ref[OWN : OWN + 1], -1),
-    ]
-    for j, (rows, row_ids, place) in enumerate(wanted):
-        total = jnp.zeros((1, size), jnp.float32)
-        for k, (_, block_ids, which) in enumerate(blocks):
-            total = total + pair_counts(
-                unit_ref[k * size : (k + 1) * size],
-                block_ids[which : which + 1],
-                rows,
-                row_ids,
-                0 if k == place else None,
-            )
-        count_refs[j][...] = total
-
-
-def more_kernel(half, ids_ref, next_ids_ref, across_ids_ref, unit_ref, across_unit_ref, *refs):
-    far, far_other, across_end, *refs = refs
+def prepare_kernel(rows_ref, ids_ref, whole_ref, first_ref, second_ref):
+    doc_count, feature_count = rows_ref.shape
+    part = doc_count // 2
+    unit = unit_rows_of(rows_ref[...])
+    ids = ids_ref[...].astype(jnp.float32)
+    for first, piece_ref in ((0, whole_ref), (0, first_ref), (part, second_ref)):
+        count = piece_ref.shape[0] - ID_ROWS
+        some = jnp.concatenate(
+            [ids[:, first : first + count], jnp.zeros((1, feature_count - count), jnp.float32)], axis=1
+        )
+        piece_ref[:count] = unit[first : first + count]
+        piece_ref[count:] = jnp.broadcast_to(some, (ID_ROWS, feature_count)).astype(jnp.bfloat16)
+
+
+def both(*pieces):
+    counts = [piece.shape[0] - ID_ROWS for piece in pieces]
+    rows = [piece[:count] for piece, count in zip(pieces, counts)]
+    ids = [piece[count:, :count].astype(jnp.float32)[:1] for piece, count in zip(pieces, counts)]
+    return jnp.concatenate(rows, axis=0), jnp.concatenate(ids, axis=1)
+
+
+def first_kernel(
+    own, across, end_a, end_b, own_other, end_other_a, end_other_b, next_own, next_other, *count_refs
+):
+    wanted = [both(own), both(end_a, end_b), both(across)]
+    blocks = [*wanted[:2], both(own_other), both(end_other_a, end_other_b)]
+    blocks += [both(next_own), both(next_other)]
+    for j, mine in enumerate(wanted):
+        count_refs[j][...] = sum(
+            pair_counts(*block, *mine, 0 if j == k < 2 else None) for k, block in enumerate(blocks)
+        )
+
+
+def more_kernel(
+    half, own, across, end_a, end_b, own_other, end_other_a, end_other_b, next_own, next_other, *refs
+):
+    far_a, far_other_a, across_a, *refs = refs
+    fresh, end = both(far_a, far_other_a), both(across_a)
+    if half == 1:
+        far_b, far_other_b, across_b, end_count_ref, *refs = refs
+        before, end_before = fresh, end
+        fresh, end = both(far_b, far_other_b), both(across_b)
+    count_refs, out_refs, end_out_ref = refs[:3], refs[3:6], refs[6]
+    wanted = [both(own), both(end_a, end_b), both(across)]
+    for j, mine in enumerate(wanted):
+        out_refs[j][...] = count_refs[j][...] + pair_counts(*fresh, *mine)
+    blocks = [fresh, *wanted[:2], both(own_other), both(end_other_a, end_other_b)]
+    blocks += [both(next_own), both(next_other)]
     if half == 0:
-        *refs, far_unit_ref, end_unit_ref = refs
+        end_out_ref[...] = sum(pair_counts(*block, *end) for block in blocks)
     else:
-        before_ref, before_end_ref, end_count_ref, *refs = refs
-    *refs, end_out_ref = refs
-    count_refs, out_refs = refs[:3], refs[3:]
-    size = ids_ref.shape[1]
-    part = far.shape[0]
-    lanes = slice(half * part, (half + 1) * part)
-    fresh = jnp.concatenate([unit_rows_of(far[...]), unit_rows_of(far_other[...])], axis=0)
-    fresh_ids = jnp.concatenate(
-        [next_ids_ref[END : END + 1, lanes], next_ids_ref[END_OTHER : END_OTHER + 1, lanes]], axis=1
-    )
-    end = unit_rows_of(across_end[...])
-    end_ids = across_ids_ref[END : END + 1, lanes]
-    wanted = [
-        (unit_ref[:size], ids_ref[OWN : OWN + 1]),
-        (unit_ref[size : 2 * size], ids_ref[END : END + 1]),
-        (across_unit_ref[...], across_ids_ref[OWN : OWN + 1]),
-    ]
-    for j, (rows, row_ids) in enumerate(wanted):
-        out_refs[j][...] = count_refs[j][...] + pair_counts(fresh, fresh_ids, rows, row_ids)
-
-    def against_column(rows, row_ids):
-        total = pair_counts(fresh, fresh_ids, rows, row_ids)
-        blocks = [(ids_ref, OWN), (ids_ref, END), (ids_ref, OTHER), (ids_ref, END_OTHER)]
-        blocks += [(next_ids_ref, OWN), (next_ids_ref, OTHER)]
-        for k, (block_ids, which) in enumerate(blocks):
-            total = total + pair_counts(
-                unit_ref[k * size : (k + 1) * size], block_ids[which : which + 1], rows, row_ids
-            )
-        return total
-
-    if half == 0:
-        far_unit_ref[...] = fresh
-        end_unit_ref[...] = end
-        end_out_ref[...] = against_column(end, end_ids)
-    else:
-        before_ids = jnp.concatenate(
-            [next_ids_ref[END : END + 1, :part], next_ids_ref[END_OTHER : END_OTHER + 1, :part]],
-            axis=1,
-        )
-        end_out_ref[:, :part] = end_count_ref[...] + pair_counts(
-            fresh, fresh_ids, before_end_ref[...], across_ids_ref[END : END + 1, :part]
-        )
-        end_out_ref[:, part:] = against_column(end, end_ids) + pair_counts(
-            before_ref[...], before_ids, end, end_ids
-        )
+        part = end_count_ref.shape[1]
+        end_out_ref[:, part:] = sum(pair_counts(*block, *end) for block in [*blocks, before])
+        end_out_ref[:, :part] = end_count_ref[...] + pair_counts(*fresh, *end_before)
 
 
 def add_kernel(counts_ref, x_ref, z_ref, xz_ref, out_ref):
     owner = lax.axis_index("owner")
-    own = jnp.where((owner == 1) | (owner == 2), counts_ref[...], 0.0)
-    out_ref[...] = own + x_ref[...] + z_ref[...] + xz_ref[...]
+    middle = (owner == 1) | (owner == 2)
+    out_ref[...] = jnp.where(middle, counts_ref[...] + x_ref[...], z_ref[...] + xz_ref[...])
 
 
 def select_kernel(capacity, counts_ref, slot_ref, out_ref):
@@ -262,85 +216,68 @@
     helpers, cores = lax.axis_size("helper"), lax.axis_size("sub")
     part = doc_count // 2
 
-    def send(x, hops, turn=0, swap=0):
+    def send(x, owners=(0, 1, 2, 3), turn=0, swap=0):
         pairs = [
             (
                 (here * helpers + h) * cores + c,
                 (there * helpers + (h ^ turn)) * cores + (c ^ swap),
             )
-            for here, there in hops
+            for here, there in enumerate(owners)
             for h in range(helpers)
             for c in range(cores)
         ]
         return lax.ppermute(x, ("owner", "helper", "sub"), pairs)
 
-    inwards, outwards = [(0, 1), (3, 2)], [(1, 0), (2, 3)]
-    middle, still = [(1, 2), (2, 1)], [(1, 1), (2, 2)]
-
-    ids = cluster_id.reshape(1, doc_count)
-    next_own = send(embeddings, middle)
-    across = send(embeddings, still, turn=1)
-    own_other = send(embeddings, still, swap=1)
-    end = [send(embeddings[first : first + part], inwards) for first in (0, part)]
-    here_ids = pair_up(ids, swap_cores(ids))
-    here_ids = pair_up(here_ids, send(here_ids, inwards))
-    next_ids = send(here_ids, middle)
-    across_ids = send(here_ids, still, turn=1)
-    end_other = [send(x, still, swap=1) for x in end]
-    far = [send(x, middle) for x in end]
-    across_end = [send(x, still, turn=1) for x in end]
-    next_other = send(next_own, still, swap=1)
-    far_other = [send(x, still, swap=1) for x in far]
-
-    rows = functools.partial(jax.ShapeDtypeStruct, dtype=jnp.bfloat16)
-    sums = functools.partial(jax.ShapeDtypeStruct, dtype=jnp.float32)
-    all_ids = (here_ids, next_ids, across_ids)
-    units, across_units, *counts = call_kernel(
-        "first",
-        first_kernel,
-        [
-            rows((6 * doc_count, feature_count)),
-            rows((doc_count, feature_count)),
-        ]
-        + [sums((1, doc_count))] * 3,
-        *all_ids,
+    neighbours, middle = (1, 0, 3, 2), (0, 2, 1, 3)
+
+    def rows(count):
+        return jax.ShapeDtypeStruct((count, feature_count), jnp.bfloat16)
+
+    def sums(count):
+        return jax.ShapeDtypeStruct((1, count), jnp.float32)
+
+    own, own_a, own_b = call_kernel(
+        "prepare",
+        prepare_kernel,
+        [rows(count + ID_ROWS) for count in (doc_count, part, part)],
         embeddings,
-        own_other,
-        next_own,
-        next_other,
-        *end,
-        *end_other,
-        across,
-    )
-    *counts, end_counts, far_units, end_units = call_kernel(
+        cluster_id.reshape(1, doc_count),
+    )
+    next_own = send(own, middle)
+    across = send(own, turn=1)
+    end_a, end_b = send(own_a, neighbours), send(own_b, neighbours)
+    own_other = send(own, swap=1)
+    far_a, far_b = send(end_a, middle), send(end_b, middle)
+    across_a, across_b = send(end_a, turn=1), send(end_b, turn=1)
+    end_other_a, end_other_b = send(end_a, swap=1), send(end_b, swap=1)
+    next_other = send(next_own, swap=1)
+
+    column = (own, across, end_a, end_b, own_other, end_other_a, end_other_b, next_own, next_other)
+    counts = call_kernel("first", first_kernel, [sums(doc_count)] * 3, *column,)
+    far_other_a = send(far_a, swap=1)
+    *counts, end_counts = call_kernel(
         "more",
         functools.partial(more_kernel, 0),
-        [sums((1, doc_count))] * 3
-        + [
-            sums((1, part)),
-            rows((2 * part, feature_count)),
-            rows((part, feature_count)),
-        ],
-        *all_ids,
-        units,
-        across_units,
-        far[0],
-        far_other[0],
-        across_end[0],
+        [sums(doc_count)] * 3 + [sums(part)],
+        *column,
+        far_a,
+        far_other_a,
+        across_a,
         *counts,
     )
+    far_b, _ = lax.optimization_barrier((far_b, counts[0]))
+    far_other_b = send(far_b, swap=1)
     *counts, end_counts = call_kernel(
         "last",
         functools.partial(more_kernel, 1),
-        [sums((1, doc_count))] * 4,
-        *all_ids,
-        units,
-        across_units,
-        far[1],
-        far_other[1],
-        across_end[1],
-        far_units,
-        end_units,
+        [sums(doc_count)] * 4,
+        *column,
+        far_a,
+        far_other_a,
+        across_a,
+        far_b,
+        far_other_b,
+        across_b,
         end_counts,
         *counts,
     )
@@ -348,11 +285,11 @@
     return call_kernel(
         "add",
         add_kernel,
-        sums((1, doc_count)),
+        sums(doc_count),
         own_counts,
-        send(across_counts, still, turn=1),
-        send(inner_counts, outwards),
-        send(end_counts, outwards, turn=1),
+        send(across_counts, turn=1),
+        send(inner_counts, neighbours),
+        send(end_counts, neighbours, turn=1),
         limit=8 * 2**20,
     )[0]
 

time: 76.6 us -> 49.3 us (0.64)
  waiting for transfers between devices: 40.8 us -> 24.1 us
  starting transfers between devices: 23.1 us -> 15.8 us
  Pallas kernels: 8.91 us -> 7.4 us
  local copies, waits for them, and re-layouts: 2.78 us -> 1.72 us
    ppermute x20 -> x17, waiting for transfers between devices: 39.4 us -> 24.1 us  [send(): return lax.ppermute(x, ('owner', 'helper', 'sub'), pairs)]
    ppermute x20 -> x17, starting transfers between devices: 23.1 us -> 15.8 us  [send(): return lax.ppermute(x, ('owner', 'helper', 'sub'), pairs)]
    pallas_call x6 -> x5, Pallas kernels: 8.91 us -> 7.4 us  [call_kernel(): pl.pallas_call(kernel, out_shape=out_shape, in_specs=[VMEM] * len(args),...]
    ppermute x1 -> x0, waiting for transfers between devices: 1.33 us -> none  [swap_cores(): return lax.ppermute(x, 'sub', [(i, i ^ 1) for i in range(cores)])]
    slice x1 -> x0, local copies, waits for them, and re-layouts: 1.07 us -> none  [body_by_column(): end = [send(embeddings[first:first + part], inwards) for first in (0, part)]]
  transfers between devices with their start and end apart: 21 -> 17, of which waited for: 4 -> 8; matrix products, arithmetic and copies ran while one was open for 1% -> 0% of each run, Pallas kernels for 8% -> 10%
where the time goes in v11:
time: 49.3 us; the launch traced here: 49.1 us
  waiting for transfers between devices  24.1 us (49%)
  starting transfers between devices  15.8 us (32%)
  Pallas kernels  7.4 us (15%)
  local copies, waits for them, and re-layouts  1.72 us (3%)
    ppermute x17, waiting for transfers between devices, send(): return lax.ppermute(x, ('owner', 'helper', 'sub'), pairs)  24.1 us
    ppermute x17, starting transfers between devices, send(): return lax.ppermute(x, ('owner', 'helper', 'sub'), pairs)  15.8 us
    pallas_call x5, Pallas kernels, call_kernel(): pl.pallas_call(kernel, out_shape=out_shape, in_specs=[VMEM] * len(args),...  7.4 us
    unnamed x4, local copies, waits for them, and re-layouts  1.72 us
  transfers between devices with their start and end apart: 17, of which 8 were waited for; matrix products, arithmetic and copies ran while one was open for 0% of the time, Pallas kernels for 10%

profile of v11, /device:TPU:0, one launch (start us, length us, event | category | flops | bytes accessed | tf_op | source)
XLA Modules:
  0.0 49.1 jit_solution(13504490953552983952)
XLA Ops:
  0.0 0.7 %copy-done.1 = s32[256]{0:T(256)S(1)} copy-done((s32[256]{0:T(256)S(1)}, s32[256]{0:T(256)}, u32[]{:S(2)}) %copy-start.1) | copy-done | bytes 1048
  0.7 1.0 %copy-done = bf16[256,1024]{1,0:T(8,128)(2,1)S(1)} copy-done((bf16[256,1024]{1,0:T(8,128)(2,1)S(1)}, bf16[256,1024]{1,0:T(8,128)(2,1)}, u32[]{:S(2)}) %copy-start) | copy-done | bytes 524312
  1.7 0.2 prepare.1
  1.9 0.7 %collective-permute-start.6 = (bf16[272,1024]{1,0:T(8,128)(2,1)S(1)}, bf16[272,1024]{1,0:T(8,128)(2,1)S(1)}, u32[]{:S(2)}, u32[]{:S(2)}) collective-permute-start(bf16[272,1024]{1,0:T(8,128)(2,1)S(1)} %get-tuple-element.20.own), channel_id=1, source_target_pairs={{0,0},{1,1},{2,2},{3,3},{4,8},{5,9},{6,10},{7,11},{8,4},{9,5},{10,... | collective-permute-start | bytes 1671176 | tf_op jit(solution)/shard_map/ppermute | solution.py:229
  2.6 5.9 %collective-permute-start.1 = (bf16[144,1024]{1,0:T(8,128)(2,1)S(1)}, bf16[144,1024]{1,0:T(8,128)(2,1)S(1)}, u32[]{:S(2)}, u32[]{:S(2)}) collective-permute-start(bf16[144,1024]{1,0:T(8,128)(2,1)S(1)} %get-tuple-element.21), channel_id=1, source_target_pairs={{0,4},{1,5},{2,6},{3,7},{4,0},{5,1},{6,2},{7,3},{8,12},{9,13},{10,... | collective-permute-start | bytes 884744 | tf_op jit(solution)/shard_map/ppermute | solution.py:229
  8.5 0.1 collective-permute-start.2
  8.6 1.5 %collective-permute-start = (bf16[272,1024]{1,0:T(8,128)(2,1)S(1)}, bf16[272,1024]{1,0:T(8,128)(2,1)S(1)}, u32[]{:S(2)}, u32[]{:S(2)}) collective-permute-start(bf16[272,1024]{1,0:T(8,128)(2,1)S(1)} %get-tuple-element.20.own), channel_id=1, source_target_pairs={{0,2},{1,3},{2,0},{3,1},{4,6},{5,7},{6,4},{7,5},{8,10},{9,11},{10,... | collective-permute-start | bytes 1671176 | tf_op jit(solution)/shard_map/ppermute | solution.py:229
  10.1 6.3 %collective-permute-done.1.end_a = bf16[144,1024]{1,0:T(8,128)(2,1)S(1)} collective-permute-done((bf16[144,1024]{1,0:T(8,128)(2,1)S(1)}, bf16[144,1024]{1,0:T(8,128)(2,1)S(1)}, u32[]{:S(2)}, u32[]{:S(2)}) %collective-permute-start.1) | collective-permute-done | bytes 294944 | tf_op jit(solution)/shard_map/ppermute | solution.py:229
  16.4 0.7 %collective-permute-start.8 = (bf16[144,1024]{1,0:T(8,128)(2,1)S(1)}, bf16[144,1024]{1,0:T(8,128)(2,1)S(1)}, u32[]{:S(2)}, u32[]{:S(2)}) collective-permute-start(bf16[144,1024]{1,0:T(8,128)(2,1)S(1)} %collective-permute-done.1.end_a), channel_id=1, source_target_pairs={{0,0},{1,1},{2,2},{3,3},{4,8},{5,9},{6,10},{7,11},{8,4},{9,5},{10,... | collective-permute-start | bytes 884744 | tf_op jit(solution)/shard_map/ppermute | solution.py:229
  17.1 4.5 %collective-permute-done.2.end_b = bf16[144,1024]{1,0:T(8,128)(2,1)S(1)} collective-permute-done((bf16[144,1024]{1,0:T(8,128)(2,1)S(1)}, bf16[144,1024]{1,0:T(8,128)(2,1)S(1)}, u32[]{:S(2)}, u32[]{:S(2)}) %collective-permute-start.2) | collective-permute-done | bytes 294944 | tf_op jit(solution)/shard_map/ppermute | solution.py:229
  21.5 0.0 collective-permute-start.4
  21.6 0.0 collective-permute-done.6.next_own
  21.6 0.5 %collective-permute-start.7 = (bf16[272,1024]{1,0:T(8,128)(2,1)S(1)}, bf16[272,1024]{1,0:T(8,128)(2,1)S(1)}, u32[]{:S(2)}, u32[]{:S(2)}) collective-permute-start(bf16[272,1024]{1,0:T(8,128)(2,1)S(1)} %collective-permute-done.6.next_own), channel_id=1, source_target_pairs={{0,1},{1,0},{2,3},{3,2},{4,5},{5,4},{6,7},{7,6},{8,9},{9,8},{10,11... | collective-permute-start | bytes 1671176 | tf_op jit(solution)/shard_map/ppermute | solution.py:229
  22.1 0.0 collective-permute-done.3.own_other
  22.1 0.1 collective-permute-start.5
  22.1 1.5 %collective-permute-done.across = bf16[272,1024]{1,0:T(8,128)(2,1)S(1)} collective-permute-done((bf16[272,1024]{1,0:T(8,128)(2,1)S(1)}, bf16[272,1024]{1,0:T(8,128)(2,1)S(1)}, u32[]{:S(2)}, u32[]{:S(2)}) %collective-permute-start) | collective-permute-done | bytes 557088 | tf_op jit(solution)/shard_map/ppermute | solution.py:229
  23.6 1.5 %collective-permute-start.10 = (bf16[144,1024]{1,0:T(8,128)(2,1)S(1)}, bf16[144,1024]{1,0:T(8,128)(2,1)S(1)}, u32[]{:S(2)}, u32[]{:S(2)}) collective-permute-start(bf16[144,1024]{1,0:T(8,128)(2,1)S(1)} %collective-permute-done.1.end_a), channel_id=1, source_target_pairs={{0,2},{1,3},{2,0},{3,1},{4,6},{5,7},{6,4},{7,5},{8,10},{9,11},{10,... | collective-permute-start | bytes 884744 | tf_op jit(solution)/shard_map/ppermute | solution.py:229
  25.1 0.7 %collective-permute-start.11 = (bf16[144,1024]{1,0:T(8,128)(2,1)S(1)}, bf16[144,1024]{1,0:T(8,128)(2,1)S(1)}, u32[]{:S(2)}, u32[]{:S(2)}) collective-permute-start(bf16[144,1024]{1,0:T(8,128)(2,1)S(1)} %collective-permute-done.2.end_b), channel_id=1, source_target_pairs={{0,0},{1,1},{2,2},{3,3},{4,8},{5,9},{6,10},{7,11},{8,4},{9,5},{10,... | collective-permute-start | bytes 884744 | tf_op jit(solution)/shard_map/ppermute | solution.py:229
  25.8 0.6 %collective-permute-start.13 = (bf16[144,1024]{1,0:T(8,128)(2,1)S(1)}, bf16[144,1024]{1,0:T(8,128)(2,1)S(1)}, u32[]{:S(2)}, u32[]{:S(2)}) collective-permute-start(bf16[144,1024]{1,0:T(8,128)(2,1)S(1)} %collective-permute-done.2.end_b), channel_id=1, source_target_pairs={{0,2},{1,3},{2,0},{3,1},{4,6},{5,7},{6,4},{7,5},{8,10},{9,11},{10,... | collective-permute-start | bytes 884744 | tf_op jit(solution)/shard_map/ppermute | solution.py:229
  26.4 3.0 %first.1 = (f32[1,256]{1,0:T(1,128)S(1)}, f32[1,256]{1,0:T(1,128)S(1)}, f32[1,256]{1,0:T(1,128)S(1)}) custom-call(bf16[272,1024]{1,0:T(8,128)(2,1)S(1)} %get-tuple-element.20.own, bf16[272,1024]{1,0:T(8,128)(2,1)S(1)} %collective-permute-done.across, bf16[144,1024]{1,0:T(8,128)(2,1)S(1)} %collective-permute-done.1.end_a, ...), custom_call_target="tpu_custom_call" | custom-call | tf_op jit(solution)/shard_map/first/pallas_call | solution.py:58
  29.4 4.1 %collective-permute-done.10.refs_2_ = bf16[144,1024]{1,0:T(8,128)(2,1)S(1)} collective-permute-done((bf16[144,1024]{1,0:T(8,128)(2,1)S(1)}, bf16[144,1024]{1,0:T(8,128)(2,1)S(1)}, u32[]{:S(2)}, u32[]{:S(2)}) %collective-permute-start.10) | collective-permute-done | bytes 294944 | tf_op jit(solution)/shard_map/ppermute | solution.py:229
  33.5 1.7 %more.1 = (f32[1,256]{1,0:T(1,128)S(1)}, f32[1,256]{1,0:T(1,128)S(1)}, f32[1,256]{1,0:T(1,128)S(1)}, f32[1,128]{1,0:T(1,128)S(1)}) custom-call(bf16[272,1024]{1,0:T(8,128)(2,1)S(1)} %get-tuple-element.20.own, bf16[272,1024]{1,0:T(8,128)(2,1)S(1)} %collective-permute-done.across, bf16[144,1024]{1,0:T(8,128)(2,1)S(1)} %collective-permute-done.1.end_a, ...), custom_call_target="tpu_custom_call" | custom-call | tf_op jit(solution)/shard_map/more/pallas_call | solution.py:58
  35.2 0.1 collective-permute-start.12
  35.3 3.3 %collective-permute-done.13.refs_5_ = bf16[144,1024]{1,0:T(8,128)(2,1)S(1)} collective-permute-done((bf16[144,1024]{1,0:T(8,128)(2,1)S(1)}, bf16[144,1024]{1,0:T(8,128)(2,1)S(1)}, u32[]{:S(2)}, u32[]{:S(2)}) %collective-permute-start.13) | collective-permute-done | bytes 294944 | tf_op jit(solution)/shard_map/ppermute | solution.py:229
  38.6 2.0 %last.1 = (f32[1,256]{1,0:T(1,128)S(1)}, f32[1,256]{1,0:T(1,128)S(1)}, f32[1,256]{1,0:T(1,128)S(1)}, f32[1,256]{1,0:T(1,128)S(1)}) custom-call(bf16[272,1024]{1,0:T(8,128)(2,1)S(1)} %get-tuple-element.20.own, bf16[272,1024]{1,0:T(8,128)(2,1)S(1)} %collective-permute-done.across, bf16[144,1024]{1,0:T(8,128)(2,1)S(1)} %collective-permute-done.1.end_a, ...), custom_call_target="tpu_custom_call" | custom-call | tf_op jit(solution)/shard_map/last/pallas_call | solution.py:58
  40.6 1.6 %collective-permute-start.14 = (f32[1,256]{1,0:T(1,128)S(1)}, f32[1,256]{1,0:T(1,128)S(1)}, u32[]{:S(2)}, u32[]{:S(2)}) collective-permute-start(f32[1,256]{1,0:T(1,128)S(1)} %get-tuple-element.32), channel_id=1, source_target_pairs={{0,2},{1,3},{2,0},{3,1},{4,6},{5,7},{6,4},{7,5},{8,10},{9,11},{10,... | collective-permute-start | bytes 3080 | tf_op jit(solution)/shard_map/ppermute | solution.py:229
  42.1 1.9 %collective-permute-start.15 = (f32[1,256]{1,0:T(1,128)S(1)}, f32[1,256]{1,0:T(1,128)S(1)}, u32[]{:S(2)}, u32[]{:S(2)}) collective-permute-start(f32[1,256]{1,0:T(1,128)S(1)} %get-tuple-element.33), channel_id=1, source_target_pairs={{0,4},{1,5},{2,6},{3,7},{4,0},{5,1},{6,2},{7,3},{8,12},{9,13},{10,... | collective-permute-start | bytes 3080 | tf_op jit(solution)/shard_map/ppermute | solution.py:229
  44.1 0.1 collective-permute-start.16
  44.1 0.1 collective-permute-done.14.x_ref
  44.2 1.5 %collective-permute-done.15.z_ref = f32[1,256]{1,0:T(1,128)S(1)} collective-permute-done((f32[1,256]{1,0:T(1,128)S(1)}, f32[1,256]{1,0:T(1,128)S(1)}, u32[]{:S(2)}, u32[]{:S(2)}) %collective-permute-start.15) | collective-permute-done | bytes 1056 | tf_op jit(solution)/shard_map/ppermute | solution.py:229
  45.7 2.8 %collective-permute-done.16.xz_ref = f32[1,256]{1,0:T(1,128)S(1)} collective-permute-done((f32[1,256]{1,0:T(1,128)S(1)}, f32[1,256]{1,0:T(1,128)S(1)}, u32[]{:S(2)}, u32[]{:S(2)}) %collective-permute-start.16) | collective-permute-done | bytes 1056 | tf_op jit(solution)/shard_map/ppermute | solution.py:229
  48.5 0.6 %add.1 = f32[1,256]{1,0:T(1,128)} custom-call(f32[1,256]{1,0:T(1,128)S(1)} %get-tuple-element.31.counts_ref, f32[1,256]{1,0:T(1,128)S(1)} %collective-permute-done.14.x_ref, f32[1,256]{1,0:T(1,128)S(1)} %collective-permute-done.15.z_ref, f32[1,256]{1,0:T(1,128)S(1)} %collective-permute-done.16.xz_ref), custom_call_target="tpu_custom_call" | custom-call | tf_op jit(solution)/shard_map/add/pallas_call | solution.py:58
  (11 shorter events, 0.0 us)
Async XLA Ops:
  0.0 0.7 %copy-start.1 = (s32[256]{0:T(256)S(1)}, s32[256]{0:T(256)}, u32[]{:S(2)}) copy-start(s32[256]{0:T(256)} %param.3) | copy-start | bytes 3076
  0.7 1.0 %copy-start = (bf16[256,1024]{1,0:T(8,128)(2,1)S(1)}, bf16[256,1024]{1,0:T(8,128)(2,1)}, u32[]{:S(2)}) copy-start(bf16[256,1024]{1,0:T(8,128)(2,1)} %rows_ref.1) | copy-start | bytes 1572868
  1.9 19.6 %collective-permute-start.6 = (bf16[272,1024]{1,0:T(8,128)(2,1)S(1)}, bf16[272,1024]{1,0:T(8,128)(2,1)S(1)}, u32[]{:S(2)}, u32[]{:S(2)}) collective-permute-start(bf16[272,1024]{1,0:T(8,128)(2,1)S(1)} %get-tuple-element.20.own), channel_id=1, source_target_pairs={{0,0},{1,1},{2,2},{3,3},{4,8},{5,9},{6,10},{7,11},{8,4},{9,5},{10,... | collective-permute-start | bytes 1671176 | tf_op jit(solution)/shard_map/ppermute | solution.py:229
  2.6 13.8 %collective-permute-start.1 = (bf16[144,1024]{1,0:T(8,128)(2,1)S(1)}, bf16[144,1024]{1,0:T(8,128)(2,1)S(1)}, u32[]{:S(2)}, u32[]{:S(2)}) collective-permute-start(bf16[144,1024]{1,0:T(8,128)(2,1)S(1)} %get-tuple-element.21), channel_id=1, source_target_pairs={{0,4},{1,5},{2,6},{3,7},{4,0},{5,1},{6,2},{7,3},{8,12},{9,13},{10,... | collective-permute-start | bytes 884744 | tf_op jit(solution)/shard_map/ppermute | solution.py:229
  8.5 13.0 %collective-permute-start.2 = (bf16[144,1024]{1,0:T(8,128)(2,1)S(1)}, bf16[144,1024]{1,0:T(8,128)(2,1)S(1)}, u32[]{:S(2)}, u32[]{:S(2)}) collective-permute-start(bf16[144,1024]{1,0:T(8,128)(2,1)S(1)} %get-tuple-element.22), channel_id=1, source_target_pairs={{0,4},{1,5},{2,6},{3,7},{4,0},{5,1},{6,2},{7,3},{8,12},{9,13},{10,... | collective-permute-start | bytes 884744 | tf_op jit(solution)/shard_map/ppermute | solution.py:229
  8.6 13.5 %collective-permute-start.3 = (bf16[272,1024]{1,0:T(8,128)(2,1)S(1)}, bf16[272,1024]{1,0:T(8,128)(2,1)S(1)}, u32[]{:S(2)}, u32[]{:S(2)}) collective-permute-start(bf16[272,1024]{1,0:T(8,128)(2,1)S(1)} %get-tuple-element.20.own), channel_id=1, source_target_pairs={{0,1},{1,0},{2,3},{3,2},{4,5},{5,4},{6,7},{7,6},{8,9},{9,8},{10,11... | collective-permute-start | bytes 1671176 | tf_op jit(solution)/shard_map/ppermute | solution.py:229
  8.6 15.0 %collective-permute-start = (bf16[272,1024]{1,0:T(8,128)(2,1)S(1)}, bf16[272,1024]{1,0:T(8,128)(2,1)S(1)}, u32[]{:S(2)}, u32[]{:S(2)}) collective-permute-start(bf16[272,1024]{1,0:T(8,128)(2,1)S(1)} %get-tuple-element.20.own), channel_id=1, source_target_pairs={{0,2},{1,3},{2,0},{3,1},{4,6},{5,7},{6,4},{7,5},{8,10},{9,11},{10,... | collective-permute-start | bytes 1671176 | tf_op jit(solution)/shard_map/ppermute | solution.py:229
  16.4 8.7 %collective-permute-start.8 = (bf16[144,1024]{1,0:T(8,128)(2,1)S(1)}, bf16[144,1024]{1,0:T(8,128)(2,1)S(1)}, u32[]{:S(2)}, u32[]{:S(2)}) collective-permute-start(bf16[144,1024]{1,0:T(8,128)(2,1)S(1)} %collective-permute-done.1.end_a), channel_id=1, source_target_pairs={{0,0},{1,1},{2,2},{3,3},{4,8},{5,9},{6,10},{7,11},{8,4},{9,5},{10,... | collective-permute-start | bytes 884744 | tf_op jit(solution)/shard_map/ppermute | solution.py:229
  21.5 3.6 %collective-permute-start.4 = (bf16[144,1024]{1,0:T(8,128)(2,1)S(1)}, bf16[144,1024]{1,0:T(8,128)(2,1)S(1)}, u32[]{:S(2)}, u32[]{:S(2)}) collective-permute-start(bf16[144,1024]{1,0:T(8,128)(2,1)S(1)} %collective-permute-done.1.end_a), channel_id=1, source_target_pairs={{0,1},{1,0},{2,3},{3,2},{4,5},{5,4},{6,7},{7,6},{8,9},{9,8},{10,11... | collective-permute-start | bytes 884744 | tf_op jit(solution)/shard_map/ppermute | solution.py:229
  21.6 4.9 %collective-permute-start.7 = (bf16[272,1024]{1,0:T(8,128)(2,1)S(1)}, bf16[272,1024]{1,0:T(8,128)(2,1)S(1)}, u32[]{:S(2)}, u32[]{:S(2)}) collective-permute-start(bf16[272,1024]{1,0:T(8,128)(2,1)S(1)} %collective-permute-done.6.next_own), channel_id=1, source_target_pairs={{0,1},{1,0},{2,3},{3,2},{4,5},{5,4},{6,7},{7,6},{8,9},{9,8},{10,11... | collective-permute-start | bytes 1671176 | tf_op jit(solution)/shard_map/ppermute | solution.py:229
  22.1 3.7 %collective-permute-start.5 = (bf16[144,1024]{1,0:T(8,128)(2,1)S(1)}, bf16[144,1024]{1,0:T(8,128)(2,1)S(1)}, u32[]{:S(2)}, u32[]{:S(2)}) collective-permute-start(bf16[144,1024]{1,0:T(8,128)(2,1)S(1)} %collective-permute-done.2.end_b), channel_id=1, source_target_pairs={{0,1},{1,0},{2,3},{3,2},{4,5},{5,4},{6,7},{7,6},{8,9},{9,8},{10,11... | collective-permute-start | bytes 884744 | tf_op jit(solution)/shard_map/ppermute | solution.py:229
  23.6 9.9 %collective-permute-start.10 = (bf16[144,1024]{1,0:T(8,128)(2,1)S(1)}, bf16[144,1024]{1,0:T(8,128)(2,1)S(1)}, u32[]{:S(2)}, u32[]{:S(2)}) collective-permute-start(bf16[144,1024]{1,0:T(8,128)(2,1)S(1)} %collective-permute-done.1.end_a), channel_id=1, source_target_pairs={{0,2},{1,3},{2,0},{3,1},{4,6},{5,7},{6,4},{7,5},{8,10},{9,11},{10,... | collective-permute-start | bytes 884744 | tf_op jit(solution)/shard_map/ppermute | solution.py:229
  25.1 8.4 %collective-permute-start.9 = (bf16[144,1024]{1,0:T(8,128)(2,1)S(1)}, bf16[144,1024]{1,0:T(8,128)(2,1)S(1)}, u32[]{:S(2)}, u32[]{:S(2)}) collective-permute-start(bf16[144,1024]{1,0:T(8,128)(2,1)S(1)} %collective-permute-done.8.refs_0_), channel_id=1, source_target_pairs={{0,1},{1,0},{2,3},{3,2},{4,5},{5,4},{6,7},{7,6},{8,9},{9,8},{10,11... | collective-permute-start | bytes 884744 | tf_op jit(solution)/shard_map/ppermute | solution.py:229
  25.1 10.1 %collective-permute-start.11 = (bf16[144,1024]{1,0:T(8,128)(2,1)S(1)}, bf16[144,1024]{1,0:T(8,128)(2,1)S(1)}, u32[]{:S(2)}, u32[]{:S(2)}) collective-permute-start(bf16[144,1024]{1,0:T(8,128)(2,1)S(1)} %collective-permute-done.2.end_b), channel_id=1, source_target_pairs={{0,0},{1,1},{2,2},{3,3},{4,8},{5,9},{6,10},{7,11},{8,4},{9,5},{10,... | collective-permute-start | bytes 884744 | tf_op jit(solution)/shard_map/ppermute | solution.py:229
  25.8 12.8 %collective-permute-start.13 = (bf16[144,1024]{1,0:T(8,128)(2,1)S(1)}, bf16[144,1024]{1,0:T(8,128)(2,1)S(1)}, u32[]{:S(2)}, u32[]{:S(2)}) collective-permute-start(bf16[144,1024]{1,0:T(8,128)(2,1)S(1)} %collective-permute-done.2.end_b), channel_id=1, source_target_pairs={{0,2},{1,3},{2,0},{3,1},{4,6},{5,7},{6,4},{7,5},{8,10},{9,11},{10,... | collective-permute-start | bytes 884744 | tf_op jit(solution)/shard_map/ppermute | solution.py:229
  35.2 3.4 %collective-permute-start.12 = (bf16[144,1024]{1,0:T(8,128)(2,1)S(1)}, bf16[144,1024]{1,0:T(8,128)(2,1)S(1)}, u32[]{:S(2)}, u32[]{:S(2)}) collective-permute-start(bf16[144,1024]{1,0:T(8,128)(2,1)S(1)} %collective-permute-done.11.refs_3_), channel_id=1, source_target_pairs={{0,1},{1,0},{2,3},{3,2},{4,5},{5,4},{6,7},{7,6},{8,9},{9,8},{10,11... | collective-permute-start | bytes 884744 | tf_op jit(solution)/shard_map/ppermute | solution.py:229
  40.6 3.6 %collective-permute-start.14 = (f32[1,256]{1,0:T(1,128)S(1)}, f32[1,256]{1,0:T(1,128)S(1)}, u32[]{:S(2)}, u32[]{:S(2)}) collective-permute-start(f32[1,256]{1,0:T(1,128)S(1)} %get-tuple-element.32), channel_id=1, source_target_pairs={{0,2},{1,3},{2,0},{3,1},{4,6},{5,7},{6,4},{7,5},{8,10},{9,11},{10,... | collective-permute-start | bytes 3080 | tf_op jit(solution)/shard_map/ppermute | solution.py:229
  42.1 3.6 %collective-permute-start.15 = (f32[1,256]{1,0:T(1,128)S(1)}, f32[1,256]{1,0:T(1,128)S(1)}, u32[]{:S(2)}, u32[]{:S(2)}) collective-permute-start(f32[1,256]{1,0:T(1,128)S(1)} %get-tuple-element.33), channel_id=1, source_target_pairs={{0,4},{1,5},{2,6},{3,7},{4,0},{5,1},{6,2},{7,3},{8,12},{9,13},{10,... | collective-permute-start | bytes 3080 | tf_op jit(solution)/shard_map/ppermute | solution.py:229
  44.1 4.5 %collective-permute-start.16 = (f32[1,256]{1,0:T(1,128)S(1)}, f32[1,256]{1,0:T(1,128)S(1)}, u32[]{:S(2)}, u32[]{:S(2)}) collective-permute-start(f32[1,256]{1,0:T(1,128)S(1)} %get-tuple-element.34), channel_id=1, source_target_pairs={{0,6},{1,7},{2,4},{3,5},{4,2},{5,3},{6,0},{7,1},{8,14},{9,15},{10,... | collective-permute-start | bytes 3080 | tf_op jit(solution)/shard_map/ppermute | solution.py:229

commit v12 on v7

--- a/solution.py
+++ b/solution.py
@@ -141,9 +141,10 @@
     return call_kernel("count", functools.partial(count_kernel, starts, size), out_shape, *pieces)
 
 
-def finish_kernel(starts, late_pieces, late_starts, places, *refs):
-    *piece_refs, early_ref, count_ref = refs
-    size = count_ref.shape[2]
+def finish_kernel(starts, late_pieces, late_starts, distances, *refs):
+    *piece_refs, early_ref = refs[:-2]
+    halves = refs[-2:]
+    size = halves[0].shape[1]
     early = jnp.concatenate([piece[...] for piece in piece_refs[:-late_pieces]], axis=0)
     late = jnp.concatenate([piece[...] for piece in piece_refs[-late_pieces:]], axis=0)
     own = blocks(early, starts, size)
@@ -152,9 +153,26 @@
     late_total = count_against(early, late_own, [], size) + count_against(
         late, late_own, late_starts, size
     )
-    for k, place in enumerate(places()):
+    for k, distance in enumerate(distances()):
         source, j = (total, k) if k < len(starts) else (late_total, k - len(starts))
-        count_ref[pl.ds(place, 1), 0, :] = source[:, j * size : (j + 1) * size]
+        block = source[:, j * size : (j + 1) * size]
+        keep_ref, send_ref = halves
+        half = keep_ref.shape[0]
+        for ref, first in ((keep_ref, 0), (send_ref, half)):
+
+            @pl.when((distance >= first) & (distance < first + half))
+            def _(ref=ref, first=first, block=block, distance=distance):
+                ref[pl.ds(distance - first, 1), :] = block
+
+
+def deal_kernel(width, keep_ref, got_ref, stay_ref, send_ref):
+    blocks = jnp.concatenate([keep_ref[...], got_ref[...]], axis=0)
+    stay, send = [], []
+    for first in range(0, blocks.shape[0], 2 * width):
+        stay.append(blocks[first : first + width])
+        send.append(blocks[first + width : first + 2 * width])
+    stay_ref[...] = jnp.concatenate(stay, axis=0)
+    send_ref[...] = jnp.concatenate(send, axis=0)
 
 
 def select_kernel(capacity, counts_ref, slot_ref, out_ref):
@@ -177,6 +195,24 @@
     return call_kernel("select", kernel, out_shape, counts, slot, limit=8 * 2**20)[0]
 
 
+def choose_kernel(capacity, near_ref, far_ref, slot_ref, out_ref):
+    counts = jnp.concatenate([near_ref[...], far_ref[...]], axis=0)
+    slot = slot_ref[...]
+    block = slot // capacity
+    rank = slot - block * capacity
+    hot = lax.broadcasted_iota(jnp.int32, (capacity, slot.shape[1]), 0) == rank
+    by_block = jnp.dot(
+        counts,
+        hot.astype(jnp.float32),
+        precision=lax.Precision.HIGHEST,
+        preferred_element_type=jnp.float32,
+    )
+    row = lax.broadcasted_iota(jnp.int32, by_block.shape, 0)
+    distance = ((row & 1) << 2) | (row & 2) | (row >> 2)
+    chosen = distance == block ^ chip_index()
+    out_ref[...] = jnp.sum(jnp.where(chosen, by_block, 0.0), axis=0, keepdims=True)
+
+
 def swap_cores(x):
     cores = lax.axis_size("sub")
     return lax.ppermute(x, "sub", [(i, i ^ 1) for i in range(cores)])
@@ -196,6 +232,10 @@
             for core in range(cores)
         ]
         return lax.ppermute(x, ("owner", "helper", "sub"), pairs)
+
+    def swap_chips(x, distance):
+        pairs = [(chip, chip ^ distance) for chip in range(clusters)]
+        return lax.ppermute(x, ("owner", "helper"), pairs)
 
     ids = cluster_id.reshape(1, doc_count)
     other_rows, other_ids = swap_cores(embeddings), swap_cores(ids)
@@ -234,24 +274,35 @@
     starts += [half_way + start + capacity for start in starts]
     late_starts = [0, span + capacity]
 
-    def places():
-        chip, core = chip_index(), lax.axis_index("sub")
-        return (
-            [chip ^ (p * cores + core) for p in (first, *middle)]
-            + [chip ^ (p * cores + 1 - core) for p in (first, *middle)]
-            + [chip ^ (last * cores + core), chip ^ (last * cores + 1 - core)]
-        )
-
-    counts = call_kernel(
+    def distances():
+        core = lax.axis_index("sub")
+        own = [p * cores + core for p in (first, *middle, last)]
+        other = [p * cores + 1 - core for p in (first, *middle, last)]
+        return own[:-1] + other[:-1] + [own[-1], other[-1]]
+
+    half_counts = [jax.ShapeDtypeStruct((clusters // 2, capacity), jnp.float32)] * 2
+    keep, send = call_kernel(
         "finish",
-        functools.partial(finish_kernel, starts, len(late), late_starts, places),
-        jax.ShapeDtypeStruct((clusters, 1, capacity), jnp.float32),
+        functools.partial(finish_kernel, starts, len(late), late_starts, distances),
+        half_counts,
         *early,
         *late,
         soft_counts(early, starts, capacity),
     )
-    back = lax.all_to_all(counts, ("owner", "helper"), split_axis=0, concat_axis=0, tiled=True)
-    return select(back, slot, capacity)
+    got = swap_chips(send, 4)
+    keep, send = call_kernel("deal", functools.partial(deal_kernel, 2), half_counts, keep, got)
+    got = swap_chips(send, 2)
+    keep, send = call_kernel("deal", functools.partial(deal_kernel, 1), half_counts, keep, got)
+    got = swap_chips(send, 1)
+    return call_kernel(
+        "choose",
+        functools.partial(choose_kernel, capacity),
+        jax.ShapeDtypeStruct(slot.shape, jnp.float32),
+        keep,
+        got,
+        slot,
+        limit=8 * 2**20,
+    )[0]
 
 
 def body_by_owner(embeddings, cluster_id):
@@ -297,5 +348,6 @@
         P(("groups", "owner", "helper", "sub")),
     )
     out_specs = P(("groups", "owner", "helper", "sub"))
-    body = body_by_chip if mesh.shape["helper"] == CL_OWN else body_by_owner
+    chips = tuple(mesh.shape[axis] for axis in ("owner", "helper", "sub"))
+    body = body_by_chip if chips == (4, CL_OWN, 2) else body_by_owner
     return jax.shard_map(body, mesh=mesh, in_specs=in_specs, out_specs=out_specs, check_vma=False)

time: 44.8 us -> 45.7 us (1.020)
  blocking collectives: 12.4 us -> 0 us
  waiting for transfers between devices: 7.34 us -> 14 us
  starting transfers between devices: 19.4 us -> 25.8 us
    all_to_all x1 -> x0, blocking collectives: 12.4 us -> none  [body_by_chip(): lax.all_to_all(counts, ('owner', 'helper'), split_axis=0, concat_axis=0,...]
    ppermute x0 -> x3, waiting for transfers between devices: none -> 6.69 us  [swap_chips(): return lax.ppermute(x, ('owner', 'helper'), pairs)]
    ppermute x0 -> x3, starting transfers between devices: none -> 6.43 us  [swap_chips(): return lax.ppermute(x, ('owner', 'helper'), pairs)]
    pallas_call x6 -> x8, Pallas kernels: 4.21 us -> 4.34 us  [call_kernel(): pl.pallas_call(kernel, out_shape=out_shape, in_specs=[VMEM] * len(args),...]
  transfers between devices with their start and end apart: 11 -> 14, of which waited for: 3 -> 6; matrix products, arithmetic and copies ran while one was open for 0% -> 0% of each run, Pallas kernels for 5% -> 5%
where the time goes in v12:
time: 45.7 us; the launch traced here: 45.5 us
  starting transfers between devices  25.8 us (56%)
  waiting for transfers between devices  14 us (31%)
  Pallas kernels  4.34 us (9%)
  local copies, waits for them, and re-layouts  1.27 us (3%)
    ppermute x6, starting transfers between devices, swap_cores(): return lax.ppermute(x, 'sub', [(i, i ^ 1) for i in range(cores)])  10.5 us
    ppermute x5, starting transfers between devices, across(): return lax.ppermute(x, ('owner', 'helper', 'sub'), pairs)  8.83 us
    ppermute x3, waiting for transfers between devices, swap_chips(): return lax.ppermute(x, ('owner', 'helper'), pairs)  6.69 us
    ppermute x3, starting transfers between devices, swap_chips(): return lax.ppermute(x, ('owner', 'helper'), pairs)  6.43 us
    ppermute x5, waiting for transfers between devices, across(): return lax.ppermute(x, ('owner', 'helper', 'sub'), pairs)  6.19 us
    pallas_call x8, Pallas kernels, call_kernel(): pl.pallas_call(kernel, out_shape=out_shape, in_specs=[VMEM] * len(args),...  4.34 us
    unnamed x4, local copies, waits for them, and re-layouts  1.27 us
    ppermute x6, waiting for transfers between devices, swap_cores(): return lax.ppermute(x, 'sub', [(i, i ^ 1) for i in range(cores)])  1.15 us
  transfers between devices with their start and end apart: 14, of which 6 were waited for; matrix products, arithmetic and copies ran while one was open for 0% of the time, Pallas kernels for 5%

profile of v12, /device:TPU:0, one launch (start us, length us, event | category | flops | bytes accessed | tf_op | source)
XLA Modules:
  0.0 45.5 jit_solution(17290224613371818826)
XLA Ops:
  0.0 0.5 collective-permute-start.1
  0.5 0.2 copy-done.1
  0.7 0.5 collective-permute-start.2
  1.1 1.0 %copy-done = bf16[256,1024]{1,0:T(8,128)(2,1)S(1)} copy-done((bf16[256,1024]{1,0:T(8,128)(2,1)S(1)}, bf16[256,1024]{1,0:T(8,128)(2,1)}, u32[]{:S(2)}) %copy-start) | copy-done | bytes 524312
  2.2 0.5 %route_first.1 = (bf16[64,1024]{1,0:T(8,128)(2,1)S(1)}, s32[1,256]{1,0:T(1,128)S(1)}) custom-call(bf16[256,1024]{1,0:T(8,128)(2,1)S(1)} %copy-done, s32[1,256]{1,0:T(1,128)S(1)} %bitcast.3), custom_call_target="tpu_custom_call" | custom-call | tf_op jit(solution)/shard_map/route_first/pallas_call | solution.py:92
  2.6 3.7 %collective-permute-start = (bf16[64,1024]{1,0:T(8,128)(2,1)S(1)}, bf16[64,1024]{1,0:T(8,128)(2,1)S(1)}, u32[]{:S(2)}, u32[]{:S(2)}) collective-permute-start(bf16[64,1024]{1,0:T(8,128)(2,1)S(1)} %get-tuple-element.17), channel_id=1, source_target_pairs={{0,8},{1,11},{2,10},{3,9},{4,12},{5,15},{6,14},{7,13},{8,0},{9,3},... | collective-permute-start | bytes 393224 | tf_op jit(solution)/shard_map/ppermute | solution.py:234
  6.3 0.0 collective-permute-done.2.refs_3_
  6.3 0.0 collective-permute-done.1.refs_1_
  6.3 0.7 %route_rest.1 = (bf16[64,1024]{1,0:T(8,128)(2,1)S(1)}, bf16[128,1024]{1,0:T(8,128)(2,1)S(1)}, bf16[128,1024]{1,0:T(8,128)(2,1)S(1)}, bf16[128,1024]{1,0:T(8,128)(2,1)S(1)}) custom-call(bf16[256,1024]{1,0:T(8,128)(2,1)S(1)} %copy-done, bf16[256,1024]{1,0:T(8,128)(2,1)S(1)} %collective-permute-done.1.refs_1_, s32[1,256]{1,0:T(1,128)S(1)} %get-tuple-element.18.refs_2_.slot_ref, ...), custom_call_target="tpu_custom_call" | custom-call | tf_op jit(solution)/shard_map/route_rest/pallas_call | solution.py:92
  7.0 0.1 collective-permute-start.3
  7.1 0.7 %collective-permute-start.4 = (bf16[128,1024]{1,0:T(8,128)(2,1)S(1)}, bf16[128,1024]{1,0:T(8,128)(2,1)S(1)}, u32[]{:S(2)}, u32[]{:S(2)}) collective-permute-start(bf16[128,1024]{1,0:T(8,128)(2,1)S(1)} %get-tuple-element.20), channel_id=1, source_target_pairs={{0,0},{1,3},{2,2},{3,1},{4,4},{5,7},{6,6},{7,5},{8,8},{9,11},{10,1... | collective-permute-start | bytes 786440 | tf_op jit(solution)/shard_map/ppermute | solution.py:234
  7.8 1.9 %collective-permute-start.5 = (bf16[128,1024]{1,0:T(8,128)(2,1)S(1)}, bf16[128,1024]{1,0:T(8,128)(2,1)S(1)}, u32[]{:S(2)}, u32[]{:S(2)}) collective-permute-start(bf16[128,1024]{1,0:T(8,128)(2,1)S(1)} %get-tuple-element.21), channel_id=1, source_target_pairs={{0,4},{1,7},{2,6},{3,5},{4,0},{5,3},{6,2},{7,1},{8,12},{9,15},{10,... | collective-permute-start | bytes 786440 | tf_op jit(solution)/shard_map/ppermute | solution.py:234
  9.8 2.5 %collective-permute-start.9 = (bf16[128,1024]{1,0:T(8,128)(2,1)S(1)}, bf16[128,1024]{1,0:T(8,128)(2,1)S(1)}, u32[]{:S(2)}, u32[]{:S(2)}) collective-permute-start(bf16[128,1024]{1,0:T(8,128)(2,1)S(1)} %get-tuple-element.22), channel_id=1, source_target_pairs={{0,12},{1,15},{2,14},{3,13},{4,8},{5,11},{6,10},{7,9},{8,4},{9,7},... | collective-permute-start | bytes 786440 | tf_op jit(solution)/shard_map/ppermute | solution.py:234
  12.2 3.2 %collective-permute-done.first_ref = bf16[64,1024]{1,0:T(8,128)(2,1)S(1)} collective-permute-done((bf16[64,1024]{1,0:T(8,128)(2,1)S(1)}, bf16[64,1024]{1,0:T(8,128)(2,1)S(1)}, u32[]{:S(2)}, u32[]{:S(2)}) %collective-permute-start) | collective-permute-done | bytes 131104 | tf_op jit(solution)/shard_map/ppermute | solution.py:234
  15.4 3.0 %collective-permute-done.3.second_ref = bf16[64,1024]{1,0:T(8,128)(2,1)S(1)} collective-permute-done((bf16[64,1024]{1,0:T(8,128)(2,1)S(1)}, bf16[64,1024]{1,0:T(8,128)(2,1)S(1)}, u32[]{:S(2)}, u32[]{:S(2)}) %collective-permute-start.3) | collective-permute-done | bytes 131104 | tf_op jit(solution)/shard_map/ppermute | solution.py:234
  18.4 0.9 %collective-permute-start.6 = (bf16[128,1024]{1,0:T(8,128)(2,1)S(1)}, bf16[128,1024]{1,0:T(8,128)(2,1)S(1)}, u32[]{:S(2)}, u32[]{:S(2)}) collective-permute-start(bf16[128,1024]{1,0:T(8,128)(2,1)S(1)} %join.1.refs_0_), channel_id=1, source_target_pairs={{0,1},{1,0},{2,3},{3,2},{4,5},{5,4},{6,7},{7,6},{8,9},{9,8},{10,11... | collective-permute-start | bytes 786440 | tf_op jit(solution)/shard_map/ppermute | solution.py:218
  19.4 0.1 collective-permute-start.7
  19.5 0.0 collective-permute-done.5.refs_2_
  19.5 8.6 %collective-permute-start.8 = (bf16[128,1024]{1,0:T(8,128)(2,1)S(1)}, bf16[128,1024]{1,0:T(8,128)(2,1)S(1)}, u32[]{:S(2)}, u32[]{:S(2)}) collective-permute-start(bf16[128,1024]{1,0:T(8,128)(2,1)S(1)} %collective-permute-done.5.refs_2_), channel_id=1, source_target_pairs={{0,1},{1,0},{2,3},{3,2},{4,5},{5,4},{6,7},{7,6},{8,9},{9,8},{10,11... | collective-permute-start | bytes 786440 | tf_op jit(solution)/shard_map/ppermute | solution.py:218
  28.1 0.0 collective-permute-start.10
  28.1 0.0 collective-permute-done.6.refs_3_
  28.1 0.0 collective-permute-done.7.refs_4_
  28.1 1.1 %collective-permute-done.8.refs_5_ = bf16[128,1024]{1,0:T(8,128)(2,1)S(1)} collective-permute-done((bf16[128,1024]{1,0:T(8,128)(2,1)S(1)}, bf16[128,1024]{1,0:T(8,128)(2,1)S(1)}, u32[]{:S(2)}, u32[]{:S(2)}) %collective-permute-start.8) | collective-permute-done | bytes 262176 | tf_op jit(solution)/shard_map/ppermute | solution.py:218
  29.2 1.2 %count.1.refs_8_ = f32[1,384]{1,0:T(1,128)S(1)} custom-call(bf16[128,1024]{1,0:T(8,128)(2,1)S(1)} %join.1.refs_0_, bf16[128,1024]{1,0:T(8,128)(2,1)S(1)} %collective-permute-done.4.refs_1_, bf16[128,1024]{1,0:T(8,128)(2,1)S(1)} %collective-permute-done.5.refs_2_, bf16[128,1024]{1,0:T(8,128)(2,1)S(1)} %collective-permute-done.6.refs_3_, ...), custom_call_target="tpu_custom_call" | custom-call | tf_op jit(solution)/shard_map/count/pallas_call | solution.py:92
  30.4 1.2 %finish.1 = (f32[4,64]{1,0:T(4,128)S(1)}, f32[4,64]{1,0:T(4,128)S(1)}) custom-call(bf16[128,1024]{1,0:T(8,128)(2,1)S(1)} %join.1.refs_0_, bf16[128,1024]{1,0:T(8,128)(2,1)S(1)} %collective-permute-done.4.refs_1_, bf16[128,1024]{1,0:T(8,128)(2,1)S(1)} %collective-permute-done.5.refs_2_, bf16[128,1024]{1,0:T(8,128)(2,1)S(1)} %collective-permute-done.6.refs_3_, ...), custom_call_target="tpu_custom_call" | custom-call | tf_op jit(solution)/shard_map/finish/pallas_call | solution.py:92
  31.6 4.4 %collective-permute-start.11 = (f32[4,64]{1,0:T(4,128)S(1)}, f32[4,64]{1,0:T(4,128)S(1)}, u32[]{:S(2)}, u32[]{:S(2)}) collective-permute-start(f32[4,64]{1,0:T(4,128)S(1)} %get-tuple-element.24), channel_id=1, source_target_pairs={{0,8},{2,10},{4,12},{6,14},{8,0},{10,2},{12,4},{14,6},{1,9},{3,11}... | collective-permute-start | bytes 3080 | tf_op jit(solution)/shard_map/ppermute | solution.py:238
  36.0 1.6 %collective-permute-done.11.got_ref = f32[4,64]{1,0:T(4,128)S(1)} collective-permute-done((f32[4,64]{1,0:T(4,128)S(1)}, f32[4,64]{1,0:T(4,128)S(1)}, u32[]{:S(2)}, u32[]{:S(2)}) %collective-permute-start.11) | collective-permute-done | bytes 1056 | tf_op jit(solution)/shard_map/ppermute | solution.py:238
  37.6 1.0 %collective-permute-start.12 = (f32[4,64]{1,0:T(4,128)S(1)}, f32[4,64]{1,0:T(4,128)S(1)}, u32[]{:S(2)}, u32[]{:S(2)}) collective-permute-start(f32[4,64]{1,0:T(4,128)S(1)} %get-tuple-element.26), channel_id=1, source_target_pairs={{0,4},{2,6},{4,0},{6,2},{8,12},{10,14},{12,8},{14,10},{1,5},{3,7},... | collective-permute-start | bytes 3080 | tf_op jit(solution)/shard_map/ppermute | solution.py:238
  38.6 2.6 %collective-permute-done.12.got_ref = f32[4,64]{1,0:T(4,128)S(1)} collective-permute-done((f32[4,64]{1,0:T(4,128)S(1)}, f32[4,64]{1,0:T(4,128)S(1)}, u32[]{:S(2)}, u32[]{:S(2)}) %collective-permute-start.12) | collective-permute-done | bytes 1056 | tf_op jit(solution)/shard_map/ppermute | solution.py:238
  41.2 1.0 %collective-permute-start.13 = (f32[4,64]{1,0:T(4,128)S(1)}, f32[4,64]{1,0:T(4,128)S(1)}, u32[]{:S(2)}, u32[]{:S(2)}) collective-permute-start(f32[4,64]{1,0:T(4,128)S(1)} %get-tuple-element.28), channel_id=1, source_target_pairs={{0,2},{2,0},{4,6},{6,4},{8,10},{10,8},{12,14},{14,12},{1,3},{3,1},... | collective-permute-start | bytes 3080 | tf_op jit(solution)/shard_map/ppermute | solution.py:238
  42.2 2.5 %collective-permute-done.13.far_ref = f32[4,64]{1,0:T(4,128)S(1)} collective-permute-done((f32[4,64]{1,0:T(4,128)S(1)}, f32[4,64]{1,0:T(4,128)S(1)}, u32[]{:S(2)}, u32[]{:S(2)}) %collective-permute-start.13) | collective-permute-done | bytes 1056 | tf_op jit(solution)/shard_map/ppermute | solution.py:238
  44.8 0.7 %choose.1 = f32[1,256]{1,0:T(1,128)} custom-call(f32[4,64]{1,0:T(4,128)S(1)} %get-tuple-element.27.near_ref, f32[4,64]{1,0:T(4,128)S(1)} %collective-permute-done.13.far_ref, s32[1,256]{1,0:T(1,128)S(1)} %get-tuple-element.18.refs_2_.slot_ref), custom_call_target="tpu_custom_call" | custom-call | tf_op jit(solution)/shard_map/choose/pallas_call | solution.py:92
  (8 shorter events, 0.0 us)
Async XLA Ops:
  0.0 0.7 %copy-start.1 = (s32[256]{0:T(256)S(1)}, s32[256]{0:T(256)}, u32[]{:S(2)}) copy-start(s32[256]{0:T(256)} %param.3) | copy-start | bytes 3076
  0.0 6.3 %collective-permute-start.1 = (bf16[256,1024]{1,0:T(8,128)(2,1)}, bf16[256,1024]{1,0:T(8,128)(2,1)S(1)}, u32[]{:S(2)}, u32[]{:S(2)}) collective-permute-start(bf16[256,1024]{1,0:T(8,128)(2,1)} %refs_0_.1), channel_id=1, source_target_pairs={{0,1},{1,0},{2,3},{3,2},{4,5},{5,4},{6,7},{7,6},{8,9},{9,8},{10,11... | collective-permute-start | bytes 1572872 | tf_op jit(solution)/shard_map/ppermute | solution.py:218
  0.7 5.6 %collective-permute-start.2 = (s32[1,256]{1,0:T(1,128)S(1)}, s32[1,256]{1,0:T(1,128)S(1)}, u32[]{:S(2)}, u32[]{:S(2)}) collective-permute-start(s32[1,256]{1,0:T(1,128)S(1)} %bitcast.2), channel_id=1, source_target_pairs={{0,1},{1,0},{2,3},{3,2},{4,5},{5,4},{6,7},{7,6},{8,9},{9,8},{10,11... | collective-permute-start | bytes 3080 | tf_op jit(solution)/shard_map/ppermute | solution.py:218
  1.1 1.0 %copy-start = (bf16[256,1024]{1,0:T(8,128)(2,1)S(1)}, bf16[256,1024]{1,0:T(8,128)(2,1)}, u32[]{:S(2)}) copy-start(bf16[256,1024]{1,0:T(8,128)(2,1)} %refs_0_.1) | copy-start | bytes 1572868
  2.6 12.8 %collective-permute-start = (bf16[64,1024]{1,0:T(8,128)(2,1)S(1)}, bf16[64,1024]{1,0:T(8,128)(2,1)S(1)}, u32[]{:S(2)}, u32[]{:S(2)}) collective-permute-start(bf16[64,1024]{1,0:T(8,128)(2,1)S(1)} %get-tuple-element.17), channel_id=1, source_target_pairs={{0,8},{1,11},{2,10},{3,9},{4,12},{5,15},{6,14},{7,13},{8,0},{9,3},... | collective-permute-start | bytes 393224 | tf_op jit(solution)/shard_map/ppermute | solution.py:234
  7.0 11.4 %collective-permute-start.3 = (bf16[64,1024]{1,0:T(8,128)(2,1)S(1)}, bf16[64,1024]{1,0:T(8,128)(2,1)S(1)}, u32[]{:S(2)}, u32[]{:S(2)}) collective-permute-start(bf16[64,1024]{1,0:T(8,128)(2,1)S(1)} %get-tuple-element.19), channel_id=1, source_target_pairs={{0,8},{1,11},{2,10},{3,9},{4,12},{5,15},{6,14},{7,13},{8,0},{9,3},... | collective-permute-start | bytes 393224 | tf_op jit(solution)/shard_map/ppermute | solution.py:234
  7.1 12.3 %collective-permute-start.4 = (bf16[128,1024]{1,0:T(8,128)(2,1)S(1)}, bf16[128,1024]{1,0:T(8,128)(2,1)S(1)}, u32[]{:S(2)}, u32[]{:S(2)}) collective-permute-start(bf16[128,1024]{1,0:T(8,128)(2,1)S(1)} %get-tuple-element.20), channel_id=1, source_target_pairs={{0,0},{1,3},{2,2},{3,1},{4,4},{5,7},{6,6},{7,5},{8,8},{9,11},{10,1... | collective-permute-start | bytes 786440 | tf_op jit(solution)/shard_map/ppermute | solution.py:234
  7.8 11.7 %collective-permute-start.5 = (bf16[128,1024]{1,0:T(8,128)(2,1)S(1)}, bf16[128,1024]{1,0:T(8,128)(2,1)S(1)}, u32[]{:S(2)}, u32[]{:S(2)}) collective-permute-start(bf16[128,1024]{1,0:T(8,128)(2,1)S(1)} %get-tuple-element.21), channel_id=1, source_target_pairs={{0,4},{1,7},{2,6},{3,5},{4,0},{5,3},{6,2},{7,1},{8,12},{9,15},{10,... | collective-permute-start | bytes 786440 | tf_op jit(solution)/shard_map/ppermute | solution.py:234
  9.8 18.3 %collective-permute-start.9 = (bf16[128,1024]{1,0:T(8,128)(2,1)S(1)}, bf16[128,1024]{1,0:T(8,128)(2,1)S(1)}, u32[]{:S(2)}, u32[]{:S(2)}) collective-permute-start(bf16[128,1024]{1,0:T(8,128)(2,1)S(1)} %get-tuple-element.22), channel_id=1, source_target_pairs={{0,12},{1,15},{2,14},{3,13},{4,8},{5,11},{6,10},{7,9},{8,4},{9,7},... | collective-permute-start | bytes 786440 | tf_op jit(solution)/shard_map/ppermute | solution.py:234
  18.4 9.6 %collective-permute-start.6 = (bf16[128,1024]{1,0:T(8,128)(2,1)S(1)}, bf16[128,1024]{1,0:T(8,128)(2,1)S(1)}, u32[]{:S(2)}, u32[]{:S(2)}) collective-permute-start(bf16[128,1024]{1,0:T(8,128)(2,1)S(1)} %join.1.refs_0_), channel_id=1, source_target_pairs={{0,1},{1,0},{2,3},{3,2},{4,5},{5,4},{6,7},{7,6},{8,9},{9,8},{10,11... | collective-permute-start | bytes 786440 | tf_op jit(solution)/shard_map/ppermute | solution.py:218
  19.4 8.7 %collective-permute-start.7 = (bf16[128,1024]{1,0:T(8,128)(2,1)S(1)}, bf16[128,1024]{1,0:T(8,128)(2,1)S(1)}, u32[]{:S(2)}, u32[]{:S(2)}) collective-permute-start(bf16[128,1024]{1,0:T(8,128)(2,1)S(1)} %collective-permute-done.4.refs_1_), channel_id=1, source_target_pairs={{0,1},{1,0},{2,3},{3,2},{4,5},{5,4},{6,7},{7,6},{8,9},{9,8},{10,11... | collective-permute-start | bytes 786440 | tf_op jit(solution)/shard_map/ppermute | solution.py:218
  19.5 9.8 %collective-permute-start.8 = (bf16[128,1024]{1,0:T(8,128)(2,1)S(1)}, bf16[128,1024]{1,0:T(8,128)(2,1)S(1)}, u32[]{:S(2)}, u32[]{:S(2)}) collective-permute-start(bf16[128,1024]{1,0:T(8,128)(2,1)S(1)} %collective-permute-done.5.refs_2_), channel_id=1, source_target_pairs={{0,1},{1,0},{2,3},{3,2},{4,5},{5,4},{6,7},{7,6},{8,9},{9,8},{10,11... | collective-permute-start | bytes 786440 | tf_op jit(solution)/shard_map/ppermute | solution.py:218
  28.1 2.3 %collective-permute-start.10 = (bf16[128,1024]{1,0:T(8,128)(2,1)S(1)}, bf16[128,1024]{1,0:T(8,128)(2,1)S(1)}, u32[]{:S(2)}, u32[]{:S(2)}) collective-permute-start(bf16[128,1024]{1,0:T(8,128)(2,1)S(1)} %collective-permute-done.9.refs_6_), channel_id=1, source_target_pairs={{0,1},{1,0},{2,3},{3,2},{4,5},{5,4},{6,7},{7,6},{8,9},{9,8},{10,11... | collective-permute-start | bytes 786440 | tf_op jit(solution)/shard_map/ppermute | solution.py:218
  31.6 5.9 %collective-permute-start.11 = (f32[4,64]{1,0:T(4,128)S(1)}, f32[4,64]{1,0:T(4,128)S(1)}, u32[]{:S(2)}, u32[]{:S(2)}) collective-permute-start(f32[4,64]{1,0:T(4,128)S(1)} %get-tuple-element.24), channel_id=1, source_target_pairs={{0,8},{2,10},{4,12},{6,14},{8,0},{10,2},{12,4},{14,6},{1,9},{3,11}... | collective-permute-start | bytes 3080 | tf_op jit(solution)/shard_map/ppermute | solution.py:238
  37.6 3.6 %collective-permute-start.12 = (f32[4,64]{1,0:T(4,128)S(1)}, f32[4,64]{1,0:T(4,128)S(1)}, u32[]{:S(2)}, u32[]{:S(2)}) collective-permute-start(f32[4,64]{1,0:T(4,128)S(1)} %get-tuple-element.26), channel_id=1, source_target_pairs={{0,4},{2,6},{4,0},{6,2},{8,12},{10,14},{12,8},{14,10},{1,5},{3,7},... | collective-permute-start | bytes 3080 | tf_op jit(solution)/shard_map/ppermute | solution.py:238
  41.2 3.6 %collective-permute-start.13 = (f32[4,64]{1,0:T(4,128)S(1)}, f32[4,64]{1,0:T(4,128)S(1)}, u32[]{:S(2)}, u32[]{:S(2)}) collective-permute-start(f32[4,64]{1,0:T(4,128)S(1)} %get-tuple-element.28), channel_id=1, source_target_pairs={{0,2},{2,0},{4,6},{6,4},{8,10},{10,8},{12,14},{14,12},{1,3},{3,1},... | collective-permute-start | bytes 3080 | tf_op jit(solution)/shard_map/ppermute | solution.py:238

commit v13 on v7

--- a/solution.py
+++ b/solution.py
@@ -51,13 +51,13 @@
 
 
 def slots_of_steps(slot, capacity, steps):
-    cores = lax.axis_size("sub")
+    half = CL_OWN * lax.axis_size("owner") // lax.axis_size("sub")
     by_distance = slot ^ (chip_index() * capacity)
     distance = by_distance // capacity
     rank = by_distance - distance * capacity
     step = jnp.full_like(slot, -1)
     for place, p in enumerate(steps):
-        step = jnp.where(distance == p * cores + lax.axis_index("sub"), place, step)
+        step = jnp.where(distance == p + half * lax.axis_index("sub"), place, step)
     return jnp.where(step < 0, -1, step * capacity + rank)
 
 
@@ -191,7 +191,7 @@
 
     def across(x, p):
         pairs = [
-            (chip * cores + core, (chip ^ (p * cores + core)) * cores + core)
+            (chip * cores + core, (chip ^ (p + steps * core)) * cores + core)
             for chip in range(clusters)
             for core in range(cores)
         ]
@@ -199,7 +199,7 @@
 
     ids = cluster_id.reshape(1, doc_count)
     other_rows, other_ids = swap_cores(embeddings), swap_cores(ids)
-    first, last = steps // 2, steps - 1
+    first, last = 0, steps - 1
     middle = [p for p in range(steps) if p not in (first, last)]
     half = jax.ShapeDtypeStruct((capacity, feature_count), jnp.bfloat16)
     whole = jax.ShapeDtypeStruct((cores * capacity, feature_count), jnp.bfloat16)
@@ -237,9 +237,9 @@
     def places():
         chip, core = chip_index(), lax.axis_index("sub")
         return (
-            [chip ^ (p * cores + core) for p in (first, *middle)]
-            + [chip ^ (p * cores + 1 - core) for p in (first, *middle)]
-            + [chip ^ (last * cores + core), chip ^ (last * cores + 1 - core)]
+            [chip ^ (p + steps * core) for p in (first, *middle)]
+            + [chip ^ (p + steps * (1 - core)) for p in (first, *middle)]
+            + [chip ^ (last + steps * core), chip ^ (last + steps * (1 - core))]
         )
 
     counts = call_kernel(

time: 44.8 us -> 46.7 us (1.042)
  starting transfers between devices: 19.4 us -> 27.3 us
  waiting for transfers between devices: 7.34 us -> 1.04 us
    ppermute x6, starting transfers between devices: 10.5 us -> 21.8 us  [swap_cores(): return lax.ppermute(x, 'sub', [(i, i ^ 1) for i in range(cores)])]
    ppermute x5, waiting for transfers between devices: 6.19 us -> 0.01 us  [across(): return lax.ppermute(x, ('owner', 'helper', 'sub'), pairs)]
    ppermute x5, starting transfers between devices: 8.83 us -> 5.47 us  [across(): return lax.ppermute(x, ('owner', 'helper', 'sub'), pairs)]
  transfers between devices with their start and end apart: 11 -> 11, of which waited for: 3 -> 2; matrix products, arithmetic and copies ran while one was open for 0% -> 0% of each run, Pallas kernels for 5% -> 5%
where the time goes in v13:
time: 46.7 us; the launch traced here: 46.4 us
  starting transfers between devices  27.3 us (58%)
  blocking collectives  12.5 us (27%)
  Pallas kernels  4.22 us (9%)
  local copies, waits for them, and re-layouts  1.27 us (3%)
  waiting for transfers between devices  1.04 us (2%)
    ppermute x6, starting transfers between devices, swap_cores(): return lax.ppermute(x, 'sub', [(i, i ^ 1) for i in range(cores)])  21.8 us
    all_to_all x1, blocking collectives, body_by_chip(): lax.all_to_all(counts, ('owner', 'helper'), split_axis=0, concat_axis=0,...  12.5 us
    ppermute x5, starting transfers between devices, across(): return lax.ppermute(x, ('owner', 'helper', 'sub'), pairs)  5.47 us
    pallas_call x6, Pallas kernels, call_kernel(): pl.pallas_call(kernel, out_shape=out_shape, in_specs=[VMEM] * len(args),...  4.22 us
    unnamed x4, local copies, waits for them, and re-layouts  1.27 us
    ppermute x6, waiting for transfers between devices, swap_cores(): return lax.ppermute(x, 'sub', [(i, i ^ 1) for i in range(cores)])  1.03 us
  transfers between devices with their start and end apart: 11, of which 2 were waited for; matrix products, arithmetic and copies ran while one was open for 0% of the time, Pallas kernels for 5%

profile of v13, /device:TPU:0, one launch (start us, length us, event | category | flops | bytes accessed | tf_op | source)
XLA Modules:
  0.0 46.4 jit_solution(7353562722835293635)
XLA Ops:
  0.0 0.0 copy-start.1
  0.0 0.5 collective-permute-start.1
  0.5 0.2 copy-done.1
  0.7 0.5 collective-permute-start.2
  1.1 0.0 copy-start
  1.1 1.0 %copy-done = bf16[256,1024]{1,0:T(8,128)(2,1)S(1)} copy-done((bf16[256,1024]{1,0:T(8,128)(2,1)S(1)}, bf16[256,1024]{1,0:T(8,128)(2,1)}, u32[]{:S(2)}) %copy-start) | copy-done | bytes 524312
  2.2 0.5 %route_first.1 = (bf16[64,1024]{1,0:T(8,128)(2,1)S(1)}, s32[1,256]{1,0:T(1,128)S(1)}) custom-call(bf16[256,1024]{1,0:T(8,128)(2,1)S(1)} %copy-done, s32[1,256]{1,0:T(1,128)S(1)} %bitcast.3), custom_call_target="tpu_custom_call" | custom-call | tf_op jit(solution)/shard_map/route_first/pallas_call | solution.py:92
  2.6 0.7 %collective-permute-start = (bf16[64,1024]{1,0:T(8,128)(2,1)S(1)}, bf16[64,1024]{1,0:T(8,128)(2,1)S(1)}, u32[]{:S(2)}, u32[]{:S(2)}) collective-permute-start(bf16[64,1024]{1,0:T(8,128)(2,1)S(1)} %get-tuple-element.11), channel_id=1, source_target_pairs={{0,0},{1,9},{2,2},{3,11},{4,4},{5,13},{6,6},{7,15},{8,8},{9,1},{10... | collective-permute-start | bytes 393224 | tf_op jit(solution)/shard_map/ppermute | solution.py:198
  3.3 0.0 collective-permute-done.2.refs_3_
  3.3 0.0 collective-permute-done.1.refs_1_
  3.3 0.7 %route_rest.1 = (bf16[64,1024]{1,0:T(8,128)(2,1)S(1)}, bf16[128,1024]{1,0:T(8,128)(2,1)S(1)}, bf16[128,1024]{1,0:T(8,128)(2,1)S(1)}, bf16[128,1024]{1,0:T(8,128)(2,1)S(1)}) custom-call(bf16[256,1024]{1,0:T(8,128)(2,1)S(1)} %copy-done, bf16[256,1024]{1,0:T(8,128)(2,1)S(1)} %collective-permute-done.1.refs_1_, s32[1,256]{1,0:T(1,128)S(1)} %get-tuple-element.12.refs_2_.slot_ref, ...), custom_call_target="tpu_custom_call" | custom-call | tf_op jit(solution)/shard_map/route_rest/pallas_call | solution.py:92
  4.1 0.7 %collective-permute-start.3 = (bf16[64,1024]{1,0:T(8,128)(2,1)S(1)}, bf16[64,1024]{1,0:T(8,128)(2,1)S(1)}, u32[]{:S(2)}, u32[]{:S(2)}) collective-permute-start(bf16[64,1024]{1,0:T(8,128)(2,1)S(1)} %get-tuple-element.13), channel_id=1, source_target_pairs={{0,0},{1,9},{2,2},{3,11},{4,4},{5,13},{6,6},{7,15},{8,8},{9,1},{10... | collective-permute-start | bytes 393224 | tf_op jit(solution)/shard_map/ppermute | solution.py:198
  4.8 2.6 %collective-permute-start.4 = (bf16[128,1024]{1,0:T(8,128)(2,1)S(1)}, bf16[128,1024]{1,0:T(8,128)(2,1)S(1)}, u32[]{:S(2)}, u32[]{:S(2)}) collective-permute-start(bf16[128,1024]{1,0:T(8,128)(2,1)S(1)} %get-tuple-element.14), channel_id=1, source_target_pairs={{0,2},{1,11},{2,0},{3,9},{4,6},{5,15},{6,4},{7,13},{8,10},{9,3},{1... | collective-permute-start | bytes 786440 | tf_op jit(solution)/shard_map/ppermute | solution.py:198
  7.3 1.6 %collective-permute-start.5 = (bf16[128,1024]{1,0:T(8,128)(2,1)S(1)}, bf16[128,1024]{1,0:T(8,128)(2,1)S(1)}, u32[]{:S(2)}, u32[]{:S(2)}) collective-permute-start(bf16[128,1024]{1,0:T(8,128)(2,1)S(1)} %get-tuple-element.15), channel_id=1, source_target_pairs={{0,4},{1,13},{2,6},{3,15},{4,0},{5,9},{6,2},{7,11},{8,12},{9,5},{1... | collective-permute-start | bytes 786440 | tf_op jit(solution)/shard_map/ppermute | solution.py:198
  8.9 0.0 collective-permute-start.9
  8.9 0.0 collective-permute-done.first_ref
  8.9 0.0 collective-permute-done.3.second_ref
  8.9 8.8 %collective-permute-start.6 = (bf16[128,1024]{1,0:T(8,128)(2,1)S(1)}, bf16[128,1024]{1,0:T(8,128)(2,1)S(1)}, u32[]{:S(2)}, u32[]{:S(2)}) collective-permute-start(bf16[128,1024]{1,0:T(8,128)(2,1)S(1)} %join.1.refs_0_), channel_id=1, source_target_pairs={{0,1},{1,0},{2,3},{3,2},{4,5},{5,4},{6,7},{7,6},{8,9},{9,8},{10,11... | collective-permute-start | bytes 786440 | tf_op jit(solution)/shard_map/ppermute | solution.py:182
  17.8 0.0 collective-permute-done.4.refs_1_
  17.8 11.6 %collective-permute-start.7 = (bf16[128,1024]{1,0:T(8,128)(2,1)S(1)}, bf16[128,1024]{1,0:T(8,128)(2,1)S(1)}, u32[]{:S(2)}, u32[]{:S(2)}) collective-permute-start(bf16[128,1024]{1,0:T(8,128)(2,1)S(1)} %collective-permute-done.4.refs_1_), channel_id=1, source_target_pairs={{0,1},{1,0},{2,3},{3,2},{4,5},{5,4},{6,7},{7,6},{8,9},{9,8},{10,11... | collective-permute-start | bytes 786440 | tf_op jit(solution)/shard_map/ppermute | solution.py:182
  29.4 0.0 collective-permute-done.5.refs_2_
  29.4 0.0 collective-permute-start.8
  29.4 0.0 collective-permute-done.9.refs_6_
  29.4 0.5 %collective-permute-start.10 = (bf16[128,1024]{1,0:T(8,128)(2,1)S(1)}, bf16[128,1024]{1,0:T(8,128)(2,1)S(1)}, u32[]{:S(2)}, u32[]{:S(2)}) collective-permute-start(bf16[128,1024]{1,0:T(8,128)(2,1)S(1)} %collective-permute-done.9.refs_6_), channel_id=1, source_target_pairs={{0,1},{1,0},{2,3},{3,2},{4,5},{5,4},{6,7},{7,6},{8,9},{9,8},{10,11... | collective-permute-start | bytes 786440 | tf_op jit(solution)/shard_map/ppermute | solution.py:182
  29.9 0.0 collective-permute-done.6.refs_3_
  29.9 0.6 %collective-permute-done.7.refs_4_ = bf16[128,1024]{1,0:T(8,128)(2,1)S(1)} collective-permute-done((bf16[128,1024]{1,0:T(8,128)(2,1)S(1)}, bf16[128,1024]{1,0:T(8,128)(2,1)S(1)}, u32[]{:S(2)}, u32[]{:S(2)}) %collective-permute-start.7) | collective-permute-done | bytes 262176 | tf_op jit(solution)/shard_map/ppermute | solution.py:182
  30.5 0.4 collective-permute-done.8.refs_5_
  30.9 1.1 %count.1.refs_8_ = f32[1,384]{1,0:T(1,128)S(1)} custom-call(bf16[128,1024]{1,0:T(8,128)(2,1)S(1)} %join.1.refs_0_, bf16[128,1024]{1,0:T(8,128)(2,1)S(1)} %collective-permute-done.4.refs_1_, bf16[128,1024]{1,0:T(8,128)(2,1)S(1)} %collective-permute-done.5.refs_2_, bf16[128,1024]{1,0:T(8,128)(2,1)S(1)} %collective-permute-done.6.refs_3_, ...), custom_call_target="tpu_custom_call" | custom-call | tf_op jit(solution)/shard_map/count/pallas_call | solution.py:92
  32.1 0.0 collective-permute-done.10.refs_7_
  32.1 1.1 %finish.1 = f32[8,1,64]{2,1,0:T(1,128)S(1)} custom-call(bf16[128,1024]{1,0:T(8,128)(2,1)S(1)} %join.1.refs_0_, bf16[128,1024]{1,0:T(8,128)(2,1)S(1)} %collective-permute-done.4.refs_1_, bf16[128,1024]{1,0:T(8,128)(2,1)S(1)} %collective-permute-done.5.refs_2_, bf16[128,1024]{1,0:T(8,128)(2,1)S(1)} %collective-permute-done.6.refs_3_, ...), custom_call_target="tpu_custom_call" | custom-call | tf_op jit(solution)/shard_map/finish/pallas_call | solution.py:92
  33.2 12.5 %all_to_all.5.counts_ref = f32[8,1,64]{2,1,0:T(1,128)S(1)} all-to-all(f32[8,1,64]{2,1,0:T(1,128)S(1)} %finish.1), channel_id=1, replica_groups=mesh['groups'=2,'owner'=4,'helper'=2,'sub'=2] {'owner','helper'}, dimensions={0} | all-to-all | bytes 4096 | tf_op jit(solution)/shard_map/all_to_all | solution.py:253
  45.7 0.7 %select.1 = f32[1,256]{1,0:T(1,128)} custom-call(f32[8,1,64]{2,1,0:T(1,128)S(1)} %all_to_all.5.counts_ref, s32[1,256]{1,0:T(1,128)S(1)} %get-tuple-element.12.refs_2_.slot_ref), custom_call_target="tpu_custom_call" | custom-call | tf_op jit(solution)/shard_map/select/pallas_call | solution.py:92
  (1 shorter events, 0.0 us)
Async XLA Ops:
  0.0 0.7 %copy-start.1 = (s32[256]{0:T(256)S(1)}, s32[256]{0:T(256)}, u32[]{:S(2)}) copy-start(s32[256]{0:T(256)} %param.3) | copy-start | bytes 3076
  0.0 3.3 %collective-permute-start.1 = (bf16[256,1024]{1,0:T(8,128)(2,1)}, bf16[256,1024]{1,0:T(8,128)(2,1)S(1)}, u32[]{:S(2)}, u32[]{:S(2)}) collective-permute-start(bf16[256,1024]{1,0:T(8,128)(2,1)} %refs_0_.1), channel_id=1, source_target_pairs={{0,1},{1,0},{2,3},{3,2},{4,5},{5,4},{6,7},{7,6},{8,9},{9,8},{10,11... | collective-permute-start | bytes 1572872 | tf_op jit(solution)/shard_map/ppermute | solution.py:182
  0.7 2.6 %collective-permute-start.2 = (s32[1,256]{1,0:T(1,128)S(1)}, s32[1,256]{1,0:T(1,128)S(1)}, u32[]{:S(2)}, u32[]{:S(2)}) collective-permute-start(s32[1,256]{1,0:T(1,128)S(1)} %bitcast.2), channel_id=1, source_target_pairs={{0,1},{1,0},{2,3},{3,2},{4,5},{5,4},{6,7},{7,6},{8,9},{9,8},{10,11... | collective-permute-start | bytes 3080 | tf_op jit(solution)/shard_map/ppermute | solution.py:182
  1.1 1.0 %copy-start = (bf16[256,1024]{1,0:T(8,128)(2,1)S(1)}, bf16[256,1024]{1,0:T(8,128)(2,1)}, u32[]{:S(2)}) copy-start(bf16[256,1024]{1,0:T(8,128)(2,1)} %refs_0_.1) | copy-start | bytes 1572868
  2.6 6.3 %collective-permute-start = (bf16[64,1024]{1,0:T(8,128)(2,1)S(1)}, bf16[64,1024]{1,0:T(8,128)(2,1)S(1)}, u32[]{:S(2)}, u32[]{:S(2)}) collective-permute-start(bf16[64,1024]{1,0:T(8,128)(2,1)S(1)} %get-tuple-element.11), channel_id=1, source_target_pairs={{0,0},{1,9},{2,2},{3,11},{4,4},{5,13},{6,6},{7,15},{8,8},{9,1},{10... | collective-permute-start | bytes 393224 | tf_op jit(solution)/shard_map/ppermute | solution.py:198
  4.1 4.8 %collective-permute-start.3 = (bf16[64,1024]{1,0:T(8,128)(2,1)S(1)}, bf16[64,1024]{1,0:T(8,128)(2,1)S(1)}, u32[]{:S(2)}, u32[]{:S(2)}) collective-permute-start(bf16[64,1024]{1,0:T(8,128)(2,1)S(1)} %get-tuple-element.13), channel_id=1, source_target_pairs={{0,0},{1,9},{2,2},{3,11},{4,4},{5,13},{6,6},{7,15},{8,8},{9,1},{10... | collective-permute-start | bytes 393224 | tf_op jit(solution)/shard_map/ppermute | solution.py:198
  4.8 13.0 %collective-permute-start.4 = (bf16[128,1024]{1,0:T(8,128)(2,1)S(1)}, bf16[128,1024]{1,0:T(8,128)(2,1)S(1)}, u32[]{:S(2)}, u32[]{:S(2)}) collective-permute-start(bf16[128,1024]{1,0:T(8,128)(2,1)S(1)} %get-tuple-element.14), channel_id=1, source_target_pairs={{0,2},{1,11},{2,0},{3,9},{4,6},{5,15},{6,4},{7,13},{8,10},{9,3},{1... | collective-permute-start | bytes 786440 | tf_op jit(solution)/shard_map/ppermute | solution.py:198
  7.3 22.0 %collective-permute-start.5 = (bf16[128,1024]{1,0:T(8,128)(2,1)S(1)}, bf16[128,1024]{1,0:T(8,128)(2,1)S(1)}, u32[]{:S(2)}, u32[]{:S(2)}) collective-permute-start(bf16[128,1024]{1,0:T(8,128)(2,1)S(1)} %get-tuple-element.15), channel_id=1, source_target_pairs={{0,4},{1,13},{2,6},{3,15},{4,0},{5,9},{6,2},{7,11},{8,12},{9,5},{1... | collective-permute-start | bytes 786440 | tf_op jit(solution)/shard_map/ppermute | solution.py:198
  8.9 20.5 %collective-permute-start.9 = (bf16[128,1024]{1,0:T(8,128)(2,1)S(1)}, bf16[128,1024]{1,0:T(8,128)(2,1)S(1)}, u32[]{:S(2)}, u32[]{:S(2)}) collective-permute-start(bf16[128,1024]{1,0:T(8,128)(2,1)S(1)} %get-tuple-element.16), channel_id=1, source_target_pairs={{0,6},{1,15},{2,4},{3,13},{4,2},{5,11},{6,0},{7,9},{8,14},{9,7},{1... | collective-permute-start | bytes 786440 | tf_op jit(solution)/shard_map/ppermute | solution.py:198
  8.9 20.9 %collective-permute-start.6 = (bf16[128,1024]{1,0:T(8,128)(2,1)S(1)}, bf16[128,1024]{1,0:T(8,128)(2,1)S(1)}, u32[]{:S(2)}, u32[]{:S(2)}) collective-permute-start(bf16[128,1024]{1,0:T(8,128)(2,1)S(1)} %join.1.refs_0_), channel_id=1, source_target_pairs={{0,1},{1,0},{2,3},{3,2},{4,5},{5,4},{6,7},{7,6},{8,9},{9,8},{10,11... | collective-permute-start | bytes 786440 | tf_op jit(solution)/shard_map/ppermute | solution.py:182
  17.8 12.8 %collective-permute-start.7 = (bf16[128,1024]{1,0:T(8,128)(2,1)S(1)}, bf16[128,1024]{1,0:T(8,128)(2,1)S(1)}, u32[]{:S(2)}, u32[]{:S(2)}) collective-permute-start(bf16[128,1024]{1,0:T(8,128)(2,1)S(1)} %collective-permute-done.4.refs_1_), channel_id=1, source_target_pairs={{0,1},{1,0},{2,3},{3,2},{4,5},{5,4},{6,7},{7,6},{8,9},{9,8},{10,11... | collective-permute-start | bytes 786440 | tf_op jit(solution)/shard_map/ppermute | solution.py:182
  29.4 1.5 %collective-permute-start.8 = (bf16[128,1024]{1,0:T(8,128)(2,1)S(1)}, bf16[128,1024]{1,0:T(8,128)(2,1)S(1)}, u32[]{:S(2)}, u32[]{:S(2)}) collective-permute-start(bf16[128,1024]{1,0:T(8,128)(2,1)S(1)} %collective-permute-done.5.refs_2_), channel_id=1, source_target_pairs={{0,1},{1,0},{2,3},{3,2},{4,5},{5,4},{6,7},{7,6},{8,9},{9,8},{10,11... | collective-permute-start | bytes 786440 | tf_op jit(solution)/shard_map/ppermute | solution.py:182
  29.4 2.7 %collective-permute-start.10 = (bf16[128,1024]{1,0:T(8,128)(2,1)S(1)}, bf16[128,1024]{1,0:T(8,128)(2,1)S(1)}, u32[]{:S(2)}, u32[]{:S(2)}) collective-permute-start(bf16[128,1024]{1,0:T(8,128)(2,1)S(1)} %collective-permute-done.9.refs_6_), channel_id=1, source_target_pairs={{0,1},{1,0},{2,3},{3,2},{4,5},{5,4},{6,7},{7,6},{8,9},{9,8},{10,11... | collective-permute-start | bytes 786440 | tf_op jit(solution)/shard_map/ppermute | solution.py:182

commit v14 on v11

--- a/solution.py
+++ b/solution.py
@@ -124,66 +124,85 @@
     return jnp.sum(jnp.where(keep, weights, 0.0), axis=0, keepdims=True)
 
 
-def prepare_kernel(rows_ref, ids_ref, whole_ref, first_ref, second_ref):
+def prepare_kernel(rows_ref, ids_ref, piece_ref):
     doc_count, feature_count = rows_ref.shape
-    part = doc_count // 2
-    unit = unit_rows_of(rows_ref[...])
-    ids = ids_ref[...].astype(jnp.float32)
-    for first, piece_ref in ((0, whole_ref), (0, first_ref), (part, second_ref)):
-        count = piece_ref.shape[0] - ID_ROWS
-        some = jnp.concatenate(
-            [ids[:, first : first + count], jnp.zeros((1, feature_count - count), jnp.float32)], axis=1
+    ids = jnp.concatenate(
+        [ids_ref[...].astype(jnp.float32), jnp.zeros((1, feature_count - doc_count), jnp.float32)],
+        axis=1,
+    )
+    piece_ref[:doc_count] = unit_rows_of(rows_ref[...])
+    piece_ref[doc_count:] = jnp.broadcast_to(ids, (ID_ROWS, feature_count)).astype(jnp.bfloat16)
+
+
+def split(piece):
+    count = piece.shape[0] - ID_ROWS
+    return piece[:count], piece[count:, :count].astype(jnp.float32)[:1]
+
+
+def count_all(others, wanted, same):
+    return [
+        sum(
+            pair_counts(*other, *mine, 0 if same.get(j) == k else None)
+            for k, other in enumerate(others)
         )
-        piece_ref[:count] = unit[first : first + count]
-        piece_ref[count:] = jnp.broadcast_to(some, (ID_ROWS, feature_count)).astype(jnp.bfloat16)
-
-
-def both(*pieces):
-    counts = [piece.shape[0] - ID_ROWS for piece in pieces]
-    rows = [piece[:count] for piece, count in zip(pieces, counts)]
-    ids = [piece[count:, :count].astype(jnp.float32)[:1] for piece, count in zip(pieces, counts)]
+        for j, mine in enumerate(wanted)
+    ]
+
+
+def counts_kernel(others, same, *refs):
+    *block_refs, out_ref = refs
+    blocks = [split(block) for block in block_refs]
+    wanted = [blocks[k] for k in same] + blocks[others:]
+    totals = count_all(blocks[:others], wanted, {j: k for j, k in enumerate(same)})
+    for j, total in enumerate(totals):
+        out_ref[j : j + 1] = total
+
+
+def halve_kernel(piece_ref, first_ref, second_ref):
+    count = piece_ref.shape[0] - ID_ROWS
+    part = count // 2
+    for k, half_ref in enumerate((first_ref, second_ref)):
+        rows = slice(k * part, (k + 1) * part)
+        half_ref[:part] = piece_ref[rows]
+        half_ref[part:] = jnp.zeros_like(half_ref[part:])
+        half_ref[part:, :part] = piece_ref[count:, rows]
+
+
+def joined(*pieces):
+    rows, ids = zip(*[split(piece) for piece in pieces])
     return jnp.concatenate(rows, axis=0), jnp.concatenate(ids, axis=1)
 
 
-def first_kernel(
-    own, across, end_a, end_b, own_other, end_other_a, end_other_b, next_own, next_other, *count_refs
-):
-    wanted = [both(own), both(end_a, end_b), both(across)]
-    blocks = [*wanted[:2], both(own_other), both(end_other_a, end_other_b)]
-    blocks += [both(next_own), both(next_other)]
-    for j, mine in enumerate(wanted):
-        count_refs[j][...] = sum(
-            pair_counts(*block, *mine, 0 if j == k < 2 else None) for k, block in enumerate(blocks)
-        )
-
-
-def more_kernel(
-    half, own, across, end_a, end_b, own_other, end_other_a, end_other_b, next_own, next_other, *refs
-):
-    far_a, far_other_a, across_a, *refs = refs
-    fresh, end = both(far_a, far_other_a), both(across_a)
-    if half == 1:
-        far_b, far_other_b, across_b, end_count_ref, *refs = refs
-        before, end_before = fresh, end
-        fresh, end = both(far_b, far_other_b), both(across_b)
-    count_refs, out_refs, end_out_ref = refs[:3], refs[3:6], refs[6]
-    wanted = [both(own), both(end_a, end_b), both(across)]
-    for j, mine in enumerate(wanted):
-        out_refs[j][...] = count_refs[j][...] + pair_counts(*fresh, *mine)
-    blocks = [fresh, *wanted[:2], both(own_other), both(end_other_a, end_other_b)]
-    blocks += [both(next_own), both(next_other)]
-    if half == 0:
-        end_out_ref[...] = sum(pair_counts(*block, *end) for block in blocks)
-    else:
-        part = end_count_ref.shape[1]
-        end_out_ref[:, part:] = sum(pair_counts(*block, *end) for block in [*blocks, before])
-        end_out_ref[:, :part] = end_count_ref[...] + pair_counts(*fresh, *end_before)
-
-
-def add_kernel(counts_ref, x_ref, z_ref, xz_ref, out_ref):
+def more_kernel(own, end, next_own, x_end, x_end_oa, x_end_ob, out_ref):
+    others = [split(own), split(end), split(next_own)]
+    for j, total in enumerate(count_all(others, [split(x_end), joined(x_end_oa, x_end_ob)], {})):
+        out_ref[j : j + 1] = total
+
+
+def last_kernel(far_ref, *refs):
+    *block_refs, x_end_oa, x_end_ob, before_ref, across_ref, here_ref, there_ref = refs
+    wanted = [split(block) for block in block_refs] + [joined(x_end_oa, x_end_ob)]
+    for j, total in enumerate(count_all([split(far_ref)], wanted, {})):
+        out_ref, row = (here_ref, j) if j < 4 else (there_ref, j - 4)
+        old = across_ref[j // 4 : j // 4 + 1] if row == 3 else before_ref[j - j // 4 : j - j // 4 + 1]
+        out_ref[row : row + 1] = old + total
+
+
+def cores_kernel(here_ref, back_ref, stay_ref, go_ref):
+    total = here_ref[...] + back_ref[...]
+    stay_ref[...] = total[:2]
+    go_ref[...] = total[2:]
+
+
+def across_kernel(stay_ref, back_ref, own_ref, end_ref):
+    total = stay_ref[...] + back_ref[...]
+    own_ref[...] = total[:1]
+    end_ref[...] = total[1:]
+
+
+def choose_kernel(own_ref, end_ref, out_ref):
     owner = lax.axis_index("owner")
-    middle = (owner == 1) | (owner == 2)
-    out_ref[...] = jnp.where(middle, counts_ref[...] + x_ref[...], z_ref[...] + xz_ref[...])
+    out_ref[...] = jnp.where((owner == 1) | (owner == 2), own_ref[...], end_ref[...])
 
 
 def select_kernel(capacity, counts_ref, slot_ref, out_ref):
@@ -214,83 +233,92 @@
 def body_by_column(embeddings, cluster_id):
     doc_count, feature_count = embeddings.shape
     helpers, cores = lax.axis_size("helper"), lax.axis_size("sub")
-    part = doc_count // 2
-
-    def send(x, owners=(0, 1, 2, 3), turn=0, swap=0):
+
+    def send(x, owners=(0, 1, 2, 3), turns=(0, 0, 0, 0), swap=0):
         pairs = [
             (
                 (here * helpers + h) * cores + c,
                 (there * helpers + (h ^ turn)) * cores + (c ^ swap),
             )
-            for here, there in enumerate(owners)
+            for here, (there, turn) in enumerate(zip(owners, turns))
             for h in range(helpers)
             for c in range(cores)
         ]
         return lax.ppermute(x, ("owner", "helper", "sub"), pairs)
 
-    neighbours, middle = (1, 0, 3, 2), (0, 2, 1, 3)
-
-    def rows(count):
-        return jax.ShapeDtypeStruct((count, feature_count), jnp.bfloat16)
-
-    def sums(count):
-        return jax.ShapeDtypeStruct((1, count), jnp.float32)
-
-    own, own_a, own_b = call_kernel(
+    def along(x):
+        return send(x, owners=(1, 0, 3, 2))
+
+    def middle(x):
+        return send(x, owners=(0, 2, 1, 3), turns=(1, 0, 0, 1))
+
+    def across(x):
+        return send(x, turns=(1, 1, 1, 1))
+
+    def other(x):
+        return send(x, swap=1)
+
+    def sums(count, blocks=1):
+        return jax.ShapeDtypeStruct((blocks, count), jnp.float32)
+
+    own = call_kernel(
         "prepare",
         prepare_kernel,
-        [rows(count + ID_ROWS) for count in (doc_count, part, part)],
+        jax.ShapeDtypeStruct((doc_count + ID_ROWS, feature_count), jnp.bfloat16),
         embeddings,
         cluster_id.reshape(1, doc_count),
     )
-    next_own = send(own, middle)
-    across = send(own, turn=1)
-    end_a, end_b = send(own_a, neighbours), send(own_b, neighbours)
-    own_other = send(own, swap=1)
-    far_a, far_b = send(end_a, middle), send(end_b, middle)
-    across_a, across_b = send(end_a, turn=1), send(end_b, turn=1)
-    end_other_a, end_other_b = send(end_a, swap=1), send(end_b, swap=1)
-    next_other = send(next_own, swap=1)
-
-    column = (own, across, end_a, end_b, own_other, end_other_a, end_other_b, next_own, next_other)
-    counts = call_kernel("first", first_kernel, [sums(doc_count)] * 3, *column,)
-    far_other_a = send(far_a, swap=1)
-    *counts, end_counts = call_kernel(
+    x, end, next_own, own_o = across(own), along(own), middle(own), other(own)
+    far, x_end = middle(end), across(end)
+    end_o, x_o = other(end), other(x)
+
+    before = call_kernel(
+        "first",
+        functools.partial(counts_kernel, 3, (0, 1)),
+        sums(doc_count, 6),
+        own,
+        end,
+        next_own,
+        x,
+        own_o,
+        end_o,
+        x_o,
+    )
+    late_x_end, _ = lax.optimization_barrier((x_end, before))
+    half = jax.ShapeDtypeStruct((doc_count // 2 + ID_ROWS, feature_count), jnp.bfloat16)
+    x_end_o = [other(x) for x in call_kernel("halve", halve_kernel, [half] * 2, late_x_end)]
+    before_x = call_kernel(
         "more",
-        functools.partial(more_kernel, 0),
-        [sums(doc_count)] * 3 + [sums(part)],
-        *column,
-        far_a,
-        far_other_a,
-        across_a,
-        *counts,
-    )
-    far_b, _ = lax.optimization_barrier((far_b, counts[0]))
-    far_other_b = send(far_b, swap=1)
-    *counts, end_counts = call_kernel(
+        more_kernel,
+        sums(doc_count, 2),
+        own,
+        end,
+        next_own,
+        x_end,
+        *x_end_o,
+    )
+    here, there = call_kernel(
         "last",
-        functools.partial(more_kernel, 1),
-        [sums(doc_count)] * 4,
-        *column,
-        far_a,
-        far_other_a,
-        across_a,
-        far_b,
-        far_other_b,
-        across_b,
-        end_counts,
-        *counts,
-    )
-    own_counts, inner_counts, across_counts = counts
+        last_kernel,
+        [sums(doc_count, 4)] * 2,
+        far,
+        own,
+        end,
+        x,
+        x_end,
+        own_o,
+        end_o,
+        x_o,
+        *x_end_o,
+        before,
+        before_x,
+    )
+    stay, go = call_kernel("cores", cores_kernel, [sums(doc_count, 2)] * 2, here, other(there))
+    own_sum, end_sum = call_kernel(
+        "across", across_kernel, [sums(doc_count)] * 2, stay, across(go)
+    )
     return call_kernel(
-        "add",
-        add_kernel,
-        sums(doc_count),
-        own_counts,
-        send(across_counts, turn=1),
-        send(inner_counts, neighbours),
-        send(end_counts, neighbours, turn=1),
-        limit=8 * 2**20,
+        "choose", choose_kernel, sums(doc_count), own_sum, along(end_sum), limit=8 * 2**20
     )[0]
 
 

time: 49.3 us -> 65.7 us (1.33)
  waiting for transfers between devices: 24.1 us -> 47.8 us
  starting transfers between devices: 15.8 us -> 9.29 us
  Pallas kernels: 7.4 us -> 6.66 us
    ppermute x17 -> x13, waiting for transfers between devices: 24.1 us -> 47.8 us  [send(): return lax.ppermute(x, ('owner', 'helper', 'sub'), pairs)]
    ppermute x17 -> x13, starting transfers between devices: 15.8 us -> 9.29 us  [send(): return lax.ppermute(x, ('owner', 'helper', 'sub'), pairs)]
    pallas_call x5 -> x8, Pallas kernels: 7.4 us -> 6.66 us  [call_kernel(): pl.pallas_call(kernel, out_shape=out_shape, in_specs=[VMEM] * len(args),...]
  transfers between devices with their start and end apart: 17 -> 13, of which waited for: 8 -> 10; matrix products, arithmetic and copies ran while one was open for 0% -> 0% of each run, Pallas kernels for 10% -> 6%
where the time goes in v14:
time: 65.7 us; the launch traced here: 65.5 us
  waiting for transfers between devices  47.8 us (73%)
  starting transfers between devices  9.29 us (14%)
  Pallas kernels  6.66 us (10%)
  local copies, waits for them, and re-layouts  1.72 us (3%)
    ppermute x13, waiting for transfers between devices, send(): return lax.ppermute(x, ('owner', 'helper', 'sub'), pairs)  47.8 us
    ppermute x13, starting transfers between devices, send(): return lax.ppermute(x, ('owner', 'helper', 'sub'), pairs)  9.29 us
    pallas_call x8, Pallas kernels, call_kernel(): pl.pallas_call(kernel, out_shape=out_shape, in_specs=[VMEM] * len(args),...  6.66 us
    unnamed x4, local copies, waits for them, and re-layouts  1.72 us
  transfers between devices with their start and end apart: 13, of which 10 were waited for; matrix products, arithmetic and copies ran while one was open for 0% of the time, Pallas kernels for 6%

profile of v14, /device:TPU:0, one launch (start us, length us, event | category | flops | bytes accessed | tf_op | source)
XLA Modules:
  0.0 65.5 jit_solution(12184685462764030666)
XLA Ops:
  0.0 0.7 %copy-done.1 = s32[256]{0:T(256)S(1)} copy-done((s32[256]{0:T(256)S(1)}, s32[256]{0:T(256)}, u32[]{:S(2)}) %copy-start.1) | copy-done | bytes 1048
  0.7 1.0 %copy-done = bf16[256,1024]{1,0:T(8,128)(2,1)S(1)} copy-done((bf16[256,1024]{1,0:T(8,128)(2,1)S(1)}, bf16[256,1024]{1,0:T(8,128)(2,1)}, u32[]{:S(2)}) %copy-start) | copy-done | bytes 524312
  1.7 0.2 prepare.1.refs_0_.own
  1.9 3.1 %collective-permute-start = (bf16[272,1024]{1,0:T(8,128)(2,1)S(1)}, bf16[272,1024]{1,0:T(8,128)(2,1)S(1)}, u32[]{:S(2)}, u32[]{:S(2)}) collective-permute-start(bf16[272,1024]{1,0:T(8,128)(2,1)S(1)} %prepare.1.refs_0_.own), channel_id=1, source_target_pairs={{0,4},{1,5},{2,6},{3,7},{4,0},{5,1},{6,2},{7,3},{8,12},{9,13},{10,... | collective-permute-start | bytes 1671176 | tf_op jit(solution)/shard_map/ppermute | solution.py:247
  5.0 1.5 %collective-permute-start.2 = (bf16[272,1024]{1,0:T(8,128)(2,1)S(1)}, bf16[272,1024]{1,0:T(8,128)(2,1)S(1)}, u32[]{:S(2)}, u32[]{:S(2)}) collective-permute-start(bf16[272,1024]{1,0:T(8,128)(2,1)S(1)} %prepare.1.refs_0_.own), channel_id=1, source_target_pairs={{0,2},{1,3},{2,0},{3,1},{4,6},{5,7},{6,4},{7,5},{8,10},{9,11},{10,... | collective-permute-start | bytes 1671176 | tf_op jit(solution)/shard_map/ppermute | solution.py:247
  6.5 0.0 collective-permute-start.4
  6.5 0.5 collective-permute-start.7
  7.0 10.6 %collective-permute-done.refs_1_.end = bf16[272,1024]{1,0:T(8,128)(2,1)S(1)} collective-permute-done((bf16[272,1024]{1,0:T(8,128)(2,1)S(1)}, bf16[272,1024]{1,0:T(8,128)(2,1)S(1)}, u32[]{:S(2)}, u32[]{:S(2)}) %collective-permute-start) | collective-permute-done | bytes 557088 | tf_op jit(solution)/shard_map/ppermute | solution.py:247
  17.6 0.0 collective-permute-start.5
  17.6 2.9 %collective-permute-done.2.refs_3_.refs_2_ = bf16[272,1024]{1,0:T(8,128)(2,1)S(1)} collective-permute-done((bf16[272,1024]{1,0:T(8,128)(2,1)S(1)}, bf16[272,1024]{1,0:T(8,128)(2,1)S(1)}, u32[]{:S(2)}, u32[]{:S(2)}) %collective-permute-start.2) | collective-permute-done | bytes 557088 | tf_op jit(solution)/shard_map/ppermute | solution.py:247
  20.6 0.0 collective-permute-start.6
  20.6 1.5 %collective-permute-start.3 = (bf16[272,1024]{1,0:T(8,128)(2,1)S(1)}, bf16[272,1024]{1,0:T(8,128)(2,1)S(1)}, u32[]{:S(2)}, u32[]{:S(2)}) collective-permute-start(bf16[272,1024]{1,0:T(8,128)(2,1)S(1)} %collective-permute-done.refs_1_.end), channel_id=1, source_target_pairs={{0,2},{1,3},{2,0},{3,1},{4,6},{5,7},{6,4},{7,5},{8,10},{9,11},{10,... | collective-permute-start | bytes 1671176 | tf_op jit(solution)/shard_map/ppermute | solution.py:247
  22.1 0.0 collective-permute-done.4.refs_4_
  22.1 0.5 collective-permute-start.1
  22.6 9.9 %collective-permute-done.7.refs_2_.next_own = bf16[272,1024]{1,0:T(8,128)(2,1)S(1)} collective-permute-done((bf16[272,1024]{1,0:T(8,128)(2,1)S(1)}, bf16[272,1024]{1,0:T(8,128)(2,1)S(1)}, u32[]{:S(2)}, u32[]{:S(2)}) %collective-permute-start.7) | collective-permute-done | bytes 557088 | tf_op jit(solution)/shard_map/ppermute | solution.py:247
  32.5 0.0 collective-permute-done.5.refs_5_
  32.5 0.0 collective-permute-done.6.refs_6_
  32.5 3.0 %first.1.refs_9_ = f32[6,256]{1,0:T(8,128)S(1)} custom-call(bf16[272,1024]{1,0:T(8,128)(2,1)S(1)} %prepare.1.refs_0_.own, bf16[272,1024]{1,0:T(8,128)(2,1)S(1)} %collective-permute-done.refs_1_.end, bf16[272,1024]{1,0:T(8,128)(2,1)S(1)} %collective-permute-done.7.refs_2_.next_own, bf16[272,1024]{1,0:T(8,128)(2,1)S(1)} %collective-permute-done.2.refs_3_.refs_2_, ...), custom_call_target="tpu_custom_call" | custom-call | tf_op jit(solution)/shard_map/first/pallas_call | solution.py:58
  35.5 8.9 %collective-permute-done.3.piece_ref.x_end.refs_3_ = bf16[272,1024]{1,0:T(8,128)(2,1)S(1)} collective-permute-done((bf16[272,1024]{1,0:T(8,128)(2,1)S(1)}, bf16[272,1024]{1,0:T(8,128)(2,1)S(1)}, u32[]{:S(2)}, u32[]{:S(2)}) %collective-permute-start.3) | collective-permute-done | bytes 557088 | tf_op jit(solution)/shard_map/ppermute | solution.py:247
  44.5 0.1 collective-permute-start.8
  44.6 0.5 collective-permute-start.9
  45.1 1.1 %collective-permute-done.8.x_end_oa.refs_7_ = bf16[144,1024]{1,0:T(8,128)(2,1)S(1)} collective-permute-done((bf16[144,1024]{1,0:T(8,128)(2,1)S(1)}, bf16[144,1024]{1,0:T(8,128)(2,1)S(1)}, u32[]{:S(2)}, u32[]{:S(2)}) %collective-permute-start.8) | collective-permute-done | bytes 294944 | tf_op jit(solution)/shard_map/ppermute | solution.py:247
  46.1 0.4 collective-permute-done.9.x_end_ob.refs_8_
  46.5 1.2 %more.1.refs_10_ = f32[2,256]{1,0:T(2,128)S(1)} custom-call(bf16[272,1024]{1,0:T(8,128)(2,1)S(1)} %prepare.1.refs_0_.own, bf16[272,1024]{1,0:T(8,128)(2,1)S(1)} %collective-permute-done.refs_1_.end, bf16[272,1024]{1,0:T(8,128)(2,1)S(1)} %collective-permute-done.7.refs_2_.next_own, bf16[272,1024]{1,0:T(8,128)(2,1)S(1)} %collective-permute-done.3.piece_ref.x_end.refs_3_, ...), custom_call_target="tpu_custom_call" | custom-call | tf_op jit(solution)/shard_map/more/pallas_call | solution.py:58
  47.8 7.1 %collective-permute-done.1.far_ref = bf16[272,1024]{1,0:T(8,128)(2,1)S(1)} collective-permute-done((bf16[272,1024]{1,0:T(8,128)(2,1)S(1)}, bf16[272,1024]{1,0:T(8,128)(2,1)S(1)}, u32[]{:S(2)}, u32[]{:S(2)}) %collective-permute-start.1) | collective-permute-done | bytes 557088 | tf_op jit(solution)/shard_map/ppermute | solution.py:247
  54.9 1.6 %last.1 = (f32[4,256]{1,0:T(4,128)S(1)}, f32[4,256]{1,0:T(4,128)S(1)}) custom-call(bf16[272,1024]{1,0:T(8,128)(2,1)S(1)} %collective-permute-done.1.far_ref, bf16[272,1024]{1,0:T(8,128)(2,1)S(1)} %prepare.1.refs_0_.own, bf16[272,1024]{1,0:T(8,128)(2,1)S(1)} %collective-permute-done.refs_1_.end, bf16[272,1024]{1,0:T(8,128)(2,1)S(1)} %collective-permute-done.2.refs_3_.refs_2_, ...), custom_call_target="tpu_custom_call" | custom-call | tf_op jit(solution)/shard_map/last/pallas_call | solution.py:58
  56.5 0.1 collective-permute-start.10
  56.6 1.2 %collective-permute-done.10.back_ref = f32[4,256]{1,0:T(4,128)S(1)} collective-permute-done((f32[4,256]{1,0:T(4,128)S(1)}, f32[4,256]{1,0:T(4,128)S(1)}, u32[]{:S(2)}, u32[]{:S(2)}) %collective-permute-start.10) | collective-permute-done | bytes 4128 | tf_op jit(solution)/shard_map/ppermute | solution.py:247
  57.8 1.5 %collective-permute-start.11 = (f32[2,256]{1,0:T(2,128)S(1)}, f32[2,256]{1,0:T(2,128)S(1)}, u32[]{:S(2)}, u32[]{:S(2)}) collective-permute-start(f32[2,256]{1,0:T(2,128)S(1)} %get-tuple-element.20), channel_id=1, source_target_pairs={{0,2},{1,3},{2,0},{3,1},{4,6},{5,7},{6,4},{7,5},{8,10},{9,11},{10,... | collective-permute-start | bytes 6152 | tf_op jit(solution)/shard_map/ppermute | solution.py:247
  59.3 2.1 %collective-permute-done.11.back_ref = f32[2,256]{1,0:T(2,128)S(1)} collective-permute-done((f32[2,256]{1,0:T(2,128)S(1)}, f32[2,256]{1,0:T(2,128)S(1)}, u32[]{:S(2)}, u32[]{:S(2)}) %collective-permute-start.11) | collective-permute-done | bytes 2080 | tf_op jit(solution)/shard_map/ppermute | solution.py:247
  61.4 3.6 %collective-permute-done.12.end_ref = f32[1,256]{1,0:T(1,128)S(1)} collective-permute-done((f32[1,256]{1,0:T(1,128)S(1)}, f32[1,256]{1,0:T(1,128)S(1)}, u32[]{:S(2)}, u32[]{:S(2)}) %collective-permute-start.12) | collective-permute-done | bytes 1056 | tf_op jit(solution)/shard_map/ppermute | solution.py:247
  64.9 0.6 choose.1
  (6 shorter events, 0.1 us)
Async XLA Ops:
  0.0 0.7 %copy-start.1 = (s32[256]{0:T(256)S(1)}, s32[256]{0:T(256)}, u32[]{:S(2)}) copy-start(s32[256]{0:T(256)} %param.3) | copy-start | bytes 3076
  0.7 1.0 %copy-start = (bf16[256,1024]{1,0:T(8,128)(2,1)S(1)}, bf16[256,1024]{1,0:T(8,128)(2,1)}, u32[]{:S(2)}) copy-start(bf16[256,1024]{1,0:T(8,128)(2,1)} %rows_ref.1) | copy-start | bytes 1572868
  1.9 15.7 %collective-permute-start = (bf16[272,1024]{1,0:T(8,128)(2,1)S(1)}, bf16[272,1024]{1,0:T(8,128)(2,1)S(1)}, u32[]{:S(2)}, u32[]{:S(2)}) collective-permute-start(bf16[272,1024]{1,0:T(8,128)(2,1)S(1)} %prepare.1.refs_0_.own), channel_id=1, source_target_pairs={{0,4},{1,5},{2,6},{3,7},{4,0},{5,1},{6,2},{7,3},{8,12},{9,13},{10,... | collective-permute-start | bytes 1671176 | tf_op jit(solution)/shard_map/ppermute | solution.py:247
  5.0 15.6 %collective-permute-start.2 = (bf16[272,1024]{1,0:T(8,128)(2,1)S(1)}, bf16[272,1024]{1,0:T(8,128)(2,1)S(1)}, u32[]{:S(2)}, u32[]{:S(2)}) collective-permute-start(bf16[272,1024]{1,0:T(8,128)(2,1)S(1)} %prepare.1.refs_0_.own), channel_id=1, source_target_pairs={{0,2},{1,3},{2,0},{3,1},{4,6},{5,7},{6,4},{7,5},{8,10},{9,11},{10,... | collective-permute-start | bytes 1671176 | tf_op jit(solution)/shard_map/ppermute | solution.py:247
  6.5 15.6 %collective-permute-start.4 = (bf16[272,1024]{1,0:T(8,128)(2,1)S(1)}, bf16[272,1024]{1,0:T(8,128)(2,1)S(1)}, u32[]{:S(2)}, u32[]{:S(2)}) collective-permute-start(bf16[272,1024]{1,0:T(8,128)(2,1)S(1)} %prepare.1.refs_0_.own), channel_id=1, source_target_pairs={{0,1},{1,0},{2,3},{3,2},{4,5},{5,4},{6,7},{7,6},{8,9},{9,8},{10,11... | collective-permute-start | bytes 1671176 | tf_op jit(solution)/shard_map/ppermute | solution.py:247
  6.5 26.0 %collective-permute-start.7 = (bf16[272,1024]{1,0:T(8,128)(2,1)S(1)}, bf16[272,1024]{1,0:T(8,128)(2,1)S(1)}, u32[]{:S(2)}, u32[]{:S(2)}) collective-permute-start(bf16[272,1024]{1,0:T(8,128)(2,1)S(1)} %prepare.1.refs_0_.own), channel_id=1, source_target_pairs={{0,2},{1,3},{2,0},{3,1},{4,8},{5,9},{6,10},{7,11},{8,4},{9,5},{10,... | collective-permute-start | bytes 1671176 | tf_op jit(solution)/shard_map/ppermute | solution.py:247
  17.6 14.9 %collective-permute-start.5 = (bf16[272,1024]{1,0:T(8,128)(2,1)S(1)}, bf16[272,1024]{1,0:T(8,128)(2,1)S(1)}, u32[]{:S(2)}, u32[]{:S(2)}) collective-permute-start(bf16[272,1024]{1,0:T(8,128)(2,1)S(1)} %collective-permute-done.refs_1_.end), channel_id=1, source_target_pairs={{0,1},{1,0},{2,3},{3,2},{4,5},{5,4},{6,7},{7,6},{8,9},{9,8},{10,11... | collective-permute-start | bytes 1671176 | tf_op jit(solution)/shard_map/ppermute | solution.py:247
  20.6 11.9 %collective-permute-start.6 = (bf16[272,1024]{1,0:T(8,128)(2,1)S(1)}, bf16[272,1024]{1,0:T(8,128)(2,1)S(1)}, u32[]{:S(2)}, u32[]{:S(2)}) collective-permute-start(bf16[272,1024]{1,0:T(8,128)(2,1)S(1)} %collective-permute-done.2.refs_3_.refs_2_), channel_id=1, source_target_pairs={{0,1},{1,0},{2,3},{3,2},{4,5},{5,4},{6,7},{7,6},{8,9},{9,8},{10,11... | collective-permute-start | bytes 1671176 | tf_op jit(solution)/shard_map/ppermute | solution.py:247
  20.6 23.9 %collective-permute-start.3 = (bf16[272,1024]{1,0:T(8,128)(2,1)S(1)}, bf16[272,1024]{1,0:T(8,128)(2,1)S(1)}, u32[]{:S(2)}, u32[]{:S(2)}) collective-permute-start(bf16[272,1024]{1,0:T(8,128)(2,1)S(1)} %collective-permute-done.refs_1_.end), channel_id=1, source_target_pairs={{0,2},{1,3},{2,0},{3,1},{4,6},{5,7},{6,4},{7,5},{8,10},{9,11},{10,... | collective-permute-start | bytes 1671176 | tf_op jit(solution)/shard_map/ppermute | solution.py:247
  22.1 32.8 %collective-permute-start.1 = (bf16[272,1024]{1,0:T(8,128)(2,1)S(1)}, bf16[272,1024]{1,0:T(8,128)(2,1)S(1)}, u32[]{:S(2)}, u32[]{:S(2)}) collective-permute-start(bf16[272,1024]{1,0:T(8,128)(2,1)S(1)} %collective-permute-done.refs_1_.end), channel_id=1, source_target_pairs={{0,2},{1,3},{2,0},{3,1},{4,8},{5,9},{6,10},{7,11},{8,4},{9,5},{10,... | collective-permute-start | bytes 1671176 | tf_op jit(solution)/shard_map/ppermute | solution.py:247
  44.5 1.6 %collective-permute-start.8 = (bf16[144,1024]{1,0:T(8,128)(2,1)S(1)}, bf16[144,1024]{1,0:T(8,128)(2,1)S(1)}, u32[]{:S(2)}, u32[]{:S(2)}) collective-permute-start(bf16[144,1024]{1,0:T(8,128)(2,1)S(1)} %get-tuple-element.15), channel_id=1, source_target_pairs={{0,1},{1,0},{2,3},{3,2},{4,5},{5,4},{6,7},{7,6},{8,9},{9,8},{10,11... | collective-permute-start | bytes 884744 | tf_op jit(solution)/shard_map/ppermute | solution.py:247
  44.6 2.0 %collective-permute-start.9 = (bf16[144,1024]{1,0:T(8,128)(2,1)S(1)}, bf16[144,1024]{1,0:T(8,128)(2,1)S(1)}, u32[]{:S(2)}, u32[]{:S(2)}) collective-permute-start(bf16[144,1024]{1,0:T(8,128)(2,1)S(1)} %get-tuple-element.16), channel_id=1, source_target_pairs={{0,1},{1,0},{2,3},{3,2},{4,5},{5,4},{6,7},{7,6},{8,9},{9,8},{10,11... | collective-permute-start | bytes 884744 | tf_op jit(solution)/shard_map/ppermute | solution.py:247
  56.5 1.2 %collective-permute-start.10 = (f32[4,256]{1,0:T(4,128)S(1)}, f32[4,256]{1,0:T(4,128)S(1)}, u32[]{:S(2)}, u32[]{:S(2)}) collective-permute-start(f32[4,256]{1,0:T(4,128)S(1)} %get-tuple-element.18), channel_id=1, source_target_pairs={{0,1},{1,0},{2,3},{3,2},{4,5},{5,4},{6,7},{7,6},{8,9},{9,8},{10,11... | collective-permute-start | bytes 12296 | tf_op jit(solution)/shard_map/ppermute | solution.py:247
  57.8 3.6 %collective-permute-start.11 = (f32[2,256]{1,0:T(2,128)S(1)}, f32[2,256]{1,0:T(2,128)S(1)}, u32[]{:S(2)}, u32[]{:S(2)}) collective-permute-start(f32[2,256]{1,0:T(2,128)S(1)} %get-tuple-element.20), channel_id=1, source_target_pairs={{0,2},{1,3},{2,0},{3,1},{4,6},{5,7},{6,4},{7,5},{8,10},{9,11},{10,... | collective-permute-start | bytes 6152 | tf_op jit(solution)/shard_map/ppermute | solution.py:247
  61.4 3.6 %collective-permute-start.12 = (f32[1,256]{1,0:T(1,128)S(1)}, f32[1,256]{1,0:T(1,128)S(1)}, u32[]{:S(2)}, u32[]{:S(2)}) collective-permute-start(f32[1,256]{1,0:T(1,128)S(1)} %get-tuple-element.22), channel_id=1, source_target_pairs={{0,4},{1,5},{2,6},{3,7},{4,0},{5,1},{6,2},{7,3},{8,12},{9,13},{10,... | collective-permute-start | bytes 3080 | tf_op jit(solution)/shard_map/ppermute | solution.py:247

commit v15 on v14

--- a/solution.py
+++ b/solution.py
@@ -158,14 +158,13 @@
         out_ref[j : j + 1] = total
 
 
-def halve_kernel(piece_ref, first_ref, second_ref):
+def half_kernel(which, piece_ref, half_ref):
     count = piece_ref.shape[0] - ID_ROWS
     part = count // 2
-    for k, half_ref in enumerate((first_ref, second_ref)):
-        rows = slice(k * part, (k + 1) * part)
-        half_ref[:part] = piece_ref[rows]
-        half_ref[part:] = jnp.zeros_like(half_ref[part:])
-        half_ref[part:, :part] = piece_ref[count:, rows]
+    rows = slice(which * part, (which + 1) * part)
+    half_ref[:part] = piece_ref[rows]
+    half_ref[part:] = jnp.zeros_like(half_ref[part:])
+    half_ref[part:, :part] = piece_ref[count:, rows]
 
 
 def joined(*pieces):
@@ -173,15 +172,18 @@
     return jnp.concatenate(rows, axis=0), jnp.concatenate(ids, axis=1)
 
 
-def more_kernel(own, end, next_own, x_end, x_end_oa, x_end_ob, out_ref):
+def more_kernel(own, end, next_own, x_end_a, x_end_b, x_end_oa, x_end_ob, out_ref):
     others = [split(own), split(end), split(next_own)]
-    for j, total in enumerate(count_all(others, [split(x_end), joined(x_end_oa, x_end_ob)], {})):
+    wanted = [joined(x_end_a, x_end_b), joined(x_end_oa, x_end_ob)]
+    for j, total in enumerate(count_all(others, wanted, {})):
         out_ref[j : j + 1] = total
 
 
 def last_kernel(far_ref, *refs):
-    *block_refs, x_end_oa, x_end_ob, before_ref, across_ref, here_ref, there_ref = refs
-    wanted = [split(block) for block in block_refs] + [joined(x_end_oa, x_end_ob)]
+    own, end, x, x_end_a, x_end_b, own_o, end_o, x_o, x_end_oa, x_end_ob, *refs = refs
+    before_ref, across_ref, here_ref, there_ref = refs
+    wanted = [split(own), split(end), split(x), joined(x_end_a, x_end_b)]
+    wanted += [split(own_o), split(end_o), split(x_o), joined(x_end_oa, x_end_ob)]
     for j, total in enumerate(count_all([split(far_ref)], wanted, {})):
         out_ref, row = (here_ref, j) if j < 4 else (there_ref, j - 4)
         old = across_ref[j // 4 : j // 4 + 1] if row == 3 else before_ref[j - j // 4 : j - j // 4 + 1]
@@ -234,13 +236,13 @@
     doc_count, feature_count = embeddings.shape
     helpers, cores = lax.axis_size("helper"), lax.axis_size("sub")
 
-    def send(x, owners=(0, 1, 2, 3), turns=(0, 0, 0, 0), swap=0):
+    def send(x, owners=(0, 1, 2, 3), turns=(0, 0, 0, 0), swaps=(0, 0, 0, 0)):
         pairs = [
             (
                 (here * helpers + h) * cores + c,
                 (there * helpers + (h ^ turn)) * cores + (c ^ swap),
             )
-            for here, (there, turn) in enumerate(zip(owners, turns))
+            for here, (there, turn, swap) in enumerate(zip(owners, turns, swaps))
             for h in range(helpers)
             for c in range(cores)
         ]
@@ -250,13 +252,16 @@
         return send(x, owners=(1, 0, 3, 2))
 
     def middle(x):
-        return send(x, owners=(0, 2, 1, 3), turns=(1, 0, 0, 1))
+        return send(x, owners=(0, 2, 1, 3), swaps=(1, 0, 0, 1))
 
     def across(x):
         return send(x, turns=(1, 1, 1, 1))
 
+    def middle_across(x):
+        return send(x, turns=(0, 1, 1, 0), swaps=(1, 0, 0, 1))
+
     def other(x):
-        return send(x, swap=1)
+        return send(x, swaps=(1, 1, 1, 1))
 
     def sums(count, blocks=1):
         return jax.ShapeDtypeStruct((blocks, count), jnp.float32)
@@ -268,9 +273,14 @@
         embeddings,
         cluster_id.reshape(1, doc_count),
     )
-    x, end, next_own, own_o = across(own), along(own), middle(own), other(own)
-    far, x_end = middle(end), across(end)
+    next_own, end, x, own_o = middle(own), along(own), across(own), other(own)
+    far = middle(end)
+    half = jax.ShapeDtypeStruct((doc_count // 2 + ID_ROWS, feature_count), jnp.bfloat16)
+    end_half = call_kernel("half", functools.partial(half_kernel, 0), half, end)
+    x_half = call_kernel("half", functools.partial(half_kernel, 1), half, x)
+    x_end = [middle_across(end_half), along(x_half)]
     end_o, x_o = other(end), other(x)
+    x_end_o = [other(piece) for piece in x_end]
 
     before = call_kernel(
         "first",
@@ -284,18 +294,8 @@
         end_o,
         x_o,
     )
-    late_x_end, _ = lax.optimization_barrier((x_end, before))
-    half = jax.ShapeDtypeStruct((doc_count // 2 + ID_ROWS, feature_count), jnp.bfloat16)
-    x_end_o = [other(x) for x in call_kernel("halve", halve_kernel, [half] * 2, late_x_end)]
     before_x = call_kernel(
-        "more",
-        more_kernel,
-        sums(doc_count, 2),
-        own,
-        end,
-        next_own,
-        x_end,
-        *x_end_o,
+        "more", more_kernel, sums(doc_count, 2), own, end, next_own, *x_end, *x_end_o,
     )
     here, there = call_kernel(
         "last",
@@ -305,7 +305,7 @@
         own,
         end,
         x,
-        x_end,
+        *x_end,
         own_o,
         end_o,
         x_o,
@@ -315,7 +315,7 @@
     )
     stay, go = call_kernel("cores", cores_kernel, [sums(doc_count, 2)] * 2, here, other(there))
     own_sum, end_sum = call_kernel(
-        "across", across_kernel, [sums(doc_count)] * 2, stay, across(go)
+        "across", across_kernel, [sums(doc_count)] * 2, stay, middle_across(go)
     )
     return call_kernel(
         "choose", choose_kernel, sums(doc_count), own_sum, along(end_sum), limit=8 * 2**20

time: 65.7 us -> 46.3 us (0.70)
  waiting for transfers between devices: 47.8 us -> 19.5 us
  starting transfers between devices: 9.29 us -> 18.2 us
    ppermute x13 -> x14, waiting for transfers between devices: 47.8 us -> 19.5 us  [send(): return lax.ppermute(x, ('owner', 'helper', 'sub'), pairs)]
    ppermute x13 -> x14, starting transfers between devices: 9.29 us -> 18.2 us  [send(): return lax.ppermute(x, ('owner', 'helper', 'sub'), pairs)]
    pallas_call x8 -> x9, Pallas kernels: 6.66 us -> 6.62 us  [call_kernel(): pl.pallas_call(kernel, out_shape=out_shape, in_specs=[VMEM] * len(args),...]
  transfers between devices with their start and end apart: 13 -> 14, of which waited for: 10 -> 5; matrix products, arithmetic and copies ran while one was open for 0% -> 0% of each run, Pallas kernels for 6% -> 9%
where the time goes in v15:
time: 46.3 us; the launch traced here: 46.2 us
  waiting for transfers between devices  19.5 us (42%)
  starting transfers between devices  18.2 us (39%)
  Pallas kernels  6.62 us (14%)
  local copies, waits for them, and re-layouts  1.72 us (4%)
    ppermute x14, waiting for transfers between devices, send(): return lax.ppermute(x, ('owner', 'helper', 'sub'), pairs)  19.5 us
    ppermute x14, starting transfers between devices, send(): return lax.ppermute(x, ('owner', 'helper', 'sub'), pairs)  18.2 us
    pallas_call x9, Pallas kernels, call_kernel(): pl.pallas_call(kernel, out_shape=out_shape, in_specs=[VMEM] * len(args),...  6.62 us
    unnamed x4, local copies, waits for them, and re-layouts  1.72 us
  transfers between devices with their start and end apart: 14, of which 5 were waited for; matrix products, arithmetic and copies ran while one was open for 0% of the time, Pallas kernels for 9%

profile of v15, /device:TPU:0, one launch (start us, length us, event | category | flops | bytes accessed | tf_op | source)
XLA Modules:
  0.0 46.2 jit_solution(6113960161817630803)
XLA Ops:
  0.0 0.7 %copy-done.1 = s32[256]{0:T(256)S(1)} copy-done((s32[256]{0:T(256)S(1)}, s32[256]{0:T(256)}, u32[]{:S(2)}) %copy-start.1) | copy-done | bytes 1048
  0.7 1.0 %copy-done = bf16[256,1024]{1,0:T(8,128)(2,1)S(1)} copy-done((bf16[256,1024]{1,0:T(8,128)(2,1)S(1)}, bf16[256,1024]{1,0:T(8,128)(2,1)}, u32[]{:S(2)}) %copy-start) | copy-done | bytes 524312
  1.7 0.2 prepare.1.refs_0_.own
  1.9 3.0 %collective-permute-start.2 = (bf16[272,1024]{1,0:T(8,128)(2,1)S(1)}, bf16[272,1024]{1,0:T(8,128)(2,1)S(1)}, u32[]{:S(2)}, u32[]{:S(2)}) collective-permute-start(bf16[272,1024]{1,0:T(8,128)(2,1)S(1)} %prepare.1.refs_0_.own), channel_id=1, source_target_pairs={{0,2},{1,3},{2,0},{3,1},{4,6},{5,7},{6,4},{7,5},{8,10},{9,11},{10,... | collective-permute-start | bytes 1671176 | tf_op jit(solution)/shard_map/ppermute | solution.py:249
  4.9 1.6 %collective-permute-start = (bf16[272,1024]{1,0:T(8,128)(2,1)S(1)}, bf16[272,1024]{1,0:T(8,128)(2,1)S(1)}, u32[]{:S(2)}, u32[]{:S(2)}) collective-permute-start(bf16[272,1024]{1,0:T(8,128)(2,1)S(1)} %prepare.1.refs_0_.own), channel_id=1, source_target_pairs={{0,4},{1,5},{2,6},{3,7},{4,0},{5,1},{6,2},{7,3},{8,12},{9,13},{10,... | collective-permute-start | bytes 1671176 | tf_op jit(solution)/shard_map/ppermute | solution.py:249
  6.5 0.0 collective-permute-start.10
  6.5 0.5 %collective-permute-start.5 = (bf16[272,1024]{1,0:T(8,128)(2,1)S(1)}, bf16[272,1024]{1,0:T(8,128)(2,1)S(1)}, u32[]{:S(2)}, u32[]{:S(2)}) collective-permute-start(bf16[272,1024]{1,0:T(8,128)(2,1)S(1)} %prepare.1.refs_0_.own), channel_id=1, source_target_pairs={{0,1},{1,0},{2,3},{3,2},{4,5},{5,4},{6,7},{7,6},{8,9},{9,8},{10,11... | collective-permute-start | bytes 1671176 | tf_op jit(solution)/shard_map/ppermute | solution.py:249
  7.0 10.5 %collective-permute-done.2.piece_ref.refs_3_.refs_2_ = bf16[272,1024]{1,0:T(8,128)(2,1)S(1)} collective-permute-done((bf16[272,1024]{1,0:T(8,128)(2,1)S(1)}, bf16[272,1024]{1,0:T(8,128)(2,1)S(1)}, u32[]{:S(2)}, u32[]{:S(2)}) %collective-permute-start.2) | collective-permute-done | bytes 557088 | tf_op jit(solution)/shard_map/ppermute | solution.py:249
  17.6 1.9 %collective-permute-start.4 = (bf16[144,1024]{1,0:T(8,128)(2,1)S(1)}, bf16[144,1024]{1,0:T(8,128)(2,1)S(1)}, u32[]{:S(2)}, u32[]{:S(2)}) collective-permute-start(bf16[144,1024]{1,0:T(8,128)(2,1)S(1)} %half.3), channel_id=1, source_target_pairs={{0,4},{1,5},{2,6},{3,7},{4,0},{5,1},{6,2},{7,3},{8,12},{9,13},{10,... | collective-permute-start | bytes 884744 | tf_op jit(solution)/shard_map/ppermute | solution.py:249
  19.5 0.0 collective-permute-done.piece_ref.refs_1_.end
  19.5 0.1 collective-permute-start.3
  19.6 0.5 %collective-permute-start.7 = (bf16[272,1024]{1,0:T(8,128)(2,1)S(1)}, bf16[272,1024]{1,0:T(8,128)(2,1)S(1)}, u32[]{:S(2)}, u32[]{:S(2)}) collective-permute-start(bf16[272,1024]{1,0:T(8,128)(2,1)S(1)} %collective-permute-done.2.piece_ref.refs_3_.refs_2_), channel_id=1, source_target_pairs={{0,1},{1,0},{2,3},{3,2},{4,5},{5,4},{6,7},{7,6},{8,9},{9,8},{10,11... | collective-permute-start | bytes 1671176 | tf_op jit(solution)/shard_map/ppermute | solution.py:249
  20.1 0.0 collective-permute-done.10.refs_2_.next_own
  20.1 0.1 collective-permute-start.6
  20.1 0.0 collective-permute-done.5.refs_4_.refs_5_
  20.2 0.4 collective-permute-start.1
  20.6 5.2 %collective-permute-done.4.x_end_b.refs_4_ = bf16[144,1024]{1,0:T(8,128)(2,1)S(1)} collective-permute-done((bf16[144,1024]{1,0:T(8,128)(2,1)S(1)}, bf16[144,1024]{1,0:T(8,128)(2,1)S(1)}, u32[]{:S(2)}, u32[]{:S(2)}) %collective-permute-start.4) | collective-permute-done | bytes 294944 | tf_op jit(solution)/shard_map/ppermute | solution.py:249
  25.8 0.0 collective-permute-start.9
  25.8 0.0 collective-permute-done.3.x_end_a.refs_3_
  25.8 0.5 %collective-permute-start.8 = (bf16[144,1024]{1,0:T(8,128)(2,1)S(1)}, bf16[144,1024]{1,0:T(8,128)(2,1)S(1)}, u32[]{:S(2)}, u32[]{:S(2)}) collective-permute-start(bf16[144,1024]{1,0:T(8,128)(2,1)S(1)} %collective-permute-done.3.x_end_a.refs_3_), channel_id=1, source_target_pairs={{0,1},{1,0},{2,3},{3,2},{4,5},{5,4},{6,7},{7,6},{8,9},{9,8},{10,11... | collective-permute-start | bytes 884744 | tf_op jit(solution)/shard_map/ppermute | solution.py:249
  26.4 3.0 %first.1.refs_10_ = f32[6,256]{1,0:T(8,128)S(1)} custom-call(bf16[272,1024]{1,0:T(8,128)(2,1)S(1)} %prepare.1.refs_0_.own, bf16[272,1024]{1,0:T(8,128)(2,1)S(1)} %collective-permute-done.piece_ref.refs_1_.end, bf16[272,1024]{1,0:T(8,128)(2,1)S(1)} %collective-permute-done.10.refs_2_.next_own, ...), custom_call_target="tpu_custom_call" | custom-call | tf_op jit(solution)/shard_map/first/pallas_call | solution.py:58
  29.3 0.0 collective-permute-done.8.x_end_oa.refs_8_
  29.3 1.2 %more.1.refs_11_ = f32[2,256]{1,0:T(2,128)S(1)} custom-call(bf16[272,1024]{1,0:T(8,128)(2,1)S(1)} %prepare.1.refs_0_.own, bf16[272,1024]{1,0:T(8,128)(2,1)S(1)} %collective-permute-done.piece_ref.refs_1_.end, bf16[272,1024]{1,0:T(8,128)(2,1)S(1)} %collective-permute-done.10.refs_2_.next_own, bf16[144,1024]{1,0:T(8,128)(2,1)S(1)} %collective-permute-done.3.x_end_a.refs_3_, ...), custom_call_target="tpu_custom_call" | custom-call | tf_op jit(solution)/shard_map/more/pallas_call | solution.py:58
  30.6 0.0 collective-permute-done.1.far_ref
  30.6 1.6 %last.1 = (f32[4,256]{1,0:T(4,128)S(1)}, f32[4,256]{1,0:T(4,128)S(1)}) custom-call(bf16[272,1024]{1,0:T(8,128)(2,1)S(1)} %collective-permute-done.1.far_ref, bf16[272,1024]{1,0:T(8,128)(2,1)S(1)} %prepare.1.refs_0_.own, bf16[272,1024]{1,0:T(8,128)(2,1)S(1)} %collective-permute-done.piece_ref.refs_1_.end, ...), custom_call_target="tpu_custom_call" | custom-call | tf_op jit(solution)/shard_map/last/pallas_call | solution.py:58
  32.2 0.1 collective-permute-start.11
  32.3 1.2 %collective-permute-done.11.back_ref = f32[4,256]{1,0:T(4,128)S(1)} collective-permute-done((f32[4,256]{1,0:T(4,128)S(1)}, f32[4,256]{1,0:T(4,128)S(1)}, u32[]{:S(2)}, u32[]{:S(2)}) %collective-permute-start.11) | collective-permute-done | bytes 4128 | tf_op jit(solution)/shard_map/ppermute | solution.py:249
  33.5 0.2 collective-permute-start.12
  33.6 1.0 %collective-permute-done.12.back_ref = f32[2,256]{1,0:T(2,128)S(1)} collective-permute-done((f32[2,256]{1,0:T(2,128)S(1)}, f32[2,256]{1,0:T(2,128)S(1)}, u32[]{:S(2)}, u32[]{:S(2)}) %collective-permute-start.12) | collective-permute-done | bytes 2080 | tf_op jit(solution)/shard_map/ppermute | solution.py:249
  34.6 9.4 %collective-permute-start.13 = (f32[1,256]{1,0:T(1,128)S(1)}, f32[1,256]{1,0:T(1,128)S(1)}, u32[]{:S(2)}, u32[]{:S(2)}) collective-permute-start(f32[1,256]{1,0:T(1,128)S(1)} %get-tuple-element.16), channel_id=1, source_target_pairs={{0,4},{1,5},{2,6},{3,7},{4,0},{5,1},{6,2},{7,3},{8,12},{9,13},{10,... | collective-permute-start | bytes 3080 | tf_op jit(solution)/shard_map/ppermute | solution.py:249
  44.0 1.5 %collective-permute-done.13.end_ref = f32[1,256]{1,0:T(1,128)S(1)} collective-permute-done((f32[1,256]{1,0:T(1,128)S(1)}, f32[1,256]{1,0:T(1,128)S(1)}, u32[]{:S(2)}, u32[]{:S(2)}) %collective-permute-start.13) | collective-permute-done | bytes 1056 | tf_op jit(solution)/shard_map/ppermute | solution.py:249
  45.6 0.6 %choose.1 = f32[1,256]{1,0:T(1,128)} custom-call(f32[1,256]{1,0:T(1,128)S(1)} %get-tuple-element.15.own_ref, f32[1,256]{1,0:T(1,128)S(1)} %collective-permute-done.13.end_ref), custom_call_target="tpu_custom_call" | custom-call | tf_op jit(solution)/shard_map/choose/pallas_call | solution.py:58
  (9 shorter events, 0.1 us)
Async XLA Ops:
  0.0 0.7 %copy-start.1 = (s32[256]{0:T(256)S(1)}, s32[256]{0:T(256)}, u32[]{:S(2)}) copy-start(s32[256]{0:T(256)} %param.3) | copy-start | bytes 3076
  0.7 1.0 %copy-start = (bf16[256,1024]{1,0:T(8,128)(2,1)S(1)}, bf16[256,1024]{1,0:T(8,128)(2,1)}, u32[]{:S(2)}) copy-start(bf16[256,1024]{1,0:T(8,128)(2,1)} %rows_ref.1) | copy-start | bytes 1572868
  1.9 15.6 %collective-permute-start.2 = (bf16[272,1024]{1,0:T(8,128)(2,1)S(1)}, bf16[272,1024]{1,0:T(8,128)(2,1)S(1)}, u32[]{:S(2)}, u32[]{:S(2)}) collective-permute-start(bf16[272,1024]{1,0:T(8,128)(2,1)S(1)} %prepare.1.refs_0_.own), channel_id=1, source_target_pairs={{0,2},{1,3},{2,0},{3,1},{4,6},{5,7},{6,4},{7,5},{8,10},{9,11},{10,... | collective-permute-start | bytes 1671176 | tf_op jit(solution)/shard_map/ppermute | solution.py:249
  4.9 14.5 %collective-permute-start = (bf16[272,1024]{1,0:T(8,128)(2,1)S(1)}, bf16[272,1024]{1,0:T(8,128)(2,1)S(1)}, u32[]{:S(2)}, u32[]{:S(2)}) collective-permute-start(bf16[272,1024]{1,0:T(8,128)(2,1)S(1)} %prepare.1.refs_0_.own), channel_id=1, source_target_pairs={{0,4},{1,5},{2,6},{3,7},{4,0},{5,1},{6,2},{7,3},{8,12},{9,13},{10,... | collective-permute-start | bytes 1671176 | tf_op jit(solution)/shard_map/ppermute | solution.py:249
  6.5 13.6 %collective-permute-start.10 = (bf16[272,1024]{1,0:T(8,128)(2,1)S(1)}, bf16[272,1024]{1,0:T(8,128)(2,1)S(1)}, u32[]{:S(2)}, u32[]{:S(2)}) collective-permute-start(bf16[272,1024]{1,0:T(8,128)(2,1)S(1)} %prepare.1.refs_0_.own), channel_id=1, source_target_pairs={{0,1},{1,0},{2,3},{3,2},{4,8},{5,9},{6,10},{7,11},{8,4},{9,5},{10,... | collective-permute-start | bytes 1671176 | tf_op jit(solution)/shard_map/ppermute | solution.py:249
  6.5 13.7 %collective-permute-start.5 = (bf16[272,1024]{1,0:T(8,128)(2,1)S(1)}, bf16[272,1024]{1,0:T(8,128)(2,1)S(1)}, u32[]{:S(2)}, u32[]{:S(2)}) collective-permute-start(bf16[272,1024]{1,0:T(8,128)(2,1)S(1)} %prepare.1.refs_0_.own), channel_id=1, source_target_pairs={{0,1},{1,0},{2,3},{3,2},{4,5},{5,4},{6,7},{7,6},{8,9},{9,8},{10,11... | collective-permute-start | bytes 1671176 | tf_op jit(solution)/shard_map/ppermute | solution.py:249
  17.6 8.3 %collective-permute-start.4 = (bf16[144,1024]{1,0:T(8,128)(2,1)S(1)}, bf16[144,1024]{1,0:T(8,128)(2,1)S(1)}, u32[]{:S(2)}, u32[]{:S(2)}) collective-permute-start(bf16[144,1024]{1,0:T(8,128)(2,1)S(1)} %half.3), channel_id=1, source_target_pairs={{0,4},{1,5},{2,6},{3,7},{4,0},{5,1},{6,2},{7,3},{8,12},{9,13},{10,... | collective-permute-start | bytes 884744 | tf_op jit(solution)/shard_map/ppermute | solution.py:249
  19.5 6.3 %collective-permute-start.3 = (bf16[144,1024]{1,0:T(8,128)(2,1)S(1)}, bf16[144,1024]{1,0:T(8,128)(2,1)S(1)}, u32[]{:S(2)}, u32[]{:S(2)}) collective-permute-start(bf16[144,1024]{1,0:T(8,128)(2,1)S(1)} %half.2), channel_id=1, source_target_pairs={{0,1},{1,0},{2,3},{3,2},{4,6},{5,7},{6,4},{7,5},{8,10},{9,11},{10,... | collective-permute-start | bytes 884744 | tf_op jit(solution)/shard_map/ppermute | solution.py:249
  19.6 6.8 %collective-permute-start.7 = (bf16[272,1024]{1,0:T(8,128)(2,1)S(1)}, bf16[272,1024]{1,0:T(8,128)(2,1)S(1)}, u32[]{:S(2)}, u32[]{:S(2)}) collective-permute-start(bf16[272,1024]{1,0:T(8,128)(2,1)S(1)} %collective-permute-done.2.piece_ref.refs_3_.refs_2_), channel_id=1, source_target_pairs={{0,1},{1,0},{2,3},{3,2},{4,5},{5,4},{6,7},{7,6},{8,9},{9,8},{10,11... | collective-permute-start | bytes 1671176 | tf_op jit(solution)/shard_map/ppermute | solution.py:249
  20.1 6.3 %collective-permute-start.6 = (bf16[272,1024]{1,0:T(8,128)(2,1)S(1)}, bf16[272,1024]{1,0:T(8,128)(2,1)S(1)}, u32[]{:S(2)}, u32[]{:S(2)}) collective-permute-start(bf16[272,1024]{1,0:T(8,128)(2,1)S(1)} %collective-permute-done.piece_ref.refs_1_.end), channel_id=1, source_target_pairs={{0,1},{1,0},{2,3},{3,2},{4,5},{5,4},{6,7},{7,6},{8,9},{9,8},{10,11... | collective-permute-start | bytes 1671176 | tf_op jit(solution)/shard_map/ppermute | solution.py:249
  20.2 10.4 %collective-permute-start.1 = (bf16[272,1024]{1,0:T(8,128)(2,1)S(1)}, bf16[272,1024]{1,0:T(8,128)(2,1)S(1)}, u32[]{:S(2)}, u32[]{:S(2)}) collective-permute-start(bf16[272,1024]{1,0:T(8,128)(2,1)S(1)} %collective-permute-done.piece_ref.refs_1_.end), channel_id=1, source_target_pairs={{0,1},{1,0},{2,3},{3,2},{4,8},{5,9},{6,10},{7,11},{8,4},{9,5},{10,... | collective-permute-start | bytes 1671176 | tf_op jit(solution)/shard_map/ppermute | solution.py:249
  25.8 3.5 %collective-permute-start.9 = (bf16[144,1024]{1,0:T(8,128)(2,1)S(1)}, bf16[144,1024]{1,0:T(8,128)(2,1)S(1)}, u32[]{:S(2)}, u32[]{:S(2)}) collective-permute-start(bf16[144,1024]{1,0:T(8,128)(2,1)S(1)} %collective-permute-done.4.x_end_b.refs_4_), channel_id=1, source_target_pairs={{0,1},{1,0},{2,3},{3,2},{4,5},{5,4},{6,7},{7,6},{8,9},{9,8},{10,11... | collective-permute-start | bytes 884744 | tf_op jit(solution)/shard_map/ppermute | solution.py:249
  25.8 3.5 %collective-permute-start.8 = (bf16[144,1024]{1,0:T(8,128)(2,1)S(1)}, bf16[144,1024]{1,0:T(8,128)(2,1)S(1)}, u32[]{:S(2)}, u32[]{:S(2)}) collective-permute-start(bf16[144,1024]{1,0:T(8,128)(2,1)S(1)} %collective-permute-done.3.x_end_a.refs_3_), channel_id=1, source_target_pairs={{0,1},{1,0},{2,3},{3,2},{4,5},{5,4},{6,7},{7,6},{8,9},{9,8},{10,11... | collective-permute-start | bytes 884744 | tf_op jit(solution)/shard_map/ppermute | solution.py:249
  32.2 1.2 %collective-permute-start.11 = (f32[4,256]{1,0:T(4,128)S(1)}, f32[4,256]{1,0:T(4,128)S(1)}, u32[]{:S(2)}, u32[]{:S(2)}) collective-permute-start(f32[4,256]{1,0:T(4,128)S(1)} %get-tuple-element.12), channel_id=1, source_target_pairs={{0,1},{1,0},{2,3},{3,2},{4,5},{5,4},{6,7},{7,6},{8,9},{9,8},{10,11... | collective-permute-start | bytes 12296 | tf_op jit(solution)/shard_map/ppermute | solution.py:249
  33.5 1.2 %collective-permute-start.12 = (f32[2,256]{1,0:T(2,128)S(1)}, f32[2,256]{1,0:T(2,128)S(1)}, u32[]{:S(2)}, u32[]{:S(2)}) collective-permute-start(f32[2,256]{1,0:T(2,128)S(1)} %get-tuple-element.14), channel_id=1, source_target_pairs={{0,1},{1,0},{2,3},{3,2},{4,6},{5,7},{6,4},{7,5},{8,10},{9,11},{10,... | collective-permute-start | bytes 6152 | tf_op jit(solution)/shard_map/ppermute | solution.py:249
  34.6 11.0 %collective-permute-start.13 = (f32[1,256]{1,0:T(1,128)S(1)}, f32[1,256]{1,0:T(1,128)S(1)}, u32[]{:S(2)}, u32[]{:S(2)}) collective-permute-start(f32[1,256]{1,0:T(1,128)S(1)} %get-tuple-element.16), channel_id=1, source_target_pairs={{0,4},{1,5},{2,6},{3,7},{4,0},{5,1},{6,2},{7,3},{8,12},{9,13},{10,... | collective-permute-start | bytes 3080 | tf_op jit(solution)/shard_map/ppermute | solution.py:249

commit v16 on v15

--- a/solution.py
+++ b/solution.py
@@ -124,14 +124,17 @@
     return jnp.sum(jnp.where(keep, weights, 0.0), axis=0, keepdims=True)
 
 
-def prepare_kernel(rows_ref, ids_ref, piece_ref):
+def prepare_kernel(rows_ref, ids_ref, *piece_refs):
     doc_count, feature_count = rows_ref.shape
-    ids = jnp.concatenate(
-        [ids_ref[...].astype(jnp.float32), jnp.zeros((1, feature_count - doc_count), jnp.float32)],
-        axis=1,
-    )
-    piece_ref[:doc_count] = unit_rows_of(rows_ref[...])
-    piece_ref[doc_count:] = jnp.broadcast_to(ids, (ID_ROWS, feature_count)).astype(jnp.bfloat16)
+    unit = unit_rows_of(rows_ref[...])
+    ids = ids_ref[...].astype(jnp.float32)
+    for piece_ref, first in zip(piece_refs, (0, 0, doc_count // 2)):
+        count = piece_ref.shape[0] - ID_ROWS
+        some = jnp.concatenate(
+            [ids[:, first : first + count], jnp.zeros((1, feature_count - count), jnp.float32)], axis=1
+        )
+        piece_ref[:count] = unit[first : first + count]
+        piece_ref[count:] = jnp.broadcast_to(some, (ID_ROWS, feature_count)).astype(jnp.bfloat16)
 
 
 def split(piece):
@@ -149,22 +152,18 @@
     ]
 
 
-def counts_kernel(others, same, *refs):
-    *block_refs, out_ref = refs
-    blocks = [split(block) for block in block_refs]
-    wanted = [blocks[k] for k in same] + blocks[others:]
-    totals = count_all(blocks[:others], wanted, {j: k for j, k in enumerate(same)})
-    for j, total in enumerate(totals):
+def first_kernel(own, end, next_own, x_a, x_b, own_o, end_o, x_oa, x_ob, out_ref):
+    others = [split(own), split(end), split(next_own)]
+    wanted = [*others[:2], joined(x_a, x_b), split(own_o), split(end_o), joined(x_oa, x_ob)]
+    for j, total in enumerate(count_all(others, wanted, {0: 0, 1: 1})):
         out_ref[j : j + 1] = total
 
 
-def half_kernel(which, piece_ref, half_ref):
+def half_kernel(piece_ref, half_ref):
     count = piece_ref.shape[0] - ID_ROWS
-    part = count // 2
-    rows = slice(which * part, (which + 1) * part)
-    half_ref[:part] = piece_ref[rows]
-    half_ref[part:] = jnp.zeros_like(half_ref[part:])
-    half_ref[part:, :part] = piece_ref[count:, rows]
+    part = half_ref.shape[0] - ID_ROWS
+    half_ref[:part] = piece_ref[:part]
+    half_ref[part:] = piece_ref[count:]
 
 
 def joined(*pieces):
@@ -180,31 +179,39 @@
 
 
 def last_kernel(far_ref, *refs):
-    own, end, x, x_end_a, x_end_b, own_o, end_o, x_o, x_end_oa, x_end_ob, *refs = refs
-    before_ref, across_ref, here_ref, there_ref = refs
-    wanted = [split(own), split(end), split(x), joined(x_end_a, x_end_b)]
-    wanted += [split(own_o), split(end_o), split(x_o), joined(x_end_oa, x_end_ob)]
+    own, end, x_a, x_b, x_end_a, x_end_b, *refs = refs
+    own_o, end_o, x_oa, x_ob, x_end_oa, x_end_ob, before_ref, across_ref, out_ref = refs
+    wanted = [split(own), split(end), joined(x_a, x_b), joined(x_end_a, x_end_b)]
+    wanted += [split(own_o), split(end_o), joined(x_oa, x_ob), joined(x_end_oa, x_end_ob)]
     for j, total in enumerate(count_all([split(far_ref)], wanted, {})):
-        out_ref, row = (here_ref, j) if j < 4 else (there_ref, j - 4)
-        old = across_ref[j // 4 : j // 4 + 1] if row == 3 else before_ref[j - j // 4 : j - j // 4 + 1]
-        out_ref[row : row + 1] = old + total
-
-
-def cores_kernel(here_ref, back_ref, stay_ref, go_ref):
-    total = here_ref[...] + back_ref[...]
-    stay_ref[...] = total[:2]
-    go_ref[...] = total[2:]
-
-
-def across_kernel(stay_ref, back_ref, own_ref, end_ref):
-    total = stay_ref[...] + back_ref[...]
-    own_ref[...] = total[:1]
-    end_ref[...] = total[1:]
-
-
-def choose_kernel(own_ref, end_ref, out_ref):
+        kind = j % 4
+        old_ref, row = (across_ref, j // 4) if kind == 3 else (before_ref, j - j // 4)
+        out_ref[j : j + 1] = old_ref[row : row + 1] + total
+
+
+def cores_kernel(here_ref, got_ref, stay_ref, go_ref):
+    here, got = here_ref[...], got_ref[...]
+    half = here.shape[0] // 2
+    own, other = here[:half] + got[half:], here[half:] + got[:half]
+    stay_ref[...] = jnp.concatenate([own[:2], other[:2]], axis=0)
+    go_ref[...] = jnp.concatenate([own[2:], other[2:]], axis=0)
+
+
+def across_kernel(stay_ref, got_ref, own_ref, end_ref):
+    total = stay_ref[...] + got_ref[...]
+    own_ref[...] = jnp.concatenate([total[:1], total[2:3]], axis=0)
+    end_ref[...] = jnp.concatenate([total[1:2], total[3:]], axis=0)
+
+
+def along_kernel(own_ref, end_ref, here_ref, there_ref):
     owner = lax.axis_index("owner")
-    out_ref[...] = jnp.where((owner == 1) | (owner == 2), own_ref[...], end_ref[...])
+    total = jnp.where((owner == 1) | (owner == 2), own_ref[...], end_ref[...])
+    here_ref[...] = total[:1]
+    there_ref[...] = total[1:]
+
+
+def choose_kernel(here_ref, there_ref, out_ref):
+    out_ref[...] = jnp.where(lax.axis_index("sub") == 1, here_ref[...], there_ref[...])
 
 
 def select_kernel(capacity, counts_ref, slot_ref, out_ref):
@@ -236,26 +243,24 @@
     doc_count, feature_count = embeddings.shape
     helpers, cores = lax.axis_size("helper"), lax.axis_size("sub")
 
-    def send(x, owners=(0, 1, 2, 3), turns=(0, 0, 0, 0), swaps=(0, 0, 0, 0)):
-        pairs = [
-            (
-                (here * helpers + h) * cores + c,
-                (there * helpers + (h ^ turn)) * cores + (c ^ swap),
-            )
-            for here, (there, turn, swap) in enumerate(zip(owners, turns, swaps))
-            for h in range(helpers)
-            for c in range(cores)
-        ]
+    def send(x, owners=(0, 1, 2, 3), turns=(0, 0, 0, 0), swaps=(0, 0, 0, 0), still=()):
+        pairs = []
+        for here, (there, turn, swap) in enumerate(zip(owners, turns, swaps)):
+            for h in range(helpers):
+                for c in range(cores):
+                    source = (here * helpers + h) * cores + c
+                    target = (there * helpers + (h ^ turn)) * cores + (c ^ swap)
+                    pairs.append((source, source if c in still else target))
         return lax.ppermute(x, ("owner", "helper", "sub"), pairs)
 
-    def along(x):
-        return send(x, owners=(1, 0, 3, 2))
+    def along(x, still=()):
+        return send(x, owners=(1, 0, 3, 2), still=still)
 
     def middle(x):
         return send(x, owners=(0, 2, 1, 3), swaps=(1, 0, 0, 1))
 
-    def across(x):
-        return send(x, turns=(1, 1, 1, 1))
+    def across(x, still=()):
+        return send(x, turns=(1, 1, 1, 1), still=still)
 
     def middle_across(x):
         return send(x, turns=(0, 1, 1, 0), swaps=(1, 0, 0, 1))
@@ -266,59 +271,62 @@
     def sums(count, blocks=1):
         return jax.ShapeDtypeStruct((blocks, count), jnp.float32)
 
-    own = call_kernel(
-        "prepare",
-        prepare_kernel,
-        jax.ShapeDtypeStruct((doc_count + ID_ROWS, feature_count), jnp.bfloat16),
-        embeddings,
-        cluster_id.reshape(1, doc_count),
-    )
-    next_own, end, x, own_o = middle(own), along(own), across(own), other(own)
+    part = doc_count // 2
+    pieces = [
+        jax.ShapeDtypeStruct((count + ID_ROWS, feature_count), jnp.bfloat16)
+        for count in (doc_count, part, part)
+    ]
+    own, own_a, own_b = call_kernel(
+        "prepare", prepare_kernel, pieces, embeddings, cluster_id.reshape(1, doc_count)
+    )
+    end, next_own, own_o = along(own), middle(own), other(own)
+    x = [across(own_a), across(own_b)]
     far = middle(end)
-    half = jax.ShapeDtypeStruct((doc_count // 2 + ID_ROWS, feature_count), jnp.bfloat16)
-    end_half = call_kernel("half", functools.partial(half_kernel, 0), half, end)
-    x_half = call_kernel("half", functools.partial(half_kernel, 1), half, x)
-    x_end = [middle_across(end_half), along(x_half)]
-    end_o, x_o = other(end), other(x)
+    end_a = call_kernel("half", half_kernel, pieces[1], end)
+    x_end = [middle_across(end_a), along(x[1])]
+    end_o, x_o = other(end), [other(piece) for piece in x]
     x_end_o = [other(piece) for piece in x_end]
 
     before = call_kernel(
         "first",
-        functools.partial(counts_kernel, 3, (0, 1)),
+        first_kernel,
         sums(doc_count, 6),
         own,
         end,
         next_own,
-        x,
+        *x,
         own_o,
         end_o,
-        x_o,
+        *x_o,
     )
     before_x = call_kernel(
         "more", more_kernel, sums(doc_count, 2), own, end, next_own, *x_end, *x_end_o,
     )
-    here, there = call_kernel(
+    here = call_kernel(
         "last",
         last_kernel,
-        [sums(doc_count, 4)] * 2,
+        sums(doc_count, 8),
         far,
         own,
         end,
-        x,
+        *x,
         *x_end,
         own_o,
         end_o,
-        x_o,
+        *x_o,
         *x_end_o,
         before,
         before_x,
     )
-    stay, go = call_kernel("cores", cores_kernel, [sums(doc_count, 2)] * 2, here, other(there))
+    stay, go = call_kernel("cores", cores_kernel, [sums(doc_count, 4)] * 2, here, other(here))
     own_sum, end_sum = call_kernel(
-        "across", across_kernel, [sums(doc_count)] * 2, stay, middle_across(go)
+        "across", across_kernel, [sums(doc_count, 2)] * 2, stay, across(go, still=(0,))
+    )
+    here, there = call_kernel(
+        "along", along_kernel, [sums(doc_count)] * 2, own_sum, along(end_sum, still=(0,))
     )
     return call_kernel(
-        "choose", choose_kernel, sums(doc_count), own_sum, along(end_sum), limit=8 * 2**20
+        "choose", choose_kernel, sums(doc_count), here, other(there), limit=8 * 2**20
     )[0]
 
 

time: 46.3 us -> 52.1 us (1.13)
  starting transfers between devices: 18.2 us -> 22.5 us
  waiting for transfers between devices: 19.5 us -> 21 us
    ppermute x14 -> x17, starting transfers between devices: 18.2 us -> 22.5 us  [send(): return lax.ppermute(x, ('owner', 'helper', 'sub'), pairs)]
    ppermute x14 -> x17, waiting for transfers between devices: 19.5 us -> 21 us  [send(): return lax.ppermute(x, ('owner', 'helper', 'sub'), pairs)]
  transfers between devices with their start and end apart: 14 -> 17, of which waited for: 5 -> 5; matrix products, arithmetic and copies ran while one was open for 0% -> 0% of each run, Pallas kernels for 9% -> 8%
where the time goes in v16:
time: 52.1 us; the launch traced here: 51.9 us
  starting transfers between devices  22.5 us (43%)
  waiting for transfers between devices  21 us (40%)
  Pallas kernels  6.64 us (13%)
  local copies, waits for them, and re-layouts  1.72 us (3%)
    ppermute x17, starting transfers between devices, send(): return lax.ppermute(x, ('owner', 'helper', 'sub'), pairs)  22.5 us
    ppermute x17, waiting for transfers between devices, send(): return lax.ppermute(x, ('owner', 'helper', 'sub'), pairs)  21 us
    pallas_call x9, Pallas kernels, call_kernel(): pl.pallas_call(kernel, out_shape=out_shape, in_specs=[VMEM] * len(args),...  6.64 us
    unnamed x4, local copies, waits for them, and re-layouts  1.72 us
  transfers between devices with their start and end apart: 17, of which 5 were waited for; matrix products, arithmetic and copies ran while one was open for 0% of the time, Pallas kernels for 8%

profile of v16, /device:TPU:0, one launch (start us, length us, event | category | flops | bytes accessed | tf_op | source)
XLA Modules:
  0.0 51.9 jit_solution(15206434171543499111)
XLA Ops:
  0.0 0.7 %copy-done.1 = s32[256]{0:T(256)S(1)} copy-done((s32[256]{0:T(256)S(1)}, s32[256]{0:T(256)}, u32[]{:S(2)}) %copy-start.1) | copy-done | bytes 1048
  0.7 1.0 %copy-done = bf16[256,1024]{1,0:T(8,128)(2,1)S(1)} copy-done((bf16[256,1024]{1,0:T(8,128)(2,1)S(1)}, bf16[256,1024]{1,0:T(8,128)(2,1)}, u32[]{:S(2)}) %copy-start) | copy-done | bytes 524312
  1.7 0.2 prepare.1
  1.9 3.1 %collective-permute-start = (bf16[272,1024]{1,0:T(8,128)(2,1)S(1)}, bf16[272,1024]{1,0:T(8,128)(2,1)S(1)}, u32[]{:S(2)}, u32[]{:S(2)}) collective-permute-start(bf16[272,1024]{1,0:T(8,128)(2,1)S(1)} %get-tuple-element.14.own.refs_0_), channel_id=1, source_target_pairs={{0,4},{1,5},{2,6},{3,7},{4,0},{5,1},{6,2},{7,3},{8,12},{9,13},{10,... | collective-permute-start | bytes 1671176 | tf_op jit(solution)/shard_map/ppermute | solution.py:254
  5.0 0.5 collective-permute-start.6
  5.5 1.5 %collective-permute-start.2 = (bf16[144,1024]{1,0:T(8,128)(2,1)S(1)}, bf16[144,1024]{1,0:T(8,128)(2,1)S(1)}, u32[]{:S(2)}, u32[]{:S(2)}) collective-permute-start(bf16[144,1024]{1,0:T(8,128)(2,1)S(1)} %get-tuple-element.15), channel_id=1, source_target_pairs={{0,2},{1,3},{2,0},{3,1},{4,6},{5,7},{6,4},{7,5},{8,10},{9,11},{10,... | collective-permute-start | bytes 884744 | tf_op jit(solution)/shard_map/ppermute | solution.py:254
  7.0 0.5 %collective-permute-start.3 = (bf16[144,1024]{1,0:T(8,128)(2,1)S(1)}, bf16[144,1024]{1,0:T(8,128)(2,1)S(1)}, u32[]{:S(2)}, u32[]{:S(2)}) collective-permute-start(bf16[144,1024]{1,0:T(8,128)(2,1)S(1)} %get-tuple-element.16), channel_id=1, source_target_pairs={{0,2},{1,3},{2,0},{3,1},{4,6},{5,7},{6,4},{7,5},{8,10},{9,11},{10,... | collective-permute-start | bytes 884744 | tf_op jit(solution)/shard_map/ppermute | solution.py:254
  7.5 7.8 %collective-permute-done.2.x_a.refs_2_ = bf16[144,1024]{1,0:T(8,128)(2,1)S(1)} collective-permute-done((bf16[144,1024]{1,0:T(8,128)(2,1)S(1)}, bf16[144,1024]{1,0:T(8,128)(2,1)S(1)}, u32[]{:S(2)}, u32[]{:S(2)}) %collective-permute-start.2) | collective-permute-done | bytes 294944 | tf_op jit(solution)/shard_map/ppermute | solution.py:254
  15.4 0.0 collective-permute-start.8
  15.4 5.4 %collective-permute-done.3.x_b.refs_3_ = bf16[144,1024]{1,0:T(8,128)(2,1)S(1)} collective-permute-done((bf16[144,1024]{1,0:T(8,128)(2,1)S(1)}, bf16[144,1024]{1,0:T(8,128)(2,1)S(1)}, u32[]{:S(2)}, u32[]{:S(2)}) %collective-permute-start.3) | collective-permute-done | bytes 294944 | tf_op jit(solution)/shard_map/ppermute | solution.py:254
  20.8 3.1 %collective-permute-start.5 = (bf16[144,1024]{1,0:T(8,128)(2,1)S(1)}, bf16[144,1024]{1,0:T(8,128)(2,1)S(1)}, u32[]{:S(2)}, u32[]{:S(2)}) collective-permute-start(bf16[144,1024]{1,0:T(8,128)(2,1)S(1)} %collective-permute-done.3.x_b.refs_3_), channel_id=1, source_target_pairs={{0,4},{1,5},{2,6},{3,7},{4,0},{5,1},{6,2},{7,3},{8,12},{9,13},{10,... | collective-permute-start | bytes 884744 | tf_op jit(solution)/shard_map/ppermute | solution.py:254
  23.9 0.1 collective-permute-start.4
  24.0 0.0 collective-permute-done.12.next_own
  24.0 0.5 collective-permute-start.7
  24.5 0.0 collective-permute-done.6.own_o.refs_6_
  24.5 0.1 collective-permute-start.1
  24.6 0.4 collective-permute-start.9
  25.0 5.8 %collective-permute-done.5.x_end_b.refs_5_ = bf16[144,1024]{1,0:T(8,128)(2,1)S(1)} collective-permute-done((bf16[144,1024]{1,0:T(8,128)(2,1)S(1)}, bf16[144,1024]{1,0:T(8,128)(2,1)S(1)}, u32[]{:S(2)}, u32[]{:S(2)}) %collective-permute-start.5) | collective-permute-done | bytes 294944 | tf_op jit(solution)/shard_map/ppermute | solution.py:254
  30.8 0.0 collective-permute-start.11
  30.8 0.0 collective-permute-done.4.x_end_a.refs_4_
  30.8 0.5 collective-permute-start.10
  31.3 0.0 collective-permute-done.9.x_ob.refs_9_
  31.3 3.0 %first.1.refs_12_ = f32[6,256]{1,0:T(8,128)S(1)} custom-call(bf16[272,1024]{1,0:T(8,128)(2,1)S(1)} %get-tuple-element.14.own.refs_0_, bf16[272,1024]{1,0:T(8,128)(2,1)S(1)} %collective-permute-done.piece_ref.end.refs_1_, bf16[272,1024]{1,0:T(8,128)(2,1)S(1)} %collective-permute-done.12.next_own, bf16[144,1024]{1,0:T(8,128)(2,1)S(1)} %collective-permute-done.2.x_a.refs_2_, ...), custom_call_target="tpu_custom_call" | custom-call | tf_op jit(solution)/shard_map/first/pallas_call | solution.py:58
  34.3 1.2 %more.1.refs_13_ = f32[2,256]{1,0:T(2,128)S(1)} custom-call(bf16[272,1024]{1,0:T(8,128)(2,1)S(1)} %get-tuple-element.14.own.refs_0_, bf16[272,1024]{1,0:T(8,128)(2,1)S(1)} %collective-permute-done.piece_ref.end.refs_1_, bf16[272,1024]{1,0:T(8,128)(2,1)S(1)} %collective-permute-done.12.next_own, bf16[144,1024]{1,0:T(8,128)(2,1)S(1)} %collective-permute-done.4.x_end_a.refs_4_, ...), custom_call_target="tpu_custom_call" | custom-call | tf_op jit(solution)/shard_map/more/pallas_call | solution.py:58
  35.6 1.6 %last.1.here_ref = f32[8,256]{1,0:T(8,128)S(1)} custom-call(bf16[272,1024]{1,0:T(8,128)(2,1)S(1)} %collective-permute-done.1.far_ref, bf16[272,1024]{1,0:T(8,128)(2,1)S(1)} %get-tuple-element.14.own.refs_0_, bf16[272,1024]{1,0:T(8,128)(2,1)S(1)} %collective-permute-done.piece_ref.end.refs_1_, bf16[144,1024]{1,0:T(8,128)(2,1)S(1)} %collective-permute-done.2.x_a.refs_2_, ...), custom_call_target="tpu_custom_call" | custom-call | tf_op jit(solution)/shard_map/last/pallas_call | solution.py:58
  37.2 0.1 collective-permute-start.13
  37.3 1.2 %collective-permute-done.13.got_ref = f32[8,256]{1,0:T(8,128)S(1)} collective-permute-done((f32[8,256]{1,0:T(8,128)S(1)}, f32[8,256]{1,0:T(8,128)S(1)}, u32[]{:S(2)}, u32[]{:S(2)}) %collective-permute-start.13) | collective-permute-done | bytes 8224 | tf_op jit(solution)/shard_map/ppermute | solution.py:254
  38.4 0.7 %collective-permute-start.14 = (f32[4,256]{1,0:T(4,128)S(1)}, f32[4,256]{1,0:T(4,128)S(1)}, u32[]{:S(2)}, u32[]{:S(2)}) collective-permute-start(f32[4,256]{1,0:T(4,128)S(1)} %get-tuple-element.18), channel_id=1, source_target_pairs={{0,0},{1,3},{2,2},{3,1},{4,4},{5,7},{6,6},{7,5},{8,8},{9,11},{10,1... | collective-permute-start | bytes 12296 | tf_op jit(solution)/shard_map/ppermute | solution.py:254
  39.1 0.7 %collective-permute-start.15 = (f32[2,256]{1,0:T(2,128)S(1)}, f32[2,256]{1,0:T(2,128)S(1)}, u32[]{:S(2)}, u32[]{:S(2)}) collective-permute-start(f32[2,256]{1,0:T(2,128)S(1)} %get-tuple-element.20), channel_id=1, source_target_pairs={{0,0},{1,5},{2,2},{3,7},{4,4},{5,1},{6,6},{7,3},{8,8},{9,13},{10,1... | collective-permute-start | bytes 6152 | tf_op jit(solution)/shard_map/ppermute | solution.py:254
  39.8 10.7 %collective-permute-start.16 = (f32[1,256]{1,0:T(1,128)S(1)}, f32[1,256]{1,0:T(1,128)S(1)}, u32[]{:S(2)}, u32[]{:S(2)}) collective-permute-start(f32[1,256]{1,0:T(1,128)S(1)} %get-tuple-element.22), channel_id=1, source_target_pairs={{0,1},{1,0},{2,3},{3,2},{4,5},{5,4},{6,7},{7,6},{8,9},{9,8},{10,11... | collective-permute-start | bytes 3080 | tf_op jit(solution)/shard_map/ppermute | solution.py:254
  50.5 0.8 %collective-permute-done.16.there_ref = f32[1,256]{1,0:T(1,128)S(1)} collective-permute-done((f32[1,256]{1,0:T(1,128)S(1)}, f32[1,256]{1,0:T(1,128)S(1)}, u32[]{:S(2)}, u32[]{:S(2)}) %collective-permute-start.16) | collective-permute-done | bytes 1056 | tf_op jit(solution)/shard_map/ppermute | solution.py:254
  51.4 0.6 %choose.1 = f32[1,256]{1,0:T(1,128)} custom-call(f32[1,256]{1,0:T(1,128)S(1)} %get-tuple-element.21.here_ref, f32[1,256]{1,0:T(1,128)S(1)} %collective-permute-done.16.there_ref), custom_call_target="tpu_custom_call" | custom-call | tf_op jit(solution)/shard_map/choose/pallas_call | solution.py:58
  (15 shorter events, 0.1 us)
Async XLA Ops:
  0.0 0.7 %copy-start.1 = (s32[256]{0:T(256)S(1)}, s32[256]{0:T(256)}, u32[]{:S(2)}) copy-start(s32[256]{0:T(256)} %param.3) | copy-start | bytes 3076
  0.7 1.0 %copy-start = (bf16[256,1024]{1,0:T(8,128)(2,1)S(1)}, bf16[256,1024]{1,0:T(8,128)(2,1)}, u32[]{:S(2)}) copy-start(bf16[256,1024]{1,0:T(8,128)(2,1)} %rows_ref.1) | copy-start | bytes 1572868
  1.9 22.0 %collective-permute-start = (bf16[272,1024]{1,0:T(8,128)(2,1)S(1)}, bf16[272,1024]{1,0:T(8,128)(2,1)S(1)}, u32[]{:S(2)}, u32[]{:S(2)}) collective-permute-start(bf16[272,1024]{1,0:T(8,128)(2,1)S(1)} %get-tuple-element.14.own.refs_0_), channel_id=1, source_target_pairs={{0,4},{1,5},{2,6},{3,7},{4,0},{5,1},{6,2},{7,3},{8,12},{9,13},{10,... | collective-permute-start | bytes 1671176 | tf_op jit(solution)/shard_map/ppermute | solution.py:254
  5.0 19.0 %collective-permute-start.12 = (bf16[272,1024]{1,0:T(8,128)(2,1)S(1)}, bf16[272,1024]{1,0:T(8,128)(2,1)S(1)}, u32[]{:S(2)}, u32[]{:S(2)}) collective-permute-start(bf16[272,1024]{1,0:T(8,128)(2,1)S(1)} %get-tuple-element.14.own.refs_0_), channel_id=1, source_target_pairs={{0,1},{1,0},{2,3},{3,2},{4,8},{5,9},{6,10},{7,11},{8,4},{9,5},{10,... | collective-permute-start | bytes 1671176 | tf_op jit(solution)/shard_map/ppermute | solution.py:254
  5.0 19.5 %collective-permute-start.6 = (bf16[272,1024]{1,0:T(8,128)(2,1)S(1)}, bf16[272,1024]{1,0:T(8,128)(2,1)S(1)}, u32[]{:S(2)}, u32[]{:S(2)}) collective-permute-start(bf16[272,1024]{1,0:T(8,128)(2,1)S(1)} %get-tuple-element.14.own.refs_0_), channel_id=1, source_target_pairs={{0,1},{1,0},{2,3},{3,2},{4,5},{5,4},{6,7},{7,6},{8,9},{9,8},{10,11... | collective-permute-start | bytes 1671176 | tf_op jit(solution)/shard_map/ppermute | solution.py:254
  5.5 9.9 %collective-permute-start.2 = (bf16[144,1024]{1,0:T(8,128)(2,1)S(1)}, bf16[144,1024]{1,0:T(8,128)(2,1)S(1)}, u32[]{:S(2)}, u32[]{:S(2)}) collective-permute-start(bf16[144,1024]{1,0:T(8,128)(2,1)S(1)} %get-tuple-element.15), channel_id=1, source_target_pairs={{0,2},{1,3},{2,0},{3,1},{4,6},{5,7},{6,4},{7,5},{8,10},{9,11},{10,... | collective-permute-start | bytes 884744 | tf_op jit(solution)/shard_map/ppermute | solution.py:254
  7.0 13.7 %collective-permute-start.3 = (bf16[144,1024]{1,0:T(8,128)(2,1)S(1)}, bf16[144,1024]{1,0:T(8,128)(2,1)S(1)}, u32[]{:S(2)}, u32[]{:S(2)}) collective-permute-start(bf16[144,1024]{1,0:T(8,128)(2,1)S(1)} %get-tuple-element.16), channel_id=1, source_target_pairs={{0,2},{1,3},{2,0},{3,1},{4,6},{5,7},{6,4},{7,5},{8,10},{9,11},{10,... | collective-permute-start | bytes 884744 | tf_op jit(solution)/shard_map/ppermute | solution.py:254
  15.4 9.2 %collective-permute-start.8 = (bf16[144,1024]{1,0:T(8,128)(2,1)S(1)}, bf16[144,1024]{1,0:T(8,128)(2,1)S(1)}, u32[]{:S(2)}, u32[]{:S(2)}) collective-permute-start(bf16[144,1024]{1,0:T(8,128)(2,1)S(1)} %collective-permute-done.2.x_a.refs_2_), channel_id=1, source_target_pairs={{0,1},{1,0},{2,3},{3,2},{4,5},{5,4},{6,7},{7,6},{8,9},{9,8},{10,11... | collective-permute-start | bytes 884744 | tf_op jit(solution)/shard_map/ppermute | solution.py:254
  20.8 10.0 %collective-permute-start.5 = (bf16[144,1024]{1,0:T(8,128)(2,1)S(1)}, bf16[144,1024]{1,0:T(8,128)(2,1)S(1)}, u32[]{:S(2)}, u32[]{:S(2)}) collective-permute-start(bf16[144,1024]{1,0:T(8,128)(2,1)S(1)} %collective-permute-done.3.x_b.refs_3_), channel_id=1, source_target_pairs={{0,4},{1,5},{2,6},{3,7},{4,0},{5,1},{6,2},{7,3},{8,12},{9,13},{10,... | collective-permute-start | bytes 884744 | tf_op jit(solution)/shard_map/ppermute | solution.py:254
  23.9 6.9 %collective-permute-start.4 = (bf16[144,1024]{1,0:T(8,128)(2,1)S(1)}, bf16[144,1024]{1,0:T(8,128)(2,1)S(1)}, u32[]{:S(2)}, u32[]{:S(2)}) collective-permute-start(bf16[144,1024]{1,0:T(8,128)(2,1)S(1)} %half.1), channel_id=1, source_target_pairs={{0,1},{1,0},{2,3},{3,2},{4,6},{5,7},{6,4},{7,5},{8,10},{9,11},{10,... | collective-permute-start | bytes 884744 | tf_op jit(solution)/shard_map/ppermute | solution.py:254
  24.0 7.3 %collective-permute-start.7 = (bf16[272,1024]{1,0:T(8,128)(2,1)S(1)}, bf16[272,1024]{1,0:T(8,128)(2,1)S(1)}, u32[]{:S(2)}, u32[]{:S(2)}) collective-permute-start(bf16[272,1024]{1,0:T(8,128)(2,1)S(1)} %collective-permute-done.piece_ref.end.refs_1_), channel_id=1, source_target_pairs={{0,1},{1,0},{2,3},{3,2},{4,5},{5,4},{6,7},{7,6},{8,9},{9,8},{10,11... | collective-permute-start | bytes 1671176 | tf_op jit(solution)/shard_map/ppermute | solution.py:254
  24.5 11.0 %collective-permute-start.1 = (bf16[272,1024]{1,0:T(8,128)(2,1)S(1)}, bf16[272,1024]{1,0:T(8,128)(2,1)S(1)}, u32[]{:S(2)}, u32[]{:S(2)}) collective-permute-start(bf16[272,1024]{1,0:T(8,128)(2,1)S(1)} %collective-permute-done.piece_ref.end.refs_1_), channel_id=1, source_target_pairs={{0,1},{1,0},{2,3},{3,2},{4,8},{5,9},{6,10},{7,11},{8,4},{9,5},{10,... | collective-permute-start | bytes 1671176 | tf_op jit(solution)/shard_map/ppermute | solution.py:254
  24.6 6.7 %collective-permute-start.9 = (bf16[144,1024]{1,0:T(8,128)(2,1)S(1)}, bf16[144,1024]{1,0:T(8,128)(2,1)S(1)}, u32[]{:S(2)}, u32[]{:S(2)}) collective-permute-start(bf16[144,1024]{1,0:T(8,128)(2,1)S(1)} %collective-permute-done.3.x_b.refs_3_), channel_id=1, source_target_pairs={{0,1},{1,0},{2,3},{3,2},{4,5},{5,4},{6,7},{7,6},{8,9},{9,8},{10,11... | collective-permute-start | bytes 884744 | tf_op jit(solution)/shard_map/ppermute | solution.py:254
  30.8 3.5 %collective-permute-start.11 = (bf16[144,1024]{1,0:T(8,128)(2,1)S(1)}, bf16[144,1024]{1,0:T(8,128)(2,1)S(1)}, u32[]{:S(2)}, u32[]{:S(2)}) collective-permute-start(bf16[144,1024]{1,0:T(8,128)(2,1)S(1)} %collective-permute-done.5.x_end_b.refs_5_), channel_id=1, source_target_pairs={{0,1},{1,0},{2,3},{3,2},{4,5},{5,4},{6,7},{7,6},{8,9},{9,8},{10,11... | collective-permute-start | bytes 884744 | tf_op jit(solution)/shard_map/ppermute | solution.py:254
  30.8 3.5 %collective-permute-start.10 = (bf16[144,1024]{1,0:T(8,128)(2,1)S(1)}, bf16[144,1024]{1,0:T(8,128)(2,1)S(1)}, u32[]{:S(2)}, u32[]{:S(2)}) collective-permute-start(bf16[144,1024]{1,0:T(8,128)(2,1)S(1)} %collective-permute-done.4.x_end_a.refs_4_), channel_id=1, source_target_pairs={{0,1},{1,0},{2,3},{3,2},{4,5},{5,4},{6,7},{7,6},{8,9},{9,8},{10,11... | collective-permute-start | bytes 884744 | tf_op jit(solution)/shard_map/ppermute | solution.py:254
  37.2 1.2 %collective-permute-start.13 = (f32[8,256]{1,0:T(8,128)S(1)}, f32[8,256]{1,0:T(8,128)S(1)}, u32[]{:S(2)}, u32[]{:S(2)}) collective-permute-start(f32[8,256]{1,0:T(8,128)S(1)} %last.1.here_ref), channel_id=1, source_target_pairs={{0,1},{1,0},{2,3},{3,2},{4,5},{5,4},{6,7},{7,6},{8,9},{9,8},{10,11... | collective-permute-start | bytes 24584 | tf_op jit(solution)/shard_map/ppermute | solution.py:254
  38.4 0.7 %collective-permute-start.14 = (f32[4,256]{1,0:T(4,128)S(1)}, f32[4,256]{1,0:T(4,128)S(1)}, u32[]{:S(2)}, u32[]{:S(2)}) collective-permute-start(f32[4,256]{1,0:T(4,128)S(1)} %get-tuple-element.18), channel_id=1, source_target_pairs={{0,0},{1,3},{2,2},{3,1},{4,4},{5,7},{6,6},{7,5},{8,8},{9,11},{10,1... | collective-permute-start | bytes 12296 | tf_op jit(solution)/shard_map/ppermute | solution.py:254
  39.1 0.7 %collective-permute-start.15 = (f32[2,256]{1,0:T(2,128)S(1)}, f32[2,256]{1,0:T(2,128)S(1)}, u32[]{:S(2)}, u32[]{:S(2)}) collective-permute-start(f32[2,256]{1,0:T(2,128)S(1)} %get-tuple-element.20), channel_id=1, source_target_pairs={{0,0},{1,5},{2,2},{3,7},{4,4},{5,1},{6,6},{7,3},{8,8},{9,13},{10,1... | collective-permute-start | bytes 6152 | tf_op jit(solution)/shard_map/ppermute | solution.py:254
  39.8 11.5 %collective-permute-start.16 = (f32[1,256]{1,0:T(1,128)S(1)}, f32[1,256]{1,0:T(1,128)S(1)}, u32[]{:S(2)}, u32[]{:S(2)}) collective-permute-start(f32[1,256]{1,0:T(1,128)S(1)} %get-tuple-element.22), channel_id=1, source_target_pairs={{0,1},{1,0},{2,3},{3,2},{4,5},{5,4},{6,7},{7,6},{8,9},{9,8},{10,11... | collective-permute-start | bytes 3080 | tf_op jit(solution)/shard_map/ppermute | solution.py:254

commit v17 on v7

--- a/solution.py
+++ b/solution.py
@@ -106,54 +106,72 @@
     out_ref[rows:] = second_ref[...]
 
 
-def blocks(rows, starts, size):
-    return jnp.concatenate([rows[start : start + size] for start in starts], axis=0)
-
-
-def count_against(rows, own, starts, size):
-    column = lax.broadcasted_iota(jnp.int32, (1, own.shape[0]), 1)
-    itself = jnp.full_like(column, -1)
-    for k, start in enumerate(starts):
-        itself = jnp.where(column // size == k, column + (start - k * size), itself)
+def count_against(pieces, own, size, starts=()):
     slope = -math.log2(math.e) / sharpness
     total = jnp.zeros((1, own.shape[0]), jnp.float32)
-    for first in range(0, rows.shape[0], TILE):
-        other = rows[first : first + TILE]
-        scores = lax.dot_general(
-            other, own, (((1,), (1,)), ((), ())), preferred_element_type=jnp.float32
-        )
-        weights = 1.0 / (1.0 + jnp.exp2(scores * slope - threshold * slope))
-        keep = other[:, :1].astype(jnp.float32) < 0.5 * EMPTY
-        if starts:
-            keep = keep & (lax.broadcasted_iota(jnp.int32, scores.shape, 0) + first != itself)
-        total = total + jnp.sum(jnp.where(keep, weights, 0.0), axis=0, keepdims=True)
+    first = 0
+    for piece in pieces:
+        for row in range(0, piece.shape[0], TILE):
+            other = piece[row : row + TILE]
+            count = other.shape[0]
+            scores = lax.dot_general(
+                other, own, (((1,), (1,)), ((), ())), preferred_element_type=jnp.float32
+            )
+            odds = 1.0 + jnp.minimum(jnp.exp2(scores * slope - threshold * slope), 1e30)
+            weights = pl.reciprocal(odds, approx=True)
+            weights = weights * (2.0 - odds * weights)
+            weights = jnp.where(other[:, :1].astype(jnp.float32) < 0.5 * EMPTY, weights, 0.0)
+            for k, start in enumerate(starts):
+                if start + size > first and start < first + count:
+                    itself = lax.broadcasted_iota(jnp.int32, weights.shape, 1) + (
+                        start - k * size - first
+                    )
+                    inside = lax.broadcasted_iota(jnp.int32, weights.shape, 1) // size == k
+                    same = lax.broadcasted_iota(jnp.int32, weights.shape, 0) == itself
+                    weights = jnp.where(inside & same, 0.0, weights)
+            total = total + jnp.sum(weights, axis=0, keepdims=True)
+            first += count
     return total
 
 
 def count_kernel(starts, size, *refs):
-    *piece_refs, count_ref = refs
-    rows = jnp.concatenate([piece[...] for piece in piece_refs], axis=0)
-    count_ref[...] = count_against(rows, blocks(rows, starts, size), starts, size)
+    *piece_refs, own_ref, count_ref = refs
+    rows, first = [], 0
+    for piece in piece_refs:
+        for start in starts:
+            if first <= start < first + piece.shape[0]:
+                rows.append(piece[start - first : start - first + size])
+        first += piece.shape[0]
+    own = jnp.concatenate(rows, axis=0)
+    own_ref[...] = own
+    count_ref[...] = count_against(piece_refs, own, size, starts)
 
 
 def soft_counts(pieces, starts, size):
-    out_shape = jax.ShapeDtypeStruct((1, len(starts) * size), jnp.float32)
-    return call_kernel("count", functools.partial(count_kernel, starts, size), out_shape, *pieces)
-
-
-def finish_kernel(starts, late_pieces, late_starts, places, *refs):
-    *piece_refs, early_ref, count_ref = refs
-    size = count_ref.shape[2]
-    early = jnp.concatenate([piece[...] for piece in piece_refs[:-late_pieces]], axis=0)
-    late = jnp.concatenate([piece[...] for piece in piece_refs[-late_pieces:]], axis=0)
-    own = blocks(early, starts, size)
-    late_own = blocks(late, late_starts, size)
-    total = early_ref[...] + count_against(late, own, [], size)
-    late_total = count_against(early, late_own, [], size) + count_against(
-        late, late_own, late_starts, size
-    )
+    count = len(starts) * size
+    return call_kernel(
+        "count",
+        functools.partial(count_kernel, starts, size),
+        [
+            jax.ShapeDtypeStruct((count, pieces[0].shape[1]), jnp.bfloat16),
+            jax.ShapeDtypeStruct((1, count), jnp.float32),
+        ],
+        *pieces,
+    )
+
+
+def finish_kernel(size, places, *refs):
+    *early_refs, here_ref, there_ref, own_ref, early_ref, count_ref = refs
+    late_refs = [here_ref, there_ref]
+    late_own = jnp.concatenate([here_ref[:size], there_ref[size:]], axis=0)
+    starts = [0, here_ref.shape[0] + size]
+    total = early_ref[...] + count_against(late_refs, own_ref[...], size)
+    late_total = count_against(early_refs, late_own, size) + count_against(
+        late_refs, late_own, size, starts
+    )
+    early_blocks = own_ref.shape[0] // size
     for k, place in enumerate(places()):
-        source, j = (total, k) if k < len(starts) else (late_total, k - len(starts))
+        source, j = (total, k) if k < early_blocks else (late_total, k - early_blocks)
         count_ref[pl.ds(place, 1), 0, :] = source[:, j * size : (j + 1) * size]
 
 
@@ -232,7 +250,6 @@
     half_way = span * (steps - 1)
     starts = [k * span for k in range(steps - 1)]
     starts += [half_way + start + capacity for start in starts]
-    late_starts = [0, span + capacity]
 
     def places():
         chip, core = chip_index(), lax.axis_index("sub")
@@ -244,11 +261,11 @@
 
     counts = call_kernel(
         "finish",
-        functools.partial(finish_kernel, starts, len(late), late_starts, places),
+        functools.partial(finish_kernel, capacity, places),
         jax.ShapeDtypeStruct((clusters, 1, capacity), jnp.float32),
         *early,
         *late,
-        soft_counts(early, starts, capacity),
+        *soft_counts(early, starts, capacity),
     )
     back = lax.all_to_all(counts, ("owner", "helper"), split_axis=0, concat_axis=0, tiled=True)
     return select(back, slot, capacity)
@@ -283,7 +300,7 @@
     for step in range(CL_OWN, helpers, CL_OWN):
         turn = [(i, (i + step) % helpers) for i in range(helpers)]
         others += [lax.ppermute(x, "helper", turn) for x in (own, others[0])]
-    counts = soft_counts([own, *others], [0], own.shape[0])
+    _, counts = soft_counts([own, *others], [0], own.shape[0])
     counts = counts.reshape(CL_OWN, owners, capacity)
     kept, given = counts[0], partner(counts[1])
     counts = jnp.where(mine == 0, jnp.stack([kept, given], 1), jnp.stack([given, kept], 1))

time: 44.8 us -> 45.5 us (1.016)
  Pallas kernels: 4.21 us -> 4.91 us
    pallas_call x6, Pallas kernels: 4.21 us -> 4.91 us  [call_kernel(): pl.pallas_call(kernel, out_shape=out_shape, in_specs=[VMEM] * len(args),...]
  transfers between devices with their start and end apart: 11 -> 11, of which waited for: 3 -> 3; matrix products, arithmetic and copies ran while one was open for 0% -> 0% of each run, Pallas kernels for 5% -> 6%
where the time goes in v17:
time: 45.5 us; the launch traced here: 45.3 us
  starting transfers between devices  19.4 us (43%)
  blocking collectives  12.3 us (27%)
  waiting for transfers between devices  7.35 us (16%)
  Pallas kernels  4.91 us (11%)
  local copies, waits for them, and re-layouts  1.27 us (3%)
    all_to_all x1, blocking collectives, body_by_chip(): lax.all_to_all(counts, ('owner', 'helper'), split_axis=0, concat_axis=0,...  12.3 us
    ppermute x6, starting transfers between devices, swap_cores(): return lax.ppermute(x, 'sub', [(i, i ^ 1) for i in range(cores)])  10.5 us
    ppermute x5, starting transfers between devices, across(): return lax.ppermute(x, ('owner', 'helper', 'sub'), pairs)  8.83 us
    ppermute x5, waiting for transfers between devices, across(): return lax.ppermute(x, ('owner', 'helper', 'sub'), pairs)  6.19 us
    pallas_call x6, Pallas kernels, call_kernel(): pl.pallas_call(kernel, out_shape=out_shape, in_specs=[VMEM] * len(args),...  4.91 us
    unnamed x4, local copies, waits for them, and re-layouts  1.27 us
    ppermute x6, waiting for transfers between devices, swap_cores(): return lax.ppermute(x, 'sub', [(i, i ^ 1) for i in range(cores)])  1.15 us
  transfers between devices with their start and end apart: 11, of which 3 were waited for; matrix products, arithmetic and copies ran while one was open for 0% of the time, Pallas kernels for 6%

profile of v17, /device:TPU:0, one launch (start us, length us, event | category | flops | bytes accessed | tf_op | source)
XLA Modules:
  0.0 45.3 jit_solution(12493701460145316997)
XLA Ops:
  0.0 0.0 copy-start.1
  0.0 0.5 collective-permute-start.1
  0.5 0.2 copy-done.1
  0.7 0.5 collective-permute-start.2
  1.1 0.0 copy-start
  1.1 1.0 %copy-done = bf16[256,1024]{1,0:T(8,128)(2,1)S(1)} copy-done((bf16[256,1024]{1,0:T(8,128)(2,1)S(1)}, bf16[256,1024]{1,0:T(8,128)(2,1)}, u32[]{:S(2)}) %copy-start) | copy-done | bytes 524312
  2.2 0.5 %route_first.1 = (bf16[64,1024]{1,0:T(8,128)(2,1)S(1)}, s32[1,256]{1,0:T(1,128)S(1)}) custom-call(bf16[256,1024]{1,0:T(8,128)(2,1)S(1)} %copy-done, s32[1,256]{1,0:T(1,128)S(1)} %bitcast.3), custom_call_target="tpu_custom_call" | custom-call | tf_op jit(solution)/shard_map/route_first/pallas_call | solution.py:92
  2.6 3.7 %collective-permute-start = (bf16[64,1024]{1,0:T(8,128)(2,1)S(1)}, bf16[64,1024]{1,0:T(8,128)(2,1)S(1)}, u32[]{:S(2)}, u32[]{:S(2)}) collective-permute-start(bf16[64,1024]{1,0:T(8,128)(2,1)S(1)} %get-tuple-element.13), channel_id=1, source_target_pairs={{0,8},{1,11},{2,10},{3,9},{4,12},{5,15},{6,14},{7,13},{8,0},{9,3},... | collective-permute-start | bytes 393224 | tf_op jit(solution)/shard_map/ppermute | solution.py:216
  6.3 0.0 collective-permute-done.2.refs_3_
  6.3 0.0 collective-permute-done.1.refs_1_
  6.3 0.7 %route_rest.1 = (bf16[64,1024]{1,0:T(8,128)(2,1)S(1)}, bf16[128,1024]{1,0:T(8,128)(2,1)S(1)}, bf16[128,1024]{1,0:T(8,128)(2,1)S(1)}, bf16[128,1024]{1,0:T(8,128)(2,1)S(1)}) custom-call(bf16[256,1024]{1,0:T(8,128)(2,1)S(1)} %copy-done, bf16[256,1024]{1,0:T(8,128)(2,1)S(1)} %collective-permute-done.1.refs_1_, s32[1,256]{1,0:T(1,128)S(1)} %get-tuple-element.14.refs_2_.slot_ref, ...), custom_call_target="tpu_custom_call" | custom-call | tf_op jit(solution)/shard_map/route_rest/pallas_call | solution.py:92
  7.0 0.1 collective-permute-start.3
  7.1 0.7 %collective-permute-start.4 = (bf16[128,1024]{1,0:T(8,128)(2,1)S(1)}, bf16[128,1024]{1,0:T(8,128)(2,1)S(1)}, u32[]{:S(2)}, u32[]{:S(2)}) collective-permute-start(bf16[128,1024]{1,0:T(8,128)(2,1)S(1)} %get-tuple-element.16), channel_id=1, source_target_pairs={{0,0},{1,3},{2,2},{3,1},{4,4},{5,7},{6,6},{7,5},{8,8},{9,11},{10,1... | collective-permute-start | bytes 786440 | tf_op jit(solution)/shard_map/ppermute | solution.py:216
  7.8 1.9 %collective-permute-start.5 = (bf16[128,1024]{1,0:T(8,128)(2,1)S(1)}, bf16[128,1024]{1,0:T(8,128)(2,1)S(1)}, u32[]{:S(2)}, u32[]{:S(2)}) collective-permute-start(bf16[128,1024]{1,0:T(8,128)(2,1)S(1)} %get-tuple-element.17), channel_id=1, source_target_pairs={{0,4},{1,7},{2,6},{3,5},{4,0},{5,3},{6,2},{7,1},{8,12},{9,15},{10,... | collective-permute-start | bytes 786440 | tf_op jit(solution)/shard_map/ppermute | solution.py:216
  9.8 2.5 %collective-permute-start.9 = (bf16[128,1024]{1,0:T(8,128)(2,1)S(1)}, bf16[128,1024]{1,0:T(8,128)(2,1)S(1)}, u32[]{:S(2)}, u32[]{:S(2)}) collective-permute-start(bf16[128,1024]{1,0:T(8,128)(2,1)S(1)} %get-tuple-element.18), channel_id=1, source_target_pairs={{0,12},{1,15},{2,14},{3,13},{4,8},{5,11},{6,10},{7,9},{8,4},{9,7},... | collective-permute-start | bytes 786440 | tf_op jit(solution)/shard_map/ppermute | solution.py:216
  12.2 3.2 %collective-permute-done.first_ref = bf16[64,1024]{1,0:T(8,128)(2,1)S(1)} collective-permute-done((bf16[64,1024]{1,0:T(8,128)(2,1)S(1)}, bf16[64,1024]{1,0:T(8,128)(2,1)S(1)}, u32[]{:S(2)}, u32[]{:S(2)}) %collective-permute-start) | collective-permute-done | bytes 131104 | tf_op jit(solution)/shard_map/ppermute | solution.py:216
  15.4 3.0 %collective-permute-done.3.second_ref = bf16[64,1024]{1,0:T(8,128)(2,1)S(1)} collective-permute-done((bf16[64,1024]{1,0:T(8,128)(2,1)S(1)}, bf16[64,1024]{1,0:T(8,128)(2,1)S(1)}, u32[]{:S(2)}, u32[]{:S(2)}) %collective-permute-start.3) | collective-permute-done | bytes 131104 | tf_op jit(solution)/shard_map/ppermute | solution.py:216
  18.4 0.9 %collective-permute-start.6 = (bf16[128,1024]{1,0:T(8,128)(2,1)S(1)}, bf16[128,1024]{1,0:T(8,128)(2,1)S(1)}, u32[]{:S(2)}, u32[]{:S(2)}) collective-permute-start(bf16[128,1024]{1,0:T(8,128)(2,1)S(1)} %join.1.refs_0_), channel_id=1, source_target_pairs={{0,1},{1,0},{2,3},{3,2},{4,5},{5,4},{6,7},{7,6},{8,9},{9,8},{10,11... | collective-permute-start | bytes 786440 | tf_op jit(solution)/shard_map/ppermute | solution.py:200
  19.4 0.0 collective-permute-done.4.refs_1_
  19.4 0.1 collective-permute-start.7
  19.5 0.0 collective-permute-done.5.refs_2_
  19.5 8.6 %collective-permute-start.8 = (bf16[128,1024]{1,0:T(8,128)(2,1)S(1)}, bf16[128,1024]{1,0:T(8,128)(2,1)S(1)}, u32[]{:S(2)}, u32[]{:S(2)}) collective-permute-start(bf16[128,1024]{1,0:T(8,128)(2,1)S(1)} %collective-permute-done.5.refs_2_), channel_id=1, source_target_pairs={{0,1},{1,0},{2,3},{3,2},{4,5},{5,4},{6,7},{7,6},{8,9},{9,8},{10,11... | collective-permute-start | bytes 786440 | tf_op jit(solution)/shard_map/ppermute | solution.py:200
  28.1 0.0 collective-permute-done.9.refs_6_
  28.1 0.0 collective-permute-start.10
  28.1 0.0 collective-permute-done.6.refs_3_
  28.1 0.0 collective-permute-done.7.refs_4_
  28.1 1.1 %collective-permute-done.8.refs_5_ = bf16[128,1024]{1,0:T(8,128)(2,1)S(1)} collective-permute-done((bf16[128,1024]{1,0:T(8,128)(2,1)S(1)}, bf16[128,1024]{1,0:T(8,128)(2,1)S(1)}, u32[]{:S(2)}, u32[]{:S(2)}) %collective-permute-start.8) | collective-permute-done | bytes 262176 | tf_op jit(solution)/shard_map/ppermute | solution.py:200
  29.2 1.6 %count.1 = (bf16[384,1024]{1,0:T(8,128)(2,1)S(1)}, f32[1,384]{1,0:T(1,128)S(1)}) custom-call(bf16[128,1024]{1,0:T(8,128)(2,1)S(1)} %join.1.refs_0_, bf16[128,1024]{1,0:T(8,128)(2,1)S(1)} %collective-permute-done.4.refs_1_, bf16[128,1024]{1,0:T(8,128)(2,1)S(1)} %collective-permute-done.5.refs_2_, bf16[128,1024]{1,0:T(8,128)(2,1)S(1)} %collective-permute-done.6.refs_3_, ...), custom_call_target="tpu_custom_call" | custom-call | tf_op jit(solution)/shard_map/count/pallas_call | solution.py:92
  30.9 0.0 collective-permute-done.10.refs_7_
  30.9 1.3 %finish.1 = f32[8,1,64]{2,1,0:T(1,128)S(1)} custom-call(bf16[128,1024]{1,0:T(8,128)(2,1)S(1)} %join.1.refs_0_, bf16[128,1024]{1,0:T(8,128)(2,1)S(1)} %collective-permute-done.4.refs_1_, bf16[128,1024]{1,0:T(8,128)(2,1)S(1)} %collective-permute-done.5.refs_2_, bf16[128,1024]{1,0:T(8,128)(2,1)S(1)} %collective-permute-done.6.refs_3_, ...), custom_call_target="tpu_custom_call" | custom-call | tf_op jit(solution)/shard_map/finish/pallas_call | solution.py:92
  32.2 12.3 %all_to_all.5.counts_ref = f32[8,1,64]{2,1,0:T(1,128)S(1)} all-to-all(f32[8,1,64]{2,1,0:T(1,128)S(1)} %finish.1), channel_id=1, replica_groups=mesh['groups'=2,'owner'=4,'helper'=2,'sub'=2] {'owner','helper'}, dimensions={0} | all-to-all | bytes 4096 | tf_op jit(solution)/shard_map/all_to_all | solution.py:270
  44.5 0.7 %select.1 = f32[1,256]{1,0:T(1,128)} custom-call(f32[8,1,64]{2,1,0:T(1,128)S(1)} %all_to_all.5.counts_ref, s32[1,256]{1,0:T(1,128)S(1)} %get-tuple-element.14.refs_2_.slot_ref), custom_call_target="tpu_custom_call" | custom-call | tf_op jit(solution)/shard_map/select/pallas_call | solution.py:92
  (1 shorter events, 0.0 us)
Async XLA Ops:
  0.0 0.7 %copy-start.1 = (s32[256]{0:T(256)S(1)}, s32[256]{0:T(256)}, u32[]{:S(2)}) copy-start(s32[256]{0:T(256)} %param.3) | copy-start | bytes 3076
  0.0 6.3 %collective-permute-start.1 = (bf16[256,1024]{1,0:T(8,128)(2,1)}, bf16[256,1024]{1,0:T(8,128)(2,1)S(1)}, u32[]{:S(2)}, u32[]{:S(2)}) collective-permute-start(bf16[256,1024]{1,0:T(8,128)(2,1)} %refs_0_.1), channel_id=1, source_target_pairs={{0,1},{1,0},{2,3},{3,2},{4,5},{5,4},{6,7},{7,6},{8,9},{9,8},{10,11... | collective-permute-start | bytes 1572872 | tf_op jit(solution)/shard_map/ppermute | solution.py:200
  0.7 5.6 %collective-permute-start.2 = (s32[1,256]{1,0:T(1,128)S(1)}, s32[1,256]{1,0:T(1,128)S(1)}, u32[]{:S(2)}, u32[]{:S(2)}) collective-permute-start(s32[1,256]{1,0:T(1,128)S(1)} %bitcast.2), channel_id=1, source_target_pairs={{0,1},{1,0},{2,3},{3,2},{4,5},{5,4},{6,7},{7,6},{8,9},{9,8},{10,11... | collective-permute-start | bytes 3080 | tf_op jit(solution)/shard_map/ppermute | solution.py:200
  1.1 1.0 %copy-start = (bf16[256,1024]{1,0:T(8,128)(2,1)S(1)}, bf16[256,1024]{1,0:T(8,128)(2,1)}, u32[]{:S(2)}) copy-start(bf16[256,1024]{1,0:T(8,128)(2,1)} %refs_0_.1) | copy-start | bytes 1572868
  2.6 12.8 %collective-permute-start = (bf16[64,1024]{1,0:T(8,128)(2,1)S(1)}, bf16[64,1024]{1,0:T(8,128)(2,1)S(1)}, u32[]{:S(2)}, u32[]{:S(2)}) collective-permute-start(bf16[64,1024]{1,0:T(8,128)(2,1)S(1)} %get-tuple-element.13), channel_id=1, source_target_pairs={{0,8},{1,11},{2,10},{3,9},{4,12},{5,15},{6,14},{7,13},{8,0},{9,3},... | collective-permute-start | bytes 393224 | tf_op jit(solution)/shard_map/ppermute | solution.py:216
  7.0 11.4 %collective-permute-start.3 = (bf16[64,1024]{1,0:T(8,128)(2,1)S(1)}, bf16[64,1024]{1,0:T(8,128)(2,1)S(1)}, u32[]{:S(2)}, u32[]{:S(2)}) collective-permute-start(bf16[64,1024]{1,0:T(8,128)(2,1)S(1)} %get-tuple-element.15), channel_id=1, source_target_pairs={{0,8},{1,11},{2,10},{3,9},{4,12},{5,15},{6,14},{7,13},{8,0},{9,3},... | collective-permute-start | bytes 393224 | tf_op jit(solution)/shard_map/ppermute | solution.py:216
  7.1 12.3 %collective-permute-start.4 = (bf16[128,1024]{1,0:T(8,128)(2,1)S(1)}, bf16[128,1024]{1,0:T(8,128)(2,1)S(1)}, u32[]{:S(2)}, u32[]{:S(2)}) collective-permute-start(bf16[128,1024]{1,0:T(8,128)(2,1)S(1)} %get-tuple-element.16), channel_id=1, source_target_pairs={{0,0},{1,3},{2,2},{3,1},{4,4},{5,7},{6,6},{7,5},{8,8},{9,11},{10,1... | collective-permute-start | bytes 786440 | tf_op jit(solution)/shard_map/ppermute | solution.py:216
  7.8 11.7 %collective-permute-start.5 = (bf16[128,1024]{1,0:T(8,128)(2,1)S(1)}, bf16[128,1024]{1,0:T(8,128)(2,1)S(1)}, u32[]{:S(2)}, u32[]{:S(2)}) collective-permute-start(bf16[128,1024]{1,0:T(8,128)(2,1)S(1)} %get-tuple-element.17), channel_id=1, source_target_pairs={{0,4},{1,7},{2,6},{3,5},{4,0},{5,3},{6,2},{7,1},{8,12},{9,15},{10,... | collective-permute-start | bytes 786440 | tf_op jit(solution)/shard_map/ppermute | solution.py:216
  9.8 18.3 %collective-permute-start.9 = (bf16[128,1024]{1,0:T(8,128)(2,1)S(1)}, bf16[128,1024]{1,0:T(8,128)(2,1)S(1)}, u32[]{:S(2)}, u32[]{:S(2)}) collective-permute-start(bf16[128,1024]{1,0:T(8,128)(2,1)S(1)} %get-tuple-element.18), channel_id=1, source_target_pairs={{0,12},{1,15},{2,14},{3,13},{4,8},{5,11},{6,10},{7,9},{8,4},{9,7},... | collective-permute-start | bytes 786440 | tf_op jit(solution)/shard_map/ppermute | solution.py:216
  18.4 9.6 %collective-permute-start.6 = (bf16[128,1024]{1,0:T(8,128)(2,1)S(1)}, bf16[128,1024]{1,0:T(8,128)(2,1)S(1)}, u32[]{:S(2)}, u32[]{:S(2)}) collective-permute-start(bf16[128,1024]{1,0:T(8,128)(2,1)S(1)} %join.1.refs_0_), channel_id=1, source_target_pairs={{0,1},{1,0},{2,3},{3,2},{4,5},{5,4},{6,7},{7,6},{8,9},{9,8},{10,11... | collective-permute-start | bytes 786440 | tf_op jit(solution)/shard_map/ppermute | solution.py:200
  19.4 8.7 %collective-permute-start.7 = (bf16[128,1024]{1,0:T(8,128)(2,1)S(1)}, bf16[128,1024]{1,0:T(8,128)(2,1)S(1)}, u32[]{:S(2)}, u32[]{:S(2)}) collective-permute-start(bf16[128,1024]{1,0:T(8,128)(2,1)S(1)} %collective-permute-done.4.refs_1_), channel_id=1, source_target_pairs={{0,1},{1,0},{2,3},{3,2},{4,5},{5,4},{6,7},{7,6},{8,9},{9,8},{10,11... | collective-permute-start | bytes 786440 | tf_op jit(solution)/shard_map/ppermute | solution.py:200
  19.5 9.8 %collective-permute-start.8 = (bf16[128,1024]{1,0:T(8,128)(2,1)S(1)}, bf16[128,1024]{1,0:T(8,128)(2,1)S(1)}, u32[]{:S(2)}, u32[]{:S(2)}) collective-permute-start(bf16[128,1024]{1,0:T(8,128)(2,1)S(1)} %collective-permute-done.5.refs_2_), channel_id=1, source_target_pairs={{0,1},{1,0},{2,3},{3,2},{4,5},{5,4},{6,7},{7,6},{8,9},{9,8},{10,11... | collective-permute-start | bytes 786440 | tf_op jit(solution)/shard_map/ppermute | solution.py:200
  28.1 2.8 %collective-permute-start.10 = (bf16[128,1024]{1,0:T(8,128)(2,1)S(1)}, bf16[128,1024]{1,0:T(8,128)(2,1)S(1)}, u32[]{:S(2)}, u32[]{:S(2)}) collective-permute-start(bf16[128,1024]{1,0:T(8,128)(2,1)S(1)} %collective-permute-done.9.refs_6_), channel_id=1, source_target_pairs={{0,1},{1,0},{2,3},{3,2},{4,5},{5,4},{6,7},{7,6},{8,9},{9,8},{10,11... | collective-permute-start | bytes 786440 | tf_op jit(solution)/shard_map/ppermute | solution.py:200

commit v18 on v7

--- a/solution.py
+++ b/solution.py
@@ -15,7 +15,7 @@
 sharpness = 0.05
 
 EMPTY = 4.0
-TILE = 256
+TILE = 1024
 VMEM = pl.BlockSpec(memory_space=pltpu.VMEM)
 
 

time: 44.8 us -> 44.8 us (level)
  no operation moved by 1% of the time
where the time goes in v18:
time: 44.8 us; the launch traced here: 44.6 us
  starting transfers between devices  19.4 us (43%)
  blocking collectives  12.3 us (27%)
  waiting for transfers between devices  7.34 us (16%)
  Pallas kernels  4.25 us (9%)
  local copies, waits for them, and re-layouts  1.27 us (3%)
    all_to_all x1, blocking collectives, body_by_chip(): lax.all_to_all(counts, ('owner', 'helper'), split_axis=0, concat_axis=0,...  12.3 us
    ppermute x6, starting transfers between devices, swap_cores(): return lax.ppermute(x, 'sub', [(i, i ^ 1) for i in range(cores)])  10.5 us
    ppermute x5, starting transfers between devices, across(): return lax.ppermute(x, ('owner', 'helper', 'sub'), pairs)  8.83 us
    ppermute x5, waiting for transfers between devices, across(): return lax.ppermute(x, ('owner', 'helper', 'sub'), pairs)  6.19 us
    pallas_call x6, Pallas kernels, call_kernel(): pl.pallas_call(kernel, out_shape=out_shape, in_specs=[VMEM] * len(args),...  4.25 us
    unnamed x4, local copies, waits for them, and re-layouts  1.27 us
    ppermute x6, waiting for transfers between devices, swap_cores(): return lax.ppermute(x, 'sub', [(i, i ^ 1) for i in range(cores)])  1.15 us
  transfers between devices with their start and end apart: 11, of which 3 were waited for; matrix products, arithmetic and copies ran while one was open for 0% of the time, Pallas kernels for 5%

profile of v18, /device:TPU:0, one launch (start us, length us, event | category | flops | bytes accessed | tf_op | source)
XLA Modules:
  0.0 44.6 jit_solution(11715266522598652779)
XLA Ops:
  0.0 0.0 copy-start.1
  0.0 0.5 %collective-permute-start.1 = (bf16[256,1024]{1,0:T(8,128)(2,1)}, bf16[256,1024]{1,0:T(8,128)(2,1)S(1)}, u32[]{:S(2)}, u32[]{:S(2)}) collective-permute-start(bf16[256,1024]{1,0:T(8,128)(2,1)} %refs_0_.1), channel_id=1, source_target_pairs={{0,1},{1,0},{2,3},{3,2},{4,5},{5,4},{6,7},{7,6},{8,9},{9,8},{10,11... | collective-permute-start | bytes 1572872 | tf_op jit(solution)/shard_map/ppermute | solution.py:182
  0.5 0.2 copy-done.1
  0.7 0.5 %collective-permute-start.2 = (s32[1,256]{1,0:T(1,128)S(1)}, s32[1,256]{1,0:T(1,128)S(1)}, u32[]{:S(2)}, u32[]{:S(2)}) collective-permute-start(s32[1,256]{1,0:T(1,128)S(1)} %bitcast.2), channel_id=1, source_target_pairs={{0,1},{1,0},{2,3},{3,2},{4,5},{5,4},{6,7},{7,6},{8,9},{9,8},{10,11... | collective-permute-start | bytes 3080 | tf_op jit(solution)/shard_map/ppermute | solution.py:182
  1.1 0.0 copy-start
  1.1 1.0 %copy-done = bf16[256,1024]{1,0:T(8,128)(2,1)S(1)} copy-done((bf16[256,1024]{1,0:T(8,128)(2,1)S(1)}, bf16[256,1024]{1,0:T(8,128)(2,1)}, u32[]{:S(2)}) %copy-start) | copy-done | bytes 524312
  2.2 0.5 %route_first.1 = (bf16[64,1024]{1,0:T(8,128)(2,1)S(1)}, s32[1,256]{1,0:T(1,128)S(1)}) custom-call(bf16[256,1024]{1,0:T(8,128)(2,1)S(1)} %copy-done, s32[1,256]{1,0:T(1,128)S(1)} %bitcast.3), custom_call_target="tpu_custom_call" | custom-call | tf_op jit(solution)/shard_map/route_first/pallas_call | solution.py:92
  2.6 3.7 %collective-permute-start = (bf16[64,1024]{1,0:T(8,128)(2,1)S(1)}, bf16[64,1024]{1,0:T(8,128)(2,1)S(1)}, u32[]{:S(2)}, u32[]{:S(2)}) collective-permute-start(bf16[64,1024]{1,0:T(8,128)(2,1)S(1)} %get-tuple-element.11), channel_id=1, source_target_pairs={{0,8},{1,11},{2,10},{3,9},{4,12},{5,15},{6,14},{7,13},{8,0},{9,3},... | collective-permute-start | bytes 393224 | tf_op jit(solution)/shard_map/ppermute | solution.py:198
  6.3 0.0 collective-permute-done.2.refs_3_
  6.3 0.0 collective-permute-done.1.refs_1_
  6.3 0.7 %route_rest.1 = (bf16[64,1024]{1,0:T(8,128)(2,1)S(1)}, bf16[128,1024]{1,0:T(8,128)(2,1)S(1)}, bf16[128,1024]{1,0:T(8,128)(2,1)S(1)}, bf16[128,1024]{1,0:T(8,128)(2,1)S(1)}) custom-call(bf16[256,1024]{1,0:T(8,128)(2,1)S(1)} %copy-done, bf16[256,1024]{1,0:T(8,128)(2,1)S(1)} %collective-permute-done.1.refs_1_, s32[1,256]{1,0:T(1,128)S(1)} %get-tuple-element.12.refs_2_.slot_ref, ...), custom_call_target="tpu_custom_call" | custom-call | tf_op jit(solution)/shard_map/route_rest/pallas_call | solution.py:92
  7.0 0.1 collective-permute-start.3
  7.1 0.7 %collective-permute-start.4 = (bf16[128,1024]{1,0:T(8,128)(2,1)S(1)}, bf16[128,1024]{1,0:T(8,128)(2,1)S(1)}, u32[]{:S(2)}, u32[]{:S(2)}) collective-permute-start(bf16[128,1024]{1,0:T(8,128)(2,1)S(1)} %get-tuple-element.14), channel_id=1, source_target_pairs={{0,0},{1,3},{2,2},{3,1},{4,4},{5,7},{6,6},{7,5},{8,8},{9,11},{10,1... | collective-permute-start | bytes 786440 | tf_op jit(solution)/shard_map/ppermute | solution.py:198
  7.8 1.9 %collective-permute-start.5 = (bf16[128,1024]{1,0:T(8,128)(2,1)S(1)}, bf16[128,1024]{1,0:T(8,128)(2,1)S(1)}, u32[]{:S(2)}, u32[]{:S(2)}) collective-permute-start(bf16[128,1024]{1,0:T(8,128)(2,1)S(1)} %get-tuple-element.15), channel_id=1, source_target_pairs={{0,4},{1,7},{2,6},{3,5},{4,0},{5,3},{6,2},{7,1},{8,12},{9,15},{10,... | collective-permute-start | bytes 786440 | tf_op jit(solution)/shard_map/ppermute | solution.py:198
  9.8 2.5 %collective-permute-start.9 = (bf16[128,1024]{1,0:T(8,128)(2,1)S(1)}, bf16[128,1024]{1,0:T(8,128)(2,1)S(1)}, u32[]{:S(2)}, u32[]{:S(2)}) collective-permute-start(bf16[128,1024]{1,0:T(8,128)(2,1)S(1)} %get-tuple-element.16), channel_id=1, source_target_pairs={{0,12},{1,15},{2,14},{3,13},{4,8},{5,11},{6,10},{7,9},{8,4},{9,7},... | collective-permute-start | bytes 786440 | tf_op jit(solution)/shard_map/ppermute | solution.py:198
  12.2 3.2 %collective-permute-done.first_ref = bf16[64,1024]{1,0:T(8,128)(2,1)S(1)} collective-permute-done((bf16[64,1024]{1,0:T(8,128)(2,1)S(1)}, bf16[64,1024]{1,0:T(8,128)(2,1)S(1)}, u32[]{:S(2)}, u32[]{:S(2)}) %collective-permute-start) | collective-permute-done | bytes 131104 | tf_op jit(solution)/shard_map/ppermute | solution.py:198
  15.4 3.0 %collective-permute-done.3.second_ref = bf16[64,1024]{1,0:T(8,128)(2,1)S(1)} collective-permute-done((bf16[64,1024]{1,0:T(8,128)(2,1)S(1)}, bf16[64,1024]{1,0:T(8,128)(2,1)S(1)}, u32[]{:S(2)}, u32[]{:S(2)}) %collective-permute-start.3) | collective-permute-done | bytes 131104 | tf_op jit(solution)/shard_map/ppermute | solution.py:198
  18.4 0.9 %collective-permute-start.6 = (bf16[128,1024]{1,0:T(8,128)(2,1)S(1)}, bf16[128,1024]{1,0:T(8,128)(2,1)S(1)}, u32[]{:S(2)}, u32[]{:S(2)}) collective-permute-start(bf16[128,1024]{1,0:T(8,128)(2,1)S(1)} %join.1.refs_0_), channel_id=1, source_target_pairs={{0,1},{1,0},{2,3},{3,2},{4,5},{5,4},{6,7},{7,6},{8,9},{9,8},{10,11... | collective-permute-start | bytes 786440 | tf_op jit(solution)/shard_map/ppermute | solution.py:182
  19.4 0.0 collective-permute-done.4.refs_1_
  19.4 0.1 collective-permute-start.7
  19.5 0.0 collective-permute-done.5.refs_2_
  19.5 8.6 %collective-permute-start.8 = (bf16[128,1024]{1,0:T(8,128)(2,1)S(1)}, bf16[128,1024]{1,0:T(8,128)(2,1)S(1)}, u32[]{:S(2)}, u32[]{:S(2)}) collective-permute-start(bf16[128,1024]{1,0:T(8,128)(2,1)S(1)} %collective-permute-done.5.refs_2_), channel_id=1, source_target_pairs={{0,1},{1,0},{2,3},{3,2},{4,5},{5,4},{6,7},{7,6},{8,9},{9,8},{10,11... | collective-permute-start | bytes 786440 | tf_op jit(solution)/shard_map/ppermute | solution.py:182
  28.1 0.0 collective-permute-done.9.refs_6_
  28.1 0.0 collective-permute-start.10
  28.1 0.0 collective-permute-done.6.refs_3_
  28.1 0.0 collective-permute-done.7.refs_4_
  28.1 1.1 %collective-permute-done.8.refs_5_ = bf16[128,1024]{1,0:T(8,128)(2,1)S(1)} collective-permute-done((bf16[128,1024]{1,0:T(8,128)(2,1)S(1)}, bf16[128,1024]{1,0:T(8,128)(2,1)S(1)}, u32[]{:S(2)}, u32[]{:S(2)}) %collective-permute-start.8) | collective-permute-done | bytes 262176 | tf_op jit(solution)/shard_map/ppermute | solution.py:182
  29.2 1.2 %count.1.refs_8_ = f32[1,384]{1,0:T(1,128)S(1)} custom-call(bf16[128,1024]{1,0:T(8,128)(2,1)S(1)} %join.1.refs_0_, bf16[128,1024]{1,0:T(8,128)(2,1)S(1)} %collective-permute-done.4.refs_1_, bf16[128,1024]{1,0:T(8,128)(2,1)S(1)} %collective-permute-done.5.refs_2_, bf16[128,1024]{1,0:T(8,128)(2,1)S(1)} %collective-permute-done.6.refs_3_, ...), custom_call_target="tpu_custom_call" | custom-call | tf_op jit(solution)/shard_map/count/pallas_call | solution.py:92
  30.4 0.0 collective-permute-done.10.refs_7_
  30.4 1.1 %finish.1 = f32[8,1,64]{2,1,0:T(1,128)S(1)} custom-call(bf16[128,1024]{1,0:T(8,128)(2,1)S(1)} %join.1.refs_0_, bf16[128,1024]{1,0:T(8,128)(2,1)S(1)} %collective-permute-done.4.refs_1_, bf16[128,1024]{1,0:T(8,128)(2,1)S(1)} %collective-permute-done.5.refs_2_, bf16[128,1024]{1,0:T(8,128)(2,1)S(1)} %collective-permute-done.6.refs_3_, ...), custom_call_target="tpu_custom_call" | custom-call | tf_op jit(solution)/shard_map/finish/pallas_call | solution.py:92
  31.6 12.3 %all_to_all.5.counts_ref = f32[8,1,64]{2,1,0:T(1,128)S(1)} all-to-all(f32[8,1,64]{2,1,0:T(1,128)S(1)} %finish.1), channel_id=1, replica_groups=mesh['groups'=2,'owner'=4,'helper'=2,'sub'=2] {'owner','helper'}, dimensions={0} | all-to-all | bytes 4096 | tf_op jit(solution)/shard_map/all_to_all | solution.py:253
  43.9 0.7 %select.1 = f32[1,256]{1,0:T(1,128)} custom-call(f32[8,1,64]{2,1,0:T(1,128)S(1)} %all_to_all.5.counts_ref, s32[1,256]{1,0:T(1,128)S(1)} %get-tuple-element.12.refs_2_.slot_ref), custom_call_target="tpu_custom_call" | custom-call | tf_op jit(solution)/shard_map/select/pallas_call | solution.py:92
  (1 shorter events, 0.0 us)
Async XLA Ops:
  0.0 0.7 %copy-start.1 = (s32[256]{0:T(256)S(1)}, s32[256]{0:T(256)}, u32[]{:S(2)}) copy-start(s32[256]{0:T(256)} %param.3) | copy-start | bytes 3076
  0.0 6.3 %collective-permute-start.1 = (bf16[256,1024]{1,0:T(8,128)(2,1)}, bf16[256,1024]{1,0:T(8,128)(2,1)S(1)}, u32[]{:S(2)}, u32[]{:S(2)}) collective-permute-start(bf16[256,1024]{1,0:T(8,128)(2,1)} %refs_0_.1), channel_id=1, source_target_pairs={{0,1},{1,0},{2,3},{3,2},{4,5},{5,4},{6,7},{7,6},{8,9},{9,8},{10,11... | collective-permute-start | bytes 1572872 | tf_op jit(solution)/shard_map/ppermute | solution.py:182
  0.7 5.6 %collective-permute-start.2 = (s32[1,256]{1,0:T(1,128)S(1)}, s32[1,256]{1,0:T(1,128)S(1)}, u32[]{:S(2)}, u32[]{:S(2)}) collective-permute-start(s32[1,256]{1,0:T(1,128)S(1)} %bitcast.2), channel_id=1, source_target_pairs={{0,1},{1,0},{2,3},{3,2},{4,5},{5,4},{6,7},{7,6},{8,9},{9,8},{10,11... | collective-permute-start | bytes 3080 | tf_op jit(solution)/shard_map/ppermute | solution.py:182
  1.1 1.0 %copy-start = (bf16[256,1024]{1,0:T(8,128)(2,1)S(1)}, bf16[256,1024]{1,0:T(8,128)(2,1)}, u32[]{:S(2)}) copy-start(bf16[256,1024]{1,0:T(8,128)(2,1)} %refs_0_.1) | copy-start | bytes 1572868
  2.6 12.8 %collective-permute-start = (bf16[64,1024]{1,0:T(8,128)(2,1)S(1)}, bf16[64,1024]{1,0:T(8,128)(2,1)S(1)}, u32[]{:S(2)}, u32[]{:S(2)}) collective-permute-start(bf16[64,1024]{1,0:T(8,128)(2,1)S(1)} %get-tuple-element.11), channel_id=1, source_target_pairs={{0,8},{1,11},{2,10},{3,9},{4,12},{5,15},{6,14},{7,13},{8,0},{9,3},... | collective-permute-start | bytes 393224 | tf_op jit(solution)/shard_map/ppermute | solution.py:198
  7.0 11.4 %collective-permute-start.3 = (bf16[64,1024]{1,0:T(8,128)(2,1)S(1)}, bf16[64,1024]{1,0:T(8,128)(2,1)S(1)}, u32[]{:S(2)}, u32[]{:S(2)}) collective-permute-start(bf16[64,1024]{1,0:T(8,128)(2,1)S(1)} %get-tuple-element.13), channel_id=1, source_target_pairs={{0,8},{1,11},{2,10},{3,9},{4,12},{5,15},{6,14},{7,13},{8,0},{9,3},... | collective-permute-start | bytes 393224 | tf_op jit(solution)/shard_map/ppermute | solution.py:198
  7.1 12.3 %collective-permute-start.4 = (bf16[128,1024]{1,0:T(8,128)(2,1)S(1)}, bf16[128,1024]{1,0:T(8,128)(2,1)S(1)}, u32[]{:S(2)}, u32[]{:S(2)}) collective-permute-start(bf16[128,1024]{1,0:T(8,128)(2,1)S(1)} %get-tuple-element.14), channel_id=1, source_target_pairs={{0,0},{1,3},{2,2},{3,1},{4,4},{5,7},{6,6},{7,5},{8,8},{9,11},{10,1... | collective-permute-start | bytes 786440 | tf_op jit(solution)/shard_map/ppermute | solution.py:198
  7.8 11.7 %collective-permute-start.5 = (bf16[128,1024]{1,0:T(8,128)(2,1)S(1)}, bf16[128,1024]{1,0:T(8,128)(2,1)S(1)}, u32[]{:S(2)}, u32[]{:S(2)}) collective-permute-start(bf16[128,1024]{1,0:T(8,128)(2,1)S(1)} %get-tuple-element.15), channel_id=1, source_target_pairs={{0,4},{1,7},{2,6},{3,5},{4,0},{5,3},{6,2},{7,1},{8,12},{9,15},{10,... | collective-permute-start | bytes 786440 | tf_op jit(solution)/shard_map/ppermute | solution.py:198
  9.8 18.3 %collective-permute-start.9 = (bf16[128,1024]{1,0:T(8,128)(2,1)S(1)}, bf16[128,1024]{1,0:T(8,128)(2,1)S(1)}, u32[]{:S(2)}, u32[]{:S(2)}) collective-permute-start(bf16[128,1024]{1,0:T(8,128)(2,1)S(1)} %get-tuple-element.16), channel_id=1, source_target_pairs={{0,12},{1,15},{2,14},{3,13},{4,8},{5,11},{6,10},{7,9},{8,4},{9,7},... | collective-permute-start | bytes 786440 | tf_op jit(solution)/shard_map/ppermute | solution.py:198
  18.4 9.6 %collective-permute-start.6 = (bf16[128,1024]{1,0:T(8,128)(2,1)S(1)}, bf16[128,1024]{1,0:T(8,128)(2,1)S(1)}, u32[]{:S(2)}, u32[]{:S(2)}) collective-permute-start(bf16[128,1024]{1,0:T(8,128)(2,1)S(1)} %join.1.refs_0_), channel_id=1, source_target_pairs={{0,1},{1,0},{2,3},{3,2},{4,5},{5,4},{6,7},{7,6},{8,9},{9,8},{10,11... | collective-permute-start | bytes 786440 | tf_op jit(solution)/shard_map/ppermute | solution.py:182
  19.4 8.7 %collective-permute-start.7 = (bf16[128,1024]{1,0:T(8,128)(2,1)S(1)}, bf16[128,1024]{1,0:T(8,128)(2,1)S(1)}, u32[]{:S(2)}, u32[]{:S(2)}) collective-permute-start(bf16[128,1024]{1,0:T(8,128)(2,1)S(1)} %collective-permute-done.4.refs_1_), channel_id=1, source_target_pairs={{0,1},{1,0},{2,3},{3,2},{4,5},{5,4},{6,7},{7,6},{8,9},{9,8},{10,11... | collective-permute-start | bytes 786440 | tf_op jit(solution)/shard_map/ppermute | solution.py:182
  19.5 9.8 %collective-permute-start.8 = (bf16[128,1024]{1,0:T(8,128)(2,1)S(1)}, bf16[128,1024]{1,0:T(8,128)(2,1)S(1)}, u32[]{:S(2)}, u32[]{:S(2)}) collective-permute-start(bf16[128,1024]{1,0:T(8,128)(2,1)S(1)} %collective-permute-done.5.refs_2_), channel_id=1, source_target_pairs={{0,1},{1,0},{2,3},{3,2},{4,5},{5,4},{6,7},{7,6},{8,9},{9,8},{10,11... | collective-permute-start | bytes 786440 | tf_op jit(solution)/shard_map/ppermute | solution.py:182
  28.1 2.4 %collective-permute-start.10 = (bf16[128,1024]{1,0:T(8,128)(2,1)S(1)}, bf16[128,1024]{1,0:T(8,128)(2,1)S(1)}, u32[]{:S(2)}, u32[]{:S(2)}) collective-permute-start(bf16[128,1024]{1,0:T(8,128)(2,1)S(1)} %collective-permute-done.9.refs_6_), channel_id=1, source_target_pairs={{0,1},{1,0},{2,3},{3,2},{4,5},{5,4},{6,7},{7,6},{8,9},{9,8},{10,11... | collective-permute-start | bytes 786440 | tf_op jit(solution)/shard_map/ppermute | solution.py:182

commit v19 on v18

--- a/solution.py
+++ b/solution.py
@@ -16,6 +16,7 @@
 
 EMPTY = 4.0
 TILE = 1024
+LANES = 128
 VMEM = pl.BlockSpec(memory_space=pltpu.VMEM)
 
 
@@ -141,9 +142,9 @@
     return call_kernel("count", functools.partial(count_kernel, starts, size), out_shape, *pieces)
 
 
-def finish_kernel(starts, late_pieces, late_starts, places, *refs):
+def finish_kernel(starts, late_pieces, late_starts, places, here_size, *refs):
     *piece_refs, early_ref, count_ref = refs
-    size = count_ref.shape[2]
+    size = here_size
     early = jnp.concatenate([piece[...] for piece in piece_refs[:-late_pieces]], axis=0)
     late = jnp.concatenate([piece[...] for piece in piece_refs[-late_pieces:]], axis=0)
     own = blocks(early, starts, size)
@@ -154,11 +155,13 @@
     )
     for k, place in enumerate(places()):
         source, j = (total, k) if k < len(starts) else (late_total, k - len(starts))
-        count_ref[pl.ds(place, 1), 0, :] = source[:, j * size : (j + 1) * size]
+        block = source[:, j * size : (j + 1) * size]
+        padding = jnp.zeros((1, count_ref.shape[2] - size), jnp.float32)
+        count_ref[pl.ds(place, 1), 0, :] = jnp.concatenate([block, padding], axis=1)
 
 
 def select_kernel(capacity, counts_ref, slot_ref, out_ref):
-    counts = counts_ref[:, 0, :]
+    counts = counts_ref[:, 0, :][:, :capacity]
     slot = slot_ref[...]
     doc_count = slot.shape[1]
     block = slot // capacity
@@ -244,8 +247,8 @@
 
     counts = call_kernel(
         "finish",
-        functools.partial(finish_kernel, starts, len(late), late_starts, places),
-        jax.ShapeDtypeStruct((clusters, 1, capacity), jnp.float32),
+        functools.partial(finish_kernel, starts, len(late), late_starts, places, capacity),
+        jax.ShapeDtypeStruct((clusters, 1, LANES), jnp.float32),
         *early,
         *late,
         soft_counts(early, starts, capacity),

time: 44.8 us -> 44.8 us (level)
  no operation moved by 1% of the time
where the time goes in v19:
time: 44.8 us; the launch traced here: 44.6 us
  starting transfers between devices  19.4 us (43%)
  blocking collectives  12.3 us (27%)
  waiting for transfers between devices  7.34 us (16%)
  Pallas kernels  4.26 us (10%)
  local copies, waits for them, and re-layouts  1.27 us (3%)
    all_to_all x1, blocking collectives, body_by_chip(): lax.all_to_all(counts, ('owner', 'helper'), split_axis=0, concat_axis=0,...  12.3 us
    ppermute x6, starting transfers between devices, swap_cores(): return lax.ppermute(x, 'sub', [(i, i ^ 1) for i in range(cores)])  10.5 us
    ppermute x5, starting transfers between devices, across(): return lax.ppermute(x, ('owner', 'helper', 'sub'), pairs)  8.83 us
    ppermute x5, waiting for transfers between devices, across(): return lax.ppermute(x, ('owner', 'helper', 'sub'), pairs)  6.19 us
    pallas_call x6, Pallas kernels, call_kernel(): pl.pallas_call(kernel, out_shape=out_shape, in_specs=[VMEM] * len(args),...  4.26 us
    unnamed x4, local copies, waits for them, and re-layouts  1.27 us
    ppermute x6, waiting for transfers between devices, swap_cores(): return lax.ppermute(x, 'sub', [(i, i ^ 1) for i in range(cores)])  1.15 us
  transfers between devices with their start and end apart: 11, of which 3 were waited for; matrix products, arithmetic and copies ran while one was open for 0% of the time, Pallas kernels for 5%

profile of v19, /device:TPU:0, one launch (start us, length us, event | category | flops | bytes accessed | tf_op | source)
XLA Modules:
  0.0 44.6 jit_solution(5577637106131831357)
XLA Ops:
  0.0 0.0 copy-start.1
  0.0 0.5 %collective-permute-start.1 = (bf16[256,1024]{1,0:T(8,128)(2,1)}, bf16[256,1024]{1,0:T(8,128)(2,1)S(1)}, u32[]{:S(2)}, u32[]{:S(2)}) collective-permute-start(bf16[256,1024]{1,0:T(8,128)(2,1)} %refs_0_.1), channel_id=1, source_target_pairs={{0,1},{1,0},{2,3},{3,2},{4,5},{5,4},{6,7},{7,6},{8,9},{9,8},{10,11... | collective-permute-start | bytes 1572872 | tf_op jit(solution)/shard_map/ppermute | solution.py:185
  0.5 0.2 copy-done.1
  0.7 0.5 %collective-permute-start.2 = (s32[1,256]{1,0:T(1,128)S(1)}, s32[1,256]{1,0:T(1,128)S(1)}, u32[]{:S(2)}, u32[]{:S(2)}) collective-permute-start(s32[1,256]{1,0:T(1,128)S(1)} %bitcast.2), channel_id=1, source_target_pairs={{0,1},{1,0},{2,3},{3,2},{4,5},{5,4},{6,7},{7,6},{8,9},{9,8},{10,11... | collective-permute-start | bytes 3080 | tf_op jit(solution)/shard_map/ppermute | solution.py:185
  1.1 0.0 copy-start
  1.1 1.0 %copy-done = bf16[256,1024]{1,0:T(8,128)(2,1)S(1)} copy-done((bf16[256,1024]{1,0:T(8,128)(2,1)S(1)}, bf16[256,1024]{1,0:T(8,128)(2,1)}, u32[]{:S(2)}) %copy-start) | copy-done | bytes 524312
  2.2 0.5 %route_first.1 = (bf16[64,1024]{1,0:T(8,128)(2,1)S(1)}, s32[1,256]{1,0:T(1,128)S(1)}) custom-call(bf16[256,1024]{1,0:T(8,128)(2,1)S(1)} %copy-done, s32[1,256]{1,0:T(1,128)S(1)} %bitcast.3), custom_call_target="tpu_custom_call" | custom-call | tf_op jit(solution)/shard_map/route_first/pallas_call | solution.py:93
  2.6 3.7 %collective-permute-start = (bf16[64,1024]{1,0:T(8,128)(2,1)S(1)}, bf16[64,1024]{1,0:T(8,128)(2,1)S(1)}, u32[]{:S(2)}, u32[]{:S(2)}) collective-permute-start(bf16[64,1024]{1,0:T(8,128)(2,1)S(1)} %get-tuple-element.11), channel_id=1, source_target_pairs={{0,8},{1,11},{2,10},{3,9},{4,12},{5,15},{6,14},{7,13},{8,0},{9,3},... | collective-permute-start | bytes 393224 | tf_op jit(solution)/shard_map/ppermute | solution.py:201
  6.3 0.0 collective-permute-done.2.refs_3_
  6.3 0.0 collective-permute-done.1.refs_1_
  6.3 0.7 %route_rest.1 = (bf16[64,1024]{1,0:T(8,128)(2,1)S(1)}, bf16[128,1024]{1,0:T(8,128)(2,1)S(1)}, bf16[128,1024]{1,0:T(8,128)(2,1)S(1)}, bf16[128,1024]{1,0:T(8,128)(2,1)S(1)}) custom-call(bf16[256,1024]{1,0:T(8,128)(2,1)S(1)} %copy-done, bf16[256,1024]{1,0:T(8,128)(2,1)S(1)} %collective-permute-done.1.refs_1_, s32[1,256]{1,0:T(1,128)S(1)} %get-tuple-element.12.refs_2_.slot_ref, ...), custom_call_target="tpu_custom_call" | custom-call | tf_op jit(solution)/shard_map/route_rest/pallas_call | solution.py:93
  7.0 0.1 collective-permute-start.3
  7.1 0.7 %collective-permute-start.4 = (bf16[128,1024]{1,0:T(8,128)(2,1)S(1)}, bf16[128,1024]{1,0:T(8,128)(2,1)S(1)}, u32[]{:S(2)}, u32[]{:S(2)}) collective-permute-start(bf16[128,1024]{1,0:T(8,128)(2,1)S(1)} %get-tuple-element.14), channel_id=1, source_target_pairs={{0,0},{1,3},{2,2},{3,1},{4,4},{5,7},{6,6},{7,5},{8,8},{9,11},{10,1... | collective-permute-start | bytes 786440 | tf_op jit(solution)/shard_map/ppermute | solution.py:201
  7.8 1.9 %collective-permute-start.5 = (bf16[128,1024]{1,0:T(8,128)(2,1)S(1)}, bf16[128,1024]{1,0:T(8,128)(2,1)S(1)}, u32[]{:S(2)}, u32[]{:S(2)}) collective-permute-start(bf16[128,1024]{1,0:T(8,128)(2,1)S(1)} %get-tuple-element.15), channel_id=1, source_target_pairs={{0,4},{1,7},{2,6},{3,5},{4,0},{5,3},{6,2},{7,1},{8,12},{9,15},{10,... | collective-permute-start | bytes 786440 | tf_op jit(solution)/shard_map/ppermute | solution.py:201
  9.8 2.5 %collective-permute-start.9 = (bf16[128,1024]{1,0:T(8,128)(2,1)S(1)}, bf16[128,1024]{1,0:T(8,128)(2,1)S(1)}, u32[]{:S(2)}, u32[]{:S(2)}) collective-permute-start(bf16[128,1024]{1,0:T(8,128)(2,1)S(1)} %get-tuple-element.16), channel_id=1, source_target_pairs={{0,12},{1,15},{2,14},{3,13},{4,8},{5,11},{6,10},{7,9},{8,4},{9,7},... | collective-permute-start | bytes 786440 | tf_op jit(solution)/shard_map/ppermute | solution.py:201
  12.2 3.2 %collective-permute-done.first_ref = bf16[64,1024]{1,0:T(8,128)(2,1)S(1)} collective-permute-done((bf16[64,1024]{1,0:T(8,128)(2,1)S(1)}, bf16[64,1024]{1,0:T(8,128)(2,1)S(1)}, u32[]{:S(2)}, u32[]{:S(2)}) %collective-permute-start) | collective-permute-done | bytes 131104 | tf_op jit(solution)/shard_map/ppermute | solution.py:201
  15.4 3.0 %collective-permute-done.3.second_ref = bf16[64,1024]{1,0:T(8,128)(2,1)S(1)} collective-permute-done((bf16[64,1024]{1,0:T(8,128)(2,1)S(1)}, bf16[64,1024]{1,0:T(8,128)(2,1)S(1)}, u32[]{:S(2)}, u32[]{:S(2)}) %collective-permute-start.3) | collective-permute-done | bytes 131104 | tf_op jit(solution)/shard_map/ppermute | solution.py:201
  18.4 0.9 %collective-permute-start.6 = (bf16[128,1024]{1,0:T(8,128)(2,1)S(1)}, bf16[128,1024]{1,0:T(8,128)(2,1)S(1)}, u32[]{:S(2)}, u32[]{:S(2)}) collective-permute-start(bf16[128,1024]{1,0:T(8,128)(2,1)S(1)} %join.1.refs_0_), channel_id=1, source_target_pairs={{0,1},{1,0},{2,3},{3,2},{4,5},{5,4},{6,7},{7,6},{8,9},{9,8},{10,11... | collective-permute-start | bytes 786440 | tf_op jit(solution)/shard_map/ppermute | solution.py:185
  19.4 0.0 collective-permute-done.4.refs_1_
  19.4 0.1 collective-permute-start.7
  19.5 0.0 collective-permute-done.5.refs_2_
  19.5 8.6 %collective-permute-start.8 = (bf16[128,1024]{1,0:T(8,128)(2,1)S(1)}, bf16[128,1024]{1,0:T(8,128)(2,1)S(1)}, u32[]{:S(2)}, u32[]{:S(2)}) collective-permute-start(bf16[128,1024]{1,0:T(8,128)(2,1)S(1)} %collective-permute-done.5.refs_2_), channel_id=1, source_target_pairs={{0,1},{1,0},{2,3},{3,2},{4,5},{5,4},{6,7},{7,6},{8,9},{9,8},{10,11... | collective-permute-start | bytes 786440 | tf_op jit(solution)/shard_map/ppermute | solution.py:185
  28.1 0.0 collective-permute-done.9.refs_6_
  28.1 0.0 collective-permute-start.10
  28.1 0.0 collective-permute-done.6.refs_3_
  28.1 0.0 collective-permute-done.7.refs_4_
  28.1 1.1 %collective-permute-done.8.refs_5_ = bf16[128,1024]{1,0:T(8,128)(2,1)S(1)} collective-permute-done((bf16[128,1024]{1,0:T(8,128)(2,1)S(1)}, bf16[128,1024]{1,0:T(8,128)(2,1)S(1)}, u32[]{:S(2)}, u32[]{:S(2)}) %collective-permute-start.8) | collective-permute-done | bytes 262176 | tf_op jit(solution)/shard_map/ppermute | solution.py:185
  29.2 1.2 %count.1.refs_8_ = f32[1,384]{1,0:T(1,128)S(1)} custom-call(bf16[128,1024]{1,0:T(8,128)(2,1)S(1)} %join.1.refs_0_, bf16[128,1024]{1,0:T(8,128)(2,1)S(1)} %collective-permute-done.4.refs_1_, bf16[128,1024]{1,0:T(8,128)(2,1)S(1)} %collective-permute-done.5.refs_2_, bf16[128,1024]{1,0:T(8,128)(2,1)S(1)} %collective-permute-done.6.refs_3_, ...), custom_call_target="tpu_custom_call" | custom-call | tf_op jit(solution)/shard_map/count/pallas_call | solution.py:93
  30.4 0.0 collective-permute-done.10.refs_7_
  30.4 1.1 %finish.1 = f32[8,1,128]{2,1,0:T(1,128)S(1)} custom-call(bf16[128,1024]{1,0:T(8,128)(2,1)S(1)} %join.1.refs_0_, bf16[128,1024]{1,0:T(8,128)(2,1)S(1)} %collective-permute-done.4.refs_1_, bf16[128,1024]{1,0:T(8,128)(2,1)S(1)} %collective-permute-done.5.refs_2_, bf16[128,1024]{1,0:T(8,128)(2,1)S(1)} %collective-permute-done.6.refs_3_, ...), custom_call_target="tpu_custom_call" | custom-call | tf_op jit(solution)/shard_map/finish/pallas_call | solution.py:93
  31.6 12.3 %all_to_all.5.counts_ref = f32[8,1,128]{2,1,0:T(1,128)S(1)} all-to-all(f32[8,1,128]{2,1,0:T(1,128)S(1)} %finish.1), channel_id=1, replica_groups=mesh['groups'=2,'owner'=4,'helper'=2,'sub'=2] {'owner','helper'}, dimensions={0} | all-to-all | bytes 8192 | tf_op jit(solution)/shard_map/all_to_all | solution.py:256
  43.9 0.7 %select.1 = f32[1,256]{1,0:T(1,128)} custom-call(f32[8,1,128]{2,1,0:T(1,128)S(1)} %all_to_all.5.counts_ref, s32[1,256]{1,0:T(1,128)S(1)} %get-tuple-element.12.refs_2_.slot_ref), custom_call_target="tpu_custom_call" | custom-call | tf_op jit(solution)/shard_map/select/pallas_call | solution.py:93
  (1 shorter events, 0.0 us)
Async XLA Ops:
  0.0 0.7 %copy-start.1 = (s32[256]{0:T(256)S(1)}, s32[256]{0:T(256)}, u32[]{:S(2)}) copy-start(s32[256]{0:T(256)} %param.3) | copy-start | bytes 3076
  0.0 6.3 %collective-permute-start.1 = (bf16[256,1024]{1,0:T(8,128)(2,1)}, bf16[256,1024]{1,0:T(8,128)(2,1)S(1)}, u32[]{:S(2)}, u32[]{:S(2)}) collective-permute-start(bf16[256,1024]{1,0:T(8,128)(2,1)} %refs_0_.1), channel_id=1, source_target_pairs={{0,1},{1,0},{2,3},{3,2},{4,5},{5,4},{6,7},{7,6},{8,9},{9,8},{10,11... | collective-permute-start | bytes 1572872 | tf_op jit(solution)/shard_map/ppermute | solution.py:185
  0.7 5.6 %collective-permute-start.2 = (s32[1,256]{1,0:T(1,128)S(1)}, s32[1,256]{1,0:T(1,128)S(1)}, u32[]{:S(2)}, u32[]{:S(2)}) collective-permute-start(s32[1,256]{1,0:T(1,128)S(1)} %bitcast.2), channel_id=1, source_target_pairs={{0,1},{1,0},{2,3},{3,2},{4,5},{5,4},{6,7},{7,6},{8,9},{9,8},{10,11... | collective-permute-start | bytes 3080 | tf_op jit(solution)/shard_map/ppermute | solution.py:185
  1.1 1.0 %copy-start = (bf16[256,1024]{1,0:T(8,128)(2,1)S(1)}, bf16[256,1024]{1,0:T(8,128)(2,1)}, u32[]{:S(2)}) copy-start(bf16[256,1024]{1,0:T(8,128)(2,1)} %refs_0_.1) | copy-start | bytes 1572868
  2.6 12.8 %collective-permute-start = (bf16[64,1024]{1,0:T(8,128)(2,1)S(1)}, bf16[64,1024]{1,0:T(8,128)(2,1)S(1)}, u32[]{:S(2)}, u32[]{:S(2)}) collective-permute-start(bf16[64,1024]{1,0:T(8,128)(2,1)S(1)} %get-tuple-element.11), channel_id=1, source_target_pairs={{0,8},{1,11},{2,10},{3,9},{4,12},{5,15},{6,14},{7,13},{8,0},{9,3},... | collective-permute-start | bytes 393224 | tf_op jit(solution)/shard_map/ppermute | solution.py:201
  7.0 11.4 %collective-permute-start.3 = (bf16[64,1024]{1,0:T(8,128)(2,1)S(1)}, bf16[64,1024]{1,0:T(8,128)(2,1)S(1)}, u32[]{:S(2)}, u32[]{:S(2)}) collective-permute-start(bf16[64,1024]{1,0:T(8,128)(2,1)S(1)} %get-tuple-element.13), channel_id=1, source_target_pairs={{0,8},{1,11},{2,10},{3,9},{4,12},{5,15},{6,14},{7,13},{8,0},{9,3},... | collective-permute-start | bytes 393224 | tf_op jit(solution)/shard_map/ppermute | solution.py:201
  7.1 12.3 %collective-permute-start.4 = (bf16[128,1024]{1,0:T(8,128)(2,1)S(1)}, bf16[128,1024]{1,0:T(8,128)(2,1)S(1)}, u32[]{:S(2)}, u32[]{:S(2)}) collective-permute-start(bf16[128,1024]{1,0:T(8,128)(2,1)S(1)} %get-tuple-element.14), channel_id=1, source_target_pairs={{0,0},{1,3},{2,2},{3,1},{4,4},{5,7},{6,6},{7,5},{8,8},{9,11},{10,1... | collective-permute-start | bytes 786440 | tf_op jit(solution)/shard_map/ppermute | solution.py:201
  7.8 11.7 %collective-permute-start.5 = (bf16[128,1024]{1,0:T(8,128)(2,1)S(1)}, bf16[128,1024]{1,0:T(8,128)(2,1)S(1)}, u32[]{:S(2)}, u32[]{:S(2)}) collective-permute-start(bf16[128,1024]{1,0:T(8,128)(2,1)S(1)} %get-tuple-element.15), channel_id=1, source_target_pairs={{0,4},{1,7},{2,6},{3,5},{4,0},{5,3},{6,2},{7,1},{8,12},{9,15},{10,... | collective-permute-start | bytes 786440 | tf_op jit(solution)/shard_map/ppermute | solution.py:201
  9.8 18.3 %collective-permute-start.9 = (bf16[128,1024]{1,0:T(8,128)(2,1)S(1)}, bf16[128,1024]{1,0:T(8,128)(2,1)S(1)}, u32[]{:S(2)}, u32[]{:S(2)}) collective-permute-start(bf16[128,1024]{1,0:T(8,128)(2,1)S(1)} %get-tuple-element.16), channel_id=1, source_target_pairs={{0,12},{1,15},{2,14},{3,13},{4,8},{5,11},{6,10},{7,9},{8,4},{9,7},... | collective-permute-start | bytes 786440 | tf_op jit(solution)/shard_map/ppermute | solution.py:201
  18.4 9.6 %collective-permute-start.6 = (bf16[128,1024]{1,0:T(8,128)(2,1)S(1)}, bf16[128,1024]{1,0:T(8,128)(2,1)S(1)}, u32[]{:S(2)}, u32[]{:S(2)}) collective-permute-start(bf16[128,1024]{1,0:T(8,128)(2,1)S(1)} %join.1.refs_0_), channel_id=1, source_target_pairs={{0,1},{1,0},{2,3},{3,2},{4,5},{5,4},{6,7},{7,6},{8,9},{9,8},{10,11... | collective-permute-start | bytes 786440 | tf_op jit(solution)/shard_map/ppermute | solution.py:185
  19.4 8.7 %collective-permute-start.7 = (bf16[128,1024]{1,0:T(8,128)(2,1)S(1)}, bf16[128,1024]{1,0:T(8,128)(2,1)S(1)}, u32[]{:S(2)}, u32[]{:S(2)}) collective-permute-start(bf16[128,1024]{1,0:T(8,128)(2,1)S(1)} %collective-permute-done.4.refs_1_), channel_id=1, source_target_pairs={{0,1},{1,0},{2,3},{3,2},{4,5},{5,4},{6,7},{7,6},{8,9},{9,8},{10,11... | collective-permute-start | bytes 786440 | tf_op jit(solution)/shard_map/ppermute | solution.py:185
  19.5 9.8 %collective-permute-start.8 = (bf16[128,1024]{1,0:T(8,128)(2,1)S(1)}, bf16[128,1024]{1,0:T(8,128)(2,1)S(1)}, u32[]{:S(2)}, u32[]{:S(2)}) collective-permute-start(bf16[128,1024]{1,0:T(8,128)(2,1)S(1)} %collective-permute-done.5.refs_2_), channel_id=1, source_target_pairs={{0,1},{1,0},{2,3},{3,2},{4,5},{5,4},{6,7},{7,6},{8,9},{9,8},{10,11... | collective-permute-start | bytes 786440 | tf_op jit(solution)/shard_map/ppermute | solution.py:185
  28.1 2.4 %collective-permute-start.10 = (bf16[128,1024]{1,0:T(8,128)(2,1)S(1)}, bf16[128,1024]{1,0:T(8,128)(2,1)S(1)}, u32[]{:S(2)}, u32[]{:S(2)}) collective-permute-start(bf16[128,1024]{1,0:T(8,128)(2,1)S(1)} %collective-permute-done.9.refs_6_), channel_id=1, source_target_pairs={{0,1},{1,0},{2,3},{3,2},{4,5},{5,4},{6,7},{7,6},{8,9},{9,8},{10,11... | collective-permute-start | bytes 786440 | tf_op jit(solution)/shard_map/ppermute | solution.py:185

commit v20 on v8

--- a/solution.py
+++ b/solution.py
@@ -15,7 +15,7 @@
 sharpness = 0.05
 
 EMPTY = 4.0
-TILE = 256
+TILE = 1024
 VMEM = pl.BlockSpec(memory_space=pltpu.VMEM)
 
 
@@ -106,6 +106,11 @@
     rows = first_ref.shape[0]
     out_ref[:rows] = first_ref[...]
     out_ref[rows:] = second_ref[...]
+
+
+def relay_kernel(a_ref, b_ref, c_ref, d_ref):
+    c_ref[...] = a_ref[...]
+    d_ref[...] = b_ref[...]
 
 
 def blocks(rows, starts, size):
@@ -215,7 +220,7 @@
     )
     first_own = across(first_own, first)
 
-    def route_rest(name, halves, steps):
+    def route_rest(name, halves, steps, slot, flops=0):
         return call_kernel(
             name,
             functools.partial(route_rest_kernel, clusters, capacity, halves, steps),
@@ -224,14 +229,17 @@
             other_rows,
             slot,
             other_ids,
+            flops=flops,
         )
 
-    first_other, last_piece = route_rest("route_far", [first], [last])
+    near = route_rest("route_near", [], middle, slot)
+    later_slot, _ = lax.optimization_barrier((slot, near[0]))
+    near = [across(piece, p) for piece, p in zip(near, middle)]
+    near = call_kernel("relay", relay_kernel, [whole] * 2, *near, flops=10**10)
+    first_other, last_piece = route_rest("route_far", [first], [last], later_slot, 10**10)
     first_other, last_piece = across(first_other, first), across(last_piece, last)
-    near = route_rest("route_near", [], middle)
-    near = [across(piece, p) for piece, p in zip(near, middle)]
-
-    first_both = call_kernel("join", join_kernel, whole, first_own, first_other, flops=10**10)
+
+    first_both = call_kernel("join", join_kernel, whole, first_own, first_other, )
     early = [first_both, *near]
     early += [swap_cores(x) for x in early]
     late = [last_piece, swap_cores(last_piece)]

time: 45.5 us -> 44.8 us (0.985)
  waiting for transfers between devices: 18 us -> 4.7 us
  starting transfers between devices: 11 us -> 22.8 us
  blocking collectives: 10.2 us -> 11 us
    ppermute x5, waiting for transfers between devices: 16.9 us -> 3.38 us  [across(): return lax.ppermute(x, ('owner', 'helper', 'sub'), pairs)]
    ppermute x6, starting transfers between devices: 2.6 us -> 14 us  [swap_cores(): return lax.ppermute(x, 'sub', [(i, i ^ 1) for i in range(cores)])]
    all_to_all x1, blocking collectives: 10.2 us -> 11 us  [body_by_chip(): lax.all_to_all(counts, ('owner', 'helper'), split_axis=0, concat_axis=0,...]
    pallas_call x7 -> x8, Pallas kernels: 4.67 us -> 4.75 us  [call_kernel(): pl.pallas_call(kernel, out_shape=out_shape, in_specs=[VMEM] * len(args),...]
  transfers between devices with their start and end apart: 11 -> 11, of which waited for: 4 -> 5; matrix products, arithmetic and copies ran while one was open for 0% -> 0% of each run, Pallas kernels for 6% -> 7%
where the time goes in v20:
time: 44.8 us; the launch traced here: 44.6 us
  starting transfers between devices  22.8 us (51%)
  blocking collectives  11 us (25%)
  Pallas kernels  4.75 us (11%)
  waiting for transfers between devices  4.7 us (10%)
  local copies, waits for them, and re-layouts  1.27 us (3%)
    ppermute x6, starting transfers between devices, swap_cores(): return lax.ppermute(x, 'sub', [(i, i ^ 1) for i in range(cores)])  14 us
    all_to_all x1, blocking collectives, body_by_chip(): lax.all_to_all(counts, ('owner', 'helper'), split_axis=0, concat_axis=0,...  11 us
    ppermute x5, starting transfers between devices, across(): return lax.ppermute(x, ('owner', 'helper', 'sub'), pairs)  8.85 us
    pallas_call x8, Pallas kernels, call_kernel(): pl.pallas_call(kernel, out_shape=out_shape, in_specs=[VMEM] * len(args),...  4.75 us
    ppermute x5, waiting for transfers between devices, across(): return lax.ppermute(x, ('owner', 'helper', 'sub'), pairs)  3.38 us
    ppermute x6, waiting for transfers between devices, swap_cores(): return lax.ppermute(x, 'sub', [(i, i ^ 1) for i in range(cores)])  1.32 us
    unnamed x4, local copies, waits for them, and re-layouts  1.27 us
  transfers between devices with their start and end apart: 11, of which 5 were waited for; matrix products, arithmetic and copies ran while one was open for 0% of the time, Pallas kernels for 7%

profile of v20, /device:TPU:0, one launch (start us, length us, event | category | flops | bytes accessed | tf_op | source)
XLA Modules:
  0.0 44.6 jit_solution(16926695347101816119)
XLA Ops:
  0.0 0.0 copy-start.1
  0.0 0.5 %collective-permute-start.1 = (bf16[256,1024]{1,0:T(8,128)(2,1)}, bf16[256,1024]{1,0:T(8,128)(2,1)S(1)}, u32[]{:S(2)}, u32[]{:S(2)}) collective-permute-start(bf16[256,1024]{1,0:T(8,128)(2,1)} %refs_0_.3), channel_id=1, source_target_pairs={{0,1},{1,0},{2,3},{3,2},{4,5},{5,4},{6,7},{7,6},{8,9},{9,8},{10,11... | collective-permute-start | bytes 1572872 | tf_op jit(solution)/shard_map/ppermute | solution.py:189
  0.5 0.2 copy-done.1
  0.7 0.5 %collective-permute-start.2 = (s32[1,256]{1,0:T(1,128)S(1)}, s32[1,256]{1,0:T(1,128)S(1)}, u32[]{:S(2)}, u32[]{:S(2)}) collective-permute-start(s32[1,256]{1,0:T(1,128)S(1)} %bitcast.2), channel_id=1, source_target_pairs={{0,1},{1,0},{2,3},{3,2},{4,5},{5,4},{6,7},{7,6},{8,9},{9,8},{10,11... | collective-permute-start | bytes 3080 | tf_op jit(solution)/shard_map/ppermute | solution.py:189
  1.1 1.0 %copy-done = bf16[256,1024]{1,0:T(8,128)(2,1)S(1)} copy-done((bf16[256,1024]{1,0:T(8,128)(2,1)S(1)}, bf16[256,1024]{1,0:T(8,128)(2,1)}, u32[]{:S(2)}) %copy-start) | copy-done | bytes 524312
  2.2 0.5 %route_first.1 = (bf16[64,1024]{1,0:T(8,128)(2,1)S(1)}, s32[1,256]{1,0:T(1,128)S(1)}) custom-call(bf16[256,1024]{1,0:T(8,128)(2,1)S(1)} %copy-done, s32[1,256]{1,0:T(1,128)S(1)} %bitcast.3), custom_call_target="tpu_custom_call" | custom-call | tf_op jit(solution)/shard_map/route_first/pallas_call | solution.py:94
  2.6 3.7 %collective-permute-start = (bf16[64,1024]{1,0:T(8,128)(2,1)S(1)}, bf16[64,1024]{1,0:T(8,128)(2,1)S(1)}, u32[]{:S(2)}, u32[]{:S(2)}) collective-permute-start(bf16[64,1024]{1,0:T(8,128)(2,1)S(1)} %get-tuple-element.14), channel_id=1, source_target_pairs={{0,8},{1,11},{2,10},{3,9},{4,12},{5,15},{6,14},{7,13},{8,0},{9,3},... | collective-permute-start | bytes 393224 | tf_op jit(solution)/shard_map/ppermute | solution.py:205
  6.3 0.0 collective-permute-done.2.refs_3_
  6.3 0.0 collective-permute-done.1.refs_1_
  6.3 0.6 %route_near.1 = (bf16[128,1024]{1,0:T(8,128)(2,1)S(1)}, bf16[128,1024]{1,0:T(8,128)(2,1)S(1)}) custom-call(bf16[256,1024]{1,0:T(8,128)(2,1)S(1)} %copy-done, bf16[256,1024]{1,0:T(8,128)(2,1)S(1)} %collective-permute-done.1.refs_1_, s32[1,256]{1,0:T(1,128)S(1)} %get-tuple-element.17.refs_2_.slot_ref, s32[1,256]{1,0:T(1,128)S(1)} %collective-permute-done.2.refs_3_), custom_call_target="tpu_custom_call" | custom-call | tf_op jit(solution)/shard_map/route_near/pallas_call | solution.py:94
  6.9 0.7 %collective-permute-start.4 = (bf16[128,1024]{1,0:T(8,128)(2,1)S(1)}, bf16[128,1024]{1,0:T(8,128)(2,1)S(1)}, u32[]{:S(2)}, u32[]{:S(2)}) collective-permute-start(bf16[128,1024]{1,0:T(8,128)(2,1)S(1)} %get-tuple-element.16), channel_id=1, source_target_pairs={{0,0},{1,3},{2,2},{3,1},{4,4},{5,7},{6,6},{7,5},{8,8},{9,11},{10,1... | collective-permute-start | bytes 786440 | tf_op jit(solution)/shard_map/ppermute | solution.py:205
  7.6 1.6 %collective-permute-start.5 = (bf16[128,1024]{1,0:T(8,128)(2,1)S(1)}, bf16[128,1024]{1,0:T(8,128)(2,1)S(1)}, u32[]{:S(2)}, u32[]{:S(2)}) collective-permute-start(bf16[128,1024]{1,0:T(8,128)(2,1)S(1)} %get-tuple-element.19), channel_id=1, source_target_pairs={{0,4},{1,7},{2,6},{3,5},{4,0},{5,3},{6,2},{7,1},{8,12},{9,15},{10,... | collective-permute-start | bytes 786440 | tf_op jit(solution)/shard_map/ppermute | solution.py:205
  9.2 0.6 %route_far.1 = (bf16[64,1024]{1,0:T(8,128)(2,1)S(1)}, bf16[128,1024]{1,0:T(8,128)(2,1)S(1)}) custom-call(bf16[256,1024]{1,0:T(8,128)(2,1)S(1)} %copy-done, bf16[256,1024]{1,0:T(8,128)(2,1)S(1)} %collective-permute-done.1.refs_1_, s32[1,256]{1,0:T(1,128)S(1)} %get-tuple-element.17.refs_2_.slot_ref, s32[1,256]{1,0:T(1,128)S(1)} %collective-permute-done.2.refs_3_), custom_call_target="tpu_custom_call" | custom-call | flops 10000000000 | tf_op jit(solution)/shard_map/route_far/pallas_call | solution.py:94
  9.8 0.4 collective-permute-start.3
  10.2 2.5 %collective-permute-start.9 = (bf16[128,1024]{1,0:T(8,128)(2,1)S(1)}, bf16[128,1024]{1,0:T(8,128)(2,1)S(1)}, u32[]{:S(2)}, u32[]{:S(2)}) collective-permute-start(bf16[128,1024]{1,0:T(8,128)(2,1)S(1)} %get-tuple-element.22), channel_id=1, source_target_pairs={{0,12},{1,15},{2,14},{3,13},{4,8},{5,11},{6,10},{7,9},{8,4},{9,7},... | collective-permute-start | bytes 786440 | tf_op jit(solution)/shard_map/ppermute | solution.py:205
  12.7 0.1 collective-permute-done.first_ref
  12.8 3.3 %collective-permute-done.3.second_ref = bf16[64,1024]{1,0:T(8,128)(2,1)S(1)} collective-permute-done((bf16[64,1024]{1,0:T(8,128)(2,1)S(1)}, bf16[64,1024]{1,0:T(8,128)(2,1)S(1)}, u32[]{:S(2)}, u32[]{:S(2)}) %collective-permute-start.3) | collective-permute-done | bytes 131104 | tf_op jit(solution)/shard_map/ppermute | solution.py:205
  16.1 12.4 %collective-permute-start.6 = (bf16[128,1024]{1,0:T(8,128)(2,1)S(1)}, bf16[128,1024]{1,0:T(8,128)(2,1)S(1)}, u32[]{:S(2)}, u32[]{:S(2)}) collective-permute-start(bf16[128,1024]{1,0:T(8,128)(2,1)S(1)} %join.1.refs_0_), channel_id=1, source_target_pairs={{0,1},{1,0},{2,3},{3,2},{4,5},{5,4},{6,7},{7,6},{8,9},{9,8},{10,11... | collective-permute-start | bytes 786440 | tf_op jit(solution)/shard_map/ppermute | solution.py:189
  28.5 0.0 collective-permute-done.5.b_ref
  28.5 0.0 collective-permute-done.4.a_ref
  28.6 0.1 collective-permute-start.7
  28.7 0.5 %collective-permute-start.8 = (bf16[128,1024]{1,0:T(8,128)(2,1)S(1)}, bf16[128,1024]{1,0:T(8,128)(2,1)S(1)}, u32[]{:S(2)}, u32[]{:S(2)}) collective-permute-start(bf16[128,1024]{1,0:T(8,128)(2,1)S(1)} %get-tuple-element.21.refs_2_), channel_id=1, source_target_pairs={{0,1},{1,0},{2,3},{3,2},{4,5},{5,4},{6,7},{7,6},{8,9},{9,8},{10,11... | collective-permute-start | bytes 786440 | tf_op jit(solution)/shard_map/ppermute | solution.py:189
  29.1 0.0 collective-permute-done.9.refs_6_
  29.1 0.1 collective-permute-start.10
  29.2 0.5 %collective-permute-done.6.refs_3_ = bf16[128,1024]{1,0:T(8,128)(2,1)S(1)} collective-permute-done((bf16[128,1024]{1,0:T(8,128)(2,1)S(1)}, bf16[128,1024]{1,0:T(8,128)(2,1)S(1)}, u32[]{:S(2)}, u32[]{:S(2)}) %collective-permute-start.6) | collective-permute-done | bytes 262176 | tf_op jit(solution)/shard_map/ppermute | solution.py:189
  29.7 0.5 %collective-permute-done.7.refs_4_ = bf16[128,1024]{1,0:T(8,128)(2,1)S(1)} collective-permute-done((bf16[128,1024]{1,0:T(8,128)(2,1)S(1)}, bf16[128,1024]{1,0:T(8,128)(2,1)S(1)}, u32[]{:S(2)}, u32[]{:S(2)}) %collective-permute-start.7) | collective-permute-done | bytes 262176 | tf_op jit(solution)/shard_map/ppermute | solution.py:189
  30.2 0.4 collective-permute-done.8.refs_5_
  30.5 1.2 %count.1.refs_8_ = f32[1,384]{1,0:T(1,128)S(1)} custom-call(bf16[128,1024]{1,0:T(8,128)(2,1)S(1)} %join.1.refs_0_, bf16[128,1024]{1,0:T(8,128)(2,1)S(1)} %get-tuple-element.20.refs_1_, bf16[128,1024]{1,0:T(8,128)(2,1)S(1)} %get-tuple-element.21.refs_2_, bf16[128,1024]{1,0:T(8,128)(2,1)S(1)} %collective-permute-done.6.refs_3_, ...), custom_call_target="tpu_custom_call" | custom-call | tf_op jit(solution)/shard_map/count/pallas_call | solution.py:94
  31.7 0.0 collective-permute-done.10.refs_7_
  31.7 1.1 %finish.1 = f32[8,1,64]{2,1,0:T(1,128)S(1)} custom-call(bf16[128,1024]{1,0:T(8,128)(2,1)S(1)} %join.1.refs_0_, bf16[128,1024]{1,0:T(8,128)(2,1)S(1)} %get-tuple-element.20.refs_1_, bf16[128,1024]{1,0:T(8,128)(2,1)S(1)} %get-tuple-element.21.refs_2_, bf16[128,1024]{1,0:T(8,128)(2,1)S(1)} %collective-permute-done.6.refs_3_, ...), custom_call_target="tpu_custom_call" | custom-call | tf_op jit(solution)/shard_map/finish/pallas_call | solution.py:94
  32.9 11.0 %all_to_all.5.counts_ref = f32[8,1,64]{2,1,0:T(1,128)S(1)} all-to-all(f32[8,1,64]{2,1,0:T(1,128)S(1)} %finish.1), channel_id=1, replica_groups=mesh['groups'=2,'owner'=4,'helper'=2,'sub'=2] {'owner','helper'}, dimensions={0} | all-to-all | bytes 4096 | tf_op jit(solution)/shard_map/all_to_all | solution.py:268
  43.9 0.7 %select.1 = f32[1,256]{1,0:T(1,128)} custom-call(f32[8,1,64]{2,1,0:T(1,128)S(1)} %all_to_all.5.counts_ref, s32[1,256]{1,0:T(1,128)S(1)} %get-tuple-element.17.refs_2_.slot_ref), custom_call_target="tpu_custom_call" | custom-call | tf_op jit(solution)/shard_map/select/pallas_call | solution.py:94
  (3 shorter events, 0.1 us)
Async XLA Ops:
  0.0 0.7 %copy-start.1 = (s32[256]{0:T(256)S(1)}, s32[256]{0:T(256)}, u32[]{:S(2)}) copy-start(s32[256]{0:T(256)} %param.3) | copy-start | bytes 3076
  0.0 6.3 %collective-permute-start.1 = (bf16[256,1024]{1,0:T(8,128)(2,1)}, bf16[256,1024]{1,0:T(8,128)(2,1)S(1)}, u32[]{:S(2)}, u32[]{:S(2)}) collective-permute-start(bf16[256,1024]{1,0:T(8,128)(2,1)} %refs_0_.3), channel_id=1, source_target_pairs={{0,1},{1,0},{2,3},{3,2},{4,5},{5,4},{6,7},{7,6},{8,9},{9,8},{10,11... | collective-permute-start | bytes 1572872 | tf_op jit(solution)/shard_map/ppermute | solution.py:189
  0.7 5.6 %collective-permute-start.2 = (s32[1,256]{1,0:T(1,128)S(1)}, s32[1,256]{1,0:T(1,128)S(1)}, u32[]{:S(2)}, u32[]{:S(2)}) collective-permute-start(s32[1,256]{1,0:T(1,128)S(1)} %bitcast.2), channel_id=1, source_target_pairs={{0,1},{1,0},{2,3},{3,2},{4,5},{5,4},{6,7},{7,6},{8,9},{9,8},{10,11... | collective-permute-start | bytes 3080 | tf_op jit(solution)/shard_map/ppermute | solution.py:189
  1.1 1.0 %copy-start = (bf16[256,1024]{1,0:T(8,128)(2,1)S(1)}, bf16[256,1024]{1,0:T(8,128)(2,1)}, u32[]{:S(2)}) copy-start(bf16[256,1024]{1,0:T(8,128)(2,1)} %refs_0_.3) | copy-start | bytes 1572868
  2.6 10.2 %collective-permute-start = (bf16[64,1024]{1,0:T(8,128)(2,1)S(1)}, bf16[64,1024]{1,0:T(8,128)(2,1)S(1)}, u32[]{:S(2)}, u32[]{:S(2)}) collective-permute-start(bf16[64,1024]{1,0:T(8,128)(2,1)S(1)} %get-tuple-element.14), channel_id=1, source_target_pairs={{0,8},{1,11},{2,10},{3,9},{4,12},{5,15},{6,14},{7,13},{8,0},{9,3},... | collective-permute-start | bytes 393224 | tf_op jit(solution)/shard_map/ppermute | solution.py:205
  6.9 21.6 %collective-permute-start.4 = (bf16[128,1024]{1,0:T(8,128)(2,1)S(1)}, bf16[128,1024]{1,0:T(8,128)(2,1)S(1)}, u32[]{:S(2)}, u32[]{:S(2)}) collective-permute-start(bf16[128,1024]{1,0:T(8,128)(2,1)S(1)} %get-tuple-element.16), channel_id=1, source_target_pairs={{0,0},{1,3},{2,2},{3,1},{4,4},{5,7},{6,6},{7,5},{8,8},{9,11},{10,1... | collective-permute-start | bytes 786440 | tf_op jit(solution)/shard_map/ppermute | solution.py:205
  7.6 20.9 %collective-permute-start.5 = (bf16[128,1024]{1,0:T(8,128)(2,1)S(1)}, bf16[128,1024]{1,0:T(8,128)(2,1)S(1)}, u32[]{:S(2)}, u32[]{:S(2)}) collective-permute-start(bf16[128,1024]{1,0:T(8,128)(2,1)S(1)} %get-tuple-element.19), channel_id=1, source_target_pairs={{0,4},{1,7},{2,6},{3,5},{4,0},{5,3},{6,2},{7,1},{8,12},{9,15},{10,... | collective-permute-start | bytes 786440 | tf_op jit(solution)/shard_map/ppermute | solution.py:205
  9.8 6.2 %collective-permute-start.3 = (bf16[64,1024]{1,0:T(8,128)(2,1)S(1)}, bf16[64,1024]{1,0:T(8,128)(2,1)S(1)}, u32[]{:S(2)}, u32[]{:S(2)}) collective-permute-start(bf16[64,1024]{1,0:T(8,128)(2,1)S(1)} %get-tuple-element.18), channel_id=1, source_target_pairs={{0,8},{1,11},{2,10},{3,9},{4,12},{5,15},{6,14},{7,13},{8,0},{9,3},... | collective-permute-start | bytes 393224 | tf_op jit(solution)/shard_map/ppermute | solution.py:205
  10.2 18.9 %collective-permute-start.9 = (bf16[128,1024]{1,0:T(8,128)(2,1)S(1)}, bf16[128,1024]{1,0:T(8,128)(2,1)S(1)}, u32[]{:S(2)}, u32[]{:S(2)}) collective-permute-start(bf16[128,1024]{1,0:T(8,128)(2,1)S(1)} %get-tuple-element.22), channel_id=1, source_target_pairs={{0,12},{1,15},{2,14},{3,13},{4,8},{5,11},{6,10},{7,9},{8,4},{9,7},... | collective-permute-start | bytes 786440 | tf_op jit(solution)/shard_map/ppermute | solution.py:205
  16.1 13.6 %collective-permute-start.6 = (bf16[128,1024]{1,0:T(8,128)(2,1)S(1)}, bf16[128,1024]{1,0:T(8,128)(2,1)S(1)}, u32[]{:S(2)}, u32[]{:S(2)}) collective-permute-start(bf16[128,1024]{1,0:T(8,128)(2,1)S(1)} %join.1.refs_0_), channel_id=1, source_target_pairs={{0,1},{1,0},{2,3},{3,2},{4,5},{5,4},{6,7},{7,6},{8,9},{9,8},{10,11... | collective-permute-start | bytes 786440 | tf_op jit(solution)/shard_map/ppermute | solution.py:189
  28.6 1.6 %collective-permute-start.7 = (bf16[128,1024]{1,0:T(8,128)(2,1)S(1)}, bf16[128,1024]{1,0:T(8,128)(2,1)S(1)}, u32[]{:S(2)}, u32[]{:S(2)}) collective-permute-start(bf16[128,1024]{1,0:T(8,128)(2,1)S(1)} %get-tuple-element.20.refs_1_), channel_id=1, source_target_pairs={{0,1},{1,0},{2,3},{3,2},{4,5},{5,4},{6,7},{7,6},{8,9},{9,8},{10,11... | collective-permute-start | bytes 786440 | tf_op jit(solution)/shard_map/ppermute | solution.py:189
  28.7 1.9 %collective-permute-start.8 = (bf16[128,1024]{1,0:T(8,128)(2,1)S(1)}, bf16[128,1024]{1,0:T(8,128)(2,1)S(1)}, u32[]{:S(2)}, u32[]{:S(2)}) collective-permute-start(bf16[128,1024]{1,0:T(8,128)(2,1)S(1)} %get-tuple-element.21.refs_2_), channel_id=1, source_target_pairs={{0,1},{1,0},{2,3},{3,2},{4,5},{5,4},{6,7},{7,6},{8,9},{9,8},{10,11... | collective-permute-start | bytes 786440 | tf_op jit(solution)/shard_map/ppermute | solution.py:189
  29.1 2.6 %collective-permute-start.10 = (bf16[128,1024]{1,0:T(8,128)(2,1)S(1)}, bf16[128,1024]{1,0:T(8,128)(2,1)S(1)}, u32[]{:S(2)}, u32[]{:S(2)}) collective-permute-start(bf16[128,1024]{1,0:T(8,128)(2,1)S(1)} %collective-permute-done.9.refs_6_), channel_id=1, source_target_pairs={{0,1},{1,0},{2,3},{3,2},{4,5},{5,4},{6,7},{7,6},{8,9},{9,8},{10,11... | collective-permute-start | bytes 786440 | tf_op jit(solution)/shard_map/ppermute | solution.py:189

commit v21 on v18

--- a/solution.py
+++ b/solution.py
@@ -152,12 +152,13 @@
     late_total = count_against(early, late_own, [], size) + count_against(
         late, late_own, late_starts, size
     )
+    count_ref[...] = jnp.zeros_like(count_ref)
     for k, place in enumerate(places()):
         source, j = (total, k) if k < len(starts) else (late_total, k - len(starts))
         count_ref[pl.ds(place, 1), 0, :] = source[:, j * size : (j + 1) * size]
 
 
-def select_kernel(capacity, counts_ref, slot_ref, out_ref):
+def select_kernel(clusters, capacity, counts_ref, slot_ref, out_ref):
     counts = counts_ref[:, 0, :]
     slot = slot_ref[...]
     doc_count = slot.shape[1]
@@ -167,13 +168,15 @@
     by_block = jnp.dot(
         counts, hot, precision=lax.Precision.HIGHEST, preferred_element_type=jnp.float32
     )
-    chosen = lax.broadcasted_iota(jnp.int32, by_block.shape, 0) == block
+    cores = counts.shape[0] // clusters
+    core = lax.axis_index("sub") if cores > 1 else 0
+    chosen = lax.broadcasted_iota(jnp.int32, by_block.shape, 0) == block * cores + core
     out_ref[...] = jnp.sum(jnp.where(chosen, by_block, 0.0), axis=0, keepdims=True)
 
 
-def select(counts, slot, capacity):
+def select(counts, slot, clusters, capacity):
     out_shape = jax.ShapeDtypeStruct(slot.shape, jnp.float32)
-    kernel = functools.partial(select_kernel, capacity)
+    kernel = functools.partial(select_kernel, clusters, capacity)
     return call_kernel("select", kernel, out_shape, counts, slot, limit=8 * 2**20)[0]
 
 
@@ -236,22 +239,23 @@
 
     def places():
         chip, core = chip_index(), lax.axis_index("sub")
-        return (
-            [chip ^ (p * cores + core) for p in (first, *middle)]
-            + [chip ^ (p * cores + 1 - core) for p in (first, *middle)]
-            + [chip ^ (last * cores + core), chip ^ (last * cores + 1 - core)]
-        )
+        own = [chip ^ (p * cores + core) for p in (first, *middle, last)]
+        other = [chip ^ (p * cores + 1 - core) for p in (first, *middle, last)]
+        chips = own[:-1] + other[:-1] + [own[-1], other[-1]]
+        return [there * cores + core for there in chips]
 
     counts = call_kernel(
         "finish",
         functools.partial(finish_kernel, starts, len(late), late_starts, places),
-        jax.ShapeDtypeStruct((clusters, 1, capacity), jnp.float32),
+        jax.ShapeDtypeStruct((clusters * cores, 1, capacity), jnp.float32),
         *early,
         *late,
         soft_counts(early, starts, capacity),
     )
-    back = lax.all_to_all(counts, ("owner", "helper"), split_axis=0, concat_axis=0, tiled=True)
-    return select(back, slot, capacity)
+    back = lax.all_to_all(
+        counts, ("owner", "helper", "sub"), split_axis=0, concat_axis=0, tiled=True
+    )
+    return select(back, slot, clusters, capacity)
 
 
 def body_by_owner(embeddings, cluster_id):
@@ -288,7 +292,7 @@
     kept, given = counts[0], partner(counts[1])
     counts = jnp.where(mine == 0, jnp.stack([kept, given], 1), jnp.stack([given, kept], 1))
     back = lax.all_to_all(counts, "owner", split_axis=0, concat_axis=0, tiled=True)
-    return select(back.reshape(clusters, 1, capacity), slot, capacity)
+    return select(back.reshape(clusters, 1, capacity), slot, clusters, capacity)
 
 
 def solution(mesh):

time: 44.8 us -> 44.9 us (level)
  no operation moved by 1% of the time
where the time goes in v21:
time: 44.9 us; the launch traced here: 44.7 us
  starting transfers between devices  19.4 us (43%)
  blocking collectives  12.4 us (28%)
  waiting for transfers between devices  7.34 us (16%)
  Pallas kernels  4.26 us (9%)
  local copies, waits for them, and re-layouts  1.27 us (3%)
    all_to_all x1, blocking collectives, body_by_chip(): lax.all_to_all(counts, ('owner', 'helper', 'sub'), split_axis=0, concat_a...  12.4 us
    ppermute x6, starting transfers between devices, swap_cores(): return lax.ppermute(x, 'sub', [(i, i ^ 1) for i in range(cores)])  10.5 us
    ppermute x5, starting transfers between devices, across(): return lax.ppermute(x, ('owner', 'helper', 'sub'), pairs)  8.83 us
    ppermute x5, waiting for transfers between devices, across(): return lax.ppermute(x, ('owner', 'helper', 'sub'), pairs)  6.19 us
    pallas_call x6, Pallas kernels, call_kernel(): pl.pallas_call(kernel, out_shape=out_shape, in_specs=[VMEM] * len(args),...  4.26 us
    unnamed x4, local copies, waits for them, and re-layouts  1.27 us
    ppermute x6, waiting for transfers between devices, swap_cores(): return lax.ppermute(x, 'sub', [(i, i ^ 1) for i in range(cores)])  1.15 us
  transfers between devices with their start and end apart: 11, of which 3 were waited for; matrix products, arithmetic and copies ran while one was open for 0% of the time, Pallas kernels for 5%

profile of v21, /device:TPU:0, one launch (start us, length us, event | category | flops | bytes accessed | tf_op | source)
XLA Modules:
  0.0 44.7 jit_solution(14979598203336291477)
XLA Ops:
  0.0 0.0 copy-start.1
  0.0 0.5 %collective-permute-start.1 = (bf16[256,1024]{1,0:T(8,128)(2,1)}, bf16[256,1024]{1,0:T(8,128)(2,1)S(1)}, u32[]{:S(2)}, u32[]{:S(2)}) collective-permute-start(bf16[256,1024]{1,0:T(8,128)(2,1)} %refs_0_.1), channel_id=1, source_target_pairs={{0,1},{1,0},{2,3},{3,2},{4,5},{5,4},{6,7},{7,6},{8,9},{9,8},{10,11... | collective-permute-start | bytes 1572872 | tf_op jit(solution)/shard_map/ppermute | solution.py:185
  0.5 0.2 copy-done.1
  0.7 0.5 %collective-permute-start.2 = (s32[1,256]{1,0:T(1,128)S(1)}, s32[1,256]{1,0:T(1,128)S(1)}, u32[]{:S(2)}, u32[]{:S(2)}) collective-permute-start(s32[1,256]{1,0:T(1,128)S(1)} %bitcast.2), channel_id=1, source_target_pairs={{0,1},{1,0},{2,3},{3,2},{4,5},{5,4},{6,7},{7,6},{8,9},{9,8},{10,11... | collective-permute-start | bytes 3080 | tf_op jit(solution)/shard_map/ppermute | solution.py:185
  1.1 0.0 copy-start
  1.1 1.0 %copy-done = bf16[256,1024]{1,0:T(8,128)(2,1)S(1)} copy-done((bf16[256,1024]{1,0:T(8,128)(2,1)S(1)}, bf16[256,1024]{1,0:T(8,128)(2,1)}, u32[]{:S(2)}) %copy-start) | copy-done | bytes 524312
  2.2 0.5 %route_first.1 = (bf16[64,1024]{1,0:T(8,128)(2,1)S(1)}, s32[1,256]{1,0:T(1,128)S(1)}) custom-call(bf16[256,1024]{1,0:T(8,128)(2,1)S(1)} %copy-done, s32[1,256]{1,0:T(1,128)S(1)} %bitcast.3), custom_call_target="tpu_custom_call" | custom-call | tf_op jit(solution)/shard_map/route_first/pallas_call | solution.py:92
  2.6 3.7 %collective-permute-start = (bf16[64,1024]{1,0:T(8,128)(2,1)S(1)}, bf16[64,1024]{1,0:T(8,128)(2,1)S(1)}, u32[]{:S(2)}, u32[]{:S(2)}) collective-permute-start(bf16[64,1024]{1,0:T(8,128)(2,1)S(1)} %get-tuple-element.11), channel_id=1, source_target_pairs={{0,8},{1,11},{2,10},{3,9},{4,12},{5,15},{6,14},{7,13},{8,0},{9,3},... | collective-permute-start | bytes 393224 | tf_op jit(solution)/shard_map/ppermute | solution.py:201
  6.3 0.0 collective-permute-done.2.refs_3_
  6.3 0.0 collective-permute-done.1.refs_1_
  6.3 0.7 %route_rest.1 = (bf16[64,1024]{1,0:T(8,128)(2,1)S(1)}, bf16[128,1024]{1,0:T(8,128)(2,1)S(1)}, bf16[128,1024]{1,0:T(8,128)(2,1)S(1)}, bf16[128,1024]{1,0:T(8,128)(2,1)S(1)}) custom-call(bf16[256,1024]{1,0:T(8,128)(2,1)S(1)} %copy-done, bf16[256,1024]{1,0:T(8,128)(2,1)S(1)} %collective-permute-done.1.refs_1_, s32[1,256]{1,0:T(1,128)S(1)} %get-tuple-element.12.refs_2_.slot_ref, ...), custom_call_target="tpu_custom_call" | custom-call | tf_op jit(solution)/shard_map/route_rest/pallas_call | solution.py:92
  7.0 0.1 collective-permute-start.3
  7.1 0.7 %collective-permute-start.4 = (bf16[128,1024]{1,0:T(8,128)(2,1)S(1)}, bf16[128,1024]{1,0:T(8,128)(2,1)S(1)}, u32[]{:S(2)}, u32[]{:S(2)}) collective-permute-start(bf16[128,1024]{1,0:T(8,128)(2,1)S(1)} %get-tuple-element.14), channel_id=1, source_target_pairs={{0,0},{1,3},{2,2},{3,1},{4,4},{5,7},{6,6},{7,5},{8,8},{9,11},{10,1... | collective-permute-start | bytes 786440 | tf_op jit(solution)/shard_map/ppermute | solution.py:201
  7.8 1.9 %collective-permute-start.5 = (bf16[128,1024]{1,0:T(8,128)(2,1)S(1)}, bf16[128,1024]{1,0:T(8,128)(2,1)S(1)}, u32[]{:S(2)}, u32[]{:S(2)}) collective-permute-start(bf16[128,1024]{1,0:T(8,128)(2,1)S(1)} %get-tuple-element.15), channel_id=1, source_target_pairs={{0,4},{1,7},{2,6},{3,5},{4,0},{5,3},{6,2},{7,1},{8,12},{9,15},{10,... | collective-permute-start | bytes 786440 | tf_op jit(solution)/shard_map/ppermute | solution.py:201
  9.8 2.5 %collective-permute-start.9 = (bf16[128,1024]{1,0:T(8,128)(2,1)S(1)}, bf16[128,1024]{1,0:T(8,128)(2,1)S(1)}, u32[]{:S(2)}, u32[]{:S(2)}) collective-permute-start(bf16[128,1024]{1,0:T(8,128)(2,1)S(1)} %get-tuple-element.16), channel_id=1, source_target_pairs={{0,12},{1,15},{2,14},{3,13},{4,8},{5,11},{6,10},{7,9},{8,4},{9,7},... | collective-permute-start | bytes 786440 | tf_op jit(solution)/shard_map/ppermute | solution.py:201
  12.2 3.2 %collective-permute-done.first_ref = bf16[64,1024]{1,0:T(8,128)(2,1)S(1)} collective-permute-done((bf16[64,1024]{1,0:T(8,128)(2,1)S(1)}, bf16[64,1024]{1,0:T(8,128)(2,1)S(1)}, u32[]{:S(2)}, u32[]{:S(2)}) %collective-permute-start) | collective-permute-done | bytes 131104 | tf_op jit(solution)/shard_map/ppermute | solution.py:201
  15.4 3.0 %collective-permute-done.3.second_ref = bf16[64,1024]{1,0:T(8,128)(2,1)S(1)} collective-permute-done((bf16[64,1024]{1,0:T(8,128)(2,1)S(1)}, bf16[64,1024]{1,0:T(8,128)(2,1)S(1)}, u32[]{:S(2)}, u32[]{:S(2)}) %collective-permute-start.3) | collective-permute-done | bytes 131104 | tf_op jit(solution)/shard_map/ppermute | solution.py:201
  18.4 0.9 %collective-permute-start.6 = (bf16[128,1024]{1,0:T(8,128)(2,1)S(1)}, bf16[128,1024]{1,0:T(8,128)(2,1)S(1)}, u32[]{:S(2)}, u32[]{:S(2)}) collective-permute-start(bf16[128,1024]{1,0:T(8,128)(2,1)S(1)} %join.1.refs_0_), channel_id=1, source_target_pairs={{0,1},{1,0},{2,3},{3,2},{4,5},{5,4},{6,7},{7,6},{8,9},{9,8},{10,11... | collective-permute-start | bytes 786440 | tf_op jit(solution)/shard_map/ppermute | solution.py:185
  19.4 0.0 collective-permute-done.4.refs_1_
  19.4 0.1 collective-permute-start.7
  19.5 0.0 collective-permute-done.5.refs_2_
  19.5 8.6 %collective-permute-start.8 = (bf16[128,1024]{1,0:T(8,128)(2,1)S(1)}, bf16[128,1024]{1,0:T(8,128)(2,1)S(1)}, u32[]{:S(2)}, u32[]{:S(2)}) collective-permute-start(bf16[128,1024]{1,0:T(8,128)(2,1)S(1)} %collective-permute-done.5.refs_2_), channel_id=1, source_target_pairs={{0,1},{1,0},{2,3},{3,2},{4,5},{5,4},{6,7},{7,6},{8,9},{9,8},{10,11... | collective-permute-start | bytes 786440 | tf_op jit(solution)/shard_map/ppermute | solution.py:185
  28.1 0.0 collective-permute-done.9.refs_6_
  28.1 0.0 collective-permute-start.10
  28.1 0.0 collective-permute-done.6.refs_3_
  28.1 0.0 collective-permute-done.7.refs_4_
  28.1 1.1 %collective-permute-done.8.refs_5_ = bf16[128,1024]{1,0:T(8,128)(2,1)S(1)} collective-permute-done((bf16[128,1024]{1,0:T(8,128)(2,1)S(1)}, bf16[128,1024]{1,0:T(8,128)(2,1)S(1)}, u32[]{:S(2)}, u32[]{:S(2)}) %collective-permute-start.8) | collective-permute-done | bytes 262176 | tf_op jit(solution)/shard_map/ppermute | solution.py:185
  29.2 1.2 %count.1.refs_8_ = f32[1,384]{1,0:T(1,128)S(1)} custom-call(bf16[128,1024]{1,0:T(8,128)(2,1)S(1)} %join.1.refs_0_, bf16[128,1024]{1,0:T(8,128)(2,1)S(1)} %collective-permute-done.4.refs_1_, bf16[128,1024]{1,0:T(8,128)(2,1)S(1)} %collective-permute-done.5.refs_2_, bf16[128,1024]{1,0:T(8,128)(2,1)S(1)} %collective-permute-done.6.refs_3_, ...), custom_call_target="tpu_custom_call" | custom-call | tf_op jit(solution)/shard_map/count/pallas_call | solution.py:92
  30.4 0.0 collective-permute-done.10.refs_7_
  30.4 1.1 %finish.1 = f32[16,1,64]{2,1,0:T(1,128)S(1)} custom-call(bf16[128,1024]{1,0:T(8,128)(2,1)S(1)} %join.1.refs_0_, bf16[128,1024]{1,0:T(8,128)(2,1)S(1)} %collective-permute-done.4.refs_1_, bf16[128,1024]{1,0:T(8,128)(2,1)S(1)} %collective-permute-done.5.refs_2_, bf16[128,1024]{1,0:T(8,128)(2,1)S(1)} %collective-permute-done.6.refs_3_, ...), custom_call_target="tpu_custom_call" | custom-call | tf_op jit(solution)/shard_map/finish/pallas_call | solution.py:92
  31.6 12.4 %all_to_all.5.counts_ref = f32[16,1,64]{2,1,0:T(1,128)S(1)} all-to-all(f32[16,1,64]{2,1,0:T(1,128)S(1)} %finish.1), channel_id=1, replica_groups=mesh['groups'=2,'owner'=4,'helper'=2,'sub'=2] {'owner','helper','sub'}, dimensions={0} | all-to-all | bytes 8192 | tf_op jit(solution)/shard_map/all_to_all | solution.py:255
  43.9 0.7 %select.1 = f32[1,256]{1,0:T(1,128)} custom-call(f32[16,1,64]{2,1,0:T(1,128)S(1)} %all_to_all.5.counts_ref, s32[1,256]{1,0:T(1,128)S(1)} %get-tuple-element.12.refs_2_.slot_ref), custom_call_target="tpu_custom_call" | custom-call | tf_op jit(solution)/shard_map/select/pallas_call | solution.py:92
  (1 shorter events, 0.0 us)
Async XLA Ops:
  0.0 0.7 %copy-start.1 = (s32[256]{0:T(256)S(1)}, s32[256]{0:T(256)}, u32[]{:S(2)}) copy-start(s32[256]{0:T(256)} %param.3) | copy-start | bytes 3076
  0.0 6.3 %collective-permute-start.1 = (bf16[256,1024]{1,0:T(8,128)(2,1)}, bf16[256,1024]{1,0:T(8,128)(2,1)S(1)}, u32[]{:S(2)}, u32[]{:S(2)}) collective-permute-start(bf16[256,1024]{1,0:T(8,128)(2,1)} %refs_0_.1), channel_id=1, source_target_pairs={{0,1},{1,0},{2,3},{3,2},{4,5},{5,4},{6,7},{7,6},{8,9},{9,8},{10,11... | collective-permute-start | bytes 1572872 | tf_op jit(solution)/shard_map/ppermute | solution.py:185
  0.7 5.6 %collective-permute-start.2 = (s32[1,256]{1,0:T(1,128)S(1)}, s32[1,256]{1,0:T(1,128)S(1)}, u32[]{:S(2)}, u32[]{:S(2)}) collective-permute-start(s32[1,256]{1,0:T(1,128)S(1)} %bitcast.2), channel_id=1, source_target_pairs={{0,1},{1,0},{2,3},{3,2},{4,5},{5,4},{6,7},{7,6},{8,9},{9,8},{10,11... | collective-permute-start | bytes 3080 | tf_op jit(solution)/shard_map/ppermute | solution.py:185
  1.1 1.0 %copy-start = (bf16[256,1024]{1,0:T(8,128)(2,1)S(1)}, bf16[256,1024]{1,0:T(8,128)(2,1)}, u32[]{:S(2)}) copy-start(bf16[256,1024]{1,0:T(8,128)(2,1)} %refs_0_.1) | copy-start | bytes 1572868
  2.6 12.8 %collective-permute-start = (bf16[64,1024]{1,0:T(8,128)(2,1)S(1)}, bf16[64,1024]{1,0:T(8,128)(2,1)S(1)}, u32[]{:S(2)}, u32[]{:S(2)}) collective-permute-start(bf16[64,1024]{1,0:T(8,128)(2,1)S(1)} %get-tuple-element.11), channel_id=1, source_target_pairs={{0,8},{1,11},{2,10},{3,9},{4,12},{5,15},{6,14},{7,13},{8,0},{9,3},... | collective-permute-start | bytes 393224 | tf_op jit(solution)/shard_map/ppermute | solution.py:201
  7.0 11.4 %collective-permute-start.3 = (bf16[64,1024]{1,0:T(8,128)(2,1)S(1)}, bf16[64,1024]{1,0:T(8,128)(2,1)S(1)}, u32[]{:S(2)}, u32[]{:S(2)}) collective-permute-start(bf16[64,1024]{1,0:T(8,128)(2,1)S(1)} %get-tuple-element.13), channel_id=1, source_target_pairs={{0,8},{1,11},{2,10},{3,9},{4,12},{5,15},{6,14},{7,13},{8,0},{9,3},... | collective-permute-start | bytes 393224 | tf_op jit(solution)/shard_map/ppermute | solution.py:201
  7.1 12.3 %collective-permute-start.4 = (bf16[128,1024]{1,0:T(8,128)(2,1)S(1)}, bf16[128,1024]{1,0:T(8,128)(2,1)S(1)}, u32[]{:S(2)}, u32[]{:S(2)}) collective-permute-start(bf16[128,1024]{1,0:T(8,128)(2,1)S(1)} %get-tuple-element.14), channel_id=1, source_target_pairs={{0,0},{1,3},{2,2},{3,1},{4,4},{5,7},{6,6},{7,5},{8,8},{9,11},{10,1... | collective-permute-start | bytes 786440 | tf_op jit(solution)/shard_map/ppermute | solution.py:201
  7.8 11.7 %collective-permute-start.5 = (bf16[128,1024]{1,0:T(8,128)(2,1)S(1)}, bf16[128,1024]{1,0:T(8,128)(2,1)S(1)}, u32[]{:S(2)}, u32[]{:S(2)}) collective-permute-start(bf16[128,1024]{1,0:T(8,128)(2,1)S(1)} %get-tuple-element.15), channel_id=1, source_target_pairs={{0,4},{1,7},{2,6},{3,5},{4,0},{5,3},{6,2},{7,1},{8,12},{9,15},{10,... | collective-permute-start | bytes 786440 | tf_op jit(solution)/shard_map/ppermute | solution.py:201
  9.8 18.3 %collective-permute-start.9 = (bf16[128,1024]{1,0:T(8,128)(2,1)S(1)}, bf16[128,1024]{1,0:T(8,128)(2,1)S(1)}, u32[]{:S(2)}, u32[]{:S(2)}) collective-permute-start(bf16[128,1024]{1,0:T(8,128)(2,1)S(1)} %get-tuple-element.16), channel_id=1, source_target_pairs={{0,12},{1,15},{2,14},{3,13},{4,8},{5,11},{6,10},{7,9},{8,4},{9,7},... | collective-permute-start | bytes 786440 | tf_op jit(solution)/shard_map/ppermute | solution.py:201
  18.4 9.6 %collective-permute-start.6 = (bf16[128,1024]{1,0:T(8,128)(2,1)S(1)}, bf16[128,1024]{1,0:T(8,128)(2,1)S(1)}, u32[]{:S(2)}, u32[]{:S(2)}) collective-permute-start(bf16[128,1024]{1,0:T(8,128)(2,1)S(1)} %join.1.refs_0_), channel_id=1, source_target_pairs={{0,1},{1,0},{2,3},{3,2},{4,5},{5,4},{6,7},{7,6},{8,9},{9,8},{10,11... | collective-permute-start | bytes 786440 | tf_op jit(solution)/shard_map/ppermute | solution.py:185
  19.4 8.7 %collective-permute-start.7 = (bf16[128,1024]{1,0:T(8,128)(2,1)S(1)}, bf16[128,1024]{1,0:T(8,128)(2,1)S(1)}, u32[]{:S(2)}, u32[]{:S(2)}) collective-permute-start(bf16[128,1024]{1,0:T(8,128)(2,1)S(1)} %collective-permute-done.4.refs_1_), channel_id=1, source_target_pairs={{0,1},{1,0},{2,3},{3,2},{4,5},{5,4},{6,7},{7,6},{8,9},{9,8},{10,11... | collective-permute-start | bytes 786440 | tf_op jit(solution)/shard_map/ppermute | solution.py:185
  19.5 9.8 %collective-permute-start.8 = (bf16[128,1024]{1,0:T(8,128)(2,1)S(1)}, bf16[128,1024]{1,0:T(8,128)(2,1)S(1)}, u32[]{:S(2)}, u32[]{:S(2)}) collective-permute-start(bf16[128,1024]{1,0:T(8,128)(2,1)S(1)} %collective-permute-done.5.refs_2_), channel_id=1, source_target_pairs={{0,1},{1,0},{2,3},{3,2},{4,5},{5,4},{6,7},{7,6},{8,9},{9,8},{10,11... | collective-permute-start | bytes 786440 | tf_op jit(solution)/shard_map/ppermute | solution.py:185
  28.1 2.4 %collective-permute-start.10 = (bf16[128,1024]{1,0:T(8,128)(2,1)S(1)}, bf16[128,1024]{1,0:T(8,128)(2,1)S(1)}, u32[]{:S(2)}, u32[]{:S(2)}) collective-permute-start(bf16[128,1024]{1,0:T(8,128)(2,1)S(1)} %collective-permute-done.9.refs_6_), channel_id=1, source_target_pairs={{0,1},{1,0},{2,3},{3,2},{4,5},{5,4},{6,7},{7,6},{8,9},{9,8},{10,11... | collective-permute-start | bytes 786440 | tf_op jit(solution)/shard_map/ppermute | solution.py:185

commit v22 on v21

--- a/solution.py
+++ b/solution.py
@@ -100,10 +100,18 @@
     )(*args)
 
 
-def join_kernel(first_ref, second_ref, out_ref):
-    rows = first_ref.shape[0]
-    out_ref[:rows] = first_ref[...]
-    out_ref[rows:] = second_ref[...]
+def pass_kernel(*refs):
+    half = len(refs) // 2
+    for in_ref, out_ref in zip(refs[:half], refs[half:]):
+        out_ref[...] = in_ref[...]
+
+
+def halve_kernel(*refs):
+    pieces = len(refs) // 3
+    for k, piece in enumerate(refs[:pieces]):
+        first, second = refs[pieces + 2 * k : pieces + 2 * k + 2]
+        first[...] = piece[: first.shape[0]]
+        second[...] = piece[first.shape[0] :]
 
 
 def blocks(rows, starts, size):
@@ -141,21 +149,31 @@
     return call_kernel("count", functools.partial(count_kernel, starts, size), out_shape, *pieces)
 
 
-def finish_kernel(starts, late_pieces, late_starts, places, *refs):
-    *piece_refs, early_ref, count_ref = refs
-    size = count_ref.shape[2]
-    early = jnp.concatenate([piece[...] for piece in piece_refs[:-late_pieces]], axis=0)
-    late = jnp.concatenate([piece[...] for piece in piece_refs[-late_pieces:]], axis=0)
-    own = blocks(early, starts, size)
-    late_own = blocks(late, late_starts, size)
-    total = early_ref[...] + count_against(late, own, [], size)
-    late_total = count_against(early, late_own, [], size) + count_against(
-        late, late_own, late_starts, size
-    )
-    count_ref[...] = jnp.zeros_like(count_ref)
+def late_kernel(*refs):
+    *piece_refs, late_ref, early_ref, own_ref = refs
+    early = jnp.concatenate([piece[...] for piece in piece_refs], axis=0)
+    late = late_ref[...]
+    size = late.shape[0]
+    early_ref[...] = count_against(late, early, [], size)
+    own_ref[...] = count_against(early, late, [], size) + count_against(late, late, [0], size)
+
+
+def finish_kernel(starts, places, late_ref, other_ref, counts_ref, early_ref, own_ref, out_ref):
+    size = out_ref.shape[2]
+    late = late_ref[...]
+    own = own_ref[...] + count_against(other_ref[...], late, [], size)
+    early = early_ref[...]
+    blocks_early = early.shape[1] // size
+    out_ref[...] = jnp.zeros_like(out_ref)
     for k, place in enumerate(places()):
-        source, j = (total, k) if k < len(starts) else (late_total, k - len(starts))
-        count_ref[pl.ds(place, 1), 0, :] = source[:, j * size : (j + 1) * size]
+        if k < blocks_early:
+            block = early[:, k * size : (k + 1) * size]
+            if k * size in starts:
+                j = starts.index(k * size)
+                block = block + counts_ref[:, j * size : (j + 1) * size]
+        else:
+            block = own[:, (k - blocks_early) * size : (k - blocks_early + 1) * size]
+        out_ref[pl.ds(place, 1), 0, :] = block
 
 
 def select_kernel(clusters, capacity, counts_ref, slot_ref, out_ref):
@@ -168,9 +186,8 @@
     by_block = jnp.dot(
         counts, hot, precision=lax.Precision.HIGHEST, preferred_element_type=jnp.float32
     )
-    cores = counts.shape[0] // clusters
-    core = lax.axis_index("sub") if cores > 1 else 0
-    chosen = lax.broadcasted_iota(jnp.int32, by_block.shape, 0) == block * cores + core
+    parts = counts.shape[0] // clusters
+    chosen = lax.broadcasted_iota(jnp.int32, by_block.shape, 0) // parts == block
     out_ref[...] = jnp.sum(jnp.where(chosen, by_block, 0.0), axis=0, keepdims=True)
 
 
@@ -227,30 +244,47 @@
     first_other = across(first_other, first)
     rest = [across(piece, p) for piece, p in zip(rest, [*middle, last])]
 
-    first_both = call_kernel("join", join_kernel, whole, first_own, first_other, flops=10**10)
-    early = [first_both, *rest[:-1]]
-    early += [swap_cores(x) for x in early]
-    late = [rest[-1], swap_cores(rest[-1])]
+    firsts = call_kernel(
+        "pass", pass_kernel, [half] * 2, first_own, first_other, flops=10**10
+    )
+    *near, last_piece = rest
+    halves = call_kernel("halve", halve_kernel, [half] * (2 * len(near)), *near, flops=10**10)
+    early = [*firsts, *near]
+    early += [swap_cores(x) for x in (*firsts, *halves)]
+
     span = cores * capacity
     half_way = span * (steps - 1)
     starts = [k * span for k in range(steps - 1)]
     starts += [half_way + start + capacity for start in starts]
-    late_starts = [0, span + capacity]
+    counts = soft_counts(early, starts, capacity)
+
+    late_piece, _ = lax.optimization_barrier((last_piece, counts))
+    late_other = swap_cores(late_piece)
+    sums = [
+        jax.ShapeDtypeStruct((1, 2 * half_way), jnp.float32),
+        jax.ShapeDtypeStruct((1, span), jnp.float32),
+    ]
+    early_sums, own_sums = call_kernel("late", late_kernel, sums, *early, last_piece)
 
     def places():
         chip, core = chip_index(), lax.axis_index("sub")
-        own = [chip ^ (p * cores + core) for p in (first, *middle, last)]
-        other = [chip ^ (p * cores + 1 - core) for p in (first, *middle, last)]
-        chips = own[:-1] + other[:-1] + [own[-1], other[-1]]
-        return [there * cores + core for there in chips]
+        devices = []
+        for here in (core, 1 - core):
+            for p in (first, *middle):
+                there = (chip ^ (p * cores + here)) * cores
+                devices += [there + here, there + 1 - here]
+        there = (chip ^ (last * cores + core)) * cores
+        return devices + [there + core, there + 1 - core]
 
     counts = call_kernel(
         "finish",
-        functools.partial(finish_kernel, starts, len(late), late_starts, places),
+        functools.partial(finish_kernel, starts, places),
         jax.ShapeDtypeStruct((clusters * cores, 1, capacity), jnp.float32),
-        *early,
-        *late,
-        soft_counts(early, starts, capacity),
+        last_piece,
+        late_other,
+        counts,
+        early_sums,
+        own_sums,
     )
     back = lax.all_to_all(
         counts, ("owner", "helper", "sub"), split_axis=0, concat_axis=0, tiled=True

time: 44.9 us -> 46.7 us (1.040)
  waiting for transfers between devices: 7.34 us -> 18.6 us
  starting transfers between devices: 19.4 us -> 12 us
  blocking collectives: 12.4 us -> 9.92 us
    ppermute x5, waiting for transfers between devices: 6.19 us -> 17.1 us  [across(): return lax.ppermute(x, ('owner', 'helper', 'sub'), pairs)]
    ppermute x6 -> x9, starting transfers between devices: 10.5 us -> 3.64 us  [swap_cores(): return lax.ppermute(x, 'sub', [(i, i ^ 1) for i in range(cores)])]
    all_to_all x1, blocking collectives: 12.4 us -> 9.92 us  [body_by_chip(): lax.all_to_all(counts, ('owner', 'helper', 'sub'), split_axis=0, concat_a...]
    pallas_call x6 -> x8, Pallas kernels: 4.26 us -> 4.64 us  [call_kernel(): pl.pallas_call(kernel, out_shape=out_shape, in_specs=[VMEM] * len(args),...]
    ppermute x6 -> x9, waiting for transfers between devices: 1.15 us -> 1.5 us  [swap_cores(): return lax.ppermute(x, 'sub', [(i, i ^ 1) for i in range(cores)])]
  transfers between devices with their start and end apart: 11 -> 14, of which waited for: 3 -> 8; matrix products, arithmetic and copies ran while one was open for 0% -> 0% of each run, Pallas kernels for 5% -> 8%
where the time goes in v22:
time: 46.7 us; the launch traced here: 46.5 us
  waiting for transfers between devices  18.6 us (40%)
  starting transfers between devices  12 us (26%)
  blocking collectives  9.92 us (21%)
  Pallas kernels  4.64 us (10%)
  local copies, waits for them, and re-layouts  1.27 us (3%)
    ppermute x5, waiting for transfers between devices, across(): return lax.ppermute(x, ('owner', 'helper', 'sub'), pairs)  17.1 us
    all_to_all x1, blocking collectives, body_by_chip(): lax.all_to_all(counts, ('owner', 'helper', 'sub'), split_axis=0, concat_a...  9.92 us
    ppermute x5, starting transfers between devices, across(): return lax.ppermute(x, ('owner', 'helper', 'sub'), pairs)  8.38 us
    pallas_call x8, Pallas kernels, call_kernel(): pl.pallas_call(kernel, out_shape=out_shape, in_specs=[VMEM] * len(args),...  4.64 us
    ppermute x9, starting transfers between devices, swap_cores(): return lax.ppermute(x, 'sub', [(i, i ^ 1) for i in range(cores)])  3.64 us
    ppermute x9, waiting for transfers between devices, swap_cores(): return lax.ppermute(x, 'sub', [(i, i ^ 1) for i in range(cores)])  1.5 us
    unnamed x4, local copies, waits for them, and re-layouts  1.27 us
  transfers between devices with their start and end apart: 14, of which 8 were waited for; matrix products, arithmetic and copies ran while one was open for 0% of the time, Pallas kernels for 8%

profile of v22, /device:TPU:0, one launch (start us, length us, event | category | flops | bytes accessed | tf_op | source)
XLA Modules:
  0.0 46.5 jit_solution(11644585225465164218)
XLA Ops:
  0.0 0.5 collective-permute-start
  0.5 0.2 copy-done.1
  0.7 0.5 collective-permute-start.1
  1.1 1.0 %copy-done = bf16[256,1024]{1,0:T(8,128)(2,1)S(1)} copy-done((bf16[256,1024]{1,0:T(8,128)(2,1)S(1)}, bf16[256,1024]{1,0:T(8,128)(2,1)}, u32[]{:S(2)}) %copy-start) | copy-done | bytes 524312
  2.2 0.5 %route_first.1 = (bf16[64,1024]{1,0:T(8,128)(2,1)S(1)}, s32[1,256]{1,0:T(1,128)S(1)}) custom-call(bf16[256,1024]{1,0:T(8,128)(2,1)S(1)} %copy-done, s32[1,256]{1,0:T(1,128)S(1)} %bitcast.3), custom_call_target="tpu_custom_call" | custom-call | tf_op jit(solution)/shard_map/route_first/pallas_call | solution.py:92
  2.6 3.7 %collective-permute-start.3 = (bf16[64,1024]{1,0:T(8,128)(2,1)S(1)}, bf16[64,1024]{1,0:T(8,128)(2,1)S(1)}, u32[]{:S(2)}, u32[]{:S(2)}) collective-permute-start(bf16[64,1024]{1,0:T(8,128)(2,1)S(1)} %get-tuple-element.22), channel_id=1, source_target_pairs={{0,8},{1,11},{2,10},{3,9},{4,12},{5,15},{6,14},{7,13},{8,0},{9,3},... | collective-permute-start | bytes 393224 | tf_op jit(solution)/shard_map/ppermute | solution.py:218
  6.3 0.0 collective-permute-done.1.refs_3_
  6.3 0.7 %route_rest.1 = (bf16[64,1024]{1,0:T(8,128)(2,1)S(1)}, bf16[128,1024]{1,0:T(8,128)(2,1)S(1)}, bf16[128,1024]{1,0:T(8,128)(2,1)S(1)}, bf16[128,1024]{1,0:T(8,128)(2,1)S(1)}) custom-call(bf16[256,1024]{1,0:T(8,128)(2,1)S(1)} %copy-done, bf16[256,1024]{1,0:T(8,128)(2,1)S(1)} %collective-permute-done.refs_1_, s32[1,256]{1,0:T(1,128)S(1)} %get-tuple-element.20.refs_2_.slot_ref, ...), custom_call_target="tpu_custom_call" | custom-call | tf_op jit(solution)/shard_map/route_rest/pallas_call | solution.py:92
  7.0 0.1 collective-permute-start.4
  7.1 3.9 %collective-permute-start.2 = (bf16[128,1024]{1,0:T(8,128)(2,1)S(1)}, bf16[128,1024]{1,0:T(8,128)(2,1)S(1)}, u32[]{:S(2)}, u32[]{:S(2)}) collective-permute-start(bf16[128,1024]{1,0:T(8,128)(2,1)S(1)} %get-tuple-element.21), channel_id=1, source_target_pairs={{0,12},{1,15},{2,14},{3,13},{4,8},{5,11},{6,10},{7,9},{8,4},{9,7},... | collective-permute-start | bytes 786440 | tf_op jit(solution)/shard_map/ppermute | solution.py:218
  11.0 0.7 %collective-permute-start.5 = (bf16[128,1024]{1,0:T(8,128)(2,1)S(1)}, bf16[128,1024]{1,0:T(8,128)(2,1)S(1)}, u32[]{:S(2)}, u32[]{:S(2)}) collective-permute-start(bf16[128,1024]{1,0:T(8,128)(2,1)S(1)} %get-tuple-element.26), channel_id=1, source_target_pairs={{0,0},{1,3},{2,2},{3,1},{4,4},{5,7},{6,6},{7,5},{8,8},{9,11},{10,1... | collective-permute-start | bytes 786440 | tf_op jit(solution)/shard_map/ppermute | solution.py:218
  11.7 0.1 collective-permute-start.6
  11.8 9.3 %collective-permute-done.3.refs_0_ = bf16[64,1024]{1,0:T(8,128)(2,1)S(1)} collective-permute-done((bf16[64,1024]{1,0:T(8,128)(2,1)S(1)}, bf16[64,1024]{1,0:T(8,128)(2,1)S(1)}, u32[]{:S(2)}, u32[]{:S(2)}) %collective-permute-start.3) | collective-permute-done | bytes 131104 | tf_op jit(solution)/shard_map/ppermute | solution.py:218
  21.1 2.9 %collective-permute-done.4.refs_1_ = bf16[64,1024]{1,0:T(8,128)(2,1)S(1)} collective-permute-done((bf16[64,1024]{1,0:T(8,128)(2,1)S(1)}, bf16[64,1024]{1,0:T(8,128)(2,1)S(1)}, u32[]{:S(2)}, u32[]{:S(2)}) %collective-permute-start.4) | collective-permute-done | bytes 131104 | tf_op jit(solution)/shard_map/ppermute | solution.py:218
  24.1 0.9 %collective-permute-start.7 = (bf16[64,1024]{1,0:T(8,128)(2,1)S(1)}, bf16[64,1024]{1,0:T(8,128)(2,1)S(1)}, u32[]{:S(2)}, u32[]{:S(2)}) collective-permute-start(bf16[64,1024]{1,0:T(8,128)(2,1)S(1)} %get-tuple-element.24.refs_0_), channel_id=1, source_target_pairs={{0,1},{1,0},{2,3},{3,2},{4,5},{5,4},{6,7},{7,6},{8,9},{9,8},{10,11... | collective-permute-start | bytes 393224 | tf_op jit(solution)/shard_map/ppermute | solution.py:202
  25.0 0.1 collective-permute-start.8
  25.1 4.8 %collective-permute-done.6.refs_1_.refs_3_ = bf16[128,1024]{1,0:T(8,128)(2,1)S(1)} collective-permute-done((bf16[128,1024]{1,0:T(8,128)(2,1)S(1)}, bf16[128,1024]{1,0:T(8,128)(2,1)S(1)}, u32[]{:S(2)}, u32[]{:S(2)}) %collective-permute-start.6) | collective-permute-done | bytes 262176 | tf_op jit(solution)/shard_map/ppermute | solution.py:218
  29.9 0.9 %collective-permute-start.9 = (bf16[64,1024]{1,0:T(8,128)(2,1)S(1)}, bf16[64,1024]{1,0:T(8,128)(2,1)S(1)}, u32[]{:S(2)}, u32[]{:S(2)}) collective-permute-start(bf16[64,1024]{1,0:T(8,128)(2,1)S(1)} %get-tuple-element.28), channel_id=1, source_target_pairs={{0,1},{1,0},{2,3},{3,2},{4,5},{5,4},{6,7},{7,6},{8,9},{9,8},{10,11... | collective-permute-start | bytes 393224 | tf_op jit(solution)/shard_map/ppermute | solution.py:202
  30.8 0.1 collective-permute-start.10
  30.9 0.4 collective-permute-start.11
  31.3 0.1 collective-permute-start.12
  31.4 0.4 collective-permute-done.9.refs_6_
  31.8 0.4 collective-permute-done.10.refs_7_
  32.2 0.2 collective-permute-done.11.refs_8_
  32.4 0.3 collective-permute-done.12.refs_9_
  32.7 1.2 %count.1.counts_ref = f32[1,384]{1,0:T(1,128)S(1)} custom-call(bf16[64,1024]{1,0:T(8,128)(2,1)S(1)} %get-tuple-element.24.refs_0_, bf16[64,1024]{1,0:T(8,128)(2,1)S(1)} %get-tuple-element.25.refs_1_, bf16[128,1024]{1,0:T(8,128)(2,1)S(1)} %collective-permute-done.5.refs_0_.refs_2_, bf16[128,1024]{1,0:T(8,128)(2,1)S(1)} %collective-permute-done.6.refs_1_.refs_3_, ...), custom_call_target="tpu_custom_call" | custom-call | tf_op jit(solution)/shard_map/count/pallas_call | solution.py:92
  33.9 0.2 collective-permute-start.13
  34.2 1.1 %late.1 = (f32[1,768]{1,0:T(1,128)S(1)}, f32[1,128]{1,0:T(1,128)S(1)}) custom-call(bf16[64,1024]{1,0:T(8,128)(2,1)S(1)} %get-tuple-element.24.refs_0_, bf16[64,1024]{1,0:T(8,128)(2,1)S(1)} %get-tuple-element.25.refs_1_, bf16[128,1024]{1,0:T(8,128)(2,1)S(1)} %collective-permute-done.5.refs_0_.refs_2_, ...), custom_call_target="tpu_custom_call" | custom-call | tf_op jit(solution)/shard_map/late/pallas_call | solution.py:92
  35.3 0.2 collective-permute-done.13.other_ref
  35.5 0.3 finish.1
  35.8 9.9 %all_to_all.5.counts_ref = f32[16,1,64]{2,1,0:T(1,128)S(1)} all-to-all(f32[16,1,64]{2,1,0:T(1,128)S(1)} %finish.1), channel_id=1, replica_groups=mesh['groups'=2,'owner'=4,'helper'=2,'sub'=2] {'owner','helper','sub'}, dimensions={0} | all-to-all | bytes 8192 | tf_op jit(solution)/shard_map/all_to_all | solution.py:289
  45.8 0.7 %select.1 = f32[1,256]{1,0:T(1,128)} custom-call(f32[16,1,64]{2,1,0:T(1,128)S(1)} %all_to_all.5.counts_ref, s32[1,256]{1,0:T(1,128)S(1)} %get-tuple-element.20.refs_2_.slot_ref), custom_call_target="tpu_custom_call" | custom-call | tf_op jit(solution)/shard_map/select/pallas_call | solution.py:92
  (9 shorter events, 0.1 us)
Async XLA Ops:
  0.0 0.7 %copy-start.1 = (s32[256]{0:T(256)S(1)}, s32[256]{0:T(256)}, u32[]{:S(2)}) copy-start(s32[256]{0:T(256)} %param.3) | copy-start | bytes 3076
  0.0 6.3 %collective-permute-start = (bf16[256,1024]{1,0:T(8,128)(2,1)}, bf16[256,1024]{1,0:T(8,128)(2,1)S(1)}, u32[]{:S(2)}, u32[]{:S(2)}) collective-permute-start(bf16[256,1024]{1,0:T(8,128)(2,1)} %refs_0_.1), channel_id=1, source_target_pairs={{0,1},{1,0},{2,3},{3,2},{4,5},{5,4},{6,7},{7,6},{8,9},{9,8},{10,11... | collective-permute-start | bytes 1572872 | tf_op jit(solution)/shard_map/ppermute | solution.py:202
  0.7 5.6 %collective-permute-start.1 = (s32[1,256]{1,0:T(1,128)S(1)}, s32[1,256]{1,0:T(1,128)S(1)}, u32[]{:S(2)}, u32[]{:S(2)}) collective-permute-start(s32[1,256]{1,0:T(1,128)S(1)} %bitcast.2), channel_id=1, source_target_pairs={{0,1},{1,0},{2,3},{3,2},{4,5},{5,4},{6,7},{7,6},{8,9},{9,8},{10,11... | collective-permute-start | bytes 3080 | tf_op jit(solution)/shard_map/ppermute | solution.py:202
  1.1 1.0 %copy-start = (bf16[256,1024]{1,0:T(8,128)(2,1)S(1)}, bf16[256,1024]{1,0:T(8,128)(2,1)}, u32[]{:S(2)}) copy-start(bf16[256,1024]{1,0:T(8,128)(2,1)} %refs_0_.1) | copy-start | bytes 1572868
  2.6 18.5 %collective-permute-start.3 = (bf16[64,1024]{1,0:T(8,128)(2,1)S(1)}, bf16[64,1024]{1,0:T(8,128)(2,1)S(1)}, u32[]{:S(2)}, u32[]{:S(2)}) collective-permute-start(bf16[64,1024]{1,0:T(8,128)(2,1)S(1)} %get-tuple-element.22), channel_id=1, source_target_pairs={{0,8},{1,11},{2,10},{3,9},{4,12},{5,15},{6,14},{7,13},{8,0},{9,3},... | collective-permute-start | bytes 393224 | tf_op jit(solution)/shard_map/ppermute | solution.py:218
  7.0 17.0 %collective-permute-start.4 = (bf16[64,1024]{1,0:T(8,128)(2,1)S(1)}, bf16[64,1024]{1,0:T(8,128)(2,1)S(1)}, u32[]{:S(2)}, u32[]{:S(2)}) collective-permute-start(bf16[64,1024]{1,0:T(8,128)(2,1)S(1)} %get-tuple-element.23), channel_id=1, source_target_pairs={{0,8},{1,11},{2,10},{3,9},{4,12},{5,15},{6,14},{7,13},{8,0},{9,3},... | collective-permute-start | bytes 393224 | tf_op jit(solution)/shard_map/ppermute | solution.py:218
  7.1 26.8 %collective-permute-start.2 = (bf16[128,1024]{1,0:T(8,128)(2,1)S(1)}, bf16[128,1024]{1,0:T(8,128)(2,1)S(1)}, u32[]{:S(2)}, u32[]{:S(2)}) collective-permute-start(bf16[128,1024]{1,0:T(8,128)(2,1)S(1)} %get-tuple-element.21), channel_id=1, source_target_pairs={{0,12},{1,15},{2,14},{3,13},{4,8},{5,11},{6,10},{7,9},{8,4},{9,7},... | collective-permute-start | bytes 786440 | tf_op jit(solution)/shard_map/ppermute | solution.py:218
  11.0 14.0 %collective-permute-start.5 = (bf16[128,1024]{1,0:T(8,128)(2,1)S(1)}, bf16[128,1024]{1,0:T(8,128)(2,1)S(1)}, u32[]{:S(2)}, u32[]{:S(2)}) collective-permute-start(bf16[128,1024]{1,0:T(8,128)(2,1)S(1)} %get-tuple-element.26), channel_id=1, source_target_pairs={{0,0},{1,3},{2,2},{3,1},{4,4},{5,7},{6,6},{7,5},{8,8},{9,11},{10,1... | collective-permute-start | bytes 786440 | tf_op jit(solution)/shard_map/ppermute | solution.py:218
  11.7 18.2 %collective-permute-start.6 = (bf16[128,1024]{1,0:T(8,128)(2,1)S(1)}, bf16[128,1024]{1,0:T(8,128)(2,1)S(1)}, u32[]{:S(2)}, u32[]{:S(2)}) collective-permute-start(bf16[128,1024]{1,0:T(8,128)(2,1)S(1)} %get-tuple-element.27), channel_id=1, source_target_pairs={{0,4},{1,7},{2,6},{3,5},{4,0},{5,3},{6,2},{7,1},{8,12},{9,15},{10,... | collective-permute-start | bytes 786440 | tf_op jit(solution)/shard_map/ppermute | solution.py:218
  24.1 6.9 %collective-permute-start.7 = (bf16[64,1024]{1,0:T(8,128)(2,1)S(1)}, bf16[64,1024]{1,0:T(8,128)(2,1)S(1)}, u32[]{:S(2)}, u32[]{:S(2)}) collective-permute-start(bf16[64,1024]{1,0:T(8,128)(2,1)S(1)} %get-tuple-element.24.refs_0_), channel_id=1, source_target_pairs={{0,1},{1,0},{2,3},{3,2},{4,5},{5,4},{6,7},{7,6},{8,9},{9,8},{10,11... | collective-permute-start | bytes 393224 | tf_op jit(solution)/shard_map/ppermute | solution.py:202
  25.0 6.3 %collective-permute-start.8 = (bf16[64,1024]{1,0:T(8,128)(2,1)S(1)}, bf16[64,1024]{1,0:T(8,128)(2,1)S(1)}, u32[]{:S(2)}, u32[]{:S(2)}) collective-permute-start(bf16[64,1024]{1,0:T(8,128)(2,1)S(1)} %get-tuple-element.25.refs_1_), channel_id=1, source_target_pairs={{0,1},{1,0},{2,3},{3,2},{4,5},{5,4},{6,7},{7,6},{8,9},{9,8},{10,11... | collective-permute-start | bytes 393224 | tf_op jit(solution)/shard_map/ppermute | solution.py:202
  29.9 1.9 %collective-permute-start.9 = (bf16[64,1024]{1,0:T(8,128)(2,1)S(1)}, bf16[64,1024]{1,0:T(8,128)(2,1)S(1)}, u32[]{:S(2)}, u32[]{:S(2)}) collective-permute-start(bf16[64,1024]{1,0:T(8,128)(2,1)S(1)} %get-tuple-element.28), channel_id=1, source_target_pairs={{0,1},{1,0},{2,3},{3,2},{4,5},{5,4},{6,7},{7,6},{8,9},{9,8},{10,11... | collective-permute-start | bytes 393224 | tf_op jit(solution)/shard_map/ppermute | solution.py:202
  30.8 1.3 %collective-permute-start.10 = (bf16[64,1024]{1,0:T(8,128)(2,1)S(1)}, bf16[64,1024]{1,0:T(8,128)(2,1)S(1)}, u32[]{:S(2)}, u32[]{:S(2)}) collective-permute-start(bf16[64,1024]{1,0:T(8,128)(2,1)S(1)} %get-tuple-element.29), channel_id=1, source_target_pairs={{0,1},{1,0},{2,3},{3,2},{4,5},{5,4},{6,7},{7,6},{8,9},{9,8},{10,11... | collective-permute-start | bytes 393224 | tf_op jit(solution)/shard_map/ppermute | solution.py:202
  30.9 1.5 %collective-permute-start.11 = (bf16[64,1024]{1,0:T(8,128)(2,1)S(1)}, bf16[64,1024]{1,0:T(8,128)(2,1)S(1)}, u32[]{:S(2)}, u32[]{:S(2)}) collective-permute-start(bf16[64,1024]{1,0:T(8,128)(2,1)S(1)} %get-tuple-element.30), channel_id=1, source_target_pairs={{0,1},{1,0},{2,3},{3,2},{4,5},{5,4},{6,7},{7,6},{8,9},{9,8},{10,11... | collective-permute-start | bytes 393224 | tf_op jit(solution)/shard_map/ppermute | solution.py:202
  31.3 1.3 %collective-permute-start.12 = (bf16[64,1024]{1,0:T(8,128)(2,1)S(1)}, bf16[64,1024]{1,0:T(8,128)(2,1)S(1)}, u32[]{:S(2)}, u32[]{:S(2)}) collective-permute-start(bf16[64,1024]{1,0:T(8,128)(2,1)S(1)} %get-tuple-element.31), channel_id=1, source_target_pairs={{0,1},{1,0},{2,3},{3,2},{4,5},{5,4},{6,7},{7,6},{8,9},{9,8},{10,11... | collective-permute-start | bytes 393224 | tf_op jit(solution)/shard_map/ppermute | solution.py:202
  33.9 1.6 %collective-permute-start.13 = (bf16[128,1024]{1,0:T(8,128)(2,1)S(1)}, bf16[128,1024]{1,0:T(8,128)(2,1)S(1)}, u32[]{:S(2)}, u32[]{:S(2)}) collective-permute-start(bf16[128,1024]{1,0:T(8,128)(2,1)S(1)} %collective-permute-done.2.refs_10_.late_ref), channel_id=1, source_target_pairs={{0,1},{1,0},{2,3},{3,2},{4,5},{5,4},{6,7},{7,6},{8,9},{9,8},{10,11... | collective-permute-start | bytes 786440 | tf_op jit(solution)/shard_map/ppermute | solution.py:202

commit v23 on v22

--- a/solution.py
+++ b/solution.py
@@ -67,18 +67,20 @@
     piece_ref[...] = lay(rows_ref, slots_of_steps(slot, capacity, [step]), capacity)
 
 
-def route_rest_kernel(clusters, capacity, first, steps, *refs):
-    own_rows, other_rows, own_slot, other_ids, first_ref, *piece_refs = refs
+def route_rest_kernel(clusters, capacity, halves, steps, *refs):
+    own_rows, other_rows, own_slot, other_ids, *piece_refs = refs
+    half_refs, whole_refs = piece_refs[: len(halves)], piece_refs[len(halves) :]
     slot = slots_of_steps(own_slot[...], capacity, steps)
     laid = lay(own_rows, slot, len(steps) * capacity)
-    for k, piece in enumerate(piece_refs):
+    for k, piece in enumerate(whole_refs):
         piece[:capacity] = laid[k * capacity : (k + 1) * capacity]
     slot = slots_of(other_ids[...], clusters, capacity)
-    slot = slots_of_steps(slot, capacity, [first, *steps])
-    laid = lay(other_rows, slot, (1 + len(steps)) * capacity)
-    first_ref[...] = laid[:capacity]
-    for k, piece in enumerate(piece_refs):
-        piece[capacity:] = laid[(k + 1) * capacity : (k + 2) * capacity]
+    slot = slots_of_steps(slot, capacity, [*halves, *steps])
+    laid = lay(other_rows, slot, (len(halves) + len(steps)) * capacity)
+    for k, piece in enumerate(half_refs):
+        piece[...] = laid[k * capacity : (k + 1) * capacity]
+    for k, piece in enumerate(whole_refs, len(halves)):
+        piece[capacity:] = laid[k * capacity : (k + 1) * capacity]
 
 
 def route_kernel(clusters, capacity, rows_ref, ids_ref, piece_ref, slot_ref):
@@ -232,22 +234,28 @@
         ids,
     )
     first_own = across(first_own, first)
-    first_other, *rest = call_kernel(
-        "route_rest",
-        functools.partial(route_rest_kernel, clusters, capacity, first, [*middle, last]),
-        [half] + [whole] * (steps - 1),
-        embeddings,
-        other_rows,
-        slot,
-        other_ids,
-    )
-    first_other = across(first_other, first)
-    rest = [across(piece, p) for piece, p in zip(rest, [*middle, last])]
+
+    def route_rest(name, halves, steps, slot, flops=0):
+        return call_kernel(
+            name,
+            functools.partial(route_rest_kernel, clusters, capacity, halves, steps),
+            [half] * len(halves) + [whole] * len(steps),
+            embeddings,
+            other_rows,
+            slot,
+            other_ids,
+            flops=flops,
+        )
+
+    near = route_rest("route_near", [], middle, slot)
+    later_slot, _ = lax.optimization_barrier((slot, near[0]))
+    near = [across(piece, p) for piece, p in zip(near, middle)]
+    first_other, last_piece = route_rest("route_far", [first], [last], later_slot, 10**10)
+    first_other, last_piece = across(first_other, first), across(last_piece, last)
 
     firsts = call_kernel(
-        "pass", pass_kernel, [half] * 2, first_own, first_other, flops=10**10
-    )
-    *near, last_piece = rest
+        "pass", pass_kernel, [half] * 2, first_own, first_other
+    )
     halves = call_kernel("halve", halve_kernel, [half] * (2 * len(near)), *near, flops=10**10)
     early = [*firsts, *near]
     early += [swap_cores(x) for x in (*firsts, *halves)]

time: 46.7 us -> 44.3 us (0.949)
  waiting for transfers between devices: 18.6 us -> 5.04 us
  starting transfers between devices: 12 us -> 23.6 us
  blocking collectives: 9.92 us -> 8.97 us
    ppermute x5, waiting for transfers between devices: 17.1 us -> 3.37 us  [across(): return lax.ppermute(x, ('owner', 'helper', 'sub'), pairs)]
    ppermute x9, starting transfers between devices: 3.64 us -> 14.8 us  [swap_cores(): return lax.ppermute(x, 'sub', [(i, i ^ 1) for i in range(cores)])]
    all_to_all x1, blocking collectives: 9.92 us -> 8.97 us  [body_by_chip(): lax.all_to_all(counts, ('owner', 'helper', 'sub'), split_axis=0, concat_a...]
    pallas_call x8 -> x9, Pallas kernels: 4.64 us -> 5.1 us  [call_kernel(): pl.pallas_call(kernel, out_shape=out_shape, in_specs=[VMEM] * len(args),...]
  transfers between devices with their start and end apart: 14 -> 14, of which waited for: 8 -> 8; matrix products, arithmetic and copies ran while one was open for 0% -> 0% of each run, Pallas kernels for 8% -> 9%
where the time goes in v23:
time: 44.3 us; the launch traced here: 44.1 us
  starting transfers between devices  23.6 us (53%)
  blocking collectives  8.97 us (20%)
  Pallas kernels  5.1 us (12%)
  waiting for transfers between devices  5.04 us (11%)
  local copies, waits for them, and re-layouts  1.27 us (3%)
    ppermute x9, starting transfers between devices, swap_cores(): return lax.ppermute(x, 'sub', [(i, i ^ 1) for i in range(cores)])  14.8 us
    all_to_all x1, blocking collectives, body_by_chip(): lax.all_to_all(counts, ('owner', 'helper', 'sub'), split_axis=0, concat_a...  8.97 us
    ppermute x5, starting transfers between devices, across(): return lax.ppermute(x, ('owner', 'helper', 'sub'), pairs)  8.85 us
    pallas_call x9, Pallas kernels, call_kernel(): pl.pallas_call(kernel, out_shape=out_shape, in_specs=[VMEM] * len(args),...  5.1 us
    ppermute x5, waiting for transfers between devices, across(): return lax.ppermute(x, ('owner', 'helper', 'sub'), pairs)  3.37 us
    ppermute x9, waiting for transfers between devices, swap_cores(): return lax.ppermute(x, 'sub', [(i, i ^ 1) for i in range(cores)])  1.67 us
    unnamed x4, local copies, waits for them, and re-layouts  1.27 us
  transfers between devices with their start and end apart: 14, of which 8 were waited for; matrix products, arithmetic and copies ran while one was open for 0% of the time, Pallas kernels for 9%

profile of v23, /device:TPU:0, one launch (start us, length us, event | category | flops | bytes accessed | tf_op | source)
XLA Modules:
  0.0 44.1 jit_solution(9252572499170890231)
XLA Ops:
  0.0 0.5 %collective-permute-start = (bf16[256,1024]{1,0:T(8,128)(2,1)}, bf16[256,1024]{1,0:T(8,128)(2,1)S(1)}, u32[]{:S(2)}, u32[]{:S(2)}) collective-permute-start(bf16[256,1024]{1,0:T(8,128)(2,1)} %refs_0_.3), channel_id=1, source_target_pairs={{0,1},{1,0},{2,3},{3,2},{4,5},{5,4},{6,7},{7,6},{8,9},{9,8},{10,11... | collective-permute-start | bytes 1572872 | tf_op jit(solution)/shard_map/ppermute | solution.py:204
  0.5 0.2 copy-done.1
  0.7 0.5 %collective-permute-start.1 = (s32[1,256]{1,0:T(1,128)S(1)}, s32[1,256]{1,0:T(1,128)S(1)}, u32[]{:S(2)}, u32[]{:S(2)}) collective-permute-start(s32[1,256]{1,0:T(1,128)S(1)} %bitcast.2), channel_id=1, source_target_pairs={{0,1},{1,0},{2,3},{3,2},{4,5},{5,4},{6,7},{7,6},{8,9},{9,8},{10,11... | collective-permute-start | bytes 3080 | tf_op jit(solution)/shard_map/ppermute | solution.py:204
  1.1 1.0 %copy-done = bf16[256,1024]{1,0:T(8,128)(2,1)S(1)} copy-done((bf16[256,1024]{1,0:T(8,128)(2,1)S(1)}, bf16[256,1024]{1,0:T(8,128)(2,1)}, u32[]{:S(2)}) %copy-start) | copy-done | bytes 524312
  2.2 0.5 %route_first.1 = (bf16[64,1024]{1,0:T(8,128)(2,1)S(1)}, s32[1,256]{1,0:T(1,128)S(1)}) custom-call(bf16[256,1024]{1,0:T(8,128)(2,1)S(1)} %copy-done, s32[1,256]{1,0:T(1,128)S(1)} %bitcast.3), custom_call_target="tpu_custom_call" | custom-call | tf_op jit(solution)/shard_map/route_first/pallas_call | solution.py:94
  2.6 3.7 %collective-permute-start.3 = (bf16[64,1024]{1,0:T(8,128)(2,1)S(1)}, bf16[64,1024]{1,0:T(8,128)(2,1)S(1)}, u32[]{:S(2)}, u32[]{:S(2)}) collective-permute-start(bf16[64,1024]{1,0:T(8,128)(2,1)S(1)} %get-tuple-element.25), channel_id=1, source_target_pairs={{0,8},{1,11},{2,10},{3,9},{4,12},{5,15},{6,14},{7,13},{8,0},{9,3},... | collective-permute-start | bytes 393224 | tf_op jit(solution)/shard_map/ppermute | solution.py:220
  6.3 0.6 %route_near.1 = (bf16[128,1024]{1,0:T(8,128)(2,1)S(1)}, bf16[128,1024]{1,0:T(8,128)(2,1)S(1)}) custom-call(bf16[256,1024]{1,0:T(8,128)(2,1)S(1)} %copy-done, bf16[256,1024]{1,0:T(8,128)(2,1)S(1)} %collective-permute-done.refs_1_, s32[1,256]{1,0:T(1,128)S(1)} %get-tuple-element.23.refs_2_.slot_ref, s32[1,256]{1,0:T(1,128)S(1)} %collective-permute-done.1.refs_3_), custom_call_target="tpu_custom_call" | custom-call | tf_op jit(solution)/shard_map/route_near/pallas_call | solution.py:94
  6.9 0.7 %collective-permute-start.5 = (bf16[128,1024]{1,0:T(8,128)(2,1)S(1)}, bf16[128,1024]{1,0:T(8,128)(2,1)S(1)}, u32[]{:S(2)}, u32[]{:S(2)}) collective-permute-start(bf16[128,1024]{1,0:T(8,128)(2,1)S(1)} %get-tuple-element.22), channel_id=1, source_target_pairs={{0,0},{1,3},{2,2},{3,1},{4,4},{5,7},{6,6},{7,5},{8,8},{9,11},{10,1... | collective-permute-start | bytes 786440 | tf_op jit(solution)/shard_map/ppermute | solution.py:220
  7.6 1.6 %collective-permute-start.6 = (bf16[128,1024]{1,0:T(8,128)(2,1)S(1)}, bf16[128,1024]{1,0:T(8,128)(2,1)S(1)}, u32[]{:S(2)}, u32[]{:S(2)}) collective-permute-start(bf16[128,1024]{1,0:T(8,128)(2,1)S(1)} %get-tuple-element.29), channel_id=1, source_target_pairs={{0,4},{1,7},{2,6},{3,5},{4,0},{5,3},{6,2},{7,1},{8,12},{9,15},{10,... | collective-permute-start | bytes 786440 | tf_op jit(solution)/shard_map/ppermute | solution.py:220
  9.2 0.6 %route_far.1 = (bf16[64,1024]{1,0:T(8,128)(2,1)S(1)}, bf16[128,1024]{1,0:T(8,128)(2,1)S(1)}) custom-call(bf16[256,1024]{1,0:T(8,128)(2,1)S(1)} %copy-done, bf16[256,1024]{1,0:T(8,128)(2,1)S(1)} %collective-permute-done.refs_1_, s32[1,256]{1,0:T(1,128)S(1)} %get-tuple-element.23.refs_2_.slot_ref, s32[1,256]{1,0:T(1,128)S(1)} %collective-permute-done.1.refs_3_), custom_call_target="tpu_custom_call" | custom-call | flops 10000000000 | tf_op jit(solution)/shard_map/route_far/pallas_call | solution.py:94
  9.8 0.4 collective-permute-start.4
  10.2 2.5 %collective-permute-start.2 = (bf16[128,1024]{1,0:T(8,128)(2,1)S(1)}, bf16[128,1024]{1,0:T(8,128)(2,1)S(1)}, u32[]{:S(2)}, u32[]{:S(2)}) collective-permute-start(bf16[128,1024]{1,0:T(8,128)(2,1)S(1)} %get-tuple-element.24), channel_id=1, source_target_pairs={{0,12},{1,15},{2,14},{3,13},{4,8},{5,11},{6,10},{7,9},{8,4},{9,7},... | collective-permute-start | bytes 786440 | tf_op jit(solution)/shard_map/ppermute | solution.py:220
  12.7 0.1 collective-permute-done.3.refs_0_
  12.8 3.3 %collective-permute-done.4.refs_1_ = bf16[64,1024]{1,0:T(8,128)(2,1)S(1)} collective-permute-done((bf16[64,1024]{1,0:T(8,128)(2,1)S(1)}, bf16[64,1024]{1,0:T(8,128)(2,1)S(1)}, u32[]{:S(2)}, u32[]{:S(2)}) %collective-permute-start.4) | collective-permute-done | bytes 131104 | tf_op jit(solution)/shard_map/ppermute | solution.py:220
  16.1 12.4 %collective-permute-start.7 = (bf16[64,1024]{1,0:T(8,128)(2,1)S(1)}, bf16[64,1024]{1,0:T(8,128)(2,1)S(1)}, u32[]{:S(2)}, u32[]{:S(2)}) collective-permute-start(bf16[64,1024]{1,0:T(8,128)(2,1)S(1)} %get-tuple-element.27.refs_0_), channel_id=1, source_target_pairs={{0,1},{1,0},{2,3},{3,2},{4,5},{5,4},{6,7},{7,6},{8,9},{9,8},{10,11... | collective-permute-start | bytes 393224 | tf_op jit(solution)/shard_map/ppermute | solution.py:204
  28.5 0.1 collective-permute-start.8
  28.6 0.5 %collective-permute-start.9 = (bf16[64,1024]{1,0:T(8,128)(2,1)S(1)}, bf16[64,1024]{1,0:T(8,128)(2,1)S(1)}, u32[]{:S(2)}, u32[]{:S(2)}) collective-permute-start(bf16[64,1024]{1,0:T(8,128)(2,1)S(1)} %get-tuple-element.30), channel_id=1, source_target_pairs={{0,1},{1,0},{2,3},{3,2},{4,5},{5,4},{6,7},{7,6},{8,9},{9,8},{10,11... | collective-permute-start | bytes 393224 | tf_op jit(solution)/shard_map/ppermute | solution.py:204
  29.1 0.1 collective-permute-start.10
  29.2 0.3 collective-permute-done.7.refs_4_
  29.5 0.4 collective-permute-start.11
  29.9 0.2 collective-permute-start.12
  30.0 0.1 collective-permute-done.9.refs_6_
  30.1 0.4 collective-permute-done.10.refs_7_
  30.5 0.4 collective-permute-done.11.refs_8_
  30.8 0.4 collective-permute-done.12.refs_9_
  31.2 1.2 %count.1.counts_ref = f32[1,384]{1,0:T(1,128)S(1)} custom-call(bf16[64,1024]{1,0:T(8,128)(2,1)S(1)} %get-tuple-element.27.refs_0_, bf16[64,1024]{1,0:T(8,128)(2,1)S(1)} %get-tuple-element.28.refs_1_, bf16[128,1024]{1,0:T(8,128)(2,1)S(1)} %collective-permute-done.5.refs_0_.refs_2_, bf16[128,1024]{1,0:T(8,128)(2,1)S(1)} %collective-permute-done.6.refs_1_.refs_3_, ...), custom_call_target="tpu_custom_call" | custom-call | tf_op jit(solution)/shard_map/count/pallas_call | solution.py:94
  32.4 0.2 collective-permute-start.13
  32.7 1.1 %late.1 = (f32[1,768]{1,0:T(1,128)S(1)}, f32[1,128]{1,0:T(1,128)S(1)}) custom-call(bf16[64,1024]{1,0:T(8,128)(2,1)S(1)} %get-tuple-element.27.refs_0_, bf16[64,1024]{1,0:T(8,128)(2,1)S(1)} %get-tuple-element.28.refs_1_, bf16[128,1024]{1,0:T(8,128)(2,1)S(1)} %collective-permute-done.5.refs_0_.refs_2_, ...), custom_call_target="tpu_custom_call" | custom-call | tf_op jit(solution)/shard_map/late/pallas_call | solution.py:94
  33.8 0.2 collective-permute-done.13.other_ref
  34.0 0.3 finish.1
  34.3 9.0 %all_to_all.5.counts_ref = f32[16,1,64]{2,1,0:T(1,128)S(1)} all-to-all(f32[16,1,64]{2,1,0:T(1,128)S(1)} %finish.1), channel_id=1, replica_groups=mesh['groups'=2,'owner'=4,'helper'=2,'sub'=2] {'owner','helper','sub'}, dimensions={0} | all-to-all | bytes 8192 | tf_op jit(solution)/shard_map/all_to_all | solution.py:297
  43.3 0.7 %select.1 = f32[1,256]{1,0:T(1,128)} custom-call(f32[16,1,64]{2,1,0:T(1,128)S(1)} %all_to_all.5.counts_ref, s32[1,256]{1,0:T(1,128)S(1)} %get-tuple-element.23.refs_2_.slot_ref), custom_call_target="tpu_custom_call" | custom-call | tf_op jit(solution)/shard_map/select/pallas_call | solution.py:94
  (10 shorter events, 0.1 us)
Async XLA Ops:
  0.0 0.7 %copy-start.1 = (s32[256]{0:T(256)S(1)}, s32[256]{0:T(256)}, u32[]{:S(2)}) copy-start(s32[256]{0:T(256)} %param.3) | copy-start | bytes 3076
  0.0 6.3 %collective-permute-start = (bf16[256,1024]{1,0:T(8,128)(2,1)}, bf16[256,1024]{1,0:T(8,128)(2,1)S(1)}, u32[]{:S(2)}, u32[]{:S(2)}) collective-permute-start(bf16[256,1024]{1,0:T(8,128)(2,1)} %refs_0_.3), channel_id=1, source_target_pairs={{0,1},{1,0},{2,3},{3,2},{4,5},{5,4},{6,7},{7,6},{8,9},{9,8},{10,11... | collective-permute-start | bytes 1572872 | tf_op jit(solution)/shard_map/ppermute | solution.py:204
  0.7 5.6 %collective-permute-start.1 = (s32[1,256]{1,0:T(1,128)S(1)}, s32[1,256]{1,0:T(1,128)S(1)}, u32[]{:S(2)}, u32[]{:S(2)}) collective-permute-start(s32[1,256]{1,0:T(1,128)S(1)} %bitcast.2), channel_id=1, source_target_pairs={{0,1},{1,0},{2,3},{3,2},{4,5},{5,4},{6,7},{7,6},{8,9},{9,8},{10,11... | collective-permute-start | bytes 3080 | tf_op jit(solution)/shard_map/ppermute | solution.py:204
  1.1 1.0 %copy-start = (bf16[256,1024]{1,0:T(8,128)(2,1)S(1)}, bf16[256,1024]{1,0:T(8,128)(2,1)}, u32[]{:S(2)}) copy-start(bf16[256,1024]{1,0:T(8,128)(2,1)} %refs_0_.3) | copy-start | bytes 1572868
  2.6 10.2 %collective-permute-start.3 = (bf16[64,1024]{1,0:T(8,128)(2,1)S(1)}, bf16[64,1024]{1,0:T(8,128)(2,1)S(1)}, u32[]{:S(2)}, u32[]{:S(2)}) collective-permute-start(bf16[64,1024]{1,0:T(8,128)(2,1)S(1)} %get-tuple-element.25), channel_id=1, source_target_pairs={{0,8},{1,11},{2,10},{3,9},{4,12},{5,15},{6,14},{7,13},{8,0},{9,3},... | collective-permute-start | bytes 393224 | tf_op jit(solution)/shard_map/ppermute | solution.py:220
  6.9 21.7 %collective-permute-start.5 = (bf16[128,1024]{1,0:T(8,128)(2,1)S(1)}, bf16[128,1024]{1,0:T(8,128)(2,1)S(1)}, u32[]{:S(2)}, u32[]{:S(2)}) collective-permute-start(bf16[128,1024]{1,0:T(8,128)(2,1)S(1)} %get-tuple-element.22), channel_id=1, source_target_pairs={{0,0},{1,3},{2,2},{3,1},{4,4},{5,7},{6,6},{7,5},{8,8},{9,11},{10,1... | collective-permute-start | bytes 786440 | tf_op jit(solution)/shard_map/ppermute | solution.py:220
  7.6 21.0 %collective-permute-start.6 = (bf16[128,1024]{1,0:T(8,128)(2,1)S(1)}, bf16[128,1024]{1,0:T(8,128)(2,1)S(1)}, u32[]{:S(2)}, u32[]{:S(2)}) collective-permute-start(bf16[128,1024]{1,0:T(8,128)(2,1)S(1)} %get-tuple-element.29), channel_id=1, source_target_pairs={{0,4},{1,7},{2,6},{3,5},{4,0},{5,3},{6,2},{7,1},{8,12},{9,15},{10,... | collective-permute-start | bytes 786440 | tf_op jit(solution)/shard_map/ppermute | solution.py:220
  9.8 6.2 %collective-permute-start.4 = (bf16[64,1024]{1,0:T(8,128)(2,1)S(1)}, bf16[64,1024]{1,0:T(8,128)(2,1)S(1)}, u32[]{:S(2)}, u32[]{:S(2)}) collective-permute-start(bf16[64,1024]{1,0:T(8,128)(2,1)S(1)} %get-tuple-element.26), channel_id=1, source_target_pairs={{0,8},{1,11},{2,10},{3,9},{4,12},{5,15},{6,14},{7,13},{8,0},{9,3},... | collective-permute-start | bytes 393224 | tf_op jit(solution)/shard_map/ppermute | solution.py:220
  10.2 22.2 %collective-permute-start.2 = (bf16[128,1024]{1,0:T(8,128)(2,1)S(1)}, bf16[128,1024]{1,0:T(8,128)(2,1)S(1)}, u32[]{:S(2)}, u32[]{:S(2)}) collective-permute-start(bf16[128,1024]{1,0:T(8,128)(2,1)S(1)} %get-tuple-element.24), channel_id=1, source_target_pairs={{0,12},{1,15},{2,14},{3,13},{4,8},{5,11},{6,10},{7,9},{8,4},{9,7},... | collective-permute-start | bytes 786440 | tf_op jit(solution)/shard_map/ppermute | solution.py:220
  16.1 13.4 %collective-permute-start.7 = (bf16[64,1024]{1,0:T(8,128)(2,1)S(1)}, bf16[64,1024]{1,0:T(8,128)(2,1)S(1)}, u32[]{:S(2)}, u32[]{:S(2)}) collective-permute-start(bf16[64,1024]{1,0:T(8,128)(2,1)S(1)} %get-tuple-element.27.refs_0_), channel_id=1, source_target_pairs={{0,1},{1,0},{2,3},{3,2},{4,5},{5,4},{6,7},{7,6},{8,9},{9,8},{10,11... | collective-permute-start | bytes 393224 | tf_op jit(solution)/shard_map/ppermute | solution.py:204
  28.5 1.4 %collective-permute-start.8 = (bf16[64,1024]{1,0:T(8,128)(2,1)S(1)}, bf16[64,1024]{1,0:T(8,128)(2,1)S(1)}, u32[]{:S(2)}, u32[]{:S(2)}) collective-permute-start(bf16[64,1024]{1,0:T(8,128)(2,1)S(1)} %get-tuple-element.28.refs_1_), channel_id=1, source_target_pairs={{0,1},{1,0},{2,3},{3,2},{4,5},{5,4},{6,7},{7,6},{8,9},{9,8},{10,11... | collective-permute-start | bytes 393224 | tf_op jit(solution)/shard_map/ppermute | solution.py:204
  28.6 1.5 %collective-permute-start.9 = (bf16[64,1024]{1,0:T(8,128)(2,1)S(1)}, bf16[64,1024]{1,0:T(8,128)(2,1)S(1)}, u32[]{:S(2)}, u32[]{:S(2)}) collective-permute-start(bf16[64,1024]{1,0:T(8,128)(2,1)S(1)} %get-tuple-element.30), channel_id=1, source_target_pairs={{0,1},{1,0},{2,3},{3,2},{4,5},{5,4},{6,7},{7,6},{8,9},{9,8},{10,11... | collective-permute-start | bytes 393224 | tf_op jit(solution)/shard_map/ppermute | solution.py:204
  29.1 1.3 %collective-permute-start.10 = (bf16[64,1024]{1,0:T(8,128)(2,1)S(1)}, bf16[64,1024]{1,0:T(8,128)(2,1)S(1)}, u32[]{:S(2)}, u32[]{:S(2)}) collective-permute-start(bf16[64,1024]{1,0:T(8,128)(2,1)S(1)} %get-tuple-element.31), channel_id=1, source_target_pairs={{0,1},{1,0},{2,3},{3,2},{4,5},{5,4},{6,7},{7,6},{8,9},{9,8},{10,11... | collective-permute-start | bytes 393224 | tf_op jit(solution)/shard_map/ppermute | solution.py:204
  29.5 1.3 %collective-permute-start.11 = (bf16[64,1024]{1,0:T(8,128)(2,1)S(1)}, bf16[64,1024]{1,0:T(8,128)(2,1)S(1)}, u32[]{:S(2)}, u32[]{:S(2)}) collective-permute-start(bf16[64,1024]{1,0:T(8,128)(2,1)S(1)} %get-tuple-element.32), channel_id=1, source_target_pairs={{0,1},{1,0},{2,3},{3,2},{4,5},{5,4},{6,7},{7,6},{8,9},{9,8},{10,11... | collective-permute-start | bytes 393224 | tf_op jit(solution)/shard_map/ppermute | solution.py:204
  29.9 1.3 %collective-permute-start.12 = (bf16[64,1024]{1,0:T(8,128)(2,1)S(1)}, bf16[64,1024]{1,0:T(8,128)(2,1)S(1)}, u32[]{:S(2)}, u32[]{:S(2)}) collective-permute-start(bf16[64,1024]{1,0:T(8,128)(2,1)S(1)} %get-tuple-element.33), channel_id=1, source_target_pairs={{0,1},{1,0},{2,3},{3,2},{4,5},{5,4},{6,7},{7,6},{8,9},{9,8},{10,11... | collective-permute-start | bytes 393224 | tf_op jit(solution)/shard_map/ppermute | solution.py:204
  32.4 1.6 %collective-permute-start.13 = (bf16[128,1024]{1,0:T(8,128)(2,1)S(1)}, bf16[128,1024]{1,0:T(8,128)(2,1)S(1)}, u32[]{:S(2)}, u32[]{:S(2)}) collective-permute-start(bf16[128,1024]{1,0:T(8,128)(2,1)S(1)} %collective-permute-done.2.refs_10_.late_ref), channel_id=1, source_target_pairs={{0,1},{1,0},{2,3},{3,2},{4,5},{5,4},{6,7},{7,6},{8,9},{9,8},{10,11... | collective-permute-start | bytes 786440 | tf_op jit(solution)/shard_map/ppermute | solution.py:204

commit v24 on v23

--- a/solution.py
+++ b/solution.py
@@ -108,12 +108,12 @@
         out_ref[...] = in_ref[...]
 
 
-def halve_kernel(*refs):
-    pieces = len(refs) // 3
-    for k, piece in enumerate(refs[:pieces]):
-        first, second = refs[pieces + 2 * k : pieces + 2 * k + 2]
-        first[...] = piece[: first.shape[0]]
-        second[...] = piece[first.shape[0] :]
+def regroup_kernel(pieces, *refs):
+    rows = jnp.concatenate([ref[...] for ref in refs[:pieces]], axis=0)
+    first = 0
+    for part in refs[pieces:]:
+        part[...] = rows[first : first + part.shape[0]]
+        first += part.shape[0]
 
 
 def blocks(rows, starts, size):
@@ -253,15 +253,16 @@
     first_other, last_piece = route_rest("route_far", [first], [last], later_slot, 10**10)
     first_other, last_piece = across(first_other, first), across(last_piece, last)
 
-    firsts = call_kernel(
-        "pass", pass_kernel, [half] * 2, first_own, first_other
-    )
-    halves = call_kernel("halve", halve_kernel, [half] * (2 * len(near)), *near, flops=10**10)
-    early = [*firsts, *near]
-    early += [swap_cores(x) for x in (*firsts, *halves)]
+    (first_own,) = call_kernel("pass", pass_kernel, [half], first_own)
+    early = [first_own, first_other, *near]
+    half_way = cores * capacity * (steps - 1)
+    part = jax.ShapeDtypeStruct((half_way // 4, feature_count), jnp.bfloat16)
+    parts = call_kernel(
+        "regroup", functools.partial(regroup_kernel, len(early)), [part] * 4, *early, flops=10**10
+    )
+    early += [swap_cores(x) for x in parts]
 
     span = cores * capacity
-    half_way = span * (steps - 1)
     starts = [k * span for k in range(steps - 1)]
     starts += [half_way + start + capacity for start in starts]
     counts = soft_counts(early, starts, capacity)

time: 44.3 us -> 44 us (level)
  starting transfers between devices: 23.6 us -> 21.7 us
  waiting for transfers between devices: 5.04 us -> 6.02 us
  blocking collectives: 8.97 us -> 9.68 us
    ppermute x9 -> x7, starting transfers between devices: 14.8 us -> 10.7 us  [swap_cores(): return lax.ppermute(x, 'sub', [(i, i ^ 1) for i in range(cores)])]
    ppermute x5, starting transfers between devices: 8.85 us -> 11 us  [across(): return lax.ppermute(x, ('owner', 'helper', 'sub'), pairs)]
    ppermute x5, waiting for transfers between devices: 3.37 us -> 4.48 us  [across(): return lax.ppermute(x, ('owner', 'helper', 'sub'), pairs)]
    all_to_all x1, blocking collectives: 8.97 us -> 9.68 us  [body_by_chip(): lax.all_to_all(counts, ('owner', 'helper', 'sub'), split_axis=0, concat_a...]
    ppermute x9 -> x7, waiting for transfers between devices: 1.67 us -> 1.54 us  [swap_cores(): return lax.ppermute(x, 'sub', [(i, i ^ 1) for i in range(cores)])]
  transfers between devices with their start and end apart: 14 -> 12, of which waited for: 8 -> 7; matrix products, arithmetic and copies ran while one was open for 0% -> 0% of each run, Pallas kernels for 9% -> 9%
where the time goes in v24:
time: 44 us; the launch traced here: 43.8 us
  starting transfers between devices  21.7 us (49%)
  blocking collectives  9.68 us (22%)
  waiting for transfers between devices  6.02 us (14%)
  Pallas kernels  5.11 us (12%)
  local copies, waits for them, and re-layouts  1.27 us (3%)
    ppermute x5, starting transfers between devices, across(): return lax.ppermute(x, ('owner', 'helper', 'sub'), pairs)  11 us
    ppermute x7, starting transfers between devices, swap_cores(): return lax.ppermute(x, 'sub', [(i, i ^ 1) for i in range(cores)])  10.7 us
    all_to_all x1, blocking collectives, body_by_chip(): lax.all_to_all(counts, ('owner', 'helper', 'sub'), split_axis=0, concat_a...  9.68 us
    pallas_call x9, Pallas kernels, call_kernel(): pl.pallas_call(kernel, out_shape=out_shape, in_specs=[VMEM] * len(args),...  5.11 us
    ppermute x5, waiting for transfers between devices, across(): return lax.ppermute(x, ('owner', 'helper', 'sub'), pairs)  4.48 us
    ppermute x7, waiting for transfers between devices, swap_cores(): return lax.ppermute(x, 'sub', [(i, i ^ 1) for i in range(cores)])  1.54 us
    unnamed x4, local copies, waits for them, and re-layouts  1.27 us
  transfers between devices with their start and end apart: 12, of which 7 were waited for; matrix products, arithmetic and copies ran while one was open for 0% of the time, Pallas kernels for 9%

profile of v24, /device:TPU:0, one launch (start us, length us, event | category | flops | bytes accessed | tf_op | source)
XLA Modules:
  0.0 43.8 jit_solution(18266081905023549138)
XLA Ops:
  0.0 0.5 %collective-permute-start = (bf16[256,1024]{1,0:T(8,128)(2,1)}, bf16[256,1024]{1,0:T(8,128)(2,1)S(1)}, u32[]{:S(2)}, u32[]{:S(2)}) collective-permute-start(bf16[256,1024]{1,0:T(8,128)(2,1)} %refs_0_.3), channel_id=1, source_target_pairs={{0,1},{1,0},{2,3},{3,2},{4,5},{5,4},{6,7},{7,6},{8,9},{9,8},{10,11... | collective-permute-start | bytes 1572872 | tf_op jit(solution)/shard_map/ppermute | solution.py:204
  0.5 0.2 copy-done.1
  0.7 0.5 %collective-permute-start.1 = (s32[1,256]{1,0:T(1,128)S(1)}, s32[1,256]{1,0:T(1,128)S(1)}, u32[]{:S(2)}, u32[]{:S(2)}) collective-permute-start(s32[1,256]{1,0:T(1,128)S(1)} %bitcast.2), channel_id=1, source_target_pairs={{0,1},{1,0},{2,3},{3,2},{4,5},{5,4},{6,7},{7,6},{8,9},{9,8},{10,11... | collective-permute-start | bytes 3080 | tf_op jit(solution)/shard_map/ppermute | solution.py:204
  1.1 1.0 %copy-done = bf16[256,1024]{1,0:T(8,128)(2,1)S(1)} copy-done((bf16[256,1024]{1,0:T(8,128)(2,1)S(1)}, bf16[256,1024]{1,0:T(8,128)(2,1)}, u32[]{:S(2)}) %copy-start) | copy-done | bytes 524312
  2.2 0.5 %route_first.1 = (bf16[64,1024]{1,0:T(8,128)(2,1)S(1)}, s32[1,256]{1,0:T(1,128)S(1)}) custom-call(bf16[256,1024]{1,0:T(8,128)(2,1)S(1)} %copy-done, s32[1,256]{1,0:T(1,128)S(1)} %bitcast.3), custom_call_target="tpu_custom_call" | custom-call | tf_op jit(solution)/shard_map/route_first/pallas_call | solution.py:94
  2.6 3.7 %collective-permute-start.3 = (bf16[64,1024]{1,0:T(8,128)(2,1)S(1)}, bf16[64,1024]{1,0:T(8,128)(2,1)S(1)}, u32[]{:S(2)}, u32[]{:S(2)}) collective-permute-start(bf16[64,1024]{1,0:T(8,128)(2,1)S(1)} %get-tuple-element.23), channel_id=1, source_target_pairs={{0,8},{1,11},{2,10},{3,9},{4,12},{5,15},{6,14},{7,13},{8,0},{9,3},... | collective-permute-start | bytes 393224 | tf_op jit(solution)/shard_map/ppermute | solution.py:220
  6.3 0.0 collective-permute-done.1.refs_3_
  6.3 0.0 collective-permute-done.refs_1_
  6.3 0.6 %route_near.1 = (bf16[128,1024]{1,0:T(8,128)(2,1)S(1)}, bf16[128,1024]{1,0:T(8,128)(2,1)S(1)}) custom-call(bf16[256,1024]{1,0:T(8,128)(2,1)S(1)} %copy-done, bf16[256,1024]{1,0:T(8,128)(2,1)S(1)} %collective-permute-done.refs_1_, s32[1,256]{1,0:T(1,128)S(1)} %get-tuple-element.21.refs_2_.slot_ref, s32[1,256]{1,0:T(1,128)S(1)} %collective-permute-done.1.refs_3_), custom_call_target="tpu_custom_call" | custom-call | tf_op jit(solution)/shard_map/route_near/pallas_call | solution.py:94
  6.9 0.7 %collective-permute-start.5 = (bf16[128,1024]{1,0:T(8,128)(2,1)S(1)}, bf16[128,1024]{1,0:T(8,128)(2,1)S(1)}, u32[]{:S(2)}, u32[]{:S(2)}) collective-permute-start(bf16[128,1024]{1,0:T(8,128)(2,1)S(1)} %get-tuple-element.20), channel_id=1, source_target_pairs={{0,0},{1,3},{2,2},{3,1},{4,4},{5,7},{6,6},{7,5},{8,8},{9,11},{10,1... | collective-permute-start | bytes 786440 | tf_op jit(solution)/shard_map/ppermute | solution.py:220
  7.6 1.6 %collective-permute-start.6 = (bf16[128,1024]{1,0:T(8,128)(2,1)S(1)}, bf16[128,1024]{1,0:T(8,128)(2,1)S(1)}, u32[]{:S(2)}, u32[]{:S(2)}) collective-permute-start(bf16[128,1024]{1,0:T(8,128)(2,1)S(1)} %get-tuple-element.25), channel_id=1, source_target_pairs={{0,4},{1,7},{2,6},{3,5},{4,0},{5,3},{6,2},{7,1},{8,12},{9,15},{10,... | collective-permute-start | bytes 786440 | tf_op jit(solution)/shard_map/ppermute | solution.py:220
  9.2 0.6 %route_far.1 = (bf16[64,1024]{1,0:T(8,128)(2,1)S(1)}, bf16[128,1024]{1,0:T(8,128)(2,1)S(1)}) custom-call(bf16[256,1024]{1,0:T(8,128)(2,1)S(1)} %copy-done, bf16[256,1024]{1,0:T(8,128)(2,1)S(1)} %collective-permute-done.refs_1_, s32[1,256]{1,0:T(1,128)S(1)} %get-tuple-element.21.refs_2_.slot_ref, s32[1,256]{1,0:T(1,128)S(1)} %collective-permute-done.1.refs_3_), custom_call_target="tpu_custom_call" | custom-call | flops 10000000000 | tf_op jit(solution)/shard_map/route_far/pallas_call | solution.py:94
  9.8 0.4 collective-permute-start.4
  10.2 2.6 %collective-permute-done.3.refs_0_ = bf16[64,1024]{1,0:T(8,128)(2,1)S(1)} collective-permute-done((bf16[64,1024]{1,0:T(8,128)(2,1)S(1)}, bf16[64,1024]{1,0:T(8,128)(2,1)S(1)}, u32[]{:S(2)}, u32[]{:S(2)}) %collective-permute-start.3) | collective-permute-done | bytes 131104 | tf_op jit(solution)/shard_map/ppermute | solution.py:220
  12.8 4.6 %collective-permute-start.2 = (bf16[128,1024]{1,0:T(8,128)(2,1)S(1)}, bf16[128,1024]{1,0:T(8,128)(2,1)S(1)}, u32[]{:S(2)}, u32[]{:S(2)}) collective-permute-start(bf16[128,1024]{1,0:T(8,128)(2,1)S(1)} %get-tuple-element.22), channel_id=1, source_target_pairs={{0,12},{1,15},{2,14},{3,13},{4,8},{5,11},{6,10},{7,9},{8,4},{9,7},... | collective-permute-start | bytes 786440 | tf_op jit(solution)/shard_map/ppermute | solution.py:220
  17.4 1.9 %collective-permute-done.6.refs_3_ = bf16[128,1024]{1,0:T(8,128)(2,1)S(1)} collective-permute-done((bf16[128,1024]{1,0:T(8,128)(2,1)S(1)}, bf16[128,1024]{1,0:T(8,128)(2,1)S(1)}, u32[]{:S(2)}, u32[]{:S(2)}) %collective-permute-start.6) | collective-permute-done | bytes 262176 | tf_op jit(solution)/shard_map/ppermute | solution.py:220
  19.3 0.1 regroup.1
  19.4 8.9 %collective-permute-start.7 = (bf16[96,1024]{1,0:T(8,128)(2,1)S(1)}, bf16[96,1024]{1,0:T(8,128)(2,1)S(1)}, u32[]{:S(2)}, u32[]{:S(2)}) collective-permute-start(bf16[96,1024]{1,0:T(8,128)(2,1)S(1)} %get-tuple-element.26), channel_id=1, source_target_pairs={{0,1},{1,0},{2,3},{3,2},{4,5},{5,4},{6,7},{7,6},{8,9},{9,8},{10,11... | collective-permute-start | bytes 589832 | tf_op jit(solution)/shard_map/ppermute | solution.py:204
  28.3 0.1 collective-permute-start.8
  28.3 0.4 collective-permute-start.9
  28.8 0.1 collective-permute-start.10
  28.8 0.5 %collective-permute-done.7.refs_4_ = bf16[96,1024]{1,0:T(8,128)(2,1)S(1)} collective-permute-done((bf16[96,1024]{1,0:T(8,128)(2,1)S(1)}, bf16[96,1024]{1,0:T(8,128)(2,1)S(1)}, u32[]{:S(2)}, u32[]{:S(2)}) %collective-permute-start.7) | collective-permute-done | bytes 196640 | tf_op jit(solution)/shard_map/ppermute | solution.py:204
  29.3 0.4 collective-permute-done.8.refs_5_
  29.7 0.3 collective-permute-done.9.refs_6_
  30.0 0.3 collective-permute-done.10.refs_7_
  30.3 1.2 %count.1.counts_ref = f32[1,384]{1,0:T(1,128)S(1)} custom-call(bf16[64,1024]{1,0:T(8,128)(2,1)S(1)} %pass.1.refs_0_, bf16[64,1024]{1,0:T(8,128)(2,1)S(1)} %collective-permute-done.4.refs_1_, bf16[128,1024]{1,0:T(8,128)(2,1)S(1)} %collective-permute-done.5.refs_2_, bf16[128,1024]{1,0:T(8,128)(2,1)S(1)} %collective-permute-done.6.refs_3_, ...), custom_call_target="tpu_custom_call" | custom-call | tf_op jit(solution)/shard_map/count/pallas_call | solution.py:94
  31.5 0.3 collective-permute-start.11
  31.8 1.1 %late.1 = (f32[1,768]{1,0:T(1,128)S(1)}, f32[1,128]{1,0:T(1,128)S(1)}) custom-call(bf16[64,1024]{1,0:T(8,128)(2,1)S(1)} %pass.1.refs_0_, bf16[64,1024]{1,0:T(8,128)(2,1)S(1)} %collective-permute-done.4.refs_1_, bf16[128,1024]{1,0:T(8,128)(2,1)S(1)} %collective-permute-done.5.refs_2_, bf16[128,1024]{1,0:T(8,128)(2,1)S(1)} %collective-permute-done.6.refs_3_, ...), custom_call_target="tpu_custom_call" | custom-call | tf_op jit(solution)/shard_map/late/pallas_call | solution.py:94
  33.0 0.1 collective-permute-done.11.other_ref
  33.1 0.3 finish.1
  33.4 9.7 %all_to_all.5.counts_ref = f32[16,1,64]{2,1,0:T(1,128)S(1)} all-to-all(f32[16,1,64]{2,1,0:T(1,128)S(1)} %finish.1), channel_id=1, replica_groups=mesh['groups'=2,'owner'=4,'helper'=2,'sub'=2] {'owner','helper','sub'}, dimensions={0} | all-to-all | bytes 8192 | tf_op jit(solution)/shard_map/all_to_all | solution.py:298
  43.1 0.7 %select.1 = f32[1,256]{1,0:T(1,128)} custom-call(f32[16,1,64]{2,1,0:T(1,128)S(1)} %all_to_all.5.counts_ref, s32[1,256]{1,0:T(1,128)S(1)} %get-tuple-element.21.refs_2_.slot_ref), custom_call_target="tpu_custom_call" | custom-call | tf_op jit(solution)/shard_map/select/pallas_call | solution.py:94
  (6 shorter events, 0.0 us)
Async XLA Ops:
  0.0 0.7 %copy-start.1 = (s32[256]{0:T(256)S(1)}, s32[256]{0:T(256)}, u32[]{:S(2)}) copy-start(s32[256]{0:T(256)} %param.3) | copy-start | bytes 3076
  0.0 6.3 %collective-permute-start = (bf16[256,1024]{1,0:T(8,128)(2,1)}, bf16[256,1024]{1,0:T(8,128)(2,1)S(1)}, u32[]{:S(2)}, u32[]{:S(2)}) collective-permute-start(bf16[256,1024]{1,0:T(8,128)(2,1)} %refs_0_.3), channel_id=1, source_target_pairs={{0,1},{1,0},{2,3},{3,2},{4,5},{5,4},{6,7},{7,6},{8,9},{9,8},{10,11... | collective-permute-start | bytes 1572872 | tf_op jit(solution)/shard_map/ppermute | solution.py:204
  0.7 5.6 %collective-permute-start.1 = (s32[1,256]{1,0:T(1,128)S(1)}, s32[1,256]{1,0:T(1,128)S(1)}, u32[]{:S(2)}, u32[]{:S(2)}) collective-permute-start(s32[1,256]{1,0:T(1,128)S(1)} %bitcast.2), channel_id=1, source_target_pairs={{0,1},{1,0},{2,3},{3,2},{4,5},{5,4},{6,7},{7,6},{8,9},{9,8},{10,11... | collective-permute-start | bytes 3080 | tf_op jit(solution)/shard_map/ppermute | solution.py:204
  1.1 1.0 %copy-start = (bf16[256,1024]{1,0:T(8,128)(2,1)S(1)}, bf16[256,1024]{1,0:T(8,128)(2,1)}, u32[]{:S(2)}) copy-start(bf16[256,1024]{1,0:T(8,128)(2,1)} %refs_0_.3) | copy-start | bytes 1572868
  2.6 10.2 %collective-permute-start.3 = (bf16[64,1024]{1,0:T(8,128)(2,1)S(1)}, bf16[64,1024]{1,0:T(8,128)(2,1)S(1)}, u32[]{:S(2)}, u32[]{:S(2)}) collective-permute-start(bf16[64,1024]{1,0:T(8,128)(2,1)S(1)} %get-tuple-element.23), channel_id=1, source_target_pairs={{0,8},{1,11},{2,10},{3,9},{4,12},{5,15},{6,14},{7,13},{8,0},{9,3},... | collective-permute-start | bytes 393224 | tf_op jit(solution)/shard_map/ppermute | solution.py:220
  6.9 12.4 %collective-permute-start.5 = (bf16[128,1024]{1,0:T(8,128)(2,1)S(1)}, bf16[128,1024]{1,0:T(8,128)(2,1)S(1)}, u32[]{:S(2)}, u32[]{:S(2)}) collective-permute-start(bf16[128,1024]{1,0:T(8,128)(2,1)S(1)} %get-tuple-element.20), channel_id=1, source_target_pairs={{0,0},{1,3},{2,2},{3,1},{4,4},{5,7},{6,6},{7,5},{8,8},{9,11},{10,1... | collective-permute-start | bytes 786440 | tf_op jit(solution)/shard_map/ppermute | solution.py:220
  7.6 11.7 %collective-permute-start.6 = (bf16[128,1024]{1,0:T(8,128)(2,1)S(1)}, bf16[128,1024]{1,0:T(8,128)(2,1)S(1)}, u32[]{:S(2)}, u32[]{:S(2)}) collective-permute-start(bf16[128,1024]{1,0:T(8,128)(2,1)S(1)} %get-tuple-element.25), channel_id=1, source_target_pairs={{0,4},{1,7},{2,6},{3,5},{4,0},{5,3},{6,2},{7,1},{8,12},{9,15},{10,... | collective-permute-start | bytes 786440 | tf_op jit(solution)/shard_map/ppermute | solution.py:220
  9.8 7.6 %collective-permute-start.4 = (bf16[64,1024]{1,0:T(8,128)(2,1)S(1)}, bf16[64,1024]{1,0:T(8,128)(2,1)S(1)}, u32[]{:S(2)}, u32[]{:S(2)}) collective-permute-start(bf16[64,1024]{1,0:T(8,128)(2,1)S(1)} %get-tuple-element.24), channel_id=1, source_target_pairs={{0,8},{1,11},{2,10},{3,9},{4,12},{5,15},{6,14},{7,13},{8,0},{9,3},... | collective-permute-start | bytes 393224 | tf_op jit(solution)/shard_map/ppermute | solution.py:220
  12.8 18.7 %collective-permute-start.2 = (bf16[128,1024]{1,0:T(8,128)(2,1)S(1)}, bf16[128,1024]{1,0:T(8,128)(2,1)S(1)}, u32[]{:S(2)}, u32[]{:S(2)}) collective-permute-start(bf16[128,1024]{1,0:T(8,128)(2,1)S(1)} %get-tuple-element.22), channel_id=1, source_target_pairs={{0,12},{1,15},{2,14},{3,13},{4,8},{5,11},{6,10},{7,9},{8,4},{9,7},... | collective-permute-start | bytes 786440 | tf_op jit(solution)/shard_map/ppermute | solution.py:220
  19.4 9.9 %collective-permute-start.7 = (bf16[96,1024]{1,0:T(8,128)(2,1)S(1)}, bf16[96,1024]{1,0:T(8,128)(2,1)S(1)}, u32[]{:S(2)}, u32[]{:S(2)}) collective-permute-start(bf16[96,1024]{1,0:T(8,128)(2,1)S(1)} %get-tuple-element.26), channel_id=1, source_target_pairs={{0,1},{1,0},{2,3},{3,2},{4,5},{5,4},{6,7},{7,6},{8,9},{9,8},{10,11... | collective-permute-start | bytes 589832 | tf_op jit(solution)/shard_map/ppermute | solution.py:204
  28.3 1.4 %collective-permute-start.8 = (bf16[96,1024]{1,0:T(8,128)(2,1)S(1)}, bf16[96,1024]{1,0:T(8,128)(2,1)S(1)}, u32[]{:S(2)}, u32[]{:S(2)}) collective-permute-start(bf16[96,1024]{1,0:T(8,128)(2,1)S(1)} %get-tuple-element.27), channel_id=1, source_target_pairs={{0,1},{1,0},{2,3},{3,2},{4,5},{5,4},{6,7},{7,6},{8,9},{9,8},{10,11... | collective-permute-start | bytes 589832 | tf_op jit(solution)/shard_map/ppermute | solution.py:204
  28.3 1.6 %collective-permute-start.9 = (bf16[96,1024]{1,0:T(8,128)(2,1)S(1)}, bf16[96,1024]{1,0:T(8,128)(2,1)S(1)}, u32[]{:S(2)}, u32[]{:S(2)}) collective-permute-start(bf16[96,1024]{1,0:T(8,128)(2,1)S(1)} %get-tuple-element.28), channel_id=1, source_target_pairs={{0,1},{1,0},{2,3},{3,2},{4,5},{5,4},{6,7},{7,6},{8,9},{9,8},{10,11... | collective-permute-start | bytes 589832 | tf_op jit(solution)/shard_map/ppermute | solution.py:204
  28.8 1.5 %collective-permute-start.10 = (bf16[96,1024]{1,0:T(8,128)(2,1)S(1)}, bf16[96,1024]{1,0:T(8,128)(2,1)S(1)}, u32[]{:S(2)}, u32[]{:S(2)}) collective-permute-start(bf16[96,1024]{1,0:T(8,128)(2,1)S(1)} %get-tuple-element.29), channel_id=1, source_target_pairs={{0,1},{1,0},{2,3},{3,2},{4,5},{5,4},{6,7},{7,6},{8,9},{9,8},{10,11... | collective-permute-start | bytes 589832 | tf_op jit(solution)/shard_map/ppermute | solution.py:204
  31.5 1.6 %collective-permute-start.11 = (bf16[128,1024]{1,0:T(8,128)(2,1)S(1)}, bf16[128,1024]{1,0:T(8,128)(2,1)S(1)}, u32[]{:S(2)}, u32[]{:S(2)}) collective-permute-start(bf16[128,1024]{1,0:T(8,128)(2,1)S(1)} %collective-permute-done.2.refs_8_.late_ref), channel_id=1, source_target_pairs={{0,1},{1,0},{2,3},{3,2},{4,5},{5,4},{6,7},{7,6},{8,9},{9,8},{10,11... | collective-permute-start | bytes 786440 | tf_op jit(solution)/shard_map/ppermute | solution.py:204

commit v25 on v24

--- a/solution.py
+++ b/solution.py
@@ -221,7 +221,7 @@
 
     ids = cluster_id.reshape(1, doc_count)
     other_rows, other_ids = swap_cores(embeddings), swap_cores(ids)
-    first, last = steps // 2, steps - 1
+    first, last = steps - 1, steps // 2
     middle = [p for p in range(steps) if p not in (first, last)]
     half = jax.ShapeDtypeStruct((capacity, feature_count), jnp.bfloat16)
     whole = jax.ShapeDtypeStruct((cores * capacity, feature_count), jnp.bfloat16)

time: 44 us -> 45 us (1.023)
  waiting for transfers between devices: 6.02 us -> 10.7 us
  starting transfers between devices: 21.7 us -> 17.5 us
    ppermute x5, waiting for transfers between devices: 4.48 us -> 9.29 us  [across(): return lax.ppermute(x, ('owner', 'helper', 'sub'), pairs)]
    ppermute x7, starting transfers between devices: 10.7 us -> 7.08 us  [swap_cores(): return lax.ppermute(x, 'sub', [(i, i ^ 1) for i in range(cores)])]
    ppermute x5, starting transfers between devices: 11 us -> 10.4 us  [across(): return lax.ppermute(x, ('owner', 'helper', 'sub'), pairs)]
where the time goes in v25:
time: 45 us; the launch traced here: 44.8 us
  starting transfers between devices  17.5 us (39%)
  waiting for transfers between devices  10.7 us (24%)
  blocking collectives  10.1 us (22%)
  Pallas kernels  5.11 us (11%)
  local copies, waits for them, and re-layouts  1.27 us (3%)
    ppermute x5, starting transfers between devices, across(): return lax.ppermute(x, ('owner', 'helper', 'sub'), pairs)  10.4 us
    all_to_all x1, blocking collectives, body_by_chip(): lax.all_to_all(counts, ('owner', 'helper', 'sub'), split_axis=0, concat_a...  10.1 us
    ppermute x5, waiting for transfers between devices, across(): return lax.ppermute(x, ('owner', 'helper', 'sub'), pairs)  9.29 us
    ppermute x7, starting transfers between devices, swap_cores(): return lax.ppermute(x, 'sub', [(i, i ^ 1) for i in range(cores)])  7.08 us
    pallas_call x9, Pallas kernels, call_kernel(): pl.pallas_call(kernel, out_shape=out_shape, in_specs=[VMEM] * len(args),...  5.11 us
    ppermute x7, waiting for transfers between devices, swap_cores(): return lax.ppermute(x, 'sub', [(i, i ^ 1) for i in range(cores)])  1.44 us
    unnamed x4, local copies, waits for them, and re-layouts  1.27 us
  transfers between devices with their start and end apart: 12, of which 7 were waited for; matrix products, arithmetic and copies ran while one was open for 0% of the time, Pallas kernels for 9%

profile of v25, /device:TPU:0, one launch (start us, length us, event | category | flops | bytes accessed | tf_op | source)
XLA Modules:
  0.0 44.8 jit_solution(2551461602457879496)
XLA Ops:
  0.0 0.5 %collective-permute-start = (bf16[256,1024]{1,0:T(8,128)(2,1)}, bf16[256,1024]{1,0:T(8,128)(2,1)S(1)}, u32[]{:S(2)}, u32[]{:S(2)}) collective-permute-start(bf16[256,1024]{1,0:T(8,128)(2,1)} %refs_0_.3), channel_id=1, source_target_pairs={{0,1},{1,0},{2,3},{3,2},{4,5},{5,4},{6,7},{7,6},{8,9},{9,8},{10,11... | collective-permute-start | bytes 1572872 | tf_op jit(solution)/shard_map/ppermute | solution.py:204
  0.5 0.2 copy-done.1
  0.7 0.5 %collective-permute-start.1 = (s32[1,256]{1,0:T(1,128)S(1)}, s32[1,256]{1,0:T(1,128)S(1)}, u32[]{:S(2)}, u32[]{:S(2)}) collective-permute-start(s32[1,256]{1,0:T(1,128)S(1)} %bitcast.2), channel_id=1, source_target_pairs={{0,1},{1,0},{2,3},{3,2},{4,5},{5,4},{6,7},{7,6},{8,9},{9,8},{10,11... | collective-permute-start | bytes 3080 | tf_op jit(solution)/shard_map/ppermute | solution.py:204
  1.1 1.0 %copy-done = bf16[256,1024]{1,0:T(8,128)(2,1)S(1)} copy-done((bf16[256,1024]{1,0:T(8,128)(2,1)S(1)}, bf16[256,1024]{1,0:T(8,128)(2,1)}, u32[]{:S(2)}) %copy-start) | copy-done | bytes 524312
  2.2 0.5 %route_first.1 = (bf16[64,1024]{1,0:T(8,128)(2,1)S(1)}, s32[1,256]{1,0:T(1,128)S(1)}) custom-call(bf16[256,1024]{1,0:T(8,128)(2,1)S(1)} %copy-done, s32[1,256]{1,0:T(1,128)S(1)} %bitcast.3), custom_call_target="tpu_custom_call" | custom-call | tf_op jit(solution)/shard_map/route_first/pallas_call | solution.py:94
  2.6 4.7 %collective-permute-start.3 = (bf16[64,1024]{1,0:T(8,128)(2,1)S(1)}, bf16[64,1024]{1,0:T(8,128)(2,1)S(1)}, u32[]{:S(2)}, u32[]{:S(2)}) collective-permute-start(bf16[64,1024]{1,0:T(8,128)(2,1)S(1)} %get-tuple-element.23), channel_id=1, source_target_pairs={{0,12},{1,15},{2,14},{3,13},{4,8},{5,11},{6,10},{7,9},{8,4},{9,7},... | collective-permute-start | bytes 393224 | tf_op jit(solution)/shard_map/ppermute | solution.py:220
  7.3 0.0 collective-permute-done.refs_1_
  7.3 0.6 %route_near.1 = (bf16[128,1024]{1,0:T(8,128)(2,1)S(1)}, bf16[128,1024]{1,0:T(8,128)(2,1)S(1)}) custom-call(bf16[256,1024]{1,0:T(8,128)(2,1)S(1)} %copy-done, bf16[256,1024]{1,0:T(8,128)(2,1)S(1)} %collective-permute-done.refs_1_, s32[1,256]{1,0:T(1,128)S(1)} %get-tuple-element.21.refs_2_.slot_ref, s32[1,256]{1,0:T(1,128)S(1)} %collective-permute-done.1.refs_3_), custom_call_target="tpu_custom_call" | custom-call | tf_op jit(solution)/shard_map/route_near/pallas_call | solution.py:94
  7.9 0.7 %collective-permute-start.5 = (bf16[128,1024]{1,0:T(8,128)(2,1)S(1)}, bf16[128,1024]{1,0:T(8,128)(2,1)S(1)}, u32[]{:S(2)}, u32[]{:S(2)}) collective-permute-start(bf16[128,1024]{1,0:T(8,128)(2,1)S(1)} %get-tuple-element.20), channel_id=1, source_target_pairs={{0,0},{1,3},{2,2},{3,1},{4,4},{5,7},{6,6},{7,5},{8,8},{9,11},{10,1... | collective-permute-start | bytes 786440 | tf_op jit(solution)/shard_map/ppermute | solution.py:220
  8.6 0.1 collective-permute-start.6
  8.7 0.6 %route_far.1 = (bf16[64,1024]{1,0:T(8,128)(2,1)S(1)}, bf16[128,1024]{1,0:T(8,128)(2,1)S(1)}) custom-call(bf16[256,1024]{1,0:T(8,128)(2,1)S(1)} %copy-done, bf16[256,1024]{1,0:T(8,128)(2,1)S(1)} %collective-permute-done.refs_1_, s32[1,256]{1,0:T(1,128)S(1)} %get-tuple-element.21.refs_2_.slot_ref, s32[1,256]{1,0:T(1,128)S(1)} %collective-permute-done.1.refs_3_), custom_call_target="tpu_custom_call" | custom-call | flops 10000000000 | tf_op jit(solution)/shard_map/route_far/pallas_call | solution.py:94
  9.3 0.9 %collective-permute-start.4 = (bf16[64,1024]{1,0:T(8,128)(2,1)S(1)}, bf16[64,1024]{1,0:T(8,128)(2,1)S(1)}, u32[]{:S(2)}, u32[]{:S(2)}) collective-permute-start(bf16[64,1024]{1,0:T(8,128)(2,1)S(1)} %get-tuple-element.24), channel_id=1, source_target_pairs={{0,12},{1,15},{2,14},{3,13},{4,8},{5,11},{6,10},{7,9},{8,4},{9,7},... | collective-permute-start | bytes 393224 | tf_op jit(solution)/shard_map/ppermute | solution.py:220
  10.2 0.9 %collective-permute-done.3.refs_0_ = bf16[64,1024]{1,0:T(8,128)(2,1)S(1)} collective-permute-done((bf16[64,1024]{1,0:T(8,128)(2,1)S(1)}, bf16[64,1024]{1,0:T(8,128)(2,1)S(1)}, u32[]{:S(2)}, u32[]{:S(2)}) %collective-permute-start.3) | collective-permute-done | bytes 131104 | tf_op jit(solution)/shard_map/ppermute | solution.py:220
  11.1 4.0 %collective-permute-start.2 = (bf16[128,1024]{1,0:T(8,128)(2,1)S(1)}, bf16[128,1024]{1,0:T(8,128)(2,1)S(1)}, u32[]{:S(2)}, u32[]{:S(2)}) collective-permute-start(bf16[128,1024]{1,0:T(8,128)(2,1)S(1)} %get-tuple-element.22), channel_id=1, source_target_pairs={{0,8},{1,11},{2,10},{3,9},{4,12},{5,15},{6,14},{7,13},{8,0},{9,3},... | collective-permute-start | bytes 786440 | tf_op jit(solution)/shard_map/ppermute | solution.py:220
  15.2 3.8 %collective-permute-done.4.refs_1_ = bf16[64,1024]{1,0:T(8,128)(2,1)S(1)} collective-permute-done((bf16[64,1024]{1,0:T(8,128)(2,1)S(1)}, bf16[64,1024]{1,0:T(8,128)(2,1)S(1)}, u32[]{:S(2)}, u32[]{:S(2)}) %collective-permute-start.4) | collective-permute-done | bytes 131104 | tf_op jit(solution)/shard_map/ppermute | solution.py:220
  19.0 0.1 regroup.1
  19.0 3.2 %collective-permute-start.7 = (bf16[96,1024]{1,0:T(8,128)(2,1)S(1)}, bf16[96,1024]{1,0:T(8,128)(2,1)S(1)}, u32[]{:S(2)}, u32[]{:S(2)}) collective-permute-start(bf16[96,1024]{1,0:T(8,128)(2,1)S(1)} %get-tuple-element.26), channel_id=1, source_target_pairs={{0,1},{1,0},{2,3},{3,2},{4,5},{5,4},{6,7},{7,6},{8,9},{9,8},{10,11... | collective-permute-start | bytes 589832 | tf_op jit(solution)/shard_map/ppermute | solution.py:204
  22.2 0.1 collective-permute-start.8
  22.3 0.4 collective-permute-start.9
  22.7 0.1 collective-permute-start.10
  22.8 0.5 %collective-permute-done.7.refs_4_ = bf16[96,1024]{1,0:T(8,128)(2,1)S(1)} collective-permute-done((bf16[96,1024]{1,0:T(8,128)(2,1)S(1)}, bf16[96,1024]{1,0:T(8,128)(2,1)S(1)}, u32[]{:S(2)}, u32[]{:S(2)}) %collective-permute-start.7) | collective-permute-done | bytes 196640 | tf_op jit(solution)/shard_map/ppermute | solution.py:204
  23.3 0.4 collective-permute-done.8.refs_5_
  23.7 0.3 collective-permute-done.9.refs_6_
  23.9 0.3 collective-permute-done.10.refs_7_
  24.2 1.2 %count.1.counts_ref = f32[1,384]{1,0:T(1,128)S(1)} custom-call(bf16[64,1024]{1,0:T(8,128)(2,1)S(1)} %pass.1.refs_0_, bf16[64,1024]{1,0:T(8,128)(2,1)S(1)} %collective-permute-done.4.refs_1_, bf16[128,1024]{1,0:T(8,128)(2,1)S(1)} %collective-permute-done.5.refs_2_, bf16[128,1024]{1,0:T(8,128)(2,1)S(1)} %collective-permute-done.6.refs_3_, ...), custom_call_target="tpu_custom_call" | custom-call | tf_op jit(solution)/shard_map/count/pallas_call | solution.py:94
  25.4 4.6 %collective-permute-done.2.refs_8_.late_ref = bf16[128,1024]{1,0:T(8,128)(2,1)S(1)} collective-permute-done((bf16[128,1024]{1,0:T(8,128)(2,1)S(1)}, bf16[128,1024]{1,0:T(8,128)(2,1)S(1)}, u32[]{:S(2)}, u32[]{:S(2)}) %collective-permute-start.2) | collective-permute-done | bytes 262176 | tf_op jit(solution)/shard_map/ppermute | solution.py:220
  30.0 2.4 %collective-permute-start.11 = (bf16[128,1024]{1,0:T(8,128)(2,1)S(1)}, bf16[128,1024]{1,0:T(8,128)(2,1)S(1)}, u32[]{:S(2)}, u32[]{:S(2)}) collective-permute-start(bf16[128,1024]{1,0:T(8,128)(2,1)S(1)} %collective-permute-done.2.refs_8_.late_ref), channel_id=1, source_target_pairs={{0,1},{1,0},{2,3},{3,2},{4,5},{5,4},{6,7},{7,6},{8,9},{9,8},{10,11... | collective-permute-start | bytes 786440 | tf_op jit(solution)/shard_map/ppermute | solution.py:204
  32.4 1.1 %late.1 = (f32[1,768]{1,0:T(1,128)S(1)}, f32[1,128]{1,0:T(1,128)S(1)}) custom-call(bf16[64,1024]{1,0:T(8,128)(2,1)S(1)} %pass.1.refs_0_, bf16[64,1024]{1,0:T(8,128)(2,1)S(1)} %collective-permute-done.4.refs_1_, bf16[128,1024]{1,0:T(8,128)(2,1)S(1)} %collective-permute-done.5.refs_2_, bf16[128,1024]{1,0:T(8,128)(2,1)S(1)} %collective-permute-done.6.refs_3_, ...), custom_call_target="tpu_custom_call" | custom-call | tf_op jit(solution)/shard_map/late/pallas_call | solution.py:94
  33.6 0.0 collective-permute-done.11.other_ref
  33.6 0.3 finish.1
  33.9 10.1 %all_to_all.5.counts_ref = f32[16,1,64]{2,1,0:T(1,128)S(1)} all-to-all(f32[16,1,64]{2,1,0:T(1,128)S(1)} %finish.1), channel_id=1, replica_groups=mesh['groups'=2,'owner'=4,'helper'=2,'sub'=2] {'owner','helper','sub'}, dimensions={0} | all-to-all | bytes 8192 | tf_op jit(solution)/shard_map/all_to_all | solution.py:298
  44.0 0.7 %select.1 = f32[1,256]{1,0:T(1,128)} custom-call(f32[16,1,64]{2,1,0:T(1,128)S(1)} %all_to_all.5.counts_ref, s32[1,256]{1,0:T(1,128)S(1)} %get-tuple-element.21.refs_2_.slot_ref), custom_call_target="tpu_custom_call" | custom-call | tf_op jit(solution)/shard_map/select/pallas_call | solution.py:94
  (6 shorter events, 0.0 us)
Async XLA Ops:
  0.0 0.7 %copy-start.1 = (s32[256]{0:T(256)S(1)}, s32[256]{0:T(256)}, u32[]{:S(2)}) copy-start(s32[256]{0:T(256)} %param.3) | copy-start | bytes 3076
  0.0 7.3 %collective-permute-start = (bf16[256,1024]{1,0:T(8,128)(2,1)}, bf16[256,1024]{1,0:T(8,128)(2,1)S(1)}, u32[]{:S(2)}, u32[]{:S(2)}) collective-permute-start(bf16[256,1024]{1,0:T(8,128)(2,1)} %refs_0_.3), channel_id=1, source_target_pairs={{0,1},{1,0},{2,3},{3,2},{4,5},{5,4},{6,7},{7,6},{8,9},{9,8},{10,11... | collective-permute-start | bytes 1572872 | tf_op jit(solution)/shard_map/ppermute | solution.py:204
  0.7 6.6 %collective-permute-start.1 = (s32[1,256]{1,0:T(1,128)S(1)}, s32[1,256]{1,0:T(1,128)S(1)}, u32[]{:S(2)}, u32[]{:S(2)}) collective-permute-start(s32[1,256]{1,0:T(1,128)S(1)} %bitcast.2), channel_id=1, source_target_pairs={{0,1},{1,0},{2,3},{3,2},{4,5},{5,4},{6,7},{7,6},{8,9},{9,8},{10,11... | collective-permute-start | bytes 3080 | tf_op jit(solution)/shard_map/ppermute | solution.py:204
  1.1 1.0 %copy-start = (bf16[256,1024]{1,0:T(8,128)(2,1)S(1)}, bf16[256,1024]{1,0:T(8,128)(2,1)}, u32[]{:S(2)}) copy-start(bf16[256,1024]{1,0:T(8,128)(2,1)} %refs_0_.3) | copy-start | bytes 1572868
  2.6 8.5 %collective-permute-start.3 = (bf16[64,1024]{1,0:T(8,128)(2,1)S(1)}, bf16[64,1024]{1,0:T(8,128)(2,1)S(1)}, u32[]{:S(2)}, u32[]{:S(2)}) collective-permute-start(bf16[64,1024]{1,0:T(8,128)(2,1)S(1)} %get-tuple-element.23), channel_id=1, source_target_pairs={{0,12},{1,15},{2,14},{3,13},{4,8},{5,11},{6,10},{7,9},{8,4},{9,7},... | collective-permute-start | bytes 393224 | tf_op jit(solution)/shard_map/ppermute | solution.py:220
  7.9 11.0 %collective-permute-start.5 = (bf16[128,1024]{1,0:T(8,128)(2,1)S(1)}, bf16[128,1024]{1,0:T(8,128)(2,1)S(1)}, u32[]{:S(2)}, u32[]{:S(2)}) collective-permute-start(bf16[128,1024]{1,0:T(8,128)(2,1)S(1)} %get-tuple-element.20), channel_id=1, source_target_pairs={{0,0},{1,3},{2,2},{3,1},{4,4},{5,7},{6,6},{7,5},{8,8},{9,11},{10,1... | collective-permute-start | bytes 786440 | tf_op jit(solution)/shard_map/ppermute | solution.py:220
  8.6 10.4 %collective-permute-start.6 = (bf16[128,1024]{1,0:T(8,128)(2,1)S(1)}, bf16[128,1024]{1,0:T(8,128)(2,1)S(1)}, u32[]{:S(2)}, u32[]{:S(2)}) collective-permute-start(bf16[128,1024]{1,0:T(8,128)(2,1)S(1)} %get-tuple-element.25), channel_id=1, source_target_pairs={{0,4},{1,7},{2,6},{3,5},{4,0},{5,3},{6,2},{7,1},{8,12},{9,15},{10,... | collective-permute-start | bytes 786440 | tf_op jit(solution)/shard_map/ppermute | solution.py:220
  9.3 9.7 %collective-permute-start.4 = (bf16[64,1024]{1,0:T(8,128)(2,1)S(1)}, bf16[64,1024]{1,0:T(8,128)(2,1)S(1)}, u32[]{:S(2)}, u32[]{:S(2)}) collective-permute-start(bf16[64,1024]{1,0:T(8,128)(2,1)S(1)} %get-tuple-element.24), channel_id=1, source_target_pairs={{0,12},{1,15},{2,14},{3,13},{4,8},{5,11},{6,10},{7,9},{8,4},{9,7},... | collective-permute-start | bytes 393224 | tf_op jit(solution)/shard_map/ppermute | solution.py:220
  11.1 18.9 %collective-permute-start.2 = (bf16[128,1024]{1,0:T(8,128)(2,1)S(1)}, bf16[128,1024]{1,0:T(8,128)(2,1)S(1)}, u32[]{:S(2)}, u32[]{:S(2)}) collective-permute-start(bf16[128,1024]{1,0:T(8,128)(2,1)S(1)} %get-tuple-element.22), channel_id=1, source_target_pairs={{0,8},{1,11},{2,10},{3,9},{4,12},{5,15},{6,14},{7,13},{8,0},{9,3},... | collective-permute-start | bytes 786440 | tf_op jit(solution)/shard_map/ppermute | solution.py:220
  19.0 4.3 %collective-permute-start.7 = (bf16[96,1024]{1,0:T(8,128)(2,1)S(1)}, bf16[96,1024]{1,0:T(8,128)(2,1)S(1)}, u32[]{:S(2)}, u32[]{:S(2)}) collective-permute-start(bf16[96,1024]{1,0:T(8,128)(2,1)S(1)} %get-tuple-element.26), channel_id=1, source_target_pairs={{0,1},{1,0},{2,3},{3,2},{4,5},{5,4},{6,7},{7,6},{8,9},{9,8},{10,11... | collective-permute-start | bytes 589832 | tf_op jit(solution)/shard_map/ppermute | solution.py:204
  22.2 1.4 %collective-permute-start.8 = (bf16[96,1024]{1,0:T(8,128)(2,1)S(1)}, bf16[96,1024]{1,0:T(8,128)(2,1)S(1)}, u32[]{:S(2)}, u32[]{:S(2)}) collective-permute-start(bf16[96,1024]{1,0:T(8,128)(2,1)S(1)} %get-tuple-element.27), channel_id=1, source_target_pairs={{0,1},{1,0},{2,3},{3,2},{4,5},{5,4},{6,7},{7,6},{8,9},{9,8},{10,11... | collective-permute-start | bytes 589832 | tf_op jit(solution)/shard_map/ppermute | solution.py:204
  22.3 1.6 %collective-permute-start.9 = (bf16[96,1024]{1,0:T(8,128)(2,1)S(1)}, bf16[96,1024]{1,0:T(8,128)(2,1)S(1)}, u32[]{:S(2)}, u32[]{:S(2)}) collective-permute-start(bf16[96,1024]{1,0:T(8,128)(2,1)S(1)} %get-tuple-element.28), channel_id=1, source_target_pairs={{0,1},{1,0},{2,3},{3,2},{4,5},{5,4},{6,7},{7,6},{8,9},{9,8},{10,11... | collective-permute-start | bytes 589832 | tf_op jit(solution)/shard_map/ppermute | solution.py:204
  22.7 1.5 %collective-permute-start.10 = (bf16[96,1024]{1,0:T(8,128)(2,1)S(1)}, bf16[96,1024]{1,0:T(8,128)(2,1)S(1)}, u32[]{:S(2)}, u32[]{:S(2)}) collective-permute-start(bf16[96,1024]{1,0:T(8,128)(2,1)S(1)} %get-tuple-element.29), channel_id=1, source_target_pairs={{0,1},{1,0},{2,3},{3,2},{4,5},{5,4},{6,7},{7,6},{8,9},{9,8},{10,11... | collective-permute-start | bytes 589832 | tf_op jit(solution)/shard_map/ppermute | solution.py:204
  30.0 3.6 %collective-permute-start.11 = (bf16[128,1024]{1,0:T(8,128)(2,1)S(1)}, bf16[128,1024]{1,0:T(8,128)(2,1)S(1)}, u32[]{:S(2)}, u32[]{:S(2)}) collective-permute-start(bf16[128,1024]{1,0:T(8,128)(2,1)S(1)} %collective-permute-done.2.refs_8_.late_ref), channel_id=1, source_target_pairs={{0,1},{1,0},{2,3},{3,2},{4,5},{5,4},{6,7},{7,6},{8,9},{9,8},{10,11... | collective-permute-start | bytes 786440 | tf_op jit(solution)/shard_map/ppermute | solution.py:204

commit v26 on v22

--- a/solution.py
+++ b/solution.py
@@ -106,12 +106,12 @@
         out_ref[...] = in_ref[...]
 
 
-def halve_kernel(*refs):
-    pieces = len(refs) // 3
-    for k, piece in enumerate(refs[:pieces]):
-        first, second = refs[pieces + 2 * k : pieces + 2 * k + 2]
-        first[...] = piece[: first.shape[0]]
-        second[...] = piece[first.shape[0] :]
+def regroup_kernel(pieces, *refs):
+    rows = jnp.concatenate([ref[...] for ref in refs[:pieces]], axis=0)
+    first = 0
+    for part in refs[pieces:]:
+        part[...] = rows[first : first + part.shape[0]]
+        first += part.shape[0]
 
 
 def blocks(rows, starts, size):
@@ -244,16 +244,17 @@
     first_other = across(first_other, first)
     rest = [across(piece, p) for piece, p in zip(rest, [*middle, last])]
 
-    firsts = call_kernel(
-        "pass", pass_kernel, [half] * 2, first_own, first_other, flops=10**10
-    )
+    (first_own,) = call_kernel("pass", pass_kernel, [half], first_own, flops=2*10**9)
     *near, last_piece = rest
-    halves = call_kernel("halve", halve_kernel, [half] * (2 * len(near)), *near, flops=10**10)
-    early = [*firsts, *near]
-    early += [swap_cores(x) for x in (*firsts, *halves)]
+    early = [first_own, first_other, *near]
+    half_way = cores * capacity * (steps - 1)
+    part = jax.ShapeDtypeStruct((half_way // 4, feature_count), jnp.bfloat16)
+    parts = call_kernel(
+        "regroup", functools.partial(regroup_kernel, len(early)), [part] * 4, *early, flops=10**10
+    )
+    early += [swap_cores(x) for x in parts]
 
     span = cores * capacity
-    half_way = span * (steps - 1)
     starts = [k * span for k in range(steps - 1)]
     starts += [half_way + start + capacity for start in starts]
     counts = soft_counts(early, starts, capacity)

time: 46.7 us -> 45.3 us (0.970)
  waiting for transfers between devices: 18.6 us -> 8.76 us
  starting transfers between devices: 12 us -> 19.7 us
  blocking collectives: 9.92 us -> 10.6 us
    ppermute x5, waiting for transfers between devices: 17.1 us -> 6.41 us  [across(): return lax.ppermute(x, ('owner', 'helper', 'sub'), pairs)]
    ppermute x9 -> x7, starting transfers between devices: 3.64 us -> 9.12 us  [swap_cores(): return lax.ppermute(x, 'sub', [(i, i ^ 1) for i in range(cores)])]
    ppermute x5, starting transfers between devices: 8.38 us -> 10.6 us  [across(): return lax.ppermute(x, ('owner', 'helper', 'sub'), pairs)]
    ppermute x9 -> x7, waiting for transfers between devices: 1.5 us -> 2.34 us  [swap_cores(): return lax.ppermute(x, 'sub', [(i, i ^ 1) for i in range(cores)])]
    all_to_all x1, blocking collectives: 9.92 us -> 10.6 us  [body_by_chip(): lax.all_to_all(counts, ('owner', 'helper', 'sub'), split_axis=0, concat_a...]
  transfers between devices with their start and end apart: 14 -> 12, of which waited for: 8 -> 9; matrix products, arithmetic and copies ran while one was open for 0% -> 0% of each run, Pallas kernels for 8% -> 8%
where the time goes in v26:
time: 45.3 us; the launch traced here: 45.1 us
  starting transfers between devices  19.7 us (43%)
  blocking collectives  10.6 us (23%)
  waiting for transfers between devices  8.76 us (19%)
  Pallas kernels  4.64 us (10%)
  local copies, waits for them, and re-layouts  1.27 us (3%)
    all_to_all x1, blocking collectives, body_by_chip(): lax.all_to_all(counts, ('owner', 'helper', 'sub'), split_axis=0, concat_a...  10.6 us
    ppermute x5, starting transfers between devices, across(): return lax.ppermute(x, ('owner', 'helper', 'sub'), pairs)  10.6 us
    ppermute x7, starting transfers between devices, swap_cores(): return lax.ppermute(x, 'sub', [(i, i ^ 1) for i in range(cores)])  9.12 us
    ppermute x5, waiting for transfers between devices, across(): return lax.ppermute(x, ('owner', 'helper', 'sub'), pairs)  6.41 us
    pallas_call x8, Pallas kernels, call_kernel(): pl.pallas_call(kernel, out_shape=out_shape, in_specs=[VMEM] * len(args),...  4.64 us
    ppermute x7, waiting for transfers between devices, swap_cores(): return lax.ppermute(x, 'sub', [(i, i ^ 1) for i in range(cores)])  2.34 us
    unnamed x4, local copies, waits for them, and re-layouts  1.27 us
  transfers between devices with their start and end apart: 12, of which 9 were waited for; matrix products, arithmetic and copies ran while one was open for 0% of the time, Pallas kernels for 8%

profile of v26, /device:TPU:0, one launch (start us, length us, event | category | flops | bytes accessed | tf_op | source)
XLA Modules:
  0.0 45.1 jit_solution(5291574525087893495)
XLA Ops:
  0.0 0.5 %collective-permute-start = (bf16[256,1024]{1,0:T(8,128)(2,1)}, bf16[256,1024]{1,0:T(8,128)(2,1)S(1)}, u32[]{:S(2)}, u32[]{:S(2)}) collective-permute-start(bf16[256,1024]{1,0:T(8,128)(2,1)} %refs_0_.1), channel_id=1, source_target_pairs={{0,1},{1,0},{2,3},{3,2},{4,5},{5,4},{6,7},{7,6},{8,9},{9,8},{10,11... | collective-permute-start | bytes 1572872 | tf_op jit(solution)/shard_map/ppermute | solution.py:202
  0.5 0.2 copy-done.1
  0.7 1.0 %copy-done = bf16[256,1024]{1,0:T(8,128)(2,1)S(1)} copy-done((bf16[256,1024]{1,0:T(8,128)(2,1)S(1)}, bf16[256,1024]{1,0:T(8,128)(2,1)}, u32[]{:S(2)}) %copy-start) | copy-done | bytes 524312
  1.7 0.5 %route_first.1 = (bf16[64,1024]{1,0:T(8,128)(2,1)S(1)}, s32[1,256]{1,0:T(1,128)S(1)}) custom-call(bf16[256,1024]{1,0:T(8,128)(2,1)S(1)} %copy-done, s32[1,256]{1,0:T(1,128)S(1)} %bitcast.2), custom_call_target="tpu_custom_call" | custom-call | tf_op jit(solution)/shard_map/route_first/pallas_call | solution.py:92
  2.2 4.1 %collective-permute-start.3 = (bf16[64,1024]{1,0:T(8,128)(2,1)S(1)}, bf16[64,1024]{1,0:T(8,128)(2,1)S(1)}, u32[]{:S(2)}, u32[]{:S(2)}) collective-permute-start(bf16[64,1024]{1,0:T(8,128)(2,1)S(1)} %get-tuple-element.20), channel_id=1, source_target_pairs={{0,8},{1,11},{2,10},{3,9},{4,12},{5,15},{6,14},{7,13},{8,0},{9,3},... | collective-permute-start | bytes 393224 | tf_op jit(solution)/shard_map/ppermute | solution.py:218
  6.3 0.5 %collective-permute-start.1 = (s32[1,256]{1,0:T(1,128)S(1)}, s32[1,256]{1,0:T(1,128)S(1)}, u32[]{:S(2)}, u32[]{:S(2)}) collective-permute-start(s32[1,256]{1,0:T(1,128)S(1)} %bitcast.3), channel_id=1, source_target_pairs={{0,1},{1,0},{2,3},{3,2},{4,5},{5,4},{6,7},{7,6},{8,9},{9,8},{10,11... | collective-permute-start | bytes 3080 | tf_op jit(solution)/shard_map/ppermute | solution.py:202
  6.8 0.8 %collective-permute-done.1.refs_3_ = s32[1,256]{1,0:T(1,128)S(1)} collective-permute-done((s32[1,256]{1,0:T(1,128)S(1)}, s32[1,256]{1,0:T(1,128)S(1)}, u32[]{:S(2)}, u32[]{:S(2)}) %collective-permute-start.1) | collective-permute-done | bytes 1056 | tf_op jit(solution)/shard_map/ppermute | solution.py:202
  7.6 0.0 collective-permute-done.refs_1_
  7.6 0.7 %route_rest.1 = (bf16[64,1024]{1,0:T(8,128)(2,1)S(1)}, bf16[128,1024]{1,0:T(8,128)(2,1)S(1)}, bf16[128,1024]{1,0:T(8,128)(2,1)S(1)}, bf16[128,1024]{1,0:T(8,128)(2,1)S(1)}) custom-call(bf16[256,1024]{1,0:T(8,128)(2,1)S(1)} %copy-done, bf16[256,1024]{1,0:T(8,128)(2,1)S(1)} %collective-permute-done.refs_1_, s32[1,256]{1,0:T(1,128)S(1)} %get-tuple-element.18.refs_2_.slot_ref, ...), custom_call_target="tpu_custom_call" | custom-call | tf_op jit(solution)/shard_map/route_rest/pallas_call | solution.py:92
  8.3 0.7 %collective-permute-start.5 = (bf16[128,1024]{1,0:T(8,128)(2,1)S(1)}, bf16[128,1024]{1,0:T(8,128)(2,1)S(1)}, u32[]{:S(2)}, u32[]{:S(2)}) collective-permute-start(bf16[128,1024]{1,0:T(8,128)(2,1)S(1)} %get-tuple-element.22), channel_id=1, source_target_pairs={{0,0},{1,3},{2,2},{3,1},{4,4},{5,7},{6,6},{7,5},{8,8},{9,11},{10,1... | collective-permute-start | bytes 786440 | tf_op jit(solution)/shard_map/ppermute | solution.py:218
  9.0 1.6 %collective-permute-start.6 = (bf16[128,1024]{1,0:T(8,128)(2,1)S(1)}, bf16[128,1024]{1,0:T(8,128)(2,1)S(1)}, u32[]{:S(2)}, u32[]{:S(2)}) collective-permute-start(bf16[128,1024]{1,0:T(8,128)(2,1)S(1)} %get-tuple-element.23), channel_id=1, source_target_pairs={{0,4},{1,7},{2,6},{3,5},{4,0},{5,3},{6,2},{7,1},{8,12},{9,15},{10,... | collective-permute-start | bytes 786440 | tf_op jit(solution)/shard_map/ppermute | solution.py:218
  10.7 0.3 collective-permute-start.4
  11.0 2.4 %collective-permute-done.3.refs_0_ = bf16[64,1024]{1,0:T(8,128)(2,1)S(1)} collective-permute-done((bf16[64,1024]{1,0:T(8,128)(2,1)S(1)}, bf16[64,1024]{1,0:T(8,128)(2,1)S(1)}, u32[]{:S(2)}, u32[]{:S(2)}) %collective-permute-start.3) | collective-permute-done | bytes 131104 | tf_op jit(solution)/shard_map/ppermute | solution.py:218
  13.4 3.8 %collective-permute-start.2 = (bf16[128,1024]{1,0:T(8,128)(2,1)S(1)}, bf16[128,1024]{1,0:T(8,128)(2,1)S(1)}, u32[]{:S(2)}, u32[]{:S(2)}) collective-permute-start(bf16[128,1024]{1,0:T(8,128)(2,1)S(1)} %get-tuple-element.19), channel_id=1, source_target_pairs={{0,12},{1,15},{2,14},{3,13},{4,8},{5,11},{6,10},{7,9},{8,4},{9,7},... | collective-permute-start | bytes 786440 | tf_op jit(solution)/shard_map/ppermute | solution.py:218
  17.2 1.1 %collective-permute-done.4.refs_1_ = bf16[64,1024]{1,0:T(8,128)(2,1)S(1)} collective-permute-done((bf16[64,1024]{1,0:T(8,128)(2,1)S(1)}, bf16[64,1024]{1,0:T(8,128)(2,1)S(1)}, u32[]{:S(2)}, u32[]{:S(2)}) %collective-permute-start.4) | collective-permute-done | bytes 131104 | tf_op jit(solution)/shard_map/ppermute | solution.py:218
  18.3 2.9 %collective-permute-done.6.refs_3_ = bf16[128,1024]{1,0:T(8,128)(2,1)S(1)} collective-permute-done((bf16[128,1024]{1,0:T(8,128)(2,1)S(1)}, bf16[128,1024]{1,0:T(8,128)(2,1)S(1)}, u32[]{:S(2)}, u32[]{:S(2)}) %collective-permute-start.6) | collective-permute-done | bytes 262176 | tf_op jit(solution)/shard_map/ppermute | solution.py:218
  21.3 0.1 regroup.1
  21.3 7.2 %collective-permute-start.7 = (bf16[96,1024]{1,0:T(8,128)(2,1)S(1)}, bf16[96,1024]{1,0:T(8,128)(2,1)S(1)}, u32[]{:S(2)}, u32[]{:S(2)}) collective-permute-start(bf16[96,1024]{1,0:T(8,128)(2,1)S(1)} %get-tuple-element.24), channel_id=1, source_target_pairs={{0,1},{1,0},{2,3},{3,2},{4,5},{5,4},{6,7},{7,6},{8,9},{9,8},{10,11... | collective-permute-start | bytes 589832 | tf_op jit(solution)/shard_map/ppermute | solution.py:202
  28.6 0.1 collective-permute-start.8
  28.6 0.4 collective-permute-start.9
  29.1 0.1 collective-permute-start.10
  29.1 0.5 %collective-permute-done.7.refs_4_ = bf16[96,1024]{1,0:T(8,128)(2,1)S(1)} collective-permute-done((bf16[96,1024]{1,0:T(8,128)(2,1)S(1)}, bf16[96,1024]{1,0:T(8,128)(2,1)S(1)}, u32[]{:S(2)}, u32[]{:S(2)}) %collective-permute-start.7) | collective-permute-done | bytes 196640 | tf_op jit(solution)/shard_map/ppermute | solution.py:202
  29.6 0.4 collective-permute-done.8.refs_5_
  30.0 0.3 collective-permute-done.9.refs_6_
  30.3 0.3 collective-permute-done.10.refs_7_
  30.6 1.2 %count.1.counts_ref = f32[1,384]{1,0:T(1,128)S(1)} custom-call(bf16[64,1024]{1,0:T(8,128)(2,1)S(1)} %pass.1.refs_0_, bf16[64,1024]{1,0:T(8,128)(2,1)S(1)} %collective-permute-done.4.refs_1_, bf16[128,1024]{1,0:T(8,128)(2,1)S(1)} %collective-permute-done.5.refs_2_, bf16[128,1024]{1,0:T(8,128)(2,1)S(1)} %collective-permute-done.6.refs_3_, ...), custom_call_target="tpu_custom_call" | custom-call | tf_op jit(solution)/shard_map/count/pallas_call | solution.py:92
  31.8 0.4 collective-permute-start.11
  32.1 1.1 %late.1 = (f32[1,768]{1,0:T(1,128)S(1)}, f32[1,128]{1,0:T(1,128)S(1)}) custom-call(bf16[64,1024]{1,0:T(8,128)(2,1)S(1)} %pass.1.refs_0_, bf16[64,1024]{1,0:T(8,128)(2,1)S(1)} %collective-permute-done.4.refs_1_, bf16[128,1024]{1,0:T(8,128)(2,1)S(1)} %collective-permute-done.5.refs_2_, bf16[128,1024]{1,0:T(8,128)(2,1)S(1)} %collective-permute-done.6.refs_3_, ...), custom_call_target="tpu_custom_call" | custom-call | tf_op jit(solution)/shard_map/late/pallas_call | solution.py:92
  33.3 0.1 collective-permute-done.11.other_ref
  33.4 0.3 finish.1
  33.7 10.6 %all_to_all.5.counts_ref = f32[16,1,64]{2,1,0:T(1,128)S(1)} all-to-all(f32[16,1,64]{2,1,0:T(1,128)S(1)} %finish.1), channel_id=1, replica_groups=mesh['groups'=2,'owner'=4,'helper'=2,'sub'=2] {'owner','helper','sub'}, dimensions={0} | all-to-all | bytes 8192 | tf_op jit(solution)/shard_map/all_to_all | solution.py:290
  44.3 0.7 %select.1 = f32[1,256]{1,0:T(1,128)} custom-call(f32[16,1,64]{2,1,0:T(1,128)S(1)} %all_to_all.5.counts_ref, s32[1,256]{1,0:T(1,128)S(1)} %get-tuple-element.18.refs_2_.slot_ref), custom_call_target="tpu_custom_call" | custom-call | tf_op jit(solution)/shard_map/select/pallas_call | solution.py:92
  (5 shorter events, 0.0 us)
Async XLA Ops:
  0.0 0.7 %copy-start.1 = (s32[256]{0:T(256)S(1)}, s32[256]{0:T(256)}, u32[]{:S(2)}) copy-start(s32[256]{0:T(256)} %param.3) | copy-start | bytes 3076
  0.0 7.6 %collective-permute-start = (bf16[256,1024]{1,0:T(8,128)(2,1)}, bf16[256,1024]{1,0:T(8,128)(2,1)S(1)}, u32[]{:S(2)}, u32[]{:S(2)}) collective-permute-start(bf16[256,1024]{1,0:T(8,128)(2,1)} %refs_0_.1), channel_id=1, source_target_pairs={{0,1},{1,0},{2,3},{3,2},{4,5},{5,4},{6,7},{7,6},{8,9},{9,8},{10,11... | collective-permute-start | bytes 1572872 | tf_op jit(solution)/shard_map/ppermute | solution.py:202
  0.7 1.0 %copy-start = (bf16[256,1024]{1,0:T(8,128)(2,1)S(1)}, bf16[256,1024]{1,0:T(8,128)(2,1)}, u32[]{:S(2)}) copy-start(bf16[256,1024]{1,0:T(8,128)(2,1)} %refs_0_.1) | copy-start | bytes 1572868
  2.2 11.2 %collective-permute-start.3 = (bf16[64,1024]{1,0:T(8,128)(2,1)S(1)}, bf16[64,1024]{1,0:T(8,128)(2,1)S(1)}, u32[]{:S(2)}, u32[]{:S(2)}) collective-permute-start(bf16[64,1024]{1,0:T(8,128)(2,1)S(1)} %get-tuple-element.20), channel_id=1, source_target_pairs={{0,8},{1,11},{2,10},{3,9},{4,12},{5,15},{6,14},{7,13},{8,0},{9,3},... | collective-permute-start | bytes 393224 | tf_op jit(solution)/shard_map/ppermute | solution.py:218
  6.3 1.3 %collective-permute-start.1 = (s32[1,256]{1,0:T(1,128)S(1)}, s32[1,256]{1,0:T(1,128)S(1)}, u32[]{:S(2)}, u32[]{:S(2)}) collective-permute-start(s32[1,256]{1,0:T(1,128)S(1)} %bitcast.3), channel_id=1, source_target_pairs={{0,1},{1,0},{2,3},{3,2},{4,5},{5,4},{6,7},{7,6},{8,9},{9,8},{10,11... | collective-permute-start | bytes 3080 | tf_op jit(solution)/shard_map/ppermute | solution.py:202
  8.3 10.0 %collective-permute-start.5 = (bf16[128,1024]{1,0:T(8,128)(2,1)S(1)}, bf16[128,1024]{1,0:T(8,128)(2,1)S(1)}, u32[]{:S(2)}, u32[]{:S(2)}) collective-permute-start(bf16[128,1024]{1,0:T(8,128)(2,1)S(1)} %get-tuple-element.22), channel_id=1, source_target_pairs={{0,0},{1,3},{2,2},{3,1},{4,4},{5,7},{6,6},{7,5},{8,8},{9,11},{10,1... | collective-permute-start | bytes 786440 | tf_op jit(solution)/shard_map/ppermute | solution.py:218
  9.0 12.2 %collective-permute-start.6 = (bf16[128,1024]{1,0:T(8,128)(2,1)S(1)}, bf16[128,1024]{1,0:T(8,128)(2,1)S(1)}, u32[]{:S(2)}, u32[]{:S(2)}) collective-permute-start(bf16[128,1024]{1,0:T(8,128)(2,1)S(1)} %get-tuple-element.23), channel_id=1, source_target_pairs={{0,4},{1,7},{2,6},{3,5},{4,0},{5,3},{6,2},{7,1},{8,12},{9,15},{10,... | collective-permute-start | bytes 786440 | tf_op jit(solution)/shard_map/ppermute | solution.py:218
  10.7 7.7 %collective-permute-start.4 = (bf16[64,1024]{1,0:T(8,128)(2,1)S(1)}, bf16[64,1024]{1,0:T(8,128)(2,1)S(1)}, u32[]{:S(2)}, u32[]{:S(2)}) collective-permute-start(bf16[64,1024]{1,0:T(8,128)(2,1)S(1)} %get-tuple-element.21), channel_id=1, source_target_pairs={{0,8},{1,11},{2,10},{3,9},{4,12},{5,15},{6,14},{7,13},{8,0},{9,3},... | collective-permute-start | bytes 393224 | tf_op jit(solution)/shard_map/ppermute | solution.py:218
  13.4 18.3 %collective-permute-start.2 = (bf16[128,1024]{1,0:T(8,128)(2,1)S(1)}, bf16[128,1024]{1,0:T(8,128)(2,1)S(1)}, u32[]{:S(2)}, u32[]{:S(2)}) collective-permute-start(bf16[128,1024]{1,0:T(8,128)(2,1)S(1)} %get-tuple-element.19), channel_id=1, source_target_pairs={{0,12},{1,15},{2,14},{3,13},{4,8},{5,11},{6,10},{7,9},{8,4},{9,7},... | collective-permute-start | bytes 786440 | tf_op jit(solution)/shard_map/ppermute | solution.py:218
  21.3 8.3 %collective-permute-start.7 = (bf16[96,1024]{1,0:T(8,128)(2,1)S(1)}, bf16[96,1024]{1,0:T(8,128)(2,1)S(1)}, u32[]{:S(2)}, u32[]{:S(2)}) collective-permute-start(bf16[96,1024]{1,0:T(8,128)(2,1)S(1)} %get-tuple-element.24), channel_id=1, source_target_pairs={{0,1},{1,0},{2,3},{3,2},{4,5},{5,4},{6,7},{7,6},{8,9},{9,8},{10,11... | collective-permute-start | bytes 589832 | tf_op jit(solution)/shard_map/ppermute | solution.py:202
  28.6 1.4 %collective-permute-start.8 = (bf16[96,1024]{1,0:T(8,128)(2,1)S(1)}, bf16[96,1024]{1,0:T(8,128)(2,1)S(1)}, u32[]{:S(2)}, u32[]{:S(2)}) collective-permute-start(bf16[96,1024]{1,0:T(8,128)(2,1)S(1)} %get-tuple-element.25), channel_id=1, source_target_pairs={{0,1},{1,0},{2,3},{3,2},{4,5},{5,4},{6,7},{7,6},{8,9},{9,8},{10,11... | collective-permute-start | bytes 589832 | tf_op jit(solution)/shard_map/ppermute | solution.py:202
  28.6 1.6 %collective-permute-start.9 = (bf16[96,1024]{1,0:T(8,128)(2,1)S(1)}, bf16[96,1024]{1,0:T(8,128)(2,1)S(1)}, u32[]{:S(2)}, u32[]{:S(2)}) collective-permute-start(bf16[96,1024]{1,0:T(8,128)(2,1)S(1)} %get-tuple-element.26), channel_id=1, source_target_pairs={{0,1},{1,0},{2,3},{3,2},{4,5},{5,4},{6,7},{7,6},{8,9},{9,8},{10,11... | collective-permute-start | bytes 589832 | tf_op jit(solution)/shard_map/ppermute | solution.py:202
  29.1 1.5 %collective-permute-start.10 = (bf16[96,1024]{1,0:T(8,128)(2,1)S(1)}, bf16[96,1024]{1,0:T(8,128)(2,1)S(1)}, u32[]{:S(2)}, u32[]{:S(2)}) collective-permute-start(bf16[96,1024]{1,0:T(8,128)(2,1)S(1)} %get-tuple-element.27), channel_id=1, source_target_pairs={{0,1},{1,0},{2,3},{3,2},{4,5},{5,4},{6,7},{7,6},{8,9},{9,8},{10,11... | collective-permute-start | bytes 589832 | tf_op jit(solution)/shard_map/ppermute | solution.py:202
  31.8 1.6 %collective-permute-start.11 = (bf16[128,1024]{1,0:T(8,128)(2,1)S(1)}, bf16[128,1024]{1,0:T(8,128)(2,1)S(1)}, u32[]{:S(2)}, u32[]{:S(2)}) collective-permute-start(bf16[128,1024]{1,0:T(8,128)(2,1)S(1)} %collective-permute-done.2.refs_8_.late_ref), channel_id=1, source_target_pairs={{0,1},{1,0},{2,3},{3,2},{4,5},{5,4},{6,7},{7,6},{8,9},{9,8},{10,11... | collective-permute-start | bytes 786440 | tf_op jit(solution)/shard_map/ppermute | solution.py:202

commit v27 on v24

--- a/solution.py
+++ b/solution.py
@@ -222,7 +222,7 @@
     ids = cluster_id.reshape(1, doc_count)
     other_rows, other_ids = swap_cores(embeddings), swap_cores(ids)
     first, last = steps // 2, steps - 1
-    middle = [p for p in range(steps) if p not in (first, last)]
+    middle = [p for p in reversed(range(steps)) if p not in (first, last)]
     half = jax.ShapeDtypeStruct((capacity, feature_count), jnp.bfloat16)
     whole = jax.ShapeDtypeStruct((cores * capacity, feature_count), jnp.bfloat16)
 

time: 44 us -> 44 us (level)
  transfers between devices with their start and end apart: 12 -> 12, of which waited for: 7 -> 8; matrix products, arithmetic and copies ran while one was open for 0% -> 0% of each run, Pallas kernels for 9% -> 9%
where the time goes in v27:
time: 44 us; the launch traced here: 43.8 us
  starting transfers between devices  21.5 us (49%)
  blocking collectives  9.47 us (22%)
  waiting for transfers between devices  6.39 us (15%)
  Pallas kernels  5.11 us (12%)
  local copies, waits for them, and re-layouts  1.27 us (3%)
    ppermute x5, starting transfers between devices, across(): return lax.ppermute(x, ('owner', 'helper', 'sub'), pairs)  11 us
    ppermute x7, starting transfers between devices, swap_cores(): return lax.ppermute(x, 'sub', [(i, i ^ 1) for i in range(cores)])  10.5 us
    all_to_all x1, blocking collectives, body_by_chip(): lax.all_to_all(counts, ('owner', 'helper', 'sub'), split_axis=0, concat_a...  9.47 us
    pallas_call x9, Pallas kernels, call_kernel(): pl.pallas_call(kernel, out_shape=out_shape, in_specs=[VMEM] * len(args),...  5.11 us
    ppermute x5, waiting for transfers between devices, across(): return lax.ppermute(x, ('owner', 'helper', 'sub'), pairs)  4.85 us
    ppermute x7, waiting for transfers between devices, swap_cores(): return lax.ppermute(x, 'sub', [(i, i ^ 1) for i in range(cores)])  1.54 us
    unnamed x4, local copies, waits for them, and re-layouts  1.27 us
  transfers between devices with their start and end apart: 12, of which 8 were waited for; matrix products, arithmetic and copies ran while one was open for 0% of the time, Pallas kernels for 9%

profile of v27, /device:TPU:0, one launch (start us, length us, event | category | flops | bytes accessed | tf_op | source)
XLA Modules:
  0.0 43.8 jit_solution(536937797916042666)
XLA Ops:
  0.0 0.5 %collective-permute-start = (bf16[256,1024]{1,0:T(8,128)(2,1)}, bf16[256,1024]{1,0:T(8,128)(2,1)S(1)}, u32[]{:S(2)}, u32[]{:S(2)}) collective-permute-start(bf16[256,1024]{1,0:T(8,128)(2,1)} %refs_0_.3), channel_id=1, source_target_pairs={{0,1},{1,0},{2,3},{3,2},{4,5},{5,4},{6,7},{7,6},{8,9},{9,8},{10,11... | collective-permute-start | bytes 1572872 | tf_op jit(solution)/shard_map/ppermute | solution.py:204
  0.5 0.2 copy-done.1
  0.7 0.5 %collective-permute-start.1 = (s32[1,256]{1,0:T(1,128)S(1)}, s32[1,256]{1,0:T(1,128)S(1)}, u32[]{:S(2)}, u32[]{:S(2)}) collective-permute-start(s32[1,256]{1,0:T(1,128)S(1)} %bitcast.2), channel_id=1, source_target_pairs={{0,1},{1,0},{2,3},{3,2},{4,5},{5,4},{6,7},{7,6},{8,9},{9,8},{10,11... | collective-permute-start | bytes 3080 | tf_op jit(solution)/shard_map/ppermute | solution.py:204
  1.1 1.0 %copy-done = bf16[256,1024]{1,0:T(8,128)(2,1)S(1)} copy-done((bf16[256,1024]{1,0:T(8,128)(2,1)S(1)}, bf16[256,1024]{1,0:T(8,128)(2,1)}, u32[]{:S(2)}) %copy-start) | copy-done | bytes 524312
  2.2 0.5 %route_first.1 = (bf16[64,1024]{1,0:T(8,128)(2,1)S(1)}, s32[1,256]{1,0:T(1,128)S(1)}) custom-call(bf16[256,1024]{1,0:T(8,128)(2,1)S(1)} %copy-done, s32[1,256]{1,0:T(1,128)S(1)} %bitcast.3), custom_call_target="tpu_custom_call" | custom-call | tf_op jit(solution)/shard_map/route_first/pallas_call | solution.py:94
  2.6 3.7 %collective-permute-start.3 = (bf16[64,1024]{1,0:T(8,128)(2,1)S(1)}, bf16[64,1024]{1,0:T(8,128)(2,1)S(1)}, u32[]{:S(2)}, u32[]{:S(2)}) collective-permute-start(bf16[64,1024]{1,0:T(8,128)(2,1)S(1)} %get-tuple-element.23), channel_id=1, source_target_pairs={{0,8},{1,11},{2,10},{3,9},{4,12},{5,15},{6,14},{7,13},{8,0},{9,3},... | collective-permute-start | bytes 393224 | tf_op jit(solution)/shard_map/ppermute | solution.py:220
  6.3 0.0 collective-permute-done.1.refs_3_
  6.3 0.6 %route_near.1 = (bf16[128,1024]{1,0:T(8,128)(2,1)S(1)}, bf16[128,1024]{1,0:T(8,128)(2,1)S(1)}) custom-call(bf16[256,1024]{1,0:T(8,128)(2,1)S(1)} %copy-done, bf16[256,1024]{1,0:T(8,128)(2,1)S(1)} %collective-permute-done.refs_1_, s32[1,256]{1,0:T(1,128)S(1)} %get-tuple-element.21.refs_2_.slot_ref, s32[1,256]{1,0:T(1,128)S(1)} %collective-permute-done.1.refs_3_), custom_call_target="tpu_custom_call" | custom-call | tf_op jit(solution)/shard_map/route_near/pallas_call | solution.py:94
  6.9 1.6 %collective-permute-start.5 = (bf16[128,1024]{1,0:T(8,128)(2,1)S(1)}, bf16[128,1024]{1,0:T(8,128)(2,1)S(1)}, u32[]{:S(2)}, u32[]{:S(2)}) collective-permute-start(bf16[128,1024]{1,0:T(8,128)(2,1)S(1)} %get-tuple-element.20), channel_id=1, source_target_pairs={{0,4},{1,7},{2,6},{3,5},{4,0},{5,3},{6,2},{7,1},{8,12},{9,15},{10,... | collective-permute-start | bytes 786440 | tf_op jit(solution)/shard_map/ppermute | solution.py:220
  8.6 0.7 %collective-permute-start.6 = (bf16[128,1024]{1,0:T(8,128)(2,1)S(1)}, bf16[128,1024]{1,0:T(8,128)(2,1)S(1)}, u32[]{:S(2)}, u32[]{:S(2)}) collective-permute-start(bf16[128,1024]{1,0:T(8,128)(2,1)S(1)} %get-tuple-element.25), channel_id=1, source_target_pairs={{0,0},{1,3},{2,2},{3,1},{4,4},{5,7},{6,6},{7,5},{8,8},{9,11},{10,1... | collective-permute-start | bytes 786440 | tf_op jit(solution)/shard_map/ppermute | solution.py:220
  9.2 0.6 %route_far.1 = (bf16[64,1024]{1,0:T(8,128)(2,1)S(1)}, bf16[128,1024]{1,0:T(8,128)(2,1)S(1)}) custom-call(bf16[256,1024]{1,0:T(8,128)(2,1)S(1)} %copy-done, bf16[256,1024]{1,0:T(8,128)(2,1)S(1)} %collective-permute-done.refs_1_, s32[1,256]{1,0:T(1,128)S(1)} %get-tuple-element.21.refs_2_.slot_ref, s32[1,256]{1,0:T(1,128)S(1)} %collective-permute-done.1.refs_3_), custom_call_target="tpu_custom_call" | custom-call | flops 10000000000 | tf_op jit(solution)/shard_map/route_far/pallas_call | solution.py:94
  9.8 0.4 collective-permute-start.4
  10.2 2.6 %collective-permute-done.3.refs_0_ = bf16[64,1024]{1,0:T(8,128)(2,1)S(1)} collective-permute-done((bf16[64,1024]{1,0:T(8,128)(2,1)S(1)}, bf16[64,1024]{1,0:T(8,128)(2,1)S(1)}, u32[]{:S(2)}, u32[]{:S(2)}) %collective-permute-start.3) | collective-permute-done | bytes 131104 | tf_op jit(solution)/shard_map/ppermute | solution.py:220
  12.8 4.6 %collective-permute-start.2 = (bf16[128,1024]{1,0:T(8,128)(2,1)S(1)}, bf16[128,1024]{1,0:T(8,128)(2,1)S(1)}, u32[]{:S(2)}, u32[]{:S(2)}) collective-permute-start(bf16[128,1024]{1,0:T(8,128)(2,1)S(1)} %get-tuple-element.22), channel_id=1, source_target_pairs={{0,12},{1,15},{2,14},{3,13},{4,8},{5,11},{6,10},{7,9},{8,4},{9,7},... | collective-permute-start | bytes 786440 | tf_op jit(solution)/shard_map/ppermute | solution.py:220
  17.4 0.9 %collective-permute-done.4.refs_1_ = bf16[64,1024]{1,0:T(8,128)(2,1)S(1)} collective-permute-done((bf16[64,1024]{1,0:T(8,128)(2,1)S(1)}, bf16[64,1024]{1,0:T(8,128)(2,1)S(1)}, u32[]{:S(2)}, u32[]{:S(2)}) %collective-permute-start.4) | collective-permute-done | bytes 131104 | tf_op jit(solution)/shard_map/ppermute | solution.py:220
  18.3 1.4 %collective-permute-done.5.refs_2_ = bf16[128,1024]{1,0:T(8,128)(2,1)S(1)} collective-permute-done((bf16[128,1024]{1,0:T(8,128)(2,1)S(1)}, bf16[128,1024]{1,0:T(8,128)(2,1)S(1)}, u32[]{:S(2)}, u32[]{:S(2)}) %collective-permute-start.5) | collective-permute-done | bytes 262176 | tf_op jit(solution)/shard_map/ppermute | solution.py:220
  19.7 0.1 regroup.1
  19.8 8.7 %collective-permute-start.7 = (bf16[96,1024]{1,0:T(8,128)(2,1)S(1)}, bf16[96,1024]{1,0:T(8,128)(2,1)S(1)}, u32[]{:S(2)}, u32[]{:S(2)}) collective-permute-start(bf16[96,1024]{1,0:T(8,128)(2,1)S(1)} %get-tuple-element.26), channel_id=1, source_target_pairs={{0,1},{1,0},{2,3},{3,2},{4,5},{5,4},{6,7},{7,6},{8,9},{9,8},{10,11... | collective-permute-start | bytes 589832 | tf_op jit(solution)/shard_map/ppermute | solution.py:204
  28.5 0.1 collective-permute-start.8
  28.5 0.4 collective-permute-start.9
  29.0 0.1 collective-permute-start.10
  29.1 0.5 %collective-permute-done.7.refs_4_ = bf16[96,1024]{1,0:T(8,128)(2,1)S(1)} collective-permute-done((bf16[96,1024]{1,0:T(8,128)(2,1)S(1)}, bf16[96,1024]{1,0:T(8,128)(2,1)S(1)}, u32[]{:S(2)}, u32[]{:S(2)}) %collective-permute-start.7) | collective-permute-done | bytes 196640 | tf_op jit(solution)/shard_map/ppermute | solution.py:204
  29.5 0.4 collective-permute-done.8.refs_5_
  29.9 0.3 collective-permute-done.9.refs_6_
  30.2 0.3 collective-permute-done.10.refs_7_
  30.5 1.2 %count.1.counts_ref = f32[1,384]{1,0:T(1,128)S(1)} custom-call(bf16[64,1024]{1,0:T(8,128)(2,1)S(1)} %pass.1.refs_0_, bf16[64,1024]{1,0:T(8,128)(2,1)S(1)} %collective-permute-done.4.refs_1_, bf16[128,1024]{1,0:T(8,128)(2,1)S(1)} %collective-permute-done.5.refs_2_, bf16[128,1024]{1,0:T(8,128)(2,1)S(1)} %collective-permute-done.6.refs_3_, ...), custom_call_target="tpu_custom_call" | custom-call | tf_op jit(solution)/shard_map/count/pallas_call | solution.py:94
  31.7 0.3 collective-permute-start.11
  32.0 1.1 %late.1 = (f32[1,768]{1,0:T(1,128)S(1)}, f32[1,128]{1,0:T(1,128)S(1)}) custom-call(bf16[64,1024]{1,0:T(8,128)(2,1)S(1)} %pass.1.refs_0_, bf16[64,1024]{1,0:T(8,128)(2,1)S(1)} %collective-permute-done.4.refs_1_, bf16[128,1024]{1,0:T(8,128)(2,1)S(1)} %collective-permute-done.5.refs_2_, bf16[128,1024]{1,0:T(8,128)(2,1)S(1)} %collective-permute-done.6.refs_3_, ...), custom_call_target="tpu_custom_call" | custom-call | tf_op jit(solution)/shard_map/late/pallas_call | solution.py:94
  33.2 0.1 collective-permute-done.11.other_ref
  33.3 0.3 finish.1
  33.6 9.5 %all_to_all.5.counts_ref = f32[16,1,64]{2,1,0:T(1,128)S(1)} all-to-all(f32[16,1,64]{2,1,0:T(1,128)S(1)} %finish.1), channel_id=1, replica_groups=mesh['groups'=2,'owner'=4,'helper'=2,'sub'=2] {'owner','helper','sub'}, dimensions={0} | all-to-all | bytes 8192 | tf_op jit(solution)/shard_map/all_to_all | solution.py:298
  43.1 0.7 %select.1 = f32[1,256]{1,0:T(1,128)} custom-call(f32[16,1,64]{2,1,0:T(1,128)S(1)} %all_to_all.5.counts_ref, s32[1,256]{1,0:T(1,128)S(1)} %get-tuple-element.21.refs_2_.slot_ref), custom_call_target="tpu_custom_call" | custom-call | tf_op jit(solution)/shard_map/select/pallas_call | solution.py:94
  (6 shorter events, 0.0 us)
Async XLA Ops:
  0.0 0.7 %copy-start.1 = (s32[256]{0:T(256)S(1)}, s32[256]{0:T(256)}, u32[]{:S(2)}) copy-start(s32[256]{0:T(256)} %param.3) | copy-start | bytes 3076
  0.0 6.3 %collective-permute-start = (bf16[256,1024]{1,0:T(8,128)(2,1)}, bf16[256,1024]{1,0:T(8,128)(2,1)S(1)}, u32[]{:S(2)}, u32[]{:S(2)}) collective-permute-start(bf16[256,1024]{1,0:T(8,128)(2,1)} %refs_0_.3), channel_id=1, source_target_pairs={{0,1},{1,0},{2,3},{3,2},{4,5},{5,4},{6,7},{7,6},{8,9},{9,8},{10,11... | collective-permute-start | bytes 1572872 | tf_op jit(solution)/shard_map/ppermute | solution.py:204
  0.7 5.6 %collective-permute-start.1 = (s32[1,256]{1,0:T(1,128)S(1)}, s32[1,256]{1,0:T(1,128)S(1)}, u32[]{:S(2)}, u32[]{:S(2)}) collective-permute-start(s32[1,256]{1,0:T(1,128)S(1)} %bitcast.2), channel_id=1, source_target_pairs={{0,1},{1,0},{2,3},{3,2},{4,5},{5,4},{6,7},{7,6},{8,9},{9,8},{10,11... | collective-permute-start | bytes 3080 | tf_op jit(solution)/shard_map/ppermute | solution.py:204
  1.1 1.0 %copy-start = (bf16[256,1024]{1,0:T(8,128)(2,1)S(1)}, bf16[256,1024]{1,0:T(8,128)(2,1)}, u32[]{:S(2)}) copy-start(bf16[256,1024]{1,0:T(8,128)(2,1)} %refs_0_.3) | copy-start | bytes 1572868
  2.6 10.2 %collective-permute-start.3 = (bf16[64,1024]{1,0:T(8,128)(2,1)S(1)}, bf16[64,1024]{1,0:T(8,128)(2,1)S(1)}, u32[]{:S(2)}, u32[]{:S(2)}) collective-permute-start(bf16[64,1024]{1,0:T(8,128)(2,1)S(1)} %get-tuple-element.23), channel_id=1, source_target_pairs={{0,8},{1,11},{2,10},{3,9},{4,12},{5,15},{6,14},{7,13},{8,0},{9,3},... | collective-permute-start | bytes 393224 | tf_op jit(solution)/shard_map/ppermute | solution.py:220
  6.9 12.8 %collective-permute-start.5 = (bf16[128,1024]{1,0:T(8,128)(2,1)S(1)}, bf16[128,1024]{1,0:T(8,128)(2,1)S(1)}, u32[]{:S(2)}, u32[]{:S(2)}) collective-permute-start(bf16[128,1024]{1,0:T(8,128)(2,1)S(1)} %get-tuple-element.20), channel_id=1, source_target_pairs={{0,4},{1,7},{2,6},{3,5},{4,0},{5,3},{6,2},{7,1},{8,12},{9,15},{10,... | collective-permute-start | bytes 786440 | tf_op jit(solution)/shard_map/ppermute | solution.py:220
  8.6 9.8 %collective-permute-start.6 = (bf16[128,1024]{1,0:T(8,128)(2,1)S(1)}, bf16[128,1024]{1,0:T(8,128)(2,1)S(1)}, u32[]{:S(2)}, u32[]{:S(2)}) collective-permute-start(bf16[128,1024]{1,0:T(8,128)(2,1)S(1)} %get-tuple-element.25), channel_id=1, source_target_pairs={{0,0},{1,3},{2,2},{3,1},{4,4},{5,7},{6,6},{7,5},{8,8},{9,11},{10,1... | collective-permute-start | bytes 786440 | tf_op jit(solution)/shard_map/ppermute | solution.py:220
  9.8 8.5 %collective-permute-start.4 = (bf16[64,1024]{1,0:T(8,128)(2,1)S(1)}, bf16[64,1024]{1,0:T(8,128)(2,1)S(1)}, u32[]{:S(2)}, u32[]{:S(2)}) collective-permute-start(bf16[64,1024]{1,0:T(8,128)(2,1)S(1)} %get-tuple-element.24), channel_id=1, source_target_pairs={{0,8},{1,11},{2,10},{3,9},{4,12},{5,15},{6,14},{7,13},{8,0},{9,3},... | collective-permute-start | bytes 393224 | tf_op jit(solution)/shard_map/ppermute | solution.py:220
  12.8 18.9 %collective-permute-start.2 = (bf16[128,1024]{1,0:T(8,128)(2,1)S(1)}, bf16[128,1024]{1,0:T(8,128)(2,1)S(1)}, u32[]{:S(2)}, u32[]{:S(2)}) collective-permute-start(bf16[128,1024]{1,0:T(8,128)(2,1)S(1)} %get-tuple-element.22), channel_id=1, source_target_pairs={{0,12},{1,15},{2,14},{3,13},{4,8},{5,11},{6,10},{7,9},{8,4},{9,7},... | collective-permute-start | bytes 786440 | tf_op jit(solution)/shard_map/ppermute | solution.py:220
  19.8 9.8 %collective-permute-start.7 = (bf16[96,1024]{1,0:T(8,128)(2,1)S(1)}, bf16[96,1024]{1,0:T(8,128)(2,1)S(1)}, u32[]{:S(2)}, u32[]{:S(2)}) collective-permute-start(bf16[96,1024]{1,0:T(8,128)(2,1)S(1)} %get-tuple-element.26), channel_id=1, source_target_pairs={{0,1},{1,0},{2,3},{3,2},{4,5},{5,4},{6,7},{7,6},{8,9},{9,8},{10,11... | collective-permute-start | bytes 589832 | tf_op jit(solution)/shard_map/ppermute | solution.py:204
  28.5 1.4 %collective-permute-start.8 = (bf16[96,1024]{1,0:T(8,128)(2,1)S(1)}, bf16[96,1024]{1,0:T(8,128)(2,1)S(1)}, u32[]{:S(2)}, u32[]{:S(2)}) collective-permute-start(bf16[96,1024]{1,0:T(8,128)(2,1)S(1)} %get-tuple-element.27), channel_id=1, source_target_pairs={{0,1},{1,0},{2,3},{3,2},{4,5},{5,4},{6,7},{7,6},{8,9},{9,8},{10,11... | collective-permute-start | bytes 589832 | tf_op jit(solution)/shard_map/ppermute | solution.py:204
  28.5 1.6 %collective-permute-start.9 = (bf16[96,1024]{1,0:T(8,128)(2,1)S(1)}, bf16[96,1024]{1,0:T(8,128)(2,1)S(1)}, u32[]{:S(2)}, u32[]{:S(2)}) collective-permute-start(bf16[96,1024]{1,0:T(8,128)(2,1)S(1)} %get-tuple-element.28), channel_id=1, source_target_pairs={{0,1},{1,0},{2,3},{3,2},{4,5},{5,4},{6,7},{7,6},{8,9},{9,8},{10,11... | collective-permute-start | bytes 589832 | tf_op jit(solution)/shard_map/ppermute | solution.py:204
  29.0 1.5 %collective-permute-start.10 = (bf16[96,1024]{1,0:T(8,128)(2,1)S(1)}, bf16[96,1024]{1,0:T(8,128)(2,1)S(1)}, u32[]{:S(2)}, u32[]{:S(2)}) collective-permute-start(bf16[96,1024]{1,0:T(8,128)(2,1)S(1)} %get-tuple-element.29), channel_id=1, source_target_pairs={{0,1},{1,0},{2,3},{3,2},{4,5},{5,4},{6,7},{7,6},{8,9},{9,8},{10,11... | collective-permute-start | bytes 589832 | tf_op jit(solution)/shard_map/ppermute | solution.py:204
  31.7 1.6 %collective-permute-start.11 = (bf16[128,1024]{1,0:T(8,128)(2,1)S(1)}, bf16[128,1024]{1,0:T(8,128)(2,1)S(1)}, u32[]{:S(2)}, u32[]{:S(2)}) collective-permute-start(bf16[128,1024]{1,0:T(8,128)(2,1)S(1)} %collective-permute-done.2.refs_8_.late_ref), channel_id=1, source_target_pairs={{0,1},{1,0},{2,3},{3,2},{4,5},{5,4},{6,7},{7,6},{8,9},{9,8},{10,11... | collective-permute-start | bytes 786440 | tf_op jit(solution)/shard_map/ppermute | solution.py:204

commit v28 on v24

--- a/solution.py
+++ b/solution.py
@@ -151,6 +151,13 @@
     return call_kernel("count", functools.partial(count_kernel, starts, size), out_shape, *pieces)
 
 
+def cross_kernel(pieces, *refs):
+    *piece_refs, before_ref, count_ref = refs
+    own = jnp.concatenate([piece[...] for piece in piece_refs[:pieces]], axis=0)
+    other = jnp.concatenate([piece[...] for piece in piece_refs[pieces:]], axis=0)
+    count_ref[...] = before_ref[...] + count_against(other, own, [], own.shape[0])
+
+
 def late_kernel(*refs):
     *piece_refs, late_ref, early_ref, own_ref = refs
     early = jnp.concatenate([piece[...] for piece in piece_refs], axis=0)
@@ -160,7 +167,7 @@
     own_ref[...] = count_against(early, late, [], size) + count_against(late, late, [0], size)
 
 
-def finish_kernel(starts, places, late_ref, other_ref, counts_ref, early_ref, own_ref, out_ref):
+def finish_kernel(places, late_ref, other_ref, counts_ref, early_ref, own_ref, out_ref):
     size = out_ref.shape[2]
     late = late_ref[...]
     own = own_ref[...] + count_against(other_ref[...], late, [], size)
@@ -170,9 +177,8 @@
     for k, place in enumerate(places()):
         if k < blocks_early:
             block = early[:, k * size : (k + 1) * size]
-            if k * size in starts:
-                j = starts.index(k * size)
-                block = block + counts_ref[:, j * size : (j + 1) * size]
+            if k * size < counts_ref.shape[1]:
+                block = block + counts_ref[:, k * size : (k + 1) * size]
         else:
             block = own[:, (k - blocks_early) * size : (k - blocks_early + 1) * size]
         out_ref[pl.ds(place, 1), 0, :] = block
@@ -260,18 +266,24 @@
     parts = call_kernel(
         "regroup", functools.partial(regroup_kernel, len(early)), [part] * 4, *early, flops=10**10
     )
-    early += [swap_cores(x) for x in parts]
-
-    span = cores * capacity
-    starts = [k * span for k in range(steps - 1)]
-    starts += [half_way + start + capacity for start in starts]
-    counts = soft_counts(early, starts, capacity)
+    swapped = [swap_cores(x) for x in parts]
+
+    counts = soft_counts(early, [0], half_way)
+    counts = call_kernel(
+        "cross",
+        functools.partial(cross_kernel, len(early)),
+        jax.ShapeDtypeStruct((1, half_way), jnp.float32),
+        *early,
+        *swapped,
+        counts,
+    )
+    early += swapped
 
     late_piece, _ = lax.optimization_barrier((last_piece, counts))
     late_other = swap_cores(late_piece)
     sums = [
         jax.ShapeDtypeStruct((1, 2 * half_way), jnp.float32),
-        jax.ShapeDtypeStruct((1, span), jnp.float32),
+        jax.ShapeDtypeStruct((1, cores * capacity), jnp.float32),
     ]
     early_sums, own_sums = call_kernel("late", late_kernel, sums, *early, last_piece)
 
@@ -287,7 +299,7 @@
 
     counts = call_kernel(
         "finish",
-        functools.partial(finish_kernel, starts, places),
+        functools.partial(finish_kernel, places),
         jax.ShapeDtypeStruct((clusters * cores, 1, capacity), jnp.float32),
         last_piece,
         late_other,

time: 44 us -> 44 us (level)
  waiting for transfers between devices: 6.02 us -> 5.31 us
  blocking collectives: 9.68 us -> 10.2 us
    ppermute x7, waiting for transfers between devices: 1.54 us -> 0.83 us  [swap_cores(): return lax.ppermute(x, 'sub', [(i, i ^ 1) for i in range(cores)])]
    all_to_all x1, blocking collectives: 9.68 us -> 10.2 us  [body_by_chip(): lax.all_to_all(counts, ('owner', 'helper', 'sub'), split_axis=0, concat_a...]
    pallas_call x9 -> x10, Pallas kernels: 5.11 us -> 5.26 us  [call_kernel(): pl.pallas_call(kernel, out_shape=out_shape, in_specs=[VMEM] * len(args),...]
  transfers between devices with their start and end apart: 12 -> 12, of which waited for: 7 -> 6; matrix products, arithmetic and copies ran while one was open for 0% -> 0% of each run, Pallas kernels for 9% -> 10%
where the time goes in v28:
time: 44 us; the launch traced here: 43.8 us
  starting transfers between devices  21.7 us (49%)
  blocking collectives  10.2 us (23%)
  waiting for transfers between devices  5.31 us (12%)
  Pallas kernels  5.26 us (12%)
  local copies, waits for them, and re-layouts  1.27 us (3%)
    ppermute x5, starting transfers between devices, across(): return lax.ppermute(x, ('owner', 'helper', 'sub'), pairs)  11 us
    ppermute x7, starting transfers between devices, swap_cores(): return lax.ppermute(x, 'sub', [(i, i ^ 1) for i in range(cores)])  10.7 us
    all_to_all x1, blocking collectives, body_by_chip(): lax.all_to_all(counts, ('owner', 'helper', 'sub'), split_axis=0, concat_a...  10.2 us
    pallas_call x10, Pallas kernels, call_kernel(): pl.pallas_call(kernel, out_shape=out_shape, in_specs=[VMEM] * len(args),...  5.26 us
    ppermute x5, waiting for transfers between devices, across(): return lax.ppermute(x, ('owner', 'helper', 'sub'), pairs)  4.48 us
    unnamed x4, local copies, waits for them, and re-layouts  1.27 us
  transfers between devices with their start and end apart: 12, of which 6 were waited for; matrix products, arithmetic and copies ran while one was open for 0% of the time, Pallas kernels for 10%

profile of v28, /device:TPU:0, one launch (start us, length us, event | category | flops | bytes accessed | tf_op | source)
XLA Modules:
  0.0 43.8 jit_solution(11330470365720276740)
XLA Ops:
  0.0 0.5 %collective-permute-start = (bf16[256,1024]{1,0:T(8,128)(2,1)}, bf16[256,1024]{1,0:T(8,128)(2,1)S(1)}, u32[]{:S(2)}, u32[]{:S(2)}) collective-permute-start(bf16[256,1024]{1,0:T(8,128)(2,1)} %refs_0_.3), channel_id=1, source_target_pairs={{0,1},{1,0},{2,3},{3,2},{4,5},{5,4},{6,7},{7,6},{8,9},{9,8},{10,11... | collective-permute-start | bytes 1572872 | tf_op jit(solution)/shard_map/ppermute | solution.py:210
  0.5 0.2 copy-done.1
  0.7 0.5 %collective-permute-start.1 = (s32[1,256]{1,0:T(1,128)S(1)}, s32[1,256]{1,0:T(1,128)S(1)}, u32[]{:S(2)}, u32[]{:S(2)}) collective-permute-start(s32[1,256]{1,0:T(1,128)S(1)} %bitcast.2), channel_id=1, source_target_pairs={{0,1},{1,0},{2,3},{3,2},{4,5},{5,4},{6,7},{7,6},{8,9},{9,8},{10,11... | collective-permute-start | bytes 3080 | tf_op jit(solution)/shard_map/ppermute | solution.py:210
  1.1 1.0 %copy-done = bf16[256,1024]{1,0:T(8,128)(2,1)S(1)} copy-done((bf16[256,1024]{1,0:T(8,128)(2,1)S(1)}, bf16[256,1024]{1,0:T(8,128)(2,1)}, u32[]{:S(2)}) %copy-start) | copy-done | bytes 524312
  2.2 0.5 %route_first.1 = (bf16[64,1024]{1,0:T(8,128)(2,1)S(1)}, s32[1,256]{1,0:T(1,128)S(1)}) custom-call(bf16[256,1024]{1,0:T(8,128)(2,1)S(1)} %copy-done, s32[1,256]{1,0:T(1,128)S(1)} %bitcast.3), custom_call_target="tpu_custom_call" | custom-call | tf_op jit(solution)/shard_map/route_first/pallas_call | solution.py:94
  2.6 3.7 %collective-permute-start.3 = (bf16[64,1024]{1,0:T(8,128)(2,1)S(1)}, bf16[64,1024]{1,0:T(8,128)(2,1)S(1)}, u32[]{:S(2)}, u32[]{:S(2)}) collective-permute-start(bf16[64,1024]{1,0:T(8,128)(2,1)S(1)} %get-tuple-element.23), channel_id=1, source_target_pairs={{0,8},{1,11},{2,10},{3,9},{4,12},{5,15},{6,14},{7,13},{8,0},{9,3},... | collective-permute-start | bytes 393224 | tf_op jit(solution)/shard_map/ppermute | solution.py:226
  6.3 0.0 collective-permute-done.1.refs_3_
  6.3 0.0 collective-permute-done.refs_1_
  6.3 0.6 %route_near.1 = (bf16[128,1024]{1,0:T(8,128)(2,1)S(1)}, bf16[128,1024]{1,0:T(8,128)(2,1)S(1)}) custom-call(bf16[256,1024]{1,0:T(8,128)(2,1)S(1)} %copy-done, bf16[256,1024]{1,0:T(8,128)(2,1)S(1)} %collective-permute-done.refs_1_, s32[1,256]{1,0:T(1,128)S(1)} %get-tuple-element.21.refs_2_.slot_ref, s32[1,256]{1,0:T(1,128)S(1)} %collective-permute-done.1.refs_3_), custom_call_target="tpu_custom_call" | custom-call | tf_op jit(solution)/shard_map/route_near/pallas_call | solution.py:94
  6.9 0.7 %collective-permute-start.5 = (bf16[128,1024]{1,0:T(8,128)(2,1)S(1)}, bf16[128,1024]{1,0:T(8,128)(2,1)S(1)}, u32[]{:S(2)}, u32[]{:S(2)}) collective-permute-start(bf16[128,1024]{1,0:T(8,128)(2,1)S(1)} %get-tuple-element.20), channel_id=1, source_target_pairs={{0,0},{1,3},{2,2},{3,1},{4,4},{5,7},{6,6},{7,5},{8,8},{9,11},{10,1... | collective-permute-start | bytes 786440 | tf_op jit(solution)/shard_map/ppermute | solution.py:226
  7.6 1.6 %collective-permute-start.6 = (bf16[128,1024]{1,0:T(8,128)(2,1)S(1)}, bf16[128,1024]{1,0:T(8,128)(2,1)S(1)}, u32[]{:S(2)}, u32[]{:S(2)}) collective-permute-start(bf16[128,1024]{1,0:T(8,128)(2,1)S(1)} %get-tuple-element.25), channel_id=1, source_target_pairs={{0,4},{1,7},{2,6},{3,5},{4,0},{5,3},{6,2},{7,1},{8,12},{9,15},{10,... | collective-permute-start | bytes 786440 | tf_op jit(solution)/shard_map/ppermute | solution.py:226
  9.2 0.6 %route_far.1 = (bf16[64,1024]{1,0:T(8,128)(2,1)S(1)}, bf16[128,1024]{1,0:T(8,128)(2,1)S(1)}) custom-call(bf16[256,1024]{1,0:T(8,128)(2,1)S(1)} %copy-done, bf16[256,1024]{1,0:T(8,128)(2,1)S(1)} %collective-permute-done.refs_1_, s32[1,256]{1,0:T(1,128)S(1)} %get-tuple-element.21.refs_2_.slot_ref, s32[1,256]{1,0:T(1,128)S(1)} %collective-permute-done.1.refs_3_), custom_call_target="tpu_custom_call" | custom-call | flops 10000000000 | tf_op jit(solution)/shard_map/route_far/pallas_call | solution.py:94
  9.8 0.4 collective-permute-start.4
  10.2 2.6 %collective-permute-done.3.refs_0_ = bf16[64,1024]{1,0:T(8,128)(2,1)S(1)} collective-permute-done((bf16[64,1024]{1,0:T(8,128)(2,1)S(1)}, bf16[64,1024]{1,0:T(8,128)(2,1)S(1)}, u32[]{:S(2)}, u32[]{:S(2)}) %collective-permute-start.3) | collective-permute-done | bytes 131104 | tf_op jit(solution)/shard_map/ppermute | solution.py:226
  12.8 4.6 %collective-permute-start.2 = (bf16[128,1024]{1,0:T(8,128)(2,1)S(1)}, bf16[128,1024]{1,0:T(8,128)(2,1)S(1)}, u32[]{:S(2)}, u32[]{:S(2)}) collective-permute-start(bf16[128,1024]{1,0:T(8,128)(2,1)S(1)} %get-tuple-element.22), channel_id=1, source_target_pairs={{0,12},{1,15},{2,14},{3,13},{4,8},{5,11},{6,10},{7,9},{8,4},{9,7},... | collective-permute-start | bytes 786440 | tf_op jit(solution)/shard_map/ppermute | solution.py:226
  17.4 1.9 %collective-permute-done.6.refs_3_ = bf16[128,1024]{1,0:T(8,128)(2,1)S(1)} collective-permute-done((bf16[128,1024]{1,0:T(8,128)(2,1)S(1)}, bf16[128,1024]{1,0:T(8,128)(2,1)S(1)}, u32[]{:S(2)}, u32[]{:S(2)}) %collective-permute-start.6) | collective-permute-done | bytes 262176 | tf_op jit(solution)/shard_map/ppermute | solution.py:226
  19.3 0.1 regroup.1
  19.4 8.9 %collective-permute-start.7 = (bf16[96,1024]{1,0:T(8,128)(2,1)S(1)}, bf16[96,1024]{1,0:T(8,128)(2,1)S(1)}, u32[]{:S(2)}, u32[]{:S(2)}) collective-permute-start(bf16[96,1024]{1,0:T(8,128)(2,1)S(1)} %get-tuple-element.26), channel_id=1, source_target_pairs={{0,1},{1,0},{2,3},{3,2},{4,5},{5,4},{6,7},{7,6},{8,9},{9,8},{10,11... | collective-permute-start | bytes 589832 | tf_op jit(solution)/shard_map/ppermute | solution.py:210
  28.3 0.1 collective-permute-start.8
  28.3 0.4 collective-permute-start.9
  28.8 0.1 collective-permute-start.10
  28.8 0.7 %count.1.refs_8_ = f32[1,384]{1,0:T(1,128)S(1)} custom-call(bf16[64,1024]{1,0:T(8,128)(2,1)S(1)} %pass.1.refs_0_, bf16[64,1024]{1,0:T(8,128)(2,1)S(1)} %collective-permute-done.4.refs_1_, bf16[128,1024]{1,0:T(8,128)(2,1)S(1)} %collective-permute-done.5.refs_2_, bf16[128,1024]{1,0:T(8,128)(2,1)S(1)} %collective-permute-done.6.refs_3_), custom_call_target="tpu_custom_call" | custom-call | tf_op jit(solution)/shard_map/count/pallas_call | solution.py:94
  29.5 0.2 collective-permute-done.8.refs_5_
  29.7 0.3 collective-permute-done.9.refs_6_
  30.0 0.3 collective-permute-done.10.refs_7_
  30.3 0.7 %cross.1.counts_ref = f32[1,384]{1,0:T(1,128)S(1)} custom-call(bf16[64,1024]{1,0:T(8,128)(2,1)S(1)} %pass.1.refs_0_, bf16[64,1024]{1,0:T(8,128)(2,1)S(1)} %collective-permute-done.4.refs_1_, bf16[128,1024]{1,0:T(8,128)(2,1)S(1)} %collective-permute-done.5.refs_2_, bf16[128,1024]{1,0:T(8,128)(2,1)S(1)} %collective-permute-done.6.refs_3_, ...), custom_call_target="tpu_custom_call" | custom-call | tf_op jit(solution)/shard_map/cross/pallas_call | solution.py:94
  30.9 0.3 collective-permute-start.11
  31.3 1.1 %late.1 = (f32[1,768]{1,0:T(1,128)S(1)}, f32[1,128]{1,0:T(1,128)S(1)}) custom-call(bf16[64,1024]{1,0:T(8,128)(2,1)S(1)} %pass.1.refs_0_, bf16[64,1024]{1,0:T(8,128)(2,1)S(1)} %collective-permute-done.4.refs_1_, bf16[128,1024]{1,0:T(8,128)(2,1)S(1)} %collective-permute-done.5.refs_2_, bf16[128,1024]{1,0:T(8,128)(2,1)S(1)} %collective-permute-done.6.refs_3_, ...), custom_call_target="tpu_custom_call" | custom-call | tf_op jit(solution)/shard_map/late/pallas_call | solution.py:94
  32.4 0.1 collective-permute-done.11.other_ref
  32.5 0.3 finish.1
  32.9 10.2 %all_to_all.5.counts_ref = f32[16,1,64]{2,1,0:T(1,128)S(1)} all-to-all(f32[16,1,64]{2,1,0:T(1,128)S(1)} %finish.1), channel_id=1, replica_groups=mesh['groups'=2,'owner'=4,'helper'=2,'sub'=2] {'owner','helper','sub'}, dimensions={0} | all-to-all | bytes 8192 | tf_op jit(solution)/shard_map/all_to_all | solution.py:310
  43.1 0.7 %select.1 = f32[1,256]{1,0:T(1,128)} custom-call(f32[16,1,64]{2,1,0:T(1,128)S(1)} %all_to_all.5.counts_ref, s32[1,256]{1,0:T(1,128)S(1)} %get-tuple-element.21.refs_2_.slot_ref), custom_call_target="tpu_custom_call" | custom-call | tf_op jit(solution)/shard_map/select/pallas_call | solution.py:94
  (7 shorter events, 0.0 us)
Async XLA Ops:
  0.0 0.7 %copy-start.1 = (s32[256]{0:T(256)S(1)}, s32[256]{0:T(256)}, u32[]{:S(2)}) copy-start(s32[256]{0:T(256)} %param.3) | copy-start | bytes 3076
  0.0 6.3 %collective-permute-start = (bf16[256,1024]{1,0:T(8,128)(2,1)}, bf16[256,1024]{1,0:T(8,128)(2,1)S(1)}, u32[]{:S(2)}, u32[]{:S(2)}) collective-permute-start(bf16[256,1024]{1,0:T(8,128)(2,1)} %refs_0_.3), channel_id=1, source_target_pairs={{0,1},{1,0},{2,3},{3,2},{4,5},{5,4},{6,7},{7,6},{8,9},{9,8},{10,11... | collective-permute-start | bytes 1572872 | tf_op jit(solution)/shard_map/ppermute | solution.py:210
  0.7 5.6 %collective-permute-start.1 = (s32[1,256]{1,0:T(1,128)S(1)}, s32[1,256]{1,0:T(1,128)S(1)}, u32[]{:S(2)}, u32[]{:S(2)}) collective-permute-start(s32[1,256]{1,0:T(1,128)S(1)} %bitcast.2), channel_id=1, source_target_pairs={{0,1},{1,0},{2,3},{3,2},{4,5},{5,4},{6,7},{7,6},{8,9},{9,8},{10,11... | collective-permute-start | bytes 3080 | tf_op jit(solution)/shard_map/ppermute | solution.py:210
  1.1 1.0 %copy-start = (bf16[256,1024]{1,0:T(8,128)(2,1)S(1)}, bf16[256,1024]{1,0:T(8,128)(2,1)}, u32[]{:S(2)}) copy-start(bf16[256,1024]{1,0:T(8,128)(2,1)} %refs_0_.3) | copy-start | bytes 1572868
  2.6 10.2 %collective-permute-start.3 = (bf16[64,1024]{1,0:T(8,128)(2,1)S(1)}, bf16[64,1024]{1,0:T(8,128)(2,1)S(1)}, u32[]{:S(2)}, u32[]{:S(2)}) collective-permute-start(bf16[64,1024]{1,0:T(8,128)(2,1)S(1)} %get-tuple-element.23), channel_id=1, source_target_pairs={{0,8},{1,11},{2,10},{3,9},{4,12},{5,15},{6,14},{7,13},{8,0},{9,3},... | collective-permute-start | bytes 393224 | tf_op jit(solution)/shard_map/ppermute | solution.py:226
  6.9 12.4 %collective-permute-start.5 = (bf16[128,1024]{1,0:T(8,128)(2,1)S(1)}, bf16[128,1024]{1,0:T(8,128)(2,1)S(1)}, u32[]{:S(2)}, u32[]{:S(2)}) collective-permute-start(bf16[128,1024]{1,0:T(8,128)(2,1)S(1)} %get-tuple-element.20), channel_id=1, source_target_pairs={{0,0},{1,3},{2,2},{3,1},{4,4},{5,7},{6,6},{7,5},{8,8},{9,11},{10,1... | collective-permute-start | bytes 786440 | tf_op jit(solution)/shard_map/ppermute | solution.py:226
  7.6 11.7 %collective-permute-start.6 = (bf16[128,1024]{1,0:T(8,128)(2,1)S(1)}, bf16[128,1024]{1,0:T(8,128)(2,1)S(1)}, u32[]{:S(2)}, u32[]{:S(2)}) collective-permute-start(bf16[128,1024]{1,0:T(8,128)(2,1)S(1)} %get-tuple-element.25), channel_id=1, source_target_pairs={{0,4},{1,7},{2,6},{3,5},{4,0},{5,3},{6,2},{7,1},{8,12},{9,15},{10,... | collective-permute-start | bytes 786440 | tf_op jit(solution)/shard_map/ppermute | solution.py:226
  9.8 7.6 %collective-permute-start.4 = (bf16[64,1024]{1,0:T(8,128)(2,1)S(1)}, bf16[64,1024]{1,0:T(8,128)(2,1)S(1)}, u32[]{:S(2)}, u32[]{:S(2)}) collective-permute-start(bf16[64,1024]{1,0:T(8,128)(2,1)S(1)} %get-tuple-element.24), channel_id=1, source_target_pairs={{0,8},{1,11},{2,10},{3,9},{4,12},{5,15},{6,14},{7,13},{8,0},{9,3},... | collective-permute-start | bytes 393224 | tf_op jit(solution)/shard_map/ppermute | solution.py:226
  12.8 18.1 %collective-permute-start.2 = (bf16[128,1024]{1,0:T(8,128)(2,1)S(1)}, bf16[128,1024]{1,0:T(8,128)(2,1)S(1)}, u32[]{:S(2)}, u32[]{:S(2)}) collective-permute-start(bf16[128,1024]{1,0:T(8,128)(2,1)S(1)} %get-tuple-element.22), channel_id=1, source_target_pairs={{0,12},{1,15},{2,14},{3,13},{4,8},{5,11},{6,10},{7,9},{8,4},{9,7},... | collective-permute-start | bytes 786440 | tf_op jit(solution)/shard_map/ppermute | solution.py:226
  19.4 10.1 %collective-permute-start.7 = (bf16[96,1024]{1,0:T(8,128)(2,1)S(1)}, bf16[96,1024]{1,0:T(8,128)(2,1)S(1)}, u32[]{:S(2)}, u32[]{:S(2)}) collective-permute-start(bf16[96,1024]{1,0:T(8,128)(2,1)S(1)} %get-tuple-element.26), channel_id=1, source_target_pairs={{0,1},{1,0},{2,3},{3,2},{4,5},{5,4},{6,7},{7,6},{8,9},{9,8},{10,11... | collective-permute-start | bytes 589832 | tf_op jit(solution)/shard_map/ppermute | solution.py:210
  28.3 1.4 %collective-permute-start.8 = (bf16[96,1024]{1,0:T(8,128)(2,1)S(1)}, bf16[96,1024]{1,0:T(8,128)(2,1)S(1)}, u32[]{:S(2)}, u32[]{:S(2)}) collective-permute-start(bf16[96,1024]{1,0:T(8,128)(2,1)S(1)} %get-tuple-element.27), channel_id=1, source_target_pairs={{0,1},{1,0},{2,3},{3,2},{4,5},{5,4},{6,7},{7,6},{8,9},{9,8},{10,11... | collective-permute-start | bytes 589832 | tf_op jit(solution)/shard_map/ppermute | solution.py:210
  28.3 1.6 %collective-permute-start.9 = (bf16[96,1024]{1,0:T(8,128)(2,1)S(1)}, bf16[96,1024]{1,0:T(8,128)(2,1)S(1)}, u32[]{:S(2)}, u32[]{:S(2)}) collective-permute-start(bf16[96,1024]{1,0:T(8,128)(2,1)S(1)} %get-tuple-element.28), channel_id=1, source_target_pairs={{0,1},{1,0},{2,3},{3,2},{4,5},{5,4},{6,7},{7,6},{8,9},{9,8},{10,11... | collective-permute-start | bytes 589832 | tf_op jit(solution)/shard_map/ppermute | solution.py:210
  28.8 1.5 %collective-permute-start.10 = (bf16[96,1024]{1,0:T(8,128)(2,1)S(1)}, bf16[96,1024]{1,0:T(8,128)(2,1)S(1)}, u32[]{:S(2)}, u32[]{:S(2)}) collective-permute-start(bf16[96,1024]{1,0:T(8,128)(2,1)S(1)} %get-tuple-element.29), channel_id=1, source_target_pairs={{0,1},{1,0},{2,3},{3,2},{4,5},{5,4},{6,7},{7,6},{8,9},{9,8},{10,11... | collective-permute-start | bytes 589832 | tf_op jit(solution)/shard_map/ppermute | solution.py:210
  30.9 1.6 %collective-permute-start.11 = (bf16[128,1024]{1,0:T(8,128)(2,1)S(1)}, bf16[128,1024]{1,0:T(8,128)(2,1)S(1)}, u32[]{:S(2)}, u32[]{:S(2)}) collective-permute-start(bf16[128,1024]{1,0:T(8,128)(2,1)S(1)} %collective-permute-done.2.refs_8_.late_ref), channel_id=1, source_target_pairs={{0,1},{1,0},{2,3},{3,2},{4,5},{5,4},{6,7},{7,6},{8,9},{9,8},{10,11... | collective-permute-start | bytes 786440 | tf_op jit(solution)/shard_map/ppermute | solution.py:210

commit v29 on v28

--- a/solution.py
+++ b/solution.py
@@ -184,7 +184,7 @@
         out_ref[pl.ds(place, 1), 0, :] = block
 
 
-def select_kernel(clusters, capacity, counts_ref, slot_ref, out_ref):
+def select_kernel(clusters, capacity, backwards, counts_ref, slot_ref, out_ref):
     counts = counts_ref[:, 0, :]
     slot = slot_ref[...]
     doc_count = slot.shape[1]
@@ -195,13 +195,16 @@
         counts, hot, precision=lax.Precision.HIGHEST, preferred_element_type=jnp.float32
     )
     parts = counts.shape[0] // clusters
-    chosen = lax.broadcasted_iota(jnp.int32, by_block.shape, 0) // parts == block
+    row = lax.broadcasted_iota(jnp.int32, by_block.shape, 0)
+    if backwards:
+        row = counts.shape[0] - 1 - row
+    chosen = row // parts == block
     out_ref[...] = jnp.sum(jnp.where(chosen, by_block, 0.0), axis=0, keepdims=True)
 
 
-def select(counts, slot, clusters, capacity):
+def select(counts, slot, clusters, capacity, backwards=False):
     out_shape = jax.ShapeDtypeStruct(slot.shape, jnp.float32)
-    kernel = functools.partial(select_kernel, clusters, capacity)
+    kernel = functools.partial(select_kernel, clusters, capacity, backwards)
     return call_kernel("select", kernel, out_shape, counts, slot, limit=8 * 2**20)[0]
 
 
@@ -295,7 +298,8 @@
                 there = (chip ^ (p * cores + here)) * cores
                 devices += [there + here, there + 1 - here]
         there = (chip ^ (last * cores + core)) * cores
-        return devices + [there + core, there + 1 - core]
+        devices += [there + core, there + 1 - core]
+        return [clusters * cores - 1 - device for device in devices]
 
     counts = call_kernel(
         "finish",
@@ -308,9 +312,14 @@
         own_sums,
     )
     back = lax.all_to_all(
-        counts, ("owner", "helper", "sub"), split_axis=0, concat_axis=0, tiled=True
-    )
-    return select(back, slot, clusters, capacity)
+        counts,
+        ("owner", "helper", "sub"),
+        split_axis=0,
+        concat_axis=0,
+        axis_index_groups=[list(reversed(range(clusters * cores)))],
+        tiled=True,
+    )
+    return select(back, slot, clusters, capacity, backwards=True)
 
 
 def body_by_owner(embeddings, cluster_id):

time: 44 us -> 42 us (0.955)
  blocking collectives: 10.2 us -> 8.22 us
    all_to_all x1, blocking collectives: 10.2 us -> 8.22 us  [body_by_chip(): lax.all_to_all(counts, ('owner', 'helper', 'sub'), split_axis=0, concat_a...]
where the time goes in v29:
time: 42 us; the launch traced here: 41.8 us
  starting transfers between devices  21.7 us (52%)
  blocking collectives  8.22 us (20%)
  waiting for transfers between devices  5.31 us (13%)
  Pallas kernels  5.26 us (13%)
  local copies, waits for them, and re-layouts  1.27 us (3%)
    ppermute x5, starting transfers between devices, across(): return lax.ppermute(x, ('owner', 'helper', 'sub'), pairs)  11 us
    ppermute x7, starting transfers between devices, swap_cores(): return lax.ppermute(x, 'sub', [(i, i ^ 1) for i in range(cores)])  10.7 us
    all_to_all x1, blocking collectives, body_by_chip(): lax.all_to_all(counts, ('owner', 'helper', 'sub'), split_axis=0, concat_a...  8.22 us
    pallas_call x10, Pallas kernels, call_kernel(): pl.pallas_call(kernel, out_shape=out_shape, in_specs=[VMEM] * len(args),...  5.26 us
    ppermute x5, waiting for transfers between devices, across(): return lax.ppermute(x, ('owner', 'helper', 'sub'), pairs)  4.48 us
    unnamed x4, local copies, waits for them, and re-layouts  1.27 us
  transfers between devices with their start and end apart: 12, of which 6 were waited for; matrix products, arithmetic and copies ran while one was open for 0% of the time, Pallas kernels for 10%

profile of v29, /device:TPU:0, one launch (start us, length us, event | category | flops | bytes accessed | tf_op | source)
XLA Modules:
  0.0 41.8 jit_solution(14354953478852347530)
XLA Ops:
  0.0 0.5 %collective-permute-start = (bf16[256,1024]{1,0:T(8,128)(2,1)}, bf16[256,1024]{1,0:T(8,128)(2,1)S(1)}, u32[]{:S(2)}, u32[]{:S(2)}) collective-permute-start(bf16[256,1024]{1,0:T(8,128)(2,1)} %refs_0_.3), channel_id=1, source_target_pairs={{0,1},{1,0},{2,3},{3,2},{4,5},{5,4},{6,7},{7,6},{8,9},{9,8},{10,11... | collective-permute-start | bytes 1572872 | tf_op jit(solution)/shard_map/ppermute | solution.py:213
  0.5 0.2 copy-done.1
  0.7 0.5 %collective-permute-start.1 = (s32[1,256]{1,0:T(1,128)S(1)}, s32[1,256]{1,0:T(1,128)S(1)}, u32[]{:S(2)}, u32[]{:S(2)}) collective-permute-start(s32[1,256]{1,0:T(1,128)S(1)} %bitcast.2), channel_id=1, source_target_pairs={{0,1},{1,0},{2,3},{3,2},{4,5},{5,4},{6,7},{7,6},{8,9},{9,8},{10,11... | collective-permute-start | bytes 3080 | tf_op jit(solution)/shard_map/ppermute | solution.py:213
  1.1 1.0 %copy-done = bf16[256,1024]{1,0:T(8,128)(2,1)S(1)} copy-done((bf16[256,1024]{1,0:T(8,128)(2,1)S(1)}, bf16[256,1024]{1,0:T(8,128)(2,1)}, u32[]{:S(2)}) %copy-start) | copy-done | bytes 524312
  2.2 0.5 %route_first.1 = (bf16[64,1024]{1,0:T(8,128)(2,1)S(1)}, s32[1,256]{1,0:T(1,128)S(1)}) custom-call(bf16[256,1024]{1,0:T(8,128)(2,1)S(1)} %copy-done, s32[1,256]{1,0:T(1,128)S(1)} %bitcast.3), custom_call_target="tpu_custom_call" | custom-call | tf_op jit(solution)/shard_map/route_first/pallas_call | solution.py:94
  2.6 3.7 %collective-permute-start.3 = (bf16[64,1024]{1,0:T(8,128)(2,1)S(1)}, bf16[64,1024]{1,0:T(8,128)(2,1)S(1)}, u32[]{:S(2)}, u32[]{:S(2)}) collective-permute-start(bf16[64,1024]{1,0:T(8,128)(2,1)S(1)} %get-tuple-element.23), channel_id=1, source_target_pairs={{0,8},{1,11},{2,10},{3,9},{4,12},{5,15},{6,14},{7,13},{8,0},{9,3},... | collective-permute-start | bytes 393224 | tf_op jit(solution)/shard_map/ppermute | solution.py:229
  6.3 0.0 collective-permute-done.refs_1_
  6.3 0.6 %route_near.1 = (bf16[128,1024]{1,0:T(8,128)(2,1)S(1)}, bf16[128,1024]{1,0:T(8,128)(2,1)S(1)}) custom-call(bf16[256,1024]{1,0:T(8,128)(2,1)S(1)} %copy-done, bf16[256,1024]{1,0:T(8,128)(2,1)S(1)} %collective-permute-done.refs_1_, s32[1,256]{1,0:T(1,128)S(1)} %get-tuple-element.21.refs_2_.slot_ref, s32[1,256]{1,0:T(1,128)S(1)} %collective-permute-done.1.refs_3_), custom_call_target="tpu_custom_call" | custom-call | tf_op jit(solution)/shard_map/route_near/pallas_call | solution.py:94
  6.9 0.7 %collective-permute-start.5 = (bf16[128,1024]{1,0:T(8,128)(2,1)S(1)}, bf16[128,1024]{1,0:T(8,128)(2,1)S(1)}, u32[]{:S(2)}, u32[]{:S(2)}) collective-permute-start(bf16[128,1024]{1,0:T(8,128)(2,1)S(1)} %get-tuple-element.20), channel_id=1, source_target_pairs={{0,0},{1,3},{2,2},{3,1},{4,4},{5,7},{6,6},{7,5},{8,8},{9,11},{10,1... | collective-permute-start | bytes 786440 | tf_op jit(solution)/shard_map/ppermute | solution.py:229
  7.6 1.6 %collective-permute-start.6 = (bf16[128,1024]{1,0:T(8,128)(2,1)S(1)}, bf16[128,1024]{1,0:T(8,128)(2,1)S(1)}, u32[]{:S(2)}, u32[]{:S(2)}) collective-permute-start(bf16[128,1024]{1,0:T(8,128)(2,1)S(1)} %get-tuple-element.25), channel_id=1, source_target_pairs={{0,4},{1,7},{2,6},{3,5},{4,0},{5,3},{6,2},{7,1},{8,12},{9,15},{10,... | collective-permute-start | bytes 786440 | tf_op jit(solution)/shard_map/ppermute | solution.py:229
  9.2 0.6 %route_far.1 = (bf16[64,1024]{1,0:T(8,128)(2,1)S(1)}, bf16[128,1024]{1,0:T(8,128)(2,1)S(1)}) custom-call(bf16[256,1024]{1,0:T(8,128)(2,1)S(1)} %copy-done, bf16[256,1024]{1,0:T(8,128)(2,1)S(1)} %collective-permute-done.refs_1_, s32[1,256]{1,0:T(1,128)S(1)} %get-tuple-element.21.refs_2_.slot_ref, s32[1,256]{1,0:T(1,128)S(1)} %collective-permute-done.1.refs_3_), custom_call_target="tpu_custom_call" | custom-call | flops 10000000000 | tf_op jit(solution)/shard_map/route_far/pallas_call | solution.py:94
  9.8 0.4 collective-permute-start.4
  10.2 2.6 %collective-permute-done.3.refs_0_ = bf16[64,1024]{1,0:T(8,128)(2,1)S(1)} collective-permute-done((bf16[64,1024]{1,0:T(8,128)(2,1)S(1)}, bf16[64,1024]{1,0:T(8,128)(2,1)S(1)}, u32[]{:S(2)}, u32[]{:S(2)}) %collective-permute-start.3) | collective-permute-done | bytes 131104 | tf_op jit(solution)/shard_map/ppermute | solution.py:229
  12.8 4.6 %collective-permute-start.2 = (bf16[128,1024]{1,0:T(8,128)(2,1)S(1)}, bf16[128,1024]{1,0:T(8,128)(2,1)S(1)}, u32[]{:S(2)}, u32[]{:S(2)}) collective-permute-start(bf16[128,1024]{1,0:T(8,128)(2,1)S(1)} %get-tuple-element.22), channel_id=1, source_target_pairs={{0,12},{1,15},{2,14},{3,13},{4,8},{5,11},{6,10},{7,9},{8,4},{9,7},... | collective-permute-start | bytes 786440 | tf_op jit(solution)/shard_map/ppermute | solution.py:229
  17.4 0.0 collective-permute-done.4.refs_1_
  17.4 1.9 %collective-permute-done.6.refs_3_ = bf16[128,1024]{1,0:T(8,128)(2,1)S(1)} collective-permute-done((bf16[128,1024]{1,0:T(8,128)(2,1)S(1)}, bf16[128,1024]{1,0:T(8,128)(2,1)S(1)}, u32[]{:S(2)}, u32[]{:S(2)}) %collective-permute-start.6) | collective-permute-done | bytes 262176 | tf_op jit(solution)/shard_map/ppermute | solution.py:229
  19.3 0.1 regroup.1
  19.4 8.9 %collective-permute-start.7 = (bf16[96,1024]{1,0:T(8,128)(2,1)S(1)}, bf16[96,1024]{1,0:T(8,128)(2,1)S(1)}, u32[]{:S(2)}, u32[]{:S(2)}) collective-permute-start(bf16[96,1024]{1,0:T(8,128)(2,1)S(1)} %get-tuple-element.26), channel_id=1, source_target_pairs={{0,1},{1,0},{2,3},{3,2},{4,5},{5,4},{6,7},{7,6},{8,9},{9,8},{10,11... | collective-permute-start | bytes 589832 | tf_op jit(solution)/shard_map/ppermute | solution.py:213
  28.3 0.1 collective-permute-start.8
  28.3 0.4 %collective-permute-start.9 = (bf16[96,1024]{1,0:T(8,128)(2,1)S(1)}, bf16[96,1024]{1,0:T(8,128)(2,1)S(1)}, u32[]{:S(2)}, u32[]{:S(2)}) collective-permute-start(bf16[96,1024]{1,0:T(8,128)(2,1)S(1)} %get-tuple-element.28), channel_id=1, source_target_pairs={{0,1},{1,0},{2,3},{3,2},{4,5},{5,4},{6,7},{7,6},{8,9},{9,8},{10,11... | collective-permute-start | bytes 589832 | tf_op jit(solution)/shard_map/ppermute | solution.py:213
  28.8 0.1 collective-permute-start.10
  28.8 0.7 %count.1.refs_8_ = f32[1,384]{1,0:T(1,128)S(1)} custom-call(bf16[64,1024]{1,0:T(8,128)(2,1)S(1)} %pass.1.refs_0_, bf16[64,1024]{1,0:T(8,128)(2,1)S(1)} %collective-permute-done.4.refs_1_, bf16[128,1024]{1,0:T(8,128)(2,1)S(1)} %collective-permute-done.5.refs_2_, bf16[128,1024]{1,0:T(8,128)(2,1)S(1)} %collective-permute-done.6.refs_3_), custom_call_target="tpu_custom_call" | custom-call | tf_op jit(solution)/shard_map/count/pallas_call | solution.py:94
  29.5 0.2 collective-permute-done.8.refs_5_
  29.7 0.3 collective-permute-done.9.refs_6_
  30.0 0.3 collective-permute-done.10.refs_7_
  30.3 0.7 %cross.1.counts_ref = f32[1,384]{1,0:T(1,128)S(1)} custom-call(bf16[64,1024]{1,0:T(8,128)(2,1)S(1)} %pass.1.refs_0_, bf16[64,1024]{1,0:T(8,128)(2,1)S(1)} %collective-permute-done.4.refs_1_, bf16[128,1024]{1,0:T(8,128)(2,1)S(1)} %collective-permute-done.5.refs_2_, bf16[128,1024]{1,0:T(8,128)(2,1)S(1)} %collective-permute-done.6.refs_3_, ...), custom_call_target="tpu_custom_call" | custom-call | tf_op jit(solution)/shard_map/cross/pallas_call | solution.py:94
  30.9 0.3 collective-permute-start.11
  31.3 1.1 %late.1 = (f32[1,768]{1,0:T(1,128)S(1)}, f32[1,128]{1,0:T(1,128)S(1)}) custom-call(bf16[64,1024]{1,0:T(8,128)(2,1)S(1)} %pass.1.refs_0_, bf16[64,1024]{1,0:T(8,128)(2,1)S(1)} %collective-permute-done.4.refs_1_, bf16[128,1024]{1,0:T(8,128)(2,1)S(1)} %collective-permute-done.5.refs_2_, bf16[128,1024]{1,0:T(8,128)(2,1)S(1)} %collective-permute-done.6.refs_3_, ...), custom_call_target="tpu_custom_call" | custom-call | tf_op jit(solution)/shard_map/late/pallas_call | solution.py:94
  32.4 0.1 collective-permute-done.11.other_ref
  32.5 0.3 finish.1
  32.9 8.2 %all_to_all.5.counts_ref = f32[16,1,64]{2,1,0:T(1,128)S(1)} all-to-all(f32[16,1,64]{2,1,0:T(1,128)S(1)} %finish.1), channel_id=1, replica_groups={{15,14,13,12,11,10,9,8,7,6,5,4,3,2,1,0},{31,30,29,28,27,26,25,24,23,22,..., dimensions={0} | all-to-all | bytes 8192 | tf_op jit(solution)/shard_map/all_to_all | solution.py:314
  41.1 0.7 %select.1 = f32[1,256]{1,0:T(1,128)} custom-call(f32[16,1,64]{2,1,0:T(1,128)S(1)} %all_to_all.5.counts_ref, s32[1,256]{1,0:T(1,128)S(1)} %get-tuple-element.21.refs_2_.slot_ref), custom_call_target="tpu_custom_call" | custom-call | tf_op jit(solution)/shard_map/select/pallas_call | solution.py:94
  (7 shorter events, 0.0 us)
Async XLA Ops:
  0.0 0.7 %copy-start.1 = (s32[256]{0:T(256)S(1)}, s32[256]{0:T(256)}, u32[]{:S(2)}) copy-start(s32[256]{0:T(256)} %param.3) | copy-start | bytes 3076
  0.0 6.3 %collective-permute-start = (bf16[256,1024]{1,0:T(8,128)(2,1)}, bf16[256,1024]{1,0:T(8,128)(2,1)S(1)}, u32[]{:S(2)}, u32[]{:S(2)}) collective-permute-start(bf16[256,1024]{1,0:T(8,128)(2,1)} %refs_0_.3), channel_id=1, source_target_pairs={{0,1},{1,0},{2,3},{3,2},{4,5},{5,4},{6,7},{7,6},{8,9},{9,8},{10,11... | collective-permute-start | bytes 1572872 | tf_op jit(solution)/shard_map/ppermute | solution.py:213
  0.7 5.6 %collective-permute-start.1 = (s32[1,256]{1,0:T(1,128)S(1)}, s32[1,256]{1,0:T(1,128)S(1)}, u32[]{:S(2)}, u32[]{:S(2)}) collective-permute-start(s32[1,256]{1,0:T(1,128)S(1)} %bitcast.2), channel_id=1, source_target_pairs={{0,1},{1,0},{2,3},{3,2},{4,5},{5,4},{6,7},{7,6},{8,9},{9,8},{10,11... | collective-permute-start | bytes 3080 | tf_op jit(solution)/shard_map/ppermute | solution.py:213
  1.1 1.0 %copy-start = (bf16[256,1024]{1,0:T(8,128)(2,1)S(1)}, bf16[256,1024]{1,0:T(8,128)(2,1)}, u32[]{:S(2)}) copy-start(bf16[256,1024]{1,0:T(8,128)(2,1)} %refs_0_.3) | copy-start | bytes 1572868
  2.6 10.2 %collective-permute-start.3 = (bf16[64,1024]{1,0:T(8,128)(2,1)S(1)}, bf16[64,1024]{1,0:T(8,128)(2,1)S(1)}, u32[]{:S(2)}, u32[]{:S(2)}) collective-permute-start(bf16[64,1024]{1,0:T(8,128)(2,1)S(1)} %get-tuple-element.23), channel_id=1, source_target_pairs={{0,8},{1,11},{2,10},{3,9},{4,12},{5,15},{6,14},{7,13},{8,0},{9,3},... | collective-permute-start | bytes 393224 | tf_op jit(solution)/shard_map/ppermute | solution.py:229
  6.9 12.4 %collective-permute-start.5 = (bf16[128,1024]{1,0:T(8,128)(2,1)S(1)}, bf16[128,1024]{1,0:T(8,128)(2,1)S(1)}, u32[]{:S(2)}, u32[]{:S(2)}) collective-permute-start(bf16[128,1024]{1,0:T(8,128)(2,1)S(1)} %get-tuple-element.20), channel_id=1, source_target_pairs={{0,0},{1,3},{2,2},{3,1},{4,4},{5,7},{6,6},{7,5},{8,8},{9,11},{10,1... | collective-permute-start | bytes 786440 | tf_op jit(solution)/shard_map/ppermute | solution.py:229
  7.6 11.7 %collective-permute-start.6 = (bf16[128,1024]{1,0:T(8,128)(2,1)S(1)}, bf16[128,1024]{1,0:T(8,128)(2,1)S(1)}, u32[]{:S(2)}, u32[]{:S(2)}) collective-permute-start(bf16[128,1024]{1,0:T(8,128)(2,1)S(1)} %get-tuple-element.25), channel_id=1, source_target_pairs={{0,4},{1,7},{2,6},{3,5},{4,0},{5,3},{6,2},{7,1},{8,12},{9,15},{10,... | collective-permute-start | bytes 786440 | tf_op jit(solution)/shard_map/ppermute | solution.py:229
  9.8 7.6 %collective-permute-start.4 = (bf16[64,1024]{1,0:T(8,128)(2,1)S(1)}, bf16[64,1024]{1,0:T(8,128)(2,1)S(1)}, u32[]{:S(2)}, u32[]{:S(2)}) collective-permute-start(bf16[64,1024]{1,0:T(8,128)(2,1)S(1)} %get-tuple-element.24), channel_id=1, source_target_pairs={{0,8},{1,11},{2,10},{3,9},{4,12},{5,15},{6,14},{7,13},{8,0},{9,3},... | collective-permute-start | bytes 393224 | tf_op jit(solution)/shard_map/ppermute | solution.py:229
  12.8 18.1 %collective-permute-start.2 = (bf16[128,1024]{1,0:T(8,128)(2,1)S(1)}, bf16[128,1024]{1,0:T(8,128)(2,1)S(1)}, u32[]{:S(2)}, u32[]{:S(2)}) collective-permute-start(bf16[128,1024]{1,0:T(8,128)(2,1)S(1)} %get-tuple-element.22), channel_id=1, source_target_pairs={{0,12},{1,15},{2,14},{3,13},{4,8},{5,11},{6,10},{7,9},{8,4},{9,7},... | collective-permute-start | bytes 786440 | tf_op jit(solution)/shard_map/ppermute | solution.py:229
  19.4 10.1 %collective-permute-start.7 = (bf16[96,1024]{1,0:T(8,128)(2,1)S(1)}, bf16[96,1024]{1,0:T(8,128)(2,1)S(1)}, u32[]{:S(2)}, u32[]{:S(2)}) collective-permute-start(bf16[96,1024]{1,0:T(8,128)(2,1)S(1)} %get-tuple-element.26), channel_id=1, source_target_pairs={{0,1},{1,0},{2,3},{3,2},{4,5},{5,4},{6,7},{7,6},{8,9},{9,8},{10,11... | collective-permute-start | bytes 589832 | tf_op jit(solution)/shard_map/ppermute | solution.py:213
  28.3 1.4 %collective-permute-start.8 = (bf16[96,1024]{1,0:T(8,128)(2,1)S(1)}, bf16[96,1024]{1,0:T(8,128)(2,1)S(1)}, u32[]{:S(2)}, u32[]{:S(2)}) collective-permute-start(bf16[96,1024]{1,0:T(8,128)(2,1)S(1)} %get-tuple-element.27), channel_id=1, source_target_pairs={{0,1},{1,0},{2,3},{3,2},{4,5},{5,4},{6,7},{7,6},{8,9},{9,8},{10,11... | collective-permute-start | bytes 589832 | tf_op jit(solution)/shard_map/ppermute | solution.py:213
  28.3 1.6 %collective-permute-start.9 = (bf16[96,1024]{1,0:T(8,128)(2,1)S(1)}, bf16[96,1024]{1,0:T(8,128)(2,1)S(1)}, u32[]{:S(2)}, u32[]{:S(2)}) collective-permute-start(bf16[96,1024]{1,0:T(8,128)(2,1)S(1)} %get-tuple-element.28), channel_id=1, source_target_pairs={{0,1},{1,0},{2,3},{3,2},{4,5},{5,4},{6,7},{7,6},{8,9},{9,8},{10,11... | collective-permute-start | bytes 589832 | tf_op jit(solution)/shard_map/ppermute | solution.py:213
  28.8 1.5 %collective-permute-start.10 = (bf16[96,1024]{1,0:T(8,128)(2,1)S(1)}, bf16[96,1024]{1,0:T(8,128)(2,1)S(1)}, u32[]{:S(2)}, u32[]{:S(2)}) collective-permute-start(bf16[96,1024]{1,0:T(8,128)(2,1)S(1)} %get-tuple-element.29), channel_id=1, source_target_pairs={{0,1},{1,0},{2,3},{3,2},{4,5},{5,4},{6,7},{7,6},{8,9},{9,8},{10,11... | collective-permute-start | bytes 589832 | tf_op jit(solution)/shard_map/ppermute | solution.py:213
  30.9 1.6 %collective-permute-start.11 = (bf16[128,1024]{1,0:T(8,128)(2,1)S(1)}, bf16[128,1024]{1,0:T(8,128)(2,1)S(1)}, u32[]{:S(2)}, u32[]{:S(2)}) collective-permute-start(bf16[128,1024]{1,0:T(8,128)(2,1)S(1)} %collective-permute-done.2.refs_8_.late_ref), channel_id=1, source_target_pairs={{0,1},{1,0},{2,3},{3,2},{4,5},{5,4},{6,7},{7,6},{8,9},{9,8},{10,11... | collective-permute-start | bytes 786440 | tf_op jit(solution)/shard_map/ppermute | solution.py:213

commit v30 on v29

--- a/solution.py
+++ b/solution.py
@@ -21,6 +21,18 @@
 
 def chip_index():
     return lax.axis_index("owner") * CL_OWN + lax.axis_index("helper")
+
+
+def place_of(device):
+    last = CL_OWN * 2 - 1
+    owner, rest = device // (last + 1), device % (last + 1)
+    places = (3, 1, 0, 2)
+    if isinstance(device, int):
+        return places[owner] * (last + 1) + last - rest
+    place = jnp.full_like(owner, places[0])
+    for k in range(1, len(places)):
+        place = jnp.where(owner == k, places[k], place)
+    return place * (last + 1) + last - rest
 
 
 def slots_of(ids, clusters, capacity):
@@ -197,8 +209,9 @@
     parts = counts.shape[0] // clusters
     row = lax.broadcasted_iota(jnp.int32, by_block.shape, 0)
     if backwards:
-        row = counts.shape[0] - 1 - row
-    chosen = row // parts == block
+        chosen = row // parts == place_of(block * parts) // parts
+    else:
+        chosen = row // parts == block
     out_ref[...] = jnp.sum(jnp.where(chosen, by_block, 0.0), axis=0, keepdims=True)
 
 
@@ -299,7 +312,7 @@
                 devices += [there + here, there + 1 - here]
         there = (chip ^ (last * cores + core)) * cores
         devices += [there + core, there + 1 - core]
-        return [clusters * cores - 1 - device for device in devices]
+        return [place_of(device) for device in devices]
 
     counts = call_kernel(
         "finish",
@@ -316,7 +329,7 @@
         ("owner", "helper", "sub"),
         split_axis=0,
         concat_axis=0,
-        axis_index_groups=[list(reversed(range(clusters * cores)))],
+        axis_index_groups=[sorted(range(clusters * cores), key=place_of)],
         tiled=True,
     )
     return select(back, slot, clusters, capacity, backwards=True)

time: 42 us -> 42.1 us (level)
  no operation moved by 1% of the time
where the time goes in v30:
time: 42.1 us; the launch traced here: 41.9 us
  starting transfers between devices  21.7 us (52%)
  blocking collectives  8.26 us (20%)
  waiting for transfers between devices  5.31 us (13%)
  Pallas kernels  5.26 us (12%)
  local copies, waits for them, and re-layouts  1.27 us (3%)
    ppermute x5, starting transfers between devices, across(): return lax.ppermute(x, ('owner', 'helper', 'sub'), pairs)  11 us
    ppermute x7, starting transfers between devices, swap_cores(): return lax.ppermute(x, 'sub', [(i, i ^ 1) for i in range(cores)])  10.7 us
    all_to_all x1, blocking collectives, body_by_chip(): lax.all_to_all(counts, ('owner', 'helper', 'sub'), split_axis=0, concat_a...  8.26 us
    pallas_call x10, Pallas kernels, call_kernel(): pl.pallas_call(kernel, out_shape=out_shape, in_specs=[VMEM] * len(args),...  5.26 us
    ppermute x5, waiting for transfers between devices, across(): return lax.ppermute(x, ('owner', 'helper', 'sub'), pairs)  4.48 us
    unnamed x4, local copies, waits for them, and re-layouts  1.27 us
  transfers between devices with their start and end apart: 12, of which 6 were waited for; matrix products, arithmetic and copies ran while one was open for 0% of the time, Pallas kernels for 10%

profile of v30, /device:TPU:0, one launch (start us, length us, event | category | flops | bytes accessed | tf_op | source)
XLA Modules:
  0.0 41.9 jit_solution(18261335785720753987)
XLA Ops:
  0.0 0.5 %collective-permute-start = (bf16[256,1024]{1,0:T(8,128)(2,1)}, bf16[256,1024]{1,0:T(8,128)(2,1)S(1)}, u32[]{:S(2)}, u32[]{:S(2)}) collective-permute-start(bf16[256,1024]{1,0:T(8,128)(2,1)} %refs_0_.3), channel_id=1, source_target_pairs={{0,1},{1,0},{2,3},{3,2},{4,5},{5,4},{6,7},{7,6},{8,9},{9,8},{10,11... | collective-permute-start | bytes 1572872 | tf_op jit(solution)/shard_map/ppermute | solution.py:226
  0.5 0.2 copy-done.1
  0.7 0.5 %collective-permute-start.1 = (s32[1,256]{1,0:T(1,128)S(1)}, s32[1,256]{1,0:T(1,128)S(1)}, u32[]{:S(2)}, u32[]{:S(2)}) collective-permute-start(s32[1,256]{1,0:T(1,128)S(1)} %bitcast.2), channel_id=1, source_target_pairs={{0,1},{1,0},{2,3},{3,2},{4,5},{5,4},{6,7},{7,6},{8,9},{9,8},{10,11... | collective-permute-start | bytes 3080 | tf_op jit(solution)/shard_map/ppermute | solution.py:226
  1.1 1.0 %copy-done = bf16[256,1024]{1,0:T(8,128)(2,1)S(1)} copy-done((bf16[256,1024]{1,0:T(8,128)(2,1)S(1)}, bf16[256,1024]{1,0:T(8,128)(2,1)}, u32[]{:S(2)}) %copy-start) | copy-done | bytes 524312
  2.2 0.5 %route_first.1 = (bf16[64,1024]{1,0:T(8,128)(2,1)S(1)}, s32[1,256]{1,0:T(1,128)S(1)}) custom-call(bf16[256,1024]{1,0:T(8,128)(2,1)S(1)} %copy-done, s32[1,256]{1,0:T(1,128)S(1)} %bitcast.3), custom_call_target="tpu_custom_call" | custom-call | tf_op jit(solution)/shard_map/route_first/pallas_call | solution.py:106
  2.6 3.7 %collective-permute-start.3 = (bf16[64,1024]{1,0:T(8,128)(2,1)S(1)}, bf16[64,1024]{1,0:T(8,128)(2,1)S(1)}, u32[]{:S(2)}, u32[]{:S(2)}) collective-permute-start(bf16[64,1024]{1,0:T(8,128)(2,1)S(1)} %get-tuple-element.23), channel_id=1, source_target_pairs={{0,8},{1,11},{2,10},{3,9},{4,12},{5,15},{6,14},{7,13},{8,0},{9,3},... | collective-permute-start | bytes 393224 | tf_op jit(solution)/shard_map/ppermute | solution.py:242
  6.3 0.6 %route_near.1 = (bf16[128,1024]{1,0:T(8,128)(2,1)S(1)}, bf16[128,1024]{1,0:T(8,128)(2,1)S(1)}) custom-call(bf16[256,1024]{1,0:T(8,128)(2,1)S(1)} %copy-done, bf16[256,1024]{1,0:T(8,128)(2,1)S(1)} %collective-permute-done.refs_1_, s32[1,256]{1,0:T(1,128)S(1)} %get-tuple-element.21.refs_2_.slot_ref, s32[1,256]{1,0:T(1,128)S(1)} %collective-permute-done.1.refs_3_), custom_call_target="tpu_custom_call" | custom-call | tf_op jit(solution)/shard_map/route_near/pallas_call | solution.py:106
  6.9 0.7 %collective-permute-start.5 = (bf16[128,1024]{1,0:T(8,128)(2,1)S(1)}, bf16[128,1024]{1,0:T(8,128)(2,1)S(1)}, u32[]{:S(2)}, u32[]{:S(2)}) collective-permute-start(bf16[128,1024]{1,0:T(8,128)(2,1)S(1)} %get-tuple-element.20), channel_id=1, source_target_pairs={{0,0},{1,3},{2,2},{3,1},{4,4},{5,7},{6,6},{7,5},{8,8},{9,11},{10,1... | collective-permute-start | bytes 786440 | tf_op jit(solution)/shard_map/ppermute | solution.py:242
  7.6 1.6 %collective-permute-start.6 = (bf16[128,1024]{1,0:T(8,128)(2,1)S(1)}, bf16[128,1024]{1,0:T(8,128)(2,1)S(1)}, u32[]{:S(2)}, u32[]{:S(2)}) collective-permute-start(bf16[128,1024]{1,0:T(8,128)(2,1)S(1)} %get-tuple-element.25), channel_id=1, source_target_pairs={{0,4},{1,7},{2,6},{3,5},{4,0},{5,3},{6,2},{7,1},{8,12},{9,15},{10,... | collective-permute-start | bytes 786440 | tf_op jit(solution)/shard_map/ppermute | solution.py:242
  9.2 0.6 %route_far.1 = (bf16[64,1024]{1,0:T(8,128)(2,1)S(1)}, bf16[128,1024]{1,0:T(8,128)(2,1)S(1)}) custom-call(bf16[256,1024]{1,0:T(8,128)(2,1)S(1)} %copy-done, bf16[256,1024]{1,0:T(8,128)(2,1)S(1)} %collective-permute-done.refs_1_, s32[1,256]{1,0:T(1,128)S(1)} %get-tuple-element.21.refs_2_.slot_ref, s32[1,256]{1,0:T(1,128)S(1)} %collective-permute-done.1.refs_3_), custom_call_target="tpu_custom_call" | custom-call | flops 10000000000 | tf_op jit(solution)/shard_map/route_far/pallas_call | solution.py:106
  9.8 0.4 collective-permute-start.4
  10.2 2.6 %collective-permute-done.3.refs_0_ = bf16[64,1024]{1,0:T(8,128)(2,1)S(1)} collective-permute-done((bf16[64,1024]{1,0:T(8,128)(2,1)S(1)}, bf16[64,1024]{1,0:T(8,128)(2,1)S(1)}, u32[]{:S(2)}, u32[]{:S(2)}) %collective-permute-start.3) | collective-permute-done | bytes 131104 | tf_op jit(solution)/shard_map/ppermute | solution.py:242
  12.8 4.6 %collective-permute-start.2 = (bf16[128,1024]{1,0:T(8,128)(2,1)S(1)}, bf16[128,1024]{1,0:T(8,128)(2,1)S(1)}, u32[]{:S(2)}, u32[]{:S(2)}) collective-permute-start(bf16[128,1024]{1,0:T(8,128)(2,1)S(1)} %get-tuple-element.22), channel_id=1, source_target_pairs={{0,12},{1,15},{2,14},{3,13},{4,8},{5,11},{6,10},{7,9},{8,4},{9,7},... | collective-permute-start | bytes 786440 | tf_op jit(solution)/shard_map/ppermute | solution.py:242
  17.4 1.9 %collective-permute-done.6.refs_3_ = bf16[128,1024]{1,0:T(8,128)(2,1)S(1)} collective-permute-done((bf16[128,1024]{1,0:T(8,128)(2,1)S(1)}, bf16[128,1024]{1,0:T(8,128)(2,1)S(1)}, u32[]{:S(2)}, u32[]{:S(2)}) %collective-permute-start.6) | collective-permute-done | bytes 262176 | tf_op jit(solution)/shard_map/ppermute | solution.py:242
  19.3 0.0 collective-permute-done.5.refs_2_
  19.3 0.1 regroup.1
  19.4 8.9 %collective-permute-start.7 = (bf16[96,1024]{1,0:T(8,128)(2,1)S(1)}, bf16[96,1024]{1,0:T(8,128)(2,1)S(1)}, u32[]{:S(2)}, u32[]{:S(2)}) collective-permute-start(bf16[96,1024]{1,0:T(8,128)(2,1)S(1)} %get-tuple-element.26), channel_id=1, source_target_pairs={{0,1},{1,0},{2,3},{3,2},{4,5},{5,4},{6,7},{7,6},{8,9},{9,8},{10,11... | collective-permute-start | bytes 589832 | tf_op jit(solution)/shard_map/ppermute | solution.py:226
  28.3 0.1 collective-permute-start.8
  28.3 0.4 %collective-permute-start.9 = (bf16[96,1024]{1,0:T(8,128)(2,1)S(1)}, bf16[96,1024]{1,0:T(8,128)(2,1)S(1)}, u32[]{:S(2)}, u32[]{:S(2)}) collective-permute-start(bf16[96,1024]{1,0:T(8,128)(2,1)S(1)} %get-tuple-element.28), channel_id=1, source_target_pairs={{0,1},{1,0},{2,3},{3,2},{4,5},{5,4},{6,7},{7,6},{8,9},{9,8},{10,11... | collective-permute-start | bytes 589832 | tf_op jit(solution)/shard_map/ppermute | solution.py:226
  28.8 0.1 collective-permute-start.10
  28.8 0.7 %count.1.refs_8_ = f32[1,384]{1,0:T(1,128)S(1)} custom-call(bf16[64,1024]{1,0:T(8,128)(2,1)S(1)} %pass.1.refs_0_, bf16[64,1024]{1,0:T(8,128)(2,1)S(1)} %collective-permute-done.4.refs_1_, bf16[128,1024]{1,0:T(8,128)(2,1)S(1)} %collective-permute-done.5.refs_2_, bf16[128,1024]{1,0:T(8,128)(2,1)S(1)} %collective-permute-done.6.refs_3_), custom_call_target="tpu_custom_call" | custom-call | tf_op jit(solution)/shard_map/count/pallas_call | solution.py:106
  29.5 0.0 collective-permute-done.7.refs_4_
  29.5 0.2 collective-permute-done.8.refs_5_
  29.7 0.3 collective-permute-done.9.refs_6_
  30.0 0.3 collective-permute-done.10.refs_7_
  30.3 0.7 %cross.1.counts_ref = f32[1,384]{1,0:T(1,128)S(1)} custom-call(bf16[64,1024]{1,0:T(8,128)(2,1)S(1)} %pass.1.refs_0_, bf16[64,1024]{1,0:T(8,128)(2,1)S(1)} %collective-permute-done.4.refs_1_, bf16[128,1024]{1,0:T(8,128)(2,1)S(1)} %collective-permute-done.5.refs_2_, bf16[128,1024]{1,0:T(8,128)(2,1)S(1)} %collective-permute-done.6.refs_3_, ...), custom_call_target="tpu_custom_call" | custom-call | tf_op jit(solution)/shard_map/cross/pallas_call | solution.py:106
  30.9 0.3 collective-permute-start.11
  31.3 1.1 %late.1 = (f32[1,768]{1,0:T(1,128)S(1)}, f32[1,128]{1,0:T(1,128)S(1)}) custom-call(bf16[64,1024]{1,0:T(8,128)(2,1)S(1)} %pass.1.refs_0_, bf16[64,1024]{1,0:T(8,128)(2,1)S(1)} %collective-permute-done.4.refs_1_, bf16[128,1024]{1,0:T(8,128)(2,1)S(1)} %collective-permute-done.5.refs_2_, bf16[128,1024]{1,0:T(8,128)(2,1)S(1)} %collective-permute-done.6.refs_3_, ...), custom_call_target="tpu_custom_call" | custom-call | tf_op jit(solution)/shard_map/late/pallas_call | solution.py:106
  32.4 0.1 collective-permute-done.11.other_ref
  32.5 0.3 finish.1
  32.9 8.3 %all_to_all.5.counts_ref = f32[16,1,64]{2,1,0:T(1,128)S(1)} all-to-all(f32[16,1,64]{2,1,0:T(1,128)S(1)} %finish.1), channel_id=1, replica_groups={{11,10,9,8,7,6,5,4,15,14,13,12,3,2,1,0},{27,26,25,24,23,22,21,20,31,30,..., dimensions={0} | all-to-all | bytes 8192 | tf_op jit(solution)/shard_map/all_to_all | solution.py:327
  41.1 0.7 %select.1 = f32[1,256]{1,0:T(1,128)} custom-call(f32[16,1,64]{2,1,0:T(1,128)S(1)} %all_to_all.5.counts_ref, s32[1,256]{1,0:T(1,128)S(1)} %get-tuple-element.21.refs_2_.slot_ref), custom_call_target="tpu_custom_call" | custom-call | tf_op jit(solution)/shard_map/select/pallas_call | solution.py:106
  (7 shorter events, 0.0 us)
Async XLA Ops:
  0.0 0.7 %copy-start.1 = (s32[256]{0:T(256)S(1)}, s32[256]{0:T(256)}, u32[]{:S(2)}) copy-start(s32[256]{0:T(256)} %param.3) | copy-start | bytes 3076
  0.0 6.3 %collective-permute-start = (bf16[256,1024]{1,0:T(8,128)(2,1)}, bf16[256,1024]{1,0:T(8,128)(2,1)S(1)}, u32[]{:S(2)}, u32[]{:S(2)}) collective-permute-start(bf16[256,1024]{1,0:T(8,128)(2,1)} %refs_0_.3), channel_id=1, source_target_pairs={{0,1},{1,0},{2,3},{3,2},{4,5},{5,4},{6,7},{7,6},{8,9},{9,8},{10,11... | collective-permute-start | bytes 1572872 | tf_op jit(solution)/shard_map/ppermute | solution.py:226
  0.7 5.6 %collective-permute-start.1 = (s32[1,256]{1,0:T(1,128)S(1)}, s32[1,256]{1,0:T(1,128)S(1)}, u32[]{:S(2)}, u32[]{:S(2)}) collective-permute-start(s32[1,256]{1,0:T(1,128)S(1)} %bitcast.2), channel_id=1, source_target_pairs={{0,1},{1,0},{2,3},{3,2},{4,5},{5,4},{6,7},{7,6},{8,9},{9,8},{10,11... | collective-permute-start | bytes 3080 | tf_op jit(solution)/shard_map/ppermute | solution.py:226
  1.1 1.0 %copy-start = (bf16[256,1024]{1,0:T(8,128)(2,1)S(1)}, bf16[256,1024]{1,0:T(8,128)(2,1)}, u32[]{:S(2)}) copy-start(bf16[256,1024]{1,0:T(8,128)(2,1)} %refs_0_.3) | copy-start | bytes 1572868
  2.6 10.2 %collective-permute-start.3 = (bf16[64,1024]{1,0:T(8,128)(2,1)S(1)}, bf16[64,1024]{1,0:T(8,128)(2,1)S(1)}, u32[]{:S(2)}, u32[]{:S(2)}) collective-permute-start(bf16[64,1024]{1,0:T(8,128)(2,1)S(1)} %get-tuple-element.23), channel_id=1, source_target_pairs={{0,8},{1,11},{2,10},{3,9},{4,12},{5,15},{6,14},{7,13},{8,0},{9,3},... | collective-permute-start | bytes 393224 | tf_op jit(solution)/shard_map/ppermute | solution.py:242
  6.9 12.4 %collective-permute-start.5 = (bf16[128,1024]{1,0:T(8,128)(2,1)S(1)}, bf16[128,1024]{1,0:T(8,128)(2,1)S(1)}, u32[]{:S(2)}, u32[]{:S(2)}) collective-permute-start(bf16[128,1024]{1,0:T(8,128)(2,1)S(1)} %get-tuple-element.20), channel_id=1, source_target_pairs={{0,0},{1,3},{2,2},{3,1},{4,4},{5,7},{6,6},{7,5},{8,8},{9,11},{10,1... | collective-permute-start | bytes 786440 | tf_op jit(solution)/shard_map/ppermute | solution.py:242
  7.6 11.7 %collective-permute-start.6 = (bf16[128,1024]{1,0:T(8,128)(2,1)S(1)}, bf16[128,1024]{1,0:T(8,128)(2,1)S(1)}, u32[]{:S(2)}, u32[]{:S(2)}) collective-permute-start(bf16[128,1024]{1,0:T(8,128)(2,1)S(1)} %get-tuple-element.25), channel_id=1, source_target_pairs={{0,4},{1,7},{2,6},{3,5},{4,0},{5,3},{6,2},{7,1},{8,12},{9,15},{10,... | collective-permute-start | bytes 786440 | tf_op jit(solution)/shard_map/ppermute | solution.py:242
  9.8 7.6 %collective-permute-start.4 = (bf16[64,1024]{1,0:T(8,128)(2,1)S(1)}, bf16[64,1024]{1,0:T(8,128)(2,1)S(1)}, u32[]{:S(2)}, u32[]{:S(2)}) collective-permute-start(bf16[64,1024]{1,0:T(8,128)(2,1)S(1)} %get-tuple-element.24), channel_id=1, source_target_pairs={{0,8},{1,11},{2,10},{3,9},{4,12},{5,15},{6,14},{7,13},{8,0},{9,3},... | collective-permute-start | bytes 393224 | tf_op jit(solution)/shard_map/ppermute | solution.py:242
  12.8 18.1 %collective-permute-start.2 = (bf16[128,1024]{1,0:T(8,128)(2,1)S(1)}, bf16[128,1024]{1,0:T(8,128)(2,1)S(1)}, u32[]{:S(2)}, u32[]{:S(2)}) collective-permute-start(bf16[128,1024]{1,0:T(8,128)(2,1)S(1)} %get-tuple-element.22), channel_id=1, source_target_pairs={{0,12},{1,15},{2,14},{3,13},{4,8},{5,11},{6,10},{7,9},{8,4},{9,7},... | collective-permute-start | bytes 786440 | tf_op jit(solution)/shard_map/ppermute | solution.py:242
  19.4 10.1 %collective-permute-start.7 = (bf16[96,1024]{1,0:T(8,128)(2,1)S(1)}, bf16[96,1024]{1,0:T(8,128)(2,1)S(1)}, u32[]{:S(2)}, u32[]{:S(2)}) collective-permute-start(bf16[96,1024]{1,0:T(8,128)(2,1)S(1)} %get-tuple-element.26), channel_id=1, source_target_pairs={{0,1},{1,0},{2,3},{3,2},{4,5},{5,4},{6,7},{7,6},{8,9},{9,8},{10,11... | collective-permute-start | bytes 589832 | tf_op jit(solution)/shard_map/ppermute | solution.py:226
  28.3 1.4 %collective-permute-start.8 = (bf16[96,1024]{1,0:T(8,128)(2,1)S(1)}, bf16[96,1024]{1,0:T(8,128)(2,1)S(1)}, u32[]{:S(2)}, u32[]{:S(2)}) collective-permute-start(bf16[96,1024]{1,0:T(8,128)(2,1)S(1)} %get-tuple-element.27), channel_id=1, source_target_pairs={{0,1},{1,0},{2,3},{3,2},{4,5},{5,4},{6,7},{7,6},{8,9},{9,8},{10,11... | collective-permute-start | bytes 589832 | tf_op jit(solution)/shard_map/ppermute | solution.py:226
  28.3 1.6 %collective-permute-start.9 = (bf16[96,1024]{1,0:T(8,128)(2,1)S(1)}, bf16[96,1024]{1,0:T(8,128)(2,1)S(1)}, u32[]{:S(2)}, u32[]{:S(2)}) collective-permute-start(bf16[96,1024]{1,0:T(8,128)(2,1)S(1)} %get-tuple-element.28), channel_id=1, source_target_pairs={{0,1},{1,0},{2,3},{3,2},{4,5},{5,4},{6,7},{7,6},{8,9},{9,8},{10,11... | collective-permute-start | bytes 589832 | tf_op jit(solution)/shard_map/ppermute | solution.py:226
  28.8 1.5 %collective-permute-start.10 = (bf16[96,1024]{1,0:T(8,128)(2,1)S(1)}, bf16[96,1024]{1,0:T(8,128)(2,1)S(1)}, u32[]{:S(2)}, u32[]{:S(2)}) collective-permute-start(bf16[96,1024]{1,0:T(8,128)(2,1)S(1)} %get-tuple-element.29), channel_id=1, source_target_pairs={{0,1},{1,0},{2,3},{3,2},{4,5},{5,4},{6,7},{7,6},{8,9},{9,8},{10,11... | collective-permute-start | bytes 589832 | tf_op jit(solution)/shard_map/ppermute | solution.py:226
  30.9 1.6 %collective-permute-start.11 = (bf16[128,1024]{1,0:T(8,128)(2,1)S(1)}, bf16[128,1024]{1,0:T(8,128)(2,1)S(1)}, u32[]{:S(2)}, u32[]{:S(2)}) collective-permute-start(bf16[128,1024]{1,0:T(8,128)(2,1)S(1)} %collective-permute-done.2.refs_8_.late_ref), channel_id=1, source_target_pairs={{0,1},{1,0},{2,3},{3,2},{4,5},{5,4},{6,7},{7,6},{8,9},{9,8},{10,11... | collective-permute-start | bytes 786440 | tf_op jit(solution)/shard_map/ppermute | solution.py:226

commit v31 on v30

--- a/solution.py
+++ b/solution.py
@@ -24,15 +24,18 @@
 
 
 def place_of(device):
-    last = CL_OWN * 2 - 1
-    owner, rest = device // (last + 1), device % (last + 1)
+    chip, core = device // 2, device % 2
+    owner, helper = chip // CL_OWN, chip % CL_OWN
     places = (3, 1, 0, 2)
+    chips = CL_OWN * len(places)
     if isinstance(device, int):
-        return places[owner] * (last + 1) + last - rest
+        place = places[owner] * CL_OWN + CL_OWN - 1 - helper + chips * core
+        return {chips - 1: 2 * chips - 1, 2 * chips - 1: chips - 1}.get(place, place)
     place = jnp.full_like(owner, places[0])
     for k in range(1, len(places)):
         place = jnp.where(owner == k, places[k], place)
-    return place * (last + 1) + last - rest
+    place = place * CL_OWN + CL_OWN - 1 - helper + chips * core
+    return jnp.where(chip == 0, (2 - core) * chips - 1, place)
 
 
 def slots_of(ids, clusters, capacity):
@@ -209,7 +212,9 @@
     parts = counts.shape[0] // clusters
     row = lax.broadcasted_iota(jnp.int32, by_block.shape, 0)
     if backwards:
-        chosen = row // parts == place_of(block * parts) // parts
+        chosen = row == place_of(block * parts)
+        for part in range(1, parts):
+            chosen = chosen | (row == place_of(block * parts + part))
     else:
         chosen = row // parts == block
     out_ref[...] = jnp.sum(jnp.where(chosen, by_block, 0.0), axis=0, keepdims=True)

time: 42.1 us -> 42.3 us (level)
  no operation moved by 1% of the time
where the time goes in v31:
time: 42.3 us; the launch traced here: 42 us
  starting transfers between devices  21.7 us (51%)
  blocking collectives  8.44 us (20%)
  waiting for transfers between devices  5.31 us (13%)
  Pallas kernels  5.26 us (12%)
  local copies, waits for them, and re-layouts  1.27 us (3%)
    ppermute x5, starting transfers between devices, across(): return lax.ppermute(x, ('owner', 'helper', 'sub'), pairs)  11 us
    ppermute x7, starting transfers between devices, swap_cores(): return lax.ppermute(x, 'sub', [(i, i ^ 1) for i in range(cores)])  10.7 us
    all_to_all x1, blocking collectives, body_by_chip(): lax.all_to_all(counts, ('owner', 'helper', 'sub'), split_axis=0, concat_a...  8.44 us
    pallas_call x10, Pallas kernels, call_kernel(): pl.pallas_call(kernel, out_shape=out_shape, in_specs=[VMEM] * len(args),...  5.26 us
    ppermute x5, waiting for transfers between devices, across(): return lax.ppermute(x, ('owner', 'helper', 'sub'), pairs)  4.48 us
    unnamed x4, local copies, waits for them, and re-layouts  1.27 us
  transfers between devices with their start and end apart: 12, of which 6 were waited for; matrix products, arithmetic and copies ran while one was open for 0% of the time, Pallas kernels for 10%

profile of v31, /device:TPU:0, one launch (start us, length us, event | category | flops | bytes accessed | tf_op | source)
XLA Modules:
  0.0 42.0 jit_solution(3760698197447823730)
XLA Ops:
  0.0 0.5 %collective-permute-start = (bf16[256,1024]{1,0:T(8,128)(2,1)}, bf16[256,1024]{1,0:T(8,128)(2,1)S(1)}, u32[]{:S(2)}, u32[]{:S(2)}) collective-permute-start(bf16[256,1024]{1,0:T(8,128)(2,1)} %refs_0_.3), channel_id=1, source_target_pairs={{0,1},{1,0},{2,3},{3,2},{4,5},{5,4},{6,7},{7,6},{8,9},{9,8},{10,11... | collective-permute-start | bytes 1572872 | tf_op jit(solution)/shard_map/ppermute | solution.py:231
  0.5 0.2 copy-done.1
  0.7 0.5 %collective-permute-start.1 = (s32[1,256]{1,0:T(1,128)S(1)}, s32[1,256]{1,0:T(1,128)S(1)}, u32[]{:S(2)}, u32[]{:S(2)}) collective-permute-start(s32[1,256]{1,0:T(1,128)S(1)} %bitcast.2), channel_id=1, source_target_pairs={{0,1},{1,0},{2,3},{3,2},{4,5},{5,4},{6,7},{7,6},{8,9},{9,8},{10,11... | collective-permute-start | bytes 3080 | tf_op jit(solution)/shard_map/ppermute | solution.py:231
  1.1 1.0 %copy-done = bf16[256,1024]{1,0:T(8,128)(2,1)S(1)} copy-done((bf16[256,1024]{1,0:T(8,128)(2,1)S(1)}, bf16[256,1024]{1,0:T(8,128)(2,1)}, u32[]{:S(2)}) %copy-start) | copy-done | bytes 524312
  2.2 0.5 %route_first.1 = (bf16[64,1024]{1,0:T(8,128)(2,1)S(1)}, s32[1,256]{1,0:T(1,128)S(1)}) custom-call(bf16[256,1024]{1,0:T(8,128)(2,1)S(1)} %copy-done, s32[1,256]{1,0:T(1,128)S(1)} %bitcast.3), custom_call_target="tpu_custom_call" | custom-call | tf_op jit(solution)/shard_map/route_first/pallas_call | solution.py:109
  2.6 3.7 %collective-permute-start.3 = (bf16[64,1024]{1,0:T(8,128)(2,1)S(1)}, bf16[64,1024]{1,0:T(8,128)(2,1)S(1)}, u32[]{:S(2)}, u32[]{:S(2)}) collective-permute-start(bf16[64,1024]{1,0:T(8,128)(2,1)S(1)} %get-tuple-element.23), channel_id=1, source_target_pairs={{0,8},{1,11},{2,10},{3,9},{4,12},{5,15},{6,14},{7,13},{8,0},{9,3},... | collective-permute-start | bytes 393224 | tf_op jit(solution)/shard_map/ppermute | solution.py:247
  6.3 0.0 collective-permute-done.1.refs_3_
  6.3 0.6 %route_near.1 = (bf16[128,1024]{1,0:T(8,128)(2,1)S(1)}, bf16[128,1024]{1,0:T(8,128)(2,1)S(1)}) custom-call(bf16[256,1024]{1,0:T(8,128)(2,1)S(1)} %copy-done, bf16[256,1024]{1,0:T(8,128)(2,1)S(1)} %collective-permute-done.refs_1_, s32[1,256]{1,0:T(1,128)S(1)} %get-tuple-element.21.refs_2_.slot_ref, s32[1,256]{1,0:T(1,128)S(1)} %collective-permute-done.1.refs_3_), custom_call_target="tpu_custom_call" | custom-call | tf_op jit(solution)/shard_map/route_near/pallas_call | solution.py:109
  6.9 0.7 %collective-permute-start.5 = (bf16[128,1024]{1,0:T(8,128)(2,1)S(1)}, bf16[128,1024]{1,0:T(8,128)(2,1)S(1)}, u32[]{:S(2)}, u32[]{:S(2)}) collective-permute-start(bf16[128,1024]{1,0:T(8,128)(2,1)S(1)} %get-tuple-element.20), channel_id=1, source_target_pairs={{0,0},{1,3},{2,2},{3,1},{4,4},{5,7},{6,6},{7,5},{8,8},{9,11},{10,1... | collective-permute-start | bytes 786440 | tf_op jit(solution)/shard_map/ppermute | solution.py:247
  7.6 1.6 %collective-permute-start.6 = (bf16[128,1024]{1,0:T(8,128)(2,1)S(1)}, bf16[128,1024]{1,0:T(8,128)(2,1)S(1)}, u32[]{:S(2)}, u32[]{:S(2)}) collective-permute-start(bf16[128,1024]{1,0:T(8,128)(2,1)S(1)} %get-tuple-element.25), channel_id=1, source_target_pairs={{0,4},{1,7},{2,6},{3,5},{4,0},{5,3},{6,2},{7,1},{8,12},{9,15},{10,... | collective-permute-start | bytes 786440 | tf_op jit(solution)/shard_map/ppermute | solution.py:247
  9.2 0.6 %route_far.1 = (bf16[64,1024]{1,0:T(8,128)(2,1)S(1)}, bf16[128,1024]{1,0:T(8,128)(2,1)S(1)}) custom-call(bf16[256,1024]{1,0:T(8,128)(2,1)S(1)} %copy-done, bf16[256,1024]{1,0:T(8,128)(2,1)S(1)} %collective-permute-done.refs_1_, s32[1,256]{1,0:T(1,128)S(1)} %get-tuple-element.21.refs_2_.slot_ref, s32[1,256]{1,0:T(1,128)S(1)} %collective-permute-done.1.refs_3_), custom_call_target="tpu_custom_call" | custom-call | flops 10000000000 | tf_op jit(solution)/shard_map/route_far/pallas_call | solution.py:109
  9.8 0.4 collective-permute-start.4
  10.2 2.6 %collective-permute-done.3.refs_0_ = bf16[64,1024]{1,0:T(8,128)(2,1)S(1)} collective-permute-done((bf16[64,1024]{1,0:T(8,128)(2,1)S(1)}, bf16[64,1024]{1,0:T(8,128)(2,1)S(1)}, u32[]{:S(2)}, u32[]{:S(2)}) %collective-permute-start.3) | collective-permute-done | bytes 131104 | tf_op jit(solution)/shard_map/ppermute | solution.py:247
  12.8 4.6 %collective-permute-start.2 = (bf16[128,1024]{1,0:T(8,128)(2,1)S(1)}, bf16[128,1024]{1,0:T(8,128)(2,1)S(1)}, u32[]{:S(2)}, u32[]{:S(2)}) collective-permute-start(bf16[128,1024]{1,0:T(8,128)(2,1)S(1)} %get-tuple-element.22), channel_id=1, source_target_pairs={{0,12},{1,15},{2,14},{3,13},{4,8},{5,11},{6,10},{7,9},{8,4},{9,7},... | collective-permute-start | bytes 786440 | tf_op jit(solution)/shard_map/ppermute | solution.py:247
  17.4 1.9 %collective-permute-done.6.refs_3_ = bf16[128,1024]{1,0:T(8,128)(2,1)S(1)} collective-permute-done((bf16[128,1024]{1,0:T(8,128)(2,1)S(1)}, bf16[128,1024]{1,0:T(8,128)(2,1)S(1)}, u32[]{:S(2)}, u32[]{:S(2)}) %collective-permute-start.6) | collective-permute-done | bytes 262176 | tf_op jit(solution)/shard_map/ppermute | solution.py:247
  19.3 0.1 regroup.1
  19.4 8.9 %collective-permute-start.7 = (bf16[96,1024]{1,0:T(8,128)(2,1)S(1)}, bf16[96,1024]{1,0:T(8,128)(2,1)S(1)}, u32[]{:S(2)}, u32[]{:S(2)}) collective-permute-start(bf16[96,1024]{1,0:T(8,128)(2,1)S(1)} %get-tuple-element.26), channel_id=1, source_target_pairs={{0,1},{1,0},{2,3},{3,2},{4,5},{5,4},{6,7},{7,6},{8,9},{9,8},{10,11... | collective-permute-start | bytes 589832 | tf_op jit(solution)/shard_map/ppermute | solution.py:231
  28.3 0.1 collective-permute-start.8
  28.3 0.4 %collective-permute-start.9 = (bf16[96,1024]{1,0:T(8,128)(2,1)S(1)}, bf16[96,1024]{1,0:T(8,128)(2,1)S(1)}, u32[]{:S(2)}, u32[]{:S(2)}) collective-permute-start(bf16[96,1024]{1,0:T(8,128)(2,1)S(1)} %get-tuple-element.28), channel_id=1, source_target_pairs={{0,1},{1,0},{2,3},{3,2},{4,5},{5,4},{6,7},{7,6},{8,9},{9,8},{10,11... | collective-permute-start | bytes 589832 | tf_op jit(solution)/shard_map/ppermute | solution.py:231
  28.8 0.1 collective-permute-start.10
  28.8 0.7 %count.1.refs_8_ = f32[1,384]{1,0:T(1,128)S(1)} custom-call(bf16[64,1024]{1,0:T(8,128)(2,1)S(1)} %pass.1.refs_0_, bf16[64,1024]{1,0:T(8,128)(2,1)S(1)} %collective-permute-done.4.refs_1_, bf16[128,1024]{1,0:T(8,128)(2,1)S(1)} %collective-permute-done.5.refs_2_, bf16[128,1024]{1,0:T(8,128)(2,1)S(1)} %collective-permute-done.6.refs_3_), custom_call_target="tpu_custom_call" | custom-call | tf_op jit(solution)/shard_map/count/pallas_call | solution.py:109
  29.5 0.0 collective-permute-done.7.refs_4_
  29.5 0.2 collective-permute-done.8.refs_5_
  29.7 0.3 collective-permute-done.9.refs_6_
  30.0 0.3 collective-permute-done.10.refs_7_
  30.3 0.7 %cross.1.counts_ref = f32[1,384]{1,0:T(1,128)S(1)} custom-call(bf16[64,1024]{1,0:T(8,128)(2,1)S(1)} %pass.1.refs_0_, bf16[64,1024]{1,0:T(8,128)(2,1)S(1)} %collective-permute-done.4.refs_1_, bf16[128,1024]{1,0:T(8,128)(2,1)S(1)} %collective-permute-done.5.refs_2_, bf16[128,1024]{1,0:T(8,128)(2,1)S(1)} %collective-permute-done.6.refs_3_, ...), custom_call_target="tpu_custom_call" | custom-call | tf_op jit(solution)/shard_map/cross/pallas_call | solution.py:109
  30.9 0.3 collective-permute-start.11
  31.3 1.1 %late.1 = (f32[1,768]{1,0:T(1,128)S(1)}, f32[1,128]{1,0:T(1,128)S(1)}) custom-call(bf16[64,1024]{1,0:T(8,128)(2,1)S(1)} %pass.1.refs_0_, bf16[64,1024]{1,0:T(8,128)(2,1)S(1)} %collective-permute-done.4.refs_1_, bf16[128,1024]{1,0:T(8,128)(2,1)S(1)} %collective-permute-done.5.refs_2_, bf16[128,1024]{1,0:T(8,128)(2,1)S(1)} %collective-permute-done.6.refs_3_, ...), custom_call_target="tpu_custom_call" | custom-call | tf_op jit(solution)/shard_map/late/pallas_call | solution.py:109
  32.4 0.1 collective-permute-done.11.other_ref
  32.5 0.3 finish.1
  32.9 8.4 %all_to_all.5.counts_ref = f32[16,1,64]{2,1,0:T(1,128)S(1)} all-to-all(f32[16,1,64]{2,1,0:T(1,128)S(1)} %finish.1), channel_id=1, replica_groups={{10,8,6,4,14,12,2,1,11,9,7,5,15,13,3,0},{26,24,22,20,30,28,18,17,27,25,..., dimensions={0} | all-to-all | bytes 8192 | tf_op jit(solution)/shard_map/all_to_all | solution.py:332
  41.3 0.7 %select.1 = f32[1,256]{1,0:T(1,128)} custom-call(f32[16,1,64]{2,1,0:T(1,128)S(1)} %all_to_all.5.counts_ref, s32[1,256]{1,0:T(1,128)S(1)} %get-tuple-element.21.refs_2_.slot_ref), custom_call_target="tpu_custom_call" | custom-call | tf_op jit(solution)/shard_map/select/pallas_call | solution.py:109
  (7 shorter events, 0.0 us)
Async XLA Ops:
  0.0 0.7 %copy-start.1 = (s32[256]{0:T(256)S(1)}, s32[256]{0:T(256)}, u32[]{:S(2)}) copy-start(s32[256]{0:T(256)} %param.3) | copy-start | bytes 3076
  0.0 6.3 %collective-permute-start = (bf16[256,1024]{1,0:T(8,128)(2,1)}, bf16[256,1024]{1,0:T(8,128)(2,1)S(1)}, u32[]{:S(2)}, u32[]{:S(2)}) collective-permute-start(bf16[256,1024]{1,0:T(8,128)(2,1)} %refs_0_.3), channel_id=1, source_target_pairs={{0,1},{1,0},{2,3},{3,2},{4,5},{5,4},{6,7},{7,6},{8,9},{9,8},{10,11... | collective-permute-start | bytes 1572872 | tf_op jit(solution)/shard_map/ppermute | solution.py:231
  0.7 5.6 %collective-permute-start.1 = (s32[1,256]{1,0:T(1,128)S(1)}, s32[1,256]{1,0:T(1,128)S(1)}, u32[]{:S(2)}, u32[]{:S(2)}) collective-permute-start(s32[1,256]{1,0:T(1,128)S(1)} %bitcast.2), channel_id=1, source_target_pairs={{0,1},{1,0},{2,3},{3,2},{4,5},{5,4},{6,7},{7,6},{8,9},{9,8},{10,11... | collective-permute-start | bytes 3080 | tf_op jit(solution)/shard_map/ppermute | solution.py:231
  1.1 1.0 %copy-start = (bf16[256,1024]{1,0:T(8,128)(2,1)S(1)}, bf16[256,1024]{1,0:T(8,128)(2,1)}, u32[]{:S(2)}) copy-start(bf16[256,1024]{1,0:T(8,128)(2,1)} %refs_0_.3) | copy-start | bytes 1572868
  2.6 10.2 %collective-permute-start.3 = (bf16[64,1024]{1,0:T(8,128)(2,1)S(1)}, bf16[64,1024]{1,0:T(8,128)(2,1)S(1)}, u32[]{:S(2)}, u32[]{:S(2)}) collective-permute-start(bf16[64,1024]{1,0:T(8,128)(2,1)S(1)} %get-tuple-element.23), channel_id=1, source_target_pairs={{0,8},{1,11},{2,10},{3,9},{4,12},{5,15},{6,14},{7,13},{8,0},{9,3},... | collective-permute-start | bytes 393224 | tf_op jit(solution)/shard_map/ppermute | solution.py:247
  6.9 12.4 %collective-permute-start.5 = (bf16[128,1024]{1,0:T(8,128)(2,1)S(1)}, bf16[128,1024]{1,0:T(8,128)(2,1)S(1)}, u32[]{:S(2)}, u32[]{:S(2)}) collective-permute-start(bf16[128,1024]{1,0:T(8,128)(2,1)S(1)} %get-tuple-element.20), channel_id=1, source_target_pairs={{0,0},{1,3},{2,2},{3,1},{4,4},{5,7},{6,6},{7,5},{8,8},{9,11},{10,1... | collective-permute-start | bytes 786440 | tf_op jit(solution)/shard_map/ppermute | solution.py:247
  7.6 11.7 %collective-permute-start.6 = (bf16[128,1024]{1,0:T(8,128)(2,1)S(1)}, bf16[128,1024]{1,0:T(8,128)(2,1)S(1)}, u32[]{:S(2)}, u32[]{:S(2)}) collective-permute-start(bf16[128,1024]{1,0:T(8,128)(2,1)S(1)} %get-tuple-element.25), channel_id=1, source_target_pairs={{0,4},{1,7},{2,6},{3,5},{4,0},{5,3},{6,2},{7,1},{8,12},{9,15},{10,... | collective-permute-start | bytes 786440 | tf_op jit(solution)/shard_map/ppermute | solution.py:247
  9.8 7.6 %collective-permute-start.4 = (bf16[64,1024]{1,0:T(8,128)(2,1)S(1)}, bf16[64,1024]{1,0:T(8,128)(2,1)S(1)}, u32[]{:S(2)}, u32[]{:S(2)}) collective-permute-start(bf16[64,1024]{1,0:T(8,128)(2,1)S(1)} %get-tuple-element.24), channel_id=1, source_target_pairs={{0,8},{1,11},{2,10},{3,9},{4,12},{5,15},{6,14},{7,13},{8,0},{9,3},... | collective-permute-start | bytes 393224 | tf_op jit(solution)/shard_map/ppermute | solution.py:247
  12.8 18.1 %collective-permute-start.2 = (bf16[128,1024]{1,0:T(8,128)(2,1)S(1)}, bf16[128,1024]{1,0:T(8,128)(2,1)S(1)}, u32[]{:S(2)}, u32[]{:S(2)}) collective-permute-start(bf16[128,1024]{1,0:T(8,128)(2,1)S(1)} %get-tuple-element.22), channel_id=1, source_target_pairs={{0,12},{1,15},{2,14},{3,13},{4,8},{5,11},{6,10},{7,9},{8,4},{9,7},... | collective-permute-start | bytes 786440 | tf_op jit(solution)/shard_map/ppermute | solution.py:247
  19.4 10.1 %collective-permute-start.7 = (bf16[96,1024]{1,0:T(8,128)(2,1)S(1)}, bf16[96,1024]{1,0:T(8,128)(2,1)S(1)}, u32[]{:S(2)}, u32[]{:S(2)}) collective-permute-start(bf16[96,1024]{1,0:T(8,128)(2,1)S(1)} %get-tuple-element.26), channel_id=1, source_target_pairs={{0,1},{1,0},{2,3},{3,2},{4,5},{5,4},{6,7},{7,6},{8,9},{9,8},{10,11... | collective-permute-start | bytes 589832 | tf_op jit(solution)/shard_map/ppermute | solution.py:231
  28.3 1.4 %collective-permute-start.8 = (bf16[96,1024]{1,0:T(8,128)(2,1)S(1)}, bf16[96,1024]{1,0:T(8,128)(2,1)S(1)}, u32[]{:S(2)}, u32[]{:S(2)}) collective-permute-start(bf16[96,1024]{1,0:T(8,128)(2,1)S(1)} %get-tuple-element.27), channel_id=1, source_target_pairs={{0,1},{1,0},{2,3},{3,2},{4,5},{5,4},{6,7},{7,6},{8,9},{9,8},{10,11... | collective-permute-start | bytes 589832 | tf_op jit(solution)/shard_map/ppermute | solution.py:231
  28.3 1.6 %collective-permute-start.9 = (bf16[96,1024]{1,0:T(8,128)(2,1)S(1)}, bf16[96,1024]{1,0:T(8,128)(2,1)S(1)}, u32[]{:S(2)}, u32[]{:S(2)}) collective-permute-start(bf16[96,1024]{1,0:T(8,128)(2,1)S(1)} %get-tuple-element.28), channel_id=1, source_target_pairs={{0,1},{1,0},{2,3},{3,2},{4,5},{5,4},{6,7},{7,6},{8,9},{9,8},{10,11... | collective-permute-start | bytes 589832 | tf_op jit(solution)/shard_map/ppermute | solution.py:231
  28.8 1.5 %collective-permute-start.10 = (bf16[96,1024]{1,0:T(8,128)(2,1)S(1)}, bf16[96,1024]{1,0:T(8,128)(2,1)S(1)}, u32[]{:S(2)}, u32[]{:S(2)}) collective-permute-start(bf16[96,1024]{1,0:T(8,128)(2,1)S(1)} %get-tuple-element.29), channel_id=1, source_target_pairs={{0,1},{1,0},{2,3},{3,2},{4,5},{5,4},{6,7},{7,6},{8,9},{9,8},{10,11... | collective-permute-start | bytes 589832 | tf_op jit(solution)/shard_map/ppermute | solution.py:231
  30.9 1.6 %collective-permute-start.11 = (bf16[128,1024]{1,0:T(8,128)(2,1)S(1)}, bf16[128,1024]{1,0:T(8,128)(2,1)S(1)}, u32[]{:S(2)}, u32[]{:S(2)}) collective-permute-start(bf16[128,1024]{1,0:T(8,128)(2,1)S(1)} %collective-permute-done.2.refs_8_.late_ref), channel_id=1, source_target_pairs={{0,1},{1,0},{2,3},{3,2},{4,5},{5,4},{6,7},{7,6},{8,9},{9,8},{10,11... | collective-permute-start | bytes 786440 | tf_op jit(solution)/shard_map/ppermute | solution.py:231

commit v32 on v30

--- a/solution.py
+++ b/solution.py
@@ -235,7 +235,7 @@
 
     def across(x, p):
         pairs = [
-            (chip * cores + core, (chip ^ (p * cores + core)) * cores + core)
+            (chip * cores + core, (chip ^ (p * cores + core)) * cores + (core ^ (p == 0)))
             for chip in range(clusters)
             for core in range(cores)
         ]
@@ -308,8 +308,9 @@
         devices = []
         for here in (core, 1 - core):
             for p in (first, *middle):
-                there = (chip ^ (p * cores + here)) * cores
-                devices += [there + here, there + 1 - here]
+                source = 1 - here if p == 0 else here
+                there = (chip ^ (p * cores + source)) * cores
+                devices += [there + source, there + 1 - source]
         there = (chip ^ (last * cores + core)) * cores
         devices += [there + core, there + 1 - core]
         return [place_of(device) for device in devices]

time: 42.1 us -> 42.1 us (level)
  starting transfers between devices: 21.7 us -> 14 us
  waiting for transfers between devices: 5.31 us -> 12.1 us
  blocking collectives: 8.26 us -> 9.2 us
    ppermute x7, starting transfers between devices: 10.7 us -> 2.55 us  [swap_cores(): return lax.ppermute(x, 'sub', [(i, i ^ 1) for i in range(cores)])]
    ppermute x5, waiting for transfers between devices: 4.48 us -> 11.2 us  [across(): return lax.ppermute(x, ('owner', 'helper', 'sub'), pairs)]
    all_to_all x1, blocking collectives: 8.26 us -> 9.2 us  [body_by_chip(): lax.all_to_all(counts, ('owner', 'helper', 'sub'), split_axis=0, concat_a...]
    ppermute x5, starting transfers between devices: 11 us -> 11.4 us  [across(): return lax.ppermute(x, ('owner', 'helper', 'sub'), pairs)]
  transfers between devices with their start and end apart: 12 -> 12, of which waited for: 6 -> 7; matrix products, arithmetic and copies ran while one was open for 0% -> 0% of each run, Pallas kernels for 10% -> 10%
where the time goes in v32:
time: 42.1 us; the launch traced here: 41.9 us
  starting transfers between devices  14 us (33%)
  waiting for transfers between devices  12.1 us (29%)
  blocking collectives  9.2 us (22%)
  Pallas kernels  5.27 us (13%)
  local copies, waits for them, and re-layouts  1.27 us (3%)
    ppermute x5, starting transfers between devices, across(): return lax.ppermute(x, ('owner', 'helper', 'sub'), pairs)  11.4 us
    ppermute x5, waiting for transfers between devices, across(): return lax.ppermute(x, ('owner', 'helper', 'sub'), pairs)  11.2 us
    all_to_all x1, blocking collectives, body_by_chip(): lax.all_to_all(counts, ('owner', 'helper', 'sub'), split_axis=0, concat_a...  9.2 us
    pallas_call x10, Pallas kernels, call_kernel(): pl.pallas_call(kernel, out_shape=out_shape, in_specs=[VMEM] * len(args),...  5.27 us
    ppermute x7, starting transfers between devices, swap_cores(): return lax.ppermute(x, 'sub', [(i, i ^ 1) for i in range(cores)])  2.55 us
    unnamed x4, local copies, waits for them, and re-layouts  1.27 us
  transfers between devices with their start and end apart: 12, of which 7 were waited for; matrix products, arithmetic and copies ran while one was open for 0% of the time, Pallas kernels for 10%

profile of v32, /device:TPU:0, one launch (start us, length us, event | category | flops | bytes accessed | tf_op | source)
XLA Modules:
  0.0 41.9 jit_solution(15167577696994253915)
XLA Ops:
  0.0 0.5 %collective-permute-start = (bf16[256,1024]{1,0:T(8,128)(2,1)}, bf16[256,1024]{1,0:T(8,128)(2,1)S(1)}, u32[]{:S(2)}, u32[]{:S(2)}) collective-permute-start(bf16[256,1024]{1,0:T(8,128)(2,1)} %refs_0_.3), channel_id=1, source_target_pairs={{0,1},{1,0},{2,3},{3,2},{4,5},{5,4},{6,7},{7,6},{8,9},{9,8},{10,11... | collective-permute-start | bytes 1572872 | tf_op jit(solution)/shard_map/ppermute | solution.py:226
  0.5 0.2 copy-done.1
  0.7 0.5 %collective-permute-start.1 = (s32[1,256]{1,0:T(1,128)S(1)}, s32[1,256]{1,0:T(1,128)S(1)}, u32[]{:S(2)}, u32[]{:S(2)}) collective-permute-start(s32[1,256]{1,0:T(1,128)S(1)} %bitcast.2), channel_id=1, source_target_pairs={{0,1},{1,0},{2,3},{3,2},{4,5},{5,4},{6,7},{7,6},{8,9},{9,8},{10,11... | collective-permute-start | bytes 3080 | tf_op jit(solution)/shard_map/ppermute | solution.py:226
  1.1 1.0 %copy-done = bf16[256,1024]{1,0:T(8,128)(2,1)S(1)} copy-done((bf16[256,1024]{1,0:T(8,128)(2,1)S(1)}, bf16[256,1024]{1,0:T(8,128)(2,1)}, u32[]{:S(2)}) %copy-start) | copy-done | bytes 524312
  2.2 0.5 %route_first.1 = (bf16[64,1024]{1,0:T(8,128)(2,1)S(1)}, s32[1,256]{1,0:T(1,128)S(1)}) custom-call(bf16[256,1024]{1,0:T(8,128)(2,1)S(1)} %copy-done, s32[1,256]{1,0:T(1,128)S(1)} %bitcast.3), custom_call_target="tpu_custom_call" | custom-call | tf_op jit(solution)/shard_map/route_first/pallas_call | solution.py:106
  2.6 3.7 %collective-permute-start.3 = (bf16[64,1024]{1,0:T(8,128)(2,1)S(1)}, bf16[64,1024]{1,0:T(8,128)(2,1)S(1)}, u32[]{:S(2)}, u32[]{:S(2)}) collective-permute-start(bf16[64,1024]{1,0:T(8,128)(2,1)S(1)} %get-tuple-element.23), channel_id=1, source_target_pairs={{0,8},{1,11},{2,10},{3,9},{4,12},{5,15},{6,14},{7,13},{8,0},{9,3},... | collective-permute-start | bytes 393224 | tf_op jit(solution)/shard_map/ppermute | solution.py:242
  6.3 0.0 collective-permute-done.refs_1_
  6.3 0.6 %route_near.1 = (bf16[128,1024]{1,0:T(8,128)(2,1)S(1)}, bf16[128,1024]{1,0:T(8,128)(2,1)S(1)}) custom-call(bf16[256,1024]{1,0:T(8,128)(2,1)S(1)} %copy-done, bf16[256,1024]{1,0:T(8,128)(2,1)S(1)} %collective-permute-done.refs_1_, s32[1,256]{1,0:T(1,128)S(1)} %get-tuple-element.21.refs_2_.slot_ref, s32[1,256]{1,0:T(1,128)S(1)} %collective-permute-done.1.refs_3_), custom_call_target="tpu_custom_call" | custom-call | tf_op jit(solution)/shard_map/route_near/pallas_call | solution.py:106
  6.9 1.2 %collective-permute-start.5 = (bf16[128,1024]{1,0:T(8,128)(2,1)S(1)}, bf16[128,1024]{1,0:T(8,128)(2,1)S(1)}, u32[]{:S(2)}, u32[]{:S(2)}) collective-permute-start(bf16[128,1024]{1,0:T(8,128)(2,1)S(1)} %get-tuple-element.20), channel_id=1, source_target_pairs={{0,1},{1,2},{2,3},{3,0},{4,5},{5,6},{6,7},{7,4},{8,9},{9,10},{10,1... | collective-permute-start | bytes 786440 | tf_op jit(solution)/shard_map/ppermute | solution.py:242
  8.1 1.6 %collective-permute-start.6 = (bf16[128,1024]{1,0:T(8,128)(2,1)S(1)}, bf16[128,1024]{1,0:T(8,128)(2,1)S(1)}, u32[]{:S(2)}, u32[]{:S(2)}) collective-permute-start(bf16[128,1024]{1,0:T(8,128)(2,1)S(1)} %get-tuple-element.25), channel_id=1, source_target_pairs={{0,4},{1,7},{2,6},{3,5},{4,0},{5,3},{6,2},{7,1},{8,12},{9,15},{10,... | collective-permute-start | bytes 786440 | tf_op jit(solution)/shard_map/ppermute | solution.py:242
  9.7 0.6 %route_far.1 = (bf16[64,1024]{1,0:T(8,128)(2,1)S(1)}, bf16[128,1024]{1,0:T(8,128)(2,1)S(1)}) custom-call(bf16[256,1024]{1,0:T(8,128)(2,1)S(1)} %copy-done, bf16[256,1024]{1,0:T(8,128)(2,1)S(1)} %collective-permute-done.refs_1_, s32[1,256]{1,0:T(1,128)S(1)} %get-tuple-element.21.refs_2_.slot_ref, s32[1,256]{1,0:T(1,128)S(1)} %collective-permute-done.1.refs_3_), custom_call_target="tpu_custom_call" | custom-call | flops 10000000000 | tf_op jit(solution)/shard_map/route_far/pallas_call | solution.py:106
  10.3 0.4 collective-permute-start.4
  10.7 2.1 %collective-permute-done.3.refs_0_ = bf16[64,1024]{1,0:T(8,128)(2,1)S(1)} collective-permute-done((bf16[64,1024]{1,0:T(8,128)(2,1)S(1)}, bf16[64,1024]{1,0:T(8,128)(2,1)S(1)}, u32[]{:S(2)}, u32[]{:S(2)}) %collective-permute-start.3) | collective-permute-done | bytes 131104 | tf_op jit(solution)/shard_map/ppermute | solution.py:242
  12.8 4.6 %collective-permute-start.2 = (bf16[128,1024]{1,0:T(8,128)(2,1)S(1)}, bf16[128,1024]{1,0:T(8,128)(2,1)S(1)}, u32[]{:S(2)}, u32[]{:S(2)}) collective-permute-start(bf16[128,1024]{1,0:T(8,128)(2,1)S(1)} %get-tuple-element.22), channel_id=1, source_target_pairs={{0,12},{1,15},{2,14},{3,13},{4,8},{5,11},{6,10},{7,9},{8,4},{9,7},... | collective-permute-start | bytes 786440 | tf_op jit(solution)/shard_map/ppermute | solution.py:242
  17.4 1.6 %collective-permute-done.4.refs_1_ = bf16[64,1024]{1,0:T(8,128)(2,1)S(1)} collective-permute-done((bf16[64,1024]{1,0:T(8,128)(2,1)S(1)}, bf16[64,1024]{1,0:T(8,128)(2,1)S(1)}, u32[]{:S(2)}, u32[]{:S(2)}) %collective-permute-start.4) | collective-permute-done | bytes 131104 | tf_op jit(solution)/shard_map/ppermute | solution.py:242
  19.0 7.5 %collective-permute-done.6.refs_3_ = bf16[128,1024]{1,0:T(8,128)(2,1)S(1)} collective-permute-done((bf16[128,1024]{1,0:T(8,128)(2,1)S(1)}, bf16[128,1024]{1,0:T(8,128)(2,1)S(1)}, u32[]{:S(2)}, u32[]{:S(2)}) %collective-permute-start.6) | collective-permute-done | bytes 262176 | tf_op jit(solution)/shard_map/ppermute | solution.py:242
  26.5 0.1 regroup.1
  26.6 0.7 %collective-permute-start.7 = (bf16[96,1024]{1,0:T(8,128)(2,1)S(1)}, bf16[96,1024]{1,0:T(8,128)(2,1)S(1)}, u32[]{:S(2)}, u32[]{:S(2)}) collective-permute-start(bf16[96,1024]{1,0:T(8,128)(2,1)S(1)} %get-tuple-element.26), channel_id=1, source_target_pairs={{0,1},{1,0},{2,3},{3,2},{4,5},{5,4},{6,7},{7,6},{8,9},{9,8},{10,11... | collective-permute-start | bytes 589832 | tf_op jit(solution)/shard_map/ppermute | solution.py:226
  27.3 0.1 collective-permute-start.8
  27.4 0.4 %collective-permute-start.9 = (bf16[96,1024]{1,0:T(8,128)(2,1)S(1)}, bf16[96,1024]{1,0:T(8,128)(2,1)S(1)}, u32[]{:S(2)}, u32[]{:S(2)}) collective-permute-start(bf16[96,1024]{1,0:T(8,128)(2,1)S(1)} %get-tuple-element.28), channel_id=1, source_target_pairs={{0,1},{1,0},{2,3},{3,2},{4,5},{5,4},{6,7},{7,6},{8,9},{9,8},{10,11... | collective-permute-start | bytes 589832 | tf_op jit(solution)/shard_map/ppermute | solution.py:226
  27.8 0.1 collective-permute-start.10
  27.9 0.7 %count.1.refs_8_ = f32[1,384]{1,0:T(1,128)S(1)} custom-call(bf16[64,1024]{1,0:T(8,128)(2,1)S(1)} %pass.1.refs_0_, bf16[64,1024]{1,0:T(8,128)(2,1)S(1)} %collective-permute-done.4.refs_1_, bf16[128,1024]{1,0:T(8,128)(2,1)S(1)} %collective-permute-done.5.refs_2_, bf16[128,1024]{1,0:T(8,128)(2,1)S(1)} %collective-permute-done.6.refs_3_), custom_call_target="tpu_custom_call" | custom-call | tf_op jit(solution)/shard_map/count/pallas_call | solution.py:106
  28.6 0.2 collective-permute-done.8.refs_5_
  28.8 0.3 collective-permute-done.9.refs_6_
  29.0 0.3 collective-permute-done.10.refs_7_
  29.3 0.7 %cross.1.counts_ref = f32[1,384]{1,0:T(1,128)S(1)} custom-call(bf16[64,1024]{1,0:T(8,128)(2,1)S(1)} %pass.1.refs_0_, bf16[64,1024]{1,0:T(8,128)(2,1)S(1)} %collective-permute-done.4.refs_1_, bf16[128,1024]{1,0:T(8,128)(2,1)S(1)} %collective-permute-done.5.refs_2_, bf16[128,1024]{1,0:T(8,128)(2,1)S(1)} %collective-permute-done.6.refs_3_, ...), custom_call_target="tpu_custom_call" | custom-call | tf_op jit(solution)/shard_map/cross/pallas_call | solution.py:106
  30.0 0.3 collective-permute-start.11
  30.3 1.1 %late.1 = (f32[1,768]{1,0:T(1,128)S(1)}, f32[1,128]{1,0:T(1,128)S(1)}) custom-call(bf16[64,1024]{1,0:T(8,128)(2,1)S(1)} %pass.1.refs_0_, bf16[64,1024]{1,0:T(8,128)(2,1)S(1)} %collective-permute-done.4.refs_1_, bf16[128,1024]{1,0:T(8,128)(2,1)S(1)} %collective-permute-done.5.refs_2_, bf16[128,1024]{1,0:T(8,128)(2,1)S(1)} %collective-permute-done.6.refs_3_, ...), custom_call_target="tpu_custom_call" | custom-call | tf_op jit(solution)/shard_map/late/pallas_call | solution.py:106
  31.5 0.1 collective-permute-done.11.other_ref
  31.6 0.3 finish.1
  31.9 9.2 %all_to_all.5.counts_ref = f32[16,1,64]{2,1,0:T(1,128)S(1)} all-to-all(f32[16,1,64]{2,1,0:T(1,128)S(1)} %finish.1), channel_id=1, replica_groups={{11,10,9,8,7,6,5,4,15,14,13,12,3,2,1,0},{27,26,25,24,23,22,21,20,31,30,..., dimensions={0} | all-to-all | bytes 8192 | tf_op jit(solution)/shard_map/all_to_all | solution.py:328
  41.1 0.7 %select.1 = f32[1,256]{1,0:T(1,128)} custom-call(f32[16,1,64]{2,1,0:T(1,128)S(1)} %all_to_all.5.counts_ref, s32[1,256]{1,0:T(1,128)S(1)} %get-tuple-element.21.refs_2_.slot_ref), custom_call_target="tpu_custom_call" | custom-call | tf_op jit(solution)/shard_map/select/pallas_call | solution.py:106
  (7 shorter events, 0.0 us)
Async XLA Ops:
  0.0 0.7 %copy-start.1 = (s32[256]{0:T(256)S(1)}, s32[256]{0:T(256)}, u32[]{:S(2)}) copy-start(s32[256]{0:T(256)} %param.3) | copy-start | bytes 3076
  0.0 6.3 %collective-permute-start = (bf16[256,1024]{1,0:T(8,128)(2,1)}, bf16[256,1024]{1,0:T(8,128)(2,1)S(1)}, u32[]{:S(2)}, u32[]{:S(2)}) collective-permute-start(bf16[256,1024]{1,0:T(8,128)(2,1)} %refs_0_.3), channel_id=1, source_target_pairs={{0,1},{1,0},{2,3},{3,2},{4,5},{5,4},{6,7},{7,6},{8,9},{9,8},{10,11... | collective-permute-start | bytes 1572872 | tf_op jit(solution)/shard_map/ppermute | solution.py:226
  0.7 5.6 %collective-permute-start.1 = (s32[1,256]{1,0:T(1,128)S(1)}, s32[1,256]{1,0:T(1,128)S(1)}, u32[]{:S(2)}, u32[]{:S(2)}) collective-permute-start(s32[1,256]{1,0:T(1,128)S(1)} %bitcast.2), channel_id=1, source_target_pairs={{0,1},{1,0},{2,3},{3,2},{4,5},{5,4},{6,7},{7,6},{8,9},{9,8},{10,11... | collective-permute-start | bytes 3080 | tf_op jit(solution)/shard_map/ppermute | solution.py:226
  1.1 1.0 %copy-start = (bf16[256,1024]{1,0:T(8,128)(2,1)S(1)}, bf16[256,1024]{1,0:T(8,128)(2,1)}, u32[]{:S(2)}) copy-start(bf16[256,1024]{1,0:T(8,128)(2,1)} %refs_0_.3) | copy-start | bytes 1572868
  2.6 10.2 %collective-permute-start.3 = (bf16[64,1024]{1,0:T(8,128)(2,1)S(1)}, bf16[64,1024]{1,0:T(8,128)(2,1)S(1)}, u32[]{:S(2)}, u32[]{:S(2)}) collective-permute-start(bf16[64,1024]{1,0:T(8,128)(2,1)S(1)} %get-tuple-element.23), channel_id=1, source_target_pairs={{0,8},{1,11},{2,10},{3,9},{4,12},{5,15},{6,14},{7,13},{8,0},{9,3},... | collective-permute-start | bytes 393224 | tf_op jit(solution)/shard_map/ppermute | solution.py:242
  6.9 19.6 %collective-permute-start.5 = (bf16[128,1024]{1,0:T(8,128)(2,1)S(1)}, bf16[128,1024]{1,0:T(8,128)(2,1)S(1)}, u32[]{:S(2)}, u32[]{:S(2)}) collective-permute-start(bf16[128,1024]{1,0:T(8,128)(2,1)S(1)} %get-tuple-element.20), channel_id=1, source_target_pairs={{0,1},{1,2},{2,3},{3,0},{4,5},{5,6},{6,7},{7,4},{8,9},{9,10},{10,1... | collective-permute-start | bytes 786440 | tf_op jit(solution)/shard_map/ppermute | solution.py:242
  8.1 18.4 %collective-permute-start.6 = (bf16[128,1024]{1,0:T(8,128)(2,1)S(1)}, bf16[128,1024]{1,0:T(8,128)(2,1)S(1)}, u32[]{:S(2)}, u32[]{:S(2)}) collective-permute-start(bf16[128,1024]{1,0:T(8,128)(2,1)S(1)} %get-tuple-element.25), channel_id=1, source_target_pairs={{0,4},{1,7},{2,6},{3,5},{4,0},{5,3},{6,2},{7,1},{8,12},{9,15},{10,... | collective-permute-start | bytes 786440 | tf_op jit(solution)/shard_map/ppermute | solution.py:242
  10.3 8.7 %collective-permute-start.4 = (bf16[64,1024]{1,0:T(8,128)(2,1)S(1)}, bf16[64,1024]{1,0:T(8,128)(2,1)S(1)}, u32[]{:S(2)}, u32[]{:S(2)}) collective-permute-start(bf16[64,1024]{1,0:T(8,128)(2,1)S(1)} %get-tuple-element.24), channel_id=1, source_target_pairs={{0,8},{1,11},{2,10},{3,9},{4,12},{5,15},{6,14},{7,13},{8,0},{9,3},... | collective-permute-start | bytes 393224 | tf_op jit(solution)/shard_map/ppermute | solution.py:242
  12.8 17.2 %collective-permute-start.2 = (bf16[128,1024]{1,0:T(8,128)(2,1)S(1)}, bf16[128,1024]{1,0:T(8,128)(2,1)S(1)}, u32[]{:S(2)}, u32[]{:S(2)}) collective-permute-start(bf16[128,1024]{1,0:T(8,128)(2,1)S(1)} %get-tuple-element.22), channel_id=1, source_target_pairs={{0,12},{1,15},{2,14},{3,13},{4,8},{5,11},{6,10},{7,9},{8,4},{9,7},... | collective-permute-start | bytes 786440 | tf_op jit(solution)/shard_map/ppermute | solution.py:242
  26.6 2.0 %collective-permute-start.7 = (bf16[96,1024]{1,0:T(8,128)(2,1)S(1)}, bf16[96,1024]{1,0:T(8,128)(2,1)S(1)}, u32[]{:S(2)}, u32[]{:S(2)}) collective-permute-start(bf16[96,1024]{1,0:T(8,128)(2,1)S(1)} %get-tuple-element.26), channel_id=1, source_target_pairs={{0,1},{1,0},{2,3},{3,2},{4,5},{5,4},{6,7},{7,6},{8,9},{9,8},{10,11... | collective-permute-start | bytes 589832 | tf_op jit(solution)/shard_map/ppermute | solution.py:226
  27.3 1.4 %collective-permute-start.8 = (bf16[96,1024]{1,0:T(8,128)(2,1)S(1)}, bf16[96,1024]{1,0:T(8,128)(2,1)S(1)}, u32[]{:S(2)}, u32[]{:S(2)}) collective-permute-start(bf16[96,1024]{1,0:T(8,128)(2,1)S(1)} %get-tuple-element.27), channel_id=1, source_target_pairs={{0,1},{1,0},{2,3},{3,2},{4,5},{5,4},{6,7},{7,6},{8,9},{9,8},{10,11... | collective-permute-start | bytes 589832 | tf_op jit(solution)/shard_map/ppermute | solution.py:226
  27.4 1.6 %collective-permute-start.9 = (bf16[96,1024]{1,0:T(8,128)(2,1)S(1)}, bf16[96,1024]{1,0:T(8,128)(2,1)S(1)}, u32[]{:S(2)}, u32[]{:S(2)}) collective-permute-start(bf16[96,1024]{1,0:T(8,128)(2,1)S(1)} %get-tuple-element.28), channel_id=1, source_target_pairs={{0,1},{1,0},{2,3},{3,2},{4,5},{5,4},{6,7},{7,6},{8,9},{9,8},{10,11... | collective-permute-start | bytes 589832 | tf_op jit(solution)/shard_map/ppermute | solution.py:226
  27.8 1.5 %collective-permute-start.10 = (bf16[96,1024]{1,0:T(8,128)(2,1)S(1)}, bf16[96,1024]{1,0:T(8,128)(2,1)S(1)}, u32[]{:S(2)}, u32[]{:S(2)}) collective-permute-start(bf16[96,1024]{1,0:T(8,128)(2,1)S(1)} %get-tuple-element.29), channel_id=1, source_target_pairs={{0,1},{1,0},{2,3},{3,2},{4,5},{5,4},{6,7},{7,6},{8,9},{9,8},{10,11... | collective-permute-start | bytes 589832 | tf_op jit(solution)/shard_map/ppermute | solution.py:226
  30.0 1.6 %collective-permute-start.11 = (bf16[128,1024]{1,0:T(8,128)(2,1)S(1)}, bf16[128,1024]{1,0:T(8,128)(2,1)S(1)}, u32[]{:S(2)}, u32[]{:S(2)}) collective-permute-start(bf16[128,1024]{1,0:T(8,128)(2,1)S(1)} %collective-permute-done.2.refs_8_.late_ref), channel_id=1, source_target_pairs={{0,1},{1,0},{2,3},{3,2},{4,5},{5,4},{6,7},{7,6},{8,9},{9,8},{10,11... | collective-permute-start | bytes 786440 | tf_op jit(solution)/shard_map/ppermute | solution.py:226

commit v33 on v29

--- a/solution.py
+++ b/solution.py
@@ -230,7 +230,7 @@
 
     ids = cluster_id.reshape(1, doc_count)
     other_rows, other_ids = swap_cores(embeddings), swap_cores(ids)
-    first, last = steps // 2, steps - 1
+    first, last = steps - 1, steps // 2
     middle = [p for p in range(steps) if p not in (first, last)]
     half = jax.ShapeDtypeStruct((capacity, feature_count), jnp.bfloat16)
     whole = jax.ShapeDtypeStruct((cores * capacity, feature_count), jnp.bfloat16)

time: 42 us -> 42.8 us (1.019)
  waiting for transfers between devices: 5.31 us -> 10.6 us
  starting transfers between devices: 21.7 us -> 17.5 us
    ppermute x5, waiting for transfers between devices: 4.48 us -> 9.84 us  [across(): return lax.ppermute(x, ('owner', 'helper', 'sub'), pairs)]
    ppermute x7, starting transfers between devices: 10.7 us -> 7.08 us  [swap_cores(): return lax.ppermute(x, 'sub', [(i, i ^ 1) for i in range(cores)])]
    ppermute x5, starting transfers between devices: 11 us -> 10.4 us  [across(): return lax.ppermute(x, ('owner', 'helper', 'sub'), pairs)]
where the time goes in v33:
time: 42.8 us; the launch traced here: 42.6 us
  starting transfers between devices  17.5 us (41%)
  waiting for transfers between devices  10.6 us (25%)
  blocking collectives  7.91 us (18%)
  Pallas kernels  5.25 us (12%)
  local copies, waits for them, and re-layouts  1.27 us (3%)
    ppermute x5, starting transfers between devices, across(): return lax.ppermute(x, ('owner', 'helper', 'sub'), pairs)  10.4 us
    ppermute x5, waiting for transfers between devices, across(): return lax.ppermute(x, ('owner', 'helper', 'sub'), pairs)  9.84 us
    all_to_all x1, blocking collectives, body_by_chip(): lax.all_to_all(counts, ('owner', 'helper', 'sub'), split_axis=0, concat_a...  7.91 us
    ppermute x7, starting transfers between devices, swap_cores(): return lax.ppermute(x, 'sub', [(i, i ^ 1) for i in range(cores)])  7.08 us
    pallas_call x10, Pallas kernels, call_kernel(): pl.pallas_call(kernel, out_shape=out_shape, in_specs=[VMEM] * len(args),...  5.25 us
    unnamed x4, local copies, waits for them, and re-layouts  1.27 us
  transfers between devices with their start and end apart: 12, of which 6 were waited for; matrix products, arithmetic and copies ran while one was open for 0% of the time, Pallas kernels for 10%

profile of v33, /device:TPU:0, one launch (start us, length us, event | category | flops | bytes accessed | tf_op | source)
XLA Modules:
  0.0 42.6 jit_solution(12043757079480644159)
XLA Ops:
  0.0 0.5 %collective-permute-start = (bf16[256,1024]{1,0:T(8,128)(2,1)}, bf16[256,1024]{1,0:T(8,128)(2,1)S(1)}, u32[]{:S(2)}, u32[]{:S(2)}) collective-permute-start(bf16[256,1024]{1,0:T(8,128)(2,1)} %refs_0_.3), channel_id=1, source_target_pairs={{0,1},{1,0},{2,3},{3,2},{4,5},{5,4},{6,7},{7,6},{8,9},{9,8},{10,11... | collective-permute-start | bytes 1572872 | tf_op jit(solution)/shard_map/ppermute | solution.py:213
  0.5 0.2 copy-done.1
  0.7 0.5 %collective-permute-start.1 = (s32[1,256]{1,0:T(1,128)S(1)}, s32[1,256]{1,0:T(1,128)S(1)}, u32[]{:S(2)}, u32[]{:S(2)}) collective-permute-start(s32[1,256]{1,0:T(1,128)S(1)} %bitcast.2), channel_id=1, source_target_pairs={{0,1},{1,0},{2,3},{3,2},{4,5},{5,4},{6,7},{7,6},{8,9},{9,8},{10,11... | collective-permute-start | bytes 3080 | tf_op jit(solution)/shard_map/ppermute | solution.py:213
  1.1 1.0 %copy-done = bf16[256,1024]{1,0:T(8,128)(2,1)S(1)} copy-done((bf16[256,1024]{1,0:T(8,128)(2,1)S(1)}, bf16[256,1024]{1,0:T(8,128)(2,1)}, u32[]{:S(2)}) %copy-start) | copy-done | bytes 524312
  2.2 0.5 %route_first.1 = (bf16[64,1024]{1,0:T(8,128)(2,1)S(1)}, s32[1,256]{1,0:T(1,128)S(1)}) custom-call(bf16[256,1024]{1,0:T(8,128)(2,1)S(1)} %copy-done, s32[1,256]{1,0:T(1,128)S(1)} %bitcast.3), custom_call_target="tpu_custom_call" | custom-call | tf_op jit(solution)/shard_map/route_first/pallas_call | solution.py:94
  2.6 4.7 %collective-permute-start.3 = (bf16[64,1024]{1,0:T(8,128)(2,1)S(1)}, bf16[64,1024]{1,0:T(8,128)(2,1)S(1)}, u32[]{:S(2)}, u32[]{:S(2)}) collective-permute-start(bf16[64,1024]{1,0:T(8,128)(2,1)S(1)} %get-tuple-element.23), channel_id=1, source_target_pairs={{0,12},{1,15},{2,14},{3,13},{4,8},{5,11},{6,10},{7,9},{8,4},{9,7},... | collective-permute-start | bytes 393224 | tf_op jit(solution)/shard_map/ppermute | solution.py:229
  7.3 0.0 collective-permute-done.1.refs_3_
  7.3 0.6 %route_near.1 = (bf16[128,1024]{1,0:T(8,128)(2,1)S(1)}, bf16[128,1024]{1,0:T(8,128)(2,1)S(1)}) custom-call(bf16[256,1024]{1,0:T(8,128)(2,1)S(1)} %copy-done, bf16[256,1024]{1,0:T(8,128)(2,1)S(1)} %collective-permute-done.refs_1_, s32[1,256]{1,0:T(1,128)S(1)} %get-tuple-element.21.refs_2_.slot_ref, s32[1,256]{1,0:T(1,128)S(1)} %collective-permute-done.1.refs_3_), custom_call_target="tpu_custom_call" | custom-call | tf_op jit(solution)/shard_map/route_near/pallas_call | solution.py:94
  7.9 0.7 %collective-permute-start.5 = (bf16[128,1024]{1,0:T(8,128)(2,1)S(1)}, bf16[128,1024]{1,0:T(8,128)(2,1)S(1)}, u32[]{:S(2)}, u32[]{:S(2)}) collective-permute-start(bf16[128,1024]{1,0:T(8,128)(2,1)S(1)} %get-tuple-element.20), channel_id=1, source_target_pairs={{0,0},{1,3},{2,2},{3,1},{4,4},{5,7},{6,6},{7,5},{8,8},{9,11},{10,1... | collective-permute-start | bytes 786440 | tf_op jit(solution)/shard_map/ppermute | solution.py:229
  8.6 0.1 collective-permute-start.6
  8.7 0.6 %route_far.1 = (bf16[64,1024]{1,0:T(8,128)(2,1)S(1)}, bf16[128,1024]{1,0:T(8,128)(2,1)S(1)}) custom-call(bf16[256,1024]{1,0:T(8,128)(2,1)S(1)} %copy-done, bf16[256,1024]{1,0:T(8,128)(2,1)S(1)} %collective-permute-done.refs_1_, s32[1,256]{1,0:T(1,128)S(1)} %get-tuple-element.21.refs_2_.slot_ref, s32[1,256]{1,0:T(1,128)S(1)} %collective-permute-done.1.refs_3_), custom_call_target="tpu_custom_call" | custom-call | flops 10000000000 | tf_op jit(solution)/shard_map/route_far/pallas_call | solution.py:94
  9.3 0.9 %collective-permute-start.4 = (bf16[64,1024]{1,0:T(8,128)(2,1)S(1)}, bf16[64,1024]{1,0:T(8,128)(2,1)S(1)}, u32[]{:S(2)}, u32[]{:S(2)}) collective-permute-start(bf16[64,1024]{1,0:T(8,128)(2,1)S(1)} %get-tuple-element.24), channel_id=1, source_target_pairs={{0,12},{1,15},{2,14},{3,13},{4,8},{5,11},{6,10},{7,9},{8,4},{9,7},... | collective-permute-start | bytes 393224 | tf_op jit(solution)/shard_map/ppermute | solution.py:229
  10.2 0.9 %collective-permute-done.3.refs_0_ = bf16[64,1024]{1,0:T(8,128)(2,1)S(1)} collective-permute-done((bf16[64,1024]{1,0:T(8,128)(2,1)S(1)}, bf16[64,1024]{1,0:T(8,128)(2,1)S(1)}, u32[]{:S(2)}, u32[]{:S(2)}) %collective-permute-start.3) | collective-permute-done | bytes 131104 | tf_op jit(solution)/shard_map/ppermute | solution.py:229
  11.1 4.0 %collective-permute-start.2 = (bf16[128,1024]{1,0:T(8,128)(2,1)S(1)}, bf16[128,1024]{1,0:T(8,128)(2,1)S(1)}, u32[]{:S(2)}, u32[]{:S(2)}) collective-permute-start(bf16[128,1024]{1,0:T(8,128)(2,1)S(1)} %get-tuple-element.22), channel_id=1, source_target_pairs={{0,8},{1,11},{2,10},{3,9},{4,12},{5,15},{6,14},{7,13},{8,0},{9,3},... | collective-permute-start | bytes 786440 | tf_op jit(solution)/shard_map/ppermute | solution.py:229
  15.2 3.8 %collective-permute-done.4.refs_1_ = bf16[64,1024]{1,0:T(8,128)(2,1)S(1)} collective-permute-done((bf16[64,1024]{1,0:T(8,128)(2,1)S(1)}, bf16[64,1024]{1,0:T(8,128)(2,1)S(1)}, u32[]{:S(2)}, u32[]{:S(2)}) %collective-permute-start.4) | collective-permute-done | bytes 131104 | tf_op jit(solution)/shard_map/ppermute | solution.py:229
  19.0 0.1 regroup.1
  19.0 3.2 %collective-permute-start.7 = (bf16[96,1024]{1,0:T(8,128)(2,1)S(1)}, bf16[96,1024]{1,0:T(8,128)(2,1)S(1)}, u32[]{:S(2)}, u32[]{:S(2)}) collective-permute-start(bf16[96,1024]{1,0:T(8,128)(2,1)S(1)} %get-tuple-element.26), channel_id=1, source_target_pairs={{0,1},{1,0},{2,3},{3,2},{4,5},{5,4},{6,7},{7,6},{8,9},{9,8},{10,11... | collective-permute-start | bytes 589832 | tf_op jit(solution)/shard_map/ppermute | solution.py:213
  22.2 0.1 collective-permute-start.8
  22.3 0.4 %collective-permute-start.9 = (bf16[96,1024]{1,0:T(8,128)(2,1)S(1)}, bf16[96,1024]{1,0:T(8,128)(2,1)S(1)}, u32[]{:S(2)}, u32[]{:S(2)}) collective-permute-start(bf16[96,1024]{1,0:T(8,128)(2,1)S(1)} %get-tuple-element.28), channel_id=1, source_target_pairs={{0,1},{1,0},{2,3},{3,2},{4,5},{5,4},{6,7},{7,6},{8,9},{9,8},{10,11... | collective-permute-start | bytes 589832 | tf_op jit(solution)/shard_map/ppermute | solution.py:213
  22.7 0.1 collective-permute-start.10
  22.8 0.7 %count.1.refs_8_ = f32[1,384]{1,0:T(1,128)S(1)} custom-call(bf16[64,1024]{1,0:T(8,128)(2,1)S(1)} %pass.1.refs_0_, bf16[64,1024]{1,0:T(8,128)(2,1)S(1)} %collective-permute-done.4.refs_1_, bf16[128,1024]{1,0:T(8,128)(2,1)S(1)} %collective-permute-done.5.refs_2_, bf16[128,1024]{1,0:T(8,128)(2,1)S(1)} %collective-permute-done.6.refs_3_), custom_call_target="tpu_custom_call" | custom-call | tf_op jit(solution)/shard_map/count/pallas_call | solution.py:94
  23.5 0.2 collective-permute-done.8.refs_5_
  23.7 0.3 collective-permute-done.9.refs_6_
  23.9 0.3 collective-permute-done.10.refs_7_
  24.2 0.7 %cross.1.counts_ref = f32[1,384]{1,0:T(1,128)S(1)} custom-call(bf16[64,1024]{1,0:T(8,128)(2,1)S(1)} %pass.1.refs_0_, bf16[64,1024]{1,0:T(8,128)(2,1)S(1)} %collective-permute-done.4.refs_1_, bf16[128,1024]{1,0:T(8,128)(2,1)S(1)} %collective-permute-done.5.refs_2_, bf16[128,1024]{1,0:T(8,128)(2,1)S(1)} %collective-permute-done.6.refs_3_, ...), custom_call_target="tpu_custom_call" | custom-call | tf_op jit(solution)/shard_map/cross/pallas_call | solution.py:94
  24.9 5.2 %collective-permute-done.2.refs_8_.late_ref = bf16[128,1024]{1,0:T(8,128)(2,1)S(1)} collective-permute-done((bf16[128,1024]{1,0:T(8,128)(2,1)S(1)}, bf16[128,1024]{1,0:T(8,128)(2,1)S(1)}, u32[]{:S(2)}, u32[]{:S(2)}) %collective-permute-start.2) | collective-permute-done | bytes 262176 | tf_op jit(solution)/shard_map/ppermute | solution.py:229
  30.0 2.4 %collective-permute-start.11 = (bf16[128,1024]{1,0:T(8,128)(2,1)S(1)}, bf16[128,1024]{1,0:T(8,128)(2,1)S(1)}, u32[]{:S(2)}, u32[]{:S(2)}) collective-permute-start(bf16[128,1024]{1,0:T(8,128)(2,1)S(1)} %collective-permute-done.2.refs_8_.late_ref), channel_id=1, source_target_pairs={{0,1},{1,0},{2,3},{3,2},{4,5},{5,4},{6,7},{7,6},{8,9},{9,8},{10,11... | collective-permute-start | bytes 786440 | tf_op jit(solution)/shard_map/ppermute | solution.py:213
  32.4 1.1 %late.1 = (f32[1,768]{1,0:T(1,128)S(1)}, f32[1,128]{1,0:T(1,128)S(1)}) custom-call(bf16[64,1024]{1,0:T(8,128)(2,1)S(1)} %pass.1.refs_0_, bf16[64,1024]{1,0:T(8,128)(2,1)S(1)} %collective-permute-done.4.refs_1_, bf16[128,1024]{1,0:T(8,128)(2,1)S(1)} %collective-permute-done.5.refs_2_, bf16[128,1024]{1,0:T(8,128)(2,1)S(1)} %collective-permute-done.6.refs_3_, ...), custom_call_target="tpu_custom_call" | custom-call | tf_op jit(solution)/shard_map/late/pallas_call | solution.py:94
  33.6 0.0 collective-permute-done.11.other_ref
  33.6 0.3 finish.1
  33.9 7.9 %all_to_all.5.counts_ref = f32[16,1,64]{2,1,0:T(1,128)S(1)} all-to-all(f32[16,1,64]{2,1,0:T(1,128)S(1)} %finish.1), channel_id=1, replica_groups={{15,14,13,12,11,10,9,8,7,6,5,4,3,2,1,0},{31,30,29,28,27,26,25,24,23,22,..., dimensions={0} | all-to-all | bytes 8192 | tf_op jit(solution)/shard_map/all_to_all | solution.py:314
  41.8 0.7 %select.1 = f32[1,256]{1,0:T(1,128)} custom-call(f32[16,1,64]{2,1,0:T(1,128)S(1)} %all_to_all.5.counts_ref, s32[1,256]{1,0:T(1,128)S(1)} %get-tuple-element.21.refs_2_.slot_ref), custom_call_target="tpu_custom_call" | custom-call | tf_op jit(solution)/shard_map/select/pallas_call | solution.py:94
  (7 shorter events, 0.0 us)
Async XLA Ops:
  0.0 0.7 %copy-start.1 = (s32[256]{0:T(256)S(1)}, s32[256]{0:T(256)}, u32[]{:S(2)}) copy-start(s32[256]{0:T(256)} %param.3) | copy-start | bytes 3076
  0.0 7.3 %collective-permute-start = (bf16[256,1024]{1,0:T(8,128)(2,1)}, bf16[256,1024]{1,0:T(8,128)(2,1)S(1)}, u32[]{:S(2)}, u32[]{:S(2)}) collective-permute-start(bf16[256,1024]{1,0:T(8,128)(2,1)} %refs_0_.3), channel_id=1, source_target_pairs={{0,1},{1,0},{2,3},{3,2},{4,5},{5,4},{6,7},{7,6},{8,9},{9,8},{10,11... | collective-permute-start | bytes 1572872 | tf_op jit(solution)/shard_map/ppermute | solution.py:213
  0.7 6.6 %collective-permute-start.1 = (s32[1,256]{1,0:T(1,128)S(1)}, s32[1,256]{1,0:T(1,128)S(1)}, u32[]{:S(2)}, u32[]{:S(2)}) collective-permute-start(s32[1,256]{1,0:T(1,128)S(1)} %bitcast.2), channel_id=1, source_target_pairs={{0,1},{1,0},{2,3},{3,2},{4,5},{5,4},{6,7},{7,6},{8,9},{9,8},{10,11... | collective-permute-start | bytes 3080 | tf_op jit(solution)/shard_map/ppermute | solution.py:213
  1.1 1.0 %copy-start = (bf16[256,1024]{1,0:T(8,128)(2,1)S(1)}, bf16[256,1024]{1,0:T(8,128)(2,1)}, u32[]{:S(2)}) copy-start(bf16[256,1024]{1,0:T(8,128)(2,1)} %refs_0_.3) | copy-start | bytes 1572868
  2.6 8.5 %collective-permute-start.3 = (bf16[64,1024]{1,0:T(8,128)(2,1)S(1)}, bf16[64,1024]{1,0:T(8,128)(2,1)S(1)}, u32[]{:S(2)}, u32[]{:S(2)}) collective-permute-start(bf16[64,1024]{1,0:T(8,128)(2,1)S(1)} %get-tuple-element.23), channel_id=1, source_target_pairs={{0,12},{1,15},{2,14},{3,13},{4,8},{5,11},{6,10},{7,9},{8,4},{9,7},... | collective-permute-start | bytes 393224 | tf_op jit(solution)/shard_map/ppermute | solution.py:229
  7.9 11.0 %collective-permute-start.5 = (bf16[128,1024]{1,0:T(8,128)(2,1)S(1)}, bf16[128,1024]{1,0:T(8,128)(2,1)S(1)}, u32[]{:S(2)}, u32[]{:S(2)}) collective-permute-start(bf16[128,1024]{1,0:T(8,128)(2,1)S(1)} %get-tuple-element.20), channel_id=1, source_target_pairs={{0,0},{1,3},{2,2},{3,1},{4,4},{5,7},{6,6},{7,5},{8,8},{9,11},{10,1... | collective-permute-start | bytes 786440 | tf_op jit(solution)/shard_map/ppermute | solution.py:229
  8.6 10.4 %collective-permute-start.6 = (bf16[128,1024]{1,0:T(8,128)(2,1)S(1)}, bf16[128,1024]{1,0:T(8,128)(2,1)S(1)}, u32[]{:S(2)}, u32[]{:S(2)}) collective-permute-start(bf16[128,1024]{1,0:T(8,128)(2,1)S(1)} %get-tuple-element.25), channel_id=1, source_target_pairs={{0,4},{1,7},{2,6},{3,5},{4,0},{5,3},{6,2},{7,1},{8,12},{9,15},{10,... | collective-permute-start | bytes 786440 | tf_op jit(solution)/shard_map/ppermute | solution.py:229
  9.3 9.7 %collective-permute-start.4 = (bf16[64,1024]{1,0:T(8,128)(2,1)S(1)}, bf16[64,1024]{1,0:T(8,128)(2,1)S(1)}, u32[]{:S(2)}, u32[]{:S(2)}) collective-permute-start(bf16[64,1024]{1,0:T(8,128)(2,1)S(1)} %get-tuple-element.24), channel_id=1, source_target_pairs={{0,12},{1,15},{2,14},{3,13},{4,8},{5,11},{6,10},{7,9},{8,4},{9,7},... | collective-permute-start | bytes 393224 | tf_op jit(solution)/shard_map/ppermute | solution.py:229
  11.1 18.9 %collective-permute-start.2 = (bf16[128,1024]{1,0:T(8,128)(2,1)S(1)}, bf16[128,1024]{1,0:T(8,128)(2,1)S(1)}, u32[]{:S(2)}, u32[]{:S(2)}) collective-permute-start(bf16[128,1024]{1,0:T(8,128)(2,1)S(1)} %get-tuple-element.22), channel_id=1, source_target_pairs={{0,8},{1,11},{2,10},{3,9},{4,12},{5,15},{6,14},{7,13},{8,0},{9,3},... | collective-permute-start | bytes 786440 | tf_op jit(solution)/shard_map/ppermute | solution.py:229
  19.0 4.5 %collective-permute-start.7 = (bf16[96,1024]{1,0:T(8,128)(2,1)S(1)}, bf16[96,1024]{1,0:T(8,128)(2,1)S(1)}, u32[]{:S(2)}, u32[]{:S(2)}) collective-permute-start(bf16[96,1024]{1,0:T(8,128)(2,1)S(1)} %get-tuple-element.26), channel_id=1, source_target_pairs={{0,1},{1,0},{2,3},{3,2},{4,5},{5,4},{6,7},{7,6},{8,9},{9,8},{10,11... | collective-permute-start | bytes 589832 | tf_op jit(solution)/shard_map/ppermute | solution.py:213
  22.2 1.4 %collective-permute-start.8 = (bf16[96,1024]{1,0:T(8,128)(2,1)S(1)}, bf16[96,1024]{1,0:T(8,128)(2,1)S(1)}, u32[]{:S(2)}, u32[]{:S(2)}) collective-permute-start(bf16[96,1024]{1,0:T(8,128)(2,1)S(1)} %get-tuple-element.27), channel_id=1, source_target_pairs={{0,1},{1,0},{2,3},{3,2},{4,5},{5,4},{6,7},{7,6},{8,9},{9,8},{10,11... | collective-permute-start | bytes 589832 | tf_op jit(solution)/shard_map/ppermute | solution.py:213
  22.3 1.6 %collective-permute-start.9 = (bf16[96,1024]{1,0:T(8,128)(2,1)S(1)}, bf16[96,1024]{1,0:T(8,128)(2,1)S(1)}, u32[]{:S(2)}, u32[]{:S(2)}) collective-permute-start(bf16[96,1024]{1,0:T(8,128)(2,1)S(1)} %get-tuple-element.28), channel_id=1, source_target_pairs={{0,1},{1,0},{2,3},{3,2},{4,5},{5,4},{6,7},{7,6},{8,9},{9,8},{10,11... | collective-permute-start | bytes 589832 | tf_op jit(solution)/shard_map/ppermute | solution.py:213
  22.7 1.5 %collective-permute-start.10 = (bf16[96,1024]{1,0:T(8,128)(2,1)S(1)}, bf16[96,1024]{1,0:T(8,128)(2,1)S(1)}, u32[]{:S(2)}, u32[]{:S(2)}) collective-permute-start(bf16[96,1024]{1,0:T(8,128)(2,1)S(1)} %get-tuple-element.29), channel_id=1, source_target_pairs={{0,1},{1,0},{2,3},{3,2},{4,5},{5,4},{6,7},{7,6},{8,9},{9,8},{10,11... | collective-permute-start | bytes 589832 | tf_op jit(solution)/shard_map/ppermute | solution.py:213
  30.0 3.6 %collective-permute-start.11 = (bf16[128,1024]{1,0:T(8,128)(2,1)S(1)}, bf16[128,1024]{1,0:T(8,128)(2,1)S(1)}, u32[]{:S(2)}, u32[]{:S(2)}) collective-permute-start(bf16[128,1024]{1,0:T(8,128)(2,1)S(1)} %collective-permute-done.2.refs_8_.late_ref), channel_id=1, source_target_pairs={{0,1},{1,0},{2,3},{3,2},{4,5},{5,4},{6,7},{7,6},{8,9},{9,8},{10,11... | collective-permute-start | bytes 786440 | tf_op jit(solution)/shard_map/ppermute | solution.py:213

commit v34 on v32

--- a/solution.py
+++ b/solution.py
@@ -244,7 +244,7 @@
     ids = cluster_id.reshape(1, doc_count)
     other_rows, other_ids = swap_cores(embeddings), swap_cores(ids)
     first, last = steps // 2, steps - 1
-    middle = [p for p in range(steps) if p not in (first, last)]
+    middle = [p for p in reversed(range(steps)) if p not in (first, last)]
     half = jax.ShapeDtypeStruct((capacity, feature_count), jnp.bfloat16)
     whole = jax.ShapeDtypeStruct((cores * capacity, feature_count), jnp.bfloat16)
 

time: 42.1 us -> 42.1 us (level)
  waiting for transfers between devices: 12.1 us -> 5.99 us
  starting transfers between devices: 14 us -> 19.9 us
    ppermute x7, starting transfers between devices: 2.55 us -> 8.74 us  [swap_cores(): return lax.ppermute(x, 'sub', [(i, i ^ 1) for i in range(cores)])]
    ppermute x5, waiting for transfers between devices: 11.2 us -> 5.15 us  [across(): return lax.ppermute(x, ('owner', 'helper', 'sub'), pairs)]
where the time goes in v34:
time: 42.1 us; the launch traced here: 41.9 us
  starting transfers between devices  19.9 us (47%)
  blocking collectives  9.4 us (22%)
  waiting for transfers between devices  5.99 us (14%)
  Pallas kernels  5.26 us (12%)
  local copies, waits for them, and re-layouts  1.27 us (3%)
    ppermute x5, starting transfers between devices, across(): return lax.ppermute(x, ('owner', 'helper', 'sub'), pairs)  11.1 us
    all_to_all x1, blocking collectives, body_by_chip(): lax.all_to_all(counts, ('owner', 'helper', 'sub'), split_axis=0, concat_a...  9.4 us
    ppermute x7, starting transfers between devices, swap_cores(): return lax.ppermute(x, 'sub', [(i, i ^ 1) for i in range(cores)])  8.74 us
    pallas_call x10, Pallas kernels, call_kernel(): pl.pallas_call(kernel, out_shape=out_shape, in_specs=[VMEM] * len(args),...  5.26 us
    ppermute x5, waiting for transfers between devices, across(): return lax.ppermute(x, ('owner', 'helper', 'sub'), pairs)  5.15 us
    unnamed x4, local copies, waits for them, and re-layouts  1.27 us
  transfers between devices with their start and end apart: 12, of which 7 were waited for; matrix products, arithmetic and copies ran while one was open for 0% of the time, Pallas kernels for 10%

profile of v34, /device:TPU:0, one launch (start us, length us, event | category | flops | bytes accessed | tf_op | source)
XLA Modules:
  0.0 41.9 jit_solution(12118309001698215822)
XLA Ops:
  0.0 0.5 %collective-permute-start = (bf16[256,1024]{1,0:T(8,128)(2,1)}, bf16[256,1024]{1,0:T(8,128)(2,1)S(1)}, u32[]{:S(2)}, u32[]{:S(2)}) collective-permute-start(bf16[256,1024]{1,0:T(8,128)(2,1)} %refs_0_.3), channel_id=1, source_target_pairs={{0,1},{1,0},{2,3},{3,2},{4,5},{5,4},{6,7},{7,6},{8,9},{9,8},{10,11... | collective-permute-start | bytes 1572872 | tf_op jit(solution)/shard_map/ppermute | solution.py:226
  0.5 0.2 copy-done.1
  0.7 0.5 %collective-permute-start.1 = (s32[1,256]{1,0:T(1,128)S(1)}, s32[1,256]{1,0:T(1,128)S(1)}, u32[]{:S(2)}, u32[]{:S(2)}) collective-permute-start(s32[1,256]{1,0:T(1,128)S(1)} %bitcast.2), channel_id=1, source_target_pairs={{0,1},{1,0},{2,3},{3,2},{4,5},{5,4},{6,7},{7,6},{8,9},{9,8},{10,11... | collective-permute-start | bytes 3080 | tf_op jit(solution)/shard_map/ppermute | solution.py:226
  1.1 1.0 %copy-done = bf16[256,1024]{1,0:T(8,128)(2,1)S(1)} copy-done((bf16[256,1024]{1,0:T(8,128)(2,1)S(1)}, bf16[256,1024]{1,0:T(8,128)(2,1)}, u32[]{:S(2)}) %copy-start) | copy-done | bytes 524312
  2.2 0.5 %route_first.1 = (bf16[64,1024]{1,0:T(8,128)(2,1)S(1)}, s32[1,256]{1,0:T(1,128)S(1)}) custom-call(bf16[256,1024]{1,0:T(8,128)(2,1)S(1)} %copy-done, s32[1,256]{1,0:T(1,128)S(1)} %bitcast.3), custom_call_target="tpu_custom_call" | custom-call | tf_op jit(solution)/shard_map/route_first/pallas_call | solution.py:106
  2.6 3.7 %collective-permute-start.3 = (bf16[64,1024]{1,0:T(8,128)(2,1)S(1)}, bf16[64,1024]{1,0:T(8,128)(2,1)S(1)}, u32[]{:S(2)}, u32[]{:S(2)}) collective-permute-start(bf16[64,1024]{1,0:T(8,128)(2,1)S(1)} %get-tuple-element.23), channel_id=1, source_target_pairs={{0,8},{1,11},{2,10},{3,9},{4,12},{5,15},{6,14},{7,13},{8,0},{9,3},... | collective-permute-start | bytes 393224 | tf_op jit(solution)/shard_map/ppermute | solution.py:242
  6.3 0.0 collective-permute-done.1.refs_3_
  6.3 0.6 %route_near.1 = (bf16[128,1024]{1,0:T(8,128)(2,1)S(1)}, bf16[128,1024]{1,0:T(8,128)(2,1)S(1)}) custom-call(bf16[256,1024]{1,0:T(8,128)(2,1)S(1)} %copy-done, bf16[256,1024]{1,0:T(8,128)(2,1)S(1)} %collective-permute-done.refs_1_, s32[1,256]{1,0:T(1,128)S(1)} %get-tuple-element.21.refs_2_.slot_ref, s32[1,256]{1,0:T(1,128)S(1)} %collective-permute-done.1.refs_3_), custom_call_target="tpu_custom_call" | custom-call | tf_op jit(solution)/shard_map/route_near/pallas_call | solution.py:106
  6.9 1.6 %collective-permute-start.5 = (bf16[128,1024]{1,0:T(8,128)(2,1)S(1)}, bf16[128,1024]{1,0:T(8,128)(2,1)S(1)}, u32[]{:S(2)}, u32[]{:S(2)}) collective-permute-start(bf16[128,1024]{1,0:T(8,128)(2,1)S(1)} %get-tuple-element.20), channel_id=1, source_target_pairs={{0,4},{1,7},{2,6},{3,5},{4,0},{5,3},{6,2},{7,1},{8,12},{9,15},{10,... | collective-permute-start | bytes 786440 | tf_op jit(solution)/shard_map/ppermute | solution.py:242
  8.6 0.8 %collective-permute-start.6 = (bf16[128,1024]{1,0:T(8,128)(2,1)S(1)}, bf16[128,1024]{1,0:T(8,128)(2,1)S(1)}, u32[]{:S(2)}, u32[]{:S(2)}) collective-permute-start(bf16[128,1024]{1,0:T(8,128)(2,1)S(1)} %get-tuple-element.25), channel_id=1, source_target_pairs={{0,1},{1,2},{2,3},{3,0},{4,5},{5,6},{6,7},{7,4},{8,9},{9,10},{10,1... | collective-permute-start | bytes 786440 | tf_op jit(solution)/shard_map/ppermute | solution.py:242
  9.4 0.6 %route_far.1 = (bf16[64,1024]{1,0:T(8,128)(2,1)S(1)}, bf16[128,1024]{1,0:T(8,128)(2,1)S(1)}) custom-call(bf16[256,1024]{1,0:T(8,128)(2,1)S(1)} %copy-done, bf16[256,1024]{1,0:T(8,128)(2,1)S(1)} %collective-permute-done.refs_1_, s32[1,256]{1,0:T(1,128)S(1)} %get-tuple-element.21.refs_2_.slot_ref, s32[1,256]{1,0:T(1,128)S(1)} %collective-permute-done.1.refs_3_), custom_call_target="tpu_custom_call" | custom-call | flops 10000000000 | tf_op jit(solution)/shard_map/route_far/pallas_call | solution.py:106
  10.0 0.4 collective-permute-start.4
  10.4 2.4 %collective-permute-done.3.refs_0_ = bf16[64,1024]{1,0:T(8,128)(2,1)S(1)} collective-permute-done((bf16[64,1024]{1,0:T(8,128)(2,1)S(1)}, bf16[64,1024]{1,0:T(8,128)(2,1)S(1)}, u32[]{:S(2)}, u32[]{:S(2)}) %collective-permute-start.3) | collective-permute-done | bytes 131104 | tf_op jit(solution)/shard_map/ppermute | solution.py:242
  12.8 4.6 %collective-permute-start.2 = (bf16[128,1024]{1,0:T(8,128)(2,1)S(1)}, bf16[128,1024]{1,0:T(8,128)(2,1)S(1)}, u32[]{:S(2)}, u32[]{:S(2)}) collective-permute-start(bf16[128,1024]{1,0:T(8,128)(2,1)S(1)} %get-tuple-element.22), channel_id=1, source_target_pairs={{0,12},{1,15},{2,14},{3,13},{4,8},{5,11},{6,10},{7,9},{8,4},{9,7},... | collective-permute-start | bytes 786440 | tf_op jit(solution)/shard_map/ppermute | solution.py:242
  17.4 0.9 %collective-permute-done.4.refs_1_ = bf16[64,1024]{1,0:T(8,128)(2,1)S(1)} collective-permute-done((bf16[64,1024]{1,0:T(8,128)(2,1)S(1)}, bf16[64,1024]{1,0:T(8,128)(2,1)S(1)}, u32[]{:S(2)}, u32[]{:S(2)}) %collective-permute-start.4) | collective-permute-done | bytes 131104 | tf_op jit(solution)/shard_map/ppermute | solution.py:242
  18.3 1.8 %collective-permute-done.5.refs_2_ = bf16[128,1024]{1,0:T(8,128)(2,1)S(1)} collective-permute-done((bf16[128,1024]{1,0:T(8,128)(2,1)S(1)}, bf16[128,1024]{1,0:T(8,128)(2,1)S(1)}, u32[]{:S(2)}, u32[]{:S(2)}) %collective-permute-start.5) | collective-permute-done | bytes 262176 | tf_op jit(solution)/shard_map/ppermute | solution.py:242
  20.2 0.1 regroup.1
  20.2 6.9 %collective-permute-start.7 = (bf16[96,1024]{1,0:T(8,128)(2,1)S(1)}, bf16[96,1024]{1,0:T(8,128)(2,1)S(1)}, u32[]{:S(2)}, u32[]{:S(2)}) collective-permute-start(bf16[96,1024]{1,0:T(8,128)(2,1)S(1)} %get-tuple-element.26), channel_id=1, source_target_pairs={{0,1},{1,0},{2,3},{3,2},{4,5},{5,4},{6,7},{7,6},{8,9},{9,8},{10,11... | collective-permute-start | bytes 589832 | tf_op jit(solution)/shard_map/ppermute | solution.py:226
  27.1 0.1 collective-permute-start.8
  27.2 0.4 %collective-permute-start.9 = (bf16[96,1024]{1,0:T(8,128)(2,1)S(1)}, bf16[96,1024]{1,0:T(8,128)(2,1)S(1)}, u32[]{:S(2)}, u32[]{:S(2)}) collective-permute-start(bf16[96,1024]{1,0:T(8,128)(2,1)S(1)} %get-tuple-element.28), channel_id=1, source_target_pairs={{0,1},{1,0},{2,3},{3,2},{4,5},{5,4},{6,7},{7,6},{8,9},{9,8},{10,11... | collective-permute-start | bytes 589832 | tf_op jit(solution)/shard_map/ppermute | solution.py:226
  27.6 0.1 collective-permute-start.10
  27.7 0.7 %count.1.refs_8_ = f32[1,384]{1,0:T(1,128)S(1)} custom-call(bf16[64,1024]{1,0:T(8,128)(2,1)S(1)} %pass.1.refs_0_, bf16[64,1024]{1,0:T(8,128)(2,1)S(1)} %collective-permute-done.4.refs_1_, bf16[128,1024]{1,0:T(8,128)(2,1)S(1)} %collective-permute-done.5.refs_2_, bf16[128,1024]{1,0:T(8,128)(2,1)S(1)} %collective-permute-done.6.refs_3_), custom_call_target="tpu_custom_call" | custom-call | tf_op jit(solution)/shard_map/count/pallas_call | solution.py:106
  28.4 0.2 collective-permute-done.8.refs_5_
  28.6 0.3 collective-permute-done.9.refs_6_
  28.9 0.3 collective-permute-done.10.refs_7_
  29.1 0.7 %cross.1.counts_ref = f32[1,384]{1,0:T(1,128)S(1)} custom-call(bf16[64,1024]{1,0:T(8,128)(2,1)S(1)} %pass.1.refs_0_, bf16[64,1024]{1,0:T(8,128)(2,1)S(1)} %collective-permute-done.4.refs_1_, bf16[128,1024]{1,0:T(8,128)(2,1)S(1)} %collective-permute-done.5.refs_2_, bf16[128,1024]{1,0:T(8,128)(2,1)S(1)} %collective-permute-done.6.refs_3_, ...), custom_call_target="tpu_custom_call" | custom-call | tf_op jit(solution)/shard_map/cross/pallas_call | solution.py:106
  29.8 0.3 collective-permute-start.11
  30.1 1.1 %late.1 = (f32[1,768]{1,0:T(1,128)S(1)}, f32[1,128]{1,0:T(1,128)S(1)}) custom-call(bf16[64,1024]{1,0:T(8,128)(2,1)S(1)} %pass.1.refs_0_, bf16[64,1024]{1,0:T(8,128)(2,1)S(1)} %collective-permute-done.4.refs_1_, bf16[128,1024]{1,0:T(8,128)(2,1)S(1)} %collective-permute-done.5.refs_2_, bf16[128,1024]{1,0:T(8,128)(2,1)S(1)} %collective-permute-done.6.refs_3_, ...), custom_call_target="tpu_custom_call" | custom-call | tf_op jit(solution)/shard_map/late/pallas_call | solution.py:106
  31.3 0.1 collective-permute-done.11.other_ref
  31.4 0.3 finish.1
  31.7 9.4 %all_to_all.5.counts_ref = f32[16,1,64]{2,1,0:T(1,128)S(1)} all-to-all(f32[16,1,64]{2,1,0:T(1,128)S(1)} %finish.1), channel_id=1, replica_groups={{11,10,9,8,7,6,5,4,15,14,13,12,3,2,1,0},{27,26,25,24,23,22,21,20,31,30,..., dimensions={0} | all-to-all | bytes 8192 | tf_op jit(solution)/shard_map/all_to_all | solution.py:328
  41.1 0.7 %select.1 = f32[1,256]{1,0:T(1,128)} custom-call(f32[16,1,64]{2,1,0:T(1,128)S(1)} %all_to_all.5.counts_ref, s32[1,256]{1,0:T(1,128)S(1)} %get-tuple-element.21.refs_2_.slot_ref), custom_call_target="tpu_custom_call" | custom-call | tf_op jit(solution)/shard_map/select/pallas_call | solution.py:106
  (7 shorter events, 0.0 us)
Async XLA Ops:
  0.0 0.7 %copy-start.1 = (s32[256]{0:T(256)S(1)}, s32[256]{0:T(256)}, u32[]{:S(2)}) copy-start(s32[256]{0:T(256)} %param.3) | copy-start | bytes 3076
  0.0 6.3 %collective-permute-start = (bf16[256,1024]{1,0:T(8,128)(2,1)}, bf16[256,1024]{1,0:T(8,128)(2,1)S(1)}, u32[]{:S(2)}, u32[]{:S(2)}) collective-permute-start(bf16[256,1024]{1,0:T(8,128)(2,1)} %refs_0_.3), channel_id=1, source_target_pairs={{0,1},{1,0},{2,3},{3,2},{4,5},{5,4},{6,7},{7,6},{8,9},{9,8},{10,11... | collective-permute-start | bytes 1572872 | tf_op jit(solution)/shard_map/ppermute | solution.py:226
  0.7 5.6 %collective-permute-start.1 = (s32[1,256]{1,0:T(1,128)S(1)}, s32[1,256]{1,0:T(1,128)S(1)}, u32[]{:S(2)}, u32[]{:S(2)}) collective-permute-start(s32[1,256]{1,0:T(1,128)S(1)} %bitcast.2), channel_id=1, source_target_pairs={{0,1},{1,0},{2,3},{3,2},{4,5},{5,4},{6,7},{7,6},{8,9},{9,8},{10,11... | collective-permute-start | bytes 3080 | tf_op jit(solution)/shard_map/ppermute | solution.py:226
  1.1 1.0 %copy-start = (bf16[256,1024]{1,0:T(8,128)(2,1)S(1)}, bf16[256,1024]{1,0:T(8,128)(2,1)}, u32[]{:S(2)}) copy-start(bf16[256,1024]{1,0:T(8,128)(2,1)} %refs_0_.3) | copy-start | bytes 1572868
  2.6 10.2 %collective-permute-start.3 = (bf16[64,1024]{1,0:T(8,128)(2,1)S(1)}, bf16[64,1024]{1,0:T(8,128)(2,1)S(1)}, u32[]{:S(2)}, u32[]{:S(2)}) collective-permute-start(bf16[64,1024]{1,0:T(8,128)(2,1)S(1)} %get-tuple-element.23), channel_id=1, source_target_pairs={{0,8},{1,11},{2,10},{3,9},{4,12},{5,15},{6,14},{7,13},{8,0},{9,3},... | collective-permute-start | bytes 393224 | tf_op jit(solution)/shard_map/ppermute | solution.py:242
  6.9 13.3 %collective-permute-start.5 = (bf16[128,1024]{1,0:T(8,128)(2,1)S(1)}, bf16[128,1024]{1,0:T(8,128)(2,1)S(1)}, u32[]{:S(2)}, u32[]{:S(2)}) collective-permute-start(bf16[128,1024]{1,0:T(8,128)(2,1)S(1)} %get-tuple-element.20), channel_id=1, source_target_pairs={{0,4},{1,7},{2,6},{3,5},{4,0},{5,3},{6,2},{7,1},{8,12},{9,15},{10,... | collective-permute-start | bytes 786440 | tf_op jit(solution)/shard_map/ppermute | solution.py:242
  8.6 9.8 %collective-permute-start.6 = (bf16[128,1024]{1,0:T(8,128)(2,1)S(1)}, bf16[128,1024]{1,0:T(8,128)(2,1)S(1)}, u32[]{:S(2)}, u32[]{:S(2)}) collective-permute-start(bf16[128,1024]{1,0:T(8,128)(2,1)S(1)} %get-tuple-element.25), channel_id=1, source_target_pairs={{0,1},{1,2},{2,3},{3,0},{4,5},{5,6},{6,7},{7,4},{8,9},{9,10},{10,1... | collective-permute-start | bytes 786440 | tf_op jit(solution)/shard_map/ppermute | solution.py:242
  10.0 8.3 %collective-permute-start.4 = (bf16[64,1024]{1,0:T(8,128)(2,1)S(1)}, bf16[64,1024]{1,0:T(8,128)(2,1)S(1)}, u32[]{:S(2)}, u32[]{:S(2)}) collective-permute-start(bf16[64,1024]{1,0:T(8,128)(2,1)S(1)} %get-tuple-element.24), channel_id=1, source_target_pairs={{0,8},{1,11},{2,10},{3,9},{4,12},{5,15},{6,14},{7,13},{8,0},{9,3},... | collective-permute-start | bytes 393224 | tf_op jit(solution)/shard_map/ppermute | solution.py:242
  12.8 17.0 %collective-permute-start.2 = (bf16[128,1024]{1,0:T(8,128)(2,1)S(1)}, bf16[128,1024]{1,0:T(8,128)(2,1)S(1)}, u32[]{:S(2)}, u32[]{:S(2)}) collective-permute-start(bf16[128,1024]{1,0:T(8,128)(2,1)S(1)} %get-tuple-element.22), channel_id=1, source_target_pairs={{0,12},{1,15},{2,14},{3,13},{4,8},{5,11},{6,10},{7,9},{8,4},{9,7},... | collective-permute-start | bytes 786440 | tf_op jit(solution)/shard_map/ppermute | solution.py:242
  20.2 8.2 %collective-permute-start.7 = (bf16[96,1024]{1,0:T(8,128)(2,1)S(1)}, bf16[96,1024]{1,0:T(8,128)(2,1)S(1)}, u32[]{:S(2)}, u32[]{:S(2)}) collective-permute-start(bf16[96,1024]{1,0:T(8,128)(2,1)S(1)} %get-tuple-element.26), channel_id=1, source_target_pairs={{0,1},{1,0},{2,3},{3,2},{4,5},{5,4},{6,7},{7,6},{8,9},{9,8},{10,11... | collective-permute-start | bytes 589832 | tf_op jit(solution)/shard_map/ppermute | solution.py:226
  27.1 1.4 %collective-permute-start.8 = (bf16[96,1024]{1,0:T(8,128)(2,1)S(1)}, bf16[96,1024]{1,0:T(8,128)(2,1)S(1)}, u32[]{:S(2)}, u32[]{:S(2)}) collective-permute-start(bf16[96,1024]{1,0:T(8,128)(2,1)S(1)} %get-tuple-element.27), channel_id=1, source_target_pairs={{0,1},{1,0},{2,3},{3,2},{4,5},{5,4},{6,7},{7,6},{8,9},{9,8},{10,11... | collective-permute-start | bytes 589832 | tf_op jit(solution)/shard_map/ppermute | solution.py:226
  27.2 1.6 %collective-permute-start.9 = (bf16[96,1024]{1,0:T(8,128)(2,1)S(1)}, bf16[96,1024]{1,0:T(8,128)(2,1)S(1)}, u32[]{:S(2)}, u32[]{:S(2)}) collective-permute-start(bf16[96,1024]{1,0:T(8,128)(2,1)S(1)} %get-tuple-element.28), channel_id=1, source_target_pairs={{0,1},{1,0},{2,3},{3,2},{4,5},{5,4},{6,7},{7,6},{8,9},{9,8},{10,11... | collective-permute-start | bytes 589832 | tf_op jit(solution)/shard_map/ppermute | solution.py:226
  27.6 1.5 %collective-permute-start.10 = (bf16[96,1024]{1,0:T(8,128)(2,1)S(1)}, bf16[96,1024]{1,0:T(8,128)(2,1)S(1)}, u32[]{:S(2)}, u32[]{:S(2)}) collective-permute-start(bf16[96,1024]{1,0:T(8,128)(2,1)S(1)} %get-tuple-element.29), channel_id=1, source_target_pairs={{0,1},{1,0},{2,3},{3,2},{4,5},{5,4},{6,7},{7,6},{8,9},{9,8},{10,11... | collective-permute-start | bytes 589832 | tf_op jit(solution)/shard_map/ppermute | solution.py:226
  29.8 1.6 %collective-permute-start.11 = (bf16[128,1024]{1,0:T(8,128)(2,1)S(1)}, bf16[128,1024]{1,0:T(8,128)(2,1)S(1)}, u32[]{:S(2)}, u32[]{:S(2)}) collective-permute-start(bf16[128,1024]{1,0:T(8,128)(2,1)S(1)} %collective-permute-done.2.refs_8_.late_ref), channel_id=1, source_target_pairs={{0,1},{1,0},{2,3},{3,2},{4,5},{5,4},{6,7},{7,6},{8,9},{9,8},{10,11... | collective-permute-start | bytes 786440 | tf_op jit(solution)/shard_map/ppermute | solution.py:226

commit v35 on v30

--- a/solution.py
+++ b/solution.py
@@ -203,15 +203,14 @@
     block = slot // capacity
     rank = slot - block * capacity
     hot = (lax.broadcasted_iota(jnp.int32, (capacity, doc_count), 0) == rank).astype(jnp.float32)
+    parts = counts.shape[0] // clusters
+    counts = jnp.sum(counts.reshape(clusters, parts, capacity), axis=1)
     by_block = jnp.dot(
         counts, hot, precision=lax.Precision.HIGHEST, preferred_element_type=jnp.float32
     )
-    parts = counts.shape[0] // clusters
-    row = lax.broadcasted_iota(jnp.int32, by_block.shape, 0)
     if backwards:
-        chosen = row // parts == place_of(block * parts) // parts
-    else:
-        chosen = row // parts == block
+        block = place_of(block * parts) // parts
+    chosen = lax.broadcasted_iota(jnp.int32, by_block.shape, 0) == block
     out_ref[...] = jnp.sum(jnp.where(chosen, by_block, 0.0), axis=0, keepdims=True)
 
 

time: 42.1 us -> 42.1 us (level)
  no operation moved by 1% of the time
where the time goes in v35:
time: 42.1 us; the launch traced here: 41.9 us
  starting transfers between devices  21.7 us (52%)
  blocking collectives  8.26 us (20%)
  waiting for transfers between devices  5.31 us (13%)
  Pallas kernels  5.27 us (13%)
  local copies, waits for them, and re-layouts  1.27 us (3%)
    ppermute x5, starting transfers between devices, across(): return lax.ppermute(x, ('owner', 'helper', 'sub'), pairs)  11 us
    ppermute x7, starting transfers between devices, swap_cores(): return lax.ppermute(x, 'sub', [(i, i ^ 1) for i in range(cores)])  10.7 us
    all_to_all x1, blocking collectives, body_by_chip(): lax.all_to_all(counts, ('owner', 'helper', 'sub'), split_axis=0, concat_a...  8.26 us
    pallas_call x10, Pallas kernels, call_kernel(): pl.pallas_call(kernel, out_shape=out_shape, in_specs=[VMEM] * len(args),...  5.27 us
    ppermute x5, waiting for transfers between devices, across(): return lax.ppermute(x, ('owner', 'helper', 'sub'), pairs)  4.48 us
    unnamed x4, local copies, waits for them, and re-layouts  1.27 us
  transfers between devices with their start and end apart: 12, of which 6 were waited for; matrix products, arithmetic and copies ran while one was open for 0% of the time, Pallas kernels for 10%

profile of v35, /device:TPU:0, one launch (start us, length us, event | category | flops | bytes accessed | tf_op | source)
XLA Modules:
  0.0 41.9 jit_solution(14216672494699587986)
XLA Ops:
  0.0 0.5 %collective-permute-start = (bf16[256,1024]{1,0:T(8,128)(2,1)}, bf16[256,1024]{1,0:T(8,128)(2,1)S(1)}, u32[]{:S(2)}, u32[]{:S(2)}) collective-permute-start(bf16[256,1024]{1,0:T(8,128)(2,1)} %refs_0_.3), channel_id=1, source_target_pairs={{0,1},{1,0},{2,3},{3,2},{4,5},{5,4},{6,7},{7,6},{8,9},{9,8},{10,11... | collective-permute-start | bytes 1572872 | tf_op jit(solution)/shard_map/ppermute | solution.py:225
  0.5 0.2 copy-done.1
  0.7 0.5 %collective-permute-start.1 = (s32[1,256]{1,0:T(1,128)S(1)}, s32[1,256]{1,0:T(1,128)S(1)}, u32[]{:S(2)}, u32[]{:S(2)}) collective-permute-start(s32[1,256]{1,0:T(1,128)S(1)} %bitcast.2), channel_id=1, source_target_pairs={{0,1},{1,0},{2,3},{3,2},{4,5},{5,4},{6,7},{7,6},{8,9},{9,8},{10,11... | collective-permute-start | bytes 3080 | tf_op jit(solution)/shard_map/ppermute | solution.py:225
  1.1 1.0 %copy-done = bf16[256,1024]{1,0:T(8,128)(2,1)S(1)} copy-done((bf16[256,1024]{1,0:T(8,128)(2,1)S(1)}, bf16[256,1024]{1,0:T(8,128)(2,1)}, u32[]{:S(2)}) %copy-start) | copy-done | bytes 524312
  2.2 0.5 %route_first.1 = (bf16[64,1024]{1,0:T(8,128)(2,1)S(1)}, s32[1,256]{1,0:T(1,128)S(1)}) custom-call(bf16[256,1024]{1,0:T(8,128)(2,1)S(1)} %copy-done, s32[1,256]{1,0:T(1,128)S(1)} %bitcast.3), custom_call_target="tpu_custom_call" | custom-call | tf_op jit(solution)/shard_map/route_first/pallas_call | solution.py:106
  2.6 3.7 %collective-permute-start.3 = (bf16[64,1024]{1,0:T(8,128)(2,1)S(1)}, bf16[64,1024]{1,0:T(8,128)(2,1)S(1)}, u32[]{:S(2)}, u32[]{:S(2)}) collective-permute-start(bf16[64,1024]{1,0:T(8,128)(2,1)S(1)} %get-tuple-element.23), channel_id=1, source_target_pairs={{0,8},{1,11},{2,10},{3,9},{4,12},{5,15},{6,14},{7,13},{8,0},{9,3},... | collective-permute-start | bytes 393224 | tf_op jit(solution)/shard_map/ppermute | solution.py:241
  6.3 0.6 %route_near.1 = (bf16[128,1024]{1,0:T(8,128)(2,1)S(1)}, bf16[128,1024]{1,0:T(8,128)(2,1)S(1)}) custom-call(bf16[256,1024]{1,0:T(8,128)(2,1)S(1)} %copy-done, bf16[256,1024]{1,0:T(8,128)(2,1)S(1)} %collective-permute-done.refs_1_, s32[1,256]{1,0:T(1,128)S(1)} %get-tuple-element.21.refs_2_.slot_ref, s32[1,256]{1,0:T(1,128)S(1)} %collective-permute-done.1.refs_3_), custom_call_target="tpu_custom_call" | custom-call | tf_op jit(solution)/shard_map/route_near/pallas_call | solution.py:106
  6.9 0.7 %collective-permute-start.5 = (bf16[128,1024]{1,0:T(8,128)(2,1)S(1)}, bf16[128,1024]{1,0:T(8,128)(2,1)S(1)}, u32[]{:S(2)}, u32[]{:S(2)}) collective-permute-start(bf16[128,1024]{1,0:T(8,128)(2,1)S(1)} %get-tuple-element.20), channel_id=1, source_target_pairs={{0,0},{1,3},{2,2},{3,1},{4,4},{5,7},{6,6},{7,5},{8,8},{9,11},{10,1... | collective-permute-start | bytes 786440 | tf_op jit(solution)/shard_map/ppermute | solution.py:241
  7.6 1.6 %collective-permute-start.6 = (bf16[128,1024]{1,0:T(8,128)(2,1)S(1)}, bf16[128,1024]{1,0:T(8,128)(2,1)S(1)}, u32[]{:S(2)}, u32[]{:S(2)}) collective-permute-start(bf16[128,1024]{1,0:T(8,128)(2,1)S(1)} %get-tuple-element.25), channel_id=1, source_target_pairs={{0,4},{1,7},{2,6},{3,5},{4,0},{5,3},{6,2},{7,1},{8,12},{9,15},{10,... | collective-permute-start | bytes 786440 | tf_op jit(solution)/shard_map/ppermute | solution.py:241
  9.2 0.6 %route_far.1 = (bf16[64,1024]{1,0:T(8,128)(2,1)S(1)}, bf16[128,1024]{1,0:T(8,128)(2,1)S(1)}) custom-call(bf16[256,1024]{1,0:T(8,128)(2,1)S(1)} %copy-done, bf16[256,1024]{1,0:T(8,128)(2,1)S(1)} %collective-permute-done.refs_1_, s32[1,256]{1,0:T(1,128)S(1)} %get-tuple-element.21.refs_2_.slot_ref, s32[1,256]{1,0:T(1,128)S(1)} %collective-permute-done.1.refs_3_), custom_call_target="tpu_custom_call" | custom-call | flops 10000000000 | tf_op jit(solution)/shard_map/route_far/pallas_call | solution.py:106
  9.8 0.4 collective-permute-start.4
  10.2 2.6 %collective-permute-done.3.refs_0_ = bf16[64,1024]{1,0:T(8,128)(2,1)S(1)} collective-permute-done((bf16[64,1024]{1,0:T(8,128)(2,1)S(1)}, bf16[64,1024]{1,0:T(8,128)(2,1)S(1)}, u32[]{:S(2)}, u32[]{:S(2)}) %collective-permute-start.3) | collective-permute-done | bytes 131104 | tf_op jit(solution)/shard_map/ppermute | solution.py:241
  12.8 4.6 %collective-permute-start.2 = (bf16[128,1024]{1,0:T(8,128)(2,1)S(1)}, bf16[128,1024]{1,0:T(8,128)(2,1)S(1)}, u32[]{:S(2)}, u32[]{:S(2)}) collective-permute-start(bf16[128,1024]{1,0:T(8,128)(2,1)S(1)} %get-tuple-element.22), channel_id=1, source_target_pairs={{0,12},{1,15},{2,14},{3,13},{4,8},{5,11},{6,10},{7,9},{8,4},{9,7},... | collective-permute-start | bytes 786440 | tf_op jit(solution)/shard_map/ppermute | solution.py:241
  17.4 1.9 %collective-permute-done.6.refs_3_ = bf16[128,1024]{1,0:T(8,128)(2,1)S(1)} collective-permute-done((bf16[128,1024]{1,0:T(8,128)(2,1)S(1)}, bf16[128,1024]{1,0:T(8,128)(2,1)S(1)}, u32[]{:S(2)}, u32[]{:S(2)}) %collective-permute-start.6) | collective-permute-done | bytes 262176 | tf_op jit(solution)/shard_map/ppermute | solution.py:241
  19.3 0.0 collective-permute-done.5.refs_2_
  19.3 0.1 regroup.1
  19.4 8.9 %collective-permute-start.7 = (bf16[96,1024]{1,0:T(8,128)(2,1)S(1)}, bf16[96,1024]{1,0:T(8,128)(2,1)S(1)}, u32[]{:S(2)}, u32[]{:S(2)}) collective-permute-start(bf16[96,1024]{1,0:T(8,128)(2,1)S(1)} %get-tuple-element.26), channel_id=1, source_target_pairs={{0,1},{1,0},{2,3},{3,2},{4,5},{5,4},{6,7},{7,6},{8,9},{9,8},{10,11... | collective-permute-start | bytes 589832 | tf_op jit(solution)/shard_map/ppermute | solution.py:225
  28.3 0.1 collective-permute-start.8
  28.3 0.4 %collective-permute-start.9 = (bf16[96,1024]{1,0:T(8,128)(2,1)S(1)}, bf16[96,1024]{1,0:T(8,128)(2,1)S(1)}, u32[]{:S(2)}, u32[]{:S(2)}) collective-permute-start(bf16[96,1024]{1,0:T(8,128)(2,1)S(1)} %get-tuple-element.28), channel_id=1, source_target_pairs={{0,1},{1,0},{2,3},{3,2},{4,5},{5,4},{6,7},{7,6},{8,9},{9,8},{10,11... | collective-permute-start | bytes 589832 | tf_op jit(solution)/shard_map/ppermute | solution.py:225
  28.8 0.1 collective-permute-start.10
  28.8 0.7 %count.1.refs_8_ = f32[1,384]{1,0:T(1,128)S(1)} custom-call(bf16[64,1024]{1,0:T(8,128)(2,1)S(1)} %pass.1.refs_0_, bf16[64,1024]{1,0:T(8,128)(2,1)S(1)} %collective-permute-done.4.refs_1_, bf16[128,1024]{1,0:T(8,128)(2,1)S(1)} %collective-permute-done.5.refs_2_, bf16[128,1024]{1,0:T(8,128)(2,1)S(1)} %collective-permute-done.6.refs_3_), custom_call_target="tpu_custom_call" | custom-call | tf_op jit(solution)/shard_map/count/pallas_call | solution.py:106
  29.5 0.0 collective-permute-done.7.refs_4_
  29.5 0.2 collective-permute-done.8.refs_5_
  29.7 0.3 collective-permute-done.9.refs_6_
  30.0 0.3 collective-permute-done.10.refs_7_
  30.3 0.7 %cross.1.counts_ref = f32[1,384]{1,0:T(1,128)S(1)} custom-call(bf16[64,1024]{1,0:T(8,128)(2,1)S(1)} %pass.1.refs_0_, bf16[64,1024]{1,0:T(8,128)(2,1)S(1)} %collective-permute-done.4.refs_1_, bf16[128,1024]{1,0:T(8,128)(2,1)S(1)} %collective-permute-done.5.refs_2_, bf16[128,1024]{1,0:T(8,128)(2,1)S(1)} %collective-permute-done.6.refs_3_, ...), custom_call_target="tpu_custom_call" | custom-call | tf_op jit(solution)/shard_map/cross/pallas_call | solution.py:106
  30.9 0.3 collective-permute-start.11
  31.3 1.1 %late.1 = (f32[1,768]{1,0:T(1,128)S(1)}, f32[1,128]{1,0:T(1,128)S(1)}) custom-call(bf16[64,1024]{1,0:T(8,128)(2,1)S(1)} %pass.1.refs_0_, bf16[64,1024]{1,0:T(8,128)(2,1)S(1)} %collective-permute-done.4.refs_1_, bf16[128,1024]{1,0:T(8,128)(2,1)S(1)} %collective-permute-done.5.refs_2_, bf16[128,1024]{1,0:T(8,128)(2,1)S(1)} %collective-permute-done.6.refs_3_, ...), custom_call_target="tpu_custom_call" | custom-call | tf_op jit(solution)/shard_map/late/pallas_call | solution.py:106
  32.4 0.1 collective-permute-done.11.other_ref
  32.5 0.3 finish.1
  32.9 8.3 %all_to_all.5.counts_ref = f32[16,1,64]{2,1,0:T(1,128)S(1)} all-to-all(f32[16,1,64]{2,1,0:T(1,128)S(1)} %finish.1), channel_id=1, replica_groups={{11,10,9,8,7,6,5,4,15,14,13,12,3,2,1,0},{27,26,25,24,23,22,21,20,31,30,..., dimensions={0} | all-to-all | bytes 8192 | tf_op jit(solution)/shard_map/all_to_all | solution.py:326
  41.1 0.7 %select.1 = f32[1,256]{1,0:T(1,128)} custom-call(f32[16,1,64]{2,1,0:T(1,128)S(1)} %all_to_all.5.counts_ref, s32[1,256]{1,0:T(1,128)S(1)} %get-tuple-element.21.refs_2_.slot_ref), custom_call_target="tpu_custom_call" | custom-call | tf_op jit(solution)/shard_map/select/pallas_call | solution.py:106
  (7 shorter events, 0.0 us)
Async XLA Ops:
  0.0 0.7 %copy-start.1 = (s32[256]{0:T(256)S(1)}, s32[256]{0:T(256)}, u32[]{:S(2)}) copy-start(s32[256]{0:T(256)} %param.3) | copy-start | bytes 3076
  0.0 6.3 %collective-permute-start = (bf16[256,1024]{1,0:T(8,128)(2,1)}, bf16[256,1024]{1,0:T(8,128)(2,1)S(1)}, u32[]{:S(2)}, u32[]{:S(2)}) collective-permute-start(bf16[256,1024]{1,0:T(8,128)(2,1)} %refs_0_.3), channel_id=1, source_target_pairs={{0,1},{1,0},{2,3},{3,2},{4,5},{5,4},{6,7},{7,6},{8,9},{9,8},{10,11... | collective-permute-start | bytes 1572872 | tf_op jit(solution)/shard_map/ppermute | solution.py:225
  0.7 5.6 %collective-permute-start.1 = (s32[1,256]{1,0:T(1,128)S(1)}, s32[1,256]{1,0:T(1,128)S(1)}, u32[]{:S(2)}, u32[]{:S(2)}) collective-permute-start(s32[1,256]{1,0:T(1,128)S(1)} %bitcast.2), channel_id=1, source_target_pairs={{0,1},{1,0},{2,3},{3,2},{4,5},{5,4},{6,7},{7,6},{8,9},{9,8},{10,11... | collective-permute-start | bytes 3080 | tf_op jit(solution)/shard_map/ppermute | solution.py:225
  1.1 1.0 %copy-start = (bf16[256,1024]{1,0:T(8,128)(2,1)S(1)}, bf16[256,1024]{1,0:T(8,128)(2,1)}, u32[]{:S(2)}) copy-start(bf16[256,1024]{1,0:T(8,128)(2,1)} %refs_0_.3) | copy-start | bytes 1572868
  2.6 10.2 %collective-permute-start.3 = (bf16[64,1024]{1,0:T(8,128)(2,1)S(1)}, bf16[64,1024]{1,0:T(8,128)(2,1)S(1)}, u32[]{:S(2)}, u32[]{:S(2)}) collective-permute-start(bf16[64,1024]{1,0:T(8,128)(2,1)S(1)} %get-tuple-element.23), channel_id=1, source_target_pairs={{0,8},{1,11},{2,10},{3,9},{4,12},{5,15},{6,14},{7,13},{8,0},{9,3},... | collective-permute-start | bytes 393224 | tf_op jit(solution)/shard_map/ppermute | solution.py:241
  6.9 12.4 %collective-permute-start.5 = (bf16[128,1024]{1,0:T(8,128)(2,1)S(1)}, bf16[128,1024]{1,0:T(8,128)(2,1)S(1)}, u32[]{:S(2)}, u32[]{:S(2)}) collective-permute-start(bf16[128,1024]{1,0:T(8,128)(2,1)S(1)} %get-tuple-element.20), channel_id=1, source_target_pairs={{0,0},{1,3},{2,2},{3,1},{4,4},{5,7},{6,6},{7,5},{8,8},{9,11},{10,1... | collective-permute-start | bytes 786440 | tf_op jit(solution)/shard_map/ppermute | solution.py:241
  7.6 11.7 %collective-permute-start.6 = (bf16[128,1024]{1,0:T(8,128)(2,1)S(1)}, bf16[128,1024]{1,0:T(8,128)(2,1)S(1)}, u32[]{:S(2)}, u32[]{:S(2)}) collective-permute-start(bf16[128,1024]{1,0:T(8,128)(2,1)S(1)} %get-tuple-element.25), channel_id=1, source_target_pairs={{0,4},{1,7},{2,6},{3,5},{4,0},{5,3},{6,2},{7,1},{8,12},{9,15},{10,... | collective-permute-start | bytes 786440 | tf_op jit(solution)/shard_map/ppermute | solution.py:241
  9.8 7.6 %collective-permute-start.4 = (bf16[64,1024]{1,0:T(8,128)(2,1)S(1)}, bf16[64,1024]{1,0:T(8,128)(2,1)S(1)}, u32[]{:S(2)}, u32[]{:S(2)}) collective-permute-start(bf16[64,1024]{1,0:T(8,128)(2,1)S(1)} %get-tuple-element.24), channel_id=1, source_target_pairs={{0,8},{1,11},{2,10},{3,9},{4,12},{5,15},{6,14},{7,13},{8,0},{9,3},... | collective-permute-start | bytes 393224 | tf_op jit(solution)/shard_map/ppermute | solution.py:241
  12.8 18.1 %collective-permute-start.2 = (bf16[128,1024]{1,0:T(8,128)(2,1)S(1)}, bf16[128,1024]{1,0:T(8,128)(2,1)S(1)}, u32[]{:S(2)}, u32[]{:S(2)}) collective-permute-start(bf16[128,1024]{1,0:T(8,128)(2,1)S(1)} %get-tuple-element.22), channel_id=1, source_target_pairs={{0,12},{1,15},{2,14},{3,13},{4,8},{5,11},{6,10},{7,9},{8,4},{9,7},... | collective-permute-start | bytes 786440 | tf_op jit(solution)/shard_map/ppermute | solution.py:241
  19.4 10.1 %collective-permute-start.7 = (bf16[96,1024]{1,0:T(8,128)(2,1)S(1)}, bf16[96,1024]{1,0:T(8,128)(2,1)S(1)}, u32[]{:S(2)}, u32[]{:S(2)}) collective-permute-start(bf16[96,1024]{1,0:T(8,128)(2,1)S(1)} %get-tuple-element.26), channel_id=1, source_target_pairs={{0,1},{1,0},{2,3},{3,2},{4,5},{5,4},{6,7},{7,6},{8,9},{9,8},{10,11... | collective-permute-start | bytes 589832 | tf_op jit(solution)/shard_map/ppermute | solution.py:225
  28.3 1.4 %collective-permute-start.8 = (bf16[96,1024]{1,0:T(8,128)(2,1)S(1)}, bf16[96,1024]{1,0:T(8,128)(2,1)S(1)}, u32[]{:S(2)}, u32[]{:S(2)}) collective-permute-start(bf16[96,1024]{1,0:T(8,128)(2,1)S(1)} %get-tuple-element.27), channel_id=1, source_target_pairs={{0,1},{1,0},{2,3},{3,2},{4,5},{5,4},{6,7},{7,6},{8,9},{9,8},{10,11... | collective-permute-start | bytes 589832 | tf_op jit(solution)/shard_map/ppermute | solution.py:225
  28.3 1.6 %collective-permute-start.9 = (bf16[96,1024]{1,0:T(8,128)(2,1)S(1)}, bf16[96,1024]{1,0:T(8,128)(2,1)S(1)}, u32[]{:S(2)}, u32[]{:S(2)}) collective-permute-start(bf16[96,1024]{1,0:T(8,128)(2,1)S(1)} %get-tuple-element.28), channel_id=1, source_target_pairs={{0,1},{1,0},{2,3},{3,2},{4,5},{5,4},{6,7},{7,6},{8,9},{9,8},{10,11... | collective-permute-start | bytes 589832 | tf_op jit(solution)/shard_map/ppermute | solution.py:225
  28.8 1.5 %collective-permute-start.10 = (bf16[96,1024]{1,0:T(8,128)(2,1)S(1)}, bf16[96,1024]{1,0:T(8,128)(2,1)S(1)}, u32[]{:S(2)}, u32[]{:S(2)}) collective-permute-start(bf16[96,1024]{1,0:T(8,128)(2,1)S(1)} %get-tuple-element.29), channel_id=1, source_target_pairs={{0,1},{1,0},{2,3},{3,2},{4,5},{5,4},{6,7},{7,6},{8,9},{9,8},{10,11... | collective-permute-start | bytes 589832 | tf_op jit(solution)/shard_map/ppermute | solution.py:225
  30.9 1.6 %collective-permute-start.11 = (bf16[128,1024]{1,0:T(8,128)(2,1)S(1)}, bf16[128,1024]{1,0:T(8,128)(2,1)S(1)}, u32[]{:S(2)}, u32[]{:S(2)}) collective-permute-start(bf16[128,1024]{1,0:T(8,128)(2,1)S(1)} %collective-permute-done.2.refs_8_.late_ref), channel_id=1, source_target_pairs={{0,1},{1,0},{2,3},{3,2},{4,5},{5,4},{6,7},{7,6},{8,9},{9,8},{10,11... | collective-permute-start | bytes 786440 | tf_op jit(solution)/shard_map/ppermute | solution.py:225

commit v36 on v32

--- a/solution.py
+++ b/solution.py
@@ -26,7 +26,7 @@
 def place_of(device):
     last = CL_OWN * 2 - 1
     owner, rest = device // (last + 1), device % (last + 1)
-    places = (3, 1, 0, 2)
+    places = (3, 2, 1, 0)
     if isinstance(device, int):
         return places[owner] * (last + 1) + last - rest
     place = jnp.full_like(owner, places[0])

time: 42.1 us -> 41.6 us (0.988)
  blocking collectives: 9.2 us -> 8.71 us
    all_to_all x1, blocking collectives: 9.2 us -> 8.71 us  [body_by_chip(): lax.all_to_all(counts, ('owner', 'helper', 'sub'), split_axis=0, concat_a...]
where the time goes in v36:
time: 41.6 us; the launch traced here: 41.4 us
  starting transfers between devices  14 us (34%)
  waiting for transfers between devices  12.1 us (29%)
  blocking collectives  8.71 us (21%)
  Pallas kernels  5.27 us (13%)
  local copies, waits for them, and re-layouts  1.27 us (3%)
    ppermute x5, starting transfers between devices, across(): return lax.ppermute(x, ('owner', 'helper', 'sub'), pairs)  11.4 us
    ppermute x5, waiting for transfers between devices, across(): return lax.ppermute(x, ('owner', 'helper', 'sub'), pairs)  11.2 us
    all_to_all x1, blocking collectives, body_by_chip(): lax.all_to_all(counts, ('owner', 'helper', 'sub'), split_axis=0, concat_a...  8.71 us
    pallas_call x10, Pallas kernels, call_kernel(): pl.pallas_call(kernel, out_shape=out_shape, in_specs=[VMEM] * len(args),...  5.27 us
    ppermute x7, starting transfers between devices, swap_cores(): return lax.ppermute(x, 'sub', [(i, i ^ 1) for i in range(cores)])  2.55 us
    unnamed x4, local copies, waits for them, and re-layouts  1.27 us
  transfers between devices with their start and end apart: 12, of which 7 were waited for; matrix products, arithmetic and copies ran while one was open for 0% of the time, Pallas kernels for 10%

profile of v36, /device:TPU:0, one launch (start us, length us, event | category | flops | bytes accessed | tf_op | source)
XLA Modules:
  0.0 41.4 jit_solution(13939858166084504116)
XLA Ops:
  0.0 0.5 %collective-permute-start = (bf16[256,1024]{1,0:T(8,128)(2,1)}, bf16[256,1024]{1,0:T(8,128)(2,1)S(1)}, u32[]{:S(2)}, u32[]{:S(2)}) collective-permute-start(bf16[256,1024]{1,0:T(8,128)(2,1)} %refs_0_.3), channel_id=1, source_target_pairs={{0,1},{1,0},{2,3},{3,2},{4,5},{5,4},{6,7},{7,6},{8,9},{9,8},{10,11... | collective-permute-start | bytes 1572872 | tf_op jit(solution)/shard_map/ppermute | solution.py:226
  0.5 0.2 copy-done.1
  0.7 0.5 %collective-permute-start.1 = (s32[1,256]{1,0:T(1,128)S(1)}, s32[1,256]{1,0:T(1,128)S(1)}, u32[]{:S(2)}, u32[]{:S(2)}) collective-permute-start(s32[1,256]{1,0:T(1,128)S(1)} %bitcast.2), channel_id=1, source_target_pairs={{0,1},{1,0},{2,3},{3,2},{4,5},{5,4},{6,7},{7,6},{8,9},{9,8},{10,11... | collective-permute-start | bytes 3080 | tf_op jit(solution)/shard_map/ppermute | solution.py:226
  1.1 1.0 %copy-done = bf16[256,1024]{1,0:T(8,128)(2,1)S(1)} copy-done((bf16[256,1024]{1,0:T(8,128)(2,1)S(1)}, bf16[256,1024]{1,0:T(8,128)(2,1)}, u32[]{:S(2)}) %copy-start) | copy-done | bytes 524312
  2.2 0.5 %route_first.1 = (bf16[64,1024]{1,0:T(8,128)(2,1)S(1)}, s32[1,256]{1,0:T(1,128)S(1)}) custom-call(bf16[256,1024]{1,0:T(8,128)(2,1)S(1)} %copy-done, s32[1,256]{1,0:T(1,128)S(1)} %bitcast.3), custom_call_target="tpu_custom_call" | custom-call | tf_op jit(solution)/shard_map/route_first/pallas_call | solution.py:106
  2.6 3.7 %collective-permute-start.3 = (bf16[64,1024]{1,0:T(8,128)(2,1)S(1)}, bf16[64,1024]{1,0:T(8,128)(2,1)S(1)}, u32[]{:S(2)}, u32[]{:S(2)}) collective-permute-start(bf16[64,1024]{1,0:T(8,128)(2,1)S(1)} %get-tuple-element.23), channel_id=1, source_target_pairs={{0,8},{1,11},{2,10},{3,9},{4,12},{5,15},{6,14},{7,13},{8,0},{9,3},... | collective-permute-start | bytes 393224 | tf_op jit(solution)/shard_map/ppermute | solution.py:242
  6.3 0.6 %route_near.1 = (bf16[128,1024]{1,0:T(8,128)(2,1)S(1)}, bf16[128,1024]{1,0:T(8,128)(2,1)S(1)}) custom-call(bf16[256,1024]{1,0:T(8,128)(2,1)S(1)} %copy-done, bf16[256,1024]{1,0:T(8,128)(2,1)S(1)} %collective-permute-done.refs_1_, s32[1,256]{1,0:T(1,128)S(1)} %get-tuple-element.21.refs_2_.slot_ref, s32[1,256]{1,0:T(1,128)S(1)} %collective-permute-done.1.refs_3_), custom_call_target="tpu_custom_call" | custom-call | tf_op jit(solution)/shard_map/route_near/pallas_call | solution.py:106
  6.9 1.2 %collective-permute-start.5 = (bf16[128,1024]{1,0:T(8,128)(2,1)S(1)}, bf16[128,1024]{1,0:T(8,128)(2,1)S(1)}, u32[]{:S(2)}, u32[]{:S(2)}) collective-permute-start(bf16[128,1024]{1,0:T(8,128)(2,1)S(1)} %get-tuple-element.20), channel_id=1, source_target_pairs={{0,1},{1,2},{2,3},{3,0},{4,5},{5,6},{6,7},{7,4},{8,9},{9,10},{10,1... | collective-permute-start | bytes 786440 | tf_op jit(solution)/shard_map/ppermute | solution.py:242
  8.1 1.6 %collective-permute-start.6 = (bf16[128,1024]{1,0:T(8,128)(2,1)S(1)}, bf16[128,1024]{1,0:T(8,128)(2,1)S(1)}, u32[]{:S(2)}, u32[]{:S(2)}) collective-permute-start(bf16[128,1024]{1,0:T(8,128)(2,1)S(1)} %get-tuple-element.25), channel_id=1, source_target_pairs={{0,4},{1,7},{2,6},{3,5},{4,0},{5,3},{6,2},{7,1},{8,12},{9,15},{10,... | collective-permute-start | bytes 786440 | tf_op jit(solution)/shard_map/ppermute | solution.py:242
  9.7 0.6 %route_far.1 = (bf16[64,1024]{1,0:T(8,128)(2,1)S(1)}, bf16[128,1024]{1,0:T(8,128)(2,1)S(1)}) custom-call(bf16[256,1024]{1,0:T(8,128)(2,1)S(1)} %copy-done, bf16[256,1024]{1,0:T(8,128)(2,1)S(1)} %collective-permute-done.refs_1_, s32[1,256]{1,0:T(1,128)S(1)} %get-tuple-element.21.refs_2_.slot_ref, s32[1,256]{1,0:T(1,128)S(1)} %collective-permute-done.1.refs_3_), custom_call_target="tpu_custom_call" | custom-call | flops 10000000000 | tf_op jit(solution)/shard_map/route_far/pallas_call | solution.py:106
  10.3 0.4 collective-permute-start.4
  10.7 2.1 %collective-permute-done.3.refs_0_ = bf16[64,1024]{1,0:T(8,128)(2,1)S(1)} collective-permute-done((bf16[64,1024]{1,0:T(8,128)(2,1)S(1)}, bf16[64,1024]{1,0:T(8,128)(2,1)S(1)}, u32[]{:S(2)}, u32[]{:S(2)}) %collective-permute-start.3) | collective-permute-done | bytes 131104 | tf_op jit(solution)/shard_map/ppermute | solution.py:242
  12.8 4.6 %collective-permute-start.2 = (bf16[128,1024]{1,0:T(8,128)(2,1)S(1)}, bf16[128,1024]{1,0:T(8,128)(2,1)S(1)}, u32[]{:S(2)}, u32[]{:S(2)}) collective-permute-start(bf16[128,1024]{1,0:T(8,128)(2,1)S(1)} %get-tuple-element.22), channel_id=1, source_target_pairs={{0,12},{1,15},{2,14},{3,13},{4,8},{5,11},{6,10},{7,9},{8,4},{9,7},... | collective-permute-start | bytes 786440 | tf_op jit(solution)/shard_map/ppermute | solution.py:242
  17.4 1.6 %collective-permute-done.4.refs_1_ = bf16[64,1024]{1,0:T(8,128)(2,1)S(1)} collective-permute-done((bf16[64,1024]{1,0:T(8,128)(2,1)S(1)}, bf16[64,1024]{1,0:T(8,128)(2,1)S(1)}, u32[]{:S(2)}, u32[]{:S(2)}) %collective-permute-start.4) | collective-permute-done | bytes 131104 | tf_op jit(solution)/shard_map/ppermute | solution.py:242
  19.0 7.5 %collective-permute-done.6.refs_3_ = bf16[128,1024]{1,0:T(8,128)(2,1)S(1)} collective-permute-done((bf16[128,1024]{1,0:T(8,128)(2,1)S(1)}, bf16[128,1024]{1,0:T(8,128)(2,1)S(1)}, u32[]{:S(2)}, u32[]{:S(2)}) %collective-permute-start.6) | collective-permute-done | bytes 262176 | tf_op jit(solution)/shard_map/ppermute | solution.py:242
  26.5 0.0 collective-permute-done.5.refs_2_
  26.5 0.1 regroup.1
  26.6 0.7 %collective-permute-start.7 = (bf16[96,1024]{1,0:T(8,128)(2,1)S(1)}, bf16[96,1024]{1,0:T(8,128)(2,1)S(1)}, u32[]{:S(2)}, u32[]{:S(2)}) collective-permute-start(bf16[96,1024]{1,0:T(8,128)(2,1)S(1)} %get-tuple-element.26), channel_id=1, source_target_pairs={{0,1},{1,0},{2,3},{3,2},{4,5},{5,4},{6,7},{7,6},{8,9},{9,8},{10,11... | collective-permute-start | bytes 589832 | tf_op jit(solution)/shard_map/ppermute | solution.py:226
  27.3 0.1 collective-permute-start.8
  27.4 0.4 %collective-permute-start.9 = (bf16[96,1024]{1,0:T(8,128)(2,1)S(1)}, bf16[96,1024]{1,0:T(8,128)(2,1)S(1)}, u32[]{:S(2)}, u32[]{:S(2)}) collective-permute-start(bf16[96,1024]{1,0:T(8,128)(2,1)S(1)} %get-tuple-element.28), channel_id=1, source_target_pairs={{0,1},{1,0},{2,3},{3,2},{4,5},{5,4},{6,7},{7,6},{8,9},{9,8},{10,11... | collective-permute-start | bytes 589832 | tf_op jit(solution)/shard_map/ppermute | solution.py:226
  27.8 0.1 collective-permute-start.10
  27.9 0.7 %count.1.refs_8_ = f32[1,384]{1,0:T(1,128)S(1)} custom-call(bf16[64,1024]{1,0:T(8,128)(2,1)S(1)} %pass.1.refs_0_, bf16[64,1024]{1,0:T(8,128)(2,1)S(1)} %collective-permute-done.4.refs_1_, bf16[128,1024]{1,0:T(8,128)(2,1)S(1)} %collective-permute-done.5.refs_2_, bf16[128,1024]{1,0:T(8,128)(2,1)S(1)} %collective-permute-done.6.refs_3_), custom_call_target="tpu_custom_call" | custom-call | tf_op jit(solution)/shard_map/count/pallas_call | solution.py:106
  28.6 0.2 collective-permute-done.8.refs_5_
  28.8 0.3 collective-permute-done.9.refs_6_
  29.0 0.3 collective-permute-done.10.refs_7_
  29.3 0.7 %cross.1.counts_ref = f32[1,384]{1,0:T(1,128)S(1)} custom-call(bf16[64,1024]{1,0:T(8,128)(2,1)S(1)} %pass.1.refs_0_, bf16[64,1024]{1,0:T(8,128)(2,1)S(1)} %collective-permute-done.4.refs_1_, bf16[128,1024]{1,0:T(8,128)(2,1)S(1)} %collective-permute-done.5.refs_2_, bf16[128,1024]{1,0:T(8,128)(2,1)S(1)} %collective-permute-done.6.refs_3_, ...), custom_call_target="tpu_custom_call" | custom-call | tf_op jit(solution)/shard_map/cross/pallas_call | solution.py:106
  30.0 0.3 collective-permute-start.11
  30.3 1.1 %late.1 = (f32[1,768]{1,0:T(1,128)S(1)}, f32[1,128]{1,0:T(1,128)S(1)}) custom-call(bf16[64,1024]{1,0:T(8,128)(2,1)S(1)} %pass.1.refs_0_, bf16[64,1024]{1,0:T(8,128)(2,1)S(1)} %collective-permute-done.4.refs_1_, bf16[128,1024]{1,0:T(8,128)(2,1)S(1)} %collective-permute-done.5.refs_2_, bf16[128,1024]{1,0:T(8,128)(2,1)S(1)} %collective-permute-done.6.refs_3_, ...), custom_call_target="tpu_custom_call" | custom-call | tf_op jit(solution)/shard_map/late/pallas_call | solution.py:106
  31.5 0.1 collective-permute-done.11.other_ref
  31.6 0.3 finish.1
  31.9 8.7 %all_to_all.5.counts_ref = f32[16,1,64]{2,1,0:T(1,128)S(1)} all-to-all(f32[16,1,64]{2,1,0:T(1,128)S(1)} %finish.1), channel_id=1, replica_groups={{15,14,13,12,11,10,9,8,7,6,5,4,3,2,1,0},{31,30,29,28,27,26,25,24,23,22,..., dimensions={0} | all-to-all | bytes 8192 | tf_op jit(solution)/shard_map/all_to_all | solution.py:328
  40.6 0.7 %select.1 = f32[1,256]{1,0:T(1,128)} custom-call(f32[16,1,64]{2,1,0:T(1,128)S(1)} %all_to_all.5.counts_ref, s32[1,256]{1,0:T(1,128)S(1)} %get-tuple-element.21.refs_2_.slot_ref), custom_call_target="tpu_custom_call" | custom-call | tf_op jit(solution)/shard_map/select/pallas_call | solution.py:106
  (7 shorter events, 0.0 us)
Async XLA Ops:
  0.0 0.7 %copy-start.1 = (s32[256]{0:T(256)S(1)}, s32[256]{0:T(256)}, u32[]{:S(2)}) copy-start(s32[256]{0:T(256)} %param.3) | copy-start | bytes 3076
  0.0 6.3 %collective-permute-start = (bf16[256,1024]{1,0:T(8,128)(2,1)}, bf16[256,1024]{1,0:T(8,128)(2,1)S(1)}, u32[]{:S(2)}, u32[]{:S(2)}) collective-permute-start(bf16[256,1024]{1,0:T(8,128)(2,1)} %refs_0_.3), channel_id=1, source_target_pairs={{0,1},{1,0},{2,3},{3,2},{4,5},{5,4},{6,7},{7,6},{8,9},{9,8},{10,11... | collective-permute-start | bytes 1572872 | tf_op jit(solution)/shard_map/ppermute | solution.py:226
  0.7 5.6 %collective-permute-start.1 = (s32[1,256]{1,0:T(1,128)S(1)}, s32[1,256]{1,0:T(1,128)S(1)}, u32[]{:S(2)}, u32[]{:S(2)}) collective-permute-start(s32[1,256]{1,0:T(1,128)S(1)} %bitcast.2), channel_id=1, source_target_pairs={{0,1},{1,0},{2,3},{3,2},{4,5},{5,4},{6,7},{7,6},{8,9},{9,8},{10,11... | collective-permute-start | bytes 3080 | tf_op jit(solution)/shard_map/ppermute | solution.py:226
  1.1 1.0 %copy-start = (bf16[256,1024]{1,0:T(8,128)(2,1)S(1)}, bf16[256,1024]{1,0:T(8,128)(2,1)}, u32[]{:S(2)}) copy-start(bf16[256,1024]{1,0:T(8,128)(2,1)} %refs_0_.3) | copy-start | bytes 1572868
  2.6 10.2 %collective-permute-start.3 = (bf16[64,1024]{1,0:T(8,128)(2,1)S(1)}, bf16[64,1024]{1,0:T(8,128)(2,1)S(1)}, u32[]{:S(2)}, u32[]{:S(2)}) collective-permute-start(bf16[64,1024]{1,0:T(8,128)(2,1)S(1)} %get-tuple-element.23), channel_id=1, source_target_pairs={{0,8},{1,11},{2,10},{3,9},{4,12},{5,15},{6,14},{7,13},{8,0},{9,3},... | collective-permute-start | bytes 393224 | tf_op jit(solution)/shard_map/ppermute | solution.py:242
  6.9 19.6 %collective-permute-start.5 = (bf16[128,1024]{1,0:T(8,128)(2,1)S(1)}, bf16[128,1024]{1,0:T(8,128)(2,1)S(1)}, u32[]{:S(2)}, u32[]{:S(2)}) collective-permute-start(bf16[128,1024]{1,0:T(8,128)(2,1)S(1)} %get-tuple-element.20), channel_id=1, source_target_pairs={{0,1},{1,2},{2,3},{3,0},{4,5},{5,6},{6,7},{7,4},{8,9},{9,10},{10,1... | collective-permute-start | bytes 786440 | tf_op jit(solution)/shard_map/ppermute | solution.py:242
  8.1 18.4 %collective-permute-start.6 = (bf16[128,1024]{1,0:T(8,128)(2,1)S(1)}, bf16[128,1024]{1,0:T(8,128)(2,1)S(1)}, u32[]{:S(2)}, u32[]{:S(2)}) collective-permute-start(bf16[128,1024]{1,0:T(8,128)(2,1)S(1)} %get-tuple-element.25), channel_id=1, source_target_pairs={{0,4},{1,7},{2,6},{3,5},{4,0},{5,3},{6,2},{7,1},{8,12},{9,15},{10,... | collective-permute-start | bytes 786440 | tf_op jit(solution)/shard_map/ppermute | solution.py:242
  10.3 8.7 %collective-permute-start.4 = (bf16[64,1024]{1,0:T(8,128)(2,1)S(1)}, bf16[64,1024]{1,0:T(8,128)(2,1)S(1)}, u32[]{:S(2)}, u32[]{:S(2)}) collective-permute-start(bf16[64,1024]{1,0:T(8,128)(2,1)S(1)} %get-tuple-element.24), channel_id=1, source_target_pairs={{0,8},{1,11},{2,10},{3,9},{4,12},{5,15},{6,14},{7,13},{8,0},{9,3},... | collective-permute-start | bytes 393224 | tf_op jit(solution)/shard_map/ppermute | solution.py:242
  12.8 17.2 %collective-permute-start.2 = (bf16[128,1024]{1,0:T(8,128)(2,1)S(1)}, bf16[128,1024]{1,0:T(8,128)(2,1)S(1)}, u32[]{:S(2)}, u32[]{:S(2)}) collective-permute-start(bf16[128,1024]{1,0:T(8,128)(2,1)S(1)} %get-tuple-element.22), channel_id=1, source_target_pairs={{0,12},{1,15},{2,14},{3,13},{4,8},{5,11},{6,10},{7,9},{8,4},{9,7},... | collective-permute-start | bytes 786440 | tf_op jit(solution)/shard_map/ppermute | solution.py:242
  26.6 2.0 %collective-permute-start.7 = (bf16[96,1024]{1,0:T(8,128)(2,1)S(1)}, bf16[96,1024]{1,0:T(8,128)(2,1)S(1)}, u32[]{:S(2)}, u32[]{:S(2)}) collective-permute-start(bf16[96,1024]{1,0:T(8,128)(2,1)S(1)} %get-tuple-element.26), channel_id=1, source_target_pairs={{0,1},{1,0},{2,3},{3,2},{4,5},{5,4},{6,7},{7,6},{8,9},{9,8},{10,11... | collective-permute-start | bytes 589832 | tf_op jit(solution)/shard_map/ppermute | solution.py:226
  27.3 1.4 %collective-permute-start.8 = (bf16[96,1024]{1,0:T(8,128)(2,1)S(1)}, bf16[96,1024]{1,0:T(8,128)(2,1)S(1)}, u32[]{:S(2)}, u32[]{:S(2)}) collective-permute-start(bf16[96,1024]{1,0:T(8,128)(2,1)S(1)} %get-tuple-element.27), channel_id=1, source_target_pairs={{0,1},{1,0},{2,3},{3,2},{4,5},{5,4},{6,7},{7,6},{8,9},{9,8},{10,11... | collective-permute-start | bytes 589832 | tf_op jit(solution)/shard_map/ppermute | solution.py:226
  27.4 1.6 %collective-permute-start.9 = (bf16[96,1024]{1,0:T(8,128)(2,1)S(1)}, bf16[96,1024]{1,0:T(8,128)(2,1)S(1)}, u32[]{:S(2)}, u32[]{:S(2)}) collective-permute-start(bf16[96,1024]{1,0:T(8,128)(2,1)S(1)} %get-tuple-element.28), channel_id=1, source_target_pairs={{0,1},{1,0},{2,3},{3,2},{4,5},{5,4},{6,7},{7,6},{8,9},{9,8},{10,11... | collective-permute-start | bytes 589832 | tf_op jit(solution)/shard_map/ppermute | solution.py:226
  27.8 1.5 %collective-permute-start.10 = (bf16[96,1024]{1,0:T(8,128)(2,1)S(1)}, bf16[96,1024]{1,0:T(8,128)(2,1)S(1)}, u32[]{:S(2)}, u32[]{:S(2)}) collective-permute-start(bf16[96,1024]{1,0:T(8,128)(2,1)S(1)} %get-tuple-element.29), channel_id=1, source_target_pairs={{0,1},{1,0},{2,3},{3,2},{4,5},{5,4},{6,7},{7,6},{8,9},{9,8},{10,11... | collective-permute-start | bytes 589832 | tf_op jit(solution)/shard_map/ppermute | solution.py:226
  30.0 1.6 %collective-permute-start.11 = (bf16[128,1024]{1,0:T(8,128)(2,1)S(1)}, bf16[128,1024]{1,0:T(8,128)(2,1)S(1)}, u32[]{:S(2)}, u32[]{:S(2)}) collective-permute-start(bf16[128,1024]{1,0:T(8,128)(2,1)S(1)} %collective-permute-done.2.refs_8_.late_ref), channel_id=1, source_target_pairs={{0,1},{1,0},{2,3},{3,2},{4,5},{5,4},{6,7},{7,6},{8,9},{9,8},{10,11... | collective-permute-start | bytes 786440 | tf_op jit(solution)/shard_map/ppermute | solution.py:226
